TPU v7x, 32 devices: a whole 2x2x4 slice. The times are simulated.
32 devices in a mesh: subset: 8 (over z, core), tile: 4 (over y, x).
Axes of the slice: x: 2, y: 2, z: 4, core: 2. Of those that a mesh axis runs over, the one named last changes fastest.
Arguments:
- blocks: bfloat16 [8, 4, 80, 128, 128], P('subset', 'tile'), may hold values from -11.8585412 to 11.8585412
- block_rows: int32 [8, 4, 80], P('subset', 'tile'), may hold values from 0 to 15, as said below
- block_cols: int32 [8, 4, 80], P('subset', 'tile'), may hold values from 0 to 31
- sinogram: float32 [4, 8, 16384], P(None, None, ('subset', 'tile')), may hold values from -6 to 6
Outputs:
- images: bfloat16 [8, 4, 8, 16384], P('subset', None, None, 'tile')
Inputs may be any that keep to these rules, and one draw needn't show every extreme that they name: `block_rows`: on each device every row block appears exactly 5 times, and no pair of row block and column block repeats on a device.
All inputs are finite; a program needn't handle non-finite values.
Results may differ from a plain program's by a relative error of at most 0.012.
Values may be sent and summed in bfloat16 or wider, within the bound.
No kernel may reach another device: no remote copies, remote signals or barrier semaphores. Data moves between devices by JAX's collectives and lax.ppermute only.
A program may use at most 64 MiB of HBM per device.

v0:
```python
import jax
import jax.numpy as jnp
from jax import lax
from jax.sharding import PartitionSpec as P

BS = 128
CROSSING_RAYS = 2048
PIX = 4096
RB = 16
CB = 32


relaxation = 0.5


def shifted(value, axis, by):
    length = lax.axis_size(axis)
    pairs = [(i, i + by) for i in range(length) if 0 <= i + by < length]
    return lax.ppermute(value, axis, pairs)


def per_device(blocks, block_rows, block_cols, sinogram):
    block_vals = blocks[0, 0]
    row_ids = block_rows[0, 0]
    col_ids = block_cols[0, 0]
    batches = sinogram.shape[0]
    slices = sinogram.shape[1]
    sections = lax.axis_size("subset")
    section_index = lax.axis_index("subset")
    row_onehot = (row_ids[:, None] == jnp.arange(RB, dtype=jnp.int32)[None, :]).astype(jnp.float32)
    col_hot = (col_ids[:, None] == jnp.arange(CB, dtype=jnp.int32)[None, :]).astype(jnp.float32)
    squares = jnp.sum(jnp.square(block_vals.astype(jnp.float32)), axis=2)
    norm_terms = jnp.einsum(
        "nb,nr->rb", squares, row_onehot, precision=lax.Precision.HIGHEST
    ).reshape(CROSSING_RAYS)
    norm_values = lax.psum(norm_terms, "tile")
    measured_all = lax.all_gather(sinogram, "tile", axis=2, tiled=True)

    def forward(current):
        rounded_values = current.astype(jnp.bfloat16).reshape(slices, CB, BS)
        gathered = rounded_values[:, col_ids]
        ray_products = jnp.einsum(
            "mnq,nbq->mnb", gathered, block_vals, preferred_element_type=jnp.float32
        )
        summed_rows = jnp.einsum(
            "vzj,zk->vkj", ray_products, row_onehot, precision=lax.Precision.HIGHEST
        )
        return summed_rows.reshape(slices, CROSSING_RAYS)

    def backward(weights):
        weight_rows = weights.reshape(slices, RB, BS)[:, row_ids]
        back_terms = jnp.einsum(
            "mnb,nbq->mnq", weight_rows, block_vals, preferred_element_type=jnp.float32
        )
        summed_rows = jnp.einsum(
            "mnq,nc->mcq", back_terms, col_hot, precision=lax.Precision.HIGHEST
        )
        return summed_rows.reshape(slices, PIX)

    def advance(moment, state_pair):
        image_in, images_out = state_pair
        batch_index = moment - section_index
        active = (batch_index >= 0) & (batch_index < batches)
        clamped = jnp.clip(batch_index, 0, batches - 1)
        local_terms = lax.cond(
            active,
            forward,
            lambda unused: jnp.zeros((slices, CROSSING_RAYS), jnp.float32),
            image_in,
        )
        measured = lax.dynamic_index_in_dim(measured_all, clamped, 0, keepdims=False)
        totals = lax.psum(local_terms.astype(jnp.bfloat16), "tile").astype(jnp.float32)
        weights = (relaxation * (measured - totals) / norm_values[None, :]).astype(jnp.bfloat16)
        update = lax.cond(
            active, backward, lambda unused: jnp.zeros((slices, PIX), jnp.float32), weights
        )
        image_new = image_in + update
        previous = lax.dynamic_index_in_dim(images_out, clamped, 0, keepdims=False)
        written = jnp.where(active, image_new.astype(jnp.bfloat16), previous)
        images_out = lax.dynamic_update_index_in_dim(images_out, written, clamped, 0)
        image_next = shifted(image_new, "subset", 1)
        return (image_next, images_out)

    initial = (
        jnp.zeros((slices, PIX), jnp.float32),
        jnp.zeros((batches, slices, PIX), jnp.bfloat16),
    )
    final_image, images_out = lax.fori_loop(0, batches + sections - 1, advance, initial)
    return images_out[None]


def solution(mesh):
    in_specs = (
        P("subset", "tile", None, None, None),
        P("subset", "tile", None),
        P("subset", "tile", None),
        P(None, None, ("subset", "tile")),
    )
    out_specs = P("subset", None, None, "tile")
    return jax.shard_map(
        per_device, mesh=mesh, in_specs=in_specs, out_specs=out_specs, check_vma=False
    )
```

profile of v0, /device:TPU:25, one launch (start us, length us, event | category | flops | bytes accessed | tf_op | source)
XLA Modules:
  0.0 290.8 jit_solution(6998667681582357716)
XLA Ops:
  0.0 3.3 %multiply_reduce_fusion = f32[80,128]{1,0:T(8,128)S(1)} fusion(bf16[1,1,80,128,128]{4,3,2,1,0:T(8,128)(2,1)} %param.10), kind=kLoop, calls=%fused_computation.34 | loop fusion | flops 3921920 | bytes 2662400 | tf_op jit(solution)/shard_map/reduce_sum | solution.py:32
  3.6 8.0 %psum.18 = f32[2048]{0:T(1024)S(1)} all-reduce(f32[2048]{0:T(1024)S(1)} %convolution_bitcast_fusion.2), channel_id=1, replica_groups=mesh['subset'=8,'tile'=4] {'tile'}, use_global_device_ids=true, to_apply=%region_1.0 | all-reduce | flops 2048 | bytes 16384 | tf_op jit(solution)/shard_map/psum | solution.py:36
  11.7 6.0 %all_gather.3 = f32[4,8,2048]{2,1,0:T(8,128)S(1)} all-gather(f32[4,8,512]{2,1,0:T(8,128)S(1)} %copy-done.1), channel_id=1, replica_groups=mesh['subset'=8,'tile'=4] {'tile'}, dimensions={2}, use_global_device_ids=true | all-gather | bytes 327680 | tf_op jit(solution)/shard_map/all_gather | solution.py:37
  18.5 272.4 %while.17 = (s32[]{:T(128)}, f32[8,4096]{1,0:T(8,128)S(1)}, bf16[4,8,4096]{2,1,0:T(8,128)(2,1)}, s32[]{:T(128)}, f32[4,8,2048]{2,1,0:T(8,128)S(1)}, /*index=5*/s...) while((s32[]{:T(128)}, f32[8,4096]{1,0:T(8,128)S(1)}, ...), condition=%wide.region_8.9_spmd.clone.clone, body=%wide.region_2.8_spmd.clone.clone.sunk | while | flops 89368552 | bytes 9651648 | solution.py:88
  18.5 12.1 %psum.22 = bf16[8,2048]{1,0:T(8,128)(2,1)S(1)} all-reduce(bf16[8,2048]{1,0:T(8,128)(2,1)S(1)} %get-tuple-element.398), channel_id=1, replica_groups=mesh['subset'=8,'tile'=4] {'tile'}, use_global_device_ids=true, to_apply=%region_5.5 | all-reduce | flops 16384 | bytes 65536 | tf_op jit(solution)/shard_map/while/body/eval_jaxpr/psum | solution.py:72
  32.3 1.3 collective-permute-start
  33.6 9.4 %collective-permute-done = f32[8,4096]{1,0:T(8,128)S(1)} collective-permute-done((f32[8,4096]{1,0:T(8,128)S(1)}, f32[8,4096]{1,0:T(8,128)S(1)}, u32[]{:S(2)}, u32[]{:S(2)}) %collective-permute-start) | collective-permute-done | bytes 131104 | tf_op jit(solution)/shard_map/while/body/eval_jaxpr/ppermute | solution.py:19
  43.0 11.4 %psum.22 = bf16[8,2048]{1,0:T(8,128)(2,1)S(1)} all-reduce(bf16[8,2048]{1,0:T(8,128)(2,1)S(1)} %get-tuple-element.398), channel_id=1, replica_groups=mesh['subset'=8,'tile'=4] {'tile'}, use_global_device_ids=true, to_apply=%region_5.5 | all-reduce | flops 16384 | bytes 65536 | tf_op jit(solution)/shard_map/while/body/eval_jaxpr/psum | solution.py:72
  55.9 1.3 collective-permute-start
  57.2 8.7 %collective-permute-done = f32[8,4096]{1,0:T(8,128)S(1)} collective-permute-done((f32[8,4096]{1,0:T(8,128)S(1)}, f32[8,4096]{1,0:T(8,128)S(1)}, u32[]{:S(2)}, u32[]{:S(2)}) %collective-permute-start) | collective-permute-done | bytes 131104 | tf_op jit(solution)/shard_map/while/body/eval_jaxpr/ppermute | solution.py:19
  66.0 11.6 %psum.22 = bf16[8,2048]{1,0:T(8,128)(2,1)S(1)} all-reduce(bf16[8,2048]{1,0:T(8,128)(2,1)S(1)} %get-tuple-element.398), channel_id=1, replica_groups=mesh['subset'=8,'tile'=4] {'tile'}, use_global_device_ids=true, to_apply=%region_5.5 | all-reduce | flops 16384 | bytes 65536 | tf_op jit(solution)/shard_map/while/body/eval_jaxpr/psum | solution.py:72
  79.2 1.3 collective-permute-start
  80.5 8.7 %collective-permute-done = f32[8,4096]{1,0:T(8,128)S(1)} collective-permute-done((f32[8,4096]{1,0:T(8,128)S(1)}, f32[8,4096]{1,0:T(8,128)S(1)}, u32[]{:S(2)}, u32[]{:S(2)}) %collective-permute-start) | collective-permute-done | bytes 131104 | tf_op jit(solution)/shard_map/while/body/eval_jaxpr/ppermute | solution.py:19
  89.2 10.8 %psum.22 = bf16[8,2048]{1,0:T(8,128)(2,1)S(1)} all-reduce(bf16[8,2048]{1,0:T(8,128)(2,1)S(1)} %get-tuple-element.398), channel_id=1, replica_groups=mesh['subset'=8,'tile'=4] {'tile'}, use_global_device_ids=true, to_apply=%region_5.5 | all-reduce | flops 16384 | bytes 65536 | tf_op jit(solution)/shard_map/while/body/eval_jaxpr/psum | solution.py:72
  101.7 1.3 collective-permute-start
  102.9 8.5 %collective-permute-done = f32[8,4096]{1,0:T(8,128)S(1)} collective-permute-done((f32[8,4096]{1,0:T(8,128)S(1)}, f32[8,4096]{1,0:T(8,128)S(1)}, u32[]{:S(2)}, u32[]{:S(2)}) %collective-permute-start) | collective-permute-done | bytes 131104 | tf_op jit(solution)/shard_map/while/body/eval_jaxpr/ppermute | solution.py:19
  111.5 11.8 %psum.22 = bf16[8,2048]{1,0:T(8,128)(2,1)S(1)} all-reduce(bf16[8,2048]{1,0:T(8,128)(2,1)S(1)} %get-tuple-element.398), channel_id=1, replica_groups=mesh['subset'=8,'tile'=4] {'tile'}, use_global_device_ids=true, to_apply=%region_5.5 | all-reduce | flops 16384 | bytes 65536 | tf_op jit(solution)/shard_map/while/body/eval_jaxpr/psum | solution.py:72
  124.9 1.3 collective-permute-start
  126.2 8.5 %collective-permute-done = f32[8,4096]{1,0:T(8,128)S(1)} collective-permute-done((f32[8,4096]{1,0:T(8,128)S(1)}, f32[8,4096]{1,0:T(8,128)S(1)}, u32[]{:S(2)}, u32[]{:S(2)}) %collective-permute-start) | collective-permute-done | bytes 131104 | tf_op jit(solution)/shard_map/while/body/eval_jaxpr/ppermute | solution.py:19
  134.7 11.3 %psum.22 = bf16[8,2048]{1,0:T(8,128)(2,1)S(1)} all-reduce(bf16[8,2048]{1,0:T(8,128)(2,1)S(1)} %get-tuple-element.398), channel_id=1, replica_groups=mesh['subset'=8,'tile'=4] {'tile'}, use_global_device_ids=true, to_apply=%region_5.5 | all-reduce | flops 16384 | bytes 65536 | tf_op jit(solution)/shard_map/while/body/eval_jaxpr/psum | solution.py:72
  147.6 1.3 collective-permute-start
  148.9 8.7 %collective-permute-done = f32[8,4096]{1,0:T(8,128)S(1)} collective-permute-done((f32[8,4096]{1,0:T(8,128)S(1)}, f32[8,4096]{1,0:T(8,128)S(1)}, u32[]{:S(2)}, u32[]{:S(2)}) %collective-permute-start) | collective-permute-done | bytes 131104 | tf_op jit(solution)/shard_map/while/body/eval_jaxpr/ppermute | solution.py:19
  157.7 11.6 %psum.22 = bf16[8,2048]{1,0:T(8,128)(2,1)S(1)} all-reduce(bf16[8,2048]{1,0:T(8,128)(2,1)S(1)} %get-tuple-element.398), channel_id=1, replica_groups=mesh['subset'=8,'tile'=4] {'tile'}, use_global_device_ids=true, to_apply=%region_5.5 | all-reduce | flops 16384 | bytes 65536 | tf_op jit(solution)/shard_map/while/body/eval_jaxpr/psum | solution.py:72
  170.9 1.3 collective-permute-start
  172.2 13.9 %collective-permute-done = f32[8,4096]{1,0:T(8,128)S(1)} collective-permute-done((f32[8,4096]{1,0:T(8,128)S(1)}, f32[8,4096]{1,0:T(8,128)S(1)}, u32[]{:S(2)}, u32[]{:S(2)}) %collective-permute-start) | collective-permute-done | bytes 131104 | tf_op jit(solution)/shard_map/while/body/eval_jaxpr/ppermute | solution.py:19
  186.0 2.5 conditional.8
  186.7 1.4 fusion.6
  188.5 10.7 %psum.22 = bf16[8,2048]{1,0:T(8,128)(2,1)S(1)} all-reduce(bf16[8,2048]{1,0:T(8,128)(2,1)S(1)} %get-tuple-element.398), channel_id=1, replica_groups=mesh['subset'=8,'tile'=4] {'tile'}, use_global_device_ids=true, to_apply=%region_5.5 | all-reduce | flops 16384 | bytes 65536 | tf_op jit(solution)/shard_map/while/body/eval_jaxpr/psum | solution.py:72
  200.2 1.9 conditional.9
  202.8 1.3 collective-permute-start
  204.0 9.0 %collective-permute-done = f32[8,4096]{1,0:T(8,128)S(1)} collective-permute-done((f32[8,4096]{1,0:T(8,128)S(1)}, f32[8,4096]{1,0:T(8,128)S(1)}, u32[]{:S(2)}, u32[]{:S(2)}) %collective-permute-start) | collective-permute-done | bytes 131104 | tf_op jit(solution)/shard_map/while/body/eval_jaxpr/ppermute | solution.py:19
  213.0 2.5 conditional.8
  213.7 1.4 fusion.6
  215.6 11.4 %psum.22 = bf16[8,2048]{1,0:T(8,128)(2,1)S(1)} all-reduce(bf16[8,2048]{1,0:T(8,128)(2,1)S(1)} %get-tuple-element.398), channel_id=1, replica_groups=mesh['subset'=8,'tile'=4] {'tile'}, use_global_device_ids=true, to_apply=%region_5.5 | all-reduce | flops 16384 | bytes 65536 | tf_op jit(solution)/shard_map/while/body/eval_jaxpr/psum | solution.py:72
  227.8 1.9 conditional.9
  230.4 1.3 collective-permute-start
  231.7 8.7 %collective-permute-done = f32[8,4096]{1,0:T(8,128)S(1)} collective-permute-done((f32[8,4096]{1,0:T(8,128)S(1)}, f32[8,4096]{1,0:T(8,128)S(1)}, u32[]{:S(2)}, u32[]{:S(2)}) %collective-permute-start) | collective-permute-done | bytes 131104 | tf_op jit(solution)/shard_map/while/body/eval_jaxpr/ppermute | solution.py:19
  240.4 2.5 conditional.8
  241.1 1.4 fusion.6
  242.9 11.3 %psum.22 = bf16[8,2048]{1,0:T(8,128)(2,1)S(1)} all-reduce(bf16[8,2048]{1,0:T(8,128)(2,1)S(1)} %get-tuple-element.398), channel_id=1, replica_groups=mesh['subset'=8,'tile'=4] {'tile'}, use_global_device_ids=true, to_apply=%region_5.5 | all-reduce | flops 16384 | bytes 65536 | tf_op jit(solution)/shard_map/while/body/eval_jaxpr/psum | solution.py:72
  255.1 1.9 conditional.9
  257.7 1.3 collective-permute-start
  258.9 8.7 %collective-permute-done = f32[8,4096]{1,0:T(8,128)S(1)} collective-permute-done((f32[8,4096]{1,0:T(8,128)S(1)}, f32[8,4096]{1,0:T(8,128)S(1)}, u32[]{:S(2)}, u32[]{:S(2)}) %collective-permute-start) | collective-permute-done | bytes 131104 | tf_op jit(solution)/shard_map/while/body/eval_jaxpr/ppermute | solution.py:19
  267.7 2.5 conditional.8
  268.4 1.4 fusion.6
  270.2 11.5 %psum.22 = bf16[8,2048]{1,0:T(8,128)(2,1)S(1)} all-reduce(bf16[8,2048]{1,0:T(8,128)(2,1)S(1)} %get-tuple-element.398), channel_id=1, replica_groups=mesh['subset'=8,'tile'=4] {'tile'}, use_global_device_ids=true, to_apply=%region_5.5 | all-reduce | flops 16384 | bytes 65536 | tf_op jit(solution)/shard_map/while/body/eval_jaxpr/psum | solution.py:72
  282.6 1.9 conditional.9
  286.4 4.4 %collective-permute-done = f32[8,4096]{1,0:T(8,128)S(1)} collective-permute-done((f32[8,4096]{1,0:T(8,128)S(1)}, f32[8,4096]{1,0:T(8,128)S(1)}, u32[]{:S(2)}, u32[]{:S(2)}) %collective-permute-start) | collective-permute-done | bytes 131104 | tf_op jit(solution)/shard_map/while/body/eval_jaxpr/ppermute | solution.py:19
  (143 shorter events, 31.3 us)
Async XLA Ops:
  0.0 3.4 %copy-start.3 = (s32[1,1,80]{2,1,0:T(1,128)S(1)}, s32[1,1,80]{2,1,0:T(1,128)}, u32[]{:S(2)}) copy-start(s32[1,1,80]{2,1,0:T(1,128)} %param.11) | copy-start | bytes 964
  0.0 18.4 %copy-start = (bf16[1,1,80,128,128]{4,3,2,1,0:T(8,128)(2,1)S(1)}, bf16[1,1,80,128,128]{4,3,2,1,0:T(8,128)(2,1)}, u32[]{:S(2)}) copy-start(bf16[1,1,80,128,128]{4,3,2,1,0:T(8,128)(2,1)} %param.10) | copy-start | bytes 7864324
  0.0 11.7 %copy-start.1 = (f32[4,8,512]{2,1,0:T(8,128)S(1)}, f32[4,8,512]{2,1,0:T(8,128)}, u32[]{:S(2)}) copy-start(f32[4,8,512]{2,1,0:T(8,128)} %param.13) | copy-start | bytes 196612
  0.0 18.4 %copy-start.2 = (s32[1,1,80]{2,1,0:T(1,128)S(1)}, s32[1,1,80]{2,1,0:T(1,128)}, u32[]{:S(2)}) copy-start(s32[1,1,80]{2,1,0:T(1,128)} %param.12) | copy-start | bytes 964
  32.3 10.7 %collective-permute-start = (f32[8,4096]{1,0:T(8,128)S(1)}, f32[8,4096]{1,0:T(8,128)S(1)}, u32[]{:S(2)}, u32[]{:S(2)}) collective-permute-start(f32[8,4096]{1,0:T(8,128)S(1)} %get-tuple-element.357), channel_id=1, source_target_pairs={{0,4},{4,8},{8,12},{12,16},{16,20},{20,24},{24,28},{1,5},{5,9},{9,... | collective-permute-start | bytes 393224 | tf_op jit(solution)/shard_map/while/body/eval_jaxpr/ppermute | solution.py:19
  55.9 10.0 %collective-permute-start = (f32[8,4096]{1,0:T(8,128)S(1)}, f32[8,4096]{1,0:T(8,128)S(1)}, u32[]{:S(2)}, u32[]{:S(2)}) collective-permute-start(f32[8,4096]{1,0:T(8,128)S(1)} %get-tuple-element.357), channel_id=1, source_target_pairs={{0,4},{4,8},{8,12},{12,16},{16,20},{20,24},{24,28},{1,5},{5,9},{9,... | collective-permute-start | bytes 393224 | tf_op jit(solution)/shard_map/while/body/eval_jaxpr/ppermute | solution.py:19
  79.2 10.0 %collective-permute-start = (f32[8,4096]{1,0:T(8,128)S(1)}, f32[8,4096]{1,0:T(8,128)S(1)}, u32[]{:S(2)}, u32[]{:S(2)}) collective-permute-start(f32[8,4096]{1,0:T(8,128)S(1)} %get-tuple-element.357), channel_id=1, source_target_pairs={{0,4},{4,8},{8,12},{12,16},{16,20},{20,24},{24,28},{1,5},{5,9},{9,... | collective-permute-start | bytes 393224 | tf_op jit(solution)/shard_map/while/body/eval_jaxpr/ppermute | solution.py:19
  101.7 9.8 %collective-permute-start = (f32[8,4096]{1,0:T(8,128)S(1)}, f32[8,4096]{1,0:T(8,128)S(1)}, u32[]{:S(2)}, u32[]{:S(2)}) collective-permute-start(f32[8,4096]{1,0:T(8,128)S(1)} %get-tuple-element.357), channel_id=1, source_target_pairs={{0,4},{4,8},{8,12},{12,16},{16,20},{20,24},{24,28},{1,5},{5,9},{9,... | collective-permute-start | bytes 393224 | tf_op jit(solution)/shard_map/while/body/eval_jaxpr/ppermute | solution.py:19
  124.9 9.8 %collective-permute-start = (f32[8,4096]{1,0:T(8,128)S(1)}, f32[8,4096]{1,0:T(8,128)S(1)}, u32[]{:S(2)}, u32[]{:S(2)}) collective-permute-start(f32[8,4096]{1,0:T(8,128)S(1)} %get-tuple-element.357), channel_id=1, source_target_pairs={{0,4},{4,8},{8,12},{12,16},{16,20},{20,24},{24,28},{1,5},{5,9},{9,... | collective-permute-start | bytes 393224 | tf_op jit(solution)/shard_map/while/body/eval_jaxpr/ppermute | solution.py:19
  147.6 10.0 %collective-permute-start = (f32[8,4096]{1,0:T(8,128)S(1)}, f32[8,4096]{1,0:T(8,128)S(1)}, u32[]{:S(2)}, u32[]{:S(2)}) collective-permute-start(f32[8,4096]{1,0:T(8,128)S(1)} %get-tuple-element.357), channel_id=1, source_target_pairs={{0,4},{4,8},{8,12},{12,16},{16,20},{20,24},{24,28},{1,5},{5,9},{9,... | collective-permute-start | bytes 393224 | tf_op jit(solution)/shard_map/while/body/eval_jaxpr/ppermute | solution.py:19
  170.9 15.1 %collective-permute-start = (f32[8,4096]{1,0:T(8,128)S(1)}, f32[8,4096]{1,0:T(8,128)S(1)}, u32[]{:S(2)}, u32[]{:S(2)}) collective-permute-start(f32[8,4096]{1,0:T(8,128)S(1)} %get-tuple-element.357), channel_id=1, source_target_pairs={{0,4},{4,8},{8,12},{12,16},{16,20},{20,24},{24,28},{1,5},{5,9},{9,... | collective-permute-start | bytes 393224 | tf_op jit(solution)/shard_map/while/body/eval_jaxpr/ppermute | solution.py:19
  202.8 10.3 %collective-permute-start = (f32[8,4096]{1,0:T(8,128)S(1)}, f32[8,4096]{1,0:T(8,128)S(1)}, u32[]{:S(2)}, u32[]{:S(2)}) collective-permute-start(f32[8,4096]{1,0:T(8,128)S(1)} %get-tuple-element.357), channel_id=1, source_target_pairs={{0,4},{4,8},{8,12},{12,16},{16,20},{20,24},{24,28},{1,5},{5,9},{9,... | collective-permute-start | bytes 393224 | tf_op jit(solution)/shard_map/while/body/eval_jaxpr/ppermute | solution.py:19
  230.4 10.0 %collective-permute-start = (f32[8,4096]{1,0:T(8,128)S(1)}, f32[8,4096]{1,0:T(8,128)S(1)}, u32[]{:S(2)}, u32[]{:S(2)}) collective-permute-start(f32[8,4096]{1,0:T(8,128)S(1)} %get-tuple-element.357), channel_id=1, source_target_pairs={{0,4},{4,8},{8,12},{12,16},{16,20},{20,24},{24,28},{1,5},{5,9},{9,... | collective-permute-start | bytes 393224 | tf_op jit(solution)/shard_map/while/body/eval_jaxpr/ppermute | solution.py:19
  257.7 10.0 %collective-permute-start = (f32[8,4096]{1,0:T(8,128)S(1)}, f32[8,4096]{1,0:T(8,128)S(1)}, u32[]{:S(2)}, u32[]{:S(2)}) collective-permute-start(f32[8,4096]{1,0:T(8,128)S(1)} %get-tuple-element.357), channel_id=1, source_target_pairs={{0,4},{4,8},{8,12},{12,16},{16,20},{20,24},{24,28},{1,5},{5,9},{9,... | collective-permute-start | bytes 393224 | tf_op jit(solution)/shard_map/while/body/eval_jaxpr/ppermute | solution.py:19
  285.2 5.7 %collective-permute-start = (f32[8,4096]{1,0:T(8,128)S(1)}, f32[8,4096]{1,0:T(8,128)S(1)}, u32[]{:S(2)}, u32[]{:S(2)}) collective-permute-start(f32[8,4096]{1,0:T(8,128)S(1)} %get-tuple-element.357), channel_id=1, source_target_pairs={{0,4},{4,8},{8,12},{12,16},{16,20},{20,24},{24,28},{1,5},{5,9},{9,... | collective-permute-start | bytes 393224 | tf_op jit(solution)/shard_map/while/body/eval_jaxpr/ppermute | solution.py:19
where the time goes:
time: 295 us; the launch traced here: 291 us
  blocking collectives  140 us (47%)
  waiting for transfers between devices  97.3 us (33%)
  local copies, waits for them, and re-layouts  15.7 us (5%)
  starting transfers between devices  14.1 us (5%)
  matrix products  11.9 us (4%)
  other arithmetic  11 us (4%)
    psum x11, blocking collectives, advance(): lax.psum(local_terms.astype(jnp.bfloat16), 'tile').astype(jnp.float32)  125 us
    ppermute x11, waiting for transfers between devices, shifted(): return lax.ppermute(value, axis, pairs)  97.3 us
    ppermute x11, starting transfers between devices, shifted(): return lax.ppermute(value, axis, pairs)  14.1 us
    dynamic_slice x11, local copies, waits for them, and re-layouts, advance(): previous = lax.dynamic_index_in_dim(images_out, clamped, 0, keepdims=False)  9.32 us
    psum x1, blocking collectives, per_device(): norm_values = lax.psum(norm_terms, 'tile')  8.03 us
    dynamic_update_slice x11, other arithmetic, advance(): lax.dynamic_update_index_in_dim(images_out, written, clamped, 0)  7.23 us
    all_gather x1, blocking collectives, per_device(): measured_all = lax.all_gather(sinogram, 'tile', axis=2, tiled=True)  6.03 us
  transfers between devices with their start and end apart: 11, of which 11 were waited for; matrix products, arithmetic and copies ran while one was open for 0% of the time, Pallas kernels for 0%

commit v1 on v0

v1 whole, which is shorter than its diff:
```python
import functools

import jax
import jax.numpy as jnp
from jax import lax
from jax.experimental import pallas as pl
from jax.experimental.pallas import tpu as pltpu
from jax.sharding import PartitionSpec as P

BS = 128
PIX = 4096
CB = PIX // BS
relaxation = 0.5

DIRECT = 4

NN = (((1,), (0,)), ((), ()))
NT = (((1,), (1,)), ((), ()))
VMEM = pl.BlockSpec(memory_space=pltpu.VMEM)
SMEM = pl.BlockSpec(memory_space=pltpu.SMEM)
PARAMS = pltpu.CompilerParams(vmem_limit_bytes=20 * 2**20)


def dot(lhs, rhs, dims):
    return lax.dot_general(lhs, rhs, dims, preferred_element_type=jnp.float32)


def head_kernel(pos, index, blocks, rays, term, norm_scr):
    count = blocks.shape[0]
    row_blocks = norm_scr.shape[0]
    quarter = rays.shape[0]
    slices = rays.shape[1]
    norm_scr[...] = jnp.zeros_like(norm_scr)
    on_diagonal = lax.broadcasted_iota(jnp.int32, (BS, BS), 0) == lax.broadcasted_iota(
        jnp.int32, (BS, BS), 1
    )
    for n in range(count):
        block = blocks[n]
        gram = jnp.where(on_diagonal, dot(block, block, NT), 0.0)
        part = gram[0:8]
        for k in range(8, BS, 8):
            part = part + gram[k : k + 8]
        row = index[0, n]
        norm_scr[row] = norm_scr[row] + part
    sums = jnp.sum(norm_scr[...], axis=1)
    coarse = sums.astype(jnp.bfloat16)
    fine = (sums - coarse.astype(jnp.float32)).astype(jnp.bfloat16)
    term[0:row_blocks] = jnp.zeros((row_blocks, slices, BS), jnp.bfloat16)
    for i in range(quarter):
        term[pos[1] * quarter + i] = (-rays[i]).astype(jnp.bfloat16)
    pad = slices - 2 * row_blocks
    parts = [coarse, fine]
    if pad:
        parts.append(jnp.zeros((pad, BS), jnp.bfloat16))
    term[row_blocks] = jnp.concatenate(parts, axis=0)


def weights_of(terms, row_blocks, w_scr):
    norms = 0.0
    for ref in terms:
        slab = ref[row_blocks].astype(jnp.float32)
        norms = norms + slab[0:row_blocks] + slab[row_blocks : 2 * row_blocks]
    scale = -relaxation / norms
    for r in range(row_blocks):
        total = terms[0][r].astype(jnp.float32)
        for ref in terms[1:]:
            total = total + ref[r].astype(jnp.float32)
        w_scr[r] = (total * scale[r : r + 1]).astype(jnp.bfloat16)


def back_project(index, blocks, w_scr, x_scr):
    for n in range(blocks.shape[0]):
        col = index[1, n]
        x_scr[col] = x_scr[col] + dot(w_scr[index[0, n]], blocks[n], NN)


def step_kernel(step, n_terms, has_image, *refs):
    refs = list(refs)
    pos, index_prev, index = refs[:3]
    terms = refs[3 : 3 + n_terms]
    rest = refs[3 + n_terms :]
    if has_image:
        image, offset = rest.pop(0)
    blocks_prev, blocks, rays, head, held, full, term, w_scr, x_scr, p_scr = rest
    row_blocks = p_scr.shape[0]
    quarter = rays.shape[0]
    active = pos[0] == step

    @pl.when(active)
    def _():
        weights_of(terms, row_blocks, w_scr)
        if has_image:
            x_scr[...] = image[offset : offset + CB].astype(jnp.float32)
        else:
            x_scr[...] = jnp.zeros_like(x_scr)
        back_project(index_prev, blocks_prev, w_scr, x_scr)
        base = row_blocks + 1
        full[base : base + CB] = x_scr[...].astype(jnp.bfloat16)
        p_scr[...] = jnp.zeros_like(p_scr)
        for i in range(quarter):
            p_scr[pos[1] * quarter + i] = -rays[i]
        for n in range(blocks.shape[0]):
            row = index[0, n]
            p_scr[row] = p_scr[row] + dot(full[base + index[1, n]], blocks[n], NT)
        out = p_scr[...].astype(jnp.bfloat16)
        full[0:row_blocks] = out
        full[row_blocks] = head[row_blocks]
        term[0:row_blocks] = out
        term[row_blocks] = head[row_blocks]

    @pl.when(jnp.logical_not(active))
    def _():
        full[...] = held[...]


def last_kernel(last, n_terms, *refs):
    pos, index = refs[:2]
    terms = refs[2 : 2 + n_terms]
    blocks, full, back, images, w_scr, x_scr = refs[2 + n_terms :]
    row_blocks = w_scr.shape[0]
    base = row_blocks + 1
    batches, slices, _ = images.shape
    active = pos[0] == last

    @pl.when(active)
    def _():
        weights_of(terms, row_blocks, w_scr)
        x_scr[...] = full[base : base + CB].astype(jnp.float32)
        back_project(index, blocks, w_scr, x_scr)
        for c in range(CB):
            value = x_scr[c].reshape(batches, slices, BS)
            images[:, :, c * BS : (c + 1) * BS] = value.astype(jnp.bfloat16)

    @pl.when(jnp.logical_not(active))
    def _():
        for c in range(CB):
            value = back[base + c].astype(jnp.float32).reshape(batches, slices, BS)
            images[:, :, c * BS : (c + 1) * BS] = value.astype(jnp.bfloat16)


def per_device(blocks, block_rows, block_cols, sinogram):
    blocks = blocks[0, 0]
    index = jnp.concatenate([block_rows[0], block_cols[0]], axis=0)
    batches, per_batch, rays_here = sinogram.shape
    slices = batches * per_batch
    quarter = rays_here // BS
    subsets = lax.axis_size("subset")
    tiles = lax.axis_size("tile")
    row_blocks = quarter * tiles
    pos = jnp.stack([lax.axis_index("subset"), lax.axis_index("tile")]).astype(jnp.int32)
    rays = sinogram.reshape(slices, quarter, BS).transpose(1, 0, 2)
    axes = ("subset", "tile")

    def moved(value, sources, by, turn=0):
        pairs = [
            (s * tiles + t, (s + by) * tiles + (t + turn) % tiles)
            for s in sources
            for t in range(tiles)
            if 0 <= s + by < subsets
        ]
        return lax.ppermute(value, axes, pairs)

    full_shape = jax.ShapeDtypeStruct((row_blocks + 1 + CB, slices, BS), jnp.bfloat16)
    term_shape = jax.ShapeDtypeStruct((row_blocks + 1, slices, BS), jnp.bfloat16)
    w_scr = pltpu.VMEM((row_blocks, slices, BS), jnp.bfloat16)
    x_scr = pltpu.VMEM((CB, slices, BS), jnp.float32)
    p_scr = pltpu.VMEM((row_blocks, slices, BS), jnp.float32)

    from_even = moved(blocks, range(0, subsets, 2), 1)
    from_odd = moved(blocks, range(1, subsets, 2), 1)
    head = pl.pallas_call(
        head_kernel,
        out_shape=term_shape,
        in_specs=[SMEM, SMEM, VMEM, VMEM],
        out_specs=VMEM,
        scratch_shapes=[pltpu.VMEM((row_blocks, 8, BS), jnp.float32)],
        compiler_params=PARAMS,
        name="head",
    )(pos, index, blocks, rays)
    index_prev = moved(index, range(subsets), 1)

    term = head
    full = jnp.zeros(full_shape.shape, full_shape.dtype)
    for step in range(1, subsets):
        image = None
        if tiles <= DIRECT:
            first = term if step == 1 else full
            terms = [moved(first, [step - 1], 1)]
            if step > 1:
                image = terms[0]
            terms += [moved(term, [step - 1], 1, turn) for turn in range(1, tiles)]
            n_terms = tiles
        else:
            summed = lax.psum(term.astype(jnp.float32), "tile")
            terms = [moved(summed, [step - 1], 1)]
            n_terms = 1
            if step > 1:
                image = moved(full, [step - 1], 1)
        operands = list(terms)
        if image is not None and tiles > DIRECT:
            operands.append(image)
        blocks_prev = from_even if step % 2 else from_odd

        def body(*refs, step=step, n_terms=n_terms, image=image):
            refs = list(refs)
            at = 3 + n_terms
            if image is not None:
                if tiles <= DIRECT:
                    refs.insert(at, (refs[3], row_blocks + 1))
                else:
                    refs[at] = (refs[at], row_blocks + 1)
            step_kernel(step, n_terms, image is not None, *refs)

        full, term = pl.pallas_call(
            body,
            out_shape=(full_shape, term_shape),
            in_specs=[SMEM] * 3 + [VMEM] * (len(operands) + 5),
            out_specs=(VMEM, VMEM),
            scratch_shapes=[w_scr, x_scr, p_scr],
            compiler_params=PARAMS,
            name="step",
        )(pos, index_prev, index, *operands, blocks_prev, blocks, rays, head, full)

    last = subsets - 1
    if tiles <= DIRECT:
        terms = [term] + [moved(term, [last], 0, turn) for turn in range(1, tiles)]
    else:
        terms = [lax.psum(term.astype(jnp.float32), "tile")]
    back = moved(full, range(1, subsets), -1)
    images = pl.pallas_call(
        functools.partial(last_kernel, last, len(terms)),
        out_shape=jax.ShapeDtypeStruct((batches, per_batch, PIX), jnp.bfloat16),
        in_specs=[SMEM] * 2 + [VMEM] * (len(terms) + 3),
        out_specs=VMEM,
        scratch_shapes=[w_scr, x_scr],
        compiler_params=PARAMS,
        name="last",
    )(pos, index, *terms, blocks, full, back)
    return images[None]


def solution(mesh):
    in_specs = (
        P("subset", "tile", None, None, None),
        P("subset", "tile", None),
        P("subset", "tile", None),
        P(None, None, ("subset", "tile")),
    )
    out_specs = P("subset", None, None, "tile")
    return jax.shard_map(
        per_device, mesh=mesh, in_specs=in_specs, out_specs=out_specs, check_vma=False
    )
```

time: 295 us -> 148 us (0.50); the launches traced: 291 us -> 148 us
  blocking collectives: 140 us -> 0 us
  starting transfers between devices: 14.1 us -> 35.4 us
  Pallas kernels: 0 us -> 15.1 us
  local copies, waits for them, and re-layouts: 15.7 us -> 2.66 us
  matrix products: 11.9 us -> 0 us
  other arithmetic: 11 us -> 0.76 us
  waiting for transfers between devices: 97.3 us -> 93.1 us
    psum x12 -> x0, blocking collectives: 133 us -> none  [the longest x11 125 us: advance(): lax.psum(local_terms.astype(jnp.bfloat16), 'tile').astype(jnp.float32)]
    ppermute x11 -> x35, starting transfers between devices: 14.1 us -> 35.4 us  [moved(): return lax.ppermute(value, axes, pairs)]
    pallas_call x0 -> x9, Pallas kernels: none -> 15.1 us  [the longest x7 10.4 us: per_device(): pl.pallas_call(body, out_shape=(full_shape, term_shape), in_specs=[SMEM]...]
    dot_general x17 -> x0, matrix products: 11.9 us -> none  [the longest x4 5.77 us: forward(): jnp.einsum('mnq,nbq->mnb', gathered, block_vals, preferred_element_type=j...]
    dynamic_slice x11 -> x0, local copies, waits for them, and re-layouts: 9.32 us -> none  [advance(): previous = lax.dynamic_index_in_dim(images_out, clamped, 0, keepdims=False)]
    dynamic_update_slice x11 -> x0, other arithmetic: 7.23 us -> none  [advance(): lax.dynamic_update_index_in_dim(images_out, written, clamped, 0)]
    all_gather x1 -> x0, blocking collectives: 6.03 us -> none  [per_device(): measured_all = lax.all_gather(sinogram, 'tile', axis=2, tiled=True)]
    gather x8 -> x0, local copies, waits for them, and re-layouts: 5.18 us -> none  [the longest x4 2.59 us: forward(): gathered = rounded_values[:, col_ids]]
  transfers between devices with their start and end apart: 11 -> 35, of which waited for: 11 -> 5; matrix products, arithmetic and copies ran while one was open for 0% -> 1% of each run, Pallas kernels for 0% -> 2%
where the time goes in v1:
time: 148 us
  waiting for transfers between devices  93.1 us (63%)
  starting transfers between devices  35.4 us (24%)
  Pallas kernels  15.1 us (10%)
  local copies, waits for them, and re-layouts  2.66 us (2%)
    ppermute x35, waiting for transfers between devices, moved(): return lax.ppermute(value, axes, pairs)  93.1 us
    ppermute x35, starting transfers between devices, moved(): return lax.ppermute(value, axes, pairs)  35.4 us
    pallas_call x7, Pallas kernels, per_device(): pl.pallas_call(body, out_shape=(full_shape, term_shape), in_specs=[SMEM]...  10.4 us
  transfers between devices with their start and end apart: 35, of which 5 were waited for; matrix products, arithmetic and copies ran while one was open for 1% of the time, Pallas kernels for 2%

profile of v1, /device:TPU:25, one launch (start us, length us, event | category | flops | bytes accessed | tf_op | source)
XLA Modules:
  0.0 147.5 jit_solution(9952702252194032120)
XLA Ops:
  0.0 1.3 collective-permute-start.5
  1.3 2.1 %collective-permute-start.10 = (bf16[80,128,128]{2,1,0:T(8,128)(2,1)}, bf16[80,128,128]{2,1,0:T(8,128)(2,1)}, u32[]{:S(2)}, u32[]{:S(2)}) collective-permute-start(bf16[80,128,128]{2,1,0:T(8,128)(2,1)} %bitcast.10), channel_id=1, source_target_pairs={{4,8},{5,9},{6,10},{7,11},{12,16},{13,17},{14,18},{15,19},{20,24},... | collective-permute-start | bytes 7864328 | tf_op jit(solution)/shard_map/ppermute | solution.py:161
  3.4 0.9 reshape.3
  4.4 0.7 pad_add_fusion.index.refs_2_.refs_1_
  5.1 1.7 %copy-done = bf16[1,1,80,128,128]{4,3,2,1,0:T(8,128)(2,1)S(1)} copy-done((bf16[1,1,80,128,128]{4,3,2,1,0:T(8,128)(2,1)S(1)}, bf16[1,1,80,128,128]{4,3,2,1,0:T(8,128)(2,1)}, u32[]{:S(2)}) %copy-start) | copy-done | bytes 2621464
  6.8 2.5 %head.1.refs_10_ = bf16[17,32,128]{2,1,0:T(8,128)(2,1)S(1)} custom-call(s32[2]{0:T(128)S(1)} %pad_add_fusion.1.pos.refs_0_, s32[2,80]{1,0:T(2,128)S(1)} %pad_add_fusion.index.refs_2_.refs_1_, bf16[80,128,128]{2,1,0:T(8,128)(2,1)S(1)} %bitcast.11, f32[4,32,128]{2,1,0:T(8,128)S(1)} %bitcast.20), custom_call_target="tpu_custom_call" | custom-call | tf_op jit(solution)/shard_map/head/pallas_call | solution.py:171
  9.3 0.7 collective-permute-start.4
  10.0 1.3 collective-permute-start
  11.3 0.7 collective-permute-start.3
  12.0 1.1 collective-permute-done.refs_1_
  13.7 0.7 collective-permute-start.1
  15.1 0.7 collective-permute-start.6
  15.8 0.7 collective-permute-start.9
  16.5 0.7 collective-permute-start.8
  17.2 0.7 collective-permute-start.7
  17.9 1.8 %step.8 = (bf16[49,32,128]{2,1,0:T(8,128)(2,1)S(1)}, bf16[17,32,128]{2,1,0:T(8,128)(2,1)S(1)}) custom-call(s32[2]{0:T(128)S(1)} %pad_add_fusion.1.pos.refs_0_, s32[2,80]{1,0:T(2,128)S(1)} %collective-permute-done.refs_1_, s32[2,80]{1,0:T(2,128)S(1)} %pad_add_fusion.index.refs_2_.refs_1_, bf16[49,32,128]{2,1,0:T(8,128)(2,1)S(1)} %collective-permute-done.6.refs_3_, ...), custom_call_target="tpu_custom_call" | custom-call | tf_op jit(solution)/shard_map/step/pallas_call | solution.py:214
  19.7 0.7 collective-permute-start.11
  20.4 0.7 collective-permute-start.14
  21.1 0.7 collective-permute-start.13
  21.8 0.7 collective-permute-start.12
  23.1 0.7 collective-permute-start.15
  23.8 0.7 collective-permute-start.18
  24.5 0.7 collective-permute-start.17
  25.2 0.7 collective-permute-start.16
  25.9 1.8 %step.10 = (bf16[49,32,128]{2,1,0:T(8,128)(2,1)S(1)}, bf16[17,32,128]{2,1,0:T(8,128)(2,1)S(1)}) custom-call(s32[2]{0:T(128)S(1)} %pad_add_fusion.1.pos.refs_0_, s32[2,80]{1,0:T(2,128)S(1)} %collective-permute-done.refs_1_, s32[2,80]{1,0:T(2,128)S(1)} %pad_add_fusion.index.refs_2_.refs_1_, bf16[49,32,128]{2,1,0:T(8,128)(2,1)S(1)} %collective-permute-done.15.refs_3_, ...), custom_call_target="tpu_custom_call" | custom-call | tf_op jit(solution)/shard_map/step/pallas_call | solution.py:214
  27.7 0.7 collective-permute-start.19
  28.4 0.7 collective-permute-start.22
  29.1 0.7 collective-permute-start.21
  29.7 0.7 collective-permute-start.20
  30.5 0.8 step.11
  31.3 0.7 collective-permute-start.23
  32.0 0.7 collective-permute-start.26
  32.6 0.7 collective-permute-start.25
  33.3 0.7 collective-permute-start.24
  34.0 1.8 %step.12 = (bf16[49,32,128]{2,1,0:T(8,128)(2,1)S(1)}, bf16[17,32,128]{2,1,0:T(8,128)(2,1)S(1)}) custom-call(s32[2]{0:T(128)S(1)} %pad_add_fusion.1.pos.refs_0_, s32[2,80]{1,0:T(2,128)S(1)} %collective-permute-done.refs_1_, s32[2,80]{1,0:T(2,128)S(1)} %pad_add_fusion.index.refs_2_.refs_1_, bf16[49,32,128]{2,1,0:T(8,128)(2,1)S(1)} %collective-permute-done.23.refs_3_, ...), custom_call_target="tpu_custom_call" | custom-call | tf_op jit(solution)/shard_map/step/pallas_call | solution.py:214
  35.8 1.3 collective-permute-start.27
  37.1 1.3 collective-permute-start.30
  38.4 1.3 collective-permute-start.29
  39.7 1.3 collective-permute-start.28
  41.0 84.5 %collective-permute-done.30.refs_6_ = bf16[17,32,128]{2,1,0:T(8,128)(2,1)S(1)} collective-permute-done((bf16[17,32,128]{2,1,0:T(8,128)(2,1)S(1)}, bf16[17,32,128]{2,1,0:T(8,128)(2,1)S(1)}, u32[]{:S(2)}, u32[]{:S(2)}) %collective-permute-start.30) | collective-permute-done | bytes 139296 | tf_op jit(solution)/shard_map/ppermute | solution.py:161
  125.5 3.2 %collective-permute-done.29.refs_5_ = bf16[17,32,128]{2,1,0:T(8,128)(2,1)S(1)} collective-permute-done((bf16[17,32,128]{2,1,0:T(8,128)(2,1)S(1)}, bf16[17,32,128]{2,1,0:T(8,128)(2,1)S(1)}, u32[]{:S(2)}, u32[]{:S(2)}) %collective-permute-start.29) | collective-permute-done | bytes 139296 | tf_op jit(solution)/shard_map/ppermute | solution.py:161
  128.7 3.0 %step.13 = (bf16[49,32,128]{2,1,0:T(8,128)(2,1)S(1)}, bf16[17,32,128]{2,1,0:T(8,128)(2,1)S(1)}) custom-call(s32[2]{0:T(128)S(1)} %pad_add_fusion.1.pos.refs_0_, s32[2,80]{1,0:T(2,128)S(1)} %collective-permute-done.refs_1_, s32[2,80]{1,0:T(2,128)S(1)} %pad_add_fusion.index.refs_2_.refs_1_, bf16[49,32,128]{2,1,0:T(8,128)(2,1)S(1)} %collective-permute-done.27.refs_3_, ...), custom_call_target="tpu_custom_call" | custom-call | tf_op jit(solution)/shard_map/step/pallas_call | solution.py:214
  131.7 1.3 collective-permute-start.34
  133.0 2.9 %collective-permute-start.33 = (bf16[17,32,128]{2,1,0:T(8,128)(2,1)S(1)}, bf16[17,32,128]{2,1,0:T(8,128)(2,1)S(1)}, u32[]{:S(2)}, u32[]{:S(2)}) collective-permute-start(bf16[17,32,128]{2,1,0:T(8,128)(2,1)S(1)} %get-tuple-element.31.refs_2_), channel_id=1, source_target_pairs={{28,31},{29,28},{30,29},{31,30}} | collective-permute-start | bytes 417800 | tf_op jit(solution)/shard_map/ppermute | solution.py:161
  135.9 2.7 %collective-permute-start.32 = (bf16[17,32,128]{2,1,0:T(8,128)(2,1)S(1)}, bf16[17,32,128]{2,1,0:T(8,128)(2,1)S(1)}, u32[]{:S(2)}, u32[]{:S(2)}) collective-permute-start(bf16[17,32,128]{2,1,0:T(8,128)(2,1)S(1)} %get-tuple-element.31.refs_2_), channel_id=1, source_target_pairs={{28,30},{29,31},{30,28},{31,29}} | collective-permute-start | bytes 417800 | tf_op jit(solution)/shard_map/ppermute | solution.py:161
  138.7 2.4 %collective-permute-start.31 = (bf16[17,32,128]{2,1,0:T(8,128)(2,1)S(1)}, bf16[17,32,128]{2,1,0:T(8,128)(2,1)S(1)}, u32[]{:S(2)}, u32[]{:S(2)}) collective-permute-start(bf16[17,32,128]{2,1,0:T(8,128)(2,1)S(1)} %get-tuple-element.31.refs_2_), channel_id=1, source_target_pairs={{28,29},{29,30},{30,31},{31,28}} | collective-permute-start | bytes 417800 | tf_op jit(solution)/shard_map/ppermute | solution.py:161
  141.7 3.7 %collective-permute-done.31.refs_3_ = bf16[17,32,128]{2,1,0:T(8,128)(2,1)S(1)} collective-permute-done((bf16[17,32,128]{2,1,0:T(8,128)(2,1)S(1)}, bf16[17,32,128]{2,1,0:T(8,128)(2,1)S(1)}, u32[]{:S(2)}, u32[]{:S(2)}) %collective-permute-start.31) | collective-permute-done | bytes 139296 | tf_op jit(solution)/shard_map/ppermute | solution.py:161
  145.4 2.2 %last.1 = bf16[4,8,4096]{2,1,0:T(8,128)(2,1)} custom-call(s32[2]{0:T(128)S(1)} %pad_add_fusion.1.pos.refs_0_, s32[2,80]{1,0:T(2,128)S(1)} %pad_add_fusion.index.refs_2_.refs_1_, bf16[17,32,128]{2,1,0:T(8,128)(2,1)S(1)} %get-tuple-element.31.refs_2_, bf16[17,32,128]{2,1,0:T(8,128)(2,1)S(1)} %collective-permute-done.31.refs_3_, ...), custom_call_target="tpu_custom_call" | custom-call | tf_op jit(solution)/shard_map/last/pallas_call | solution.py:230
  (38 shorter events, 2.8 us)
Async XLA Ops:
  0.0 14.4 %collective-permute-start.5 = (bf16[80,128,128]{2,1,0:T(8,128)(2,1)}, bf16[80,128,128]{2,1,0:T(8,128)(2,1)S(1)}, u32[]{:S(2)}, u32[]{:S(2)}) collective-permute-start(bf16[80,128,128]{2,1,0:T(8,128)(2,1)} %bitcast.9), channel_id=1, source_target_pairs={{0,4},{1,5},{2,6},{3,7},{8,12},{9,13},{10,14},{11,15},{16,20},{17,... | collective-permute-start | bytes 7864328 | tf_op jit(solution)/shard_map/ppermute | solution.py:161
  1.3 16.6 %collective-permute-start.10 = (bf16[80,128,128]{2,1,0:T(8,128)(2,1)}, bf16[80,128,128]{2,1,0:T(8,128)(2,1)}, u32[]{:S(2)}, u32[]{:S(2)}) collective-permute-start(bf16[80,128,128]{2,1,0:T(8,128)(2,1)} %bitcast.10), channel_id=1, source_target_pairs={{4,8},{5,9},{6,10},{7,11},{12,16},{13,17},{14,18},{15,19},{20,24},... | collective-permute-start | bytes 7864328 | tf_op jit(solution)/shard_map/ppermute | solution.py:161
  5.1 1.7 %copy-start = (bf16[1,1,80,128,128]{4,3,2,1,0:T(8,128)(2,1)S(1)}, bf16[1,1,80,128,128]{4,3,2,1,0:T(8,128)(2,1)}, u32[]{:S(2)}) copy-start(bf16[1,1,80,128,128]{4,3,2,1,0:T(8,128)(2,1)} %param.4) | copy-start | bytes 7864324
  9.3 4.4 %collective-permute-start.4 = (bf16[17,32,128]{2,1,0:T(8,128)(2,1)S(1)}, bf16[17,32,128]{2,1,0:T(8,128)(2,1)S(1)}, u32[]{:S(2)}, u32[]{:S(2)}) collective-permute-start(bf16[17,32,128]{2,1,0:T(8,128)(2,1)S(1)} %head.1.refs_10_), channel_id=1, source_target_pairs={{0,7},{1,4},{2,5},{3,6}} | collective-permute-start | bytes 417800 | tf_op jit(solution)/shard_map/ppermute | solution.py:161
  10.0 3.0 %collective-permute-start = (s32[2,80]{1,0:T(2,128)S(1)}, s32[2,80]{1,0:T(2,128)S(1)}, u32[]{:S(2)}, u32[]{:S(2)}) collective-permute-start(s32[2,80]{1,0:T(2,128)S(1)} %pad_add_fusion.index.refs_2_.refs_1_), channel_id=1, source_target_pairs={{0,4},{1,5},{2,6},{3,7},{4,8},{5,9},{6,10},{7,11},{8,12},{9,13},{1... | collective-permute-start | bytes 1928 | tf_op jit(solution)/shard_map/ppermute | solution.py:161
  11.3 3.1 %collective-permute-start.3 = (bf16[17,32,128]{2,1,0:T(8,128)(2,1)S(1)}, bf16[17,32,128]{2,1,0:T(8,128)(2,1)S(1)}, u32[]{:S(2)}, u32[]{:S(2)}) collective-permute-start(bf16[17,32,128]{2,1,0:T(8,128)(2,1)S(1)} %head.1.refs_10_), channel_id=1, source_target_pairs={{0,6},{1,7},{2,4},{3,5}} | collective-permute-start | bytes 417800 | tf_op jit(solution)/shard_map/ppermute | solution.py:161
  13.1 1.4 collective-permute-start.2
  13.7 0.7 collective-permute-start.1
  15.1 2.8 %collective-permute-start.6 = (bf16[49,32,128]{2,1,0:T(8,128)(2,1)S(1)}, bf16[49,32,128]{2,1,0:T(8,128)(2,1)S(1)}, u32[]{:S(2)}, u32[]{:S(2)}) collective-permute-start(bf16[49,32,128]{2,1,0:T(8,128)(2,1)S(1)} %get-tuple-element.19.refs_11_), channel_id=1, source_target_pairs={{4,8},{5,9},{6,10},{7,11}} | collective-permute-start | bytes 1204232 | tf_op jit(solution)/shard_map/ppermute | solution.py:161
  15.8 2.0 %collective-permute-start.9 = (bf16[17,32,128]{2,1,0:T(8,128)(2,1)S(1)}, bf16[17,32,128]{2,1,0:T(8,128)(2,1)S(1)}, u32[]{:S(2)}, u32[]{:S(2)}) collective-permute-start(bf16[17,32,128]{2,1,0:T(8,128)(2,1)S(1)} %get-tuple-element.20), channel_id=1, source_target_pairs={{4,11},{5,8},{6,9},{7,10}} | collective-permute-start | bytes 417800 | tf_op jit(solution)/shard_map/ppermute | solution.py:161
  16.5 1.4 collective-permute-start.8
  17.2 0.7 collective-permute-start.7
  19.7 2.8 %collective-permute-start.11 = (bf16[49,32,128]{2,1,0:T(8,128)(2,1)S(1)}, bf16[49,32,128]{2,1,0:T(8,128)(2,1)S(1)}, u32[]{:S(2)}, u32[]{:S(2)}) collective-permute-start(bf16[49,32,128]{2,1,0:T(8,128)(2,1)S(1)} %get-tuple-element.21.refs_11_), channel_id=1, source_target_pairs={{8,12},{9,13},{10,14},{11,15}} | collective-permute-start | bytes 1204232 | tf_op jit(solution)/shard_map/ppermute | solution.py:161
  20.4 2.0 %collective-permute-start.14 = (bf16[17,32,128]{2,1,0:T(8,128)(2,1)S(1)}, bf16[17,32,128]{2,1,0:T(8,128)(2,1)S(1)}, u32[]{:S(2)}, u32[]{:S(2)}) collective-permute-start(bf16[17,32,128]{2,1,0:T(8,128)(2,1)S(1)} %get-tuple-element.22), channel_id=1, source_target_pairs={{8,15},{9,12},{10,13},{11,14}} | collective-permute-start | bytes 417800 | tf_op jit(solution)/shard_map/ppermute | solution.py:161
  21.1 1.4 collective-permute-start.13
  21.8 0.7 collective-permute-start.12
  23.1 2.8 %collective-permute-start.15 = (bf16[49,32,128]{2,1,0:T(8,128)(2,1)S(1)}, bf16[49,32,128]{2,1,0:T(8,128)(2,1)S(1)}, u32[]{:S(2)}, u32[]{:S(2)}) collective-permute-start(bf16[49,32,128]{2,1,0:T(8,128)(2,1)S(1)} %get-tuple-element.23.refs_11_), channel_id=1, source_target_pairs={{12,16},{13,17},{14,18},{15,19}} | collective-permute-start | bytes 1204232 | tf_op jit(solution)/shard_map/ppermute | solution.py:161
  23.8 2.0 %collective-permute-start.18 = (bf16[17,32,128]{2,1,0:T(8,128)(2,1)S(1)}, bf16[17,32,128]{2,1,0:T(8,128)(2,1)S(1)}, u32[]{:S(2)}, u32[]{:S(2)}) collective-permute-start(bf16[17,32,128]{2,1,0:T(8,128)(2,1)S(1)} %get-tuple-element.24), channel_id=1, source_target_pairs={{12,19},{13,16},{14,17},{15,18}} | collective-permute-start | bytes 417800 | tf_op jit(solution)/shard_map/ppermute | solution.py:161
  24.5 1.4 collective-permute-start.17
  25.2 0.7 collective-permute-start.16
  27.7 2.8 %collective-permute-start.19 = (bf16[49,32,128]{2,1,0:T(8,128)(2,1)S(1)}, bf16[49,32,128]{2,1,0:T(8,128)(2,1)S(1)}, u32[]{:S(2)}, u32[]{:S(2)}) collective-permute-start(bf16[49,32,128]{2,1,0:T(8,128)(2,1)S(1)} %get-tuple-element.25.refs_11_), channel_id=1, source_target_pairs={{16,20},{17,21},{18,22},{19,23}} | collective-permute-start | bytes 1204232 | tf_op jit(solution)/shard_map/ppermute | solution.py:161
  28.4 2.0 %collective-permute-start.22 = (bf16[17,32,128]{2,1,0:T(8,128)(2,1)S(1)}, bf16[17,32,128]{2,1,0:T(8,128)(2,1)S(1)}, u32[]{:S(2)}, u32[]{:S(2)}) collective-permute-start(bf16[17,32,128]{2,1,0:T(8,128)(2,1)S(1)} %get-tuple-element.26), channel_id=1, source_target_pairs={{16,23},{17,20},{18,21},{19,22}} | collective-permute-start | bytes 417800 | tf_op jit(solution)/shard_map/ppermute | solution.py:161
  29.1 1.4 collective-permute-start.21
  29.7 0.7 collective-permute-start.20
  31.3 2.8 %collective-permute-start.23 = (bf16[49,32,128]{2,1,0:T(8,128)(2,1)S(1)}, bf16[49,32,128]{2,1,0:T(8,128)(2,1)S(1)}, u32[]{:S(2)}, u32[]{:S(2)}) collective-permute-start(bf16[49,32,128]{2,1,0:T(8,128)(2,1)S(1)} %get-tuple-element.27.refs_11_), channel_id=1, source_target_pairs={{20,24},{21,25},{22,26},{23,27}} | collective-permute-start | bytes 1204232 | tf_op jit(solution)/shard_map/ppermute | solution.py:161
  32.0 2.0 %collective-permute-start.26 = (bf16[17,32,128]{2,1,0:T(8,128)(2,1)S(1)}, bf16[17,32,128]{2,1,0:T(8,128)(2,1)S(1)}, u32[]{:S(2)}, u32[]{:S(2)}) collective-permute-start(bf16[17,32,128]{2,1,0:T(8,128)(2,1)S(1)} %get-tuple-element.28), channel_id=1, source_target_pairs={{20,27},{21,24},{22,25},{23,26}} | collective-permute-start | bytes 417800 | tf_op jit(solution)/shard_map/ppermute | solution.py:161
  32.6 1.4 collective-permute-start.25
  33.3 0.7 collective-permute-start.24
  35.8 92.9 %collective-permute-start.27 = (bf16[49,32,128]{2,1,0:T(8,128)(2,1)S(1)}, bf16[49,32,128]{2,1,0:T(8,128)(2,1)S(1)}, u32[]{:S(2)}, u32[]{:S(2)}) collective-permute-start(bf16[49,32,128]{2,1,0:T(8,128)(2,1)S(1)} %get-tuple-element.29.refs_11_), channel_id=1, source_target_pairs={{24,28},{25,29},{26,30},{27,31}} | collective-permute-start | bytes 1204232 | tf_op jit(solution)/shard_map/ppermute | solution.py:161
  37.1 88.4 %collective-permute-start.30 = (bf16[17,32,128]{2,1,0:T(8,128)(2,1)S(1)}, bf16[17,32,128]{2,1,0:T(8,128)(2,1)S(1)}, u32[]{:S(2)}, u32[]{:S(2)}) collective-permute-start(bf16[17,32,128]{2,1,0:T(8,128)(2,1)S(1)} %get-tuple-element.30), channel_id=1, source_target_pairs={{24,31},{25,28},{26,29},{27,30}} | collective-permute-start | bytes 417800 | tf_op jit(solution)/shard_map/ppermute | solution.py:161
  38.4 90.2 %collective-permute-start.29 = (bf16[17,32,128]{2,1,0:T(8,128)(2,1)S(1)}, bf16[17,32,128]{2,1,0:T(8,128)(2,1)S(1)}, u32[]{:S(2)}, u32[]{:S(2)}) collective-permute-start(bf16[17,32,128]{2,1,0:T(8,128)(2,1)S(1)} %get-tuple-element.30), channel_id=1, source_target_pairs={{24,30},{25,31},{26,28},{27,29}} | collective-permute-start | bytes 417800 | tf_op jit(solution)/shard_map/ppermute | solution.py:161
  39.7 88.9 %collective-permute-start.28 = (bf16[17,32,128]{2,1,0:T(8,128)(2,1)S(1)}, bf16[17,32,128]{2,1,0:T(8,128)(2,1)S(1)}, u32[]{:S(2)}, u32[]{:S(2)}) collective-permute-start(bf16[17,32,128]{2,1,0:T(8,128)(2,1)S(1)} %get-tuple-element.30), channel_id=1, source_target_pairs={{24,29},{25,30},{26,31},{27,28}} | collective-permute-start | bytes 417800 | tf_op jit(solution)/shard_map/ppermute | solution.py:161
  131.7 13.7 %collective-permute-start.34 = (bf16[49,32,128]{2,1,0:T(8,128)(2,1)S(1)}, bf16[49,32,128]{2,1,0:T(8,128)(2,1)S(1)}, u32[]{:S(2)}, u32[]{:S(2)}) collective-permute-start(bf16[49,32,128]{2,1,0:T(8,128)(2,1)S(1)} %get-tuple-element.32.refs_7_), channel_id=1, source_target_pairs={{4,0},{5,1},{6,2},{7,3},{8,4},{9,5},{10,6},{11,7},{12,8},{13,9},{1... | collective-permute-start | bytes 1204232 | tf_op jit(solution)/shard_map/ppermute | solution.py:161
  133.0 8.1 %collective-permute-start.33 = (bf16[17,32,128]{2,1,0:T(8,128)(2,1)S(1)}, bf16[17,32,128]{2,1,0:T(8,128)(2,1)S(1)}, u32[]{:S(2)}, u32[]{:S(2)}) collective-permute-start(bf16[17,32,128]{2,1,0:T(8,128)(2,1)S(1)} %get-tuple-element.31.refs_2_), channel_id=1, source_target_pairs={{28,31},{29,28},{30,29},{31,30}} | collective-permute-start | bytes 417800 | tf_op jit(solution)/shard_map/ppermute | solution.py:161
  135.9 5.8 %collective-permute-start.32 = (bf16[17,32,128]{2,1,0:T(8,128)(2,1)S(1)}, bf16[17,32,128]{2,1,0:T(8,128)(2,1)S(1)}, u32[]{:S(2)}, u32[]{:S(2)}) collective-permute-start(bf16[17,32,128]{2,1,0:T(8,128)(2,1)S(1)} %get-tuple-element.31.refs_2_), channel_id=1, source_target_pairs={{28,30},{29,31},{30,28},{31,29}} | collective-permute-start | bytes 417800 | tf_op jit(solution)/shard_map/ppermute | solution.py:161
  138.7 6.7 %collective-permute-start.31 = (bf16[17,32,128]{2,1,0:T(8,128)(2,1)S(1)}, bf16[17,32,128]{2,1,0:T(8,128)(2,1)S(1)}, u32[]{:S(2)}, u32[]{:S(2)}) collective-permute-start(bf16[17,32,128]{2,1,0:T(8,128)(2,1)S(1)} %get-tuple-element.31.refs_2_), channel_id=1, source_target_pairs={{28,29},{29,30},{30,31},{31,28}} | collective-permute-start | bytes 417800 | tf_op jit(solution)/shard_map/ppermute | solution.py:161

commit v2 on v0

v2 whole, which is shorter than its diff:
```python
import functools

import jax
import jax.numpy as jnp
from jax import lax
from jax.experimental import pallas as pl
from jax.experimental.pallas import tpu as pltpu
from jax.sharding import PartitionSpec as P

BS = 128
PIX = 4096
CB = PIX // BS
relaxation = 0.5

NN = (((1,), (0,)), ((), ()))
NT = (((1,), (1,)), ((), ()))
VMEM = pl.BlockSpec(memory_space=pltpu.VMEM)
SMEM = pl.BlockSpec(memory_space=pltpu.SMEM)
PARAMS = pltpu.CompilerParams(vmem_limit_bytes=20 * 2**20)


def dot(lhs, rhs, dims):
    return lax.dot_general(lhs, rhs, dims, preferred_element_type=jnp.float32)


def head_kernel(row_blocks, rows, cols, blocks, rays, note, table, seen):
    count = blocks.shape[2]
    each = count // row_blocks
    batches, per_batch, here = rays.shape
    quarter = here // BS
    half = note.shape[1]
    for r in range(row_blocks):
        seen[r] = r * each
    for n in range(count):
        row = rows[0, 0, n]
        at = seen[row]
        seen[row] = at + 1
        table[0, at] = n
        table[1, at] = cols[0, 0, n]
    group = half // per_batch
    for h in range(2):
        for i in range(quarter):
            parts = [rays[h * group + g, :, i * BS : (i + 1) * BS] for g in range(group)]
            note[h * quarter + i] = jnp.concatenate(parts, axis=0)
    ones = jnp.ones((16, BS), jnp.bfloat16)
    for r in range(row_blocks):
        squares = 0.0
        for k in range(each):
            block = blocks[0, 0, table[0, r * each + k]].astype(jnp.float32)
            squares = squares + block * block
        total = 0.0
        for _ in range(3):
            part = squares.astype(jnp.bfloat16)
            total = total + dot(ones, part, NT)
            squares = squares - part.astype(jnp.float32)
        note[2 * quarter, r : r + 1] = total[0:1]


def weights(core, note, terms, w_scr):
    tiles, slabs, _, _ = note.shape
    quarter = (slabs - 1) // 2
    row_blocks = w_scr.shape[0]
    norms = note[0, slabs - 1, 0:row_blocks]
    for t in range(1, tiles):
        norms = norms + note[t, slabs - 1, 0:row_blocks]
    scale = relaxation / norms
    for r in range(row_blocks):
        left = note[r // quarter, core * quarter + r % quarter]
        if terms is not None:
            total = terms[0, r].astype(jnp.float32)
            for t in range(1, tiles):
                total = total + terms[t, r].astype(jnp.float32)
            left = left - total
        w_scr[r] = (left * scale[r : r + 1]).astype(jnp.bfloat16)


def back_project(table, blocks, w_scr, image):
    row_blocks = w_scr.shape[0]
    count = blocks.shape[2]
    each = count // row_blocks
    for k in range(count):
        col = table[1, k]
        image[col] = image[col] + dot(w_scr[k // each], blocks[0, 0, table[0, k]], NN)


def project(table, blocks, image, terms):
    row_blocks = terms.shape[0]
    each = blocks.shape[2] // row_blocks
    for r in range(row_blocks):
        total = 0.0
        for k in range(r * each, (r + 1) * each):
            total = total + dot(image[table[1, k]], blocks[0, 0, table[0, k]], NT)
        terms[r] = total.astype(jnp.bfloat16)


def on_core(pos, place, run, own, other):
    active = pos[0] == place

    @pl.when(jnp.logical_and(active, pos[1] == 0))
    def _():
        run(own, other)

    @pl.when(jnp.logical_and(active, pos[1] == 1))
    def _():
        run(other, own)

    return active


def first_kernel(place, has_image, *refs):
    refs = list(refs)
    pos, table, table2, note, note2, blocks, blocks2 = refs[:7]
    refs = refs[7:]
    terms_in, image_in = None, None
    if has_image:
        terms_in, image_in = refs[:2]
        refs = refs[2:]
    image, shot, terms, w_scr = refs

    def run(first, second):
        weights(pos[1], first[1], terms_in, w_scr)
        if has_image:
            image[...] = image_in[...].astype(jnp.float32)
        else:
            image[...] = jnp.zeros_like(image)
        back_project(first[0], first[2], w_scr, image)
        shot[...] = image[...].astype(jnp.bfloat16)
        project(second[0], second[2], shot, terms)

    on_core(pos, place, run, (table, note, blocks), (table2, note2, blocks2))


def second_kernel(place, *refs):
    pos, table, table2, note, note2, blocks, blocks2 = refs[:7]
    terms_in, image_in, shot, kept_in, given_in = refs[7:12]
    image, kept, given, w_scr, x_scr = refs[12:]

    def run(first, second):
        weights(pos[1], second[1], terms_in, w_scr)
        x_scr[...] = image_in[...]
        back_project(second[0], second[2], w_scr, x_scr)
        out = x_scr[...].astype(jnp.bfloat16)
        image[...] = out

        @pl.when(pos[1] == 0)
        def _():
            kept[...] = shot[...]
            given[...] = out

        @pl.when(pos[1] == 1)
        def _():
            kept[...] = out
            given[...] = shot[...]

    active = on_core(pos, place, run, (table, note, blocks), (table2, note2, blocks2))

    @pl.when(jnp.logical_not(active))
    def _():
        kept[...] = kept_in[...]
        given[...] = given_in[...]


def project_kernel(place, pos, table, table2, image, blocks, blocks2, terms):
    def run(first, second):
        project(first[0], first[1], image, terms)

    on_core(pos, place, run, (table, blocks), (table2, blocks2))


def last_kernel(pos, kept, given, images):
    batches, per_batch, _ = images.shape
    half = kept.shape[1]
    group = half // per_batch

    def write(refs):
        for c in range(CB):
            for h in range(2):
                value = refs[h][c].astype(jnp.float32).reshape(group, per_batch, BS)
                where = slice(h * group, (h + 1) * group)
                images[where, :, c * BS : (c + 1) * BS] = value.astype(jnp.bfloat16)

    @pl.when(pos[1] == 0)
    def _():
        write((kept, given))

    @pl.when(pos[1] == 1)
    def _():
        write((given, kept))


def per_device(blocks, block_rows, block_cols, sinogram):
    batches, per_batch, here = sinogram.shape
    half = batches * per_batch // 2
    quarter = here // BS
    count = blocks.shape[2]
    subsets = lax.axis_size("subset")
    tiles = lax.axis_size("tile")
    row_blocks = quarter * tiles
    places = subsets // 2
    subset = lax.axis_index("subset")
    pos = jnp.stack([subset // 2, subset % 2]).astype(jnp.int32)

    image_shape = (CB, half, BS)
    image_out = jax.ShapeDtypeStruct(image_shape, jnp.bfloat16)
    terms_out = jax.ShapeDtypeStruct((row_blocks, half, BS), jnp.bfloat16)
    w_scr = pltpu.VMEM((row_blocks, half, BS), jnp.bfloat16)
    x_scr = pltpu.VMEM(image_shape, jnp.float32)

    def swapped(value):
        return lax.ppermute(value, "subset", [(s, s ^ 1) for s in range(subsets)])

    def call(kernel, smem, operands, out_shape, scratch, name):
        many = isinstance(out_shape, tuple)
        return pl.pallas_call(
            kernel,
            out_shape=out_shape,
            in_specs=[SMEM] * smem + [VMEM] * (len(operands) - smem),
            out_specs=(VMEM,) * len(out_shape) if many else VMEM,
            scratch_shapes=scratch,
            compiler_params=PARAMS,
            name=name,
        )(*operands)

    blocks2 = swapped(blocks)
    note, table = pl.pallas_call(
        functools.partial(head_kernel, row_blocks),
        out_shape=(
            jax.ShapeDtypeStruct((2 * quarter + 1, half, BS), jnp.float32),
            jax.ShapeDtypeStruct((2, count), jnp.int32),
        ),
        in_specs=[SMEM, SMEM, VMEM, VMEM],
        out_specs=(VMEM, SMEM),
        scratch_shapes=[pltpu.SMEM((row_blocks,), jnp.int32)],
        compiler_params=PARAMS,
        name="head",
    )(block_rows, block_cols, blocks, sinogram)
    table2 = swapped(table)
    note = lax.all_gather(note, "tile")
    note2 = swapped(note)

    kept = jnp.zeros(image_shape, jnp.bfloat16)
    given = kept
    image = None
    for place in range(places):
        fixed = [pos, table, table2, note, note2, blocks, blocks2]
        extra = []
        if place > 0:
            pairs = [(2 * place - 2 + c, 2 * place + c) for c in range(2)]
            image = lax.ppermute(image, "subset", pairs)
            terms = call(
                functools.partial(project_kernel, place),
                3,
                [pos, table, table2, image, blocks, blocks2],
                terms_out,
                [],
                "project",
            )
            extra = [lax.all_gather(terms, "tile"), image]
        image32, shot, terms = call(
            functools.partial(first_kernel, place, place > 0),
            3,
            fixed + extra,
            (jax.ShapeDtypeStruct(image_shape, jnp.float32), image_out, terms_out),
            [w_scr],
            "first",
        )
        terms = lax.all_gather(terms, "tile")
        image, kept, given = call(
            functools.partial(second_kernel, place),
            3,
            fixed + [terms, image32, shot, kept, given],
            (image_out, image_out, image_out),
            [w_scr, x_scr],
            "second",
        )
    images = call(
        last_kernel,
        1,
        [pos, kept, swapped(given)],
        jax.ShapeDtypeStruct((batches, per_batch, PIX), jnp.bfloat16),
        [],
        "last",
    )
    return images[None]


def solution(mesh):
    in_specs = (
        P("subset", "tile", None, None, None),
        P("subset", "tile", None),
        P("subset", "tile", None),
        P(None, None, ("subset", "tile")),
    )
    out_specs = P("subset", None, None, "tile")
    return jax.shard_map(
        per_device, mesh=mesh, in_specs=in_specs, out_specs=out_specs, check_vma=False
    )
```

time: 295 us -> 132 us (0.45); the launches traced: 291 us -> 131 us
  blocking collectives: 140 us -> 54.2 us
  waiting for transfers between devices: 97.3 us -> 22.6 us
  Pallas kernels: 0 us -> 28.5 us
  matrix products: 11.9 us -> 0 us
  local copies, waits for them, and re-layouts: 15.7 us -> 3.91 us
  other arithmetic: 11 us -> 0.07 us
  starting transfers between devices: 14.1 us -> 21.7 us
    psum x12 -> x0, blocking collectives: 133 us -> none  [the longest x11 125 us: advance(): lax.psum(local_terms.astype(jnp.bfloat16), 'tile').astype(jnp.float32)]
    ppermute x11 -> x7, waiting for transfers between devices: 97.3 us -> 22.6 us  [the longest x3 20.6 us: per_device(): image = lax.ppermute(image, 'subset', pairs)]
    all_gather x1 -> x8, blocking collectives: 6.03 us -> 54.2 us  [the longest x4 29.3 us: per_device(): terms = lax.all_gather(terms, 'tile')]
    pallas_call x0 -> x13, Pallas kernels: none -> 28.5 us  [the longest x12 26.5 us: call(): pl.pallas_call(kernel, out_shape=out_shape, in_specs=[SMEM] * smem + [VME...]
    dot_general x17 -> x0, matrix products: 11.9 us -> none  [the longest x4 5.77 us: forward(): jnp.einsum('mnq,nbq->mnb', gathered, block_vals, preferred_element_type=j...]
    dynamic_slice x11 -> x0, local copies, waits for them, and re-layouts: 9.32 us -> none  [advance(): previous = lax.dynamic_index_in_dim(images_out, clamped, 0, keepdims=False)]
    ppermute x11 -> x7, starting transfers between devices: 14.1 us -> 21.7 us  [the longest x4 19.1 us: swapped(): return lax.ppermute(value, 'subset', [(s, s ^ 1) for s in range(subsets)])]
    dynamic_update_slice x11 -> x0, other arithmetic: 7.23 us -> none  [advance(): lax.dynamic_update_index_in_dim(images_out, written, clamped, 0)]
  transfers between devices with their start and end apart: 11 -> 7, of which waited for: 11 -> 3; matrix products, arithmetic and copies ran while one was open for 0% -> 0% of each run, Pallas kernels for 0% -> 2%
where the time goes in v2:
time: 132 us; the launch traced here: 131 us
  blocking collectives  54.2 us (41%)
  Pallas kernels  28.5 us (22%)
  waiting for transfers between devices  22.6 us (17%)
  starting transfers between devices  21.7 us (16%)
  local copies, waits for them, and re-layouts  3.91 us (3%)
    all_gather x4, blocking collectives, per_device(): terms = lax.all_gather(terms, 'tile')  29.3 us
    pallas_call x12, Pallas kernels, call(): pl.pallas_call(kernel, out_shape=out_shape, in_specs=[SMEM] * smem + [VME...  26.5 us
    ppermute x3, waiting for transfers between devices, per_device(): image = lax.ppermute(image, 'subset', pairs)  20.6 us
    ppermute x4, starting transfers between devices, swapped(): return lax.ppermute(value, 'subset', [(s, s ^ 1) for s in range(subsets)])  19.1 us
    all_gather x3, blocking collectives, per_device(): extra = [lax.all_gather(terms, 'tile'), image]  17.7 us
    all_gather x1, blocking collectives, per_device(): note = lax.all_gather(note, 'tile')  7.11 us
    unnamed x10, local copies, waits for them, and re-layouts  3.89 us
  transfers between devices with their start and end apart: 7, of which 3 were waited for; matrix products, arithmetic and copies ran while one was open for 0% of the time, Pallas kernels for 2%

profile of v2, /device:TPU:25, one launch (start us, length us, event | category | flops | bytes accessed | tf_op | source)
XLA Modules:
  0.0 131.1 jit_solution(6671388195535162444)
XLA Ops:
  0.0 0.7 collective-permute-start.2
  0.7 0.0 copy-start
  0.7 1.7 %copy-done = bf16[1,1,80,128,128]{4,3,2,1,0:T(8,128)(2,1)S(1)} copy-done((bf16[1,1,80,128,128]{4,3,2,1,0:T(8,128)(2,1)S(1)}, bf16[1,1,80,128,128]{4,3,2,1,0:T(8,128)(2,1)}, u32[]{:S(2)}) %copy-start) | copy-done | bytes 2621464
  2.4 0.0 copy-start.2
  2.4 0.8 copy-done.2
  3.3 0.0 copy-start.3
  3.3 0.7 copy-done.3
  3.9 0.0 copy-start.4
  3.9 0.7 copy-done.4
  4.6 0.0 copy-start.1
  4.6 2.1 %head.1 = (f32[9,16,128]{2,1,0:T(8,128)S(1)}, s32[2,80]{1,0:T(2,128)S(1)}) custom-call(s32[1,1,80]{2,1,0:T(1,128)S(1)} %copy-done.3, s32[1,1,80]{2,1,0:T(1,128)S(1)} %copy-done.4, bf16[1,1,80,128,128]{4,3,2,1,0:T(8,128)(2,1)S(1)} %copy-done, f32[4,8,512]{2,1,0:T(8,128)S(1)} %copy-done.2), custom_call_target="tpu_custom_call" | custom-call | tf_op jit(solution)/shard_map/head/pallas_call | solution.py:225
  6.6 7.1 %all-gather = f32[36,16,128]{2,1,0:T(8,128)S(1)} all-gather(f32[9,16,128]{2,1,0:T(8,128)S(1)} %get-tuple-element.31), channel_id=2, replica_groups=mesh['subset'=8,'tile'=4] {'tile'}, dimensions={0}, use_global_device_ids=true | all-gather | bytes 368640 | tf_op jit(solution)/shard_map/all_gather | solution.py:238
  13.8 2.0 %collective-permute-start.1 = (f32[4,9,16,128]{3,2,1,0:T(8,128)S(1)}, f32[4,9,16,128]{3,2,1,0:T(8,128)S(1)}, u32[]{:S(2)}, u32[]{:S(2)}) collective-permute-start(f32[4,9,16,128]{3,2,1,0:T(8,128)S(1)} %bitcast.11), channel_id=1, source_target_pairs={{0,4},{4,0},{8,12},{12,8},{16,20},{20,16},{24,28},{28,24},{1,5},{5... | collective-permute-start | bytes 884744 | tf_op jit(solution)/shard_map/ppermute | solution.py:210
  15.8 0.1 collective-permute-start
  15.8 0.1 pad_add_fusion.refs_0_.pos
  15.9 1.1 collective-permute-done.refs_2_.table2
  17.0 0.0 collective-permute-done.1.refs_4_
  17.0 0.0 collective-permute-done.2.refs_6_.blocks2
  17.0 0.0 copy-done.1
  17.0 1.8 %first.4 = (f32[32,16,128]{2,1,0:T(8,128)S(1)}, bf16[32,16,128]{2,1,0:T(8,128)(2,1)S(1)}, bf16[16,16,128]{2,1,0:T(8,128)(2,1)S(1)}) custom-call(s32[2]{0:T(128)S(1)} %pad_add_fusion.refs_0_.pos, s32[2,80]{1,0:T(2,128)S(1)} %get-tuple-element.30.refs_1_.table, s32[2,80]{1,0:T(2,128)S(1)} %collective-permute-done.refs_2_.table2, ...), custom_call_target="tpu_custom_call" | custom-call | tf_op jit(solution)/shard_map/first/pallas_call | solution.py:214
  18.8 7.0 %all-gather.1 = bf16[64,16,128]{2,1,0:T(8,128)(2,1)S(1)} all-gather(bf16[16,16,128]{2,1,0:T(8,128)(2,1)S(1)} %get-tuple-element.32), channel_id=3, replica_groups=mesh['subset'=8,'tile'=4] {'tile'}, dimensions={0}, use_global_device_ids=true | all-gather | bytes 327680 | tf_op jit(solution)/shard_map/all_gather | solution.py:267
  25.8 1.8 %second.4 = (bf16[32,16,128]{2,1,0:T(8,128)(2,1)S(1)}, bf16[32,16,128]{2,1,0:T(8,128)(2,1)S(1)}, bf16[32,16,128]{2,1,0:T(8,128)(2,1)S(1)}) custom-call(s32[2]{0:T(128)S(1)} %pad_add_fusion.refs_0_.pos, s32[2,80]{1,0:T(2,128)S(1)} %get-tuple-element.30.refs_1_.table, s32[2,80]{1,0:T(2,128)S(1)} %collective-permute-done.refs_2_.table2, ...), custom_call_target="tpu_custom_call" | custom-call | tf_op jit(solution)/shard_map/second/pallas_call | solution.py:214
  27.6 0.7 collective-permute-start.3
  28.2 0.0 collective-permute-done.3.image.refs_8_
  28.2 1.8 %project.3 = bf16[16,16,128]{2,1,0:T(8,128)(2,1)S(1)} custom-call(s32[2]{0:T(128)S(1)} %pad_add_fusion.refs_0_.pos, s32[2,80]{1,0:T(2,128)S(1)} %get-tuple-element.30.refs_1_.table, s32[2,80]{1,0:T(2,128)S(1)} %collective-permute-done.refs_2_.table2, bf16[32,16,128]{2,1,0:T(8,128)(2,1)S(1)} %collective-permute-done.3.image.refs_8_, ...), custom_call_target="tpu_custom_call" | custom-call | tf_op jit(solution)/shard_map/project/pallas_call | solution.py:214
  30.0 6.0 %all-gather.2 = bf16[64,16,128]{2,1,0:T(8,128)(2,1)S(1)} all-gather(bf16[16,16,128]{2,1,0:T(8,128)(2,1)S(1)} %project.3), channel_id=4, replica_groups=mesh['subset'=8,'tile'=4] {'tile'}, dimensions={0}, use_global_device_ids=true | all-gather | bytes 327680 | tf_op jit(solution)/shard_map/all_gather | solution.py:258
  36.0 1.8 %first.5 = (f32[32,16,128]{2,1,0:T(8,128)S(1)}, bf16[32,16,128]{2,1,0:T(8,128)(2,1)S(1)}, bf16[16,16,128]{2,1,0:T(8,128)(2,1)S(1)}) custom-call(s32[2]{0:T(128)S(1)} %pad_add_fusion.refs_0_.pos, s32[2,80]{1,0:T(2,128)S(1)} %get-tuple-element.30.refs_1_.table, s32[2,80]{1,0:T(2,128)S(1)} %collective-permute-done.refs_2_.table2, ...), custom_call_target="tpu_custom_call" | custom-call | tf_op jit(solution)/shard_map/first/pallas_call | solution.py:214
  37.8 7.6 %all-gather.3 = bf16[64,16,128]{2,1,0:T(8,128)(2,1)S(1)} all-gather(bf16[16,16,128]{2,1,0:T(8,128)(2,1)S(1)} %get-tuple-element.36), channel_id=5, replica_groups=mesh['subset'=8,'tile'=4] {'tile'}, dimensions={0}, use_global_device_ids=true | all-gather | bytes 327680 | tf_op jit(solution)/shard_map/all_gather | solution.py:267
  45.4 2.0 %second.5 = (bf16[32,16,128]{2,1,0:T(8,128)(2,1)S(1)}, bf16[32,16,128]{2,1,0:T(8,128)(2,1)S(1)}, bf16[32,16,128]{2,1,0:T(8,128)(2,1)S(1)}) custom-call(s32[2]{0:T(128)S(1)} %pad_add_fusion.refs_0_.pos, s32[2,80]{1,0:T(2,128)S(1)} %get-tuple-element.30.refs_1_.table, s32[2,80]{1,0:T(2,128)S(1)} %collective-permute-done.refs_2_.table2, ...), custom_call_target="tpu_custom_call" | custom-call | tf_op jit(solution)/shard_map/second/pallas_call | solution.py:214
  47.4 0.7 collective-permute-start.4
  48.0 0.0 collective-permute-done.4.image.refs_8_
  48.1 1.8 %project.4 = bf16[16,16,128]{2,1,0:T(8,128)(2,1)S(1)} custom-call(s32[2]{0:T(128)S(1)} %pad_add_fusion.refs_0_.pos, s32[2,80]{1,0:T(2,128)S(1)} %get-tuple-element.30.refs_1_.table, s32[2,80]{1,0:T(2,128)S(1)} %collective-permute-done.refs_2_.table2, bf16[32,16,128]{2,1,0:T(8,128)(2,1)S(1)} %collective-permute-done.4.image.refs_8_, ...), custom_call_target="tpu_custom_call" | custom-call | tf_op jit(solution)/shard_map/project/pallas_call | solution.py:214
  49.8 5.7 %all-gather.4 = bf16[64,16,128]{2,1,0:T(8,128)(2,1)S(1)} all-gather(bf16[16,16,128]{2,1,0:T(8,128)(2,1)S(1)} %project.4), channel_id=6, replica_groups=mesh['subset'=8,'tile'=4] {'tile'}, dimensions={0}, use_global_device_ids=true | all-gather | bytes 327680 | tf_op jit(solution)/shard_map/all_gather | solution.py:258
  55.6 1.8 %first.6 = (f32[32,16,128]{2,1,0:T(8,128)S(1)}, bf16[32,16,128]{2,1,0:T(8,128)(2,1)S(1)}, bf16[16,16,128]{2,1,0:T(8,128)(2,1)S(1)}) custom-call(s32[2]{0:T(128)S(1)} %pad_add_fusion.refs_0_.pos, s32[2,80]{1,0:T(2,128)S(1)} %get-tuple-element.30.refs_1_.table, s32[2,80]{1,0:T(2,128)S(1)} %collective-permute-done.refs_2_.table2, ...), custom_call_target="tpu_custom_call" | custom-call | tf_op jit(solution)/shard_map/first/pallas_call | solution.py:214
  57.3 7.2 %all-gather.5 = bf16[64,16,128]{2,1,0:T(8,128)(2,1)S(1)} all-gather(bf16[16,16,128]{2,1,0:T(8,128)(2,1)S(1)} %get-tuple-element.42), channel_id=7, replica_groups=mesh['subset'=8,'tile'=4] {'tile'}, dimensions={0}, use_global_device_ids=true | all-gather | bytes 327680 | tf_op jit(solution)/shard_map/all_gather | solution.py:267
  64.6 1.8 %second.6 = (bf16[32,16,128]{2,1,0:T(8,128)(2,1)S(1)}, bf16[32,16,128]{2,1,0:T(8,128)(2,1)S(1)}, bf16[32,16,128]{2,1,0:T(8,128)(2,1)S(1)}) custom-call(s32[2]{0:T(128)S(1)} %pad_add_fusion.refs_0_.pos, s32[2,80]{1,0:T(2,128)S(1)} %get-tuple-element.30.refs_1_.table, s32[2,80]{1,0:T(2,128)S(1)} %collective-permute-done.refs_2_.table2, ...), custom_call_target="tpu_custom_call" | custom-call | tf_op jit(solution)/shard_map/second/pallas_call | solution.py:214
  66.4 1.3 collective-permute-start.5
  67.7 20.6 %collective-permute-done.5.image.refs_8_ = bf16[32,16,128]{2,1,0:T(8,128)(2,1)S(1)} collective-permute-done((bf16[32,16,128]{2,1,0:T(8,128)(2,1)S(1)}, bf16[32,16,128]{2,1,0:T(8,128)(2,1)S(1)}, u32[]{:S(2)}, u32[]{:S(2)}) %collective-permute-start.5) | collective-permute-done | bytes 131104 | tf_op jit(solution)/shard_map/ppermute | solution.py:249
  88.2 3.2 %project.5 = bf16[16,16,128]{2,1,0:T(8,128)(2,1)S(1)} custom-call(s32[2]{0:T(128)S(1)} %pad_add_fusion.refs_0_.pos, s32[2,80]{1,0:T(2,128)S(1)} %get-tuple-element.30.refs_1_.table, s32[2,80]{1,0:T(2,128)S(1)} %collective-permute-done.refs_2_.table2, bf16[32,16,128]{2,1,0:T(8,128)(2,1)S(1)} %collective-permute-done.5.image.refs_8_, ...), custom_call_target="tpu_custom_call" | custom-call | tf_op jit(solution)/shard_map/project/pallas_call | solution.py:214
  91.4 6.0 %all-gather.6 = bf16[64,16,128]{2,1,0:T(8,128)(2,1)S(1)} all-gather(bf16[16,16,128]{2,1,0:T(8,128)(2,1)S(1)} %project.5), channel_id=8, replica_groups=mesh['subset'=8,'tile'=4] {'tile'}, dimensions={0}, use_global_device_ids=true | all-gather | bytes 327680 | tf_op jit(solution)/shard_map/all_gather | solution.py:258
  97.5 4.3 %first.7 = (f32[32,16,128]{2,1,0:T(8,128)S(1)}, bf16[32,16,128]{2,1,0:T(8,128)(2,1)S(1)}, bf16[16,16,128]{2,1,0:T(8,128)(2,1)S(1)}) custom-call(s32[2]{0:T(128)S(1)} %pad_add_fusion.refs_0_.pos, s32[2,80]{1,0:T(2,128)S(1)} %get-tuple-element.30.refs_1_.table, s32[2,80]{1,0:T(2,128)S(1)} %collective-permute-done.refs_2_.table2, ...), custom_call_target="tpu_custom_call" | custom-call | tf_op jit(solution)/shard_map/first/pallas_call | solution.py:214
  101.7 7.6 %all-gather.7 = bf16[64,16,128]{2,1,0:T(8,128)(2,1)S(1)} all-gather(bf16[16,16,128]{2,1,0:T(8,128)(2,1)S(1)} %get-tuple-element.48), channel_id=9, replica_groups=mesh['subset'=8,'tile'=4] {'tile'}, dimensions={0}, use_global_device_ids=true | all-gather | bytes 327680 | tf_op jit(solution)/shard_map/all_gather | solution.py:267
  109.3 3.3 %second.7 = (bf16[32,16,128]{2,1,0:T(8,128)(2,1)}, bf16[32,16,128]{2,1,0:T(8,128)(2,1)S(1)}, bf16[32,16,128]{2,1,0:T(8,128)(2,1)S(1)}) custom-call(s32[2]{0:T(128)S(1)} %pad_add_fusion.refs_0_.pos, s32[2,80]{1,0:T(2,128)S(1)} %get-tuple-element.30.refs_1_.table, s32[2,80]{1,0:T(2,128)S(1)} %collective-permute-done.refs_2_.table2, ...), custom_call_target="tpu_custom_call" | custom-call | tf_op jit(solution)/shard_map/second/pallas_call | solution.py:214
  112.6 16.3 %collective-permute-start.6 = (bf16[32,16,128]{2,1,0:T(8,128)(2,1)S(1)}, bf16[32,16,128]{2,1,0:T(8,128)(2,1)S(1)}, u32[]{:S(2)}, u32[]{:S(2)}) collective-permute-start(bf16[32,16,128]{2,1,0:T(8,128)(2,1)S(1)} %get-tuple-element.54), channel_id=1, source_target_pairs={{0,4},{4,0},{8,12},{12,8},{16,20},{20,16},{24,28},{28,24},{1,5},{5... | collective-permute-start | bytes 393224 | tf_op jit(solution)/shard_map/ppermute | solution.py:210
  128.9 1.0 collective-permute-done.6.given
  129.8 1.3 last.1
  (1 shorter events, 0.0 us)
Async XLA Ops:
  0.0 17.0 %collective-permute-start.2 = (bf16[1,1,80,128,128]{4,3,2,1,0:T(8,128)(2,1)}, bf16[1,1,80,128,128]{4,3,2,1,0:T(8,128)(2,1)}, u32[]{:S(2)}, u32[]{:S(2)}) collective-permute-start(bf16[1,1,80,128,128]{4,3,2,1,0:T(8,128)(2,1)} %refs_5_.15), channel_id=1, source_target_pairs={{0,4},{4,0},{8,12},{12,8},{16,20},{20,16},{24,28},{28,24},{1,5},{5... | collective-permute-start | bytes 7864328 | tf_op jit(solution)/shard_map/ppermute | solution.py:210
  0.7 1.7 %copy-start = (bf16[1,1,80,128,128]{4,3,2,1,0:T(8,128)(2,1)S(1)}, bf16[1,1,80,128,128]{4,3,2,1,0:T(8,128)(2,1)}, u32[]{:S(2)}) copy-start(bf16[1,1,80,128,128]{4,3,2,1,0:T(8,128)(2,1)} %refs_5_.15) | copy-start | bytes 7864324
  2.4 0.8 copy-start.2
  3.3 0.7 copy-start.3
  3.9 0.7 copy-start.4
  4.6 12.4 %copy-start.1 = (bf16[1,1,80,128,128]{4,3,2,1,0:T(8,128)(2,1)S(1)}, bf16[1,1,80,128,128]{4,3,2,1,0:T(8,128)(2,1)}, u32[]{:S(2)}) copy-start(bf16[1,1,80,128,128]{4,3,2,1,0:T(8,128)(2,1)} %refs_5_.15) | copy-start | bytes 7864324
  13.8 3.2 %collective-permute-start.1 = (f32[4,9,16,128]{3,2,1,0:T(8,128)S(1)}, f32[4,9,16,128]{3,2,1,0:T(8,128)S(1)}, u32[]{:S(2)}, u32[]{:S(2)}) collective-permute-start(f32[4,9,16,128]{3,2,1,0:T(8,128)S(1)} %bitcast.11), channel_id=1, source_target_pairs={{0,4},{4,0},{8,12},{12,8},{16,20},{20,16},{24,28},{28,24},{1,5},{5... | collective-permute-start | bytes 884744 | tf_op jit(solution)/shard_map/ppermute | solution.py:210
  15.8 1.2 collective-permute-start
  27.6 0.7 collective-permute-start.3
  47.4 0.7 collective-permute-start.4
  66.4 21.9 %collective-permute-start.5 = (bf16[32,16,128]{2,1,0:T(8,128)(2,1)S(1)}, bf16[32,16,128]{2,1,0:T(8,128)(2,1)S(1)}, u32[]{:S(2)}, u32[]{:S(2)}) collective-permute-start(bf16[32,16,128]{2,1,0:T(8,128)(2,1)S(1)} %get-tuple-element.47), channel_id=1, source_target_pairs={{16,24},{20,28},{17,25},{21,29},{18,26},{22,30},{19,27},{23,31}} | collective-permute-start | bytes 393224 | tf_op jit(solution)/shard_map/ppermute | solution.py:249
  112.6 17.3 %collective-permute-start.6 = (bf16[32,16,128]{2,1,0:T(8,128)(2,1)S(1)}, bf16[32,16,128]{2,1,0:T(8,128)(2,1)S(1)}, u32[]{:S(2)}, u32[]{:S(2)}) collective-permute-start(bf16[32,16,128]{2,1,0:T(8,128)(2,1)S(1)} %get-tuple-element.54), channel_id=1, source_target_pairs={{0,4},{4,0},{8,12},{12,8},{16,20},{20,16},{24,28},{28,24},{1,5},{5... | collective-permute-start | bytes 393224 | tf_op jit(solution)/shard_map/ppermute | solution.py:210

commit v3 on v2

--- a/solution.py
+++ b/solution.py
@@ -12,6 +12,8 @@
 CB = PIX // BS
 relaxation = 0.5
 
+DIRECT = 4
+
 NN = (((1,), (0,)), ((), ()))
 NT = (((1,), (1,)), ((), ()))
 VMEM = pl.BlockSpec(memory_space=pltpu.VMEM)
@@ -23,12 +25,32 @@
     return lax.dot_general(lhs, rhs, dims, preferred_element_type=jnp.float32)
 
 
-def head_kernel(row_blocks, rows, cols, blocks, rays, note, table, seen):
+def head_kernel(row_blocks, chunks, pos, rows_in, cols_in, blocks_in, rays_in, *refs):
+    note, note2, table, blocks, rows, cols, rays, seen, squares, sems = refs
     count = blocks.shape[2]
     each = count // row_blocks
+    per_chunk = count // chunks
     batches, per_batch, here = rays.shape
     quarter = here // BS
     half = note.shape[1]
+    group = half // per_batch
+    small = [
+        pltpu.make_async_copy(src, dst, sems.at[i])
+        for i, (src, dst) in enumerate(((rows_in, rows), (cols_in, cols), (rays_in, rays)))
+    ]
+    large = []
+    for k in range(chunks):
+        where = pl.ds(k * per_chunk, per_chunk)
+        large.append(
+            pltpu.make_async_copy(
+                blocks_in.at[0, 0, where], blocks.at[0, 0, where], sems.at[3 + k]
+            )
+        )
+    for copy in small + large:
+        copy.start()
+    squares[...] = jnp.zeros_like(squares)
+    for copy in small:
+        copy.wait()
     for r in range(row_blocks):
         seen[r] = r * each
     for n in range(count):
@@ -37,40 +59,50 @@
         seen[row] = at + 1
         table[0, at] = n
         table[1, at] = cols[0, 0, n]
-    group = half // per_batch
-    for h in range(2):
+    for out, core in ((note, pos[1]), (note2, 1 - pos[1])):
         for i in range(quarter):
-            parts = [rays[h * group + g, :, i * BS : (i + 1) * BS] for g in range(group)]
-            note[h * quarter + i] = jnp.concatenate(parts, axis=0)
+            parts = [
+                rays[core * group + g, :, i * BS : (i + 1) * BS] for g in range(group)
+            ]
+            out[i] = jnp.concatenate(parts, axis=0)
+    for k in range(chunks):
+        large[k].wait()
+        for n in range(k * per_chunk, (k + 1) * per_chunk):
+            block = blocks[0, 0, n].astype(jnp.float32)
+            row = rows[0, 0, n]
+            squares[row] = squares[row] + block * block
     ones = jnp.ones((16, BS), jnp.bfloat16)
     for r in range(row_blocks):
-        squares = 0.0
-        for k in range(each):
-            block = blocks[0, 0, table[0, r * each + k]].astype(jnp.float32)
-            squares = squares + block * block
+        left = squares[r]
         total = 0.0
-        for _ in range(3):
-            part = squares.astype(jnp.bfloat16)
+        for _ in range(2):
+            part = left.astype(jnp.bfloat16)
             total = total + dot(ones, part, NT)
-            squares = squares - part.astype(jnp.float32)
-        note[2 * quarter, r : r + 1] = total[0:1]
-
-
-def weights(core, note, terms, w_scr):
-    tiles, slabs, _, _ = note.shape
-    quarter = (slabs - 1) // 2
+            left = left - part.astype(jnp.float32)
+        note[quarter, r : r + 1] = total[0:1]
+        note2[quarter, r : r + 1] = total[0:1]
+
+
+def slabs(refs, *where):
+    if len(refs) > 1:
+        return [ref[where] for ref in refs]
+    return [refs[0][(t,) + where] for t in range(refs[0].shape[0])]
+
+
+def weights(pos, notes, terms, w_scr, rays_scr):
     row_blocks = w_scr.shape[0]
-    norms = note[0, slabs - 1, 0:row_blocks]
-    for t in range(1, tiles):
-        norms = norms + note[t, slabs - 1, 0:row_blocks]
+    quarter = rays_scr.shape[1]
+    norms = sum(slabs(notes, quarter))[0:row_blocks]
     scale = relaxation / norms
+    if len(notes) > 1:
+        for d, ref in enumerate(notes):
+            rays_scr[pos[2] ^ d] = ref[0:quarter]
+    else:
+        rays_scr[...] = notes[0][:, 0:quarter]
     for r in range(row_blocks):
-        left = note[r // quarter, core * quarter + r % quarter]
+        left = rays_scr[r // quarter, r % quarter]
         if terms is not None:
-            total = terms[0, r].astype(jnp.float32)
-            for t in range(1, tiles):
-                total = total + terms[t, r].astype(jnp.float32)
-            left = left - total
+            left = left - sum(part.astype(jnp.float32) for part in slabs(terms, r))
         w_scr[r] = (left * scale[r : r + 1]).astype(jnp.bfloat16)
 
 
@@ -93,6 +125,12 @@
         terms[r] = total.astype(jnp.bfloat16)
 
 
+def take(refs, n):
+    taken = refs[:n]
+    del refs[:n]
+    return taken
+
+
 def on_core(pos, place, run, own, other):
     active = pos[0] == place
 
@@ -107,19 +145,19 @@
     return active
 
 
-def first_kernel(place, has_image, *refs):
+def first_kernel(place, n_notes, n_terms, *refs):
     refs = list(refs)
-    pos, table, table2, note, note2, blocks, blocks2 = refs[:7]
-    refs = refs[7:]
+    pos, table, table2, blocks, blocks2 = take(refs, 5)
+    notes, notes2 = take(refs, n_notes), take(refs, n_notes)
     terms_in, image_in = None, None
-    if has_image:
-        terms_in, image_in = refs[:2]
-        refs = refs[2:]
-    image, shot, terms, w_scr = refs
+    if n_terms:
+        terms_in = take(refs, n_terms)
+        (image_in,) = take(refs, 1)
+    image, shot, terms, w_scr, rays_scr = refs
 
     def run(first, second):
-        weights(pos[1], first[1], terms_in, w_scr)
-        if has_image:
+        weights(pos, first[1], terms_in, w_scr, rays_scr)
+        if n_terms:
             image[...] = image_in[...].astype(jnp.float32)
         else:
             image[...] = jnp.zeros_like(image)
@@ -127,16 +165,19 @@
         shot[...] = image[...].astype(jnp.bfloat16)
         project(second[0], second[2], shot, terms)
 
-    on_core(pos, place, run, (table, note, blocks), (table2, note2, blocks2))
-
-
-def second_kernel(place, *refs):
-    pos, table, table2, note, note2, blocks, blocks2 = refs[:7]
-    terms_in, image_in, shot, kept_in, given_in = refs[7:12]
-    image, kept, given, w_scr, x_scr = refs[12:]
+    on_core(pos, place, run, (table, notes, blocks), (table2, notes2, blocks2))
+
+
+def second_kernel(place, n_notes, n_terms, *refs):
+    refs = list(refs)
+    pos, table, table2, blocks, blocks2 = take(refs, 5)
+    notes, notes2 = take(refs, n_notes), take(refs, n_notes)
+    terms_in = take(refs, n_terms)
+    image_in, shot, kept_in, given_in = take(refs, 4)
+    image, kept, given, w_scr, rays_scr, x_scr = refs
 
     def run(first, second):
-        weights(pos[1], second[1], terms_in, w_scr)
+        weights(pos, second[1], terms_in, w_scr, rays_scr)
         x_scr[...] = image_in[...]
         back_project(second[0], second[2], w_scr, x_scr)
         out = x_scr[...].astype(jnp.bfloat16)
@@ -152,7 +193,7 @@
             kept[...] = out
             given[...] = shot[...]
 
-    active = on_core(pos, place, run, (table, note, blocks), (table2, note2, blocks2))
+    active = on_core(pos, place, run, (table, notes, blocks), (table2, notes2, blocks2))
 
     @pl.when(jnp.logical_not(active))
     def _():
@@ -197,17 +238,33 @@
     tiles = lax.axis_size("tile")
     row_blocks = quarter * tiles
     places = subsets // 2
+    direct = tiles <= DIRECT
     subset = lax.axis_index("subset")
-    pos = jnp.stack([subset // 2, subset % 2]).astype(jnp.int32)
+    pos = jnp.stack([subset // 2, subset % 2, lax.axis_index("tile")]).astype(jnp.int32)
 
     image_shape = (CB, half, BS)
     image_out = jax.ShapeDtypeStruct(image_shape, jnp.bfloat16)
     terms_out = jax.ShapeDtypeStruct((row_blocks, half, BS), jnp.bfloat16)
+    note_out = jax.ShapeDtypeStruct((quarter + 1, half, BS), jnp.float32)
     w_scr = pltpu.VMEM((row_blocks, half, BS), jnp.bfloat16)
+    rays_scr = pltpu.VMEM((tiles, quarter, half, BS), jnp.float32)
     x_scr = pltpu.VMEM(image_shape, jnp.float32)
 
     def swapped(value):
         return lax.ppermute(value, "subset", [(s, s ^ 1) for s in range(subsets)])
+
+    def turned(value, d, other=0):
+        pairs = [
+            (s * tiles + t, (s ^ other) * tiles + (t ^ d))
+            for s in range(subsets)
+            for t in range(tiles)
+        ]
+        return lax.ppermute(value, ("subset", "tile"), pairs)
+
+    def spread(value):
+        if direct:
+            return [value] + [turned(value, d) for d in range(1, tiles)]
+        return [lax.all_gather(value, "tile")]
 
     def call(kernel, smem, operands, out_shape, scratch, name):
         many = isinstance(out_shape, tuple)
@@ -222,27 +279,47 @@
         )(*operands)
 
     blocks2 = swapped(blocks)
-    note, table = pl.pallas_call(
-        functools.partial(head_kernel, row_blocks),
+    chunks = 8 if count % 8 == 0 else 1
+    note, note2, table, blocks = pl.pallas_call(
+        functools.partial(head_kernel, row_blocks, chunks),
         out_shape=(
-            jax.ShapeDtypeStruct((2 * quarter + 1, half, BS), jnp.float32),
+            note_out,
+            note_out,
             jax.ShapeDtypeStruct((2, count), jnp.int32),
+            pltpu.VMEM(blocks.shape, blocks.dtype),
         ),
-        in_specs=[SMEM, SMEM, VMEM, VMEM],
-        out_specs=(VMEM, SMEM),
-        scratch_shapes=[pltpu.SMEM((row_blocks,), jnp.int32)],
+        in_specs=[SMEM] + [pl.BlockSpec(memory_space=pltpu.HBM)] * 4,
+        out_specs=(VMEM, VMEM, SMEM, VMEM),
+        scratch_shapes=[
+            pltpu.SMEM(block_rows.shape, jnp.int32),
+            pltpu.SMEM(block_cols.shape, jnp.int32),
+            pltpu.VMEM(sinogram.shape, jnp.float32),
+            pltpu.SMEM((row_blocks,), jnp.int32),
+            pltpu.VMEM((row_blocks, BS, BS), jnp.float32),
+            pltpu.SemaphoreType.DMA((3 + chunks,)),
+        ],
         compiler_params=PARAMS,
         name="head",
-    )(block_rows, block_cols, blocks, sinogram)
+    )(
+        pos,
+        *(
+            pltpu.with_memory_space_constraint(value, pltpu.HBM)
+            for value in (block_rows, block_cols, blocks, sinogram)
+        ),
+    )
+    notes = spread(note)
+    if direct:
+        notes2 = [turned(note2, d, 1) for d in range(tiles)]
+    else:
+        notes2 = spread(swapped(note2))
     table2 = swapped(table)
-    note = lax.all_gather(note, "tile")
-    note2 = swapped(note)
+    blocks2 = pltpu.with_memory_space_constraint(blocks2, pltpu.VMEM)
 
     kept = jnp.zeros(image_shape, jnp.bfloat16)
     given = kept
     image = None
     for place in range(places):
-        fixed = [pos, table, table2, note, note2, blocks, blocks2]
+        fixed = [pos, table, table2, blocks, blocks2]
         extra = []
         if place > 0:
             pairs = [(2 * place - 2 + c, 2 * place + c) for c in range(2)]
@@ -255,22 +332,22 @@
                 [],
                 "project",
             )
-            extra = [lax.all_gather(terms, "tile"), image]
+            extra = spread(terms) + [image]
         image32, shot, terms = call(
-            functools.partial(first_kernel, place, place > 0),
+            functools.partial(first_kernel, place, len(notes), max(len(extra) - 1, 0)),
             3,
-            fixed + extra,
+            fixed + notes + notes2 + extra,
             (jax.ShapeDtypeStruct(image_shape, jnp.float32), image_out, terms_out),
-            [w_scr],
+            [w_scr, rays_scr],
             "first",
         )
-        terms = lax.all_gather(terms, "tile")
+        terms = spread(terms)
         image, kept, given = call(
-            functools.partial(second_kernel, place),
+            functools.partial(second_kernel, place, len(notes), len(terms)),
             3,
-            fixed + [terms, image32, shot, kept, given],
+            fixed + notes + notes2 + terms + [image32, shot, kept, given],
             (image_out, image_out, image_out),
-            [w_scr, x_scr],
+            [w_scr, rays_scr, x_scr],
             "second",
         )
     images = call(

time: 132 us -> 104 us (0.79)
  blocking collectives: 54.2 us -> 0 us
  starting transfers between devices: 21.7 us -> 43.5 us
  waiting for transfers between devices: 22.6 us -> 43.5 us
  Pallas kernels: 28.5 us -> 16.3 us
  local copies, waits for them, and re-layouts: 3.91 us -> 0.02 us
    all_gather x8 -> x0, blocking collectives: 54.2 us -> none  [the longest x4 29.3 us: per_device(): terms = lax.all_gather(terms, 'tile')]
    ppermute x0 -> x28, starting transfers between devices: none -> 24.8 us  [turned(): return lax.ppermute(value, ('subset', 'tile'), pairs)]
    ppermute x0 -> x28, waiting for transfers between devices: none -> 20.5 us  [turned(): return lax.ppermute(value, ('subset', 'tile'), pairs)]
    pallas_call x12, Pallas kernels: 26.5 us -> 13.2 us  [call(): pl.pallas_call(kernel, out_shape=out_shape, in_specs=[SMEM] * smem + [VME...]
    unnamed x10 -> x0, local copies, waits for them, and re-layouts: 3.89 us -> none
    ppermute x4 -> x3, starting transfers between devices: 19.1 us -> 16.1 us  [swapped(): return lax.ppermute(value, 'subset', [(s, s ^ 1) for s in range(subsets)])]
  transfers between devices with their start and end apart: 7 -> 34, of which waited for: 3 -> 24; matrix products, arithmetic and copies ran while one was open for 0% -> 0% of each run, Pallas kernels for 2% -> 3%
where the time goes in v3:
time: 104 us
  starting transfers between devices  43.5 us (42%)
  waiting for transfers between devices  43.5 us (42%)
  Pallas kernels  16.3 us (16%)
    ppermute x28, starting transfers between devices, turned(): return lax.ppermute(value, ('subset', 'tile'), pairs)  24.8 us
    ppermute x3, waiting for transfers between devices, per_device(): image = lax.ppermute(image, 'subset', pairs)  21.2 us
    ppermute x28, waiting for transfers between devices, turned(): return lax.ppermute(value, ('subset', 'tile'), pairs)  20.5 us
    ppermute x3, starting transfers between devices, swapped(): return lax.ppermute(value, 'subset', [(s, s ^ 1) for s in range(subsets)])  16.1 us
    pallas_call x12, Pallas kernels, call(): pl.pallas_call(kernel, out_shape=out_shape, in_specs=[SMEM] * smem + [VME...  13.2 us
    pallas_call x1, Pallas kernels, per_device(): pl.pallas_call(functools.partial(head_kernel, row_blocks, chunks), out_sh...  3.09 us
    ppermute x3, starting transfers between devices, per_device(): image = lax.ppermute(image, 'subset', pairs)  2.63 us
  transfers between devices with their start and end apart: 34, of which 24 were waited for; matrix products, arithmetic and copies ran while one was open for 0% of the time, Pallas kernels for 3%

profile of v3, /device:TPU:25, one launch (start us, length us, event | category | flops | bytes accessed | tf_op | source)
XLA Modules:
  0.0 103.6 jit_solution(16589303080063988555)
XLA Ops:
  0.0 0.7 collective-permute-start.1
  0.8 3.1 %head.1 = (f32[5,16,128]{2,1,0:T(8,128)S(1)}, f32[5,16,128]{2,1,0:T(8,128)S(1)}, s32[2,80]{1,0:T(2,128)S(1)}, bf16[1,1,80,128,128]{4,3,2,1,0:T(8,128)(2,1)S(1)}) custom-call(s32[3]{0:T(128)S(1)} %pad_add_fusion.pos.refs_0_, s32[1,1,80]{2,1,0:T(1,128)} %rows_in.1, s32[1,1,80]{2,1,0:T(1,128)} %cols_in.1, bf16[1,1,80,128,128]{4,3,2,1,0:T(8,128)(2,1)} %blocks_in.1, ...), custom_call_target="tpu_custom_call" | custom-call | tf_op jit(solution)/shard_map/head/pallas_call | solution.py:283
  3.8 2.1 %collective-permute-start.8 = (f32[5,16,128]{2,1,0:T(8,128)S(1)}, f32[5,16,128]{2,1,0:T(8,128)S(1)}, u32[]{:S(2)}, u32[]{:S(2)}) collective-permute-start(f32[5,16,128]{2,1,0:T(8,128)S(1)} %get-tuple-element.35), channel_id=1, source_target_pairs={{0,7},{1,6},{2,5},{3,4},{4,3},{5,2},{6,1},{7,0},{8,15},{9,14},{10,... | collective-permute-start | bytes 122888 | tf_op jit(solution)/shard_map/ppermute | solution.py:262
  6.0 0.6 collective-permute-start.7
  7.2 0.8 collective-permute-done.refs_2_.table2
  8.4 2.4 %collective-permute-start.4 = (f32[5,16,128]{2,1,0:T(8,128)S(1)}, f32[5,16,128]{2,1,0:T(8,128)S(1)}, u32[]{:S(2)}, u32[]{:S(2)}) collective-permute-start(f32[5,16,128]{2,1,0:T(8,128)S(1)} %get-tuple-element.34.refs_5_), channel_id=1, source_target_pairs={{0,3},{1,2},{2,1},{3,0},{4,7},{5,6},{6,5},{7,4},{8,11},{9,10},{10,... | collective-permute-start | bytes 122888 | tf_op jit(solution)/shard_map/ppermute | solution.py:262
  11.1 1.0 collective-permute-done.4.refs_8_
  12.2 1.5 %collective-permute-done.3.refs_7_ = f32[5,16,128]{2,1,0:T(8,128)S(1)} collective-permute-done((f32[5,16,128]{2,1,0:T(8,128)S(1)}, f32[5,16,128]{2,1,0:T(8,128)S(1)}, u32[]{:S(2)}, u32[]{:S(2)}) %collective-permute-start.3) | collective-permute-done | bytes 40992 | tf_op jit(solution)/shard_map/ppermute | solution.py:262
  14.3 1.5 %collective-permute-start.11 = (bf16[16,16,128]{2,1,0:T(8,128)(2,1)S(1)}, bf16[16,16,128]{2,1,0:T(8,128)(2,1)S(1)}, u32[]{:S(2)}, u32[]{:S(2)}) collective-permute-start(bf16[16,16,128]{2,1,0:T(8,128)(2,1)S(1)} %get-tuple-element.36.refs_13_), channel_id=1, source_target_pairs={{0,3},{1,2},{2,1},{3,0},{4,7},{5,6},{6,5},{7,4},{8,11},{9,10},{10,... | collective-permute-start | bytes 196616 | tf_op jit(solution)/shard_map/ppermute | solution.py:262
  15.8 0.8 collective-permute-start.10
  17.0 1.4 %collective-permute-done.11.refs_16_ = bf16[16,16,128]{2,1,0:T(8,128)(2,1)S(1)} collective-permute-done((bf16[16,16,128]{2,1,0:T(8,128)(2,1)S(1)}, bf16[16,16,128]{2,1,0:T(8,128)(2,1)S(1)}, u32[]{:S(2)}, u32[]{:S(2)}) %collective-permute-start.11) | collective-permute-done | bytes 65568 | tf_op jit(solution)/shard_map/ppermute | solution.py:262
  18.4 0.7 collective-permute-done.10.refs_15_
  19.1 0.7 collective-permute-done.9.refs_14_
  19.8 0.6 second.4
  20.4 0.7 collective-permute-start.12
  21.7 2.2 %collective-permute-start.15 = (bf16[16,16,128]{2,1,0:T(8,128)(2,1)S(1)}, bf16[16,16,128]{2,1,0:T(8,128)(2,1)S(1)}, u32[]{:S(2)}, u32[]{:S(2)}) collective-permute-start(bf16[16,16,128]{2,1,0:T(8,128)(2,1)S(1)} %project.3.refs_13_), channel_id=1, source_target_pairs={{0,3},{1,2},{2,1},{3,0},{4,7},{5,6},{6,5},{7,4},{8,11},{9,10},{10,... | collective-permute-start | bytes 196616 | tf_op jit(solution)/shard_map/ppermute | solution.py:262
  24.4 1.4 %collective-permute-done.15.refs_16_ = bf16[16,16,128]{2,1,0:T(8,128)(2,1)S(1)} collective-permute-done((bf16[16,16,128]{2,1,0:T(8,128)(2,1)S(1)}, bf16[16,16,128]{2,1,0:T(8,128)(2,1)S(1)}, u32[]{:S(2)}, u32[]{:S(2)}) %collective-permute-start.15) | collective-permute-done | bytes 65568 | tf_op jit(solution)/shard_map/ppermute | solution.py:262
  25.8 1.3 %collective-permute-done.14.refs_15_ = bf16[16,16,128]{2,1,0:T(8,128)(2,1)S(1)} collective-permute-done((bf16[16,16,128]{2,1,0:T(8,128)(2,1)S(1)}, bf16[16,16,128]{2,1,0:T(8,128)(2,1)S(1)}, u32[]{:S(2)}, u32[]{:S(2)}) %collective-permute-start.14) | collective-permute-done | bytes 65568 | tf_op jit(solution)/shard_map/ppermute | solution.py:262
  27.6 1.2 %collective-permute-start.18 = (bf16[16,16,128]{2,1,0:T(8,128)(2,1)S(1)}, bf16[16,16,128]{2,1,0:T(8,128)(2,1)S(1)}, u32[]{:S(2)}, u32[]{:S(2)}) collective-permute-start(bf16[16,16,128]{2,1,0:T(8,128)(2,1)S(1)} %get-tuple-element.40.refs_13_), channel_id=1, source_target_pairs={{0,3},{1,2},{2,1},{3,0},{4,7},{5,6},{6,5},{7,4},{8,11},{9,10},{10,... | collective-permute-start | bytes 196616 | tf_op jit(solution)/shard_map/ppermute | solution.py:262
  28.9 0.7 collective-permute-start.17
  29.6 0.8 collective-permute-start.16
  30.4 1.8 %collective-permute-done.18.refs_16_ = bf16[16,16,128]{2,1,0:T(8,128)(2,1)S(1)} collective-permute-done((bf16[16,16,128]{2,1,0:T(8,128)(2,1)S(1)}, bf16[16,16,128]{2,1,0:T(8,128)(2,1)S(1)}, u32[]{:S(2)}, u32[]{:S(2)}) %collective-permute-start.18) | collective-permute-done | bytes 65568 | tf_op jit(solution)/shard_map/ppermute | solution.py:262
  32.7 0.8 second.5
  33.5 0.7 collective-permute-start.19
  34.8 2.0 %collective-permute-start.22 = (bf16[16,16,128]{2,1,0:T(8,128)(2,1)S(1)}, bf16[16,16,128]{2,1,0:T(8,128)(2,1)S(1)}, u32[]{:S(2)}, u32[]{:S(2)}) collective-permute-start(bf16[16,16,128]{2,1,0:T(8,128)(2,1)S(1)} %project.4.refs_13_), channel_id=1, source_target_pairs={{0,3},{1,2},{2,1},{3,0},{4,7},{5,6},{6,5},{7,4},{8,11},{9,10},{10,... | collective-permute-start | bytes 196616 | tf_op jit(solution)/shard_map/ppermute | solution.py:262
  37.5 1.6 %collective-permute-done.22.refs_16_ = bf16[16,16,128]{2,1,0:T(8,128)(2,1)S(1)} collective-permute-done((bf16[16,16,128]{2,1,0:T(8,128)(2,1)S(1)}, bf16[16,16,128]{2,1,0:T(8,128)(2,1)S(1)}, u32[]{:S(2)}, u32[]{:S(2)}) %collective-permute-start.22) | collective-permute-done | bytes 65568 | tf_op jit(solution)/shard_map/ppermute | solution.py:262
  39.1 0.8 collective-permute-done.21.refs_15_
  40.7 1.3 %collective-permute-start.25 = (bf16[16,16,128]{2,1,0:T(8,128)(2,1)S(1)}, bf16[16,16,128]{2,1,0:T(8,128)(2,1)S(1)}, u32[]{:S(2)}, u32[]{:S(2)}) collective-permute-start(bf16[16,16,128]{2,1,0:T(8,128)(2,1)S(1)} %get-tuple-element.46.refs_13_), channel_id=1, source_target_pairs={{0,3},{1,2},{2,1},{3,0},{4,7},{5,6},{6,5},{7,4},{8,11},{9,10},{10,... | collective-permute-start | bytes 196616 | tf_op jit(solution)/shard_map/ppermute | solution.py:262
  42.5 0.9 collective-permute-start.23
  43.4 1.4 %collective-permute-done.25.refs_16_ = bf16[16,16,128]{2,1,0:T(8,128)(2,1)S(1)} collective-permute-done((bf16[16,16,128]{2,1,0:T(8,128)(2,1)S(1)}, bf16[16,16,128]{2,1,0:T(8,128)(2,1)S(1)}, u32[]{:S(2)}, u32[]{:S(2)}) %collective-permute-start.25) | collective-permute-done | bytes 65568 | tf_op jit(solution)/shard_map/ppermute | solution.py:262
  44.8 1.4 %collective-permute-done.24.refs_15_ = bf16[16,16,128]{2,1,0:T(8,128)(2,1)S(1)} collective-permute-done((bf16[16,16,128]{2,1,0:T(8,128)(2,1)S(1)}, bf16[16,16,128]{2,1,0:T(8,128)(2,1)S(1)}, u32[]{:S(2)}, u32[]{:S(2)}) %collective-permute-start.24) | collective-permute-done | bytes 65568 | tf_op jit(solution)/shard_map/ppermute | solution.py:262
  46.8 1.3 %collective-permute-start.26 = (bf16[32,16,128]{2,1,0:T(8,128)(2,1)S(1)}, bf16[32,16,128]{2,1,0:T(8,128)(2,1)S(1)}, u32[]{:S(2)}, u32[]{:S(2)}) collective-permute-start(bf16[32,16,128]{2,1,0:T(8,128)(2,1)S(1)} %get-tuple-element.51), channel_id=1, source_target_pairs={{16,24},{20,28},{17,25},{21,29},{18,26},{22,30},{19,27},{23,31}} | collective-permute-start | bytes 393224 | tf_op jit(solution)/shard_map/ppermute | solution.py:326
  48.1 21.2 %collective-permute-done.26.image.refs_17_ = bf16[32,16,128]{2,1,0:T(8,128)(2,1)S(1)} collective-permute-done((bf16[32,16,128]{2,1,0:T(8,128)(2,1)S(1)}, bf16[32,16,128]{2,1,0:T(8,128)(2,1)S(1)}, u32[]{:S(2)}, u32[]{:S(2)}) %collective-permute-start.26) | collective-permute-done | bytes 131104 | tf_op jit(solution)/shard_map/ppermute | solution.py:326
  69.3 2.0 %project.5.refs_13_ = bf16[16,16,128]{2,1,0:T(8,128)(2,1)S(1)} custom-call(s32[3]{0:T(128)S(1)} %pad_add_fusion.pos.refs_0_, s32[2,80]{1,0:T(2,128)S(1)} %get-tuple-element.32.refs_1_.table, s32[2,80]{1,0:T(2,128)S(1)} %collective-permute-done.refs_2_.table2, bf16[32,16,128]{2,1,0:T(8,128)(2,1)S(1)} %collective-permute-done.26.image.refs_17_, ...), custom_call_target="tpu_custom_call" | custom-call | tf_op jit(solution)/shard_map/project/pallas_call | solution.py:271
  71.3 1.7 %collective-permute-start.29 = (bf16[16,16,128]{2,1,0:T(8,128)(2,1)S(1)}, bf16[16,16,128]{2,1,0:T(8,128)(2,1)S(1)}, u32[]{:S(2)}, u32[]{:S(2)}) collective-permute-start(bf16[16,16,128]{2,1,0:T(8,128)(2,1)S(1)} %project.5.refs_13_), channel_id=1, source_target_pairs={{0,3},{1,2},{2,1},{3,0},{4,7},{5,6},{6,5},{7,4},{8,11},{9,10},{10,... | collective-permute-start | bytes 196616 | tf_op jit(solution)/shard_map/ppermute | solution.py:262
  73.0 0.7 collective-permute-start.28
  74.0 1.4 %collective-permute-done.29.refs_16_ = bf16[16,16,128]{2,1,0:T(8,128)(2,1)S(1)} collective-permute-done((bf16[16,16,128]{2,1,0:T(8,128)(2,1)S(1)}, bf16[16,16,128]{2,1,0:T(8,128)(2,1)S(1)}, u32[]{:S(2)}, u32[]{:S(2)}) %collective-permute-start.29) | collective-permute-done | bytes 65568 | tf_op jit(solution)/shard_map/ppermute | solution.py:262
  75.3 0.7 collective-permute-done.28.refs_15_
  76.1 0.7 collective-permute-done.27.refs_14_
  76.8 2.9 %first.7 = (f32[32,16,128]{2,1,0:T(8,128)S(1)}, bf16[32,16,128]{2,1,0:T(8,128)(2,1)S(1)}, bf16[16,16,128]{2,1,0:T(8,128)(2,1)S(1)}) custom-call(s32[3]{0:T(128)S(1)} %pad_add_fusion.pos.refs_0_, s32[2,80]{1,0:T(2,128)S(1)} %get-tuple-element.32.refs_1_.table, s32[2,80]{1,0:T(2,128)S(1)} %collective-permute-done.refs_2_.table2, ...), custom_call_target="tpu_custom_call" | custom-call | tf_op jit(solution)/shard_map/first/pallas_call | solution.py:271
  79.6 1.2 %collective-permute-start.32 = (bf16[16,16,128]{2,1,0:T(8,128)(2,1)S(1)}, bf16[16,16,128]{2,1,0:T(8,128)(2,1)S(1)}, u32[]{:S(2)}, u32[]{:S(2)}) collective-permute-start(bf16[16,16,128]{2,1,0:T(8,128)(2,1)S(1)} %get-tuple-element.52.refs_13_), channel_id=1, source_target_pairs={{0,3},{1,2},{2,1},{3,0},{4,7},{5,6},{6,5},{7,4},{8,11},{9,10},{10,... | collective-permute-start | bytes 196616 | tf_op jit(solution)/shard_map/ppermute | solution.py:262
  81.2 1.0 %collective-permute-start.30 = (bf16[16,16,128]{2,1,0:T(8,128)(2,1)S(1)}, bf16[16,16,128]{2,1,0:T(8,128)(2,1)S(1)}, u32[]{:S(2)}, u32[]{:S(2)}) collective-permute-start(bf16[16,16,128]{2,1,0:T(8,128)(2,1)S(1)} %get-tuple-element.52.refs_13_), channel_id=1, source_target_pairs={{0,1},{1,0},{2,3},{3,2},{4,5},{5,4},{6,7},{7,6},{8,9},{9,8},{10,11... | collective-permute-start | bytes 196616 | tf_op jit(solution)/shard_map/ppermute | solution.py:262
  82.3 1.4 %collective-permute-done.32.refs_16_ = bf16[16,16,128]{2,1,0:T(8,128)(2,1)S(1)} collective-permute-done((bf16[16,16,128]{2,1,0:T(8,128)(2,1)S(1)}, bf16[16,16,128]{2,1,0:T(8,128)(2,1)S(1)}, u32[]{:S(2)}, u32[]{:S(2)}) %collective-permute-start.32) | collective-permute-done | bytes 65568 | tf_op jit(solution)/shard_map/ppermute | solution.py:262
  83.7 0.7 collective-permute-done.31.refs_15_
  84.4 2.1 %second.7 = (bf16[32,16,128]{2,1,0:T(8,128)(2,1)}, bf16[32,16,128]{2,1,0:T(8,128)(2,1)S(1)}, bf16[32,16,128]{2,1,0:T(8,128)(2,1)S(1)}) custom-call(s32[3]{0:T(128)S(1)} %pad_add_fusion.pos.refs_0_, s32[2,80]{1,0:T(2,128)S(1)} %get-tuple-element.32.refs_1_.table, s32[2,80]{1,0:T(2,128)S(1)} %collective-permute-done.refs_2_.table2, ...), custom_call_target="tpu_custom_call" | custom-call | tf_op jit(solution)/shard_map/second/pallas_call | solution.py:271
  86.5 14.9 %collective-permute-start.33 = (bf16[32,16,128]{2,1,0:T(8,128)(2,1)S(1)}, bf16[32,16,128]{2,1,0:T(8,128)(2,1)S(1)}, u32[]{:S(2)}, u32[]{:S(2)}) collective-permute-start(bf16[32,16,128]{2,1,0:T(8,128)(2,1)S(1)} %get-tuple-element.58), channel_id=1, source_target_pairs={{0,4},{4,0},{8,12},{12,8},{16,20},{20,16},{24,28},{28,24},{1,5},{5... | collective-permute-start | bytes 393224 | tf_op jit(solution)/shard_map/ppermute | solution.py:254
  101.3 1.0 collective-permute-done.33.given
  102.3 1.3 %last.1 = bf16[4,8,4096]{2,1,0:T(8,128)(2,1)} custom-call(s32[3]{0:T(128)S(1)} %pad_add_fusion.pos.refs_0_, bf16[32,16,128]{2,1,0:T(8,128)(2,1)S(1)} %get-tuple-element.57.kept, bf16[32,16,128]{2,1,0:T(8,128)(2,1)S(1)} %collective-permute-done.33.given), custom_call_target="tpu_custom_call" | custom-call | tf_op jit(solution)/shard_map/last/pallas_call | solution.py:271
  (35 shorter events, 8.5 us)
Async XLA Ops:
  0.0 13.7 %collective-permute-start.1 = (bf16[1,1,80,128,128]{4,3,2,1,0:T(8,128)(2,1)}, bf16[1,1,80,128,128]{4,3,2,1,0:T(8,128)(2,1)S(1)}, u32[]{:S(2)}, u32[]{:S(2)}) collective-permute-start(bf16[1,1,80,128,128]{4,3,2,1,0:T(8,128)(2,1)} %blocks_in.1), channel_id=1, source_target_pairs={{0,4},{4,0},{8,12},{12,8},{16,20},{20,16},{24,28},{28,24},{1,5},{5... | collective-permute-start | bytes 7864328 | tf_op jit(solution)/shard_map/ppermute | solution.py:254
  3.8 4.5 %collective-permute-start.8 = (f32[5,16,128]{2,1,0:T(8,128)S(1)}, f32[5,16,128]{2,1,0:T(8,128)S(1)}, u32[]{:S(2)}, u32[]{:S(2)}) collective-permute-start(f32[5,16,128]{2,1,0:T(8,128)S(1)} %get-tuple-element.35), channel_id=1, source_target_pairs={{0,7},{1,6},{2,5},{3,4},{4,3},{5,2},{6,1},{7,0},{8,15},{9,14},{10,... | collective-permute-start | bytes 122888 | tf_op jit(solution)/shard_map/ppermute | solution.py:262
  6.0 4.8 %collective-permute-start.7 = (f32[5,16,128]{2,1,0:T(8,128)S(1)}, f32[5,16,128]{2,1,0:T(8,128)S(1)}, u32[]{:S(2)}, u32[]{:S(2)}) collective-permute-start(f32[5,16,128]{2,1,0:T(8,128)S(1)} %get-tuple-element.35), channel_id=1, source_target_pairs={{0,6},{1,7},{2,4},{3,5},{4,2},{5,3},{6,0},{7,1},{8,14},{9,15},{10,... | collective-permute-start | bytes 122888 | tf_op jit(solution)/shard_map/ppermute | solution.py:262
  6.6 4.2 %collective-permute-start.6 = (f32[5,16,128]{2,1,0:T(8,128)S(1)}, f32[5,16,128]{2,1,0:T(8,128)S(1)}, u32[]{:S(2)}, u32[]{:S(2)}) collective-permute-start(f32[5,16,128]{2,1,0:T(8,128)S(1)} %get-tuple-element.35), channel_id=1, source_target_pairs={{0,5},{1,4},{2,7},{3,6},{4,1},{5,0},{6,3},{7,2},{8,13},{9,12},{10,... | collective-permute-start | bytes 122888 | tf_op jit(solution)/shard_map/ppermute | solution.py:262
  6.7 1.3 %collective-permute-start = (s32[2,80]{1,0:T(2,128)S(1)}, s32[2,80]{1,0:T(2,128)S(1)}, u32[]{:S(2)}, u32[]{:S(2)}) collective-permute-start(s32[2,80]{1,0:T(2,128)S(1)} %get-tuple-element.32.refs_1_.table), channel_id=1, source_target_pairs={{0,4},{4,0},{8,12},{12,8},{16,20},{20,16},{24,28},{28,24},{1,5},{5... | collective-permute-start | bytes 1928 | tf_op jit(solution)/shard_map/ppermute | solution.py:254
  8.1 3.1 %collective-permute-start.5 = (f32[5,16,128]{2,1,0:T(8,128)S(1)}, f32[5,16,128]{2,1,0:T(8,128)S(1)}, u32[]{:S(2)}, u32[]{:S(2)}) collective-permute-start(f32[5,16,128]{2,1,0:T(8,128)S(1)} %get-tuple-element.35), channel_id=1, source_target_pairs={{0,4},{1,5},{2,6},{3,7},{4,0},{5,1},{6,2},{7,3},{8,12},{9,13},{10,... | collective-permute-start | bytes 122888 | tf_op jit(solution)/shard_map/ppermute | solution.py:262
  8.4 3.8 %collective-permute-start.4 = (f32[5,16,128]{2,1,0:T(8,128)S(1)}, f32[5,16,128]{2,1,0:T(8,128)S(1)}, u32[]{:S(2)}, u32[]{:S(2)}) collective-permute-start(f32[5,16,128]{2,1,0:T(8,128)S(1)} %get-tuple-element.34.refs_5_), channel_id=1, source_target_pairs={{0,3},{1,2},{2,1},{3,0},{4,7},{5,6},{6,5},{7,4},{8,11},{9,10},{10,... | collective-permute-start | bytes 122888 | tf_op jit(solution)/shard_map/ppermute | solution.py:262
  10.8 2.9 %collective-permute-start.3 = (f32[5,16,128]{2,1,0:T(8,128)S(1)}, f32[5,16,128]{2,1,0:T(8,128)S(1)}, u32[]{:S(2)}, u32[]{:S(2)}) collective-permute-start(f32[5,16,128]{2,1,0:T(8,128)S(1)} %get-tuple-element.34.refs_5_), channel_id=1, source_target_pairs={{0,2},{1,3},{2,0},{3,1},{4,6},{5,7},{6,4},{7,5},{8,10},{9,11},{10,... | collective-permute-start | bytes 122888 | tf_op jit(solution)/shard_map/ppermute | solution.py:262
  10.8 2.9 %collective-permute-start.2 = (f32[5,16,128]{2,1,0:T(8,128)S(1)}, f32[5,16,128]{2,1,0:T(8,128)S(1)}, u32[]{:S(2)}, u32[]{:S(2)}) collective-permute-start(f32[5,16,128]{2,1,0:T(8,128)S(1)} %get-tuple-element.34.refs_5_), channel_id=1, source_target_pairs={{0,1},{1,0},{2,3},{3,2},{4,5},{5,4},{6,7},{7,6},{8,9},{9,8},{10,11... | collective-permute-start | bytes 122888 | tf_op jit(solution)/shard_map/ppermute | solution.py:262
  14.3 4.1 %collective-permute-start.11 = (bf16[16,16,128]{2,1,0:T(8,128)(2,1)S(1)}, bf16[16,16,128]{2,1,0:T(8,128)(2,1)S(1)}, u32[]{:S(2)}, u32[]{:S(2)}) collective-permute-start(bf16[16,16,128]{2,1,0:T(8,128)(2,1)S(1)} %get-tuple-element.36.refs_13_), channel_id=1, source_target_pairs={{0,3},{1,2},{2,1},{3,0},{4,7},{5,6},{6,5},{7,4},{8,11},{9,10},{10,... | collective-permute-start | bytes 196616 | tf_op jit(solution)/shard_map/ppermute | solution.py:262
  15.8 3.3 %collective-permute-start.10 = (bf16[16,16,128]{2,1,0:T(8,128)(2,1)S(1)}, bf16[16,16,128]{2,1,0:T(8,128)(2,1)S(1)}, u32[]{:S(2)}, u32[]{:S(2)}) collective-permute-start(bf16[16,16,128]{2,1,0:T(8,128)(2,1)S(1)} %get-tuple-element.36.refs_13_), channel_id=1, source_target_pairs={{0,2},{1,3},{2,0},{3,1},{4,6},{5,7},{6,4},{7,5},{8,10},{9,11},{10,... | collective-permute-start | bytes 196616 | tf_op jit(solution)/shard_map/ppermute | solution.py:262
  16.6 3.1 %collective-permute-start.9 = (bf16[16,16,128]{2,1,0:T(8,128)(2,1)S(1)}, bf16[16,16,128]{2,1,0:T(8,128)(2,1)S(1)}, u32[]{:S(2)}, u32[]{:S(2)}) collective-permute-start(bf16[16,16,128]{2,1,0:T(8,128)(2,1)S(1)} %get-tuple-element.36.refs_13_), channel_id=1, source_target_pairs={{0,1},{1,0},{2,3},{3,2},{4,5},{5,4},{6,7},{7,6},{8,9},{9,8},{10,11... | collective-permute-start | bytes 196616 | tf_op jit(solution)/shard_map/ppermute | solution.py:262
  20.4 0.7 collective-permute-start.12
  21.7 4.1 %collective-permute-start.15 = (bf16[16,16,128]{2,1,0:T(8,128)(2,1)S(1)}, bf16[16,16,128]{2,1,0:T(8,128)(2,1)S(1)}, u32[]{:S(2)}, u32[]{:S(2)}) collective-permute-start(bf16[16,16,128]{2,1,0:T(8,128)(2,1)S(1)} %project.3.refs_13_), channel_id=1, source_target_pairs={{0,3},{1,2},{2,1},{3,0},{4,7},{5,6},{6,5},{7,4},{8,11},{9,10},{10,... | collective-permute-start | bytes 196616 | tf_op jit(solution)/shard_map/ppermute | solution.py:262
  23.9 3.1 %collective-permute-start.14 = (bf16[16,16,128]{2,1,0:T(8,128)(2,1)S(1)}, bf16[16,16,128]{2,1,0:T(8,128)(2,1)S(1)}, u32[]{:S(2)}, u32[]{:S(2)}) collective-permute-start(bf16[16,16,128]{2,1,0:T(8,128)(2,1)S(1)} %project.3.refs_13_), channel_id=1, source_target_pairs={{0,2},{1,3},{2,0},{3,1},{4,6},{5,7},{6,4},{7,5},{8,10},{9,11},{10,... | collective-permute-start | bytes 196616 | tf_op jit(solution)/shard_map/ppermute | solution.py:262
  23.9 3.1 %collective-permute-start.13 = (bf16[16,16,128]{2,1,0:T(8,128)(2,1)S(1)}, bf16[16,16,128]{2,1,0:T(8,128)(2,1)S(1)}, u32[]{:S(2)}, u32[]{:S(2)}) collective-permute-start(bf16[16,16,128]{2,1,0:T(8,128)(2,1)S(1)} %project.3.refs_13_), channel_id=1, source_target_pairs={{0,1},{1,0},{2,3},{3,2},{4,5},{5,4},{6,7},{7,6},{8,9},{9,8},{10,11... | collective-permute-start | bytes 196616 | tf_op jit(solution)/shard_map/ppermute | solution.py:262
  27.6 4.5 %collective-permute-start.18 = (bf16[16,16,128]{2,1,0:T(8,128)(2,1)S(1)}, bf16[16,16,128]{2,1,0:T(8,128)(2,1)S(1)}, u32[]{:S(2)}, u32[]{:S(2)}) collective-permute-start(bf16[16,16,128]{2,1,0:T(8,128)(2,1)S(1)} %get-tuple-element.40.refs_13_), channel_id=1, source_target_pairs={{0,3},{1,2},{2,1},{3,0},{4,7},{5,6},{6,5},{7,4},{8,11},{9,10},{10,... | collective-permute-start | bytes 196616 | tf_op jit(solution)/shard_map/ppermute | solution.py:262
  28.9 3.6 %collective-permute-start.17 = (bf16[16,16,128]{2,1,0:T(8,128)(2,1)S(1)}, bf16[16,16,128]{2,1,0:T(8,128)(2,1)S(1)}, u32[]{:S(2)}, u32[]{:S(2)}) collective-permute-start(bf16[16,16,128]{2,1,0:T(8,128)(2,1)S(1)} %get-tuple-element.40.refs_13_), channel_id=1, source_target_pairs={{0,2},{1,3},{2,0},{3,1},{4,6},{5,7},{6,4},{7,5},{8,10},{9,11},{10,... | collective-permute-start | bytes 196616 | tf_op jit(solution)/shard_map/ppermute | solution.py:262
  29.6 3.1 %collective-permute-start.16 = (bf16[16,16,128]{2,1,0:T(8,128)(2,1)S(1)}, bf16[16,16,128]{2,1,0:T(8,128)(2,1)S(1)}, u32[]{:S(2)}, u32[]{:S(2)}) collective-permute-start(bf16[16,16,128]{2,1,0:T(8,128)(2,1)S(1)} %get-tuple-element.40.refs_13_), channel_id=1, source_target_pairs={{0,1},{1,0},{2,3},{3,2},{4,5},{5,4},{6,7},{7,6},{8,9},{9,8},{10,11... | collective-permute-start | bytes 196616 | tf_op jit(solution)/shard_map/ppermute | solution.py:262
  33.5 0.7 collective-permute-start.19
  34.8 4.4 %collective-permute-start.22 = (bf16[16,16,128]{2,1,0:T(8,128)(2,1)S(1)}, bf16[16,16,128]{2,1,0:T(8,128)(2,1)S(1)}, u32[]{:S(2)}, u32[]{:S(2)}) collective-permute-start(bf16[16,16,128]{2,1,0:T(8,128)(2,1)S(1)} %project.4.refs_13_), channel_id=1, source_target_pairs={{0,3},{1,2},{2,1},{3,0},{4,7},{5,6},{6,5},{7,4},{8,11},{9,10},{10,... | collective-permute-start | bytes 196616 | tf_op jit(solution)/shard_map/ppermute | solution.py:262
  36.8 3.1 %collective-permute-start.21 = (bf16[16,16,128]{2,1,0:T(8,128)(2,1)S(1)}, bf16[16,16,128]{2,1,0:T(8,128)(2,1)S(1)}, u32[]{:S(2)}, u32[]{:S(2)}) collective-permute-start(bf16[16,16,128]{2,1,0:T(8,128)(2,1)S(1)} %project.4.refs_13_), channel_id=1, source_target_pairs={{0,2},{1,3},{2,0},{3,1},{4,6},{5,7},{6,4},{7,5},{8,10},{9,11},{10,... | collective-permute-start | bytes 196616 | tf_op jit(solution)/shard_map/ppermute | solution.py:262
  36.9 3.1 %collective-permute-start.20 = (bf16[16,16,128]{2,1,0:T(8,128)(2,1)S(1)}, bf16[16,16,128]{2,1,0:T(8,128)(2,1)S(1)}, u32[]{:S(2)}, u32[]{:S(2)}) collective-permute-start(bf16[16,16,128]{2,1,0:T(8,128)(2,1)S(1)} %project.4.refs_13_), channel_id=1, source_target_pairs={{0,1},{1,0},{2,3},{3,2},{4,5},{5,4},{6,7},{7,6},{8,9},{9,8},{10,11... | collective-permute-start | bytes 196616 | tf_op jit(solution)/shard_map/ppermute | solution.py:262
  40.7 4.1 %collective-permute-start.25 = (bf16[16,16,128]{2,1,0:T(8,128)(2,1)S(1)}, bf16[16,16,128]{2,1,0:T(8,128)(2,1)S(1)}, u32[]{:S(2)}, u32[]{:S(2)}) collective-permute-start(bf16[16,16,128]{2,1,0:T(8,128)(2,1)S(1)} %get-tuple-element.46.refs_13_), channel_id=1, source_target_pairs={{0,3},{1,2},{2,1},{3,0},{4,7},{5,6},{6,5},{7,4},{8,11},{9,10},{10,... | collective-permute-start | bytes 196616 | tf_op jit(solution)/shard_map/ppermute | solution.py:262
  41.9 4.2 %collective-permute-start.24 = (bf16[16,16,128]{2,1,0:T(8,128)(2,1)S(1)}, bf16[16,16,128]{2,1,0:T(8,128)(2,1)S(1)}, u32[]{:S(2)}, u32[]{:S(2)}) collective-permute-start(bf16[16,16,128]{2,1,0:T(8,128)(2,1)S(1)} %get-tuple-element.46.refs_13_), channel_id=1, source_target_pairs={{0,2},{1,3},{2,0},{3,1},{4,6},{5,7},{6,4},{7,5},{8,10},{9,11},{10,... | collective-permute-start | bytes 196616 | tf_op jit(solution)/shard_map/ppermute | solution.py:262
  42.5 3.7 %collective-permute-start.23 = (bf16[16,16,128]{2,1,0:T(8,128)(2,1)S(1)}, bf16[16,16,128]{2,1,0:T(8,128)(2,1)S(1)}, u32[]{:S(2)}, u32[]{:S(2)}) collective-permute-start(bf16[16,16,128]{2,1,0:T(8,128)(2,1)S(1)} %get-tuple-element.46.refs_13_), channel_id=1, source_target_pairs={{0,1},{1,0},{2,3},{3,2},{4,5},{5,4},{6,7},{7,6},{8,9},{9,8},{10,11... | collective-permute-start | bytes 196616 | tf_op jit(solution)/shard_map/ppermute | solution.py:262
  46.8 22.5 %collective-permute-start.26 = (bf16[32,16,128]{2,1,0:T(8,128)(2,1)S(1)}, bf16[32,16,128]{2,1,0:T(8,128)(2,1)S(1)}, u32[]{:S(2)}, u32[]{:S(2)}) collective-permute-start(bf16[32,16,128]{2,1,0:T(8,128)(2,1)S(1)} %get-tuple-element.51), channel_id=1, source_target_pairs={{16,24},{20,28},{17,25},{21,29},{18,26},{22,30},{19,27},{23,31}} | collective-permute-start | bytes 393224 | tf_op jit(solution)/shard_map/ppermute | solution.py:326
  71.3 4.0 %collective-permute-start.29 = (bf16[16,16,128]{2,1,0:T(8,128)(2,1)S(1)}, bf16[16,16,128]{2,1,0:T(8,128)(2,1)S(1)}, u32[]{:S(2)}, u32[]{:S(2)}) collective-permute-start(bf16[16,16,128]{2,1,0:T(8,128)(2,1)S(1)} %project.5.refs_13_), channel_id=1, source_target_pairs={{0,3},{1,2},{2,1},{3,0},{4,7},{5,6},{6,5},{7,4},{8,11},{9,10},{10,... | collective-permute-start | bytes 196616 | tf_op jit(solution)/shard_map/ppermute | solution.py:262
  73.0 3.1 %collective-permute-start.28 = (bf16[16,16,128]{2,1,0:T(8,128)(2,1)S(1)}, bf16[16,16,128]{2,1,0:T(8,128)(2,1)S(1)}, u32[]{:S(2)}, u32[]{:S(2)}) collective-permute-start(bf16[16,16,128]{2,1,0:T(8,128)(2,1)S(1)} %project.5.refs_13_), channel_id=1, source_target_pairs={{0,2},{1,3},{2,0},{3,1},{4,6},{5,7},{6,4},{7,5},{8,10},{9,11},{10,... | collective-permute-start | bytes 196616 | tf_op jit(solution)/shard_map/ppermute | solution.py:262
  73.7 3.1 %collective-permute-start.27 = (bf16[16,16,128]{2,1,0:T(8,128)(2,1)S(1)}, bf16[16,16,128]{2,1,0:T(8,128)(2,1)S(1)}, u32[]{:S(2)}, u32[]{:S(2)}) collective-permute-start(bf16[16,16,128]{2,1,0:T(8,128)(2,1)S(1)} %project.5.refs_13_), channel_id=1, source_target_pairs={{0,1},{1,0},{2,3},{3,2},{4,5},{5,4},{6,7},{7,6},{8,9},{9,8},{10,11... | collective-permute-start | bytes 196616 | tf_op jit(solution)/shard_map/ppermute | solution.py:262
  79.6 4.1 %collective-permute-start.32 = (bf16[16,16,128]{2,1,0:T(8,128)(2,1)S(1)}, bf16[16,16,128]{2,1,0:T(8,128)(2,1)S(1)}, u32[]{:S(2)}, u32[]{:S(2)}) collective-permute-start(bf16[16,16,128]{2,1,0:T(8,128)(2,1)S(1)} %get-tuple-element.52.refs_13_), channel_id=1, source_target_pairs={{0,3},{1,2},{2,1},{3,0},{4,7},{5,6},{6,5},{7,4},{8,11},{9,10},{10,... | collective-permute-start | bytes 196616 | tf_op jit(solution)/shard_map/ppermute | solution.py:262
  80.8 3.5 %collective-permute-start.31 = (bf16[16,16,128]{2,1,0:T(8,128)(2,1)S(1)}, bf16[16,16,128]{2,1,0:T(8,128)(2,1)S(1)}, u32[]{:S(2)}, u32[]{:S(2)}) collective-permute-start(bf16[16,16,128]{2,1,0:T(8,128)(2,1)S(1)} %get-tuple-element.52.refs_13_), channel_id=1, source_target_pairs={{0,2},{1,3},{2,0},{3,1},{4,6},{5,7},{6,4},{7,5},{8,10},{9,11},{10,... | collective-permute-start | bytes 196616 | tf_op jit(solution)/shard_map/ppermute | solution.py:262
  81.2 3.1 %collective-permute-start.30 = (bf16[16,16,128]{2,1,0:T(8,128)(2,1)S(1)}, bf16[16,16,128]{2,1,0:T(8,128)(2,1)S(1)}, u32[]{:S(2)}, u32[]{:S(2)}) collective-permute-start(bf16[16,16,128]{2,1,0:T(8,128)(2,1)S(1)} %get-tuple-element.52.refs_13_), channel_id=1, source_target_pairs={{0,1},{1,0},{2,3},{3,2},{4,5},{5,4},{6,7},{7,6},{8,9},{9,8},{10,11... | collective-permute-start | bytes 196616 | tf_op jit(solution)/shard_map/ppermute | solution.py:262
  86.5 15.9 %collective-permute-start.33 = (bf16[32,16,128]{2,1,0:T(8,128)(2,1)S(1)}, bf16[32,16,128]{2,1,0:T(8,128)(2,1)S(1)}, u32[]{:S(2)}, u32[]{:S(2)}) collective-permute-start(bf16[32,16,128]{2,1,0:T(8,128)(2,1)S(1)} %get-tuple-element.58), channel_id=1, source_target_pairs={{0,4},{4,0},{8,12},{12,8},{16,20},{20,16},{24,28},{28,24},{1,5},{5... | collective-permute-start | bytes 393224 | tf_op jit(solution)/shard_map/ppermute | solution.py:254

commit v4 on v3

--- a/solution.py
+++ b/solution.py
@@ -89,16 +89,22 @@
     return [refs[0][(t,) + where] for t in range(refs[0].shape[0])]
 
 
-def weights(pos, notes, terms, w_scr, rays_scr):
+def gather_rays(pos, notes, slot, rays_scr):
+    row_blocks = rays_scr.shape[0] * rays_scr.shape[1]
+    quarter = rays_scr.shape[1]
+    norms = sum(slabs(notes, slot, quarter))[0:row_blocks]
+    if len(notes) > 1:
+        for d, ref in enumerate(notes):
+            rays_scr[pos[2] ^ d] = ref[slot, 0:quarter]
+    else:
+        rays_scr[...] = notes[0][:, slot, 0:quarter]
+    return relaxation / norms
+
+
+def weights(pos, notes, slot, terms, w_scr, rays_scr):
     row_blocks = w_scr.shape[0]
     quarter = rays_scr.shape[1]
-    norms = sum(slabs(notes, quarter))[0:row_blocks]
-    scale = relaxation / norms
-    if len(notes) > 1:
-        for d, ref in enumerate(notes):
-            rays_scr[pos[2] ^ d] = ref[0:quarter]
-    else:
-        rays_scr[...] = notes[0][:, 0:quarter]
+    scale = gather_rays(pos, notes, slot, rays_scr)
     for r in range(row_blocks):
         left = rays_scr[r // quarter, r % quarter]
         if terms is not None:
@@ -145,55 +151,146 @@
     return active
 
 
-def first_kernel(place, n_notes, n_terms, *refs):
+def first_kernel(place, n_notes, *refs):
     refs = list(refs)
     pos, table, table2, blocks, blocks2 = take(refs, 5)
-    notes, notes2 = take(refs, n_notes), take(refs, n_notes)
-    terms_in, image_in = None, None
-    if n_terms:
-        terms_in = take(refs, n_terms)
-        (image_in,) = take(refs, 1)
+    notes = take(refs, n_notes)
     image, shot, terms, w_scr, rays_scr = refs
 
     def run(first, second):
-        weights(pos, first[1], terms_in, w_scr, rays_scr)
-        if n_terms:
-            image[...] = image_in[...].astype(jnp.float32)
-        else:
-            image[...] = jnp.zeros_like(image)
+        weights(pos, notes, first[1], None, w_scr, rays_scr)
+        image[...] = jnp.zeros_like(image)
         back_project(first[0], first[2], w_scr, image)
         shot[...] = image[...].astype(jnp.bfloat16)
         project(second[0], second[2], shot, terms)
 
-    on_core(pos, place, run, (table, notes, blocks), (table2, notes2, blocks2))
+    on_core(pos, place, run, (table, 0, blocks), (table2, 1, blocks2))
 
 
 def second_kernel(place, n_notes, n_terms, *refs):
     refs = list(refs)
-    pos, table, table2, blocks, blocks2 = take(refs, 5)
-    notes, notes2 = take(refs, n_notes), take(refs, n_notes)
+    info, table, table2, blocks, blocks2 = take(refs, 5)
+    pos = [info[0, i] for i in range(3)]
+    notes = take(refs, n_notes)
     terms_in = take(refs, n_terms)
-    image_in, shot, kept_in, given_in = take(refs, 4)
+    image_in, shot = take(refs, 2)
     image, kept, given, w_scr, rays_scr, x_scr = refs
 
     def run(first, second):
-        weights(pos, second[1], terms_in, w_scr, rays_scr)
+        weights(pos, notes, second[1], terms_in, w_scr, rays_scr)
         x_scr[...] = image_in[...]
         back_project(second[0], second[2], w_scr, x_scr)
-        out = x_scr[...].astype(jnp.bfloat16)
-        image[...] = out
+        image[...] = x_scr[...].astype(jnp.bfloat16)
 
         @pl.when(pos[1] == 0)
         def _():
             kept[...] = shot[...]
-            given[...] = out
+            given[...] = image[...]
 
         @pl.when(pos[1] == 1)
         def _():
-            kept[...] = out
+            kept[...] = image[...]
             given[...] = shot[...]
 
-    active = on_core(pos, place, run, (table, notes, blocks), (table2, notes2, blocks2))
+    on_core(pos, place, run, (table, 0, blocks), (table2, 1, blocks2))
+
+
+def pack_kernel(n_notes, *refs):
+    refs = list(refs)
+    pos, table, table2, blocks, blocks2 = take(refs, 5)
+    notes = take(refs, n_notes)
+    _, info, wide, tall, rays, rays_scr = refs
+    row_blocks = wide.shape[1]
+    each = wide.shape[3] // BS
+    quarter = rays_scr.shape[1]
+    for i in range(3):
+        info[0, i] = pos[i]
+
+    @pl.when(pos[0] > 0)
+    def _():
+        for slot, (tab, src) in enumerate(((table, blocks), (table2, blocks2))):
+            at = pos[1] if slot == 0 else 1 - pos[1]
+            scale = gather_rays(pos, notes, slot, rays_scr)
+            for r in range(row_blocks):
+                row = scale[r : r + 1]
+                rays[at, r] = rays_scr[r // quarter, r % quarter] * row
+                rays[at, row_blocks, r : r + 1] = row
+                for j in range(each):
+                    k = r * each + j
+                    info[1 + at, k] = tab[1, k]
+                    block = src[0, 0, tab[0, k]]
+                    wide[at, r, :, j * BS : (j + 1) * BS] = block
+                    tall[at, r, j * BS : (j + 1) * BS] = block.T
+
+
+def packed_weights(rays, slot, terms, w_scr):
+    row_blocks = w_scr.shape[0]
+    for r in range(row_blocks):
+        total = sum(part.astype(jnp.float32) for part in slabs(terms, r))
+        scale = rays[slot, row_blocks, r : r + 1]
+        w_scr[r] = (rays[slot, r] - total * scale).astype(jnp.bfloat16)
+
+
+def packed_back(info, wide, slot, w_scr, image):
+    row_blocks = wide.shape[1]
+    each = wide.shape[3] // BS
+    for r in range(row_blocks):
+        back = dot(w_scr[r], wide[slot, r], NN)
+        for j in range(each):
+            col = info[1 + slot, r * each + j]
+            image[col] = image[col] + back[:, j * BS : (j + 1) * BS]
+
+
+def packed_project(info, tall, slot, image, terms):
+    row_blocks = tall.shape[1]
+    each = tall.shape[2] // BS
+    for r in range(row_blocks):
+        parts = [image[info[1 + slot, r * each + j]] for j in range(each)]
+        total = dot(jnp.concatenate(parts, axis=1), tall[slot, r], NN)
+        terms[r] = total.astype(jnp.bfloat16)
+
+
+def later_first(place, n_terms, *refs):
+    refs = list(refs)
+    info, rays, wide, tall = take(refs, 4)
+    terms_in = take(refs, n_terms)
+    image_in, image, shot, terms, w_scr = refs
+
+    @pl.when(info[0, 0] == place)
+    def _():
+        packed_weights(rays, 0, terms_in, w_scr)
+        image[...] = image_in[...].astype(jnp.float32)
+        packed_back(info, wide, 0, w_scr, image)
+        shot[...] = image[...].astype(jnp.bfloat16)
+        packed_project(info, tall, 1, shot, terms)
+
+
+def later_second(place, n_terms, last, *refs):
+    refs = list(refs)
+    info, rays, wide = take(refs, 3)
+    terms_in = take(refs, n_terms)
+    image_in, shot, kept_in, given_in = take(refs, 4)
+    image = None if last else take(refs, 1)[0]
+    kept, given, w_scr, x_scr = refs
+    active = info[0, 0] == place
+
+    @pl.when(active)
+    def _():
+        packed_weights(rays, 1, terms_in, w_scr)
+        x_scr[...] = image_in[...]
+        packed_back(info, wide, 1, w_scr, x_scr)
+        if not last:
+            image[...] = x_scr[...].astype(jnp.bfloat16)
+
+        @pl.when(info[0, 1] == 0)
+        def _():
+            kept[...] = shot[...]
+            given[...] = x_scr[...].astype(jnp.bfloat16)
+
+        @pl.when(info[0, 1] == 1)
+        def _():
+            kept[...] = x_scr[...].astype(jnp.bfloat16)
+            given[...] = shot[...]
 
     @pl.when(jnp.logical_not(active))
     def _():
@@ -201,11 +298,10 @@
         given[...] = given_in[...]
 
 
-def project_kernel(place, pos, table, table2, image, blocks, blocks2, terms):
-    def run(first, second):
-        project(first[0], first[1], image, terms)
-
-    on_core(pos, place, run, (table, blocks), (table2, blocks2))
+def later_project(place, info, image, tall, terms):
+    @pl.when(info[0, 0] == place)
+    def _():
+        packed_project(info, tall, 0, image, terms)
 
 
 def last_kernel(pos, kept, given, images):
@@ -307,49 +403,82 @@
             for value in (block_rows, block_cols, blocks, sinogram)
         ),
     )
-    notes = spread(note)
-    if direct:
-        notes2 = [turned(note2, d, 1) for d in range(tiles)]
-    else:
-        notes2 = spread(swapped(note2))
+    notes = spread(jnp.stack([note, swapped(note2)]))
     table2 = swapped(table)
     blocks2 = pltpu.with_memory_space_constraint(blocks2, pltpu.VMEM)
-
-    kept = jnp.zeros(image_shape, jnp.bfloat16)
-    given = kept
-    image = None
-    for place in range(places):
-        fixed = [pos, table, table2, blocks, blocks2]
-        extra = []
-        if place > 0:
-            pairs = [(2 * place - 2 + c, 2 * place + c) for c in range(2)]
-            image = lax.ppermute(image, "subset", pairs)
-            terms = call(
-                functools.partial(project_kernel, place),
-                3,
-                [pos, table, table2, image, blocks, blocks2],
-                terms_out,
-                [],
-                "project",
-            )
-            extra = spread(terms) + [image]
+    fixed = [pos, table, table2, blocks, blocks2]
+    image32_out = jax.ShapeDtypeStruct(image_shape, jnp.float32)
+
+    image32, shot, terms = call(
+        functools.partial(first_kernel, 0, len(notes)),
+        3,
+        fixed + notes,
+        (image32_out, image_out, terms_out),
+        [w_scr, rays_scr],
+        "first",
+    )
+    each = count // row_blocks
+    info, wide, tall, rays = pl.pallas_call(
+        functools.partial(pack_kernel, len(notes)),
+        out_shape=(
+            jax.ShapeDtypeStruct((3, count), jnp.int32),
+            pltpu.VMEM((2, row_blocks, BS, each * BS), jnp.bfloat16),
+            pltpu.VMEM((2, row_blocks, each * BS, BS), jnp.bfloat16),
+            jax.ShapeDtypeStruct((2, row_blocks + 1, half, BS), jnp.float32),
+        ),
+        in_specs=[SMEM] * 3 + [VMEM] * (2 + len(notes)) + [pl.BlockSpec(memory_space=pl.ANY)],
+        out_specs=(SMEM, VMEM, VMEM, VMEM),
+        scratch_shapes=[rays_scr],
+        compiler_params=PARAMS,
+        name="pack",
+    )(*fixed, *notes, terms)
+    terms = spread(terms)
+    fixed[0] = info
+    image, kept, given = call(
+        functools.partial(second_kernel, 0, len(notes), len(terms)),
+        3,
+        fixed + notes + terms + [image32, shot],
+        (image_out, image_out, image_out),
+        [w_scr, rays_scr, x_scr],
+        "second",
+    )
+
+    for place in range(1, places):
+        pairs = [
+            (2 * p + c, 2 * ((2 * place - 1 - p) % places) + c)
+            for p in range(places)
+            for c in range(2)
+        ]
+        image = lax.ppermute(image, "subset", pairs)
+        terms = call(
+            functools.partial(later_project, place),
+            1,
+            [info, image, tall],
+            terms_out,
+            [],
+            "project",
+        )
+        terms = spread(terms)
         image32, shot, terms = call(
-            functools.partial(first_kernel, place, len(notes), max(len(extra) - 1, 0)),
-            3,
-            fixed + notes + notes2 + extra,
-            (jax.ShapeDtypeStruct(image_shape, jnp.float32), image_out, terms_out),
-            [w_scr, rays_scr],
+            functools.partial(later_first, place, len(terms)),
+            1,
+            [info, rays, wide, tall] + terms + [image],
+            (image32_out, image_out, terms_out),
+            [w_scr],
             "first",
         )
         terms = spread(terms)
-        image, kept, given = call(
-            functools.partial(second_kernel, place, len(notes), len(terms)),
-            3,
-            fixed + notes + notes2 + terms + [image32, shot, kept, given],
-            (image_out, image_out, image_out),
-            [w_scr, rays_scr, x_scr],
+        last = place == places - 1
+        outs = call(
+            functools.partial(later_second, place, len(terms), last),
+            1,
+            [info, rays, wide] + terms + [image32, shot, kept, given],
+            (image_out,) * (2 if last else 3),
+            [w_scr, x_scr],
             "second",
         )
+        kept, given = outs[-2:]
+        image = outs[0]
     images = call(
         last_kernel,
         1,

time: 104 us -> 95.5 us (0.918)
  waiting for transfers between devices: 43.5 us -> 31 us
  starting transfers between devices: 43.5 us -> 47.4 us
    ppermute x3, waiting for transfers between devices: 21.2 us -> 8.68 us  [per_device(): image = lax.ppermute(image, 'subset', pairs)]
    ppermute x3, starting transfers between devices: 2.63 us -> 7.91 us  [per_device(): image = lax.ppermute(image, 'subset', pairs)]
    ppermute x28 -> x24, starting transfers between devices: 24.8 us -> 21.6 us  [turned(): return lax.ppermute(value, ('subset', 'tile'), pairs)]
    pallas_call x12, Pallas kernels: 13.2 us -> 10.1 us  [call(): pl.pallas_call(kernel, out_shape=out_shape, in_specs=[SMEM] * smem + [VME...]
    pallas_call x0 -> x1, Pallas kernels: none -> 3.16 us  [per_device(): pl.pallas_call(functools.partial(pack_kernel, len(notes)), out_shape=(jax...]
    ppermute x3 -> x4, starting transfers between devices: 16.1 us -> 17.9 us  [swapped(): return lax.ppermute(value, 'subset', [(s, s ^ 1) for s in range(subsets)])]
    ppermute x28 -> x24, waiting for transfers between devices: 20.5 us -> 19.1 us  [turned(): return lax.ppermute(value, ('subset', 'tile'), pairs)]
    ppermute x3 -> x4, waiting for transfers between devices: 1.81 us -> 3.15 us  [swapped(): return lax.ppermute(value, 'subset', [(s, s ^ 1) for s in range(subsets)])]
  transfers between devices with their start and end apart: 34 -> 31, of which waited for: 24 -> 25; matrix products, arithmetic and copies ran while one was open for 0% -> 0% of each run, Pallas kernels for 3% -> 7%
where the time goes in v4:
time: 95.5 us; the launch traced here: 94.9 us
  starting transfers between devices  47.4 us (50%)
  waiting for transfers between devices  31 us (32%)
  Pallas kernels  16.3 us (17%)
    ppermute x24, starting transfers between devices, turned(): return lax.ppermute(value, ('subset', 'tile'), pairs)  21.6 us
    ppermute x24, waiting for transfers between devices, turned(): return lax.ppermute(value, ('subset', 'tile'), pairs)  19.1 us
    ppermute x4, starting transfers between devices, swapped(): return lax.ppermute(value, 'subset', [(s, s ^ 1) for s in range(subsets)])  17.9 us
    pallas_call x12, Pallas kernels, call(): pl.pallas_call(kernel, out_shape=out_shape, in_specs=[SMEM] * smem + [VME...  10.1 us
    ppermute x3, waiting for transfers between devices, per_device(): image = lax.ppermute(image, 'subset', pairs)  8.68 us
    ppermute x3, starting transfers between devices, per_device(): image = lax.ppermute(image, 'subset', pairs)  7.91 us
    pallas_call x1, Pallas kernels, per_device(): pl.pallas_call(functools.partial(pack_kernel, len(notes)), out_shape=(jax...  3.16 us
    ppermute x4, waiting for transfers between devices, swapped(): return lax.ppermute(value, 'subset', [(s, s ^ 1) for s in range(subsets)])  3.15 us
  transfers between devices with their start and end apart: 31, of which 25 were waited for; matrix products, arithmetic and copies ran while one was open for 0% of the time, Pallas kernels for 7%

profile of v4, /device:TPU:25, one launch (start us, length us, event | category | flops | bytes accessed | tf_op | source)
XLA Modules:
  0.0 94.9 jit_solution(8339043491222121742)
XLA Ops:
  0.0 0.7 collective-permute-start.1
  0.8 3.1 %head.1 = (f32[5,16,128]{2,1,0:T(8,128)S(1)}, f32[5,16,128]{2,1,0:T(8,128)S(1)}, s32[2,80]{1,0:T(2,128)S(1)}, bf16[1,1,80,128,128]{4,3,2,1,0:T(8,128)(2,1)S(1)}) custom-call(s32[3]{0:T(128)S(1)} %pad_add_fusion.pos.refs_0_, s32[1,1,80]{2,1,0:T(1,128)} %rows_in.1, s32[1,1,80]{2,1,0:T(1,128)} %cols_in.1, bf16[1,1,80,128,128]{4,3,2,1,0:T(8,128)(2,1)} %blocks_in.1, ...), custom_call_target="tpu_custom_call" | custom-call | tf_op jit(solution)/shard_map/head/pallas_call | solution.py:379
  3.9 1.3 %collective-permute-done.2 = f32[5,16,128]{2,1,0:T(8,128)S(1)} collective-permute-done((f32[5,16,128]{2,1,0:T(8,128)S(1)}, f32[5,16,128]{2,1,0:T(8,128)S(1)}, u32[]{:S(2)}, u32[]{:S(2)}) %collective-permute-start.2) | collective-permute-done | bytes 40992 | tf_op jit(solution)/shard_map/ppermute | solution.py:350
  5.3 1.2 %collective-permute-start.3 = (f32[2,5,16,128]{3,2,1,0:T(8,128)S(1)}, f32[2,5,16,128]{3,2,1,0:T(8,128)S(1)}, u32[]{:S(2)}, u32[]{:S(2)}) collective-permute-start(f32[2,5,16,128]{3,2,1,0:T(8,128)S(1)} %pad_maximum_fusion.refs_5_), channel_id=1, source_target_pairs={{0,1},{1,0},{2,3},{3,2},{4,5},{5,4},{6,7},{7,6},{8,9},{9,8},{10,11... | collective-permute-start | bytes 245768 | tf_op jit(solution)/shard_map/ppermute | solution.py:358
  6.5 1.2 %collective-permute-start.4 = (f32[2,5,16,128]{3,2,1,0:T(8,128)S(1)}, f32[2,5,16,128]{3,2,1,0:T(8,128)S(1)}, u32[]{:S(2)}, u32[]{:S(2)}) collective-permute-start(f32[2,5,16,128]{3,2,1,0:T(8,128)S(1)} %pad_maximum_fusion.refs_5_), channel_id=1, source_target_pairs={{0,2},{1,3},{2,0},{3,1},{4,6},{5,7},{6,4},{7,5},{8,10},{9,11},{10,... | collective-permute-start | bytes 245768 | tf_op jit(solution)/shard_map/ppermute | solution.py:358
  7.9 1.2 %collective-permute-start = (s32[2,80]{1,0:T(2,128)S(1)}, s32[2,80]{1,0:T(2,128)S(1)}, u32[]{:S(2)}, u32[]{:S(2)}) collective-permute-start(s32[2,80]{1,0:T(2,128)S(1)} %get-tuple-element.36.refs_1_), channel_id=1, source_target_pairs={{0,4},{4,0},{8,12},{12,8},{16,20},{20,16},{24,28},{28,24},{1,5},{5... | collective-permute-start | bytes 1928 | tf_op jit(solution)/shard_map/ppermute | solution.py:350
  9.1 0.8 collective-permute-done.refs_2_
  10.0 2.0 %collective-permute-done.5.refs_8_ = f32[2,5,16,128]{3,2,1,0:T(8,128)S(1)} collective-permute-done((f32[2,5,16,128]{3,2,1,0:T(8,128)S(1)}, f32[2,5,16,128]{3,2,1,0:T(8,128)S(1)}, u32[]{:S(2)}, u32[]{:S(2)}) %collective-permute-start.5) | collective-permute-done | bytes 81952 | tf_op jit(solution)/shard_map/ppermute | solution.py:358
  12.5 0.6 collective-permute-start.6
  13.4 1.8 %collective-permute-start.8 = (bf16[16,16,128]{2,1,0:T(8,128)(2,1)S(1)}, bf16[16,16,128]{2,1,0:T(8,128)(2,1)S(1)}, u32[]{:S(2)}, u32[]{:S(2)}) collective-permute-start(bf16[16,16,128]{2,1,0:T(8,128)(2,1)S(1)} %get-tuple-element.40.refs_9_), channel_id=1, source_target_pairs={{0,3},{1,2},{2,1},{3,0},{4,7},{5,6},{6,5},{7,4},{8,11},{9,10},{10,... | collective-permute-start | bytes 196616 | tf_op jit(solution)/shard_map/ppermute | solution.py:358
  15.2 3.2 %pack.1 = (s32[3,80]{1,0:T(4,128)S(1)}, bf16[2,16,128,640]{3,2,1,0:T(8,128)(2,1)S(1)}, bf16[2,16,640,128]{3,2,1,0:T(8,128)(2,1)S(1)}, f32[2,17,16,128]{3,2,1,0:T(8,128)S(1)}) custom-call(s32[3]{0:T(128)S(1)} %pad_add_fusion.pos.refs_0_, s32[2,80]{1,0:T(2,128)S(1)} %get-tuple-element.36.refs_1_, s32[2,80]{1,0:T(2,128)S(1)} %collective-permute-done.refs_2_, ...), custom_call_target="tpu_custom_call" | custom-call | tf_op jit(solution)/shard_map/pack/pallas_call | solution.py:421
  18.4 0.6 second.4
  19.3 3.6 %collective-permute-done.9.image.refs_8_ = bf16[32,16,128]{2,1,0:T(8,128)(2,1)S(1)} collective-permute-done((bf16[32,16,128]{2,1,0:T(8,128)(2,1)S(1)}, bf16[32,16,128]{2,1,0:T(8,128)(2,1)S(1)}, u32[]{:S(2)}, u32[]{:S(2)}) %collective-permute-start.9) | collective-permute-done | bytes 131104 | tf_op jit(solution)/shard_map/ppermute | solution.py:452
  23.5 0.6 collective-permute-start.10
  24.2 1.1 %collective-permute-start.11 = (bf16[16,16,128]{2,1,0:T(8,128)(2,1)S(1)}, bf16[16,16,128]{2,1,0:T(8,128)(2,1)S(1)}, u32[]{:S(2)}, u32[]{:S(2)}) collective-permute-start(bf16[16,16,128]{2,1,0:T(8,128)(2,1)S(1)} %project.3.refs_4_), channel_id=1, source_target_pairs={{0,2},{1,3},{2,0},{3,1},{4,6},{5,7},{6,4},{7,5},{8,10},{9,11},{10,... | collective-permute-start | bytes 196616 | tf_op jit(solution)/shard_map/ppermute | solution.py:358
  25.2 1.0 %collective-permute-start.12 = (bf16[16,16,128]{2,1,0:T(8,128)(2,1)S(1)}, bf16[16,16,128]{2,1,0:T(8,128)(2,1)S(1)}, u32[]{:S(2)}, u32[]{:S(2)}) collective-permute-start(bf16[16,16,128]{2,1,0:T(8,128)(2,1)S(1)} %project.3.refs_4_), channel_id=1, source_target_pairs={{0,3},{1,2},{2,1},{3,0},{4,7},{5,6},{6,5},{7,4},{8,11},{9,10},{10,... | collective-permute-start | bytes 196616 | tf_op jit(solution)/shard_map/ppermute | solution.py:358
  27.3 2.0 %collective-permute-done.12.refs_7_ = bf16[16,16,128]{2,1,0:T(8,128)(2,1)S(1)} collective-permute-done((bf16[16,16,128]{2,1,0:T(8,128)(2,1)S(1)}, bf16[16,16,128]{2,1,0:T(8,128)(2,1)S(1)}, u32[]{:S(2)}, u32[]{:S(2)}) %collective-permute-start.12) | collective-permute-done | bytes 65568 | tf_op jit(solution)/shard_map/ppermute | solution.py:358
  30.1 1.1 %collective-permute-start.14 = (bf16[16,16,128]{2,1,0:T(8,128)(2,1)S(1)}, bf16[16,16,128]{2,1,0:T(8,128)(2,1)S(1)}, u32[]{:S(2)}, u32[]{:S(2)}) collective-permute-start(bf16[16,16,128]{2,1,0:T(8,128)(2,1)S(1)} %get-tuple-element.48.refs_3_), channel_id=1, source_target_pairs={{0,2},{1,3},{2,0},{3,1},{4,6},{5,7},{6,4},{7,5},{8,10},{9,11},{10,... | collective-permute-start | bytes 196616 | tf_op jit(solution)/shard_map/ppermute | solution.py:358
  31.2 1.4 %collective-permute-start.15 = (bf16[16,16,128]{2,1,0:T(8,128)(2,1)S(1)}, bf16[16,16,128]{2,1,0:T(8,128)(2,1)S(1)}, u32[]{:S(2)}, u32[]{:S(2)}) collective-permute-start(bf16[16,16,128]{2,1,0:T(8,128)(2,1)S(1)} %get-tuple-element.48.refs_3_), channel_id=1, source_target_pairs={{0,3},{1,2},{2,1},{3,0},{4,7},{5,6},{6,5},{7,4},{8,11},{9,10},{10,... | collective-permute-start | bytes 196616 | tf_op jit(solution)/shard_map/ppermute | solution.py:358
  33.3 2.1 %collective-permute-done.15.refs_6_ = bf16[16,16,128]{2,1,0:T(8,128)(2,1)S(1)} collective-permute-done((bf16[16,16,128]{2,1,0:T(8,128)(2,1)S(1)}, bf16[16,16,128]{2,1,0:T(8,128)(2,1)S(1)}, u32[]{:S(2)}, u32[]{:S(2)}) %collective-permute-start.15) | collective-permute-done | bytes 65568 | tf_op jit(solution)/shard_map/ppermute | solution.py:358
  35.4 0.6 second.5
  36.0 3.1 %collective-permute-start.16 = (bf16[32,16,128]{2,1,0:T(8,128)(2,1)S(1)}, bf16[32,16,128]{2,1,0:T(8,128)(2,1)S(1)}, u32[]{:S(2)}, u32[]{:S(2)}) collective-permute-start(bf16[32,16,128]{2,1,0:T(8,128)(2,1)S(1)} %get-tuple-element.53), channel_id=1, source_target_pairs={{0,24},{4,28},{8,16},{12,20},{16,8},{20,12},{24,0},{28,4},{1,25},{... | collective-permute-start | bytes 393224 | tf_op jit(solution)/shard_map/ppermute | solution.py:452
  39.1 2.7 %collective-permute-done.16.image.refs_8_ = bf16[32,16,128]{2,1,0:T(8,128)(2,1)S(1)} collective-permute-done((bf16[32,16,128]{2,1,0:T(8,128)(2,1)S(1)}, bf16[32,16,128]{2,1,0:T(8,128)(2,1)S(1)}, u32[]{:S(2)}, u32[]{:S(2)}) %collective-permute-start.16) | collective-permute-done | bytes 131104 | tf_op jit(solution)/shard_map/ppermute | solution.py:452
  41.7 0.8 project.4.refs_4_
  42.5 0.6 collective-permute-start.17
  43.1 0.9 collective-permute-start.18
  44.0 1.2 %collective-permute-start.19 = (bf16[16,16,128]{2,1,0:T(8,128)(2,1)S(1)}, bf16[16,16,128]{2,1,0:T(8,128)(2,1)S(1)}, u32[]{:S(2)}, u32[]{:S(2)}) collective-permute-start(bf16[16,16,128]{2,1,0:T(8,128)(2,1)S(1)} %project.4.refs_4_), channel_id=1, source_target_pairs={{0,3},{1,2},{2,1},{3,0},{4,7},{5,6},{6,5},{7,4},{8,11},{9,10},{10,... | collective-permute-start | bytes 196616 | tf_op jit(solution)/shard_map/ppermute | solution.py:358
  46.2 2.1 %collective-permute-done.19.refs_7_ = bf16[16,16,128]{2,1,0:T(8,128)(2,1)S(1)} collective-permute-done((bf16[16,16,128]{2,1,0:T(8,128)(2,1)S(1)}, bf16[16,16,128]{2,1,0:T(8,128)(2,1)S(1)}, u32[]{:S(2)}, u32[]{:S(2)}) %collective-permute-start.19) | collective-permute-done | bytes 65568 | tf_op jit(solution)/shard_map/ppermute | solution.py:358
  49.3 0.9 collective-permute-start.21
  50.2 1.5 %collective-permute-start.22 = (bf16[16,16,128]{2,1,0:T(8,128)(2,1)S(1)}, bf16[16,16,128]{2,1,0:T(8,128)(2,1)S(1)}, u32[]{:S(2)}, u32[]{:S(2)}) collective-permute-start(bf16[16,16,128]{2,1,0:T(8,128)(2,1)S(1)} %get-tuple-element.54.refs_3_), channel_id=1, source_target_pairs={{0,3},{1,2},{2,1},{3,0},{4,7},{5,6},{6,5},{7,4},{8,11},{9,10},{10,... | collective-permute-start | bytes 196616 | tf_op jit(solution)/shard_map/ppermute | solution.py:358
  52.4 1.8 %collective-permute-done.22.refs_6_ = bf16[16,16,128]{2,1,0:T(8,128)(2,1)S(1)} collective-permute-done((bf16[16,16,128]{2,1,0:T(8,128)(2,1)S(1)}, bf16[16,16,128]{2,1,0:T(8,128)(2,1)S(1)}, u32[]{:S(2)}, u32[]{:S(2)}) %collective-permute-start.22) | collective-permute-done | bytes 65568 | tf_op jit(solution)/shard_map/ppermute | solution.py:358
  54.2 0.6 second.6
  54.8 4.6 %collective-permute-start.23 = (bf16[32,16,128]{2,1,0:T(8,128)(2,1)S(1)}, bf16[32,16,128]{2,1,0:T(8,128)(2,1)S(1)}, u32[]{:S(2)}, u32[]{:S(2)}) collective-permute-start(bf16[32,16,128]{2,1,0:T(8,128)(2,1)S(1)} %get-tuple-element.59), channel_id=1, source_target_pairs={{0,8},{4,12},{8,0},{12,4},{16,24},{20,28},{24,16},{28,20},{1,9},{5... | collective-permute-start | bytes 393224 | tf_op jit(solution)/shard_map/ppermute | solution.py:452
  59.3 2.4 %collective-permute-done.23.image.refs_8_ = bf16[32,16,128]{2,1,0:T(8,128)(2,1)S(1)} collective-permute-done((bf16[32,16,128]{2,1,0:T(8,128)(2,1)S(1)}, bf16[32,16,128]{2,1,0:T(8,128)(2,1)S(1)}, u32[]{:S(2)}, u32[]{:S(2)}) %collective-permute-start.23) | collective-permute-done | bytes 131104 | tf_op jit(solution)/shard_map/ppermute | solution.py:452
  61.7 1.1 %project.5.refs_4_ = bf16[16,16,128]{2,1,0:T(8,128)(2,1)S(1)} custom-call(s32[3,80]{1,0:T(4,128)S(1)} %get-tuple-element.41.refs_0_.info, bf16[32,16,128]{2,1,0:T(8,128)(2,1)S(1)} %collective-permute-done.23.image.refs_8_, bf16[2,16,640,128]{3,2,1,0:T(8,128)(2,1)S(1)} %get-tuple-element.44.tall.refs_3_), custom_call_target="tpu_custom_call" | custom-call | tf_op jit(solution)/shard_map/project/pallas_call | solution.py:367
  62.9 1.4 %collective-permute-start.25 = (bf16[16,16,128]{2,1,0:T(8,128)(2,1)S(1)}, bf16[16,16,128]{2,1,0:T(8,128)(2,1)S(1)}, u32[]{:S(2)}, u32[]{:S(2)}) collective-permute-start(bf16[16,16,128]{2,1,0:T(8,128)(2,1)S(1)} %project.5.refs_4_), channel_id=1, source_target_pairs={{0,2},{1,3},{2,0},{3,1},{4,6},{5,7},{6,4},{7,5},{8,10},{9,11},{10,... | collective-permute-start | bytes 196616 | tf_op jit(solution)/shard_map/ppermute | solution.py:358
  64.2 1.3 %collective-permute-start.26 = (bf16[16,16,128]{2,1,0:T(8,128)(2,1)S(1)}, bf16[16,16,128]{2,1,0:T(8,128)(2,1)S(1)}, u32[]{:S(2)}, u32[]{:S(2)}) collective-permute-start(bf16[16,16,128]{2,1,0:T(8,128)(2,1)S(1)} %project.5.refs_4_), channel_id=1, source_target_pairs={{0,3},{1,2},{2,1},{3,0},{4,7},{5,6},{6,5},{7,4},{8,11},{9,10},{10,... | collective-permute-start | bytes 196616 | tf_op jit(solution)/shard_map/ppermute | solution.py:358
  66.1 2.2 %collective-permute-done.26.refs_7_ = bf16[16,16,128]{2,1,0:T(8,128)(2,1)S(1)} collective-permute-done((bf16[16,16,128]{2,1,0:T(8,128)(2,1)S(1)}, bf16[16,16,128]{2,1,0:T(8,128)(2,1)S(1)}, u32[]{:S(2)}, u32[]{:S(2)}) %collective-permute-start.26) | collective-permute-done | bytes 65568 | tf_op jit(solution)/shard_map/ppermute | solution.py:358
  68.3 1.7 %first.7 = (f32[32,16,128]{2,1,0:T(8,128)S(1)}, bf16[32,16,128]{2,1,0:T(8,128)(2,1)S(1)}, bf16[16,16,128]{2,1,0:T(8,128)(2,1)S(1)}) custom-call(s32[3,80]{1,0:T(4,128)S(1)} %get-tuple-element.41.refs_0_.info, f32[2,17,16,128]{3,2,1,0:T(8,128)S(1)} %get-tuple-element.42.refs_1_, bf16[2,16,128,640]{3,2,1,0:T(8,128)(2,1)S(1)} %get-tuple-element.43.refs_2_, ...), custom_call_target="tpu_custom_call" | custom-call | tf_op jit(solution)/shard_map/first/pallas_call | solution.py:367
  69.9 0.7 collective-permute-start.27
  70.7 0.9 collective-permute-start.28
  71.5 1.1 %collective-permute-start.29 = (bf16[16,16,128]{2,1,0:T(8,128)(2,1)S(1)}, bf16[16,16,128]{2,1,0:T(8,128)(2,1)S(1)}, u32[]{:S(2)}, u32[]{:S(2)}) collective-permute-start(bf16[16,16,128]{2,1,0:T(8,128)(2,1)S(1)} %get-tuple-element.60.refs_3_), channel_id=1, source_target_pairs={{0,3},{1,2},{2,1},{3,0},{4,7},{5,6},{6,5},{7,4},{8,11},{9,10},{10,... | collective-permute-start | bytes 196616 | tf_op jit(solution)/shard_map/ppermute | solution.py:358
  72.6 0.8 collective-permute-done.27.refs_4_
  73.8 1.8 %collective-permute-done.29.refs_6_ = bf16[16,16,128]{2,1,0:T(8,128)(2,1)S(1)} collective-permute-done((bf16[16,16,128]{2,1,0:T(8,128)(2,1)S(1)}, bf16[16,16,128]{2,1,0:T(8,128)(2,1)S(1)}, u32[]{:S(2)}, u32[]{:S(2)}) %collective-permute-start.29) | collective-permute-done | bytes 65568 | tf_op jit(solution)/shard_map/ppermute | solution.py:358
  75.5 1.2 %second.7 = (bf16[32,16,128]{2,1,0:T(8,128)(2,1)S(1)}, bf16[32,16,128]{2,1,0:T(8,128)(2,1)S(1)}) custom-call(s32[3,80]{1,0:T(4,128)S(1)} %get-tuple-element.41.refs_0_.info, f32[2,17,16,128]{3,2,1,0:T(8,128)S(1)} %get-tuple-element.42.refs_1_, bf16[2,16,128,640]{3,2,1,0:T(8,128)(2,1)S(1)} %get-tuple-element.43.refs_2_, ...), custom_call_target="tpu_custom_call" | custom-call | tf_op jit(solution)/shard_map/second/pallas_call | solution.py:367
  76.7 15.9 %collective-permute-start.30 = (bf16[32,16,128]{2,1,0:T(8,128)(2,1)S(1)}, bf16[32,16,128]{2,1,0:T(8,128)(2,1)S(1)}, u32[]{:S(2)}, u32[]{:S(2)}) collective-permute-start(bf16[32,16,128]{2,1,0:T(8,128)(2,1)S(1)} %get-tuple-element.66), channel_id=1, source_target_pairs={{0,4},{4,0},{8,12},{12,8},{16,20},{20,16},{24,28},{28,24},{1,5},{5... | collective-permute-start | bytes 393224 | tf_op jit(solution)/shard_map/ppermute | solution.py:350
  92.6 1.0 %collective-permute-done.30.given = bf16[32,16,128]{2,1,0:T(8,128)(2,1)S(1)} collective-permute-done((bf16[32,16,128]{2,1,0:T(8,128)(2,1)S(1)}, bf16[32,16,128]{2,1,0:T(8,128)(2,1)S(1)}, u32[]{:S(2)}, u32[]{:S(2)}) %collective-permute-start.30) | collective-permute-done | bytes 131104 | tf_op jit(solution)/shard_map/ppermute | solution.py:350
  93.6 1.3 %last.1 = bf16[4,8,4096]{2,1,0:T(8,128)(2,1)} custom-call(s32[3]{0:T(128)S(1)} %pad_add_fusion.pos.refs_0_, bf16[32,16,128]{2,1,0:T(8,128)(2,1)S(1)} %get-tuple-element.65.kept, bf16[32,16,128]{2,1,0:T(8,128)(2,1)S(1)} %collective-permute-done.30.given), custom_call_target="tpu_custom_call" | custom-call | tf_op jit(solution)/shard_map/last/pallas_call | solution.py:367
  (30 shorter events, 8.4 us)
Async XLA Ops:
  0.0 11.9 %collective-permute-start.1 = (bf16[1,1,80,128,128]{4,3,2,1,0:T(8,128)(2,1)}, bf16[1,1,80,128,128]{4,3,2,1,0:T(8,128)(2,1)S(1)}, u32[]{:S(2)}, u32[]{:S(2)}) collective-permute-start(bf16[1,1,80,128,128]{4,3,2,1,0:T(8,128)(2,1)} %blocks_in.1), channel_id=1, source_target_pairs={{0,4},{4,0},{8,12},{12,8},{16,20},{20,16},{24,28},{28,24},{1,5},{5... | collective-permute-start | bytes 7864328 | tf_op jit(solution)/shard_map/ppermute | solution.py:350
  3.8 1.4 %collective-permute-start.2 = (f32[5,16,128]{2,1,0:T(8,128)S(1)}, f32[5,16,128]{2,1,0:T(8,128)S(1)}, u32[]{:S(2)}, u32[]{:S(2)}) collective-permute-start(f32[5,16,128]{2,1,0:T(8,128)S(1)} %get-tuple-element.39), channel_id=1, source_target_pairs={{0,4},{4,0},{8,12},{12,8},{16,20},{20,16},{24,28},{28,24},{1,5},{5... | collective-permute-start | bytes 122888 | tf_op jit(solution)/shard_map/ppermute | solution.py:350
  5.3 4.7 %collective-permute-start.3 = (f32[2,5,16,128]{3,2,1,0:T(8,128)S(1)}, f32[2,5,16,128]{3,2,1,0:T(8,128)S(1)}, u32[]{:S(2)}, u32[]{:S(2)}) collective-permute-start(f32[2,5,16,128]{3,2,1,0:T(8,128)S(1)} %pad_maximum_fusion.refs_5_), channel_id=1, source_target_pairs={{0,1},{1,0},{2,3},{3,2},{4,5},{5,4},{6,7},{7,6},{8,9},{9,8},{10,11... | collective-permute-start | bytes 245768 | tf_op jit(solution)/shard_map/ppermute | solution.py:358
  6.5 3.5 %collective-permute-start.4 = (f32[2,5,16,128]{3,2,1,0:T(8,128)S(1)}, f32[2,5,16,128]{3,2,1,0:T(8,128)S(1)}, u32[]{:S(2)}, u32[]{:S(2)}) collective-permute-start(f32[2,5,16,128]{3,2,1,0:T(8,128)S(1)} %pad_maximum_fusion.refs_5_), channel_id=1, source_target_pairs={{0,2},{1,3},{2,0},{3,1},{4,6},{5,7},{6,4},{7,5},{8,10},{9,11},{10,... | collective-permute-start | bytes 245768 | tf_op jit(solution)/shard_map/ppermute | solution.py:358
  7.7 4.2 %collective-permute-start.5 = (f32[2,5,16,128]{3,2,1,0:T(8,128)S(1)}, f32[2,5,16,128]{3,2,1,0:T(8,128)S(1)}, u32[]{:S(2)}, u32[]{:S(2)}) collective-permute-start(f32[2,5,16,128]{3,2,1,0:T(8,128)S(1)} %pad_maximum_fusion.refs_5_), channel_id=1, source_target_pairs={{0,3},{1,2},{2,1},{3,0},{4,7},{5,6},{6,5},{7,4},{8,11},{9,10},{10,... | collective-permute-start | bytes 245768 | tf_op jit(solution)/shard_map/ppermute | solution.py:358
  7.9 2.0 %collective-permute-start = (s32[2,80]{1,0:T(2,128)S(1)}, s32[2,80]{1,0:T(2,128)S(1)}, u32[]{:S(2)}, u32[]{:S(2)}) collective-permute-start(s32[2,80]{1,0:T(2,128)S(1)} %get-tuple-element.36.refs_1_), channel_id=1, source_target_pairs={{0,4},{4,0},{8,12},{12,8},{16,20},{20,16},{24,28},{28,24},{1,5},{5... | collective-permute-start | bytes 1928 | tf_op jit(solution)/shard_map/ppermute | solution.py:350
  12.5 5.9 %collective-permute-start.6 = (bf16[16,16,128]{2,1,0:T(8,128)(2,1)S(1)}, bf16[16,16,128]{2,1,0:T(8,128)(2,1)S(1)}, u32[]{:S(2)}, u32[]{:S(2)}) collective-permute-start(bf16[16,16,128]{2,1,0:T(8,128)(2,1)S(1)} %get-tuple-element.40.refs_9_), channel_id=1, source_target_pairs={{0,1},{1,0},{2,3},{3,2},{4,5},{5,4},{6,7},{7,6},{8,9},{9,8},{10,11... | collective-permute-start | bytes 196616 | tf_op jit(solution)/shard_map/ppermute | solution.py:358
  13.2 5.3 %collective-permute-start.7 = (bf16[16,16,128]{2,1,0:T(8,128)(2,1)S(1)}, bf16[16,16,128]{2,1,0:T(8,128)(2,1)S(1)}, u32[]{:S(2)}, u32[]{:S(2)}) collective-permute-start(bf16[16,16,128]{2,1,0:T(8,128)(2,1)S(1)} %get-tuple-element.40.refs_9_), channel_id=1, source_target_pairs={{0,2},{1,3},{2,0},{3,1},{4,6},{5,7},{6,4},{7,5},{8,10},{9,11},{10,... | collective-permute-start | bytes 196616 | tf_op jit(solution)/shard_map/ppermute | solution.py:358
  13.4 5.0 %collective-permute-start.8 = (bf16[16,16,128]{2,1,0:T(8,128)(2,1)S(1)}, bf16[16,16,128]{2,1,0:T(8,128)(2,1)S(1)}, u32[]{:S(2)}, u32[]{:S(2)}) collective-permute-start(bf16[16,16,128]{2,1,0:T(8,128)(2,1)S(1)} %get-tuple-element.40.refs_9_), channel_id=1, source_target_pairs={{0,3},{1,2},{2,1},{3,0},{4,7},{5,6},{6,5},{7,4},{8,11},{9,10},{10,... | collective-permute-start | bytes 196616 | tf_op jit(solution)/shard_map/ppermute | solution.py:358
  19.1 3.9 %collective-permute-start.9 = (bf16[32,16,128]{2,1,0:T(8,128)(2,1)S(1)}, bf16[32,16,128]{2,1,0:T(8,128)(2,1)S(1)}, u32[]{:S(2)}, u32[]{:S(2)}) collective-permute-start(bf16[32,16,128]{2,1,0:T(8,128)(2,1)S(1)} %get-tuple-element.47), channel_id=1, source_target_pairs={{0,8},{4,12},{8,0},{12,4},{16,24},{20,28},{24,16},{28,20},{1,9},{5... | collective-permute-start | bytes 393224 | tf_op jit(solution)/shard_map/ppermute | solution.py:452
  23.5 3.2 %collective-permute-start.10 = (bf16[16,16,128]{2,1,0:T(8,128)(2,1)S(1)}, bf16[16,16,128]{2,1,0:T(8,128)(2,1)S(1)}, u32[]{:S(2)}, u32[]{:S(2)}) collective-permute-start(bf16[16,16,128]{2,1,0:T(8,128)(2,1)S(1)} %project.3.refs_4_), channel_id=1, source_target_pairs={{0,1},{1,0},{2,3},{3,2},{4,5},{5,4},{6,7},{7,6},{8,9},{9,8},{10,11... | collective-permute-start | bytes 196616 | tf_op jit(solution)/shard_map/ppermute | solution.py:358
  24.2 3.1 %collective-permute-start.11 = (bf16[16,16,128]{2,1,0:T(8,128)(2,1)S(1)}, bf16[16,16,128]{2,1,0:T(8,128)(2,1)S(1)}, u32[]{:S(2)}, u32[]{:S(2)}) collective-permute-start(bf16[16,16,128]{2,1,0:T(8,128)(2,1)S(1)} %project.3.refs_4_), channel_id=1, source_target_pairs={{0,2},{1,3},{2,0},{3,1},{4,6},{5,7},{6,4},{7,5},{8,10},{9,11},{10,... | collective-permute-start | bytes 196616 | tf_op jit(solution)/shard_map/ppermute | solution.py:358
  25.2 4.0 %collective-permute-start.12 = (bf16[16,16,128]{2,1,0:T(8,128)(2,1)S(1)}, bf16[16,16,128]{2,1,0:T(8,128)(2,1)S(1)}, u32[]{:S(2)}, u32[]{:S(2)}) collective-permute-start(bf16[16,16,128]{2,1,0:T(8,128)(2,1)S(1)} %project.3.refs_4_), channel_id=1, source_target_pairs={{0,3},{1,2},{2,1},{3,0},{4,7},{5,6},{6,5},{7,4},{8,11},{9,10},{10,... | collective-permute-start | bytes 196616 | tf_op jit(solution)/shard_map/ppermute | solution.py:358
  29.8 3.2 %collective-permute-start.13 = (bf16[16,16,128]{2,1,0:T(8,128)(2,1)S(1)}, bf16[16,16,128]{2,1,0:T(8,128)(2,1)S(1)}, u32[]{:S(2)}, u32[]{:S(2)}) collective-permute-start(bf16[16,16,128]{2,1,0:T(8,128)(2,1)S(1)} %get-tuple-element.48.refs_3_), channel_id=1, source_target_pairs={{0,1},{1,0},{2,3},{3,2},{4,5},{5,4},{6,7},{7,6},{8,9},{9,8},{10,11... | collective-permute-start | bytes 196616 | tf_op jit(solution)/shard_map/ppermute | solution.py:358
  30.1 3.2 %collective-permute-start.14 = (bf16[16,16,128]{2,1,0:T(8,128)(2,1)S(1)}, bf16[16,16,128]{2,1,0:T(8,128)(2,1)S(1)}, u32[]{:S(2)}, u32[]{:S(2)}) collective-permute-start(bf16[16,16,128]{2,1,0:T(8,128)(2,1)S(1)} %get-tuple-element.48.refs_3_), channel_id=1, source_target_pairs={{0,2},{1,3},{2,0},{3,1},{4,6},{5,7},{6,4},{7,5},{8,10},{9,11},{10,... | collective-permute-start | bytes 196616 | tf_op jit(solution)/shard_map/ppermute | solution.py:358
  31.2 4.2 %collective-permute-start.15 = (bf16[16,16,128]{2,1,0:T(8,128)(2,1)S(1)}, bf16[16,16,128]{2,1,0:T(8,128)(2,1)S(1)}, u32[]{:S(2)}, u32[]{:S(2)}) collective-permute-start(bf16[16,16,128]{2,1,0:T(8,128)(2,1)S(1)} %get-tuple-element.48.refs_3_), channel_id=1, source_target_pairs={{0,3},{1,2},{2,1},{3,0},{4,7},{5,6},{6,5},{7,4},{8,11},{9,10},{10,... | collective-permute-start | bytes 196616 | tf_op jit(solution)/shard_map/ppermute | solution.py:358
  36.0 5.8 %collective-permute-start.16 = (bf16[32,16,128]{2,1,0:T(8,128)(2,1)S(1)}, bf16[32,16,128]{2,1,0:T(8,128)(2,1)S(1)}, u32[]{:S(2)}, u32[]{:S(2)}) collective-permute-start(bf16[32,16,128]{2,1,0:T(8,128)(2,1)S(1)} %get-tuple-element.53), channel_id=1, source_target_pairs={{0,24},{4,28},{8,16},{12,20},{16,8},{20,12},{24,0},{28,4},{1,25},{... | collective-permute-start | bytes 393224 | tf_op jit(solution)/shard_map/ppermute | solution.py:452
  42.5 3.2 %collective-permute-start.17 = (bf16[16,16,128]{2,1,0:T(8,128)(2,1)S(1)}, bf16[16,16,128]{2,1,0:T(8,128)(2,1)S(1)}, u32[]{:S(2)}, u32[]{:S(2)}) collective-permute-start(bf16[16,16,128]{2,1,0:T(8,128)(2,1)S(1)} %project.4.refs_4_), channel_id=1, source_target_pairs={{0,1},{1,0},{2,3},{3,2},{4,5},{5,4},{6,7},{7,6},{8,9},{9,8},{10,11... | collective-permute-start | bytes 196616 | tf_op jit(solution)/shard_map/ppermute | solution.py:358
  43.1 3.1 %collective-permute-start.18 = (bf16[16,16,128]{2,1,0:T(8,128)(2,1)S(1)}, bf16[16,16,128]{2,1,0:T(8,128)(2,1)S(1)}, u32[]{:S(2)}, u32[]{:S(2)}) collective-permute-start(bf16[16,16,128]{2,1,0:T(8,128)(2,1)S(1)} %project.4.refs_4_), channel_id=1, source_target_pairs={{0,2},{1,3},{2,0},{3,1},{4,6},{5,7},{6,4},{7,5},{8,10},{9,11},{10,... | collective-permute-start | bytes 196616 | tf_op jit(solution)/shard_map/ppermute | solution.py:358
  44.0 4.3 %collective-permute-start.19 = (bf16[16,16,128]{2,1,0:T(8,128)(2,1)S(1)}, bf16[16,16,128]{2,1,0:T(8,128)(2,1)S(1)}, u32[]{:S(2)}, u32[]{:S(2)}) collective-permute-start(bf16[16,16,128]{2,1,0:T(8,128)(2,1)S(1)} %project.4.refs_4_), channel_id=1, source_target_pairs={{0,3},{1,2},{2,1},{3,0},{4,7},{5,6},{6,5},{7,4},{8,11},{9,10},{10,... | collective-permute-start | bytes 196616 | tf_op jit(solution)/shard_map/ppermute | solution.py:358
  48.9 3.2 %collective-permute-start.20 = (bf16[16,16,128]{2,1,0:T(8,128)(2,1)S(1)}, bf16[16,16,128]{2,1,0:T(8,128)(2,1)S(1)}, u32[]{:S(2)}, u32[]{:S(2)}) collective-permute-start(bf16[16,16,128]{2,1,0:T(8,128)(2,1)S(1)} %get-tuple-element.54.refs_3_), channel_id=1, source_target_pairs={{0,1},{1,0},{2,3},{3,2},{4,5},{5,4},{6,7},{7,6},{8,9},{9,8},{10,11... | collective-permute-start | bytes 196616 | tf_op jit(solution)/shard_map/ppermute | solution.py:358
  49.3 3.1 %collective-permute-start.21 = (bf16[16,16,128]{2,1,0:T(8,128)(2,1)S(1)}, bf16[16,16,128]{2,1,0:T(8,128)(2,1)S(1)}, u32[]{:S(2)}, u32[]{:S(2)}) collective-permute-start(bf16[16,16,128]{2,1,0:T(8,128)(2,1)S(1)} %get-tuple-element.54.refs_3_), channel_id=1, source_target_pairs={{0,2},{1,3},{2,0},{3,1},{4,6},{5,7},{6,4},{7,5},{8,10},{9,11},{10,... | collective-permute-start | bytes 196616 | tf_op jit(solution)/shard_map/ppermute | solution.py:358
  50.2 4.0 %collective-permute-start.22 = (bf16[16,16,128]{2,1,0:T(8,128)(2,1)S(1)}, bf16[16,16,128]{2,1,0:T(8,128)(2,1)S(1)}, u32[]{:S(2)}, u32[]{:S(2)}) collective-permute-start(bf16[16,16,128]{2,1,0:T(8,128)(2,1)S(1)} %get-tuple-element.54.refs_3_), channel_id=1, source_target_pairs={{0,3},{1,2},{2,1},{3,0},{4,7},{5,6},{6,5},{7,4},{8,11},{9,10},{10,... | collective-permute-start | bytes 196616 | tf_op jit(solution)/shard_map/ppermute | solution.py:358
  54.8 6.9 %collective-permute-start.23 = (bf16[32,16,128]{2,1,0:T(8,128)(2,1)S(1)}, bf16[32,16,128]{2,1,0:T(8,128)(2,1)S(1)}, u32[]{:S(2)}, u32[]{:S(2)}) collective-permute-start(bf16[32,16,128]{2,1,0:T(8,128)(2,1)S(1)} %get-tuple-element.59), channel_id=1, source_target_pairs={{0,8},{4,12},{8,0},{12,4},{16,24},{20,28},{24,16},{28,20},{1,9},{5... | collective-permute-start | bytes 393224 | tf_op jit(solution)/shard_map/ppermute | solution.py:452
  62.8 3.2 %collective-permute-start.24 = (bf16[16,16,128]{2,1,0:T(8,128)(2,1)S(1)}, bf16[16,16,128]{2,1,0:T(8,128)(2,1)S(1)}, u32[]{:S(2)}, u32[]{:S(2)}) collective-permute-start(bf16[16,16,128]{2,1,0:T(8,128)(2,1)S(1)} %project.5.refs_4_), channel_id=1, source_target_pairs={{0,1},{1,0},{2,3},{3,2},{4,5},{5,4},{6,7},{7,6},{8,9},{9,8},{10,11... | collective-permute-start | bytes 196616 | tf_op jit(solution)/shard_map/ppermute | solution.py:358
  62.9 3.2 %collective-permute-start.25 = (bf16[16,16,128]{2,1,0:T(8,128)(2,1)S(1)}, bf16[16,16,128]{2,1,0:T(8,128)(2,1)S(1)}, u32[]{:S(2)}, u32[]{:S(2)}) collective-permute-start(bf16[16,16,128]{2,1,0:T(8,128)(2,1)S(1)} %project.5.refs_4_), channel_id=1, source_target_pairs={{0,2},{1,3},{2,0},{3,1},{4,6},{5,7},{6,4},{7,5},{8,10},{9,11},{10,... | collective-permute-start | bytes 196616 | tf_op jit(solution)/shard_map/ppermute | solution.py:358
  64.2 4.0 %collective-permute-start.26 = (bf16[16,16,128]{2,1,0:T(8,128)(2,1)S(1)}, bf16[16,16,128]{2,1,0:T(8,128)(2,1)S(1)}, u32[]{:S(2)}, u32[]{:S(2)}) collective-permute-start(bf16[16,16,128]{2,1,0:T(8,128)(2,1)S(1)} %project.5.refs_4_), channel_id=1, source_target_pairs={{0,3},{1,2},{2,1},{3,0},{4,7},{5,6},{6,5},{7,4},{8,11},{9,10},{10,... | collective-permute-start | bytes 196616 | tf_op jit(solution)/shard_map/ppermute | solution.py:358
  69.9 3.5 %collective-permute-start.27 = (bf16[16,16,128]{2,1,0:T(8,128)(2,1)S(1)}, bf16[16,16,128]{2,1,0:T(8,128)(2,1)S(1)}, u32[]{:S(2)}, u32[]{:S(2)}) collective-permute-start(bf16[16,16,128]{2,1,0:T(8,128)(2,1)S(1)} %get-tuple-element.60.refs_3_), channel_id=1, source_target_pairs={{0,1},{1,0},{2,3},{3,2},{4,5},{5,4},{6,7},{7,6},{8,9},{9,8},{10,11... | collective-permute-start | bytes 196616 | tf_op jit(solution)/shard_map/ppermute | solution.py:358
  70.7 3.1 %collective-permute-start.28 = (bf16[16,16,128]{2,1,0:T(8,128)(2,1)S(1)}, bf16[16,16,128]{2,1,0:T(8,128)(2,1)S(1)}, u32[]{:S(2)}, u32[]{:S(2)}) collective-permute-start(bf16[16,16,128]{2,1,0:T(8,128)(2,1)S(1)} %get-tuple-element.60.refs_3_), channel_id=1, source_target_pairs={{0,2},{1,3},{2,0},{3,1},{4,6},{5,7},{6,4},{7,5},{8,10},{9,11},{10,... | collective-permute-start | bytes 196616 | tf_op jit(solution)/shard_map/ppermute | solution.py:358
  71.5 4.0 %collective-permute-start.29 = (bf16[16,16,128]{2,1,0:T(8,128)(2,1)S(1)}, bf16[16,16,128]{2,1,0:T(8,128)(2,1)S(1)}, u32[]{:S(2)}, u32[]{:S(2)}) collective-permute-start(bf16[16,16,128]{2,1,0:T(8,128)(2,1)S(1)} %get-tuple-element.60.refs_3_), channel_id=1, source_target_pairs={{0,3},{1,2},{2,1},{3,0},{4,7},{5,6},{6,5},{7,4},{8,11},{9,10},{10,... | collective-permute-start | bytes 196616 | tf_op jit(solution)/shard_map/ppermute | solution.py:358
  76.7 16.9 %collective-permute-start.30 = (bf16[32,16,128]{2,1,0:T(8,128)(2,1)S(1)}, bf16[32,16,128]{2,1,0:T(8,128)(2,1)S(1)}, u32[]{:S(2)}, u32[]{:S(2)}) collective-permute-start(bf16[32,16,128]{2,1,0:T(8,128)(2,1)S(1)} %get-tuple-element.66), channel_id=1, source_target_pairs={{0,4},{4,0},{8,12},{12,8},{16,20},{20,16},{24,28},{28,24},{1,5},{5... | collective-permute-start | bytes 393224 | tf_op jit(solution)/shard_map/ppermute | solution.py:350

commit v5 on v4

--- a/solution.py
+++ b/solution.py
@@ -11,8 +11,6 @@
 PIX = 4096
 CB = PIX // BS
 relaxation = 0.5
-
-DIRECT = 4
 
 NN = (((1,), (0,)), ((), ()))
 NT = (((1,), (1,)), ((), ()))
@@ -122,13 +120,15 @@
 
 
 def project(table, blocks, image, terms):
-    row_blocks = terms.shape[0]
+    tiles, row_blocks, _, _ = terms.shape
     each = blocks.shape[2] // row_blocks
     for r in range(row_blocks):
         total = 0.0
         for k in range(r * each, (r + 1) * each):
             total = total + dot(image[table[1, k]], blocks[0, 0, table[0, k]], NT)
-        terms[r] = total.astype(jnp.bfloat16)
+        total = total.astype(jnp.bfloat16)
+        for t in range(tiles):
+            terms[t, r] = total
 
 
 def take(refs, n):
@@ -247,7 +247,9 @@
     for r in range(row_blocks):
         parts = [image[info[1 + slot, r * each + j]] for j in range(each)]
         total = dot(jnp.concatenate(parts, axis=1), tall[slot, r], NN)
-        terms[r] = total.astype(jnp.bfloat16)
+        total = total.astype(jnp.bfloat16)
+        for t in range(terms.shape[0]):
+            terms[t, r] = total
 
 
 def later_first(place, n_terms, *refs):
@@ -334,13 +336,12 @@
     tiles = lax.axis_size("tile")
     row_blocks = quarter * tiles
     places = subsets // 2
-    direct = tiles <= DIRECT
     subset = lax.axis_index("subset")
     pos = jnp.stack([subset // 2, subset % 2, lax.axis_index("tile")]).astype(jnp.int32)
 
     image_shape = (CB, half, BS)
     image_out = jax.ShapeDtypeStruct(image_shape, jnp.bfloat16)
-    terms_out = jax.ShapeDtypeStruct((row_blocks, half, BS), jnp.bfloat16)
+    terms_out = jax.ShapeDtypeStruct((tiles, row_blocks, half, BS), jnp.bfloat16)
     note_out = jax.ShapeDtypeStruct((quarter + 1, half, BS), jnp.float32)
     w_scr = pltpu.VMEM((row_blocks, half, BS), jnp.bfloat16)
     rays_scr = pltpu.VMEM((tiles, quarter, half, BS), jnp.float32)
@@ -349,18 +350,8 @@
     def swapped(value):
         return lax.ppermute(value, "subset", [(s, s ^ 1) for s in range(subsets)])
 
-    def turned(value, d, other=0):
-        pairs = [
-            (s * tiles + t, (s ^ other) * tiles + (t ^ d))
-            for s in range(subsets)
-            for t in range(tiles)
-        ]
-        return lax.ppermute(value, ("subset", "tile"), pairs)
-
-    def spread(value):
-        if direct:
-            return [value] + [turned(value, d) for d in range(1, tiles)]
-        return [lax.all_gather(value, "tile")]
+    def spread(copies):
+        return [lax.all_to_all(copies, "tile", 0, 0)]
 
     def call(kernel, smem, operands, out_shape, scratch, name):
         many = isinstance(out_shape, tuple)
@@ -403,7 +394,8 @@
             for value in (block_rows, block_cols, blocks, sinogram)
         ),
     )
-    notes = spread(jnp.stack([note, swapped(note2)]))
+    both = jnp.stack([note, swapped(note2)])
+    notes = spread(jnp.broadcast_to(both, (tiles,) + both.shape))
     table2 = swapped(table)
     blocks2 = pltpu.with_memory_space_constraint(blocks2, pltpu.VMEM)
     fixed = [pos, table, table2, blocks, blocks2]

time: 95.5 us -> 118 us (1.24)
  blocking collectives: 0 us -> 44.1 us
  starting transfers between devices: 47.4 us -> 22.8 us
  local copies, waits for them, and re-layouts: 0 us -> 15.4 us
  waiting for transfers between devices: 31 us -> 17.9 us
    all_to_all x0 -> x6, blocking collectives: none -> 44.1 us  [spread(): return [lax.all_to_all(copies, 'tile', 0, 0)]]
    ppermute x24 -> x0, starting transfers between devices: 21.6 us -> none  [turned(): return lax.ppermute(value, ('subset', 'tile'), pairs)]
    ppermute x24 -> x0, waiting for transfers between devices: 19.1 us -> none  [turned(): return lax.ppermute(value, ('subset', 'tile'), pairs)]
    unnamed x0 -> x24, local copies, waits for them, and re-layouts: none -> 14.7 us
    all_to_all x0 -> x2, starting transfers between devices: none -> 6.86 us  [spread(): return [lax.all_to_all(copies, 'tile', 0, 0)]]
    ppermute x4, starting transfers between devices: 17.9 us -> 12.7 us  [swapped(): return lax.ppermute(value, 'subset', [(s, s ^ 1) for s in range(subsets)])]
    ppermute x3, starting transfers between devices: 7.91 us -> 3.31 us  [per_device(): image = lax.ppermute(image, 'subset', pairs)]
    all_to_all x0 -> x2, waiting for transfers between devices: none -> 4.28 us  [spread(): return [lax.all_to_all(copies, 'tile', 0, 0)]]
  transfers between devices with their start and end apart: 31 -> 9, of which waited for: 25 -> 7; matrix products, arithmetic and copies ran while one was open for 0% -> 1% of each run, Pallas kernels for 7% -> 5%
where the time goes in v5:
time: 118 us; the launch traced here: 117 us
  blocking collectives  44.1 us (37%)
  starting transfers between devices  22.8 us (19%)
  waiting for transfers between devices  17.9 us (15%)
  Pallas kernels  17 us (14%)
  local copies, waits for them, and re-layouts  15.4 us (13%)
    all_to_all x6, blocking collectives, spread(): return [lax.all_to_all(copies, 'tile', 0, 0)]  44.1 us
    unnamed x24, local copies, waits for them, and re-layouts  14.7 us
    ppermute x4, starting transfers between devices, swapped(): return lax.ppermute(value, 'subset', [(s, s ^ 1) for s in range(subsets)])  12.7 us
    pallas_call x12, Pallas kernels, call(): pl.pallas_call(kernel, out_shape=out_shape, in_specs=[SMEM] * smem + [VME...  10.7 us
    ppermute x3, waiting for transfers between devices, per_device(): image = lax.ppermute(image, 'subset', pairs)  10.6 us
    all_to_all x2, starting transfers between devices, spread(): return [lax.all_to_all(copies, 'tile', 0, 0)]  6.86 us
    all_to_all x2, waiting for transfers between devices, spread(): return [lax.all_to_all(copies, 'tile', 0, 0)]  4.28 us
    ppermute x3, starting transfers between devices, per_device(): image = lax.ppermute(image, 'subset', pairs)  3.31 us
  transfers between devices with their start and end apart: 9, of which 7 were waited for; matrix products, arithmetic and copies ran while one was open for 1% of the time, Pallas kernels for 5%

profile of v5, /device:TPU:25, one launch (start us, length us, event | category | flops | bytes accessed | tf_op | source)
XLA Modules:
  0.0 117.5 jit_solution(1430217259554192039)
XLA Ops:
  0.0 0.7 collective-permute-start.1
  0.7 0.1 pad_add_fusion.pos.refs_0_
  0.8 3.1 %head.1 = (f32[5,16,128]{2,1,0:T(8,128)S(1)}, f32[5,16,128]{2,1,0:T(8,128)S(1)}, s32[2,80]{1,0:T(2,128)S(1)}, bf16[1,1,80,128,128]{4,3,2,1,0:T(8,128)(2,1)S(1)}) custom-call(s32[3]{0:T(128)S(1)} %pad_add_fusion.pos.refs_0_, s32[1,1,80]{2,1,0:T(1,128)} %rows_in.1, s32[1,1,80]{2,1,0:T(1,128)} %cols_in.1, bf16[1,1,80,128,128]{4,3,2,1,0:T(8,128)(2,1)} %blocks_in.1, ...), custom_call_target="tpu_custom_call" | custom-call | tf_op jit(solution)/shard_map/head/pallas_call | solution.py:370
  3.9 1.6 %copy-done.4 = bf16[1,1,80,128,128]{4,3,2,1,0:T(8,128)(2,1)} copy-done((bf16[1,1,80,128,128]{4,3,2,1,0:T(8,128)(2,1)}, bf16[1,1,80,128,128]{4,3,2,1,0:T(8,128)(2,1)S(1)}, u32[]{:S(2)}) %copy-start.4) | copy-done | bytes 2621464
  5.4 0.0 collective-permute-start.2
  5.4 1.2 %collective-permute-done.2 = f32[5,16,128]{2,1,0:T(8,128)S(1)} collective-permute-done((f32[5,16,128]{2,1,0:T(8,128)S(1)}, f32[5,16,128]{2,1,0:T(8,128)S(1)}, u32[]{:S(2)}, u32[]{:S(2)}) %collective-permute-start.2) | collective-permute-done | bytes 40992 | tf_op jit(solution)/shard_map/ppermute | solution.py:351
  6.7 0.7 broadcast_in_dim.6
  7.4 3.5 %all-to-all-start = ((f32[4,2,5,16,128]{4,3,2,1,0:T(8,128)}), f32[4,2,5,16,128]{4,3,2,1,0:T(8,128)S(1)}, u32[]{:S(2)}, u32[]{:S(2)}) async-start(f32[4,2,5,16,128]{4,3,2,1,0:T(8,128)} %broadcast_in_dim.6), calls=%async_computation | async-start | bytes 655360 | tf_op jit(solution)/shard_map/all_to_all | solution.py:354
  10.9 0.4 collective-permute-start
  11.3 0.8 collective-permute-done.refs_2_
  12.1 4.3 %all-to-all-done.refs_5_ = f32[4,2,5,16,128]{4,3,2,1,0:T(8,128)S(1)} async-done(((f32[4,2,5,16,128]{4,3,2,1,0:T(8,128)}), f32[4,2,5,16,128]{4,3,2,1,0:T(8,128)S(1)}, u32[]{:S(2)}, u32[]{:S(2)}) %all-to-all-start) | async-done | bytes 327712 | tf_op jit(solution)/shard_map/all_to_all | solution.py:354
  16.4 1.7 %copy-done.5 = bf16[1,1,80,128,128]{4,3,2,1,0:T(8,128)(2,1)S(1)} copy-done((bf16[1,1,80,128,128]{4,3,2,1,0:T(8,128)(2,1)S(1)}, bf16[1,1,80,128,128]{4,3,2,1,0:T(8,128)(2,1)}, u32[]{:S(2)}) %copy-start.5) | copy-done | bytes 2621464
  18.1 1.3 %first.4 = (f32[32,16,128]{2,1,0:T(8,128)S(1)}, bf16[32,16,128]{2,1,0:T(8,128)(2,1)S(1)}, bf16[4,16,16,128]{3,2,1,0:T(8,128)(2,1)}) custom-call(s32[3]{0:T(128)S(1)} %pad_add_fusion.pos.refs_0_, s32[2,80]{1,0:T(2,128)S(1)} %get-tuple-element.36.refs_1_, s32[2,80]{1,0:T(2,128)S(1)} %collective-permute-done.refs_2_, ...), custom_call_target="tpu_custom_call" | custom-call | tf_op jit(solution)/shard_map/first/pallas_call | solution.py:358
  19.4 0.6 copy-done.10
  20.1 0.7 copy-done.8
  20.8 3.4 %all-to-all-start.1 = ((bf16[4,16,16,128]{3,2,1,0:T(8,128)(2,1)}), bf16[4,16,16,128]{3,2,1,0:T(8,128)(2,1)S(1)}, u32[]{:S(2)}, u32[]{:S(2)}) async-start(bf16[4,16,16,128]{3,2,1,0:T(8,128)(2,1)} %get-tuple-element.40.refs_6_), calls=%async_computation.1 | async-start | bytes 524288 | tf_op jit(solution)/shard_map/all_to_all | solution.py:354
  24.2 1.7 %copy-done.6 = bf16[1,1,80,128,128]{4,3,2,1,0:T(8,128)(2,1)S(1)} copy-done((bf16[1,1,80,128,128]{4,3,2,1,0:T(8,128)(2,1)S(1)}, bf16[1,1,80,128,128]{4,3,2,1,0:T(8,128)(2,1)}, u32[]{:S(2)}) %copy-start.6) | copy-done | bytes 2621464
  25.9 3.2 %pack.1 = (s32[3,80]{1,0:T(4,128)S(1)}, bf16[2,16,128,640]{3,2,1,0:T(8,128)(2,1)S(1)}, bf16[2,16,640,128]{3,2,1,0:T(8,128)(2,1)S(1)}, f32[2,17,16,128]{3,2,1,0:T(8,128)S(1)}) custom-call(s32[3]{0:T(128)S(1)} %pad_add_fusion.pos.refs_0_, s32[2,80]{1,0:T(2,128)S(1)} %get-tuple-element.36.refs_1_, s32[2,80]{1,0:T(2,128)S(1)} %collective-permute-done.refs_2_, ...), custom_call_target="tpu_custom_call" | custom-call | tf_op jit(solution)/shard_map/pack/pallas_call | solution.py:413
  29.1 2.3 %copy-done = bf16[2,16,128,640]{3,2,1,0:T(8,128)(2,1)} copy-done((bf16[2,16,128,640]{3,2,1,0:T(8,128)(2,1)}, bf16[2,16,128,640]{3,2,1,0:T(8,128)(2,1)S(1)}, u32[]{:S(2)}) %copy-start) | copy-done | bytes 5242904
  31.4 2.4 %copy-done.2 = bf16[2,16,640,128]{3,2,1,0:T(8,128)(2,1)} copy-done((bf16[2,16,640,128]{3,2,1,0:T(8,128)(2,1)}, bf16[2,16,640,128]{3,2,1,0:T(8,128)(2,1)S(1)}, u32[]{:S(2)}) %copy-start.2) | copy-done | bytes 5242904
  33.8 1.7 %copy-done.7 = bf16[1,1,80,128,128]{4,3,2,1,0:T(8,128)(2,1)S(1)} copy-done((bf16[1,1,80,128,128]{4,3,2,1,0:T(8,128)(2,1)S(1)}, bf16[1,1,80,128,128]{4,3,2,1,0:T(8,128)(2,1)}, u32[]{:S(2)}) %copy-start.7) | copy-done | bytes 2621464
  35.5 0.9 copy-done.9
  36.5 0.9 copy-done.11
  37.4 0.6 second.4
  38.0 0.2 collective-permute-start.3
  38.2 3.6 %collective-permute-done.3.image.refs_5_ = bf16[32,16,128]{2,1,0:T(8,128)(2,1)S(1)} collective-permute-done((bf16[32,16,128]{2,1,0:T(8,128)(2,1)S(1)}, bf16[32,16,128]{2,1,0:T(8,128)(2,1)S(1)}, u32[]{:S(2)}, u32[]{:S(2)}) %collective-permute-start.3) | collective-permute-done | bytes 131104 | tf_op jit(solution)/shard_map/ppermute | solution.py:444
  41.9 0.6 project.3
  42.5 8.2 %all_to_all.40.refs_4_ = bf16[4,16,16,128]{3,2,1,0:T(8,128)(2,1)S(1)} all-to-all(bf16[4,16,16,128]{3,2,1,0:T(8,128)(2,1)S(1)} %project.3), channel_id=1, replica_groups=mesh['subset'=8,'tile'=4] {'tile'}, dimensions={0} | all-to-all | bytes 524288 | tf_op jit(solution)/shard_map/all_to_all | solution.py:354
  50.7 0.6 first.5
  51.3 7.0 %all_to_all.41.refs_3_ = bf16[4,16,16,128]{3,2,1,0:T(8,128)(2,1)S(1)} all-to-all(bf16[4,16,16,128]{3,2,1,0:T(8,128)(2,1)S(1)} %get-tuple-element.48), channel_id=1, replica_groups=mesh['subset'=8,'tile'=4] {'tile'}, dimensions={0} | all-to-all | bytes 524288 | tf_op jit(solution)/shard_map/all_to_all | solution.py:354
  58.3 0.6 second.5
  58.9 1.2 collective-permute-start.4
  60.0 4.6 %collective-permute-done.4.image.refs_5_ = bf16[32,16,128]{2,1,0:T(8,128)(2,1)S(1)} collective-permute-done((bf16[32,16,128]{2,1,0:T(8,128)(2,1)S(1)}, bf16[32,16,128]{2,1,0:T(8,128)(2,1)S(1)}, u32[]{:S(2)}, u32[]{:S(2)}) %collective-permute-start.4) | collective-permute-done | bytes 131104 | tf_op jit(solution)/shard_map/ppermute | solution.py:444
  64.7 0.8 project.4
  65.4 7.0 %all_to_all.42.refs_4_ = bf16[4,16,16,128]{3,2,1,0:T(8,128)(2,1)S(1)} all-to-all(bf16[4,16,16,128]{3,2,1,0:T(8,128)(2,1)S(1)} %project.4), channel_id=1, replica_groups=mesh['subset'=8,'tile'=4] {'tile'}, dimensions={0} | all-to-all | bytes 524288 | tf_op jit(solution)/shard_map/all_to_all | solution.py:354
  72.4 0.6 first.6
  73.0 7.6 %all_to_all.43.refs_3_ = bf16[4,16,16,128]{3,2,1,0:T(8,128)(2,1)S(1)} all-to-all(bf16[4,16,16,128]{3,2,1,0:T(8,128)(2,1)S(1)} %get-tuple-element.54), channel_id=1, replica_groups=mesh['subset'=8,'tile'=4] {'tile'}, dimensions={0} | all-to-all | bytes 524288 | tf_op jit(solution)/shard_map/all_to_all | solution.py:354
  80.6 0.6 second.6
  81.2 1.9 %collective-permute-start.5 = (bf16[32,16,128]{2,1,0:T(8,128)(2,1)S(1)}, bf16[32,16,128]{2,1,0:T(8,128)(2,1)S(1)}, u32[]{:S(2)}, u32[]{:S(2)}) collective-permute-start(bf16[32,16,128]{2,1,0:T(8,128)(2,1)S(1)} %get-tuple-element.59), channel_id=1, source_target_pairs={{0,8},{4,12},{8,0},{12,4},{16,24},{20,28},{24,16},{28,20},{1,9},{5... | collective-permute-start | bytes 393224 | tf_op jit(solution)/shard_map/ppermute | solution.py:444
  83.1 2.4 %collective-permute-done.5.image.refs_5_ = bf16[32,16,128]{2,1,0:T(8,128)(2,1)S(1)} collective-permute-done((bf16[32,16,128]{2,1,0:T(8,128)(2,1)S(1)}, bf16[32,16,128]{2,1,0:T(8,128)(2,1)S(1)}, u32[]{:S(2)}, u32[]{:S(2)}) %collective-permute-start.5) | collective-permute-done | bytes 131104 | tf_op jit(solution)/shard_map/ppermute | solution.py:444
  85.5 1.1 project.5
  86.6 7.0 %all_to_all.44.refs_4_ = bf16[4,16,16,128]{3,2,1,0:T(8,128)(2,1)S(1)} all-to-all(bf16[4,16,16,128]{3,2,1,0:T(8,128)(2,1)S(1)} %project.5), channel_id=1, replica_groups=mesh['subset'=8,'tile'=4] {'tile'}, dimensions={0} | all-to-all | bytes 524288 | tf_op jit(solution)/shard_map/all_to_all | solution.py:354
  93.5 1.6 %first.7 = (f32[32,16,128]{2,1,0:T(8,128)S(1)}, bf16[32,16,128]{2,1,0:T(8,128)(2,1)S(1)}, bf16[4,16,16,128]{3,2,1,0:T(8,128)(2,1)S(1)}) custom-call(s32[3,80]{1,0:T(4,128)S(1)} %get-tuple-element.41.refs_0_.info, f32[2,17,16,128]{3,2,1,0:T(8,128)S(1)} %get-tuple-element.42.refs_1_, bf16[2,16,128,640]{3,2,1,0:T(8,128)(2,1)S(1)} %copy-done.1, ...), custom_call_target="tpu_custom_call" | custom-call | tf_op jit(solution)/shard_map/first/pallas_call | solution.py:358
  95.2 7.3 %all_to_all.45.refs_3_ = bf16[4,16,16,128]{3,2,1,0:T(8,128)(2,1)S(1)} all-to-all(bf16[4,16,16,128]{3,2,1,0:T(8,128)(2,1)S(1)} %get-tuple-element.60), channel_id=1, replica_groups=mesh['subset'=8,'tile'=4] {'tile'}, dimensions={0} | all-to-all | bytes 524288 | tf_op jit(solution)/shard_map/all_to_all | solution.py:354
  102.5 1.1 second.7
  103.6 11.6 %collective-permute-start.6 = (bf16[32,16,128]{2,1,0:T(8,128)(2,1)S(1)}, bf16[32,16,128]{2,1,0:T(8,128)(2,1)S(1)}, u32[]{:S(2)}, u32[]{:S(2)}) collective-permute-start(bf16[32,16,128]{2,1,0:T(8,128)(2,1)S(1)} %get-tuple-element.66), channel_id=1, source_target_pairs={{0,4},{4,0},{8,12},{12,8},{16,20},{20,16},{24,28},{28,24},{1,5},{5... | collective-permute-start | bytes 393224 | tf_op jit(solution)/shard_map/ppermute | solution.py:351
  115.2 1.0 collective-permute-done.6.given
  116.2 1.3 %last.1 = bf16[4,8,4096]{2,1,0:T(8,128)(2,1)} custom-call(s32[3]{0:T(128)S(1)} %pad_add_fusion.pos.refs_0_, bf16[32,16,128]{2,1,0:T(8,128)(2,1)S(1)} %get-tuple-element.65.kept, bf16[32,16,128]{2,1,0:T(8,128)(2,1)S(1)} %collective-permute-done.6.given), custom_call_target="tpu_custom_call" | custom-call | tf_op jit(solution)/shard_map/last/pallas_call | solution.py:358
  (17 shorter events, 0.0 us)
Async XLA Ops:
  0.0 16.4 %collective-permute-start.1 = (bf16[1,1,80,128,128]{4,3,2,1,0:T(8,128)(2,1)}, bf16[1,1,80,128,128]{4,3,2,1,0:T(8,128)(2,1)S(1)}, u32[]{:S(2)}, u32[]{:S(2)}) collective-permute-start(bf16[1,1,80,128,128]{4,3,2,1,0:T(8,128)(2,1)} %blocks_in.1), channel_id=1, source_target_pairs={{0,4},{4,0},{8,12},{12,8},{16,20},{20,16},{24,28},{28,24},{1,5},{5... | collective-permute-start | bytes 7864328 | tf_op jit(solution)/shard_map/ppermute | solution.py:351
  3.8 1.6 %copy-start.4 = (bf16[1,1,80,128,128]{4,3,2,1,0:T(8,128)(2,1)}, bf16[1,1,80,128,128]{4,3,2,1,0:T(8,128)(2,1)S(1)}, u32[]{:S(2)}) copy-start(bf16[1,1,80,128,128]{4,3,2,1,0:T(8,128)(2,1)S(1)} %get-tuple-element.37.refs_3_) | copy-start | bytes 7864324
  5.4 1.2 %collective-permute-start.2 = (f32[5,16,128]{2,1,0:T(8,128)S(1)}, f32[5,16,128]{2,1,0:T(8,128)S(1)}, u32[]{:S(2)}, u32[]{:S(2)}) collective-permute-start(f32[5,16,128]{2,1,0:T(8,128)S(1)} %get-tuple-element.39), channel_id=1, source_target_pairs={{0,4},{4,0},{8,12},{12,8},{16,20},{20,16},{24,28},{28,24},{1,5},{5... | collective-permute-start | bytes 122888 | tf_op jit(solution)/shard_map/ppermute | solution.py:351
  7.4 9.0 %all-to-all-start = ((f32[4,2,5,16,128]{4,3,2,1,0:T(8,128)}), f32[4,2,5,16,128]{4,3,2,1,0:T(8,128)S(1)}, u32[]{:S(2)}, u32[]{:S(2)}) async-start(f32[4,2,5,16,128]{4,3,2,1,0:T(8,128)} %broadcast_in_dim.6), calls=%async_computation | async-start | bytes 655360 | tf_op jit(solution)/shard_map/all_to_all | solution.py:354
  10.9 1.2 %collective-permute-start = (s32[2,80]{1,0:T(2,128)S(1)}, s32[2,80]{1,0:T(2,128)S(1)}, u32[]{:S(2)}, u32[]{:S(2)}) collective-permute-start(s32[2,80]{1,0:T(2,128)S(1)} %get-tuple-element.36.refs_1_), channel_id=1, source_target_pairs={{0,4},{4,0},{8,12},{12,8},{16,20},{20,16},{24,28},{28,24},{1,5},{5... | collective-permute-start | bytes 1928 | tf_op jit(solution)/shard_map/ppermute | solution.py:351
  16.4 1.7 %copy-start.5 = (bf16[1,1,80,128,128]{4,3,2,1,0:T(8,128)(2,1)S(1)}, bf16[1,1,80,128,128]{4,3,2,1,0:T(8,128)(2,1)}, u32[]{:S(2)}) copy-start(bf16[1,1,80,128,128]{4,3,2,1,0:T(8,128)(2,1)} %copy-done.4) | copy-start | bytes 7864324
  19.4 0.6 copy-start.10
  20.1 0.7 copy-start.8
  20.8 13.0 %all-to-all-start.1 = ((bf16[4,16,16,128]{3,2,1,0:T(8,128)(2,1)}), bf16[4,16,16,128]{3,2,1,0:T(8,128)(2,1)S(1)}, u32[]{:S(2)}, u32[]{:S(2)}) async-start(bf16[4,16,16,128]{3,2,1,0:T(8,128)(2,1)} %get-tuple-element.40.refs_6_), calls=%async_computation.1 | async-start | bytes 524288 | tf_op jit(solution)/shard_map/all_to_all | solution.py:354
  24.2 1.7 %copy-start.6 = (bf16[1,1,80,128,128]{4,3,2,1,0:T(8,128)(2,1)S(1)}, bf16[1,1,80,128,128]{4,3,2,1,0:T(8,128)(2,1)}, u32[]{:S(2)}) copy-start(bf16[1,1,80,128,128]{4,3,2,1,0:T(8,128)(2,1)} %copy-done.4) | copy-start | bytes 7864324
  29.1 2.3 %copy-start = (bf16[2,16,128,640]{3,2,1,0:T(8,128)(2,1)}, bf16[2,16,128,640]{3,2,1,0:T(8,128)(2,1)S(1)}, u32[]{:S(2)}) copy-start(bf16[2,16,128,640]{3,2,1,0:T(8,128)(2,1)S(1)} %get-tuple-element.43.refs_2_) | copy-start | bytes 15728644
  31.4 2.4 %copy-start.2 = (bf16[2,16,640,128]{3,2,1,0:T(8,128)(2,1)}, bf16[2,16,640,128]{3,2,1,0:T(8,128)(2,1)S(1)}, u32[]{:S(2)}) copy-start(bf16[2,16,640,128]{3,2,1,0:T(8,128)(2,1)S(1)} %get-tuple-element.44.tall.refs_3_) | copy-start | bytes 15728644
  33.8 1.7 %copy-start.7 = (bf16[1,1,80,128,128]{4,3,2,1,0:T(8,128)(2,1)S(1)}, bf16[1,1,80,128,128]{4,3,2,1,0:T(8,128)(2,1)}, u32[]{:S(2)}) copy-start(bf16[1,1,80,128,128]{4,3,2,1,0:T(8,128)(2,1)} %copy-done.4) | copy-start | bytes 7864324
  35.5 0.9 copy-start.9
  36.5 0.9 copy-start.11
  37.4 4.5 %copy-start.3 = (bf16[2,16,640,128]{3,2,1,0:T(8,128)(2,1)S(1)}, bf16[2,16,640,128]{3,2,1,0:T(8,128)(2,1)}, u32[]{:S(2)}) copy-start(bf16[2,16,640,128]{3,2,1,0:T(8,128)(2,1)} %copy-done.2) | copy-start | bytes 15728644
  38.0 3.9 %collective-permute-start.3 = (bf16[32,16,128]{2,1,0:T(8,128)(2,1)S(1)}, bf16[32,16,128]{2,1,0:T(8,128)(2,1)S(1)}, u32[]{:S(2)}, u32[]{:S(2)}) collective-permute-start(bf16[32,16,128]{2,1,0:T(8,128)(2,1)S(1)} %get-tuple-element.47), channel_id=1, source_target_pairs={{0,8},{4,12},{8,0},{12,4},{16,24},{20,28},{24,16},{28,20},{1,9},{5... | collective-permute-start | bytes 393224 | tf_op jit(solution)/shard_map/ppermute | solution.py:444
  41.9 8.8 %copy-start.1 = (bf16[2,16,128,640]{3,2,1,0:T(8,128)(2,1)S(1)}, bf16[2,16,128,640]{3,2,1,0:T(8,128)(2,1)}, u32[]{:S(2)}) copy-start(bf16[2,16,128,640]{3,2,1,0:T(8,128)(2,1)} %copy-done) | copy-start | bytes 15728644
  58.9 5.8 %collective-permute-start.4 = (bf16[32,16,128]{2,1,0:T(8,128)(2,1)S(1)}, bf16[32,16,128]{2,1,0:T(8,128)(2,1)S(1)}, u32[]{:S(2)}, u32[]{:S(2)}) collective-permute-start(bf16[32,16,128]{2,1,0:T(8,128)(2,1)S(1)} %get-tuple-element.53), channel_id=1, source_target_pairs={{0,24},{4,28},{8,16},{12,20},{16,8},{20,12},{24,0},{28,4},{1,25},{... | collective-permute-start | bytes 393224 | tf_op jit(solution)/shard_map/ppermute | solution.py:444
  81.2 4.3 %collective-permute-start.5 = (bf16[32,16,128]{2,1,0:T(8,128)(2,1)S(1)}, bf16[32,16,128]{2,1,0:T(8,128)(2,1)S(1)}, u32[]{:S(2)}, u32[]{:S(2)}) collective-permute-start(bf16[32,16,128]{2,1,0:T(8,128)(2,1)S(1)} %get-tuple-element.59), channel_id=1, source_target_pairs={{0,8},{4,12},{8,0},{12,4},{16,24},{20,28},{24,16},{28,20},{1,9},{5... | collective-permute-start | bytes 393224 | tf_op jit(solution)/shard_map/ppermute | solution.py:444
  103.6 12.6 %collective-permute-start.6 = (bf16[32,16,128]{2,1,0:T(8,128)(2,1)S(1)}, bf16[32,16,128]{2,1,0:T(8,128)(2,1)S(1)}, u32[]{:S(2)}, u32[]{:S(2)}) collective-permute-start(bf16[32,16,128]{2,1,0:T(8,128)(2,1)S(1)} %get-tuple-element.66), channel_id=1, source_target_pairs={{0,4},{4,0},{8,12},{12,8},{16,20},{20,16},{24,28},{28,24},{1,5},{5... | collective-permute-start | bytes 393224 | tf_op jit(solution)/shard_map/ppermute | solution.py:351

commit v6 on v4

--- a/solution.py
+++ b/solution.py
@@ -71,16 +71,18 @@
             block = blocks[0, 0, n].astype(jnp.float32)
             row = rows[0, 0, n]
             squares[row] = squares[row] + block * block
-    ones = jnp.ones((16, BS), jnp.bfloat16)
+    ones = jnp.ones((BS, BS), jnp.bfloat16)
+    on_diagonal = lax.broadcasted_iota(jnp.int32, (BS, BS), 0) == lax.broadcasted_iota(
+        jnp.int32, (BS, BS), 1
+    )
     for r in range(row_blocks):
         left = squares[r]
-        total = 0.0
-        for _ in range(2):
-            part = left.astype(jnp.bfloat16)
-            total = total + dot(ones, part, NT)
-            left = left - part.astype(jnp.float32)
-        note[quarter, r : r + 1] = total[0:1]
-        note2[quarter, r : r + 1] = total[0:1]
+        coarse = left.astype(jnp.bfloat16)
+        fine = (left - coarse.astype(jnp.float32)).astype(jnp.bfloat16)
+        total = dot(coarse, ones, NN) + dot(fine, ones, NN)
+        total = jnp.sum(jnp.where(on_diagonal, total, 0.0), axis=0, keepdims=True)
+        note[quarter, r : r + 1] = total
+        note2[quarter, r : r + 1] = total
 
 
 def slabs(refs, *where):
@@ -94,8 +96,8 @@
     quarter = rays_scr.shape[1]
     norms = sum(slabs(notes, slot, quarter))[0:row_blocks]
     if len(notes) > 1:
-        for d, ref in enumerate(notes):
-            rays_scr[pos[2] ^ d] = ref[slot, 0:quarter]
+        for i, ref in enumerate(notes):
+            rays_scr[pos[2] ^ ((len(notes) - i) % len(notes))] = ref[slot, 0:quarter]
     else:
         rays_scr[...] = notes[0][:, slot, 0:quarter]
     return relaxation / norms
@@ -274,6 +276,15 @@
     kept, given, w_scr, x_scr = refs
     active = info[0, 0] == place
 
+    def write(out, source):
+        if not last:
+            out[...] = source[...].astype(jnp.bfloat16)
+            return
+        group, per_batch, _ = out.shape
+        for c in range(CB):
+            value = source[c].astype(jnp.float32).reshape(group, per_batch, BS)
+            out[:, :, c * BS : (c + 1) * BS] = value.astype(jnp.bfloat16)
+
     @pl.when(active)
     def _():
         packed_weights(rays, 1, terms_in, w_scr)
@@ -284,18 +295,18 @@
 
         @pl.when(info[0, 1] == 0)
         def _():
-            kept[...] = shot[...]
-            given[...] = x_scr[...].astype(jnp.bfloat16)
+            write(kept, shot)
+            write(given, x_scr)
 
         @pl.when(info[0, 1] == 1)
         def _():
-            kept[...] = x_scr[...].astype(jnp.bfloat16)
-            given[...] = shot[...]
+            write(kept, x_scr)
+            write(given, shot)
 
     @pl.when(jnp.logical_not(active))
     def _():
-        kept[...] = kept_in[...]
-        given[...] = given_in[...]
+        write(kept, kept_in)
+        write(given, given_in)
 
 
 def later_project(place, info, image, tall, terms):
@@ -304,25 +315,19 @@
         packed_project(info, tall, 0, image, terms)
 
 
-def last_kernel(pos, kept, given, images):
-    batches, per_batch, _ = images.shape
-    half = kept.shape[1]
-    group = half // per_batch
-
-    def write(refs):
-        for c in range(CB):
-            for h in range(2):
-                value = refs[h][c].astype(jnp.float32).reshape(group, per_batch, BS)
-                where = slice(h * group, (h + 1) * group)
-                images[where, :, c * BS : (c + 1) * BS] = value.astype(jnp.bfloat16)
-
-    @pl.when(pos[1] == 0)
-    def _():
-        write((kept, given))
-
-    @pl.when(pos[1] == 1)
-    def _():
-        write((given, kept))
+def last_kernel(info, kept, given, images, sems):
+    group = kept.shape[0]
+    core = info[0, 1]
+    copies = [
+        pltpu.make_async_copy(
+            source, images.at[pl.ds(half * group, group)], sems.at[i]
+        )
+        for i, (source, half) in enumerate(((kept, core), (given, 1 - core)))
+    ]
+    for copy in copies:
+        copy.start()
+    for copy in copies:
+        copy.wait()
 
 
 def per_device(blocks, block_rows, block_cols, sinogram):
@@ -359,7 +364,7 @@
 
     def spread(value):
         if direct:
-            return [value] + [turned(value, d) for d in range(1, tiles)]
+            return [value] + [turned(value, d) for d in range(tiles - 1, 0, -1)]
         return [lax.all_gather(value, "tile")]
 
     def call(kernel, smem, operands, out_shape, scratch, name):
@@ -407,6 +412,7 @@
     table2 = swapped(table)
     blocks2 = pltpu.with_memory_space_constraint(blocks2, pltpu.VMEM)
     fixed = [pos, table, table2, blocks, blocks2]
+    half_out = jax.ShapeDtypeStruct((batches // 2, per_batch, PIX), jnp.bfloat16)
     image32_out = jax.ShapeDtypeStruct(image_shape, jnp.float32)
 
     image32, shot, terms = call(
@@ -473,20 +479,21 @@
             functools.partial(later_second, place, len(terms), last),
             1,
             [info, rays, wide] + terms + [image32, shot, kept, given],
-            (image_out,) * (2 if last else 3),
+            (half_out,) * 2 if last else (image_out,) * 3,
             [w_scr, x_scr],
             "second",
         )
         kept, given = outs[-2:]
         image = outs[0]
-    images = call(
+    images = pl.pallas_call(
         last_kernel,
-        1,
-        [pos, kept, swapped(given)],
-        jax.ShapeDtypeStruct((batches, per_batch, PIX), jnp.bfloat16),
-        [],
-        "last",
-    )
+        out_shape=jax.ShapeDtypeStruct((batches, per_batch, PIX), jnp.bfloat16),
+        in_specs=[SMEM, VMEM, VMEM],
+        out_specs=pl.BlockSpec(memory_space=pl.ANY),
+        scratch_shapes=[pltpu.SemaphoreType.DMA((2,))],
+        compiler_params=PARAMS,
+        name="last",
+    )(info, kept, swapped(given))
     return images[None]
 
 

time: 95.5 us -> 92 us (0.963)
  starting transfers between devices: 47.4 us -> 45.6 us
  waiting for transfers between devices: 31 us -> 29.3 us
    ppermute x4, starting transfers between devices: 17.9 us -> 15 us  [swapped(): return lax.ppermute(value, 'subset', [(s, s ^ 1) for s in range(subsets)])]
    ppermute x24, waiting for transfers between devices: 19.1 us -> 17 us  [turned(): return lax.ppermute(value, ('subset', 'tile'), pairs)]
    pallas_call x12 -> x11, Pallas kernels: 10.1 us -> 8.78 us  [call(): pl.pallas_call(kernel, out_shape=out_shape, in_specs=[SMEM] * smem + [VME...]
    pallas_call x0 -> x1, Pallas kernels: none -> 1.28 us  [per_device(): pl.pallas_call(last_kernel, out_shape=jax.ShapeDtypeStruct((batches, per_...]
  transfers between devices with their start and end apart: 31 -> 31, of which waited for: 25 -> 26; matrix products, arithmetic and copies ran while one was open for 0% -> 0% of each run, Pallas kernels for 7% -> 7%
where the time goes in v6:
time: 92 us; the launch traced here: 91.5 us
  starting transfers between devices  45.6 us (50%)
  waiting for transfers between devices  29.3 us (32%)
  Pallas kernels  16.2 us (18%)
    ppermute x24, starting transfers between devices, turned(): return lax.ppermute(value, ('subset', 'tile'), pairs)  21.9 us
    ppermute x24, waiting for transfers between devices, turned(): return lax.ppermute(value, ('subset', 'tile'), pairs)  17 us
    ppermute x4, starting transfers between devices, swapped(): return lax.ppermute(value, 'subset', [(s, s ^ 1) for s in range(subsets)])  15 us
    ppermute x3, waiting for transfers between devices, per_device(): image = lax.ppermute(image, 'subset', pairs)  8.98 us
    pallas_call x11, Pallas kernels, call(): pl.pallas_call(kernel, out_shape=out_shape, in_specs=[SMEM] * smem + [VME...  8.78 us
    ppermute x3, starting transfers between devices, per_device(): image = lax.ppermute(image, 'subset', pairs)  8.7 us
    ppermute x4, waiting for transfers between devices, swapped(): return lax.ppermute(value, 'subset', [(s, s ^ 1) for s in range(subsets)])  3.29 us
    pallas_call x1, Pallas kernels, per_device(): pl.pallas_call(functools.partial(pack_kernel, len(notes)), out_shape=(jax...  3.16 us
  transfers between devices with their start and end apart: 31, of which 26 were waited for; matrix products, arithmetic and copies ran while one was open for 0% of the time, Pallas kernels for 7%

profile of v6, /device:TPU:25, one launch (start us, length us, event | category | flops | bytes accessed | tf_op | source)
XLA Modules:
  0.0 91.5 jit_solution(12407680817885936347)
XLA Ops:
  0.0 0.7 collective-permute-start.1
  0.8 2.9 %head.1 = (f32[5,16,128]{2,1,0:T(8,128)S(1)}, f32[5,16,128]{2,1,0:T(8,128)S(1)}, s32[2,80]{1,0:T(2,128)S(1)}, bf16[1,1,80,128,128]{4,3,2,1,0:T(8,128)(2,1)S(1)}) custom-call(s32[3]{0:T(128)S(1)} %pad_add_fusion.pos.refs_0_, s32[1,1,80]{2,1,0:T(1,128)} %rows_in.1, s32[1,1,80]{2,1,0:T(1,128)} %cols_in.1, bf16[1,1,80,128,128]{4,3,2,1,0:T(8,128)(2,1)} %blocks_in.1, ...), custom_call_target="tpu_custom_call" | custom-call | tf_op jit(solution)/shard_map/head/pallas_call | solution.py:384
  3.8 1.5 %collective-permute-done.2 = f32[5,16,128]{2,1,0:T(8,128)S(1)} collective-permute-done((f32[5,16,128]{2,1,0:T(8,128)S(1)}, f32[5,16,128]{2,1,0:T(8,128)S(1)}, u32[]{:S(2)}, u32[]{:S(2)}) %collective-permute-start.2) | collective-permute-done | bytes 40992 | tf_op jit(solution)/shard_map/ppermute | solution.py:355
  5.3 2.2 %collective-permute-start.3 = (f32[2,5,16,128]{3,2,1,0:T(8,128)S(1)}, f32[2,5,16,128]{3,2,1,0:T(8,128)S(1)}, u32[]{:S(2)}, u32[]{:S(2)}) collective-permute-start(f32[2,5,16,128]{3,2,1,0:T(8,128)S(1)} %pad_maximum_fusion.refs_5_), channel_id=1, source_target_pairs={{0,3},{1,2},{2,1},{3,0},{4,7},{5,6},{6,5},{7,4},{8,11},{9,10},{10,... | collective-permute-start | bytes 245768 | tf_op jit(solution)/shard_map/ppermute | solution.py:363
  7.9 1.2 %collective-permute-start = (s32[2,80]{1,0:T(2,128)S(1)}, s32[2,80]{1,0:T(2,128)S(1)}, u32[]{:S(2)}, u32[]{:S(2)}) collective-permute-start(s32[2,80]{1,0:T(2,128)S(1)} %get-tuple-element.36.refs_1_), channel_id=1, source_target_pairs={{0,4},{4,0},{8,12},{12,8},{16,20},{20,16},{24,28},{28,24},{1,5},{5... | collective-permute-start | bytes 1928 | tf_op jit(solution)/shard_map/ppermute | solution.py:355
  9.1 0.8 collective-permute-done.refs_2_
  10.0 1.8 %collective-permute-done.4.refs_7_ = f32[2,5,16,128]{3,2,1,0:T(8,128)S(1)} collective-permute-done((f32[2,5,16,128]{3,2,1,0:T(8,128)S(1)}, f32[2,5,16,128]{3,2,1,0:T(8,128)S(1)}, u32[]{:S(2)}, u32[]{:S(2)}) %collective-permute-start.4) | collective-permute-done | bytes 81952 | tf_op jit(solution)/shard_map/ppermute | solution.py:363
  12.4 1.0 %collective-permute-start.6 = (bf16[16,16,128]{2,1,0:T(8,128)(2,1)S(1)}, bf16[16,16,128]{2,1,0:T(8,128)(2,1)S(1)}, u32[]{:S(2)}, u32[]{:S(2)}) collective-permute-start(bf16[16,16,128]{2,1,0:T(8,128)(2,1)S(1)} %get-tuple-element.40.refs_9_), channel_id=1, source_target_pairs={{0,3},{1,2},{2,1},{3,0},{4,7},{5,6},{6,5},{7,4},{8,11},{9,10},{10,... | collective-permute-start | bytes 196616 | tf_op jit(solution)/shard_map/ppermute | solution.py:363
  13.4 2.0 %collective-permute-start.7 = (bf16[16,16,128]{2,1,0:T(8,128)(2,1)S(1)}, bf16[16,16,128]{2,1,0:T(8,128)(2,1)S(1)}, u32[]{:S(2)}, u32[]{:S(2)}) collective-permute-start(bf16[16,16,128]{2,1,0:T(8,128)(2,1)S(1)} %get-tuple-element.40.refs_9_), channel_id=1, source_target_pairs={{0,2},{1,3},{2,0},{3,1},{4,6},{5,7},{6,4},{7,5},{8,10},{9,11},{10,... | collective-permute-start | bytes 196616 | tf_op jit(solution)/shard_map/ppermute | solution.py:363
  15.4 3.2 %pack.1 = (s32[3,80]{1,0:T(4,128)S(1)}, bf16[2,16,128,640]{3,2,1,0:T(8,128)(2,1)S(1)}, bf16[2,16,640,128]{3,2,1,0:T(8,128)(2,1)S(1)}, f32[2,17,16,128]{3,2,1,0:T(8,128)S(1)}) custom-call(s32[3]{0:T(128)S(1)} %pad_add_fusion.pos.refs_0_, s32[2,80]{1,0:T(2,128)S(1)} %get-tuple-element.36.refs_1_, s32[2,80]{1,0:T(2,128)S(1)} %collective-permute-done.refs_2_, ...), custom_call_target="tpu_custom_call" | custom-call | tf_op jit(solution)/shard_map/pack/pallas_call | solution.py:427
  18.6 0.7 collective-permute-done.8.refs_12_
  20.1 3.6 %collective-permute-done.9.image.refs_8_ = bf16[32,16,128]{2,1,0:T(8,128)(2,1)S(1)} collective-permute-done((bf16[32,16,128]{2,1,0:T(8,128)(2,1)S(1)}, bf16[32,16,128]{2,1,0:T(8,128)(2,1)S(1)}, u32[]{:S(2)}, u32[]{:S(2)}) %collective-permute-start.9) | collective-permute-done | bytes 131104 | tf_op jit(solution)/shard_map/ppermute | solution.py:458
  24.3 1.0 %collective-permute-start.10 = (bf16[16,16,128]{2,1,0:T(8,128)(2,1)S(1)}, bf16[16,16,128]{2,1,0:T(8,128)(2,1)S(1)}, u32[]{:S(2)}, u32[]{:S(2)}) collective-permute-start(bf16[16,16,128]{2,1,0:T(8,128)(2,1)S(1)} %project.3.refs_4_), channel_id=1, source_target_pairs={{0,3},{1,2},{2,1},{3,0},{4,7},{5,6},{6,5},{7,4},{8,11},{9,10},{10,... | collective-permute-start | bytes 196616 | tf_op jit(solution)/shard_map/ppermute | solution.py:363
  25.4 1.0 %collective-permute-start.11 = (bf16[16,16,128]{2,1,0:T(8,128)(2,1)S(1)}, bf16[16,16,128]{2,1,0:T(8,128)(2,1)S(1)}, u32[]{:S(2)}, u32[]{:S(2)}) collective-permute-start(bf16[16,16,128]{2,1,0:T(8,128)(2,1)S(1)} %project.3.refs_4_), channel_id=1, source_target_pairs={{0,2},{1,3},{2,0},{3,1},{4,6},{5,7},{6,4},{7,5},{8,10},{9,11},{10,... | collective-permute-start | bytes 196616 | tf_op jit(solution)/shard_map/ppermute | solution.py:363
  26.4 0.7 collective-permute-start.12
  27.0 1.4 %collective-permute-done.10.refs_5_ = bf16[16,16,128]{2,1,0:T(8,128)(2,1)S(1)} collective-permute-done((bf16[16,16,128]{2,1,0:T(8,128)(2,1)S(1)}, bf16[16,16,128]{2,1,0:T(8,128)(2,1)S(1)}, u32[]{:S(2)}, u32[]{:S(2)}) %collective-permute-start.10) | collective-permute-done | bytes 65568 | tf_op jit(solution)/shard_map/ppermute | solution.py:363
  30.1 1.3 %collective-permute-start.13 = (bf16[16,16,128]{2,1,0:T(8,128)(2,1)S(1)}, bf16[16,16,128]{2,1,0:T(8,128)(2,1)S(1)}, u32[]{:S(2)}, u32[]{:S(2)}) collective-permute-start(bf16[16,16,128]{2,1,0:T(8,128)(2,1)S(1)} %get-tuple-element.48.refs_3_), channel_id=1, source_target_pairs={{0,3},{1,2},{2,1},{3,0},{4,7},{5,6},{6,5},{7,4},{8,11},{9,10},{10,... | collective-permute-start | bytes 196616 | tf_op jit(solution)/shard_map/ppermute | solution.py:363
  31.3 0.6 collective-permute-start.14
  32.0 0.8 collective-permute-start.15
  32.8 1.8 %collective-permute-done.13.refs_4_ = bf16[16,16,128]{2,1,0:T(8,128)(2,1)S(1)} collective-permute-done((bf16[16,16,128]{2,1,0:T(8,128)(2,1)S(1)}, bf16[16,16,128]{2,1,0:T(8,128)(2,1)S(1)}, u32[]{:S(2)}, u32[]{:S(2)}) %collective-permute-start.13) | collective-permute-done | bytes 65568 | tf_op jit(solution)/shard_map/ppermute | solution.py:363
  35.7 3.1 %collective-permute-start.16 = (bf16[32,16,128]{2,1,0:T(8,128)(2,1)S(1)}, bf16[32,16,128]{2,1,0:T(8,128)(2,1)S(1)}, u32[]{:S(2)}, u32[]{:S(2)}) collective-permute-start(bf16[32,16,128]{2,1,0:T(8,128)(2,1)S(1)} %get-tuple-element.53), channel_id=1, source_target_pairs={{0,24},{4,28},{8,16},{12,20},{16,8},{20,12},{24,0},{28,4},{1,25},{... | collective-permute-start | bytes 393224 | tf_op jit(solution)/shard_map/ppermute | solution.py:458
  38.8 2.7 %collective-permute-done.16.image.refs_8_ = bf16[32,16,128]{2,1,0:T(8,128)(2,1)S(1)} collective-permute-done((bf16[32,16,128]{2,1,0:T(8,128)(2,1)S(1)}, bf16[32,16,128]{2,1,0:T(8,128)(2,1)S(1)}, u32[]{:S(2)}, u32[]{:S(2)}) %collective-permute-start.16) | collective-permute-done | bytes 131104 | tf_op jit(solution)/shard_map/ppermute | solution.py:458
  41.5 0.8 project.4.refs_4_
  42.2 1.1 %collective-permute-start.17 = (bf16[16,16,128]{2,1,0:T(8,128)(2,1)S(1)}, bf16[16,16,128]{2,1,0:T(8,128)(2,1)S(1)}, u32[]{:S(2)}, u32[]{:S(2)}) collective-permute-start(bf16[16,16,128]{2,1,0:T(8,128)(2,1)S(1)} %project.4.refs_4_), channel_id=1, source_target_pairs={{0,3},{1,2},{2,1},{3,0},{4,7},{5,6},{6,5},{7,4},{8,11},{9,10},{10,... | collective-permute-start | bytes 196616 | tf_op jit(solution)/shard_map/ppermute | solution.py:363
  43.3 0.9 collective-permute-start.18
  44.2 0.7 collective-permute-start.19
  44.9 1.4 %collective-permute-done.17.refs_5_ = bf16[16,16,128]{2,1,0:T(8,128)(2,1)S(1)} collective-permute-done((bf16[16,16,128]{2,1,0:T(8,128)(2,1)S(1)}, bf16[16,16,128]{2,1,0:T(8,128)(2,1)S(1)}, u32[]{:S(2)}, u32[]{:S(2)}) %collective-permute-start.17) | collective-permute-done | bytes 65568 | tf_op jit(solution)/shard_map/ppermute | solution.py:363
  46.3 0.9 %collective-permute-done.18.refs_6_ = bf16[16,16,128]{2,1,0:T(8,128)(2,1)S(1)} collective-permute-done((bf16[16,16,128]{2,1,0:T(8,128)(2,1)S(1)}, bf16[16,16,128]{2,1,0:T(8,128)(2,1)S(1)}, u32[]{:S(2)}, u32[]{:S(2)}) %collective-permute-start.18) | collective-permute-done | bytes 65568 | tf_op jit(solution)/shard_map/ppermute | solution.py:363
  48.2 1.3 %collective-permute-start.20 = (bf16[16,16,128]{2,1,0:T(8,128)(2,1)S(1)}, bf16[16,16,128]{2,1,0:T(8,128)(2,1)S(1)}, u32[]{:S(2)}, u32[]{:S(2)}) collective-permute-start(bf16[16,16,128]{2,1,0:T(8,128)(2,1)S(1)} %get-tuple-element.54.refs_3_), channel_id=1, source_target_pairs={{0,3},{1,2},{2,1},{3,0},{4,7},{5,6},{6,5},{7,4},{8,11},{9,10},{10,... | collective-permute-start | bytes 196616 | tf_op jit(solution)/shard_map/ppermute | solution.py:363
  50.2 0.8 collective-permute-start.22
  50.9 1.4 %collective-permute-done.20.refs_4_ = bf16[16,16,128]{2,1,0:T(8,128)(2,1)S(1)} collective-permute-done((bf16[16,16,128]{2,1,0:T(8,128)(2,1)S(1)}, bf16[16,16,128]{2,1,0:T(8,128)(2,1)S(1)}, u32[]{:S(2)}, u32[]{:S(2)}) %collective-permute-start.20) | collective-permute-done | bytes 65568 | tf_op jit(solution)/shard_map/ppermute | solution.py:363
  52.3 0.7 collective-permute-done.21.refs_5_
  53.9 5.4 %collective-permute-start.23 = (bf16[32,16,128]{2,1,0:T(8,128)(2,1)S(1)}, bf16[32,16,128]{2,1,0:T(8,128)(2,1)S(1)}, u32[]{:S(2)}, u32[]{:S(2)}) collective-permute-start(bf16[32,16,128]{2,1,0:T(8,128)(2,1)S(1)} %get-tuple-element.59), channel_id=1, source_target_pairs={{0,8},{4,12},{8,0},{12,4},{16,24},{20,28},{24,16},{28,20},{1,9},{5... | collective-permute-start | bytes 393224 | tf_op jit(solution)/shard_map/ppermute | solution.py:458
  59.3 2.7 %collective-permute-done.23.image.refs_8_ = bf16[32,16,128]{2,1,0:T(8,128)(2,1)S(1)} collective-permute-done((bf16[32,16,128]{2,1,0:T(8,128)(2,1)S(1)}, bf16[32,16,128]{2,1,0:T(8,128)(2,1)S(1)}, u32[]{:S(2)}, u32[]{:S(2)}) %collective-permute-start.23) | collective-permute-done | bytes 131104 | tf_op jit(solution)/shard_map/ppermute | solution.py:458
  61.9 1.1 %project.5.refs_4_ = bf16[16,16,128]{2,1,0:T(8,128)(2,1)S(1)} custom-call(s32[3,80]{1,0:T(4,128)S(1)} %get-tuple-element.41.refs_0_.info, bf16[32,16,128]{2,1,0:T(8,128)(2,1)S(1)} %collective-permute-done.23.image.refs_8_, bf16[2,16,640,128]{3,2,1,0:T(8,128)(2,1)S(1)} %get-tuple-element.44.tall.refs_3_), custom_call_target="tpu_custom_call" | custom-call | tf_op jit(solution)/shard_map/project/pallas_call | solution.py:372
  63.0 0.9 collective-permute-start.24
  63.9 0.9 %collective-permute-start.25 = (bf16[16,16,128]{2,1,0:T(8,128)(2,1)S(1)}, bf16[16,16,128]{2,1,0:T(8,128)(2,1)S(1)}, u32[]{:S(2)}, u32[]{:S(2)}) collective-permute-start(bf16[16,16,128]{2,1,0:T(8,128)(2,1)S(1)} %project.5.refs_4_), channel_id=1, source_target_pairs={{0,2},{1,3},{2,0},{3,1},{4,6},{5,7},{6,4},{7,5},{8,10},{9,11},{10,... | collective-permute-start | bytes 196616 | tf_op jit(solution)/shard_map/ppermute | solution.py:363
  64.9 0.9 collective-permute-start.26
  65.7 1.5 %collective-permute-done.24.refs_5_ = bf16[16,16,128]{2,1,0:T(8,128)(2,1)S(1)} collective-permute-done((bf16[16,16,128]{2,1,0:T(8,128)(2,1)S(1)}, bf16[16,16,128]{2,1,0:T(8,128)(2,1)S(1)}, u32[]{:S(2)}, u32[]{:S(2)}) %collective-permute-start.24) | collective-permute-done | bytes 65568 | tf_op jit(solution)/shard_map/ppermute | solution.py:363
  68.0 1.7 %first.7 = (f32[32,16,128]{2,1,0:T(8,128)S(1)}, bf16[32,16,128]{2,1,0:T(8,128)(2,1)S(1)}, bf16[16,16,128]{2,1,0:T(8,128)(2,1)S(1)}) custom-call(s32[3,80]{1,0:T(4,128)S(1)} %get-tuple-element.41.refs_0_.info, f32[2,17,16,128]{3,2,1,0:T(8,128)S(1)} %get-tuple-element.42.refs_1_, bf16[2,16,128,640]{3,2,1,0:T(8,128)(2,1)S(1)} %get-tuple-element.43.refs_2_, ...), custom_call_target="tpu_custom_call" | custom-call | tf_op jit(solution)/shard_map/first/pallas_call | solution.py:372
  69.7 1.2 %collective-permute-start.27 = (bf16[16,16,128]{2,1,0:T(8,128)(2,1)S(1)}, bf16[16,16,128]{2,1,0:T(8,128)(2,1)S(1)}, u32[]{:S(2)}, u32[]{:S(2)}) collective-permute-start(bf16[16,16,128]{2,1,0:T(8,128)(2,1)S(1)} %get-tuple-element.60.refs_3_), channel_id=1, source_target_pairs={{0,3},{1,2},{2,1},{3,0},{4,7},{5,6},{6,5},{7,4},{8,11},{9,10},{10,... | collective-permute-start | bytes 196616 | tf_op jit(solution)/shard_map/ppermute | solution.py:363
  70.8 0.9 %collective-permute-start.28 = (bf16[16,16,128]{2,1,0:T(8,128)(2,1)S(1)}, bf16[16,16,128]{2,1,0:T(8,128)(2,1)S(1)}, u32[]{:S(2)}, u32[]{:S(2)}) collective-permute-start(bf16[16,16,128]{2,1,0:T(8,128)(2,1)S(1)} %get-tuple-element.60.refs_3_), channel_id=1, source_target_pairs={{0,2},{1,3},{2,0},{3,1},{4,6},{5,7},{6,4},{7,5},{8,10},{9,11},{10,... | collective-permute-start | bytes 196616 | tf_op jit(solution)/shard_map/ppermute | solution.py:363
  72.4 1.4 %collective-permute-done.27.refs_4_ = bf16[16,16,128]{2,1,0:T(8,128)(2,1)S(1)} collective-permute-done((bf16[16,16,128]{2,1,0:T(8,128)(2,1)S(1)}, bf16[16,16,128]{2,1,0:T(8,128)(2,1)S(1)}, u32[]{:S(2)}, u32[]{:S(2)}) %collective-permute-start.27) | collective-permute-done | bytes 65568 | tf_op jit(solution)/shard_map/ppermute | solution.py:363
  73.8 0.6 collective-permute-done.28.refs_5_
  74.9 1.2 %second.7 = (bf16[2,8,4096]{2,1,0:T(8,128)(2,1)S(1)}, bf16[2,8,4096]{2,1,0:T(8,128)(2,1)S(1)}) custom-call(s32[3,80]{1,0:T(4,128)S(1)} %get-tuple-element.41.refs_0_.info, f32[2,17,16,128]{3,2,1,0:T(8,128)S(1)} %get-tuple-element.42.refs_1_, bf16[2,16,128,640]{3,2,1,0:T(8,128)(2,1)S(1)} %get-tuple-element.43.refs_2_, ...), custom_call_target="tpu_custom_call" | custom-call | tf_op jit(solution)/shard_map/second/pallas_call | solution.py:372
  76.1 13.0 %collective-permute-start.30 = (bf16[2,8,4096]{2,1,0:T(8,128)(2,1)S(1)}, bf16[2,8,4096]{2,1,0:T(8,128)(2,1)S(1)}, u32[]{:S(2)}, u32[]{:S(2)}) collective-permute-start(bf16[2,8,4096]{2,1,0:T(8,128)(2,1)S(1)} %get-tuple-element.66), channel_id=1, source_target_pairs={{0,4},{4,0},{8,12},{12,8},{16,20},{20,16},{24,28},{28,24},{1,5},{5... | collective-permute-start | bytes 393224 | tf_op jit(solution)/shard_map/ppermute | solution.py:355
  89.1 1.0 %collective-permute-done.30.given = bf16[2,8,4096]{2,1,0:T(8,128)(2,1)S(1)} collective-permute-done((bf16[2,8,4096]{2,1,0:T(8,128)(2,1)S(1)}, bf16[2,8,4096]{2,1,0:T(8,128)(2,1)S(1)}, u32[]{:S(2)}, u32[]{:S(2)}) %collective-permute-start.30) | collective-permute-done | bytes 131104 | tf_op jit(solution)/shard_map/ppermute | solution.py:355
  90.1 1.3 %last.1 = bf16[4,8,4096]{2,1,0:T(8,128)(2,1)} custom-call(s32[3,80]{1,0:T(4,128)S(1)} %get-tuple-element.41.refs_0_.info, bf16[2,8,4096]{2,1,0:T(8,128)(2,1)S(1)} %get-tuple-element.65.kept, bf16[2,8,4096]{2,1,0:T(8,128)(2,1)S(1)} %collective-permute-done.30.given), custom_call_target="tpu_custom_call" | custom-call | tf_op jit(solution)/shard_map/last/pallas_call | solution.py:488
  (30 shorter events, 9.6 us)
Async XLA Ops:
  0.0 11.8 %collective-permute-start.1 = (bf16[1,1,80,128,128]{4,3,2,1,0:T(8,128)(2,1)}, bf16[1,1,80,128,128]{4,3,2,1,0:T(8,128)(2,1)S(1)}, u32[]{:S(2)}, u32[]{:S(2)}) collective-permute-start(bf16[1,1,80,128,128]{4,3,2,1,0:T(8,128)(2,1)} %blocks_in.1), channel_id=1, source_target_pairs={{0,4},{4,0},{8,12},{12,8},{16,20},{20,16},{24,28},{28,24},{1,5},{5... | collective-permute-start | bytes 7864328 | tf_op jit(solution)/shard_map/ppermute | solution.py:355
  3.7 1.6 %collective-permute-start.2 = (f32[5,16,128]{2,1,0:T(8,128)S(1)}, f32[5,16,128]{2,1,0:T(8,128)S(1)}, u32[]{:S(2)}, u32[]{:S(2)}) collective-permute-start(f32[5,16,128]{2,1,0:T(8,128)S(1)} %get-tuple-element.39), channel_id=1, source_target_pairs={{0,4},{4,0},{8,12},{12,8},{16,20},{20,16},{24,28},{28,24},{1,5},{5... | collective-permute-start | bytes 122888 | tf_op jit(solution)/shard_map/ppermute | solution.py:355
  5.3 4.7 %collective-permute-start.3 = (f32[2,5,16,128]{3,2,1,0:T(8,128)S(1)}, f32[2,5,16,128]{3,2,1,0:T(8,128)S(1)}, u32[]{:S(2)}, u32[]{:S(2)}) collective-permute-start(f32[2,5,16,128]{3,2,1,0:T(8,128)S(1)} %pad_maximum_fusion.refs_5_), channel_id=1, source_target_pairs={{0,3},{1,2},{2,1},{3,0},{4,7},{5,6},{6,5},{7,4},{8,11},{9,10},{10,... | collective-permute-start | bytes 245768 | tf_op jit(solution)/shard_map/ppermute | solution.py:363
  7.4 4.3 %collective-permute-start.4 = (f32[2,5,16,128]{3,2,1,0:T(8,128)S(1)}, f32[2,5,16,128]{3,2,1,0:T(8,128)S(1)}, u32[]{:S(2)}, u32[]{:S(2)}) collective-permute-start(f32[2,5,16,128]{3,2,1,0:T(8,128)S(1)} %pad_maximum_fusion.refs_5_), channel_id=1, source_target_pairs={{0,2},{1,3},{2,0},{3,1},{4,6},{5,7},{6,4},{7,5},{8,10},{9,11},{10,... | collective-permute-start | bytes 245768 | tf_op jit(solution)/shard_map/ppermute | solution.py:363
  7.7 4.1 %collective-permute-start.5 = (f32[2,5,16,128]{3,2,1,0:T(8,128)S(1)}, f32[2,5,16,128]{3,2,1,0:T(8,128)S(1)}, u32[]{:S(2)}, u32[]{:S(2)}) collective-permute-start(f32[2,5,16,128]{3,2,1,0:T(8,128)S(1)} %pad_maximum_fusion.refs_5_), channel_id=1, source_target_pairs={{0,1},{1,0},{2,3},{3,2},{4,5},{5,4},{6,7},{7,6},{8,9},{9,8},{10,11... | collective-permute-start | bytes 245768 | tf_op jit(solution)/shard_map/ppermute | solution.py:363
  7.9 2.0 %collective-permute-start = (s32[2,80]{1,0:T(2,128)S(1)}, s32[2,80]{1,0:T(2,128)S(1)}, u32[]{:S(2)}, u32[]{:S(2)}) collective-permute-start(s32[2,80]{1,0:T(2,128)S(1)} %get-tuple-element.36.refs_1_), channel_id=1, source_target_pairs={{0,4},{4,0},{8,12},{12,8},{16,20},{20,16},{24,28},{28,24},{1,5},{5... | collective-permute-start | bytes 1928 | tf_op jit(solution)/shard_map/ppermute | solution.py:355
  12.4 6.2 %collective-permute-start.6 = (bf16[16,16,128]{2,1,0:T(8,128)(2,1)S(1)}, bf16[16,16,128]{2,1,0:T(8,128)(2,1)S(1)}, u32[]{:S(2)}, u32[]{:S(2)}) collective-permute-start(bf16[16,16,128]{2,1,0:T(8,128)(2,1)S(1)} %get-tuple-element.40.refs_9_), channel_id=1, source_target_pairs={{0,3},{1,2},{2,1},{3,0},{4,7},{5,6},{6,5},{7,4},{8,11},{9,10},{10,... | collective-permute-start | bytes 196616 | tf_op jit(solution)/shard_map/ppermute | solution.py:363
  13.4 5.2 %collective-permute-start.7 = (bf16[16,16,128]{2,1,0:T(8,128)(2,1)S(1)}, bf16[16,16,128]{2,1,0:T(8,128)(2,1)S(1)}, u32[]{:S(2)}, u32[]{:S(2)}) collective-permute-start(bf16[16,16,128]{2,1,0:T(8,128)(2,1)S(1)} %get-tuple-element.40.refs_9_), channel_id=1, source_target_pairs={{0,2},{1,3},{2,0},{3,1},{4,6},{5,7},{6,4},{7,5},{8,10},{9,11},{10,... | collective-permute-start | bytes 196616 | tf_op jit(solution)/shard_map/ppermute | solution.py:363
  15.4 3.9 %collective-permute-start.8 = (bf16[16,16,128]{2,1,0:T(8,128)(2,1)S(1)}, bf16[16,16,128]{2,1,0:T(8,128)(2,1)S(1)}, u32[]{:S(2)}, u32[]{:S(2)}) collective-permute-start(bf16[16,16,128]{2,1,0:T(8,128)(2,1)S(1)} %get-tuple-element.40.refs_9_), channel_id=1, source_target_pairs={{0,1},{1,0},{2,3},{3,2},{4,5},{5,4},{6,7},{7,6},{8,9},{9,8},{10,11... | collective-permute-start | bytes 196616 | tf_op jit(solution)/shard_map/ppermute | solution.py:363
  19.9 3.9 %collective-permute-start.9 = (bf16[32,16,128]{2,1,0:T(8,128)(2,1)S(1)}, bf16[32,16,128]{2,1,0:T(8,128)(2,1)S(1)}, u32[]{:S(2)}, u32[]{:S(2)}) collective-permute-start(bf16[32,16,128]{2,1,0:T(8,128)(2,1)S(1)} %get-tuple-element.47), channel_id=1, source_target_pairs={{0,8},{4,12},{8,0},{12,4},{16,24},{20,28},{24,16},{28,20},{1,9},{5... | collective-permute-start | bytes 393224 | tf_op jit(solution)/shard_map/ppermute | solution.py:458
  24.3 4.1 %collective-permute-start.10 = (bf16[16,16,128]{2,1,0:T(8,128)(2,1)S(1)}, bf16[16,16,128]{2,1,0:T(8,128)(2,1)S(1)}, u32[]{:S(2)}, u32[]{:S(2)}) collective-permute-start(bf16[16,16,128]{2,1,0:T(8,128)(2,1)S(1)} %project.3.refs_4_), channel_id=1, source_target_pairs={{0,3},{1,2},{2,1},{3,0},{4,7},{5,6},{6,5},{7,4},{8,11},{9,10},{10,... | collective-permute-start | bytes 196616 | tf_op jit(solution)/shard_map/ppermute | solution.py:363
  25.4 3.7 %collective-permute-start.11 = (bf16[16,16,128]{2,1,0:T(8,128)(2,1)S(1)}, bf16[16,16,128]{2,1,0:T(8,128)(2,1)S(1)}, u32[]{:S(2)}, u32[]{:S(2)}) collective-permute-start(bf16[16,16,128]{2,1,0:T(8,128)(2,1)S(1)} %project.3.refs_4_), channel_id=1, source_target_pairs={{0,2},{1,3},{2,0},{3,1},{4,6},{5,7},{6,4},{7,5},{8,10},{9,11},{10,... | collective-permute-start | bytes 196616 | tf_op jit(solution)/shard_map/ppermute | solution.py:363
  26.4 3.1 %collective-permute-start.12 = (bf16[16,16,128]{2,1,0:T(8,128)(2,1)S(1)}, bf16[16,16,128]{2,1,0:T(8,128)(2,1)S(1)}, u32[]{:S(2)}, u32[]{:S(2)}) collective-permute-start(bf16[16,16,128]{2,1,0:T(8,128)(2,1)S(1)} %project.3.refs_4_), channel_id=1, source_target_pairs={{0,1},{1,0},{2,3},{3,2},{4,5},{5,4},{6,7},{7,6},{8,9},{9,8},{10,11... | collective-permute-start | bytes 196616 | tf_op jit(solution)/shard_map/ppermute | solution.py:363
  30.1 4.5 %collective-permute-start.13 = (bf16[16,16,128]{2,1,0:T(8,128)(2,1)S(1)}, bf16[16,16,128]{2,1,0:T(8,128)(2,1)S(1)}, u32[]{:S(2)}, u32[]{:S(2)}) collective-permute-start(bf16[16,16,128]{2,1,0:T(8,128)(2,1)S(1)} %get-tuple-element.48.refs_3_), channel_id=1, source_target_pairs={{0,3},{1,2},{2,1},{3,0},{4,7},{5,6},{6,5},{7,4},{8,11},{9,10},{10,... | collective-permute-start | bytes 196616 | tf_op jit(solution)/shard_map/ppermute | solution.py:363
  31.3 3.6 %collective-permute-start.14 = (bf16[16,16,128]{2,1,0:T(8,128)(2,1)S(1)}, bf16[16,16,128]{2,1,0:T(8,128)(2,1)S(1)}, u32[]{:S(2)}, u32[]{:S(2)}) collective-permute-start(bf16[16,16,128]{2,1,0:T(8,128)(2,1)S(1)} %get-tuple-element.48.refs_3_), channel_id=1, source_target_pairs={{0,2},{1,3},{2,0},{3,1},{4,6},{5,7},{6,4},{7,5},{8,10},{9,11},{10,... | collective-permute-start | bytes 196616 | tf_op jit(solution)/shard_map/ppermute | solution.py:363
  32.0 3.1 %collective-permute-start.15 = (bf16[16,16,128]{2,1,0:T(8,128)(2,1)S(1)}, bf16[16,16,128]{2,1,0:T(8,128)(2,1)S(1)}, u32[]{:S(2)}, u32[]{:S(2)}) collective-permute-start(bf16[16,16,128]{2,1,0:T(8,128)(2,1)S(1)} %get-tuple-element.48.refs_3_), channel_id=1, source_target_pairs={{0,1},{1,0},{2,3},{3,2},{4,5},{5,4},{6,7},{7,6},{8,9},{9,8},{10,11... | collective-permute-start | bytes 196616 | tf_op jit(solution)/shard_map/ppermute | solution.py:363
  35.7 5.8 %collective-permute-start.16 = (bf16[32,16,128]{2,1,0:T(8,128)(2,1)S(1)}, bf16[32,16,128]{2,1,0:T(8,128)(2,1)S(1)}, u32[]{:S(2)}, u32[]{:S(2)}) collective-permute-start(bf16[32,16,128]{2,1,0:T(8,128)(2,1)S(1)} %get-tuple-element.53), channel_id=1, source_target_pairs={{0,24},{4,28},{8,16},{12,20},{16,8},{20,12},{24,0},{28,4},{1,25},{... | collective-permute-start | bytes 393224 | tf_op jit(solution)/shard_map/ppermute | solution.py:458
  42.2 4.1 %collective-permute-start.17 = (bf16[16,16,128]{2,1,0:T(8,128)(2,1)S(1)}, bf16[16,16,128]{2,1,0:T(8,128)(2,1)S(1)}, u32[]{:S(2)}, u32[]{:S(2)}) collective-permute-start(bf16[16,16,128]{2,1,0:T(8,128)(2,1)S(1)} %project.4.refs_4_), channel_id=1, source_target_pairs={{0,3},{1,2},{2,1},{3,0},{4,7},{5,6},{6,5},{7,4},{8,11},{9,10},{10,... | collective-permute-start | bytes 196616 | tf_op jit(solution)/shard_map/ppermute | solution.py:363
  43.3 4.0 %collective-permute-start.18 = (bf16[16,16,128]{2,1,0:T(8,128)(2,1)S(1)}, bf16[16,16,128]{2,1,0:T(8,128)(2,1)S(1)}, u32[]{:S(2)}, u32[]{:S(2)}) collective-permute-start(bf16[16,16,128]{2,1,0:T(8,128)(2,1)S(1)} %project.4.refs_4_), channel_id=1, source_target_pairs={{0,2},{1,3},{2,0},{3,1},{4,6},{5,7},{6,4},{7,5},{8,10},{9,11},{10,... | collective-permute-start | bytes 196616 | tf_op jit(solution)/shard_map/ppermute | solution.py:363
  44.2 3.4 %collective-permute-start.19 = (bf16[16,16,128]{2,1,0:T(8,128)(2,1)S(1)}, bf16[16,16,128]{2,1,0:T(8,128)(2,1)S(1)}, u32[]{:S(2)}, u32[]{:S(2)}) collective-permute-start(bf16[16,16,128]{2,1,0:T(8,128)(2,1)S(1)} %project.4.refs_4_), channel_id=1, source_target_pairs={{0,1},{1,0},{2,3},{3,2},{4,5},{5,4},{6,7},{7,6},{8,9},{9,8},{10,11... | collective-permute-start | bytes 196616 | tf_op jit(solution)/shard_map/ppermute | solution.py:363
  48.2 4.1 %collective-permute-start.20 = (bf16[16,16,128]{2,1,0:T(8,128)(2,1)S(1)}, bf16[16,16,128]{2,1,0:T(8,128)(2,1)S(1)}, u32[]{:S(2)}, u32[]{:S(2)}) collective-permute-start(bf16[16,16,128]{2,1,0:T(8,128)(2,1)S(1)} %get-tuple-element.54.refs_3_), channel_id=1, source_target_pairs={{0,3},{1,2},{2,1},{3,0},{4,7},{5,6},{6,5},{7,4},{8,11},{9,10},{10,... | collective-permute-start | bytes 196616 | tf_op jit(solution)/shard_map/ppermute | solution.py:363
  49.6 3.4 %collective-permute-start.21 = (bf16[16,16,128]{2,1,0:T(8,128)(2,1)S(1)}, bf16[16,16,128]{2,1,0:T(8,128)(2,1)S(1)}, u32[]{:S(2)}, u32[]{:S(2)}) collective-permute-start(bf16[16,16,128]{2,1,0:T(8,128)(2,1)S(1)} %get-tuple-element.54.refs_3_), channel_id=1, source_target_pairs={{0,2},{1,3},{2,0},{3,1},{4,6},{5,7},{6,4},{7,5},{8,10},{9,11},{10,... | collective-permute-start | bytes 196616 | tf_op jit(solution)/shard_map/ppermute | solution.py:363
  50.2 3.1 %collective-permute-start.22 = (bf16[16,16,128]{2,1,0:T(8,128)(2,1)S(1)}, bf16[16,16,128]{2,1,0:T(8,128)(2,1)S(1)}, u32[]{:S(2)}, u32[]{:S(2)}) collective-permute-start(bf16[16,16,128]{2,1,0:T(8,128)(2,1)S(1)} %get-tuple-element.54.refs_3_), channel_id=1, source_target_pairs={{0,1},{1,0},{2,3},{3,2},{4,5},{5,4},{6,7},{7,6},{8,9},{9,8},{10,11... | collective-permute-start | bytes 196616 | tf_op jit(solution)/shard_map/ppermute | solution.py:363
  53.9 8.0 %collective-permute-start.23 = (bf16[32,16,128]{2,1,0:T(8,128)(2,1)S(1)}, bf16[32,16,128]{2,1,0:T(8,128)(2,1)S(1)}, u32[]{:S(2)}, u32[]{:S(2)}) collective-permute-start(bf16[32,16,128]{2,1,0:T(8,128)(2,1)S(1)} %get-tuple-element.59), channel_id=1, source_target_pairs={{0,8},{4,12},{8,0},{12,4},{16,24},{20,28},{24,16},{28,20},{1,9},{5... | collective-permute-start | bytes 393224 | tf_op jit(solution)/shard_map/ppermute | solution.py:458
  63.0 4.2 %collective-permute-start.24 = (bf16[16,16,128]{2,1,0:T(8,128)(2,1)S(1)}, bf16[16,16,128]{2,1,0:T(8,128)(2,1)S(1)}, u32[]{:S(2)}, u32[]{:S(2)}) collective-permute-start(bf16[16,16,128]{2,1,0:T(8,128)(2,1)S(1)} %project.5.refs_4_), channel_id=1, source_target_pairs={{0,3},{1,2},{2,1},{3,0},{4,7},{5,6},{6,5},{7,4},{8,11},{9,10},{10,... | collective-permute-start | bytes 196616 | tf_op jit(solution)/shard_map/ppermute | solution.py:363
  63.9 3.8 %collective-permute-start.25 = (bf16[16,16,128]{2,1,0:T(8,128)(2,1)S(1)}, bf16[16,16,128]{2,1,0:T(8,128)(2,1)S(1)}, u32[]{:S(2)}, u32[]{:S(2)}) collective-permute-start(bf16[16,16,128]{2,1,0:T(8,128)(2,1)S(1)} %project.5.refs_4_), channel_id=1, source_target_pairs={{0,2},{1,3},{2,0},{3,1},{4,6},{5,7},{6,4},{7,5},{8,10},{9,11},{10,... | collective-permute-start | bytes 196616 | tf_op jit(solution)/shard_map/ppermute | solution.py:363
  64.9 3.1 %collective-permute-start.26 = (bf16[16,16,128]{2,1,0:T(8,128)(2,1)S(1)}, bf16[16,16,128]{2,1,0:T(8,128)(2,1)S(1)}, u32[]{:S(2)}, u32[]{:S(2)}) collective-permute-start(bf16[16,16,128]{2,1,0:T(8,128)(2,1)S(1)} %project.5.refs_4_), channel_id=1, source_target_pairs={{0,1},{1,0},{2,3},{3,2},{4,5},{5,4},{6,7},{7,6},{8,9},{9,8},{10,11... | collective-permute-start | bytes 196616 | tf_op jit(solution)/shard_map/ppermute | solution.py:363
  69.7 4.1 %collective-permute-start.27 = (bf16[16,16,128]{2,1,0:T(8,128)(2,1)S(1)}, bf16[16,16,128]{2,1,0:T(8,128)(2,1)S(1)}, u32[]{:S(2)}, u32[]{:S(2)}) collective-permute-start(bf16[16,16,128]{2,1,0:T(8,128)(2,1)S(1)} %get-tuple-element.60.refs_3_), channel_id=1, source_target_pairs={{0,3},{1,2},{2,1},{3,0},{4,7},{5,6},{6,5},{7,4},{8,11},{9,10},{10,... | collective-permute-start | bytes 196616 | tf_op jit(solution)/shard_map/ppermute | solution.py:363
  70.8 3.6 %collective-permute-start.28 = (bf16[16,16,128]{2,1,0:T(8,128)(2,1)S(1)}, bf16[16,16,128]{2,1,0:T(8,128)(2,1)S(1)}, u32[]{:S(2)}, u32[]{:S(2)}) collective-permute-start(bf16[16,16,128]{2,1,0:T(8,128)(2,1)S(1)} %get-tuple-element.60.refs_3_), channel_id=1, source_target_pairs={{0,2},{1,3},{2,0},{3,1},{4,6},{5,7},{6,4},{7,5},{8,10},{9,11},{10,... | collective-permute-start | bytes 196616 | tf_op jit(solution)/shard_map/ppermute | solution.py:363
  71.7 3.1 %collective-permute-start.29 = (bf16[16,16,128]{2,1,0:T(8,128)(2,1)S(1)}, bf16[16,16,128]{2,1,0:T(8,128)(2,1)S(1)}, u32[]{:S(2)}, u32[]{:S(2)}) collective-permute-start(bf16[16,16,128]{2,1,0:T(8,128)(2,1)S(1)} %get-tuple-element.60.refs_3_), channel_id=1, source_target_pairs={{0,1},{1,0},{2,3},{3,2},{4,5},{5,4},{6,7},{7,6},{8,9},{9,8},{10,11... | collective-permute-start | bytes 196616 | tf_op jit(solution)/shard_map/ppermute | solution.py:363
  76.1 14.0 %collective-permute-start.30 = (bf16[2,8,4096]{2,1,0:T(8,128)(2,1)S(1)}, bf16[2,8,4096]{2,1,0:T(8,128)(2,1)S(1)}, u32[]{:S(2)}, u32[]{:S(2)}) collective-permute-start(bf16[2,8,4096]{2,1,0:T(8,128)(2,1)S(1)} %get-tuple-element.66), channel_id=1, source_target_pairs={{0,4},{4,0},{8,12},{12,8},{16,20},{20,16},{24,28},{28,24},{1,5},{5... | collective-permute-start | bytes 393224 | tf_op jit(solution)/shard_map/ppermute | solution.py:355

commit v7 on v3

v7 whole, which is shorter than its diff:
```python
import functools

import jax
import jax.numpy as jnp
from jax import lax
from jax.experimental import pallas as pl
from jax.experimental.pallas import tpu as pltpu
from jax.sharding import PartitionSpec as P

BS = 128
PIX = 4096
CB = PIX // BS
relaxation = 0.5

DIRECT = 4

NN = (((1,), (0,)), ((), ()))
NT = (((1,), (1,)), ((), ()))
VMEM = pl.BlockSpec(memory_space=pltpu.VMEM)
SMEM = pl.BlockSpec(memory_space=pltpu.SMEM)
PARAMS = pltpu.CompilerParams(vmem_limit_bytes=20 * 2**20)


def dot(lhs, rhs, dims):
    return lax.dot_general(lhs, rhs, dims, preferred_element_type=jnp.float32)


def head_kernel(row_blocks, chunks, pos, rows_in, cols_in, blocks_in, rays_in, *refs):
    note, note2, table, own, blocks, rows, cols, rays, seen, squares, sems = refs
    count = blocks.shape[2]
    each = count // row_blocks
    per_chunk = count // chunks
    batches, per_batch, here = rays.shape
    quarter = here // BS
    half = note.shape[1]
    group = half // per_batch
    small = [
        pltpu.make_async_copy(src, dst, sems.at[i])
        for i, (src, dst) in enumerate(((rows_in, rows), (cols_in, cols), (rays_in, rays)))
    ]
    large = []
    for k in range(chunks):
        where = pl.ds(k * per_chunk, per_chunk)
        large.append(
            pltpu.make_async_copy(
                blocks_in.at[0, 0, where], blocks.at[0, 0, where], sems.at[3 + k]
            )
        )
    for copy in small + large:
        copy.start()
    squares[...] = jnp.zeros_like(squares)
    for copy in small:
        copy.wait()
    for i in range(3):
        own[0, i] = pos[i]
    for r in range(row_blocks):
        seen[r] = r * each
    for n in range(count):
        row = rows[0, 0, n]
        at = seen[row]
        seen[row] = at + 1
        col = cols[0, 0, n]
        for out, first in ((table, 0), (own, 1)):
            out[first, at] = n
            out[first + 1, at] = col
    for out, core in ((note, pos[1]), (note2, 1 - pos[1])):
        for i in range(quarter):
            parts = [
                rays[core * group + g, :, i * BS : (i + 1) * BS] for g in range(group)
            ]
            out[i] = jnp.concatenate(parts, axis=0)
    for k in range(chunks):
        large[k].wait()
        for n in range(k * per_chunk, (k + 1) * per_chunk):
            block = blocks[0, 0, n].astype(jnp.float32)
            row = rows[0, 0, n]
            squares[row] = squares[row] + block * block
    ones = jnp.ones((BS, BS), jnp.bfloat16)
    on_diagonal = lax.broadcasted_iota(jnp.int32, (BS, BS), 0) == lax.broadcasted_iota(
        jnp.int32, (BS, BS), 1
    )
    for r in range(row_blocks):
        left = squares[r]
        coarse = left.astype(jnp.bfloat16)
        fine = (left - coarse.astype(jnp.float32)).astype(jnp.bfloat16)
        total = dot(coarse, ones, NN) + dot(fine, ones, NN)
        total = jnp.sum(jnp.where(on_diagonal, total, 0.0), axis=0, keepdims=True)
        note[quarter, r : r + 1] = total
        note2[quarter, r : r + 1] = total


def slabs(refs, *where):
    if len(refs) > 1:
        return [ref[where] for ref in refs]
    return [refs[0][(t,) + where] for t in range(refs[0].shape[0])]


def pack(tab, first, blocks, at, wide, tall):
    row_blocks = wide.shape[1]
    each = wide.shape[3] // BS
    for r in range(row_blocks):
        for j in range(each):
            block = blocks[0, 0, tab[first, r * each + j]]
            wide[at, r, :, j * BS : (j + 1) * BS] = block
            tall[at, r, j * BS : (j + 1) * BS] = block.T


def pack_own_kernel(own, blocks, _, wide, tall):
    pack(own, 1, blocks, own[0, 1], wide, tall)


def pack_other_kernel(own, table2, blocks2, wide_in, tall_in, info, wide, tall):
    del wide_in, tall_in
    core = own[0, 1]
    for i in range(3):
        info[0, i] = own[0, i]
    for k in range(info.shape[1]):
        info[1 + core, k] = own[2, k]
        info[2 - core, k] = table2[1, k]
    pack(table2, 0, blocks2, 1 - core, wide, tall)


def gather_rays(info, notes, rays, rays_scr):
    tiles, quarter, _, _ = rays_scr.shape
    row_blocks = tiles * quarter
    for slot in range(2):
        at = slot ^ info[0, 1]
        norms = sum(slabs(notes, at, quarter))[0:row_blocks]
        scale = relaxation / norms
        if len(notes) > 1:
            for i, ref in enumerate(notes):
                tile = info[0, 2] ^ ((len(notes) - i) % len(notes))
                rays_scr[tile] = ref[at, 0:quarter]
        else:
            rays_scr[...] = notes[0][:, at, 0:quarter]
        for r in range(row_blocks):
            row = scale[r : r + 1]
            rays[slot, r] = rays_scr[r // quarter, r % quarter] * row
            rays[slot, row_blocks, r : r + 1] = row


def weights(rays, slot, terms, w_scr):
    row_blocks = w_scr.shape[0]
    for r in range(row_blocks):
        left = rays[slot, r]
        if terms:
            total = sum(part.astype(jnp.float32) for part in slabs(terms, r))
            left = left - total * rays[slot, row_blocks, r : r + 1]
        w_scr[r] = left.astype(jnp.bfloat16)


def back_project(info, wide, slot, w_scr, image):
    row_blocks = wide.shape[1]
    each = wide.shape[3] // BS
    for r in range(row_blocks):
        back = dot(w_scr[r], wide[slot, r], NN)
        for j in range(each):
            col = info[1 + slot, r * each + j]
            image[col] = image[col] + back[:, j * BS : (j + 1) * BS]


def project(info, tall, slot, image, terms):
    row_blocks = tall.shape[1]
    each = tall.shape[2] // BS
    for r in range(row_blocks):
        parts = [image[info[1 + slot, r * each + j]] for j in range(each)]
        total = dot(jnp.concatenate(parts, axis=1), tall[slot, r], NN)
        terms[r] = total.astype(jnp.bfloat16)


def take(refs, n):
    taken = refs[:n]
    del refs[:n]
    return taken


def first_kernel(place, n_notes, n_terms, *refs):
    refs = list(refs)
    info, wide, tall = take(refs, 3)
    if place == 0:
        notes, terms_in = take(refs, n_notes), []
        image, shot, terms, rays, w_scr, rays_scr = refs
        gather_rays(info, notes, rays, rays_scr)
    else:
        rays, image_in = take(refs, 2)
        terms_in = take(refs, n_terms)
        image, shot, terms, w_scr = refs

    @pl.when(info[0, 0] == place)
    def _():
        weights(rays, 0, terms_in, w_scr)
        if place == 0:
            image[...] = jnp.zeros_like(image)
        else:
            image[...] = image_in[...].astype(jnp.float32)
        back_project(info, wide, 0, w_scr, image)
        shot[...] = image[...].astype(jnp.bfloat16)
        project(info, tall, 1, shot, terms)


def second_kernel(place, last, n_terms, *refs):
    refs = list(refs)
    info, rays, wide = take(refs, 3)
    terms_in = take(refs, n_terms)
    image_in, shot = take(refs, 2)
    held = take(refs, 2) if place > 0 else []
    image = None if last else take(refs, 1)[0]
    kept, given, w_scr, x_scr = refs
    active = info[0, 0] == place

    def write(out, source):
        if not last:
            out[...] = source[...].astype(jnp.bfloat16)
            return
        group, per_batch, _ = out.shape
        for c in range(CB):
            value = source[c].astype(jnp.float32).reshape(group, per_batch, BS)
            out[:, :, c * BS : (c + 1) * BS] = value.astype(jnp.bfloat16)

    @pl.when(active)
    def _():
        weights(rays, 1, terms_in, w_scr)
        x_scr[...] = image_in[...]
        back_project(info, wide, 1, w_scr, x_scr)
        if not last:
            image[...] = x_scr[...].astype(jnp.bfloat16)

        @pl.when(info[0, 1] == 0)
        def _():
            write(kept, shot)
            write(given, x_scr)

        @pl.when(info[0, 1] == 1)
        def _():
            write(kept, x_scr)
            write(given, shot)

    if held:

        @pl.when(jnp.logical_not(active))
        def _():
            write(kept, held[0])
            write(given, held[1])


def project_kernel(place, info, image, tall, terms):
    @pl.when(info[0, 0] == place)
    def _():
        project(info, tall, 0, image, terms)


def per_device(blocks, block_rows, block_cols, sinogram):
    batches, per_batch, here = sinogram.shape
    half = batches * per_batch // 2
    quarter = here // BS
    count = blocks.shape[2]
    subsets = lax.axis_size("subset")
    tiles = lax.axis_size("tile")
    row_blocks = quarter * tiles
    places = subsets // 2
    direct = tiles <= DIRECT
    subset = lax.axis_index("subset")
    pos = jnp.stack([subset // 2, subset % 2, lax.axis_index("tile")]).astype(jnp.int32)

    image_shape = (CB, half, BS)
    image_out = jax.ShapeDtypeStruct(image_shape, jnp.bfloat16)
    terms_out = jax.ShapeDtypeStruct((row_blocks, half, BS), jnp.bfloat16)
    note_out = jax.ShapeDtypeStruct((quarter + 1, half, BS), jnp.float32)
    w_scr = pltpu.VMEM((row_blocks, half, BS), jnp.bfloat16)
    rays_scr = pltpu.VMEM((tiles, quarter, half, BS), jnp.float32)
    x_scr = pltpu.VMEM(image_shape, jnp.float32)

    def swapped(value):
        return lax.ppermute(value, "subset", [(s, s ^ 1) for s in range(subsets)])

    def turned(value, d, other=0):
        pairs = [
            (s * tiles + t, (s ^ other) * tiles + (t ^ d))
            for s in range(subsets)
            for t in range(tiles)
        ]
        return lax.ppermute(value, ("subset", "tile"), pairs)

    def spread(value):
        if direct:
            return [value] + [turned(value, d) for d in range(tiles - 1, 0, -1)]
        return [lax.all_gather(value, "tile")]

    def call(kernel, smem, operands, out_shape, scratch, name):
        many = isinstance(out_shape, tuple)
        return pl.pallas_call(
            kernel,
            out_shape=out_shape,
            in_specs=[SMEM] * smem + [VMEM] * (len(operands) - smem),
            out_specs=(VMEM,) * len(out_shape) if many else VMEM,
            scratch_shapes=scratch,
            compiler_params=PARAMS,
            name=name,
        )(*operands)

    blocks2 = swapped(blocks)
    chunks = 8 if count % 8 == 0 else 1
    note, note2, table, own, blocks = pl.pallas_call(
        functools.partial(head_kernel, row_blocks, chunks),
        out_shape=(
            note_out,
            note_out,
            jax.ShapeDtypeStruct((2, count), jnp.int32),
            pltpu.SMEM((3, count), jnp.int32),
            pltpu.VMEM(blocks.shape, blocks.dtype),
        ),
        in_specs=[SMEM] + [pl.BlockSpec(memory_space=pltpu.HBM)] * 4,
        out_specs=(VMEM, VMEM, SMEM, SMEM, VMEM),
        scratch_shapes=[
            pltpu.SMEM(block_rows.shape, jnp.int32),
            pltpu.SMEM(block_cols.shape, jnp.int32),
            pltpu.VMEM(sinogram.shape, jnp.float32),
            pltpu.SMEM((row_blocks,), jnp.int32),
            pltpu.VMEM((row_blocks, BS, BS), jnp.float32),
            pltpu.SemaphoreType.DMA((3 + chunks,)),
        ],
        compiler_params=PARAMS,
        name="head",
    )(
        pos,
        *(
            pltpu.with_memory_space_constraint(value, pltpu.HBM)
            for value in (block_rows, block_cols, blocks, sinogram)
        ),
    )
    table2 = swapped(table)
    both = jnp.stack([note, swapped(note2)])
    notes = spread(both)

    own = pltpu.with_memory_space_constraint(own, pltpu.SMEM)
    blocks2 = pltpu.with_memory_space_constraint(blocks2, pltpu.VMEM)
    each = count // row_blocks
    packed_out = (
        pltpu.VMEM((2, row_blocks, BS, each * BS), jnp.bfloat16),
        pltpu.VMEM((2, row_blocks, each * BS, BS), jnp.bfloat16),
    )
    wide, tall = pl.pallas_call(
        pack_own_kernel,
        out_shape=packed_out,
        in_specs=[SMEM, VMEM, pl.BlockSpec(memory_space=pl.ANY)],
        out_specs=(VMEM, VMEM),
        compiler_params=PARAMS,
        name="pack_own",
    )(own, blocks, both)
    info, wide, tall = pl.pallas_call(
        pack_other_kernel,
        out_shape=(pltpu.SMEM((3, count), jnp.int32),) + packed_out,
        in_specs=[SMEM, SMEM, VMEM, VMEM, VMEM],
        out_specs=(SMEM, VMEM, VMEM),
        input_output_aliases={3: 1, 4: 2},
        compiler_params=PARAMS,
        name="pack_other",
    )(own, table2, blocks2, wide, tall)
    info = pltpu.with_memory_space_constraint(info, pltpu.SMEM)

    half_out = jax.ShapeDtypeStruct((batches // 2, per_batch, PIX), jnp.bfloat16)
    image32_out = jax.ShapeDtypeStruct(image_shape, jnp.float32)
    rays_out = jax.ShapeDtypeStruct((2, row_blocks + 1, half, BS), jnp.float32)
    rays, image, held = None, None, []
    for place in range(places):
        outs = (image32_out, image_out, terms_out)
        if place == 0:
            image32, shot, terms, rays = call(
                functools.partial(first_kernel, place, len(notes), 0),
                1,
                [info, wide, tall] + notes,
                outs + (rays_out,),
                [w_scr, rays_scr],
                "first",
            )
        else:
            pairs = [
                (2 * p + c, 2 * ((2 * place - 1 - p) % places) + c)
                for p in range(places)
                for c in range(2)
            ]
            image = lax.ppermute(image, "subset", pairs)
            terms = call(
                functools.partial(project_kernel, place),
                1,
                [info, image, tall],
                terms_out,
                [],
                "project",
            )
            terms = spread(terms)
            image32, shot, terms = call(
                functools.partial(first_kernel, place, 0, len(terms)),
                1,
                [info, wide, tall, rays, image] + terms,
                outs,
                [w_scr],
                "first",
            )
        terms = spread(terms)
        last = place == places - 1
        outs = call(
            functools.partial(second_kernel, place, last, len(terms)),
            1,
            [info, rays, wide] + terms + [image32, shot] + held,
            (half_out,) * 2 if last else (image_out,) * 3,
            [w_scr, x_scr],
            "second",
        )
        image = outs[0]
        held = list(outs[-2:])

    kept, given = held
    given = swapped(given)
    first = subset % 2 == 0
    images = jnp.concatenate(
        [jnp.where(first, kept, given), jnp.where(first, given, kept)], axis=0
    )
    return images[None]


def solution(mesh):
    in_specs = (
        P("subset", "tile", None, None, None),
        P("subset", "tile", None),
        P("subset", "tile", None),
        P(None, None, ("subset", "tile")),
    )
    out_specs = P("subset", None, None, "tile")
    return jax.shard_map(
        per_device, mesh=mesh, in_specs=in_specs, out_specs=out_specs, check_vma=False
    )
```

time: 104 us -> 83.2 us (0.80)
  waiting for transfers between devices: 43.5 us -> 30.7 us
  Pallas kernels: 16.3 us -> 7.77 us
    ppermute x3, waiting for transfers between devices: 21.2 us -> 10.1 us  [per_device(): image = lax.ppermute(image, 'subset', pairs)]
    pallas_call x12 -> x11, Pallas kernels: 13.2 us -> 2.28 us  [call(): pl.pallas_call(kernel, out_shape=out_shape, in_specs=[SMEM] * smem + [VME...]
    ppermute x3, starting transfers between devices: 2.63 us -> 6.66 us  [per_device(): image = lax.ppermute(image, 'subset', pairs)]
    ppermute x28 -> x24, starting transfers between devices: 24.8 us -> 21.7 us  [turned(): return lax.ppermute(value, ('subset', 'tile'), pairs)]
    pallas_call x0 -> x2, Pallas kernels: none -> 2.55 us  [the longest x1 1.61 us: per_device(): pl.pallas_call(pack_other_kernel, out_shape=(pltpu.SMEM((3, count), jnp.i...]
    ppermute x28 -> x24, waiting for transfers between devices: 20.5 us -> 18.2 us  [turned(): return lax.ppermute(value, ('subset', 'tile'), pairs)]
    ppermute x3 -> x4, starting transfers between devices: 16.1 us -> 15.1 us  [swapped(): return lax.ppermute(value, 'subset', [(s, s ^ 1) for s in range(subsets)])]
    ppermute x3 -> x4, waiting for transfers between devices: 1.81 us -> 2.48 us  [swapped(): return lax.ppermute(value, 'subset', [(s, s ^ 1) for s in range(subsets)])]
  transfers between devices with their start and end apart: 34 -> 31, of which waited for: 24 -> 26; matrix products, arithmetic and copies ran while one was open for 0% -> 0% of each run, Pallas kernels for 3% -> 7%
where the time goes in v7:
time: 83.2 us; the launch traced here: 82.9 us
  starting transfers between devices  43.5 us (52%)
  waiting for transfers between devices  30.7 us (37%)
  Pallas kernels  7.77 us (9%)
    ppermute x24, starting transfers between devices, turned(): return lax.ppermute(value, ('subset', 'tile'), pairs)  21.7 us
    ppermute x24, waiting for transfers between devices, turned(): return lax.ppermute(value, ('subset', 'tile'), pairs)  18.2 us
    ppermute x4, starting transfers between devices, swapped(): return lax.ppermute(value, 'subset', [(s, s ^ 1) for s in range(subsets)])  15.1 us
    ppermute x3, waiting for transfers between devices, per_device(): image = lax.ppermute(image, 'subset', pairs)  10.1 us
    ppermute x3, starting transfers between devices, per_device(): image = lax.ppermute(image, 'subset', pairs)  6.66 us
    pallas_call x1, Pallas kernels, per_device(): pl.pallas_call(functools.partial(head_kernel, row_blocks, chunks), out_sh...  2.95 us
    ppermute x4, waiting for transfers between devices, swapped(): return lax.ppermute(value, 'subset', [(s, s ^ 1) for s in range(subsets)])  2.48 us
    pallas_call x11, Pallas kernels, call(): pl.pallas_call(kernel, out_shape=out_shape, in_specs=[SMEM] * smem + [VME...  2.28 us
  transfers between devices with their start and end apart: 31, of which 26 were waited for; matrix products, arithmetic and copies ran while one was open for 0% of the time, Pallas kernels for 7%

profile of v7, /device:TPU:25, one launch (start us, length us, event | category | flops | bytes accessed | tf_op | source)
XLA Modules:
  0.0 82.9 jit_solution(12114534565034737826)
XLA Ops:
  0.0 0.7 collective-permute-start.1
  0.8 2.9 %head.1 = (f32[5,16,128]{2,1,0:T(8,128)S(1)}, f32[5,16,128]{2,1,0:T(8,128)S(1)}, s32[2,80]{1,0:T(2,128)S(1)}, s32[3,80]{1,0:T(4,128)S(4)}, bf16[1,1,80,128,128]{4,3,2,1,0:T(8,128)(2,1)S(1)}) custom-call(s32[3]{0:T(128)S(1)} %pad_add_fusion.pos, s32[1,1,80]{2,1,0:T(1,128)} %rows_in.1, s32[1,1,80]{2,1,0:T(1,128)} %cols_in.1, ...), custom_call_target="tpu_custom_call" | custom-call | tf_op jit(solution)/shard_map/head/pallas_call | solution.py:303
  3.8 1.5 %collective-permute-done.2 = f32[5,16,128]{2,1,0:T(8,128)S(1)} collective-permute-done((f32[5,16,128]{2,1,0:T(8,128)S(1)}, f32[5,16,128]{2,1,0:T(8,128)S(1)}, u32[]{:S(2)}, u32[]{:S(2)}) %collective-permute-start.2) | collective-permute-done | bytes 40992 | tf_op jit(solution)/shard_map/ppermute | solution.py:274
  5.3 2.2 %collective-permute-start.3 = (f32[2,5,16,128]{3,2,1,0:T(8,128)S(1)}, f32[2,5,16,128]{3,2,1,0:T(8,128)S(1)}, u32[]{:S(2)}, u32[]{:S(2)}) collective-permute-start(f32[2,5,16,128]{3,2,1,0:T(8,128)S(1)} %pad_maximum_fusion._.refs_3_), channel_id=1, source_target_pairs={{0,3},{1,2},{2,1},{3,0},{4,7},{5,6},{6,5},{7,4},{8,11},{9,10},{10,... | collective-permute-start | bytes 245768 | tf_op jit(solution)/shard_map/ppermute | solution.py:282
  7.9 1.2 %collective-permute-start = (s32[2,80]{1,0:T(2,128)S(1)}, s32[2,80]{1,0:T(2,128)S(1)}, u32[]{:S(2)}, u32[]{:S(2)}) collective-permute-start(s32[2,80]{1,0:T(2,128)S(1)} %get-tuple-element.40), channel_id=1, source_target_pairs={{0,4},{4,0},{8,12},{12,8},{16,20},{20,16},{24,28},{28,24},{1,5},{5... | collective-permute-start | bytes 1928 | tf_op jit(solution)/shard_map/ppermute | solution.py:274
  9.1 0.9 %pack_own.1 = (bf16[2,16,128,640]{3,2,1,0:T(8,128)(2,1)S(1)}, bf16[2,16,640,128]{3,2,1,0:T(8,128)(2,1)S(1)}) custom-call(s32[3,80]{1,0:T(4,128)S(4)} %get-tuple-element.39.own, bf16[1,1,80,128,128]{4,3,2,1,0:T(8,128)(2,1)S(1)} %get-tuple-element.41.blocks, f32[2,5,16,128]{3,2,1,0:T(8,128)S(1)} %pad_maximum_fusion._.refs_3_), custom_call_target="tpu_custom_call" | custom-call | tf_op jit(solution)/shard_map/pack_own/pallas_call | solution.py:342
  10.1 1.6 %pack_other.1 = (s32[3,80]{1,0:T(4,128)S(4)}, bf16[2,16,128,640]{3,2,1,0:T(8,128)(2,1)S(1)}, bf16[2,16,640,128]{3,2,1,0:T(8,128)(2,1)S(1)}) custom-call(s32[3,80]{1,0:T(4,128)S(4)} %get-tuple-element.39.own, s32[2,80]{1,0:T(2,128)S(1)} %collective-permute-done.table2, ...), custom_call_target="tpu_custom_call", output_to_operand_aliasing={{1}: (3, {}), {2}: (4, {})} | custom-call | tf_op jit(solution)/shard_map/pack_other/pallas_call | solution.py:350
  11.8 2.2 %collective-permute-start.6 = (bf16[16,16,128]{2,1,0:T(8,128)(2,1)S(1)}, bf16[16,16,128]{2,1,0:T(8,128)(2,1)S(1)}, u32[]{:S(2)}, u32[]{:S(2)}) collective-permute-start(bf16[16,16,128]{2,1,0:T(8,128)(2,1)S(1)} %get-tuple-element.50.refs_3_), channel_id=1, source_target_pairs={{0,3},{1,2},{2,1},{3,0},{4,7},{5,6},{6,5},{7,4},{8,11},{9,10},{10,... | collective-permute-start | bytes 196616 | tf_op jit(solution)/shard_map/ppermute | solution.py:282
  14.0 0.8 collective-permute-start.7
  14.8 1.0 %collective-permute-done.6.refs_4_ = bf16[16,16,128]{2,1,0:T(8,128)(2,1)S(1)} collective-permute-done((bf16[16,16,128]{2,1,0:T(8,128)(2,1)S(1)}, bf16[16,16,128]{2,1,0:T(8,128)(2,1)S(1)}, u32[]{:S(2)}, u32[]{:S(2)}) %collective-permute-start.6) | collective-permute-done | bytes 65568 | tf_op jit(solution)/shard_map/ppermute | solution.py:282
  15.9 2.4 %collective-permute-done.7.refs_5_ = bf16[16,16,128]{2,1,0:T(8,128)(2,1)S(1)} collective-permute-done((bf16[16,16,128]{2,1,0:T(8,128)(2,1)S(1)}, bf16[16,16,128]{2,1,0:T(8,128)(2,1)S(1)}, u32[]{:S(2)}, u32[]{:S(2)}) %collective-permute-start.7) | collective-permute-done | bytes 65568 | tf_op jit(solution)/shard_map/ppermute | solution.py:282
  18.9 3.6 %collective-permute-done.9.image.refs_4_ = bf16[32,16,128]{2,1,0:T(8,128)(2,1)S(1)} collective-permute-done((bf16[32,16,128]{2,1,0:T(8,128)(2,1)S(1)}, bf16[32,16,128]{2,1,0:T(8,128)(2,1)S(1)}, u32[]{:S(2)}, u32[]{:S(2)}) %collective-permute-start.9) | collective-permute-done | bytes 131104 | tf_op jit(solution)/shard_map/ppermute | solution.py:382
  22.5 1.0 %collective-permute-start.10 = (bf16[16,16,128]{2,1,0:T(8,128)(2,1)S(1)}, bf16[16,16,128]{2,1,0:T(8,128)(2,1)S(1)}, u32[]{:S(2)}, u32[]{:S(2)}) collective-permute-start(bf16[16,16,128]{2,1,0:T(8,128)(2,1)S(1)} %project.3.refs_5_), channel_id=1, source_target_pairs={{0,3},{1,2},{2,1},{3,0},{4,7},{5,6},{6,5},{7,4},{8,11},{9,10},{10,... | collective-permute-start | bytes 196616 | tf_op jit(solution)/shard_map/ppermute | solution.py:282
  23.5 1.0 %collective-permute-start.11 = (bf16[16,16,128]{2,1,0:T(8,128)(2,1)S(1)}, bf16[16,16,128]{2,1,0:T(8,128)(2,1)S(1)}, u32[]{:S(2)}, u32[]{:S(2)}) collective-permute-start(bf16[16,16,128]{2,1,0:T(8,128)(2,1)S(1)} %project.3.refs_5_), channel_id=1, source_target_pairs={{0,2},{1,3},{2,0},{3,1},{4,6},{5,7},{6,4},{7,5},{8,10},{9,11},{10,... | collective-permute-start | bytes 196616 | tf_op jit(solution)/shard_map/ppermute | solution.py:282
  24.5 0.7 collective-permute-start.12
  25.2 1.4 %collective-permute-done.10.refs_6_ = bf16[16,16,128]{2,1,0:T(8,128)(2,1)S(1)} collective-permute-done((bf16[16,16,128]{2,1,0:T(8,128)(2,1)S(1)}, bf16[16,16,128]{2,1,0:T(8,128)(2,1)S(1)}, u32[]{:S(2)}, u32[]{:S(2)}) %collective-permute-start.10) | collective-permute-done | bytes 65568 | tf_op jit(solution)/shard_map/ppermute | solution.py:282
  26.6 0.6 collective-permute-done.11.refs_7_
  27.6 0.9 %collective-permute-start.13 = (bf16[16,16,128]{2,1,0:T(8,128)(2,1)S(1)}, bf16[16,16,128]{2,1,0:T(8,128)(2,1)S(1)}, u32[]{:S(2)}, u32[]{:S(2)}) collective-permute-start(bf16[16,16,128]{2,1,0:T(8,128)(2,1)S(1)} %get-tuple-element.54.refs_3_), channel_id=1, source_target_pairs={{0,3},{1,2},{2,1},{3,0},{4,7},{5,6},{6,5},{7,4},{8,11},{9,10},{10,... | collective-permute-start | bytes 196616 | tf_op jit(solution)/shard_map/ppermute | solution.py:282
  28.5 0.9 %collective-permute-start.14 = (bf16[16,16,128]{2,1,0:T(8,128)(2,1)S(1)}, bf16[16,16,128]{2,1,0:T(8,128)(2,1)S(1)}, u32[]{:S(2)}, u32[]{:S(2)}) collective-permute-start(bf16[16,16,128]{2,1,0:T(8,128)(2,1)S(1)} %get-tuple-element.54.refs_3_), channel_id=1, source_target_pairs={{0,2},{1,3},{2,0},{3,1},{4,6},{5,7},{6,4},{7,5},{8,10},{9,11},{10,... | collective-permute-start | bytes 196616 | tf_op jit(solution)/shard_map/ppermute | solution.py:282
  29.5 0.8 collective-permute-start.15
  30.2 1.8 %collective-permute-done.13.refs_4_ = bf16[16,16,128]{2,1,0:T(8,128)(2,1)S(1)} collective-permute-done((bf16[16,16,128]{2,1,0:T(8,128)(2,1)S(1)}, bf16[16,16,128]{2,1,0:T(8,128)(2,1)S(1)}, u32[]{:S(2)}, u32[]{:S(2)}) %collective-permute-start.13) | collective-permute-done | bytes 65568 | tf_op jit(solution)/shard_map/ppermute | solution.py:282
  32.6 1.7 %collective-permute-start.16 = (bf16[32,16,128]{2,1,0:T(8,128)(2,1)S(1)}, bf16[32,16,128]{2,1,0:T(8,128)(2,1)S(1)}, u32[]{:S(2)}, u32[]{:S(2)}) collective-permute-start(bf16[32,16,128]{2,1,0:T(8,128)(2,1)S(1)} %get-tuple-element.59), channel_id=1, source_target_pairs={{0,24},{4,28},{8,16},{12,20},{16,8},{20,12},{24,0},{28,4},{1,25},{... | collective-permute-start | bytes 393224 | tf_op jit(solution)/shard_map/ppermute | solution.py:382
  34.3 4.1 %collective-permute-done.16.image.refs_4_ = bf16[32,16,128]{2,1,0:T(8,128)(2,1)S(1)} collective-permute-done((bf16[32,16,128]{2,1,0:T(8,128)(2,1)S(1)}, bf16[32,16,128]{2,1,0:T(8,128)(2,1)S(1)}, u32[]{:S(2)}, u32[]{:S(2)}) %collective-permute-start.16) | collective-permute-done | bytes 131104 | tf_op jit(solution)/shard_map/ppermute | solution.py:382
  38.4 1.0 %collective-permute-start.17 = (bf16[16,16,128]{2,1,0:T(8,128)(2,1)S(1)}, bf16[16,16,128]{2,1,0:T(8,128)(2,1)S(1)}, u32[]{:S(2)}, u32[]{:S(2)}) collective-permute-start(bf16[16,16,128]{2,1,0:T(8,128)(2,1)S(1)} %project.4.refs_5_), channel_id=1, source_target_pairs={{0,3},{1,2},{2,1},{3,0},{4,7},{5,6},{6,5},{7,4},{8,11},{9,10},{10,... | collective-permute-start | bytes 196616 | tf_op jit(solution)/shard_map/ppermute | solution.py:282
  39.4 1.0 %collective-permute-start.18 = (bf16[16,16,128]{2,1,0:T(8,128)(2,1)S(1)}, bf16[16,16,128]{2,1,0:T(8,128)(2,1)S(1)}, u32[]{:S(2)}, u32[]{:S(2)}) collective-permute-start(bf16[16,16,128]{2,1,0:T(8,128)(2,1)S(1)} %project.4.refs_5_), channel_id=1, source_target_pairs={{0,2},{1,3},{2,0},{3,1},{4,6},{5,7},{6,4},{7,5},{8,10},{9,11},{10,... | collective-permute-start | bytes 196616 | tf_op jit(solution)/shard_map/ppermute | solution.py:282
  40.3 0.7 collective-permute-start.19
  41.0 1.4 %collective-permute-done.17.refs_6_ = bf16[16,16,128]{2,1,0:T(8,128)(2,1)S(1)} collective-permute-done((bf16[16,16,128]{2,1,0:T(8,128)(2,1)S(1)}, bf16[16,16,128]{2,1,0:T(8,128)(2,1)S(1)}, u32[]{:S(2)}, u32[]{:S(2)}) %collective-permute-start.17) | collective-permute-done | bytes 65568 | tf_op jit(solution)/shard_map/ppermute | solution.py:282
  42.5 0.6 collective-permute-done.18.refs_7_
  43.5 1.1 %collective-permute-start.20 = (bf16[16,16,128]{2,1,0:T(8,128)(2,1)S(1)}, bf16[16,16,128]{2,1,0:T(8,128)(2,1)S(1)}, u32[]{:S(2)}, u32[]{:S(2)}) collective-permute-start(bf16[16,16,128]{2,1,0:T(8,128)(2,1)S(1)} %get-tuple-element.60.refs_3_), channel_id=1, source_target_pairs={{0,3},{1,2},{2,1},{3,0},{4,7},{5,6},{6,5},{7,4},{8,11},{9,10},{10,... | collective-permute-start | bytes 196616 | tf_op jit(solution)/shard_map/ppermute | solution.py:282
  44.6 0.8 collective-permute-start.21
  45.3 0.8 collective-permute-start.22
  46.1 1.4 %collective-permute-done.20.refs_4_ = bf16[16,16,128]{2,1,0:T(8,128)(2,1)S(1)} collective-permute-done((bf16[16,16,128]{2,1,0:T(8,128)(2,1)S(1)}, bf16[16,16,128]{2,1,0:T(8,128)(2,1)S(1)}, u32[]{:S(2)}, u32[]{:S(2)}) %collective-permute-start.20) | collective-permute-done | bytes 65568 | tf_op jit(solution)/shard_map/ppermute | solution.py:282
  47.5 0.7 collective-permute-done.21.refs_5_
  48.5 4.8 %collective-permute-start.23 = (bf16[32,16,128]{2,1,0:T(8,128)(2,1)S(1)}, bf16[32,16,128]{2,1,0:T(8,128)(2,1)S(1)}, u32[]{:S(2)}, u32[]{:S(2)}) collective-permute-start(bf16[32,16,128]{2,1,0:T(8,128)(2,1)S(1)} %get-tuple-element.65), channel_id=1, source_target_pairs={{0,8},{4,12},{8,0},{12,4},{16,24},{20,28},{24,16},{28,20},{1,9},{5... | collective-permute-start | bytes 393224 | tf_op jit(solution)/shard_map/ppermute | solution.py:382
  53.3 2.4 %collective-permute-done.23.image.refs_4_ = bf16[32,16,128]{2,1,0:T(8,128)(2,1)S(1)} collective-permute-done((bf16[32,16,128]{2,1,0:T(8,128)(2,1)S(1)}, bf16[32,16,128]{2,1,0:T(8,128)(2,1)S(1)}, u32[]{:S(2)}, u32[]{:S(2)}) %collective-permute-start.23) | collective-permute-done | bytes 131104 | tf_op jit(solution)/shard_map/ppermute | solution.py:382
  56.1 0.8 collective-permute-start.24
  57.0 1.1 %collective-permute-start.25 = (bf16[16,16,128]{2,1,0:T(8,128)(2,1)S(1)}, bf16[16,16,128]{2,1,0:T(8,128)(2,1)S(1)}, u32[]{:S(2)}, u32[]{:S(2)}) collective-permute-start(bf16[16,16,128]{2,1,0:T(8,128)(2,1)S(1)} %project.5.refs_5_), channel_id=1, source_target_pairs={{0,2},{1,3},{2,0},{3,1},{4,6},{5,7},{6,4},{7,5},{8,10},{9,11},{10,... | collective-permute-start | bytes 196616 | tf_op jit(solution)/shard_map/ppermute | solution.py:282
  58.1 0.7 collective-permute-start.26
  58.8 1.5 %collective-permute-done.24.refs_6_ = bf16[16,16,128]{2,1,0:T(8,128)(2,1)S(1)} collective-permute-done((bf16[16,16,128]{2,1,0:T(8,128)(2,1)S(1)}, bf16[16,16,128]{2,1,0:T(8,128)(2,1)S(1)}, u32[]{:S(2)}, u32[]{:S(2)}) %collective-permute-start.24) | collective-permute-done | bytes 65568 | tf_op jit(solution)/shard_map/ppermute | solution.py:282
  61.2 1.1 %first.7 = (f32[32,16,128]{2,1,0:T(8,128)S(1)}, bf16[32,16,128]{2,1,0:T(8,128)(2,1)S(1)}, bf16[16,16,128]{2,1,0:T(8,128)(2,1)S(1)}) custom-call(s32[3,80]{1,0:T(4,128)S(4)} %get-tuple-element.46.refs_0_.info, bf16[2,16,128,640]{3,2,1,0:T(8,128)(2,1)S(1)} %get-tuple-element.47.refs_1_.refs_2_, bf16[2,16,640,128]{3,2,1,0:T(8,128)(2,1)S(1)} %get-tuple-element.48.refs_2_.tall, ...), custom_call_target="tpu_custom_call" | custom-call | tf_op jit(solution)/shard_map/first/pallas_call | solution.py:291
  62.3 1.1 %collective-permute-start.27 = (bf16[16,16,128]{2,1,0:T(8,128)(2,1)S(1)}, bf16[16,16,128]{2,1,0:T(8,128)(2,1)S(1)}, u32[]{:S(2)}, u32[]{:S(2)}) collective-permute-start(bf16[16,16,128]{2,1,0:T(8,128)(2,1)S(1)} %get-tuple-element.66.refs_3_), channel_id=1, source_target_pairs={{0,3},{1,2},{2,1},{3,0},{4,7},{5,6},{6,5},{7,4},{8,11},{9,10},{10,... | collective-permute-start | bytes 196616 | tf_op jit(solution)/shard_map/ppermute | solution.py:282
  63.4 0.9 %collective-permute-start.28 = (bf16[16,16,128]{2,1,0:T(8,128)(2,1)S(1)}, bf16[16,16,128]{2,1,0:T(8,128)(2,1)S(1)}, u32[]{:S(2)}, u32[]{:S(2)}) collective-permute-start(bf16[16,16,128]{2,1,0:T(8,128)(2,1)S(1)} %get-tuple-element.66.refs_3_), channel_id=1, source_target_pairs={{0,2},{1,3},{2,0},{3,1},{4,6},{5,7},{6,4},{7,5},{8,10},{9,11},{10,... | collective-permute-start | bytes 196616 | tf_op jit(solution)/shard_map/ppermute | solution.py:282
  64.3 0.7 collective-permute-start.29
  65.0 1.4 %collective-permute-done.27.refs_4_ = bf16[16,16,128]{2,1,0:T(8,128)(2,1)S(1)} collective-permute-done((bf16[16,16,128]{2,1,0:T(8,128)(2,1)S(1)}, bf16[16,16,128]{2,1,0:T(8,128)(2,1)S(1)}, u32[]{:S(2)}, u32[]{:S(2)}) %collective-permute-start.27) | collective-permute-done | bytes 65568 | tf_op jit(solution)/shard_map/ppermute | solution.py:282
  66.4 0.6 collective-permute-done.28.refs_5_
  68.0 13.2 %collective-permute-start.30 = (bf16[2,8,4096]{2,1,0:T(8,128)(2,1)S(1)}, bf16[2,8,4096]{2,1,0:T(8,128)(2,1)S(1)}, u32[]{:S(2)}, u32[]{:S(2)}) collective-permute-start(bf16[2,8,4096]{2,1,0:T(8,128)(2,1)S(1)} %get-tuple-element.72), channel_id=1, source_target_pairs={{0,4},{4,0},{8,12},{12,8},{16,20},{20,16},{24,28},{28,24},{1,5},{5... | collective-permute-start | bytes 393224 | tf_op jit(solution)/shard_map/ppermute | solution.py:274
  81.2 1.0 %collective-permute-done.30 = bf16[2,8,4096]{2,1,0:T(8,128)(2,1)S(1)} collective-permute-done((bf16[2,8,4096]{2,1,0:T(8,128)(2,1)S(1)}, bf16[2,8,4096]{2,1,0:T(8,128)(2,1)S(1)}, u32[]{:S(2)}, u32[]{:S(2)}) %collective-permute-start.30) | collective-permute-done | bytes 131104 | tf_op jit(solution)/shard_map/ppermute | solution.py:274
  82.2 0.7 maximum_bitcast_fusion
  (32 shorter events, 5.3 us)
Async XLA Ops:
  0.0 10.1 %collective-permute-start.1 = (bf16[1,1,80,128,128]{4,3,2,1,0:T(8,128)(2,1)}, bf16[1,1,80,128,128]{4,3,2,1,0:T(8,128)(2,1)S(1)}, u32[]{:S(2)}, u32[]{:S(2)}) collective-permute-start(bf16[1,1,80,128,128]{4,3,2,1,0:T(8,128)(2,1)} %blocks_in.1), channel_id=1, source_target_pairs={{0,4},{4,0},{8,12},{12,8},{16,20},{20,16},{24,28},{28,24},{1,5},{5... | collective-permute-start | bytes 7864328 | tf_op jit(solution)/shard_map/ppermute | solution.py:274
  3.7 1.6 %collective-permute-start.2 = (f32[5,16,128]{2,1,0:T(8,128)S(1)}, f32[5,16,128]{2,1,0:T(8,128)S(1)}, u32[]{:S(2)}, u32[]{:S(2)}) collective-permute-start(f32[5,16,128]{2,1,0:T(8,128)S(1)} %get-tuple-element.43), channel_id=1, source_target_pairs={{0,4},{4,0},{8,12},{12,8},{16,20},{20,16},{24,28},{28,24},{1,5},{5... | collective-permute-start | bytes 122888 | tf_op jit(solution)/shard_map/ppermute | solution.py:274
  5.3 6.4 %collective-permute-start.3 = (f32[2,5,16,128]{3,2,1,0:T(8,128)S(1)}, f32[2,5,16,128]{3,2,1,0:T(8,128)S(1)}, u32[]{:S(2)}, u32[]{:S(2)}) collective-permute-start(f32[2,5,16,128]{3,2,1,0:T(8,128)S(1)} %pad_maximum_fusion._.refs_3_), channel_id=1, source_target_pairs={{0,3},{1,2},{2,1},{3,0},{4,7},{5,6},{6,5},{7,4},{8,11},{9,10},{10,... | collective-permute-start | bytes 245768 | tf_op jit(solution)/shard_map/ppermute | solution.py:282
  7.4 4.3 %collective-permute-start.4 = (f32[2,5,16,128]{3,2,1,0:T(8,128)S(1)}, f32[2,5,16,128]{3,2,1,0:T(8,128)S(1)}, u32[]{:S(2)}, u32[]{:S(2)}) collective-permute-start(f32[2,5,16,128]{3,2,1,0:T(8,128)S(1)} %pad_maximum_fusion._.refs_3_), channel_id=1, source_target_pairs={{0,2},{1,3},{2,0},{3,1},{4,6},{5,7},{6,4},{7,5},{8,10},{9,11},{10,... | collective-permute-start | bytes 245768 | tf_op jit(solution)/shard_map/ppermute | solution.py:282
  7.7 4.1 %collective-permute-start.5 = (f32[2,5,16,128]{3,2,1,0:T(8,128)S(1)}, f32[2,5,16,128]{3,2,1,0:T(8,128)S(1)}, u32[]{:S(2)}, u32[]{:S(2)}) collective-permute-start(f32[2,5,16,128]{3,2,1,0:T(8,128)S(1)} %pad_maximum_fusion._.refs_3_), channel_id=1, source_target_pairs={{0,1},{1,0},{2,3},{3,2},{4,5},{5,4},{6,7},{7,6},{8,9},{9,8},{10,11... | collective-permute-start | bytes 245768 | tf_op jit(solution)/shard_map/ppermute | solution.py:282
  7.9 2.2 %collective-permute-start = (s32[2,80]{1,0:T(2,128)S(1)}, s32[2,80]{1,0:T(2,128)S(1)}, u32[]{:S(2)}, u32[]{:S(2)}) collective-permute-start(s32[2,80]{1,0:T(2,128)S(1)} %get-tuple-element.40), channel_id=1, source_target_pairs={{0,4},{4,0},{8,12},{12,8},{16,20},{20,16},{24,28},{28,24},{1,5},{5... | collective-permute-start | bytes 1928 | tf_op jit(solution)/shard_map/ppermute | solution.py:274
  11.8 4.1 %collective-permute-start.6 = (bf16[16,16,128]{2,1,0:T(8,128)(2,1)S(1)}, bf16[16,16,128]{2,1,0:T(8,128)(2,1)S(1)}, u32[]{:S(2)}, u32[]{:S(2)}) collective-permute-start(bf16[16,16,128]{2,1,0:T(8,128)(2,1)S(1)} %get-tuple-element.50.refs_3_), channel_id=1, source_target_pairs={{0,3},{1,2},{2,1},{3,0},{4,7},{5,6},{6,5},{7,4},{8,11},{9,10},{10,... | collective-permute-start | bytes 196616 | tf_op jit(solution)/shard_map/ppermute | solution.py:282
  14.0 4.2 %collective-permute-start.7 = (bf16[16,16,128]{2,1,0:T(8,128)(2,1)S(1)}, bf16[16,16,128]{2,1,0:T(8,128)(2,1)S(1)}, u32[]{:S(2)}, u32[]{:S(2)}) collective-permute-start(bf16[16,16,128]{2,1,0:T(8,128)(2,1)S(1)} %get-tuple-element.50.refs_3_), channel_id=1, source_target_pairs={{0,2},{1,3},{2,0},{3,1},{4,6},{5,7},{6,4},{7,5},{8,10},{9,11},{10,... | collective-permute-start | bytes 196616 | tf_op jit(solution)/shard_map/ppermute | solution.py:282
  14.8 3.9 %collective-permute-start.8 = (bf16[16,16,128]{2,1,0:T(8,128)(2,1)S(1)}, bf16[16,16,128]{2,1,0:T(8,128)(2,1)S(1)}, u32[]{:S(2)}, u32[]{:S(2)}) collective-permute-start(bf16[16,16,128]{2,1,0:T(8,128)(2,1)S(1)} %get-tuple-element.50.refs_3_), channel_id=1, source_target_pairs={{0,1},{1,0},{2,3},{3,2},{4,5},{5,4},{6,7},{7,6},{8,9},{9,8},{10,11... | collective-permute-start | bytes 196616 | tf_op jit(solution)/shard_map/ppermute | solution.py:282
  18.7 3.8 %collective-permute-start.9 = (bf16[32,16,128]{2,1,0:T(8,128)(2,1)S(1)}, bf16[32,16,128]{2,1,0:T(8,128)(2,1)S(1)}, u32[]{:S(2)}, u32[]{:S(2)}) collective-permute-start(bf16[32,16,128]{2,1,0:T(8,128)(2,1)S(1)} %get-tuple-element.53), channel_id=1, source_target_pairs={{0,8},{4,12},{8,0},{12,4},{16,24},{20,28},{24,16},{28,20},{1,9},{5... | collective-permute-start | bytes 393224 | tf_op jit(solution)/shard_map/ppermute | solution.py:382
  22.5 4.1 %collective-permute-start.10 = (bf16[16,16,128]{2,1,0:T(8,128)(2,1)S(1)}, bf16[16,16,128]{2,1,0:T(8,128)(2,1)S(1)}, u32[]{:S(2)}, u32[]{:S(2)}) collective-permute-start(bf16[16,16,128]{2,1,0:T(8,128)(2,1)S(1)} %project.3.refs_5_), channel_id=1, source_target_pairs={{0,3},{1,2},{2,1},{3,0},{4,7},{5,6},{6,5},{7,4},{8,11},{9,10},{10,... | collective-permute-start | bytes 196616 | tf_op jit(solution)/shard_map/ppermute | solution.py:282
  23.5 3.7 %collective-permute-start.11 = (bf16[16,16,128]{2,1,0:T(8,128)(2,1)S(1)}, bf16[16,16,128]{2,1,0:T(8,128)(2,1)S(1)}, u32[]{:S(2)}, u32[]{:S(2)}) collective-permute-start(bf16[16,16,128]{2,1,0:T(8,128)(2,1)S(1)} %project.3.refs_5_), channel_id=1, source_target_pairs={{0,2},{1,3},{2,0},{3,1},{4,6},{5,7},{6,4},{7,5},{8,10},{9,11},{10,... | collective-permute-start | bytes 196616 | tf_op jit(solution)/shard_map/ppermute | solution.py:282
  24.5 3.1 %collective-permute-start.12 = (bf16[16,16,128]{2,1,0:T(8,128)(2,1)S(1)}, bf16[16,16,128]{2,1,0:T(8,128)(2,1)S(1)}, u32[]{:S(2)}, u32[]{:S(2)}) collective-permute-start(bf16[16,16,128]{2,1,0:T(8,128)(2,1)S(1)} %project.3.refs_5_), channel_id=1, source_target_pairs={{0,1},{1,0},{2,3},{3,2},{4,5},{5,4},{6,7},{7,6},{8,9},{9,8},{10,11... | collective-permute-start | bytes 196616 | tf_op jit(solution)/shard_map/ppermute | solution.py:282
  27.6 4.4 %collective-permute-start.13 = (bf16[16,16,128]{2,1,0:T(8,128)(2,1)S(1)}, bf16[16,16,128]{2,1,0:T(8,128)(2,1)S(1)}, u32[]{:S(2)}, u32[]{:S(2)}) collective-permute-start(bf16[16,16,128]{2,1,0:T(8,128)(2,1)S(1)} %get-tuple-element.54.refs_3_), channel_id=1, source_target_pairs={{0,3},{1,2},{2,1},{3,0},{4,7},{5,6},{6,5},{7,4},{8,11},{9,10},{10,... | collective-permute-start | bytes 196616 | tf_op jit(solution)/shard_map/ppermute | solution.py:282
  28.5 3.8 %collective-permute-start.14 = (bf16[16,16,128]{2,1,0:T(8,128)(2,1)S(1)}, bf16[16,16,128]{2,1,0:T(8,128)(2,1)S(1)}, u32[]{:S(2)}, u32[]{:S(2)}) collective-permute-start(bf16[16,16,128]{2,1,0:T(8,128)(2,1)S(1)} %get-tuple-element.54.refs_3_), channel_id=1, source_target_pairs={{0,2},{1,3},{2,0},{3,1},{4,6},{5,7},{6,4},{7,5},{8,10},{9,11},{10,... | collective-permute-start | bytes 196616 | tf_op jit(solution)/shard_map/ppermute | solution.py:282
  29.5 3.1 %collective-permute-start.15 = (bf16[16,16,128]{2,1,0:T(8,128)(2,1)S(1)}, bf16[16,16,128]{2,1,0:T(8,128)(2,1)S(1)}, u32[]{:S(2)}, u32[]{:S(2)}) collective-permute-start(bf16[16,16,128]{2,1,0:T(8,128)(2,1)S(1)} %get-tuple-element.54.refs_3_), channel_id=1, source_target_pairs={{0,1},{1,0},{2,3},{3,2},{4,5},{5,4},{6,7},{7,6},{8,9},{9,8},{10,11... | collective-permute-start | bytes 196616 | tf_op jit(solution)/shard_map/ppermute | solution.py:282
  32.6 5.8 %collective-permute-start.16 = (bf16[32,16,128]{2,1,0:T(8,128)(2,1)S(1)}, bf16[32,16,128]{2,1,0:T(8,128)(2,1)S(1)}, u32[]{:S(2)}, u32[]{:S(2)}) collective-permute-start(bf16[32,16,128]{2,1,0:T(8,128)(2,1)S(1)} %get-tuple-element.59), channel_id=1, source_target_pairs={{0,24},{4,28},{8,16},{12,20},{16,8},{20,12},{24,0},{28,4},{1,25},{... | collective-permute-start | bytes 393224 | tf_op jit(solution)/shard_map/ppermute | solution.py:382
  38.4 4.1 %collective-permute-start.17 = (bf16[16,16,128]{2,1,0:T(8,128)(2,1)S(1)}, bf16[16,16,128]{2,1,0:T(8,128)(2,1)S(1)}, u32[]{:S(2)}, u32[]{:S(2)}) collective-permute-start(bf16[16,16,128]{2,1,0:T(8,128)(2,1)S(1)} %project.4.refs_5_), channel_id=1, source_target_pairs={{0,3},{1,2},{2,1},{3,0},{4,7},{5,6},{6,5},{7,4},{8,11},{9,10},{10,... | collective-permute-start | bytes 196616 | tf_op jit(solution)/shard_map/ppermute | solution.py:282
  39.4 3.7 %collective-permute-start.18 = (bf16[16,16,128]{2,1,0:T(8,128)(2,1)S(1)}, bf16[16,16,128]{2,1,0:T(8,128)(2,1)S(1)}, u32[]{:S(2)}, u32[]{:S(2)}) collective-permute-start(bf16[16,16,128]{2,1,0:T(8,128)(2,1)S(1)} %project.4.refs_5_), channel_id=1, source_target_pairs={{0,2},{1,3},{2,0},{3,1},{4,6},{5,7},{6,4},{7,5},{8,10},{9,11},{10,... | collective-permute-start | bytes 196616 | tf_op jit(solution)/shard_map/ppermute | solution.py:282
  40.3 3.1 %collective-permute-start.19 = (bf16[16,16,128]{2,1,0:T(8,128)(2,1)S(1)}, bf16[16,16,128]{2,1,0:T(8,128)(2,1)S(1)}, u32[]{:S(2)}, u32[]{:S(2)}) collective-permute-start(bf16[16,16,128]{2,1,0:T(8,128)(2,1)S(1)} %project.4.refs_5_), channel_id=1, source_target_pairs={{0,1},{1,0},{2,3},{3,2},{4,5},{5,4},{6,7},{7,6},{8,9},{9,8},{10,11... | collective-permute-start | bytes 196616 | tf_op jit(solution)/shard_map/ppermute | solution.py:282
  43.5 4.1 %collective-permute-start.20 = (bf16[16,16,128]{2,1,0:T(8,128)(2,1)S(1)}, bf16[16,16,128]{2,1,0:T(8,128)(2,1)S(1)}, u32[]{:S(2)}, u32[]{:S(2)}) collective-permute-start(bf16[16,16,128]{2,1,0:T(8,128)(2,1)S(1)} %get-tuple-element.60.refs_3_), channel_id=1, source_target_pairs={{0,3},{1,2},{2,1},{3,0},{4,7},{5,6},{6,5},{7,4},{8,11},{9,10},{10,... | collective-permute-start | bytes 196616 | tf_op jit(solution)/shard_map/ppermute | solution.py:282
  44.6 3.6 %collective-permute-start.21 = (bf16[16,16,128]{2,1,0:T(8,128)(2,1)S(1)}, bf16[16,16,128]{2,1,0:T(8,128)(2,1)S(1)}, u32[]{:S(2)}, u32[]{:S(2)}) collective-permute-start(bf16[16,16,128]{2,1,0:T(8,128)(2,1)S(1)} %get-tuple-element.60.refs_3_), channel_id=1, source_target_pairs={{0,2},{1,3},{2,0},{3,1},{4,6},{5,7},{6,4},{7,5},{8,10},{9,11},{10,... | collective-permute-start | bytes 196616 | tf_op jit(solution)/shard_map/ppermute | solution.py:282
  45.3 3.1 %collective-permute-start.22 = (bf16[16,16,128]{2,1,0:T(8,128)(2,1)S(1)}, bf16[16,16,128]{2,1,0:T(8,128)(2,1)S(1)}, u32[]{:S(2)}, u32[]{:S(2)}) collective-permute-start(bf16[16,16,128]{2,1,0:T(8,128)(2,1)S(1)} %get-tuple-element.60.refs_3_), channel_id=1, source_target_pairs={{0,1},{1,0},{2,3},{3,2},{4,5},{5,4},{6,7},{7,6},{8,9},{9,8},{10,11... | collective-permute-start | bytes 196616 | tf_op jit(solution)/shard_map/ppermute | solution.py:282
  48.5 7.1 %collective-permute-start.23 = (bf16[32,16,128]{2,1,0:T(8,128)(2,1)S(1)}, bf16[32,16,128]{2,1,0:T(8,128)(2,1)S(1)}, u32[]{:S(2)}, u32[]{:S(2)}) collective-permute-start(bf16[32,16,128]{2,1,0:T(8,128)(2,1)S(1)} %get-tuple-element.65), channel_id=1, source_target_pairs={{0,8},{4,12},{8,0},{12,4},{16,24},{20,28},{24,16},{28,20},{1,9},{5... | collective-permute-start | bytes 393224 | tf_op jit(solution)/shard_map/ppermute | solution.py:382
  56.1 4.2 %collective-permute-start.24 = (bf16[16,16,128]{2,1,0:T(8,128)(2,1)S(1)}, bf16[16,16,128]{2,1,0:T(8,128)(2,1)S(1)}, u32[]{:S(2)}, u32[]{:S(2)}) collective-permute-start(bf16[16,16,128]{2,1,0:T(8,128)(2,1)S(1)} %project.5.refs_5_), channel_id=1, source_target_pairs={{0,3},{1,2},{2,1},{3,0},{4,7},{5,6},{6,5},{7,4},{8,11},{9,10},{10,... | collective-permute-start | bytes 196616 | tf_op jit(solution)/shard_map/ppermute | solution.py:282
  57.0 3.8 %collective-permute-start.25 = (bf16[16,16,128]{2,1,0:T(8,128)(2,1)S(1)}, bf16[16,16,128]{2,1,0:T(8,128)(2,1)S(1)}, u32[]{:S(2)}, u32[]{:S(2)}) collective-permute-start(bf16[16,16,128]{2,1,0:T(8,128)(2,1)S(1)} %project.5.refs_5_), channel_id=1, source_target_pairs={{0,2},{1,3},{2,0},{3,1},{4,6},{5,7},{6,4},{7,5},{8,10},{9,11},{10,... | collective-permute-start | bytes 196616 | tf_op jit(solution)/shard_map/ppermute | solution.py:282
  58.1 3.1 %collective-permute-start.26 = (bf16[16,16,128]{2,1,0:T(8,128)(2,1)S(1)}, bf16[16,16,128]{2,1,0:T(8,128)(2,1)S(1)}, u32[]{:S(2)}, u32[]{:S(2)}) collective-permute-start(bf16[16,16,128]{2,1,0:T(8,128)(2,1)S(1)} %project.5.refs_5_), channel_id=1, source_target_pairs={{0,1},{1,0},{2,3},{3,2},{4,5},{5,4},{6,7},{7,6},{8,9},{9,8},{10,11... | collective-permute-start | bytes 196616 | tf_op jit(solution)/shard_map/ppermute | solution.py:282
  62.3 4.1 %collective-permute-start.27 = (bf16[16,16,128]{2,1,0:T(8,128)(2,1)S(1)}, bf16[16,16,128]{2,1,0:T(8,128)(2,1)S(1)}, u32[]{:S(2)}, u32[]{:S(2)}) collective-permute-start(bf16[16,16,128]{2,1,0:T(8,128)(2,1)S(1)} %get-tuple-element.66.refs_3_), channel_id=1, source_target_pairs={{0,3},{1,2},{2,1},{3,0},{4,7},{5,6},{6,5},{7,4},{8,11},{9,10},{10,... | collective-permute-start | bytes 196616 | tf_op jit(solution)/shard_map/ppermute | solution.py:282
  63.4 3.7 %collective-permute-start.28 = (bf16[16,16,128]{2,1,0:T(8,128)(2,1)S(1)}, bf16[16,16,128]{2,1,0:T(8,128)(2,1)S(1)}, u32[]{:S(2)}, u32[]{:S(2)}) collective-permute-start(bf16[16,16,128]{2,1,0:T(8,128)(2,1)S(1)} %get-tuple-element.66.refs_3_), channel_id=1, source_target_pairs={{0,2},{1,3},{2,0},{3,1},{4,6},{5,7},{6,4},{7,5},{8,10},{9,11},{10,... | collective-permute-start | bytes 196616 | tf_op jit(solution)/shard_map/ppermute | solution.py:282
  64.3 3.1 %collective-permute-start.29 = (bf16[16,16,128]{2,1,0:T(8,128)(2,1)S(1)}, bf16[16,16,128]{2,1,0:T(8,128)(2,1)S(1)}, u32[]{:S(2)}, u32[]{:S(2)}) collective-permute-start(bf16[16,16,128]{2,1,0:T(8,128)(2,1)S(1)} %get-tuple-element.66.refs_3_), channel_id=1, source_target_pairs={{0,1},{1,0},{2,3},{3,2},{4,5},{5,4},{6,7},{7,6},{8,9},{9,8},{10,11... | collective-permute-start | bytes 196616 | tf_op jit(solution)/shard_map/ppermute | solution.py:282
  68.0 14.1 %collective-permute-start.30 = (bf16[2,8,4096]{2,1,0:T(8,128)(2,1)S(1)}, bf16[2,8,4096]{2,1,0:T(8,128)(2,1)S(1)}, u32[]{:S(2)}, u32[]{:S(2)}) collective-permute-start(bf16[2,8,4096]{2,1,0:T(8,128)(2,1)S(1)} %get-tuple-element.72), channel_id=1, source_target_pairs={{0,4},{4,0},{8,12},{12,8},{16,20},{20,16},{24,28},{28,24},{1,5},{5... | collective-permute-start | bytes 393224 | tf_op jit(solution)/shard_map/ppermute | solution.py:274

commit v8 on v7

--- a/solution.py
+++ b/solution.py
@@ -285,6 +285,13 @@
         if direct:
             return [value] + [turned(value, d) for d in range(tiles - 1, 0, -1)]
         return [lax.all_gather(value, "tile")]
+
+    def summed(terms):
+        d = 1
+        while 2 * d < tiles:
+            terms = terms + turned(terms, d)
+            d *= 2
+        return [terms, turned(terms, d)]
 
     def call(kernel, smem, operands, out_shape, scratch, name):
         many = isinstance(out_shape, tuple)
@@ -388,7 +395,7 @@
                 [],
                 "project",
             )
-            terms = spread(terms)
+            terms = summed(terms)
             image32, shot, terms = call(
                 functools.partial(first_kernel, place, 0, len(terms)),
                 1,
@@ -397,7 +404,7 @@
                 [w_scr],
                 "first",
             )
-        terms = spread(terms)
+        terms = summed(terms)
         last = place == places - 1
         outs = call(
             functools.partial(second_kernel, place, last, len(terms)),

time: 83.2 us -> 95.9 us (1.15)
  waiting for transfers between devices: 30.7 us -> 40 us
  starting transfers between devices: 43.5 us -> 46.9 us
    ppermute x24 -> x17, waiting for transfers between devices: 18.2 us -> 27.4 us  [turned(): return lax.ppermute(value, ('subset', 'tile'), pairs)]
    ppermute x4, starting transfers between devices: 15.1 us -> 20.4 us  [swapped(): return lax.ppermute(value, 'subset', [(s, s ^ 1) for s in range(subsets)])]
    ppermute x3, starting transfers between devices: 6.66 us -> 5.27 us  [per_device(): image = lax.ppermute(image, 'subset', pairs)]
    ppermute x24 -> x17, starting transfers between devices: 21.7 us -> 21.3 us  [turned(): return lax.ppermute(value, ('subset', 'tile'), pairs)]
  transfers between devices with their start and end apart: 31 -> 24, of which waited for: 26 -> 19; matrix products, arithmetic and copies ran while one was open for 0% -> 0% of each run, Pallas kernels for 7% -> 6%
where the time goes in v8:
time: 95.9 us; the launch traced here: 95.7 us
  starting transfers between devices  46.9 us (49%)
  waiting for transfers between devices  40 us (42%)
  Pallas kernels  7.77 us (8%)
  other arithmetic  0.98 us (1%)
    ppermute x17, waiting for transfers between devices, turned(): return lax.ppermute(value, ('subset', 'tile'), pairs)  27.4 us
    ppermute x17, starting transfers between devices, turned(): return lax.ppermute(value, ('subset', 'tile'), pairs)  21.3 us
    ppermute x4, starting transfers between devices, swapped(): return lax.ppermute(value, 'subset', [(s, s ^ 1) for s in range(subsets)])  20.4 us
    ppermute x3, waiting for transfers between devices, per_device(): image = lax.ppermute(image, 'subset', pairs)  10.1 us
    ppermute x3, starting transfers between devices, per_device(): image = lax.ppermute(image, 'subset', pairs)  5.27 us
    pallas_call x1, Pallas kernels, per_device(): pl.pallas_call(functools.partial(head_kernel, row_blocks, chunks), out_sh...  2.95 us
    ppermute x4, waiting for transfers between devices, swapped(): return lax.ppermute(value, 'subset', [(s, s ^ 1) for s in range(subsets)])  2.48 us
    pallas_call x11, Pallas kernels, call(): pl.pallas_call(kernel, out_shape=out_shape, in_specs=[SMEM] * smem + [VME...  2.28 us
  transfers between devices with their start and end apart: 24, of which 19 were waited for; matrix products, arithmetic and copies ran while one was open for 0% of the time, Pallas kernels for 6%

profile of v8, /device:TPU:25, one launch (start us, length us, event | category | flops | bytes accessed | tf_op | source)
XLA Modules:
  0.0 95.7 jit_solution(5681964673263605714)
XLA Ops:
  0.0 0.7 collective-permute-start.1
  0.8 2.9 %head.1 = (f32[5,16,128]{2,1,0:T(8,128)S(1)}, f32[5,16,128]{2,1,0:T(8,128)S(1)}, s32[2,80]{1,0:T(2,128)S(1)}, s32[3,80]{1,0:T(4,128)S(4)}, bf16[1,1,80,128,128]{4,3,2,1,0:T(8,128)(2,1)S(1)}) custom-call(s32[3]{0:T(128)S(1)} %pad_add_fusion.pos, s32[1,1,80]{2,1,0:T(1,128)} %rows_in.1, s32[1,1,80]{2,1,0:T(1,128)} %cols_in.1, ...), custom_call_target="tpu_custom_call" | custom-call | tf_op jit(solution)/shard_map/head/pallas_call | solution.py:310
  3.8 1.5 %collective-permute-done.2 = f32[5,16,128]{2,1,0:T(8,128)S(1)} collective-permute-done((f32[5,16,128]{2,1,0:T(8,128)S(1)}, f32[5,16,128]{2,1,0:T(8,128)S(1)}, u32[]{:S(2)}, u32[]{:S(2)}) %collective-permute-start.2) | collective-permute-done | bytes 40992 | tf_op jit(solution)/shard_map/ppermute | solution.py:274
  5.3 2.2 %collective-permute-start.3 = (f32[2,5,16,128]{3,2,1,0:T(8,128)S(1)}, f32[2,5,16,128]{3,2,1,0:T(8,128)S(1)}, u32[]{:S(2)}, u32[]{:S(2)}) collective-permute-start(f32[2,5,16,128]{3,2,1,0:T(8,128)S(1)} %pad_maximum_fusion._.refs_3_), channel_id=1, source_target_pairs={{0,3},{1,2},{2,1},{3,0},{4,7},{5,6},{6,5},{7,4},{8,11},{9,10},{10,... | collective-permute-start | bytes 245768 | tf_op jit(solution)/shard_map/ppermute | solution.py:282
  7.4 0.2 collective-permute-start.4
  7.7 0.3 collective-permute-start.5
  7.9 1.2 %collective-permute-start = (s32[2,80]{1,0:T(2,128)S(1)}, s32[2,80]{1,0:T(2,128)S(1)}, u32[]{:S(2)}, u32[]{:S(2)}) collective-permute-start(s32[2,80]{1,0:T(2,128)S(1)} %get-tuple-element.40), channel_id=1, source_target_pairs={{0,4},{4,0},{8,12},{12,8},{16,20},{20,16},{24,28},{28,24},{1,5},{5... | collective-permute-start | bytes 1928 | tf_op jit(solution)/shard_map/ppermute | solution.py:274
  9.1 0.9 pack_own.1
  10.1 1.6 %pack_other.1 = (s32[3,80]{1,0:T(4,128)S(4)}, bf16[2,16,128,640]{3,2,1,0:T(8,128)(2,1)S(1)}, bf16[2,16,640,128]{3,2,1,0:T(8,128)(2,1)S(1)}) custom-call(s32[3,80]{1,0:T(4,128)S(4)} %get-tuple-element.39.own, s32[2,80]{1,0:T(2,128)S(1)} %collective-permute-done.table2, ...), custom_call_target="tpu_custom_call", output_to_operand_aliasing={{1}: (3, {}), {2}: (4, {})} | custom-call | tf_op jit(solution)/shard_map/pack_other/pallas_call | solution.py:357
  11.8 1.8 %collective-permute-start.6 = (bf16[16,16,128]{2,1,0:T(8,128)(2,1)S(1)}, bf16[16,16,128]{2,1,0:T(8,128)(2,1)S(1)}, u32[]{:S(2)}, u32[]{:S(2)}) collective-permute-start(bf16[16,16,128]{2,1,0:T(8,128)(2,1)S(1)} %get-tuple-element.50), channel_id=1, source_target_pairs={{0,1},{1,0},{2,3},{3,2},{4,5},{5,4},{6,7},{7,6},{8,9},{9,8},{10,11... | collective-permute-start | bytes 196616 | tf_op jit(solution)/shard_map/ppermute | solution.py:282
  13.6 1.7 %collective-permute-done.6 = bf16[16,16,128]{2,1,0:T(8,128)(2,1)S(1)} collective-permute-done((bf16[16,16,128]{2,1,0:T(8,128)(2,1)S(1)}, bf16[16,16,128]{2,1,0:T(8,128)(2,1)S(1)}, u32[]{:S(2)}, u32[]{:S(2)}) %collective-permute-start.6) | collective-permute-done | bytes 65568 | tf_op jit(solution)/shard_map/ppermute | solution.py:282
  15.3 1.6 %collective-permute-start.7 = (bf16[16,16,128]{2,1,0:T(8,128)(2,1)S(1)}, bf16[16,16,128]{2,1,0:T(8,128)(2,1)S(1)}, u32[]{:S(2)}, u32[]{:S(2)}) collective-permute-start(bf16[16,16,128]{2,1,0:T(8,128)(2,1)S(1)} %add.28.refs_3_), channel_id=1, source_target_pairs={{0,2},{1,3},{2,0},{3,1},{4,6},{5,7},{6,4},{7,5},{8,10},{9,11},{10,... | collective-permute-start | bytes 196616 | tf_op jit(solution)/shard_map/ppermute | solution.py:282
  16.9 1.7 %collective-permute-done.7.refs_4_ = bf16[16,16,128]{2,1,0:T(8,128)(2,1)S(1)} collective-permute-done((bf16[16,16,128]{2,1,0:T(8,128)(2,1)S(1)}, bf16[16,16,128]{2,1,0:T(8,128)(2,1)S(1)}, u32[]{:S(2)}, u32[]{:S(2)}) %collective-permute-start.7) | collective-permute-done | bytes 65568 | tf_op jit(solution)/shard_map/ppermute | solution.py:282
  18.7 3.6 %collective-permute-done.8.image.refs_4_ = bf16[32,16,128]{2,1,0:T(8,128)(2,1)S(1)} collective-permute-done((bf16[32,16,128]{2,1,0:T(8,128)(2,1)S(1)}, bf16[32,16,128]{2,1,0:T(8,128)(2,1)S(1)}, u32[]{:S(2)}, u32[]{:S(2)}) %collective-permute-start.8) | collective-permute-done | bytes 131104 | tf_op jit(solution)/shard_map/ppermute | solution.py:389
  22.3 1.4 %collective-permute-start.9 = (bf16[16,16,128]{2,1,0:T(8,128)(2,1)S(1)}, bf16[16,16,128]{2,1,0:T(8,128)(2,1)S(1)}, u32[]{:S(2)}, u32[]{:S(2)}) collective-permute-start(bf16[16,16,128]{2,1,0:T(8,128)(2,1)S(1)} %project.3), channel_id=1, source_target_pairs={{0,1},{1,0},{2,3},{3,2},{4,5},{5,4},{6,7},{7,6},{8,9},{9,8},{10,11... | collective-permute-start | bytes 196616 | tf_op jit(solution)/shard_map/ppermute | solution.py:282
  23.8 2.0 %collective-permute-done.9 = bf16[16,16,128]{2,1,0:T(8,128)(2,1)S(1)} collective-permute-done((bf16[16,16,128]{2,1,0:T(8,128)(2,1)S(1)}, bf16[16,16,128]{2,1,0:T(8,128)(2,1)S(1)}, u32[]{:S(2)}, u32[]{:S(2)}) %collective-permute-start.9) | collective-permute-done | bytes 65568 | tf_op jit(solution)/shard_map/ppermute | solution.py:282
  25.8 1.5 %collective-permute-start.10 = (bf16[16,16,128]{2,1,0:T(8,128)(2,1)S(1)}, bf16[16,16,128]{2,1,0:T(8,128)(2,1)S(1)}, u32[]{:S(2)}, u32[]{:S(2)}) collective-permute-start(bf16[16,16,128]{2,1,0:T(8,128)(2,1)S(1)} %add.29.refs_5_), channel_id=1, source_target_pairs={{0,2},{1,3},{2,0},{3,1},{4,6},{5,7},{6,4},{7,5},{8,10},{9,11},{10,... | collective-permute-start | bytes 196616 | tf_op jit(solution)/shard_map/ppermute | solution.py:282
  27.3 1.7 %collective-permute-done.10.refs_6_ = bf16[16,16,128]{2,1,0:T(8,128)(2,1)S(1)} collective-permute-done((bf16[16,16,128]{2,1,0:T(8,128)(2,1)S(1)}, bf16[16,16,128]{2,1,0:T(8,128)(2,1)S(1)}, u32[]{:S(2)}, u32[]{:S(2)}) %collective-permute-start.10) | collective-permute-done | bytes 65568 | tf_op jit(solution)/shard_map/ppermute | solution.py:282
  29.0 1.4 %collective-permute-start.11 = (bf16[16,16,128]{2,1,0:T(8,128)(2,1)S(1)}, bf16[16,16,128]{2,1,0:T(8,128)(2,1)S(1)}, u32[]{:S(2)}, u32[]{:S(2)}) collective-permute-start(bf16[16,16,128]{2,1,0:T(8,128)(2,1)S(1)} %get-tuple-element.54), channel_id=1, source_target_pairs={{0,1},{1,0},{2,3},{3,2},{4,5},{5,4},{6,7},{7,6},{8,9},{9,8},{10,11... | collective-permute-start | bytes 196616 | tf_op jit(solution)/shard_map/ppermute | solution.py:282
  30.4 1.7 %collective-permute-done.11 = bf16[16,16,128]{2,1,0:T(8,128)(2,1)S(1)} collective-permute-done((bf16[16,16,128]{2,1,0:T(8,128)(2,1)S(1)}, bf16[16,16,128]{2,1,0:T(8,128)(2,1)S(1)}, u32[]{:S(2)}, u32[]{:S(2)}) %collective-permute-start.11) | collective-permute-done | bytes 65568 | tf_op jit(solution)/shard_map/ppermute | solution.py:282
  32.1 1.5 %collective-permute-start.12 = (bf16[16,16,128]{2,1,0:T(8,128)(2,1)S(1)}, bf16[16,16,128]{2,1,0:T(8,128)(2,1)S(1)}, u32[]{:S(2)}, u32[]{:S(2)}) collective-permute-start(bf16[16,16,128]{2,1,0:T(8,128)(2,1)S(1)} %add.30.refs_3_), channel_id=1, source_target_pairs={{0,2},{1,3},{2,0},{3,1},{4,6},{5,7},{6,4},{7,5},{8,10},{9,11},{10,... | collective-permute-start | bytes 196616 | tf_op jit(solution)/shard_map/ppermute | solution.py:282
  33.6 1.8 %collective-permute-done.12.refs_4_ = bf16[16,16,128]{2,1,0:T(8,128)(2,1)S(1)} collective-permute-done((bf16[16,16,128]{2,1,0:T(8,128)(2,1)S(1)}, bf16[16,16,128]{2,1,0:T(8,128)(2,1)S(1)}, u32[]{:S(2)}, u32[]{:S(2)}) %collective-permute-start.12) | collective-permute-done | bytes 65568 | tf_op jit(solution)/shard_map/ppermute | solution.py:282
  35.4 1.7 %collective-permute-start.13 = (bf16[32,16,128]{2,1,0:T(8,128)(2,1)S(1)}, bf16[32,16,128]{2,1,0:T(8,128)(2,1)S(1)}, u32[]{:S(2)}, u32[]{:S(2)}) collective-permute-start(bf16[32,16,128]{2,1,0:T(8,128)(2,1)S(1)} %get-tuple-element.59), channel_id=1, source_target_pairs={{0,24},{4,28},{8,16},{12,20},{16,8},{20,12},{24,0},{28,4},{1,25},{... | collective-permute-start | bytes 393224 | tf_op jit(solution)/shard_map/ppermute | solution.py:389
  37.1 4.1 %collective-permute-done.13.image.refs_4_ = bf16[32,16,128]{2,1,0:T(8,128)(2,1)S(1)} collective-permute-done((bf16[32,16,128]{2,1,0:T(8,128)(2,1)S(1)}, bf16[32,16,128]{2,1,0:T(8,128)(2,1)S(1)}, u32[]{:S(2)}, u32[]{:S(2)}) %collective-permute-start.13) | collective-permute-done | bytes 131104 | tf_op jit(solution)/shard_map/ppermute | solution.py:389
  41.2 1.3 %collective-permute-start.14 = (bf16[16,16,128]{2,1,0:T(8,128)(2,1)S(1)}, bf16[16,16,128]{2,1,0:T(8,128)(2,1)S(1)}, u32[]{:S(2)}, u32[]{:S(2)}) collective-permute-start(bf16[16,16,128]{2,1,0:T(8,128)(2,1)S(1)} %project.4), channel_id=1, source_target_pairs={{0,1},{1,0},{2,3},{3,2},{4,5},{5,4},{6,7},{7,6},{8,9},{9,8},{10,11... | collective-permute-start | bytes 196616 | tf_op jit(solution)/shard_map/ppermute | solution.py:282
  42.5 1.8 %collective-permute-done.14 = bf16[16,16,128]{2,1,0:T(8,128)(2,1)S(1)} collective-permute-done((bf16[16,16,128]{2,1,0:T(8,128)(2,1)S(1)}, bf16[16,16,128]{2,1,0:T(8,128)(2,1)S(1)}, u32[]{:S(2)}, u32[]{:S(2)}) %collective-permute-start.14) | collective-permute-done | bytes 65568 | tf_op jit(solution)/shard_map/ppermute | solution.py:282
  44.3 1.4 %collective-permute-start.15 = (bf16[16,16,128]{2,1,0:T(8,128)(2,1)S(1)}, bf16[16,16,128]{2,1,0:T(8,128)(2,1)S(1)}, u32[]{:S(2)}, u32[]{:S(2)}) collective-permute-start(bf16[16,16,128]{2,1,0:T(8,128)(2,1)S(1)} %add.31.refs_5_), channel_id=1, source_target_pairs={{0,2},{1,3},{2,0},{3,1},{4,6},{5,7},{6,4},{7,5},{8,10},{9,11},{10,... | collective-permute-start | bytes 196616 | tf_op jit(solution)/shard_map/ppermute | solution.py:282
  45.8 1.8 %collective-permute-done.15.refs_6_ = bf16[16,16,128]{2,1,0:T(8,128)(2,1)S(1)} collective-permute-done((bf16[16,16,128]{2,1,0:T(8,128)(2,1)S(1)}, bf16[16,16,128]{2,1,0:T(8,128)(2,1)S(1)}, u32[]{:S(2)}, u32[]{:S(2)}) %collective-permute-start.15) | collective-permute-done | bytes 65568 | tf_op jit(solution)/shard_map/ppermute | solution.py:282
  47.5 1.3 %collective-permute-start.16 = (bf16[16,16,128]{2,1,0:T(8,128)(2,1)S(1)}, bf16[16,16,128]{2,1,0:T(8,128)(2,1)S(1)}, u32[]{:S(2)}, u32[]{:S(2)}) collective-permute-start(bf16[16,16,128]{2,1,0:T(8,128)(2,1)S(1)} %get-tuple-element.60), channel_id=1, source_target_pairs={{0,1},{1,0},{2,3},{3,2},{4,5},{5,4},{6,7},{7,6},{8,9},{9,8},{10,11... | collective-permute-start | bytes 196616 | tf_op jit(solution)/shard_map/ppermute | solution.py:282
  48.9 1.8 %collective-permute-done.16 = bf16[16,16,128]{2,1,0:T(8,128)(2,1)S(1)} collective-permute-done((bf16[16,16,128]{2,1,0:T(8,128)(2,1)S(1)}, bf16[16,16,128]{2,1,0:T(8,128)(2,1)S(1)}, u32[]{:S(2)}, u32[]{:S(2)}) %collective-permute-start.16) | collective-permute-done | bytes 65568 | tf_op jit(solution)/shard_map/ppermute | solution.py:282
  50.7 1.4 %collective-permute-start.17 = (bf16[16,16,128]{2,1,0:T(8,128)(2,1)S(1)}, bf16[16,16,128]{2,1,0:T(8,128)(2,1)S(1)}, u32[]{:S(2)}, u32[]{:S(2)}) collective-permute-start(bf16[16,16,128]{2,1,0:T(8,128)(2,1)S(1)} %add.32.refs_3_), channel_id=1, source_target_pairs={{0,2},{1,3},{2,0},{3,1},{4,6},{5,7},{6,4},{7,5},{8,10},{9,11},{10,... | collective-permute-start | bytes 196616 | tf_op jit(solution)/shard_map/ppermute | solution.py:282
  52.1 1.8 %collective-permute-done.17.refs_4_ = bf16[16,16,128]{2,1,0:T(8,128)(2,1)S(1)} collective-permute-done((bf16[16,16,128]{2,1,0:T(8,128)(2,1)S(1)}, bf16[16,16,128]{2,1,0:T(8,128)(2,1)S(1)}, u32[]{:S(2)}, u32[]{:S(2)}) %collective-permute-start.17) | collective-permute-done | bytes 65568 | tf_op jit(solution)/shard_map/ppermute | solution.py:282
  53.9 3.4 %collective-permute-start.18 = (bf16[32,16,128]{2,1,0:T(8,128)(2,1)S(1)}, bf16[32,16,128]{2,1,0:T(8,128)(2,1)S(1)}, u32[]{:S(2)}, u32[]{:S(2)}) collective-permute-start(bf16[32,16,128]{2,1,0:T(8,128)(2,1)S(1)} %get-tuple-element.65), channel_id=1, source_target_pairs={{0,8},{4,12},{8,0},{12,4},{16,24},{20,28},{24,16},{28,20},{1,9},{5... | collective-permute-start | bytes 393224 | tf_op jit(solution)/shard_map/ppermute | solution.py:389
  57.3 2.4 %collective-permute-done.18.image.refs_4_ = bf16[32,16,128]{2,1,0:T(8,128)(2,1)S(1)} collective-permute-done((bf16[32,16,128]{2,1,0:T(8,128)(2,1)S(1)}, bf16[32,16,128]{2,1,0:T(8,128)(2,1)S(1)}, u32[]{:S(2)}, u32[]{:S(2)}) %collective-permute-start.18) | collective-permute-done | bytes 131104 | tf_op jit(solution)/shard_map/ppermute | solution.py:389
  59.6 0.5 project.5
  60.1 1.4 %collective-permute-start.19 = (bf16[16,16,128]{2,1,0:T(8,128)(2,1)S(1)}, bf16[16,16,128]{2,1,0:T(8,128)(2,1)S(1)}, u32[]{:S(2)}, u32[]{:S(2)}) collective-permute-start(bf16[16,16,128]{2,1,0:T(8,128)(2,1)S(1)} %project.5), channel_id=1, source_target_pairs={{0,1},{1,0},{2,3},{3,2},{4,5},{5,4},{6,7},{7,6},{8,9},{9,8},{10,11... | collective-permute-start | bytes 196616 | tf_op jit(solution)/shard_map/ppermute | solution.py:282
  61.6 2.7 %collective-permute-done.19 = bf16[16,16,128]{2,1,0:T(8,128)(2,1)S(1)} collective-permute-done((bf16[16,16,128]{2,1,0:T(8,128)(2,1)S(1)}, bf16[16,16,128]{2,1,0:T(8,128)(2,1)S(1)}, u32[]{:S(2)}, u32[]{:S(2)}) %collective-permute-start.19) | collective-permute-done | bytes 65568 | tf_op jit(solution)/shard_map/ppermute | solution.py:282
  64.3 0.9 collective-permute-start.20
  65.2 2.3 %collective-permute-done.20.refs_6_ = bf16[16,16,128]{2,1,0:T(8,128)(2,1)S(1)} collective-permute-done((bf16[16,16,128]{2,1,0:T(8,128)(2,1)S(1)}, bf16[16,16,128]{2,1,0:T(8,128)(2,1)S(1)}, u32[]{:S(2)}, u32[]{:S(2)}) %collective-permute-start.20) | collective-permute-done | bytes 65568 | tf_op jit(solution)/shard_map/ppermute | solution.py:282
  67.5 1.1 %first.7 = (f32[32,16,128]{2,1,0:T(8,128)S(1)}, bf16[32,16,128]{2,1,0:T(8,128)(2,1)S(1)}, bf16[16,16,128]{2,1,0:T(8,128)(2,1)S(1)}) custom-call(s32[3,80]{1,0:T(4,128)S(4)} %get-tuple-element.46.refs_0_.info, bf16[2,16,128,640]{3,2,1,0:T(8,128)(2,1)S(1)} %get-tuple-element.47.refs_1_.refs_2_, bf16[2,16,640,128]{3,2,1,0:T(8,128)(2,1)S(1)} %get-tuple-element.48.refs_2_.tall, ...), custom_call_target="tpu_custom_call" | custom-call | tf_op jit(solution)/shard_map/first/pallas_call | solution.py:298
  68.6 0.7 collective-permute-start.21
  69.3 2.5 %collective-permute-done.21 = bf16[16,16,128]{2,1,0:T(8,128)(2,1)S(1)} collective-permute-done((bf16[16,16,128]{2,1,0:T(8,128)(2,1)S(1)}, bf16[16,16,128]{2,1,0:T(8,128)(2,1)S(1)}, u32[]{:S(2)}, u32[]{:S(2)}) %collective-permute-start.21) | collective-permute-done | bytes 65568 | tf_op jit(solution)/shard_map/ppermute | solution.py:282
  71.8 0.9 collective-permute-start.22
  72.7 2.3 %collective-permute-done.22.refs_4_ = bf16[16,16,128]{2,1,0:T(8,128)(2,1)S(1)} collective-permute-done((bf16[16,16,128]{2,1,0:T(8,128)(2,1)S(1)}, bf16[16,16,128]{2,1,0:T(8,128)(2,1)S(1)}, u32[]{:S(2)}, u32[]{:S(2)}) %collective-permute-start.22) | collective-permute-done | bytes 65568 | tf_op jit(solution)/shard_map/ppermute | solution.py:282
  75.0 0.6 second.7
  75.6 18.4 %collective-permute-start.23 = (bf16[2,8,4096]{2,1,0:T(8,128)(2,1)S(1)}, bf16[2,8,4096]{2,1,0:T(8,128)(2,1)S(1)}, u32[]{:S(2)}, u32[]{:S(2)}) collective-permute-start(bf16[2,8,4096]{2,1,0:T(8,128)(2,1)S(1)} %get-tuple-element.72), channel_id=1, source_target_pairs={{0,4},{4,0},{8,12},{12,8},{16,20},{20,16},{24,28},{28,24},{1,5},{5... | collective-permute-start | bytes 393224 | tf_op jit(solution)/shard_map/ppermute | solution.py:274
  94.0 1.0 %collective-permute-done.23 = bf16[2,8,4096]{2,1,0:T(8,128)(2,1)S(1)} collective-permute-done((bf16[2,8,4096]{2,1,0:T(8,128)(2,1)S(1)}, bf16[2,8,4096]{2,1,0:T(8,128)(2,1)S(1)}, u32[]{:S(2)}, u32[]{:S(2)}) %collective-permute-start.23) | collective-permute-done | bytes 131104 | tf_op jit(solution)/shard_map/ppermute | solution.py:274
  95.0 0.7 maximum_bitcast_fusion
  (25 shorter events, 0.6 us)
Async XLA Ops:
  0.0 10.1 %collective-permute-start.1 = (bf16[1,1,80,128,128]{4,3,2,1,0:T(8,128)(2,1)}, bf16[1,1,80,128,128]{4,3,2,1,0:T(8,128)(2,1)S(1)}, u32[]{:S(2)}, u32[]{:S(2)}) collective-permute-start(bf16[1,1,80,128,128]{4,3,2,1,0:T(8,128)(2,1)} %blocks_in.1), channel_id=1, source_target_pairs={{0,4},{4,0},{8,12},{12,8},{16,20},{20,16},{24,28},{28,24},{1,5},{5... | collective-permute-start | bytes 7864328 | tf_op jit(solution)/shard_map/ppermute | solution.py:274
  3.7 1.6 %collective-permute-start.2 = (f32[5,16,128]{2,1,0:T(8,128)S(1)}, f32[5,16,128]{2,1,0:T(8,128)S(1)}, u32[]{:S(2)}, u32[]{:S(2)}) collective-permute-start(f32[5,16,128]{2,1,0:T(8,128)S(1)} %get-tuple-element.43), channel_id=1, source_target_pairs={{0,4},{4,0},{8,12},{12,8},{16,20},{20,16},{24,28},{28,24},{1,5},{5... | collective-permute-start | bytes 122888 | tf_op jit(solution)/shard_map/ppermute | solution.py:274
  5.3 6.4 %collective-permute-start.3 = (f32[2,5,16,128]{3,2,1,0:T(8,128)S(1)}, f32[2,5,16,128]{3,2,1,0:T(8,128)S(1)}, u32[]{:S(2)}, u32[]{:S(2)}) collective-permute-start(f32[2,5,16,128]{3,2,1,0:T(8,128)S(1)} %pad_maximum_fusion._.refs_3_), channel_id=1, source_target_pairs={{0,3},{1,2},{2,1},{3,0},{4,7},{5,6},{6,5},{7,4},{8,11},{9,10},{10,... | collective-permute-start | bytes 245768 | tf_op jit(solution)/shard_map/ppermute | solution.py:282
  7.4 4.3 %collective-permute-start.4 = (f32[2,5,16,128]{3,2,1,0:T(8,128)S(1)}, f32[2,5,16,128]{3,2,1,0:T(8,128)S(1)}, u32[]{:S(2)}, u32[]{:S(2)}) collective-permute-start(f32[2,5,16,128]{3,2,1,0:T(8,128)S(1)} %pad_maximum_fusion._.refs_3_), channel_id=1, source_target_pairs={{0,2},{1,3},{2,0},{3,1},{4,6},{5,7},{6,4},{7,5},{8,10},{9,11},{10,... | collective-permute-start | bytes 245768 | tf_op jit(solution)/shard_map/ppermute | solution.py:282
  7.7 4.1 %collective-permute-start.5 = (f32[2,5,16,128]{3,2,1,0:T(8,128)S(1)}, f32[2,5,16,128]{3,2,1,0:T(8,128)S(1)}, u32[]{:S(2)}, u32[]{:S(2)}) collective-permute-start(f32[2,5,16,128]{3,2,1,0:T(8,128)S(1)} %pad_maximum_fusion._.refs_3_), channel_id=1, source_target_pairs={{0,1},{1,0},{2,3},{3,2},{4,5},{5,4},{6,7},{7,6},{8,9},{9,8},{10,11... | collective-permute-start | bytes 245768 | tf_op jit(solution)/shard_map/ppermute | solution.py:282
  7.9 2.2 %collective-permute-start = (s32[2,80]{1,0:T(2,128)S(1)}, s32[2,80]{1,0:T(2,128)S(1)}, u32[]{:S(2)}, u32[]{:S(2)}) collective-permute-start(s32[2,80]{1,0:T(2,128)S(1)} %get-tuple-element.40), channel_id=1, source_target_pairs={{0,4},{4,0},{8,12},{12,8},{16,20},{20,16},{24,28},{28,24},{1,5},{5... | collective-permute-start | bytes 1928 | tf_op jit(solution)/shard_map/ppermute | solution.py:274
  11.8 3.5 %collective-permute-start.6 = (bf16[16,16,128]{2,1,0:T(8,128)(2,1)S(1)}, bf16[16,16,128]{2,1,0:T(8,128)(2,1)S(1)}, u32[]{:S(2)}, u32[]{:S(2)}) collective-permute-start(bf16[16,16,128]{2,1,0:T(8,128)(2,1)S(1)} %get-tuple-element.50), channel_id=1, source_target_pairs={{0,1},{1,0},{2,3},{3,2},{4,5},{5,4},{6,7},{7,6},{8,9},{9,8},{10,11... | collective-permute-start | bytes 196616 | tf_op jit(solution)/shard_map/ppermute | solution.py:282
  15.3 3.2 %collective-permute-start.7 = (bf16[16,16,128]{2,1,0:T(8,128)(2,1)S(1)}, bf16[16,16,128]{2,1,0:T(8,128)(2,1)S(1)}, u32[]{:S(2)}, u32[]{:S(2)}) collective-permute-start(bf16[16,16,128]{2,1,0:T(8,128)(2,1)S(1)} %add.28.refs_3_), channel_id=1, source_target_pairs={{0,2},{1,3},{2,0},{3,1},{4,6},{5,7},{6,4},{7,5},{8,10},{9,11},{10,... | collective-permute-start | bytes 196616 | tf_op jit(solution)/shard_map/ppermute | solution.py:282
  18.5 3.8 %collective-permute-start.8 = (bf16[32,16,128]{2,1,0:T(8,128)(2,1)S(1)}, bf16[32,16,128]{2,1,0:T(8,128)(2,1)S(1)}, u32[]{:S(2)}, u32[]{:S(2)}) collective-permute-start(bf16[32,16,128]{2,1,0:T(8,128)(2,1)S(1)} %get-tuple-element.53), channel_id=1, source_target_pairs={{0,8},{4,12},{8,0},{12,4},{16,24},{20,28},{24,16},{28,20},{1,9},{5... | collective-permute-start | bytes 393224 | tf_op jit(solution)/shard_map/ppermute | solution.py:389
  22.3 3.4 %collective-permute-start.9 = (bf16[16,16,128]{2,1,0:T(8,128)(2,1)S(1)}, bf16[16,16,128]{2,1,0:T(8,128)(2,1)S(1)}, u32[]{:S(2)}, u32[]{:S(2)}) collective-permute-start(bf16[16,16,128]{2,1,0:T(8,128)(2,1)S(1)} %project.3), channel_id=1, source_target_pairs={{0,1},{1,0},{2,3},{3,2},{4,5},{5,4},{6,7},{7,6},{8,9},{9,8},{10,11... | collective-permute-start | bytes 196616 | tf_op jit(solution)/shard_map/ppermute | solution.py:282
  25.8 3.2 %collective-permute-start.10 = (bf16[16,16,128]{2,1,0:T(8,128)(2,1)S(1)}, bf16[16,16,128]{2,1,0:T(8,128)(2,1)S(1)}, u32[]{:S(2)}, u32[]{:S(2)}) collective-permute-start(bf16[16,16,128]{2,1,0:T(8,128)(2,1)S(1)} %add.29.refs_5_), channel_id=1, source_target_pairs={{0,2},{1,3},{2,0},{3,1},{4,6},{5,7},{6,4},{7,5},{8,10},{9,11},{10,... | collective-permute-start | bytes 196616 | tf_op jit(solution)/shard_map/ppermute | solution.py:282
  29.0 3.1 %collective-permute-start.11 = (bf16[16,16,128]{2,1,0:T(8,128)(2,1)S(1)}, bf16[16,16,128]{2,1,0:T(8,128)(2,1)S(1)}, u32[]{:S(2)}, u32[]{:S(2)}) collective-permute-start(bf16[16,16,128]{2,1,0:T(8,128)(2,1)S(1)} %get-tuple-element.54), channel_id=1, source_target_pairs={{0,1},{1,0},{2,3},{3,2},{4,5},{5,4},{6,7},{7,6},{8,9},{9,8},{10,11... | collective-permute-start | bytes 196616 | tf_op jit(solution)/shard_map/ppermute | solution.py:282
  32.1 3.3 %collective-permute-start.12 = (bf16[16,16,128]{2,1,0:T(8,128)(2,1)S(1)}, bf16[16,16,128]{2,1,0:T(8,128)(2,1)S(1)}, u32[]{:S(2)}, u32[]{:S(2)}) collective-permute-start(bf16[16,16,128]{2,1,0:T(8,128)(2,1)S(1)} %add.30.refs_3_), channel_id=1, source_target_pairs={{0,2},{1,3},{2,0},{3,1},{4,6},{5,7},{6,4},{7,5},{8,10},{9,11},{10,... | collective-permute-start | bytes 196616 | tf_op jit(solution)/shard_map/ppermute | solution.py:282
  35.4 5.8 %collective-permute-start.13 = (bf16[32,16,128]{2,1,0:T(8,128)(2,1)S(1)}, bf16[32,16,128]{2,1,0:T(8,128)(2,1)S(1)}, u32[]{:S(2)}, u32[]{:S(2)}) collective-permute-start(bf16[32,16,128]{2,1,0:T(8,128)(2,1)S(1)} %get-tuple-element.59), channel_id=1, source_target_pairs={{0,24},{4,28},{8,16},{12,20},{16,8},{20,12},{24,0},{28,4},{1,25},{... | collective-permute-start | bytes 393224 | tf_op jit(solution)/shard_map/ppermute | solution.py:389
  41.2 3.1 %collective-permute-start.14 = (bf16[16,16,128]{2,1,0:T(8,128)(2,1)S(1)}, bf16[16,16,128]{2,1,0:T(8,128)(2,1)S(1)}, u32[]{:S(2)}, u32[]{:S(2)}) collective-permute-start(bf16[16,16,128]{2,1,0:T(8,128)(2,1)S(1)} %project.4), channel_id=1, source_target_pairs={{0,1},{1,0},{2,3},{3,2},{4,5},{5,4},{6,7},{7,6},{8,9},{9,8},{10,11... | collective-permute-start | bytes 196616 | tf_op jit(solution)/shard_map/ppermute | solution.py:282
  44.3 3.2 %collective-permute-start.15 = (bf16[16,16,128]{2,1,0:T(8,128)(2,1)S(1)}, bf16[16,16,128]{2,1,0:T(8,128)(2,1)S(1)}, u32[]{:S(2)}, u32[]{:S(2)}) collective-permute-start(bf16[16,16,128]{2,1,0:T(8,128)(2,1)S(1)} %add.31.refs_5_), channel_id=1, source_target_pairs={{0,2},{1,3},{2,0},{3,1},{4,6},{5,7},{6,4},{7,5},{8,10},{9,11},{10,... | collective-permute-start | bytes 196616 | tf_op jit(solution)/shard_map/ppermute | solution.py:282
  47.5 3.1 %collective-permute-start.16 = (bf16[16,16,128]{2,1,0:T(8,128)(2,1)S(1)}, bf16[16,16,128]{2,1,0:T(8,128)(2,1)S(1)}, u32[]{:S(2)}, u32[]{:S(2)}) collective-permute-start(bf16[16,16,128]{2,1,0:T(8,128)(2,1)S(1)} %get-tuple-element.60), channel_id=1, source_target_pairs={{0,1},{1,0},{2,3},{3,2},{4,5},{5,4},{6,7},{7,6},{8,9},{9,8},{10,11... | collective-permute-start | bytes 196616 | tf_op jit(solution)/shard_map/ppermute | solution.py:282
  50.7 3.2 %collective-permute-start.17 = (bf16[16,16,128]{2,1,0:T(8,128)(2,1)S(1)}, bf16[16,16,128]{2,1,0:T(8,128)(2,1)S(1)}, u32[]{:S(2)}, u32[]{:S(2)}) collective-permute-start(bf16[16,16,128]{2,1,0:T(8,128)(2,1)S(1)} %add.32.refs_3_), channel_id=1, source_target_pairs={{0,2},{1,3},{2,0},{3,1},{4,6},{5,7},{6,4},{7,5},{8,10},{9,11},{10,... | collective-permute-start | bytes 196616 | tf_op jit(solution)/shard_map/ppermute | solution.py:282
  53.9 5.7 %collective-permute-start.18 = (bf16[32,16,128]{2,1,0:T(8,128)(2,1)S(1)}, bf16[32,16,128]{2,1,0:T(8,128)(2,1)S(1)}, u32[]{:S(2)}, u32[]{:S(2)}) collective-permute-start(bf16[32,16,128]{2,1,0:T(8,128)(2,1)S(1)} %get-tuple-element.65), channel_id=1, source_target_pairs={{0,8},{4,12},{8,0},{12,4},{16,24},{20,28},{24,16},{28,20},{1,9},{5... | collective-permute-start | bytes 393224 | tf_op jit(solution)/shard_map/ppermute | solution.py:389
  60.1 4.2 %collective-permute-start.19 = (bf16[16,16,128]{2,1,0:T(8,128)(2,1)S(1)}, bf16[16,16,128]{2,1,0:T(8,128)(2,1)S(1)}, u32[]{:S(2)}, u32[]{:S(2)}) collective-permute-start(bf16[16,16,128]{2,1,0:T(8,128)(2,1)S(1)} %project.5), channel_id=1, source_target_pairs={{0,1},{1,0},{2,3},{3,2},{4,5},{5,4},{6,7},{7,6},{8,9},{9,8},{10,11... | collective-permute-start | bytes 196616 | tf_op jit(solution)/shard_map/ppermute | solution.py:282
  64.3 3.2 %collective-permute-start.20 = (bf16[16,16,128]{2,1,0:T(8,128)(2,1)S(1)}, bf16[16,16,128]{2,1,0:T(8,128)(2,1)S(1)}, u32[]{:S(2)}, u32[]{:S(2)}) collective-permute-start(bf16[16,16,128]{2,1,0:T(8,128)(2,1)S(1)} %add.33.refs_5_), channel_id=1, source_target_pairs={{0,2},{1,3},{2,0},{3,1},{4,6},{5,7},{6,4},{7,5},{8,10},{9,11},{10,... | collective-permute-start | bytes 196616 | tf_op jit(solution)/shard_map/ppermute | solution.py:282
  68.6 3.2 %collective-permute-start.21 = (bf16[16,16,128]{2,1,0:T(8,128)(2,1)S(1)}, bf16[16,16,128]{2,1,0:T(8,128)(2,1)S(1)}, u32[]{:S(2)}, u32[]{:S(2)}) collective-permute-start(bf16[16,16,128]{2,1,0:T(8,128)(2,1)S(1)} %get-tuple-element.66), channel_id=1, source_target_pairs={{0,1},{1,0},{2,3},{3,2},{4,5},{5,4},{6,7},{7,6},{8,9},{9,8},{10,11... | collective-permute-start | bytes 196616 | tf_op jit(solution)/shard_map/ppermute | solution.py:282
  71.8 3.2 %collective-permute-start.22 = (bf16[16,16,128]{2,1,0:T(8,128)(2,1)S(1)}, bf16[16,16,128]{2,1,0:T(8,128)(2,1)S(1)}, u32[]{:S(2)}, u32[]{:S(2)}) collective-permute-start(bf16[16,16,128]{2,1,0:T(8,128)(2,1)S(1)} %add.34.refs_3_), channel_id=1, source_target_pairs={{0,2},{1,3},{2,0},{3,1},{4,6},{5,7},{6,4},{7,5},{8,10},{9,11},{10,... | collective-permute-start | bytes 196616 | tf_op jit(solution)/shard_map/ppermute | solution.py:282
  75.6 19.4 %collective-permute-start.23 = (bf16[2,8,4096]{2,1,0:T(8,128)(2,1)S(1)}, bf16[2,8,4096]{2,1,0:T(8,128)(2,1)S(1)}, u32[]{:S(2)}, u32[]{:S(2)}) collective-permute-start(bf16[2,8,4096]{2,1,0:T(8,128)(2,1)S(1)} %get-tuple-element.72), channel_id=1, source_target_pairs={{0,4},{4,0},{8,12},{12,8},{16,20},{20,16},{24,28},{28,24},{1,5},{5... | collective-permute-start | bytes 393224 | tf_op jit(solution)/shard_map/ppermute | solution.py:274

commit v9 on v7

v9 whole, which is shorter than its diff:
```python
import functools

import jax
import jax.numpy as jnp
from jax import lax
from jax.experimental import pallas as pl
from jax.experimental.pallas import tpu as pltpu
from jax.sharding import PartitionSpec as P

BS = 128
PIX = 4096
CB = PIX // BS
relaxation = 0.5

DIRECT = 4

NN = (((1,), (0,)), ((), ()))
NT = (((1,), (1,)), ((), ()))
VMEM = pl.BlockSpec(memory_space=pltpu.VMEM)
SMEM = pl.BlockSpec(memory_space=pltpu.SMEM)
PARAMS = pltpu.CompilerParams(vmem_limit_bytes=20 * 2**20)


def dot(lhs, rhs, dims):
    return lax.dot_general(lhs, rhs, dims, preferred_element_type=jnp.float32)


def head_kernel(row_blocks, chunks, pos, rows_in, cols_in, blocks_in, rays_in, *refs):
    note, table, own, blocks, rows, cols, rays, seen, squares, sems = refs
    count = blocks.shape[2]
    each = count // row_blocks
    per_chunk = count // chunks
    batches, per_batch, here = rays.shape
    quarter = here // BS
    small = [
        pltpu.make_async_copy(src, dst, sems.at[i])
        for i, (src, dst) in enumerate(((rows_in, rows), (cols_in, cols), (rays_in, rays)))
    ]
    large = []
    for k in range(chunks):
        where = pl.ds(k * per_chunk, per_chunk)
        large.append(
            pltpu.make_async_copy(
                blocks_in.at[0, 0, where], blocks.at[0, 0, where], sems.at[3 + k]
            )
        )
    for copy in small + large:
        copy.start()
    squares[...] = jnp.zeros_like(squares)
    for copy in small:
        copy.wait()
    for i in range(3):
        own[0, i] = pos[i]
    for r in range(row_blocks):
        seen[r] = r * each
    for n in range(count):
        row = rows[0, 0, n]
        at = seen[row]
        seen[row] = at + 1
        col = cols[0, 0, n]
        for out, first in ((table, 0), (own, 1)):
            out[first, at] = n
            out[first + 1, at] = col
    for i in range(quarter):
        parts = [rays[g, :, i * BS : (i + 1) * BS] for g in range(batches)]
        note[i] = jnp.concatenate(parts, axis=0)
    for k in range(chunks):
        large[k].wait()
        for n in range(k * per_chunk, (k + 1) * per_chunk):
            block = blocks[0, 0, n].astype(jnp.float32)
            row = rows[0, 0, n]
            squares[row] = squares[row] + block * block
    ones = jnp.ones((BS, BS), jnp.bfloat16)
    on_diagonal = lax.broadcasted_iota(jnp.int32, (BS, BS), 0) == lax.broadcasted_iota(
        jnp.int32, (BS, BS), 1
    )
    for r in range(row_blocks):
        left = squares[r]
        coarse = left.astype(jnp.bfloat16)
        fine = (left - coarse.astype(jnp.float32)).astype(jnp.bfloat16)
        total = dot(coarse, ones, NN) + dot(fine, ones, NN)
        total = jnp.sum(jnp.where(on_diagonal, total, 0.0), axis=0, keepdims=True)
        note[quarter, r : r + 1] = total


def pack_own_kernel(own, blocks, _, wide):
    row_blocks = wide.shape[0]
    each = wide.shape[2] // BS
    for r in range(row_blocks):
        for j in range(each):
            block = blocks[0, 0, own[1, r * each + j]]
            wide[r, :, j * BS : (j + 1) * BS] = block


def pack_other_kernel(own, table2, blocks2, info, tall):
    row_blocks = tall.shape[0]
    each = tall.shape[1] // BS
    for i in range(3):
        info[0, i] = own[0, i]
    for r in range(row_blocks):
        for j in range(each):
            k = r * each + j
            info[1, k] = own[2, k]
            info[2, k] = table2[1, k]
            block = blocks2[0, 0, table2[0, k]]
            tall[r, j * BS : (j + 1) * BS] = block.T


def gather_rays(info, notes, rays, rays_scr):
    tiles, quarter, _, _ = rays_scr.shape
    row_blocks = tiles * quarter
    if len(notes) > 1:
        norms = sum(ref[quarter] for ref in notes)[0:row_blocks]
        for i, ref in enumerate(notes):
            rays_scr[info[0, 2] ^ i] = ref[0:quarter]
    else:
        norms = sum(notes[0][t, quarter] for t in range(tiles))[0:row_blocks]
        rays_scr[...] = notes[0][:, 0:quarter]
    scale = relaxation / norms
    for r in range(row_blocks):
        row = scale[r : r + 1]
        rays[r] = rays_scr[r // quarter, r % quarter] * row
        rays[row_blocks, r : r + 1] = row


def weights(rays, terms, w_scr):
    row_blocks = w_scr.shape[0]
    for r in range(row_blocks):
        left = rays[r]
        if terms:
            total = sum(ref[r].astype(jnp.float32) for ref in terms)
            left = left - total * rays[row_blocks, r : r + 1]
        w_scr[r] = left.astype(jnp.bfloat16)


def back_project(info, wide, w_scr, image):
    row_blocks = wide.shape[0]
    each = wide.shape[2] // BS
    for r in range(row_blocks):
        back = dot(w_scr[r], wide[r], NN)
        for j in range(each):
            col = info[1, r * each + j]
            image[col] = image[col] + back[:, j * BS : (j + 1) * BS]


def project(info, tall, image, terms):
    row_blocks = tall.shape[0]
    each = tall.shape[1] // BS
    for r in range(row_blocks):
        parts = [image[info[2, r * each + j]] for j in range(each)]
        total = dot(jnp.concatenate(parts, axis=1), tall[r], NN)
        terms[r] = total.astype(jnp.bfloat16)


def take(refs, n):
    taken = refs[:n]
    del refs[:n]
    return taken


def on_core(info, place, core):
    return jnp.logical_and(info[0, 0] == place, info[0, 1] == core)


def project_kernel(place, info, image, tall, terms):
    @pl.when(on_core(info, place, 1))
    def _():
        project(info, tall, image, terms)


def first_kernel(place, n_notes, n_terms, *refs):
    refs = list(refs)
    info, wide, tall = take(refs, 3)
    if place == 0:
        notes, terms_in = take(refs, n_notes), []
        shot, terms, rays, w_scr, x_scr, rays_scr = refs
        gather_rays(info, notes, rays, rays_scr)
    else:
        rays, image_in = take(refs, 2)
        terms_in = take(refs, n_terms)
        shot, terms, w_scr, x_scr = refs

    @pl.when(on_core(info, place, 0))
    def _():
        weights(rays, terms_in, w_scr)
        if place == 0:
            x_scr[...] = jnp.zeros_like(x_scr)
        else:
            x_scr[...] = image_in[...].astype(jnp.float32)
        back_project(info, wide, w_scr, x_scr)
        shot[...] = x_scr[...].astype(jnp.bfloat16)
        project(info, tall, shot, terms)


def second_kernel(place, last, n_terms, *refs):
    refs = list(refs)
    info, rays, wide, image_in, shot = take(refs, 5)
    terms_in = take(refs, n_terms)
    held = take(refs, 1) if place > 0 else []
    image = None if last else take(refs, 1)[0]
    out, w_scr, x_scr = refs
    batches, per_batch, _ = out.shape

    def write(source):
        if not last:
            out[...] = source[...].astype(jnp.bfloat16)
            return
        for c in range(CB):
            value = source[c].astype(jnp.float32).reshape(batches, per_batch, BS)
            out[:, :, c * BS : (c + 1) * BS] = value.astype(jnp.bfloat16)

    @pl.when(on_core(info, place, 1))
    def _():
        weights(rays, terms_in, w_scr)
        x_scr[...] = image_in[...].astype(jnp.float32)
        back_project(info, wide, w_scr, x_scr)
        if not last:
            image[...] = x_scr[...].astype(jnp.bfloat16)
        write(x_scr)

    @pl.when(on_core(info, place, 0))
    def _():
        write(shot)

    if held:

        @pl.when(info[0, 0] != place)
        def _():
            write(held[0])


def per_device(blocks, block_rows, block_cols, sinogram):
    batches, per_batch, here = sinogram.shape
    slices = batches * per_batch
    quarter = here // BS
    count = blocks.shape[2]
    subsets = lax.axis_size("subset")
    tiles = lax.axis_size("tile")
    row_blocks = quarter * tiles
    each = count // row_blocks
    places = subsets // 2
    direct = tiles <= DIRECT
    subset = lax.axis_index("subset")
    pos = jnp.stack([subset // 2, subset % 2, lax.axis_index("tile")]).astype(jnp.int32)

    image_shape = (CB, slices, BS)
    image_out = jax.ShapeDtypeStruct(image_shape, jnp.bfloat16)
    terms_out = jax.ShapeDtypeStruct((row_blocks, slices, BS), jnp.bfloat16)
    rays_out = jax.ShapeDtypeStruct((row_blocks + 1, slices, BS), jnp.float32)
    final_out = jax.ShapeDtypeStruct((batches, per_batch, PIX), jnp.bfloat16)
    w_scr = pltpu.VMEM((row_blocks, slices, BS), jnp.bfloat16)
    x_scr = pltpu.VMEM(image_shape, jnp.float32)
    rays_scr = pltpu.VMEM((tiles, quarter, slices, BS), jnp.float32)

    def sent(value, target):
        pairs = []
        for p in range(places):
            for c in range(2):
                for t in range(tiles):
                    q, e, u = target(p, c, t)
                    pairs.append(((2 * p + c) * tiles + t, (2 * q + e) * tiles + u))
        return lax.ppermute(value, ("subset", "tile"), pairs)

    def swapped(value):
        return sent(value, lambda p, c, t: (p, 1 - c, t))

    def spread(value):
        if direct:
            far = range(1, tiles)
            return [value] + [sent(value, lambda p, c, t: (p, c, t ^ d)) for d in far]
        return [lax.all_gather(value, "tile")]

    def passed(terms, core):
        if not direct:
            return [swapped(lax.psum(terms, "tile"))]
        return [
            sent(terms, lambda p, c, t: (p, 1 - c, t ^ d if c == core else t))
            for d in range(tiles)
        ]

    def call(kernel, smem, operands, out_shape, scratch, name):
        many = isinstance(out_shape, tuple)
        return pl.pallas_call(
            kernel,
            out_shape=out_shape,
            in_specs=[SMEM] * smem + [VMEM] * (len(operands) - smem),
            out_specs=(VMEM,) * len(out_shape) if many else VMEM,
            scratch_shapes=scratch,
            compiler_params=PARAMS,
            name=name,
        )(*operands)

    blocks2 = swapped(blocks)
    chunks = 8 if count % 8 == 0 else 1
    note, table, own, blocks = pl.pallas_call(
        functools.partial(head_kernel, row_blocks, chunks),
        out_shape=(
            jax.ShapeDtypeStruct((quarter + 1, slices, BS), jnp.float32),
            jax.ShapeDtypeStruct((2, count), jnp.int32),
            pltpu.SMEM((3, count), jnp.int32),
            pltpu.VMEM(blocks.shape, blocks.dtype),
        ),
        in_specs=[SMEM] + [pl.BlockSpec(memory_space=pltpu.HBM)] * 4,
        out_specs=(VMEM, SMEM, SMEM, VMEM),
        scratch_shapes=[
            pltpu.SMEM(block_rows.shape, jnp.int32),
            pltpu.SMEM(block_cols.shape, jnp.int32),
            pltpu.VMEM(sinogram.shape, jnp.float32),
            pltpu.SMEM((row_blocks,), jnp.int32),
            pltpu.VMEM((row_blocks, BS, BS), jnp.float32),
            pltpu.SemaphoreType.DMA((3 + chunks,)),
        ],
        compiler_params=PARAMS,
        name="head",
    )(
        pos,
        *(
            pltpu.with_memory_space_constraint(value, pltpu.HBM)
            for value in (block_rows, block_cols, blocks, sinogram)
        ),
    )
    notes = spread(note)
    table2 = swapped(table)

    own = pltpu.with_memory_space_constraint(own, pltpu.SMEM)
    blocks2 = pltpu.with_memory_space_constraint(blocks2, pltpu.VMEM)
    wide = pl.pallas_call(
        pack_own_kernel,
        out_shape=pltpu.VMEM((row_blocks, BS, each * BS), jnp.bfloat16),
        in_specs=[SMEM, VMEM, pl.BlockSpec(memory_space=pl.ANY)],
        out_specs=VMEM,
        compiler_params=PARAMS,
        name="pack_own",
    )(own, blocks, note)
    info, tall = pl.pallas_call(
        pack_other_kernel,
        out_shape=(
            pltpu.SMEM((3, count), jnp.int32),
            pltpu.VMEM((row_blocks, each * BS, BS), jnp.bfloat16),
        ),
        in_specs=[SMEM, SMEM, VMEM],
        out_specs=(SMEM, VMEM),
        compiler_params=PARAMS,
        name="pack_other",
    )(own, table2, blocks2)
    info = pltpu.with_memory_space_constraint(info, pltpu.SMEM)

    held = []
    image, rays = None, None
    for place in range(places):
        if place == 0:
            shot, terms, rays = call(
                functools.partial(first_kernel, place, len(notes), 0),
                1,
                [info, wide, tall] + notes,
                (image_out, terms_out, rays_out),
                [w_scr, x_scr, rays_scr],
                "first",
            )
        else:
            def hop(p, c, t):
                return ((2 * place - 1 - p) % places, c, t) if c else (p, c, t ^ 1)

            image = sent(image, hop)
            terms = call(
                functools.partial(project_kernel, place),
                1,
                [info, image, tall],
                terms_out,
                [],
                "project",
            )
            image = swapped(image)
            terms = passed(terms, 1)
            shot, terms = call(
                functools.partial(first_kernel, place, 0, len(terms)),
                1,
                [info, wide, tall, rays, image] + terms,
                (image_out, terms_out),
                [w_scr, x_scr],
                "first",
            )
        image = swapped(shot)
        terms = passed(terms, 0)
        last = place == places - 1
        outs = call(
            functools.partial(second_kernel, place, last, len(terms)),
            1,
            [info, rays, wide, image, shot] + terms + held,
            final_out if last else (image_out, image_out),
            [w_scr, x_scr],
            "second",
        )
        if last:
            return outs[None]
        image = outs[0]
        held = [outs[1]]


def solution(mesh):
    in_specs = (
        P("subset", "tile", None, None, None),
        P("subset", "tile", None),
        P("subset", "tile", None),
        P(None, None, ("subset", "tile")),
    )
    out_specs = P("subset", None, None, "tile")
    return jax.shard_map(
        per_device, mesh=mesh, in_specs=in_specs, out_specs=out_specs, check_vma=False
    )
```

time: 83.2 us -> 81.2 us (0.976)
  starting transfers between devices: 43.5 us -> 36.7 us
  waiting for transfers between devices: 30.7 us -> 37.1 us
    ppermute x31 -> x43, starting transfers between devices: 43.5 us -> 36.7 us  [sent(): return lax.ppermute(value, ('subset', 'tile'), pairs)]
    ppermute x31 -> x43, waiting for transfers between devices: 30.7 us -> 37.1 us  [sent(): return lax.ppermute(value, ('subset', 'tile'), pairs)]
  transfers between devices with their start and end apart: 31 -> 43, of which waited for: 26 -> 19; matrix products, arithmetic and copies ran while one was open for 0% -> 0% of each run, Pallas kernels for 7% -> 7%
where the time goes in v9:
time: 81.2 us; the launch traced here: 81.1 us
  waiting for transfers between devices  37.1 us (46%)
  starting transfers between devices  36.7 us (45%)
  Pallas kernels  7.03 us (9%)
    ppermute x43, waiting for transfers between devices, sent(): return lax.ppermute(value, ('subset', 'tile'), pairs)  37.1 us
    ppermute x43, starting transfers between devices, sent(): return lax.ppermute(value, ('subset', 'tile'), pairs)  36.7 us
    pallas_call x1, Pallas kernels, per_device(): pl.pallas_call(functools.partial(head_kernel, row_blocks, chunks), out_sh...  3.06 us
    pallas_call x11, Pallas kernels, call(): pl.pallas_call(kernel, out_shape=out_shape, in_specs=[SMEM] * smem + [VME...  2.17 us
  transfers between devices with their start and end apart: 43, of which 19 were waited for; matrix products, arithmetic and copies ran while one was open for 0% of the time, Pallas kernels for 7%

profile of v9, /device:TPU:25, one launch (start us, length us, event | category | flops | bytes accessed | tf_op | source)
XLA Modules:
  0.0 81.1 jit_solution(14059384202686025765)
XLA Ops:
  0.0 0.7 collective-permute-start.1
  0.8 3.1 %head.1 = (f32[5,32,128]{2,1,0:T(8,128)S(1)}, s32[2,80]{1,0:T(2,128)S(1)}, s32[3,80]{1,0:T(4,128)S(4)}, bf16[1,1,80,128,128]{4,3,2,1,0:T(8,128)(2,1)S(1)}) custom-call(s32[3]{0:T(128)S(1)} %pad_add_fusion.pos, s32[1,1,80]{2,1,0:T(1,128)} %rows_in.1, s32[1,1,80]{2,1,0:T(1,128)} %cols_in.1, bf16[1,1,80,128,128]{4,3,2,1,0:T(8,128)(2,1)} %blocks_in.1, ...), custom_call_target="tpu_custom_call" | custom-call | tf_op jit(solution)/shard_map/head/pallas_call | solution.py:295
  3.8 2.2 %collective-permute-start.4 = (f32[5,32,128]{2,1,0:T(8,128)S(1)}, f32[5,32,128]{2,1,0:T(8,128)S(1)}, u32[]{:S(2)}, u32[]{:S(2)}) collective-permute-start(f32[5,32,128]{2,1,0:T(8,128)S(1)} %get-tuple-element.30._.refs_3_), channel_id=1, source_target_pairs={{0,3},{1,2},{2,1},{3,0},{4,7},{5,6},{6,5},{7,4},{8,11},{9,10},{10,... | collective-permute-start | bytes 245768 | tf_op jit(solution)/shard_map/ppermute | solution.py:262
  6.3 0.3 collective-permute-start.2
  6.5 0.8 %collective-permute-start = (s32[2,80]{1,0:T(2,128)S(1)}, s32[2,80]{1,0:T(2,128)S(1)}, u32[]{:S(2)}, u32[]{:S(2)}) collective-permute-start(s32[2,80]{1,0:T(2,128)S(1)} %get-tuple-element.27), channel_id=1, source_target_pairs={{0,4},{1,5},{2,6},{3,7},{4,0},{5,1},{6,2},{7,3},{8,12},{9,13},{10,... | collective-permute-start | bytes 1928 | tf_op jit(solution)/shard_map/ppermute | solution.py:262
  7.4 0.5 pack_own.1.refs_1_.refs_2_
  7.9 0.3 collective-permute-done.table2
  8.2 1.3 %pack_other.1 = (s32[3,80]{1,0:T(4,128)S(4)}, bf16[16,640,128]{2,1,0:T(8,128)(2,1)S(1)}) custom-call(s32[3,80]{1,0:T(4,128)S(4)} %get-tuple-element.26.own, s32[2,80]{1,0:T(2,128)S(1)} %collective-permute-done.table2, bf16[1,1,80,128,128]{4,3,2,1,0:T(8,128)(2,1)S(1)} %collective-permute-done.1.blocks2), custom_call_target="tpu_custom_call" | custom-call | tf_op jit(solution)/shard_map/pack_other/pallas_call | solution.py:335
  9.6 1.2 %collective-permute-done.3.refs_5_ = f32[5,32,128]{2,1,0:T(8,128)S(1)} collective-permute-done((f32[5,32,128]{2,1,0:T(8,128)S(1)}, f32[5,32,128]{2,1,0:T(8,128)S(1)}, u32[]{:S(2)}, u32[]{:S(2)}) %collective-permute-start.3) | collective-permute-done | bytes 81952 | tf_op jit(solution)/shard_map/ppermute | solution.py:262
  10.8 0.8 collective-permute-start.5
  11.6 1.7 %collective-permute-start.8 = (bf16[16,32,128]{2,1,0:T(8,128)(2,1)S(1)}, bf16[16,32,128]{2,1,0:T(8,128)(2,1)S(1)}, u32[]{:S(2)}, u32[]{:S(2)}) collective-permute-start(bf16[16,32,128]{2,1,0:T(8,128)(2,1)S(1)} %get-tuple-element.34), channel_id=1, source_target_pairs={{0,6},{1,7},{2,4},{3,5},{4,0},{5,1},{6,2},{7,3},{8,14},{9,15},{10,... | collective-permute-start | bytes 393224 | tf_op jit(solution)/shard_map/ppermute | solution.py:262
  13.4 1.3 %collective-permute-start.6 = (bf16[16,32,128]{2,1,0:T(8,128)(2,1)S(1)}, bf16[16,32,128]{2,1,0:T(8,128)(2,1)S(1)}, u32[]{:S(2)}, u32[]{:S(2)}) collective-permute-start(bf16[16,32,128]{2,1,0:T(8,128)(2,1)S(1)} %get-tuple-element.34), channel_id=1, source_target_pairs={{0,4},{1,5},{2,6},{3,7},{4,0},{5,1},{6,2},{7,3},{8,12},{9,13},{10,... | collective-permute-start | bytes 393224 | tf_op jit(solution)/shard_map/ppermute | solution.py:262
  14.7 2.2 %collective-permute-done.9.refs_8_ = bf16[16,32,128]{2,1,0:T(8,128)(2,1)S(1)} collective-permute-done((bf16[16,32,128]{2,1,0:T(8,128)(2,1)S(1)}, bf16[16,32,128]{2,1,0:T(8,128)(2,1)S(1)}, u32[]{:S(2)}, u32[]{:S(2)}) %collective-permute-start.9) | collective-permute-done | bytes 131104 | tf_op jit(solution)/shard_map/ppermute | solution.py:262
  17.0 1.3 %collective-permute-done.8.refs_7_ = bf16[16,32,128]{2,1,0:T(8,128)(2,1)S(1)} collective-permute-done((bf16[16,32,128]{2,1,0:T(8,128)(2,1)S(1)}, bf16[16,32,128]{2,1,0:T(8,128)(2,1)S(1)}, u32[]{:S(2)}, u32[]{:S(2)}) %collective-permute-start.8) | collective-permute-done | bytes 131104 | tf_op jit(solution)/shard_map/ppermute | solution.py:262
  18.6 5.1 %collective-permute-done.10.image = bf16[32,32,128]{2,1,0:T(8,128)(2,1)S(1)} collective-permute-done((bf16[32,32,128]{2,1,0:T(8,128)(2,1)S(1)}, bf16[32,32,128]{2,1,0:T(8,128)(2,1)S(1)}, u32[]{:S(2)}, u32[]{:S(2)}) %collective-permute-start.10) | collective-permute-done | bytes 262176 | tf_op jit(solution)/shard_map/ppermute | solution.py:262
  23.8 1.5 %collective-permute-start.15 = (bf16[16,32,128]{2,1,0:T(8,128)(2,1)S(1)}, bf16[16,32,128]{2,1,0:T(8,128)(2,1)S(1)}, u32[]{:S(2)}, u32[]{:S(2)}) collective-permute-start(bf16[16,32,128]{2,1,0:T(8,128)(2,1)S(1)} %project.3), channel_id=1, source_target_pairs={{0,4},{1,5},{2,6},{3,7},{4,3},{5,2},{6,1},{7,0},{8,12},{9,13},{10,... | collective-permute-start | bytes 393224 | tf_op jit(solution)/shard_map/ppermute | solution.py:262
  25.3 1.1 %collective-permute-start.13 = (bf16[16,32,128]{2,1,0:T(8,128)(2,1)S(1)}, bf16[16,32,128]{2,1,0:T(8,128)(2,1)S(1)}, u32[]{:S(2)}, u32[]{:S(2)}) collective-permute-start(bf16[16,32,128]{2,1,0:T(8,128)(2,1)S(1)} %project.3), channel_id=1, source_target_pairs={{0,4},{1,5},{2,6},{3,7},{4,1},{5,0},{6,3},{7,2},{8,12},{9,13},{10,... | collective-permute-start | bytes 393224 | tf_op jit(solution)/shard_map/ppermute | solution.py:262
  26.3 0.9 %collective-permute-done.15.refs_8_ = bf16[16,32,128]{2,1,0:T(8,128)(2,1)S(1)} collective-permute-done((bf16[16,32,128]{2,1,0:T(8,128)(2,1)S(1)}, bf16[16,32,128]{2,1,0:T(8,128)(2,1)S(1)}, u32[]{:S(2)}, u32[]{:S(2)}) %collective-permute-start.15) | collective-permute-done | bytes 131104 | tf_op jit(solution)/shard_map/ppermute | solution.py:262
  27.2 1.4 %collective-permute-done.14.refs_7_ = bf16[16,32,128]{2,1,0:T(8,128)(2,1)S(1)} collective-permute-done((bf16[16,32,128]{2,1,0:T(8,128)(2,1)S(1)}, bf16[16,32,128]{2,1,0:T(8,128)(2,1)S(1)}, u32[]{:S(2)}, u32[]{:S(2)}) %collective-permute-start.14) | collective-permute-done | bytes 131104 | tf_op jit(solution)/shard_map/ppermute | solution.py:262
  28.6 1.9 %collective-permute-start.16 = (bf16[32,32,128]{2,1,0:T(8,128)(2,1)S(1)}, bf16[32,32,128]{2,1,0:T(8,128)(2,1)S(1)}, u32[]{:S(2)}, u32[]{:S(2)}) collective-permute-start(bf16[32,32,128]{2,1,0:T(8,128)(2,1)S(1)} %get-tuple-element.36.refs_4_), channel_id=1, source_target_pairs={{0,4},{1,5},{2,6},{3,7},{4,0},{5,1},{6,2},{7,3},{8,12},{9,13},{10,... | collective-permute-start | bytes 786440 | tf_op jit(solution)/shard_map/ppermute | solution.py:262
  30.6 1.5 %collective-permute-start.19 = (bf16[16,32,128]{2,1,0:T(8,128)(2,1)S(1)}, bf16[16,32,128]{2,1,0:T(8,128)(2,1)S(1)}, u32[]{:S(2)}, u32[]{:S(2)}) collective-permute-start(bf16[16,32,128]{2,1,0:T(8,128)(2,1)S(1)} %get-tuple-element.37), channel_id=1, source_target_pairs={{0,6},{1,7},{2,4},{3,5},{4,0},{5,1},{6,2},{7,3},{8,14},{9,15},{10,... | collective-permute-start | bytes 393224 | tf_op jit(solution)/shard_map/ppermute | solution.py:262
  32.1 1.2 %collective-permute-start.17 = (bf16[16,32,128]{2,1,0:T(8,128)(2,1)S(1)}, bf16[16,32,128]{2,1,0:T(8,128)(2,1)S(1)}, u32[]{:S(2)}, u32[]{:S(2)}) collective-permute-start(bf16[16,32,128]{2,1,0:T(8,128)(2,1)S(1)} %get-tuple-element.37), channel_id=1, source_target_pairs={{0,4},{1,5},{2,6},{3,7},{4,0},{5,1},{6,2},{7,3},{8,12},{9,13},{10,... | collective-permute-start | bytes 393224 | tf_op jit(solution)/shard_map/ppermute | solution.py:262
  33.2 2.6 %collective-permute-done.20.refs_8_ = bf16[16,32,128]{2,1,0:T(8,128)(2,1)S(1)} collective-permute-done((bf16[16,32,128]{2,1,0:T(8,128)(2,1)S(1)}, bf16[16,32,128]{2,1,0:T(8,128)(2,1)S(1)}, u32[]{:S(2)}, u32[]{:S(2)}) %collective-permute-start.20) | collective-permute-done | bytes 131104 | tf_op jit(solution)/shard_map/ppermute | solution.py:262
  35.9 0.9 %collective-permute-done.19.refs_7_ = bf16[16,32,128]{2,1,0:T(8,128)(2,1)S(1)} collective-permute-done((bf16[16,32,128]{2,1,0:T(8,128)(2,1)S(1)}, bf16[16,32,128]{2,1,0:T(8,128)(2,1)S(1)}, u32[]{:S(2)}, u32[]{:S(2)}) %collective-permute-start.19) | collective-permute-done | bytes 131104 | tf_op jit(solution)/shard_map/ppermute | solution.py:262
  36.9 1.8 %collective-permute-start.21 = (bf16[32,32,128]{2,1,0:T(8,128)(2,1)S(1)}, bf16[32,32,128]{2,1,0:T(8,128)(2,1)S(1)}, u32[]{:S(2)}, u32[]{:S(2)}) collective-permute-start(bf16[32,32,128]{2,1,0:T(8,128)(2,1)S(1)} %get-tuple-element.39), channel_id=1, source_target_pairs={{0,1},{1,0},{2,3},{3,2},{4,28},{5,29},{6,30},{7,31},{8,9},{9,8},{1... | collective-permute-start | bytes 786440 | tf_op jit(solution)/shard_map/ppermute | solution.py:262
  38.7 5.4 %collective-permute-done.21.image = bf16[32,32,128]{2,1,0:T(8,128)(2,1)S(1)} collective-permute-done((bf16[32,32,128]{2,1,0:T(8,128)(2,1)S(1)}, bf16[32,32,128]{2,1,0:T(8,128)(2,1)S(1)}, u32[]{:S(2)}, u32[]{:S(2)}) %collective-permute-start.21) | collective-permute-done | bytes 262176 | tf_op jit(solution)/shard_map/ppermute | solution.py:262
  44.1 1.6 %collective-permute-start.26 = (bf16[16,32,128]{2,1,0:T(8,128)(2,1)S(1)}, bf16[16,32,128]{2,1,0:T(8,128)(2,1)S(1)}, u32[]{:S(2)}, u32[]{:S(2)}) collective-permute-start(bf16[16,32,128]{2,1,0:T(8,128)(2,1)S(1)} %project.4), channel_id=1, source_target_pairs={{0,4},{1,5},{2,6},{3,7},{4,3},{5,2},{6,1},{7,0},{8,12},{9,13},{10,... | collective-permute-start | bytes 393224 | tf_op jit(solution)/shard_map/ppermute | solution.py:262
  45.7 1.1 %collective-permute-start.24 = (bf16[16,32,128]{2,1,0:T(8,128)(2,1)S(1)}, bf16[16,32,128]{2,1,0:T(8,128)(2,1)S(1)}, u32[]{:S(2)}, u32[]{:S(2)}) collective-permute-start(bf16[16,32,128]{2,1,0:T(8,128)(2,1)S(1)} %project.4), channel_id=1, source_target_pairs={{0,4},{1,5},{2,6},{3,7},{4,1},{5,0},{6,3},{7,2},{8,12},{9,13},{10,... | collective-permute-start | bytes 393224 | tf_op jit(solution)/shard_map/ppermute | solution.py:262
  46.7 0.9 %collective-permute-done.26.refs_8_ = bf16[16,32,128]{2,1,0:T(8,128)(2,1)S(1)} collective-permute-done((bf16[16,32,128]{2,1,0:T(8,128)(2,1)S(1)}, bf16[16,32,128]{2,1,0:T(8,128)(2,1)S(1)}, u32[]{:S(2)}, u32[]{:S(2)}) %collective-permute-start.26) | collective-permute-done | bytes 131104 | tf_op jit(solution)/shard_map/ppermute | solution.py:262
  47.6 1.4 %collective-permute-done.25.refs_7_ = bf16[16,32,128]{2,1,0:T(8,128)(2,1)S(1)} collective-permute-done((bf16[16,32,128]{2,1,0:T(8,128)(2,1)S(1)}, bf16[16,32,128]{2,1,0:T(8,128)(2,1)S(1)}, u32[]{:S(2)}, u32[]{:S(2)}) %collective-permute-start.25) | collective-permute-done | bytes 131104 | tf_op jit(solution)/shard_map/ppermute | solution.py:262
  49.0 1.9 %collective-permute-start.27 = (bf16[32,32,128]{2,1,0:T(8,128)(2,1)S(1)}, bf16[32,32,128]{2,1,0:T(8,128)(2,1)S(1)}, u32[]{:S(2)}, u32[]{:S(2)}) collective-permute-start(bf16[32,32,128]{2,1,0:T(8,128)(2,1)S(1)} %get-tuple-element.40.refs_4_), channel_id=1, source_target_pairs={{0,4},{1,5},{2,6},{3,7},{4,0},{5,1},{6,2},{7,3},{8,12},{9,13},{10,... | collective-permute-start | bytes 786440 | tf_op jit(solution)/shard_map/ppermute | solution.py:262
  50.9 1.5 %collective-permute-start.30 = (bf16[16,32,128]{2,1,0:T(8,128)(2,1)S(1)}, bf16[16,32,128]{2,1,0:T(8,128)(2,1)S(1)}, u32[]{:S(2)}, u32[]{:S(2)}) collective-permute-start(bf16[16,32,128]{2,1,0:T(8,128)(2,1)S(1)} %get-tuple-element.41), channel_id=1, source_target_pairs={{0,6},{1,7},{2,4},{3,5},{4,0},{5,1},{6,2},{7,3},{8,14},{9,15},{10,... | collective-permute-start | bytes 393224 | tf_op jit(solution)/shard_map/ppermute | solution.py:262
  52.5 1.2 %collective-permute-start.28 = (bf16[16,32,128]{2,1,0:T(8,128)(2,1)S(1)}, bf16[16,32,128]{2,1,0:T(8,128)(2,1)S(1)}, u32[]{:S(2)}, u32[]{:S(2)}) collective-permute-start(bf16[16,32,128]{2,1,0:T(8,128)(2,1)S(1)} %get-tuple-element.41), channel_id=1, source_target_pairs={{0,4},{1,5},{2,6},{3,7},{4,0},{5,1},{6,2},{7,3},{8,12},{9,13},{10,... | collective-permute-start | bytes 393224 | tf_op jit(solution)/shard_map/ppermute | solution.py:262
  53.6 2.6 %collective-permute-done.31.refs_8_ = bf16[16,32,128]{2,1,0:T(8,128)(2,1)S(1)} collective-permute-done((bf16[16,32,128]{2,1,0:T(8,128)(2,1)S(1)}, bf16[16,32,128]{2,1,0:T(8,128)(2,1)S(1)}, u32[]{:S(2)}, u32[]{:S(2)}) %collective-permute-start.31) | collective-permute-done | bytes 131104 | tf_op jit(solution)/shard_map/ppermute | solution.py:262
  56.3 0.9 %collective-permute-done.30.refs_7_ = bf16[16,32,128]{2,1,0:T(8,128)(2,1)S(1)} collective-permute-done((bf16[16,32,128]{2,1,0:T(8,128)(2,1)S(1)}, bf16[16,32,128]{2,1,0:T(8,128)(2,1)S(1)}, u32[]{:S(2)}, u32[]{:S(2)}) %collective-permute-start.30) | collective-permute-done | bytes 131104 | tf_op jit(solution)/shard_map/ppermute | solution.py:262
  57.5 4.1 %collective-permute-start.32 = (bf16[32,32,128]{2,1,0:T(8,128)(2,1)S(1)}, bf16[32,32,128]{2,1,0:T(8,128)(2,1)S(1)}, u32[]{:S(2)}, u32[]{:S(2)}) collective-permute-start(bf16[32,32,128]{2,1,0:T(8,128)(2,1)S(1)} %get-tuple-element.43), channel_id=1, source_target_pairs={{0,1},{1,0},{2,3},{3,2},{4,12},{5,13},{6,14},{7,15},{8,9},{9,8},{1... | collective-permute-start | bytes 786440 | tf_op jit(solution)/shard_map/ppermute | solution.py:262
  61.6 3.8 %collective-permute-done.32.image = bf16[32,32,128]{2,1,0:T(8,128)(2,1)S(1)} collective-permute-done((bf16[32,32,128]{2,1,0:T(8,128)(2,1)S(1)}, bf16[32,32,128]{2,1,0:T(8,128)(2,1)S(1)}, u32[]{:S(2)}, u32[]{:S(2)}) %collective-permute-start.32) | collective-permute-done | bytes 262176 | tf_op jit(solution)/shard_map/ppermute | solution.py:262
  65.4 0.5 project.5
  65.9 1.0 %collective-permute-start.37 = (bf16[16,32,128]{2,1,0:T(8,128)(2,1)S(1)}, bf16[16,32,128]{2,1,0:T(8,128)(2,1)S(1)}, u32[]{:S(2)}, u32[]{:S(2)}) collective-permute-start(bf16[16,32,128]{2,1,0:T(8,128)(2,1)S(1)} %project.5), channel_id=1, source_target_pairs={{0,4},{1,5},{2,6},{3,7},{4,3},{5,2},{6,1},{7,0},{8,12},{9,13},{10,... | collective-permute-start | bytes 393224 | tf_op jit(solution)/shard_map/ppermute | solution.py:262
  67.0 1.0 %collective-permute-start.35 = (bf16[16,32,128]{2,1,0:T(8,128)(2,1)S(1)}, bf16[16,32,128]{2,1,0:T(8,128)(2,1)S(1)}, u32[]{:S(2)}, u32[]{:S(2)}) collective-permute-start(bf16[16,32,128]{2,1,0:T(8,128)(2,1)S(1)} %project.5), channel_id=1, source_target_pairs={{0,4},{1,5},{2,6},{3,7},{4,1},{5,0},{6,3},{7,2},{8,12},{9,13},{10,... | collective-permute-start | bytes 393224 | tf_op jit(solution)/shard_map/ppermute | solution.py:262
  67.9 1.0 %collective-permute-done.37.refs_8_ = bf16[16,32,128]{2,1,0:T(8,128)(2,1)S(1)} collective-permute-done((bf16[16,32,128]{2,1,0:T(8,128)(2,1)S(1)}, bf16[16,32,128]{2,1,0:T(8,128)(2,1)S(1)}, u32[]{:S(2)}, u32[]{:S(2)}) %collective-permute-start.37) | collective-permute-done | bytes 131104 | tf_op jit(solution)/shard_map/ppermute | solution.py:262
  68.9 1.4 %collective-permute-done.36.refs_7_ = bf16[16,32,128]{2,1,0:T(8,128)(2,1)S(1)} collective-permute-done((bf16[16,32,128]{2,1,0:T(8,128)(2,1)S(1)}, bf16[16,32,128]{2,1,0:T(8,128)(2,1)S(1)}, u32[]{:S(2)}, u32[]{:S(2)}) %collective-permute-start.36) | collective-permute-done | bytes 131104 | tf_op jit(solution)/shard_map/ppermute | solution.py:262
  70.3 3.2 %collective-permute-start.38 = (bf16[32,32,128]{2,1,0:T(8,128)(2,1)S(1)}, bf16[32,32,128]{2,1,0:T(8,128)(2,1)S(1)}, u32[]{:S(2)}, u32[]{:S(2)}) collective-permute-start(bf16[32,32,128]{2,1,0:T(8,128)(2,1)S(1)} %get-tuple-element.44.refs_4_), channel_id=1, source_target_pairs={{0,4},{1,5},{2,6},{3,7},{4,0},{5,1},{6,2},{7,3},{8,12},{9,13},{10,... | collective-permute-start | bytes 786440 | tf_op jit(solution)/shard_map/ppermute | solution.py:262
  73.6 1.5 %collective-permute-start.41 = (bf16[16,32,128]{2,1,0:T(8,128)(2,1)S(1)}, bf16[16,32,128]{2,1,0:T(8,128)(2,1)S(1)}, u32[]{:S(2)}, u32[]{:S(2)}) collective-permute-start(bf16[16,32,128]{2,1,0:T(8,128)(2,1)S(1)} %get-tuple-element.45), channel_id=1, source_target_pairs={{0,6},{1,7},{2,4},{3,5},{4,0},{5,1},{6,2},{7,3},{8,14},{9,15},{10,... | collective-permute-start | bytes 393224 | tf_op jit(solution)/shard_map/ppermute | solution.py:262
  75.1 1.0 %collective-permute-start.39 = (bf16[16,32,128]{2,1,0:T(8,128)(2,1)S(1)}, bf16[16,32,128]{2,1,0:T(8,128)(2,1)S(1)}, u32[]{:S(2)}, u32[]{:S(2)}) collective-permute-start(bf16[16,32,128]{2,1,0:T(8,128)(2,1)S(1)} %get-tuple-element.45), channel_id=1, source_target_pairs={{0,4},{1,5},{2,6},{3,7},{4,0},{5,1},{6,2},{7,3},{8,12},{9,13},{10,... | collective-permute-start | bytes 393224 | tf_op jit(solution)/shard_map/ppermute | solution.py:262
  76.1 2.8 %collective-permute-done.42.refs_8_ = bf16[16,32,128]{2,1,0:T(8,128)(2,1)S(1)} collective-permute-done((bf16[16,32,128]{2,1,0:T(8,128)(2,1)S(1)}, bf16[16,32,128]{2,1,0:T(8,128)(2,1)S(1)}, u32[]{:S(2)}, u32[]{:S(2)}) %collective-permute-start.42) | collective-permute-done | bytes 131104 | tf_op jit(solution)/shard_map/ppermute | solution.py:262
  78.9 0.7 collective-permute-done.41.refs_7_
  79.7 1.4 %second.7 = bf16[4,8,4096]{2,1,0:T(8,128)(2,1)} custom-call(s32[3,80]{1,0:T(4,128)S(4)} %get-tuple-element.28.refs_0_.info, f32[17,32,128]{2,1,0:T(8,128)S(1)} %get-tuple-element.32.refs_1_.refs_3_, bf16[16,128,640]{2,1,0:T(8,128)(2,1)S(1)} %pack_own.1.refs_1_.refs_2_, bf16[32,32,128]{2,1,0:T(8,128)(2,1)S(1)} %collective-permute-done.38.refs_3_, ...), custom_call_target="tpu_custom_call" | custom-call | tf_op jit(solution)/shard_map/second/pallas_call | solution.py:283
  (53 shorter events, 1.6 us)
Async XLA Ops:
  0.0 8.2 %collective-permute-start.1 = (bf16[1,1,80,128,128]{4,3,2,1,0:T(8,128)(2,1)}, bf16[1,1,80,128,128]{4,3,2,1,0:T(8,128)(2,1)S(1)}, u32[]{:S(2)}, u32[]{:S(2)}) collective-permute-start(bf16[1,1,80,128,128]{4,3,2,1,0:T(8,128)(2,1)} %blocks_in.1), channel_id=1, source_target_pairs={{0,4},{1,5},{2,6},{3,7},{4,0},{5,1},{6,2},{7,3},{8,12},{9,13},{10,... | collective-permute-start | bytes 7864328 | tf_op jit(solution)/shard_map/ppermute | solution.py:262
  3.8 5.7 %collective-permute-start.4 = (f32[5,32,128]{2,1,0:T(8,128)S(1)}, f32[5,32,128]{2,1,0:T(8,128)S(1)}, u32[]{:S(2)}, u32[]{:S(2)}) collective-permute-start(f32[5,32,128]{2,1,0:T(8,128)S(1)} %get-tuple-element.30._.refs_3_), channel_id=1, source_target_pairs={{0,3},{1,2},{2,1},{3,0},{4,7},{5,6},{6,5},{7,4},{8,11},{9,10},{10,... | collective-permute-start | bytes 245768 | tf_op jit(solution)/shard_map/ppermute | solution.py:262
  6.1 4.7 %collective-permute-start.3 = (f32[5,32,128]{2,1,0:T(8,128)S(1)}, f32[5,32,128]{2,1,0:T(8,128)S(1)}, u32[]{:S(2)}, u32[]{:S(2)}) collective-permute-start(f32[5,32,128]{2,1,0:T(8,128)S(1)} %get-tuple-element.30._.refs_3_), channel_id=1, source_target_pairs={{0,2},{1,3},{2,0},{3,1},{4,6},{5,7},{6,4},{7,5},{8,10},{9,11},{10,... | collective-permute-start | bytes 245768 | tf_op jit(solution)/shard_map/ppermute | solution.py:262
  6.3 4.5 %collective-permute-start.2 = (f32[5,32,128]{2,1,0:T(8,128)S(1)}, f32[5,32,128]{2,1,0:T(8,128)S(1)}, u32[]{:S(2)}, u32[]{:S(2)}) collective-permute-start(f32[5,32,128]{2,1,0:T(8,128)S(1)} %get-tuple-element.30._.refs_3_), channel_id=1, source_target_pairs={{0,1},{1,0},{2,3},{3,2},{4,5},{5,4},{6,7},{7,6},{8,9},{9,8},{10,11... | collective-permute-start | bytes 245768 | tf_op jit(solution)/shard_map/ppermute | solution.py:262
  6.5 1.7 %collective-permute-start = (s32[2,80]{1,0:T(2,128)S(1)}, s32[2,80]{1,0:T(2,128)S(1)}, u32[]{:S(2)}, u32[]{:S(2)}) collective-permute-start(s32[2,80]{1,0:T(2,128)S(1)} %get-tuple-element.27), channel_id=1, source_target_pairs={{0,4},{1,5},{2,6},{3,7},{4,0},{5,1},{6,2},{7,3},{8,12},{9,13},{10,... | collective-permute-start | bytes 1928 | tf_op jit(solution)/shard_map/ppermute | solution.py:262
  10.8 7.5 %collective-permute-start.5 = (bf16[32,32,128]{2,1,0:T(8,128)(2,1)S(1)}, bf16[32,32,128]{2,1,0:T(8,128)(2,1)S(1)}, u32[]{:S(2)}, u32[]{:S(2)}) collective-permute-start(bf16[32,32,128]{2,1,0:T(8,128)(2,1)S(1)} %get-tuple-element.33.refs_4_), channel_id=1, source_target_pairs={{0,4},{1,5},{2,6},{3,7},{4,0},{5,1},{6,2},{7,3},{8,12},{9,13},{10,... | collective-permute-start | bytes 786440 | tf_op jit(solution)/shard_map/ppermute | solution.py:262
  11.6 5.4 %collective-permute-start.9 = (bf16[16,32,128]{2,1,0:T(8,128)(2,1)S(1)}, bf16[16,32,128]{2,1,0:T(8,128)(2,1)S(1)}, u32[]{:S(2)}, u32[]{:S(2)}) collective-permute-start(bf16[16,32,128]{2,1,0:T(8,128)(2,1)S(1)} %get-tuple-element.34), channel_id=1, source_target_pairs={{0,7},{1,6},{2,5},{3,4},{4,0},{5,1},{6,2},{7,3},{8,15},{9,14},{10,... | collective-permute-start | bytes 393224 | tf_op jit(solution)/shard_map/ppermute | solution.py:262
  11.6 6.6 %collective-permute-start.8 = (bf16[16,32,128]{2,1,0:T(8,128)(2,1)S(1)}, bf16[16,32,128]{2,1,0:T(8,128)(2,1)S(1)}, u32[]{:S(2)}, u32[]{:S(2)}) collective-permute-start(bf16[16,32,128]{2,1,0:T(8,128)(2,1)S(1)} %get-tuple-element.34), channel_id=1, source_target_pairs={{0,6},{1,7},{2,4},{3,5},{4,0},{5,1},{6,2},{7,3},{8,14},{9,15},{10,... | collective-permute-start | bytes 393224 | tf_op jit(solution)/shard_map/ppermute | solution.py:262
  13.4 4.9 %collective-permute-start.7 = (bf16[16,32,128]{2,1,0:T(8,128)(2,1)S(1)}, bf16[16,32,128]{2,1,0:T(8,128)(2,1)S(1)}, u32[]{:S(2)}, u32[]{:S(2)}) collective-permute-start(bf16[16,32,128]{2,1,0:T(8,128)(2,1)S(1)} %get-tuple-element.34), channel_id=1, source_target_pairs={{0,5},{1,4},{2,7},{3,6},{4,0},{5,1},{6,2},{7,3},{8,13},{9,12},{10,... | collective-permute-start | bytes 393224 | tf_op jit(solution)/shard_map/ppermute | solution.py:262
  13.4 4.9 %collective-permute-start.6 = (bf16[16,32,128]{2,1,0:T(8,128)(2,1)S(1)}, bf16[16,32,128]{2,1,0:T(8,128)(2,1)S(1)}, u32[]{:S(2)}, u32[]{:S(2)}) collective-permute-start(bf16[16,32,128]{2,1,0:T(8,128)(2,1)S(1)} %get-tuple-element.34), channel_id=1, source_target_pairs={{0,4},{1,5},{2,6},{3,7},{4,0},{5,1},{6,2},{7,3},{8,12},{9,13},{10,... | collective-permute-start | bytes 393224 | tf_op jit(solution)/shard_map/ppermute | solution.py:262
  18.3 5.3 %collective-permute-start.10 = (bf16[32,32,128]{2,1,0:T(8,128)(2,1)S(1)}, bf16[32,32,128]{2,1,0:T(8,128)(2,1)S(1)}, u32[]{:S(2)}, u32[]{:S(2)}) collective-permute-start(bf16[32,32,128]{2,1,0:T(8,128)(2,1)S(1)} %get-tuple-element.35), channel_id=1, source_target_pairs={{0,1},{1,0},{2,3},{3,2},{4,12},{5,13},{6,14},{7,15},{8,9},{9,8},{1... | collective-permute-start | bytes 786440 | tf_op jit(solution)/shard_map/ppermute | solution.py:262
  23.6 5.0 %collective-permute-start.11 = (bf16[32,32,128]{2,1,0:T(8,128)(2,1)S(1)}, bf16[32,32,128]{2,1,0:T(8,128)(2,1)S(1)}, u32[]{:S(2)}, u32[]{:S(2)}) collective-permute-start(bf16[32,32,128]{2,1,0:T(8,128)(2,1)S(1)} %collective-permute-done.10.image), channel_id=1, source_target_pairs={{0,4},{1,5},{2,6},{3,7},{4,0},{5,1},{6,2},{7,3},{8,12},{9,13},{10,... | collective-permute-start | bytes 786440 | tf_op jit(solution)/shard_map/ppermute | solution.py:262
  23.8 3.5 %collective-permute-start.15 = (bf16[16,32,128]{2,1,0:T(8,128)(2,1)S(1)}, bf16[16,32,128]{2,1,0:T(8,128)(2,1)S(1)}, u32[]{:S(2)}, u32[]{:S(2)}) collective-permute-start(bf16[16,32,128]{2,1,0:T(8,128)(2,1)S(1)} %project.3), channel_id=1, source_target_pairs={{0,4},{1,5},{2,6},{3,7},{4,3},{5,2},{6,1},{7,0},{8,12},{9,13},{10,... | collective-permute-start | bytes 393224 | tf_op jit(solution)/shard_map/ppermute | solution.py:262
  25.3 3.3 %collective-permute-start.14 = (bf16[16,32,128]{2,1,0:T(8,128)(2,1)S(1)}, bf16[16,32,128]{2,1,0:T(8,128)(2,1)S(1)}, u32[]{:S(2)}, u32[]{:S(2)}) collective-permute-start(bf16[16,32,128]{2,1,0:T(8,128)(2,1)S(1)} %project.3), channel_id=1, source_target_pairs={{0,4},{1,5},{2,6},{3,7},{4,2},{5,3},{6,0},{7,1},{8,12},{9,13},{10,... | collective-permute-start | bytes 393224 | tf_op jit(solution)/shard_map/ppermute | solution.py:262
  25.3 3.4 %collective-permute-start.13 = (bf16[16,32,128]{2,1,0:T(8,128)(2,1)S(1)}, bf16[16,32,128]{2,1,0:T(8,128)(2,1)S(1)}, u32[]{:S(2)}, u32[]{:S(2)}) collective-permute-start(bf16[16,32,128]{2,1,0:T(8,128)(2,1)S(1)} %project.3), channel_id=1, source_target_pairs={{0,4},{1,5},{2,6},{3,7},{4,1},{5,0},{6,3},{7,2},{8,12},{9,13},{10,... | collective-permute-start | bytes 393224 | tf_op jit(solution)/shard_map/ppermute | solution.py:262
  26.3 2.3 %collective-permute-start.12 = (bf16[16,32,128]{2,1,0:T(8,128)(2,1)S(1)}, bf16[16,32,128]{2,1,0:T(8,128)(2,1)S(1)}, u32[]{:S(2)}, u32[]{:S(2)}) collective-permute-start(bf16[16,32,128]{2,1,0:T(8,128)(2,1)S(1)} %project.3), channel_id=1, source_target_pairs={{0,4},{1,5},{2,6},{3,7},{4,0},{5,1},{6,2},{7,3},{8,12},{9,13},{10,... | collective-permute-start | bytes 393224 | tf_op jit(solution)/shard_map/ppermute | solution.py:262
  28.6 8.2 %collective-permute-start.16 = (bf16[32,32,128]{2,1,0:T(8,128)(2,1)S(1)}, bf16[32,32,128]{2,1,0:T(8,128)(2,1)S(1)}, u32[]{:S(2)}, u32[]{:S(2)}) collective-permute-start(bf16[32,32,128]{2,1,0:T(8,128)(2,1)S(1)} %get-tuple-element.36.refs_4_), channel_id=1, source_target_pairs={{0,4},{1,5},{2,6},{3,7},{4,0},{5,1},{6,2},{7,3},{8,12},{9,13},{10,... | collective-permute-start | bytes 786440 | tf_op jit(solution)/shard_map/ppermute | solution.py:262
  30.5 5.4 %collective-permute-start.20 = (bf16[16,32,128]{2,1,0:T(8,128)(2,1)S(1)}, bf16[16,32,128]{2,1,0:T(8,128)(2,1)S(1)}, u32[]{:S(2)}, u32[]{:S(2)}) collective-permute-start(bf16[16,32,128]{2,1,0:T(8,128)(2,1)S(1)} %get-tuple-element.37), channel_id=1, source_target_pairs={{0,7},{1,6},{2,5},{3,4},{4,0},{5,1},{6,2},{7,3},{8,15},{9,14},{10,... | collective-permute-start | bytes 393224 | tf_op jit(solution)/shard_map/ppermute | solution.py:262
  30.6 6.3 %collective-permute-start.19 = (bf16[16,32,128]{2,1,0:T(8,128)(2,1)S(1)}, bf16[16,32,128]{2,1,0:T(8,128)(2,1)S(1)}, u32[]{:S(2)}, u32[]{:S(2)}) collective-permute-start(bf16[16,32,128]{2,1,0:T(8,128)(2,1)S(1)} %get-tuple-element.37), channel_id=1, source_target_pairs={{0,6},{1,7},{2,4},{3,5},{4,0},{5,1},{6,2},{7,3},{8,14},{9,15},{10,... | collective-permute-start | bytes 393224 | tf_op jit(solution)/shard_map/ppermute | solution.py:262
  32.1 4.8 %collective-permute-start.18 = (bf16[16,32,128]{2,1,0:T(8,128)(2,1)S(1)}, bf16[16,32,128]{2,1,0:T(8,128)(2,1)S(1)}, u32[]{:S(2)}, u32[]{:S(2)}) collective-permute-start(bf16[16,32,128]{2,1,0:T(8,128)(2,1)S(1)} %get-tuple-element.37), channel_id=1, source_target_pairs={{0,5},{1,4},{2,7},{3,6},{4,0},{5,1},{6,2},{7,3},{8,13},{9,12},{10,... | collective-permute-start | bytes 393224 | tf_op jit(solution)/shard_map/ppermute | solution.py:262
  32.1 4.8 %collective-permute-start.17 = (bf16[16,32,128]{2,1,0:T(8,128)(2,1)S(1)}, bf16[16,32,128]{2,1,0:T(8,128)(2,1)S(1)}, u32[]{:S(2)}, u32[]{:S(2)}) collective-permute-start(bf16[16,32,128]{2,1,0:T(8,128)(2,1)S(1)} %get-tuple-element.37), channel_id=1, source_target_pairs={{0,4},{1,5},{2,6},{3,7},{4,0},{5,1},{6,2},{7,3},{8,12},{9,13},{10,... | collective-permute-start | bytes 393224 | tf_op jit(solution)/shard_map/ppermute | solution.py:262
  36.9 7.2 %collective-permute-start.21 = (bf16[32,32,128]{2,1,0:T(8,128)(2,1)S(1)}, bf16[32,32,128]{2,1,0:T(8,128)(2,1)S(1)}, u32[]{:S(2)}, u32[]{:S(2)}) collective-permute-start(bf16[32,32,128]{2,1,0:T(8,128)(2,1)S(1)} %get-tuple-element.39), channel_id=1, source_target_pairs={{0,1},{1,0},{2,3},{3,2},{4,28},{5,29},{6,30},{7,31},{8,9},{9,8},{1... | collective-permute-start | bytes 786440 | tf_op jit(solution)/shard_map/ppermute | solution.py:262
  44.1 5.0 %collective-permute-start.22 = (bf16[32,32,128]{2,1,0:T(8,128)(2,1)S(1)}, bf16[32,32,128]{2,1,0:T(8,128)(2,1)S(1)}, u32[]{:S(2)}, u32[]{:S(2)}) collective-permute-start(bf16[32,32,128]{2,1,0:T(8,128)(2,1)S(1)} %collective-permute-done.21.image), channel_id=1, source_target_pairs={{0,4},{1,5},{2,6},{3,7},{4,0},{5,1},{6,2},{7,3},{8,12},{9,13},{10,... | collective-permute-start | bytes 786440 | tf_op jit(solution)/shard_map/ppermute | solution.py:262
  44.1 3.5 %collective-permute-start.26 = (bf16[16,32,128]{2,1,0:T(8,128)(2,1)S(1)}, bf16[16,32,128]{2,1,0:T(8,128)(2,1)S(1)}, u32[]{:S(2)}, u32[]{:S(2)}) collective-permute-start(bf16[16,32,128]{2,1,0:T(8,128)(2,1)S(1)} %project.4), channel_id=1, source_target_pairs={{0,4},{1,5},{2,6},{3,7},{4,3},{5,2},{6,1},{7,0},{8,12},{9,13},{10,... | collective-permute-start | bytes 393224 | tf_op jit(solution)/shard_map/ppermute | solution.py:262
  45.6 3.3 %collective-permute-start.25 = (bf16[16,32,128]{2,1,0:T(8,128)(2,1)S(1)}, bf16[16,32,128]{2,1,0:T(8,128)(2,1)S(1)}, u32[]{:S(2)}, u32[]{:S(2)}) collective-permute-start(bf16[16,32,128]{2,1,0:T(8,128)(2,1)S(1)} %project.4), channel_id=1, source_target_pairs={{0,4},{1,5},{2,6},{3,7},{4,2},{5,3},{6,0},{7,1},{8,12},{9,13},{10,... | collective-permute-start | bytes 393224 | tf_op jit(solution)/shard_map/ppermute | solution.py:262
  45.7 3.4 %collective-permute-start.24 = (bf16[16,32,128]{2,1,0:T(8,128)(2,1)S(1)}, bf16[16,32,128]{2,1,0:T(8,128)(2,1)S(1)}, u32[]{:S(2)}, u32[]{:S(2)}) collective-permute-start(bf16[16,32,128]{2,1,0:T(8,128)(2,1)S(1)} %project.4), channel_id=1, source_target_pairs={{0,4},{1,5},{2,6},{3,7},{4,1},{5,0},{6,3},{7,2},{8,12},{9,13},{10,... | collective-permute-start | bytes 393224 | tf_op jit(solution)/shard_map/ppermute | solution.py:262
  46.7 2.3 %collective-permute-start.23 = (bf16[16,32,128]{2,1,0:T(8,128)(2,1)S(1)}, bf16[16,32,128]{2,1,0:T(8,128)(2,1)S(1)}, u32[]{:S(2)}, u32[]{:S(2)}) collective-permute-start(bf16[16,32,128]{2,1,0:T(8,128)(2,1)S(1)} %project.4), channel_id=1, source_target_pairs={{0,4},{1,5},{2,6},{3,7},{4,0},{5,1},{6,2},{7,3},{8,12},{9,13},{10,... | collective-permute-start | bytes 393224 | tf_op jit(solution)/shard_map/ppermute | solution.py:262
  49.0 8.2 %collective-permute-start.27 = (bf16[32,32,128]{2,1,0:T(8,128)(2,1)S(1)}, bf16[32,32,128]{2,1,0:T(8,128)(2,1)S(1)}, u32[]{:S(2)}, u32[]{:S(2)}) collective-permute-start(bf16[32,32,128]{2,1,0:T(8,128)(2,1)S(1)} %get-tuple-element.40.refs_4_), channel_id=1, source_target_pairs={{0,4},{1,5},{2,6},{3,7},{4,0},{5,1},{6,2},{7,3},{8,12},{9,13},{10,... | collective-permute-start | bytes 786440 | tf_op jit(solution)/shard_map/ppermute | solution.py:262
  50.9 5.4 %collective-permute-start.31 = (bf16[16,32,128]{2,1,0:T(8,128)(2,1)S(1)}, bf16[16,32,128]{2,1,0:T(8,128)(2,1)S(1)}, u32[]{:S(2)}, u32[]{:S(2)}) collective-permute-start(bf16[16,32,128]{2,1,0:T(8,128)(2,1)S(1)} %get-tuple-element.41), channel_id=1, source_target_pairs={{0,7},{1,6},{2,5},{3,4},{4,0},{5,1},{6,2},{7,3},{8,15},{9,14},{10,... | collective-permute-start | bytes 393224 | tf_op jit(solution)/shard_map/ppermute | solution.py:262
  50.9 6.2 %collective-permute-start.30 = (bf16[16,32,128]{2,1,0:T(8,128)(2,1)S(1)}, bf16[16,32,128]{2,1,0:T(8,128)(2,1)S(1)}, u32[]{:S(2)}, u32[]{:S(2)}) collective-permute-start(bf16[16,32,128]{2,1,0:T(8,128)(2,1)S(1)} %get-tuple-element.41), channel_id=1, source_target_pairs={{0,6},{1,7},{2,4},{3,5},{4,0},{5,1},{6,2},{7,3},{8,14},{9,15},{10,... | collective-permute-start | bytes 393224 | tf_op jit(solution)/shard_map/ppermute | solution.py:262
  52.5 4.8 %collective-permute-start.29 = (bf16[16,32,128]{2,1,0:T(8,128)(2,1)S(1)}, bf16[16,32,128]{2,1,0:T(8,128)(2,1)S(1)}, u32[]{:S(2)}, u32[]{:S(2)}) collective-permute-start(bf16[16,32,128]{2,1,0:T(8,128)(2,1)S(1)} %get-tuple-element.41), channel_id=1, source_target_pairs={{0,5},{1,4},{2,7},{3,6},{4,0},{5,1},{6,2},{7,3},{8,13},{9,12},{10,... | collective-permute-start | bytes 393224 | tf_op jit(solution)/shard_map/ppermute | solution.py:262
  52.5 4.8 %collective-permute-start.28 = (bf16[16,32,128]{2,1,0:T(8,128)(2,1)S(1)}, bf16[16,32,128]{2,1,0:T(8,128)(2,1)S(1)}, u32[]{:S(2)}, u32[]{:S(2)}) collective-permute-start(bf16[16,32,128]{2,1,0:T(8,128)(2,1)S(1)} %get-tuple-element.41), channel_id=1, source_target_pairs={{0,4},{1,5},{2,6},{3,7},{4,0},{5,1},{6,2},{7,3},{8,12},{9,13},{10,... | collective-permute-start | bytes 393224 | tf_op jit(solution)/shard_map/ppermute | solution.py:262
  57.5 7.9 %collective-permute-start.32 = (bf16[32,32,128]{2,1,0:T(8,128)(2,1)S(1)}, bf16[32,32,128]{2,1,0:T(8,128)(2,1)S(1)}, u32[]{:S(2)}, u32[]{:S(2)}) collective-permute-start(bf16[32,32,128]{2,1,0:T(8,128)(2,1)S(1)} %get-tuple-element.43), channel_id=1, source_target_pairs={{0,1},{1,0},{2,3},{3,2},{4,12},{5,13},{6,14},{7,15},{8,9},{9,8},{1... | collective-permute-start | bytes 786440 | tf_op jit(solution)/shard_map/ppermute | solution.py:262
  65.4 5.0 %collective-permute-start.33 = (bf16[32,32,128]{2,1,0:T(8,128)(2,1)S(1)}, bf16[32,32,128]{2,1,0:T(8,128)(2,1)S(1)}, u32[]{:S(2)}, u32[]{:S(2)}) collective-permute-start(bf16[32,32,128]{2,1,0:T(8,128)(2,1)S(1)} %collective-permute-done.32.image), channel_id=1, source_target_pairs={{0,4},{1,5},{2,6},{3,7},{4,0},{5,1},{6,2},{7,3},{8,12},{9,13},{10,... | collective-permute-start | bytes 786440 | tf_op jit(solution)/shard_map/ppermute | solution.py:262
  65.9 3.0 %collective-permute-start.37 = (bf16[16,32,128]{2,1,0:T(8,128)(2,1)S(1)}, bf16[16,32,128]{2,1,0:T(8,128)(2,1)S(1)}, u32[]{:S(2)}, u32[]{:S(2)}) collective-permute-start(bf16[16,32,128]{2,1,0:T(8,128)(2,1)S(1)} %project.5), channel_id=1, source_target_pairs={{0,4},{1,5},{2,6},{3,7},{4,3},{5,2},{6,1},{7,0},{8,12},{9,13},{10,... | collective-permute-start | bytes 393224 | tf_op jit(solution)/shard_map/ppermute | solution.py:262
  66.9 3.3 %collective-permute-start.36 = (bf16[16,32,128]{2,1,0:T(8,128)(2,1)S(1)}, bf16[16,32,128]{2,1,0:T(8,128)(2,1)S(1)}, u32[]{:S(2)}, u32[]{:S(2)}) collective-permute-start(bf16[16,32,128]{2,1,0:T(8,128)(2,1)S(1)} %project.5), channel_id=1, source_target_pairs={{0,4},{1,5},{2,6},{3,7},{4,2},{5,3},{6,0},{7,1},{8,12},{9,13},{10,... | collective-permute-start | bytes 393224 | tf_op jit(solution)/shard_map/ppermute | solution.py:262
  67.0 3.3 %collective-permute-start.35 = (bf16[16,32,128]{2,1,0:T(8,128)(2,1)S(1)}, bf16[16,32,128]{2,1,0:T(8,128)(2,1)S(1)}, u32[]{:S(2)}, u32[]{:S(2)}) collective-permute-start(bf16[16,32,128]{2,1,0:T(8,128)(2,1)S(1)} %project.5), channel_id=1, source_target_pairs={{0,4},{1,5},{2,6},{3,7},{4,1},{5,0},{6,3},{7,2},{8,12},{9,13},{10,... | collective-permute-start | bytes 393224 | tf_op jit(solution)/shard_map/ppermute | solution.py:262
  67.9 2.4 %collective-permute-start.34 = (bf16[16,32,128]{2,1,0:T(8,128)(2,1)S(1)}, bf16[16,32,128]{2,1,0:T(8,128)(2,1)S(1)}, u32[]{:S(2)}, u32[]{:S(2)}) collective-permute-start(bf16[16,32,128]{2,1,0:T(8,128)(2,1)S(1)} %project.5), channel_id=1, source_target_pairs={{0,4},{1,5},{2,6},{3,7},{4,0},{5,1},{6,2},{7,3},{8,12},{9,13},{10,... | collective-permute-start | bytes 393224 | tf_op jit(solution)/shard_map/ppermute | solution.py:262
  70.3 9.4 %collective-permute-start.38 = (bf16[32,32,128]{2,1,0:T(8,128)(2,1)S(1)}, bf16[32,32,128]{2,1,0:T(8,128)(2,1)S(1)}, u32[]{:S(2)}, u32[]{:S(2)}) collective-permute-start(bf16[32,32,128]{2,1,0:T(8,128)(2,1)S(1)} %get-tuple-element.44.refs_4_), channel_id=1, source_target_pairs={{0,4},{1,5},{2,6},{3,7},{4,0},{5,1},{6,2},{7,3},{8,12},{9,13},{10,... | collective-permute-start | bytes 786440 | tf_op jit(solution)/shard_map/ppermute | solution.py:262
  73.5 5.4 %collective-permute-start.42 = (bf16[16,32,128]{2,1,0:T(8,128)(2,1)S(1)}, bf16[16,32,128]{2,1,0:T(8,128)(2,1)S(1)}, u32[]{:S(2)}, u32[]{:S(2)}) collective-permute-start(bf16[16,32,128]{2,1,0:T(8,128)(2,1)S(1)} %get-tuple-element.45), channel_id=1, source_target_pairs={{0,7},{1,6},{2,5},{3,4},{4,0},{5,1},{6,2},{7,3},{8,15},{9,14},{10,... | collective-permute-start | bytes 393224 | tf_op jit(solution)/shard_map/ppermute | solution.py:262
  73.6 6.1 %collective-permute-start.41 = (bf16[16,32,128]{2,1,0:T(8,128)(2,1)S(1)}, bf16[16,32,128]{2,1,0:T(8,128)(2,1)S(1)}, u32[]{:S(2)}, u32[]{:S(2)}) collective-permute-start(bf16[16,32,128]{2,1,0:T(8,128)(2,1)S(1)} %get-tuple-element.45), channel_id=1, source_target_pairs={{0,6},{1,7},{2,4},{3,5},{4,0},{5,1},{6,2},{7,3},{8,14},{9,15},{10,... | collective-permute-start | bytes 393224 | tf_op jit(solution)/shard_map/ppermute | solution.py:262
  75.1 4.6 %collective-permute-start.40 = (bf16[16,32,128]{2,1,0:T(8,128)(2,1)S(1)}, bf16[16,32,128]{2,1,0:T(8,128)(2,1)S(1)}, u32[]{:S(2)}, u32[]{:S(2)}) collective-permute-start(bf16[16,32,128]{2,1,0:T(8,128)(2,1)S(1)} %get-tuple-element.45), channel_id=1, source_target_pairs={{0,5},{1,4},{2,7},{3,6},{4,0},{5,1},{6,2},{7,3},{8,13},{9,12},{10,... | collective-permute-start | bytes 393224 | tf_op jit(solution)/shard_map/ppermute | solution.py:262
  75.1 4.6 %collective-permute-start.39 = (bf16[16,32,128]{2,1,0:T(8,128)(2,1)S(1)}, bf16[16,32,128]{2,1,0:T(8,128)(2,1)S(1)}, u32[]{:S(2)}, u32[]{:S(2)}) collective-permute-start(bf16[16,32,128]{2,1,0:T(8,128)(2,1)S(1)} %get-tuple-element.45), channel_id=1, source_target_pairs={{0,4},{1,5},{2,6},{3,7},{4,0},{5,1},{6,2},{7,3},{8,12},{9,13},{10,... | collective-permute-start | bytes 393224 | tf_op jit(solution)/shard_map/ppermute | solution.py:262

commit v10 on v9

--- a/solution.py
+++ b/solution.py
@@ -162,23 +162,23 @@
     return jnp.logical_and(info[0, 0] == place, info[0, 1] == core)
 
 
-def project_kernel(place, info, image, tall, terms):
-    @pl.when(on_core(info, place, 1))
+def project_kernel(place, core, info, image, tall, terms):
+    @pl.when(on_core(info, place, core))
     def _():
         project(info, tall, image, terms)
 
 
 def first_kernel(place, n_notes, n_terms, *refs):
     refs = list(refs)
-    info, wide, tall = take(refs, 3)
+    info, wide = take(refs, 2)
     if place == 0:
         notes, terms_in = take(refs, n_notes), []
-        shot, terms, rays, w_scr, x_scr, rays_scr = refs
+        shot, rays, w_scr, x_scr, rays_scr = refs
         gather_rays(info, notes, rays, rays_scr)
     else:
         rays, image_in = take(refs, 2)
         terms_in = take(refs, n_terms)
-        shot, terms, w_scr, x_scr = refs
+        shot, w_scr, x_scr = refs
 
     @pl.when(on_core(info, place, 0))
     def _():
@@ -189,7 +189,6 @@
             x_scr[...] = image_in[...].astype(jnp.float32)
         back_project(info, wide, w_scr, x_scr)
         shot[...] = x_scr[...].astype(jnp.bfloat16)
-        project(info, tall, shot, terms)
 
 
 def second_kernel(place, last, n_terms, *refs):
@@ -273,10 +272,16 @@
     def passed(terms, core):
         if not direct:
             return [swapped(lax.psum(terms, "tile"))]
-        return [
-            sent(terms, lambda p, c, t: (p, 1 - c, t ^ d if c == core else t))
-            for d in range(tiles)
-        ]
+
+        def way(d):
+            def target(p, c, t):
+                if c == core:
+                    return p, 1 - c, t ^ d
+                return (p + 1) % places if d > 1 else p, 1 - c, t
+
+            return target
+
+        return [sent(terms, way(d)) for d in range(tiles)]
 
     def call(kernel, smem, operands, out_shape, scratch, name):
         many = isinstance(out_shape, tuple)
@@ -345,15 +350,25 @@
     )(own, table2, blocks2)
     info = pltpu.with_memory_space_constraint(info, pltpu.SMEM)
 
+    def projected(image, place, core):
+        return call(
+            functools.partial(project_kernel, place, core),
+            1,
+            [info, image, tall],
+            terms_out,
+            [],
+            "project",
+        )
+
     held = []
     image, rays = None, None
     for place in range(places):
         if place == 0:
-            shot, terms, rays = call(
+            shot, rays = call(
                 functools.partial(first_kernel, place, len(notes), 0),
                 1,
-                [info, wide, tall] + notes,
-                (image_out, terms_out, rays_out),
+                [info, wide] + notes,
+                (image_out, rays_out),
                 [w_scr, x_scr, rays_scr],
                 "first",
             )
@@ -362,26 +377,18 @@
                 return ((2 * place - 1 - p) % places, c, t) if c else (p, c, t ^ 1)
 
             image = sent(image, hop)
-            terms = call(
-                functools.partial(project_kernel, place),
-                1,
-                [info, image, tall],
-                terms_out,
-                [],
-                "project",
-            )
+            terms = passed(projected(image, place, 1), 1)
             image = swapped(image)
-            terms = passed(terms, 1)
-            shot, terms = call(
+            shot = call(
                 functools.partial(first_kernel, place, 0, len(terms)),
                 1,
-                [info, wide, tall, rays, image] + terms,
-                (image_out, terms_out),
+                [info, wide, rays, image] + terms,
+                image_out,
                 [w_scr, x_scr],
                 "first",
             )
+        terms = passed(projected(shot, place, 0), 0)
         image = swapped(shot)
-        terms = passed(terms, 0)
         last = place == places - 1
         outs = call(
             functools.partial(second_kernel, place, last, len(terms)),

time: 81.2 us -> 89.3 us (1.100)
  the two profiles are of different devices: /device:TPU:25 before, /device:TPU:0 now
where the time goes in v10:
time: 89.3 us; the launch traced here: 89.1 us
  waiting for transfers between devices  51.1 us (57%)
  starting transfers between devices  30.6 us (34%)
  Pallas kernels  7.21 us (8%)
    ppermute x43, waiting for transfers between devices, sent(): return lax.ppermute(value, ('subset', 'tile'), pairs)  51.1 us
    ppermute x43, starting transfers between devices, sent(): return lax.ppermute(value, ('subset', 'tile'), pairs)  30.6 us
    pallas_call x1, Pallas kernels, per_device(): pl.pallas_call(functools.partial(head_kernel, row_blocks, chunks), out_sh...  3.06 us
    pallas_call x15, Pallas kernels, call(): pl.pallas_call(kernel, out_shape=out_shape, in_specs=[SMEM] * smem + [VME...  2.35 us
  transfers between devices with their start and end apart: 43, of which 22 were waited for; matrix products, arithmetic and copies ran while one was open for 0% of the time, Pallas kernels for 6%

profile of v10, /device:TPU:0, one launch (start us, length us, event | category | flops | bytes accessed | tf_op | source)
XLA Modules:
  0.0 89.1 jit_solution(13474862763003950975)
XLA Ops:
  0.0 0.5 collective-permute-start.1
  0.5 3.1 %head.1 = (f32[5,32,128]{2,1,0:T(8,128)S(1)}, s32[2,80]{1,0:T(2,128)S(1)}, s32[3,80]{1,0:T(4,128)S(4)}, bf16[1,1,80,128,128]{4,3,2,1,0:T(8,128)(2,1)S(1)}) custom-call(s32[3]{0:T(128)S(1)} %pad_add_fusion.pos, s32[1,1,80]{2,1,0:T(1,128)} %rows_in.1, s32[1,1,80]{2,1,0:T(1,128)} %cols_in.1, bf16[1,1,80,128,128]{4,3,2,1,0:T(8,128)(2,1)} %blocks_in.1, ...), custom_call_target="tpu_custom_call" | custom-call | tf_op jit(solution)/shard_map/head/pallas_call | solution.py:300
  3.6 3.5 %collective-permute-start.4 = (f32[5,32,128]{2,1,0:T(8,128)S(1)}, f32[5,32,128]{2,1,0:T(8,128)S(1)}, u32[]{:S(2)}, u32[]{:S(2)}) collective-permute-start(f32[5,32,128]{2,1,0:T(8,128)S(1)} %get-tuple-element.23._.refs_2_), channel_id=1, source_target_pairs={{0,3},{1,2},{2,1},{3,0},{4,7},{5,6},{6,5},{7,4},{8,11},{9,10},{10,... | collective-permute-start | bytes 245768 | tf_op jit(solution)/shard_map/ppermute | solution.py:261
  7.1 0.5 collective-permute-start.3
  7.8 0.5 pack_own.1.refs_1_.refs_2_
  8.2 0.7 collective-permute-done.table2
  8.9 1.3 %pack_other.1 = (s32[3,80]{1,0:T(4,128)S(4)}, bf16[16,640,128]{2,1,0:T(8,128)(2,1)S(1)}) custom-call(s32[3,80]{1,0:T(4,128)S(4)} %get-tuple-element.19.own, s32[2,80]{1,0:T(2,128)S(1)} %collective-permute-done.table2, bf16[1,1,80,128,128]{4,3,2,1,0:T(8,128)(2,1)S(1)} %collective-permute-done.1.blocks2), custom_call_target="tpu_custom_call" | custom-call | tf_op jit(solution)/shard_map/pack_other/pallas_call | solution.py:340
  10.3 1.7 %collective-permute-done.3.refs_4_ = f32[5,32,128]{2,1,0:T(8,128)S(1)} collective-permute-done((f32[5,32,128]{2,1,0:T(8,128)S(1)}, f32[5,32,128]{2,1,0:T(8,128)S(1)}, u32[]{:S(2)}, u32[]{:S(2)}) %collective-permute-start.3) | collective-permute-done | bytes 81952 | tf_op jit(solution)/shard_map/ppermute | solution.py:261
  12.2 0.7 first.4
  13.0 0.6 project.7
  13.6 1.1 %collective-permute-start.9 = (bf16[16,32,128]{2,1,0:T(8,128)(2,1)S(1)}, bf16[16,32,128]{2,1,0:T(8,128)(2,1)S(1)}, u32[]{:S(2)}, u32[]{:S(2)}) collective-permute-start(bf16[16,32,128]{2,1,0:T(8,128)(2,1)S(1)} %project.7), channel_id=1, source_target_pairs={{0,7},{1,6},{2,5},{3,4},{4,8},{5,9},{6,10},{7,11},{8,15},{9,14},{1... | collective-permute-start | bytes 393224 | tf_op jit(solution)/shard_map/ppermute | solution.py:261
  14.7 0.5 collective-permute-start.8
  15.2 1.5 %collective-permute-start.7 = (bf16[16,32,128]{2,1,0:T(8,128)(2,1)S(1)}, bf16[16,32,128]{2,1,0:T(8,128)(2,1)S(1)}, u32[]{:S(2)}, u32[]{:S(2)}) collective-permute-start(bf16[16,32,128]{2,1,0:T(8,128)(2,1)S(1)} %project.7), channel_id=1, source_target_pairs={{0,5},{1,4},{2,7},{3,6},{4,0},{5,1},{6,2},{7,3},{8,13},{9,12},{10,... | collective-permute-start | bytes 393224 | tf_op jit(solution)/shard_map/ppermute | solution.py:261
  16.7 3.1 %collective-permute-done.9.refs_8_ = bf16[16,32,128]{2,1,0:T(8,128)(2,1)S(1)} collective-permute-done((bf16[16,32,128]{2,1,0:T(8,128)(2,1)S(1)}, bf16[16,32,128]{2,1,0:T(8,128)(2,1)S(1)}, u32[]{:S(2)}, u32[]{:S(2)}) %collective-permute-start.9) | collective-permute-done | bytes 131104 | tf_op jit(solution)/shard_map/ppermute | solution.py:261
  19.8 1.4 %collective-permute-done.8.refs_7_ = bf16[16,32,128]{2,1,0:T(8,128)(2,1)S(1)} collective-permute-done((bf16[16,32,128]{2,1,0:T(8,128)(2,1)S(1)}, bf16[16,32,128]{2,1,0:T(8,128)(2,1)S(1)}, u32[]{:S(2)}, u32[]{:S(2)}) %collective-permute-start.8) | collective-permute-done | bytes 131104 | tf_op jit(solution)/shard_map/ppermute | solution.py:261
  21.3 1.6 %collective-permute-start.10 = (bf16[32,32,128]{2,1,0:T(8,128)(2,1)S(1)}, bf16[32,32,128]{2,1,0:T(8,128)(2,1)S(1)}, u32[]{:S(2)}, u32[]{:S(2)}) collective-permute-start(bf16[32,32,128]{2,1,0:T(8,128)(2,1)S(1)} %get-tuple-element.27), channel_id=1, source_target_pairs={{0,1},{1,0},{2,3},{3,2},{4,12},{5,13},{6,14},{7,15},{8,9},{9,8},{1... | collective-permute-start | bytes 786440 | tf_op jit(solution)/shard_map/ppermute | solution.py:261
  22.9 4.8 %collective-permute-done.10.image = bf16[32,32,128]{2,1,0:T(8,128)(2,1)S(1)} collective-permute-done((bf16[32,32,128]{2,1,0:T(8,128)(2,1)S(1)}, bf16[32,32,128]{2,1,0:T(8,128)(2,1)S(1)}, u32[]{:S(2)}, u32[]{:S(2)}) %collective-permute-start.10) | collective-permute-done | bytes 262176 | tf_op jit(solution)/shard_map/ppermute | solution.py:261
  27.9 0.5 collective-permute-start.14
  28.4 1.0 %collective-permute-start.13 = (bf16[16,32,128]{2,1,0:T(8,128)(2,1)S(1)}, bf16[16,32,128]{2,1,0:T(8,128)(2,1)S(1)}, u32[]{:S(2)}, u32[]{:S(2)}) collective-permute-start(bf16[16,32,128]{2,1,0:T(8,128)(2,1)S(1)} %project.8), channel_id=1, source_target_pairs={{0,4},{1,5},{2,6},{3,7},{4,1},{5,0},{6,3},{7,2},{8,12},{9,13},{10,... | collective-permute-start | bytes 393224 | tf_op jit(solution)/shard_map/ppermute | solution.py:261
  29.7 3.4 %collective-permute-done.15.refs_7_ = bf16[16,32,128]{2,1,0:T(8,128)(2,1)S(1)} collective-permute-done((bf16[16,32,128]{2,1,0:T(8,128)(2,1)S(1)}, bf16[16,32,128]{2,1,0:T(8,128)(2,1)S(1)}, u32[]{:S(2)}, u32[]{:S(2)}) %collective-permute-start.15) | collective-permute-done | bytes 131104 | tf_op jit(solution)/shard_map/ppermute | solution.py:261
  33.1 1.3 %collective-permute-done.14.refs_6_ = bf16[16,32,128]{2,1,0:T(8,128)(2,1)S(1)} collective-permute-done((bf16[16,32,128]{2,1,0:T(8,128)(2,1)S(1)}, bf16[16,32,128]{2,1,0:T(8,128)(2,1)S(1)}, u32[]{:S(2)}, u32[]{:S(2)}) %collective-permute-start.14) | collective-permute-done | bytes 131104 | tf_op jit(solution)/shard_map/ppermute | solution.py:261
  34.5 1.4 %collective-permute-start.16 = (bf16[32,32,128]{2,1,0:T(8,128)(2,1)S(1)}, bf16[32,32,128]{2,1,0:T(8,128)(2,1)S(1)}, u32[]{:S(2)}, u32[]{:S(2)}) collective-permute-start(bf16[32,32,128]{2,1,0:T(8,128)(2,1)S(1)} %first.5.image.refs_4_), channel_id=1, source_target_pairs={{0,4},{1,5},{2,6},{3,7},{4,0},{5,1},{6,2},{7,3},{8,12},{9,13},{10,... | collective-permute-start | bytes 786440 | tf_op jit(solution)/shard_map/ppermute | solution.py:261
  35.9 1.3 %collective-permute-start.20 = (bf16[16,32,128]{2,1,0:T(8,128)(2,1)S(1)}, bf16[16,32,128]{2,1,0:T(8,128)(2,1)S(1)}, u32[]{:S(2)}, u32[]{:S(2)}) collective-permute-start(bf16[16,32,128]{2,1,0:T(8,128)(2,1)S(1)} %project.9), channel_id=1, source_target_pairs={{0,7},{1,6},{2,5},{3,4},{4,8},{5,9},{6,10},{7,11},{8,15},{9,14},{1... | collective-permute-start | bytes 393224 | tf_op jit(solution)/shard_map/ppermute | solution.py:261
  37.7 4.4 %collective-permute-done.20.refs_8_ = bf16[16,32,128]{2,1,0:T(8,128)(2,1)S(1)} collective-permute-done((bf16[16,32,128]{2,1,0:T(8,128)(2,1)S(1)}, bf16[16,32,128]{2,1,0:T(8,128)(2,1)S(1)}, u32[]{:S(2)}, u32[]{:S(2)}) %collective-permute-start.20) | collective-permute-done | bytes 131104 | tf_op jit(solution)/shard_map/ppermute | solution.py:261
  42.1 1.4 %collective-permute-done.19.refs_7_ = bf16[16,32,128]{2,1,0:T(8,128)(2,1)S(1)} collective-permute-done((bf16[16,32,128]{2,1,0:T(8,128)(2,1)S(1)}, bf16[16,32,128]{2,1,0:T(8,128)(2,1)S(1)}, u32[]{:S(2)}, u32[]{:S(2)}) %collective-permute-start.19) | collective-permute-done | bytes 131104 | tf_op jit(solution)/shard_map/ppermute | solution.py:261
  43.6 1.6 %collective-permute-start.21 = (bf16[32,32,128]{2,1,0:T(8,128)(2,1)S(1)}, bf16[32,32,128]{2,1,0:T(8,128)(2,1)S(1)}, u32[]{:S(2)}, u32[]{:S(2)}) collective-permute-start(bf16[32,32,128]{2,1,0:T(8,128)(2,1)S(1)} %get-tuple-element.29), channel_id=1, source_target_pairs={{0,1},{1,0},{2,3},{3,2},{4,28},{5,29},{6,30},{7,31},{8,9},{9,8},{1... | collective-permute-start | bytes 786440 | tf_op jit(solution)/shard_map/ppermute | solution.py:261
  45.2 4.8 %collective-permute-done.21.image = bf16[32,32,128]{2,1,0:T(8,128)(2,1)S(1)} collective-permute-done((bf16[32,32,128]{2,1,0:T(8,128)(2,1)S(1)}, bf16[32,32,128]{2,1,0:T(8,128)(2,1)S(1)}, u32[]{:S(2)}, u32[]{:S(2)}) %collective-permute-start.21) | collective-permute-done | bytes 262176 | tf_op jit(solution)/shard_map/ppermute | solution.py:261
  50.5 1.6 %collective-permute-start.25 = (bf16[16,32,128]{2,1,0:T(8,128)(2,1)S(1)}, bf16[16,32,128]{2,1,0:T(8,128)(2,1)S(1)}, u32[]{:S(2)}, u32[]{:S(2)}) collective-permute-start(bf16[16,32,128]{2,1,0:T(8,128)(2,1)S(1)} %project.10), channel_id=1, source_target_pairs={{0,12},{1,13},{2,14},{3,15},{4,2},{5,3},{6,0},{7,1},{8,20},{9,21},... | collective-permute-start | bytes 393224 | tf_op jit(solution)/shard_map/ppermute | solution.py:261
  52.1 1.5 %collective-permute-start.23 = (bf16[16,32,128]{2,1,0:T(8,128)(2,1)S(1)}, bf16[16,32,128]{2,1,0:T(8,128)(2,1)S(1)}, u32[]{:S(2)}, u32[]{:S(2)}) collective-permute-start(bf16[16,32,128]{2,1,0:T(8,128)(2,1)S(1)} %project.10), channel_id=1, source_target_pairs={{0,4},{1,5},{2,6},{3,7},{4,0},{5,1},{6,2},{7,3},{8,12},{9,13},{10,... | collective-permute-start | bytes 393224 | tf_op jit(solution)/shard_map/ppermute | solution.py:261
  53.6 2.1 %collective-permute-done.26.refs_7_ = bf16[16,32,128]{2,1,0:T(8,128)(2,1)S(1)} collective-permute-done((bf16[16,32,128]{2,1,0:T(8,128)(2,1)S(1)}, bf16[16,32,128]{2,1,0:T(8,128)(2,1)S(1)}, u32[]{:S(2)}, u32[]{:S(2)}) %collective-permute-start.26) | collective-permute-done | bytes 131104 | tf_op jit(solution)/shard_map/ppermute | solution.py:261
  55.7 1.1 %collective-permute-done.25.refs_6_ = bf16[16,32,128]{2,1,0:T(8,128)(2,1)S(1)} collective-permute-done((bf16[16,32,128]{2,1,0:T(8,128)(2,1)S(1)}, bf16[16,32,128]{2,1,0:T(8,128)(2,1)S(1)}, u32[]{:S(2)}, u32[]{:S(2)}) %collective-permute-start.25) | collective-permute-done | bytes 131104 | tf_op jit(solution)/shard_map/ppermute | solution.py:261
  56.8 1.4 %collective-permute-start.27 = (bf16[32,32,128]{2,1,0:T(8,128)(2,1)S(1)}, bf16[32,32,128]{2,1,0:T(8,128)(2,1)S(1)}, u32[]{:S(2)}, u32[]{:S(2)}) collective-permute-start(bf16[32,32,128]{2,1,0:T(8,128)(2,1)S(1)} %first.6.image.refs_4_), channel_id=1, source_target_pairs={{0,4},{1,5},{2,6},{3,7},{4,0},{5,1},{6,2},{7,3},{8,12},{9,13},{10,... | collective-permute-start | bytes 786440 | tf_op jit(solution)/shard_map/ppermute | solution.py:261
  58.2 1.3 %collective-permute-start.31 = (bf16[16,32,128]{2,1,0:T(8,128)(2,1)S(1)}, bf16[16,32,128]{2,1,0:T(8,128)(2,1)S(1)}, u32[]{:S(2)}, u32[]{:S(2)}) collective-permute-start(bf16[16,32,128]{2,1,0:T(8,128)(2,1)S(1)} %project.11), channel_id=1, source_target_pairs={{0,7},{1,6},{2,5},{3,4},{4,8},{5,9},{6,10},{7,11},{8,15},{9,14},{1... | collective-permute-start | bytes 393224 | tf_op jit(solution)/shard_map/ppermute | solution.py:261
  59.5 1.5 %collective-permute-start.29 = (bf16[16,32,128]{2,1,0:T(8,128)(2,1)S(1)}, bf16[16,32,128]{2,1,0:T(8,128)(2,1)S(1)}, u32[]{:S(2)}, u32[]{:S(2)}) collective-permute-start(bf16[16,32,128]{2,1,0:T(8,128)(2,1)S(1)} %project.11), channel_id=1, source_target_pairs={{0,5},{1,4},{2,7},{3,6},{4,0},{5,1},{6,2},{7,3},{8,13},{9,12},{10,... | collective-permute-start | bytes 393224 | tf_op jit(solution)/shard_map/ppermute | solution.py:261
  61.0 3.4 %collective-permute-done.31.refs_8_ = bf16[16,32,128]{2,1,0:T(8,128)(2,1)S(1)} collective-permute-done((bf16[16,32,128]{2,1,0:T(8,128)(2,1)S(1)}, bf16[16,32,128]{2,1,0:T(8,128)(2,1)S(1)}, u32[]{:S(2)}, u32[]{:S(2)}) %collective-permute-start.31) | collective-permute-done | bytes 131104 | tf_op jit(solution)/shard_map/ppermute | solution.py:261
  64.4 1.4 %collective-permute-done.30.refs_7_ = bf16[16,32,128]{2,1,0:T(8,128)(2,1)S(1)} collective-permute-done((bf16[16,32,128]{2,1,0:T(8,128)(2,1)S(1)}, bf16[16,32,128]{2,1,0:T(8,128)(2,1)S(1)}, u32[]{:S(2)}, u32[]{:S(2)}) %collective-permute-start.30) | collective-permute-done | bytes 131104 | tf_op jit(solution)/shard_map/ppermute | solution.py:261
  66.1 1.6 %collective-permute-start.32 = (bf16[32,32,128]{2,1,0:T(8,128)(2,1)S(1)}, bf16[32,32,128]{2,1,0:T(8,128)(2,1)S(1)}, u32[]{:S(2)}, u32[]{:S(2)}) collective-permute-start(bf16[32,32,128]{2,1,0:T(8,128)(2,1)S(1)} %get-tuple-element.31), channel_id=1, source_target_pairs={{0,1},{1,0},{2,3},{3,2},{4,12},{5,13},{6,14},{7,15},{8,9},{9,8},{1... | collective-permute-start | bytes 786440 | tf_op jit(solution)/shard_map/ppermute | solution.py:261
  67.7 4.8 %collective-permute-done.32.image = bf16[32,32,128]{2,1,0:T(8,128)(2,1)S(1)} collective-permute-done((bf16[32,32,128]{2,1,0:T(8,128)(2,1)S(1)}, bf16[32,32,128]{2,1,0:T(8,128)(2,1)S(1)}, u32[]{:S(2)}, u32[]{:S(2)}) %collective-permute-start.32) | collective-permute-done | bytes 262176 | tf_op jit(solution)/shard_map/ppermute | solution.py:261
  72.5 0.6 collective-permute-start.36
  73.1 1.1 %collective-permute-start.35 = (bf16[16,32,128]{2,1,0:T(8,128)(2,1)S(1)}, bf16[16,32,128]{2,1,0:T(8,128)(2,1)S(1)}, u32[]{:S(2)}, u32[]{:S(2)}) collective-permute-start(bf16[16,32,128]{2,1,0:T(8,128)(2,1)S(1)} %project.12), channel_id=1, source_target_pairs={{0,4},{1,5},{2,6},{3,7},{4,1},{5,0},{6,3},{7,2},{8,12},{9,13},{10,... | collective-permute-start | bytes 393224 | tf_op jit(solution)/shard_map/ppermute | solution.py:261
  74.4 3.6 %collective-permute-done.37.refs_7_ = bf16[16,32,128]{2,1,0:T(8,128)(2,1)S(1)} collective-permute-done((bf16[16,32,128]{2,1,0:T(8,128)(2,1)S(1)}, bf16[16,32,128]{2,1,0:T(8,128)(2,1)S(1)}, u32[]{:S(2)}, u32[]{:S(2)}) %collective-permute-start.37) | collective-permute-done | bytes 131104 | tf_op jit(solution)/shard_map/ppermute | solution.py:261
  77.9 1.3 %collective-permute-done.36.refs_6_ = bf16[16,32,128]{2,1,0:T(8,128)(2,1)S(1)} collective-permute-done((bf16[16,32,128]{2,1,0:T(8,128)(2,1)S(1)}, bf16[16,32,128]{2,1,0:T(8,128)(2,1)S(1)}, u32[]{:S(2)}, u32[]{:S(2)}) %collective-permute-start.36) | collective-permute-done | bytes 131104 | tf_op jit(solution)/shard_map/ppermute | solution.py:261
  79.3 1.4 %collective-permute-start.38 = (bf16[32,32,128]{2,1,0:T(8,128)(2,1)S(1)}, bf16[32,32,128]{2,1,0:T(8,128)(2,1)S(1)}, u32[]{:S(2)}, u32[]{:S(2)}) collective-permute-start(bf16[32,32,128]{2,1,0:T(8,128)(2,1)S(1)} %first.7.image.refs_4_), channel_id=1, source_target_pairs={{0,4},{1,5},{2,6},{3,7},{4,0},{5,1},{6,2},{7,3},{8,12},{9,13},{10,... | collective-permute-start | bytes 786440 | tf_op jit(solution)/shard_map/ppermute | solution.py:261
  80.7 1.3 %collective-permute-start.42 = (bf16[16,32,128]{2,1,0:T(8,128)(2,1)S(1)}, bf16[16,32,128]{2,1,0:T(8,128)(2,1)S(1)}, u32[]{:S(2)}, u32[]{:S(2)}) collective-permute-start(bf16[16,32,128]{2,1,0:T(8,128)(2,1)S(1)} %project.13), channel_id=1, source_target_pairs={{0,7},{1,6},{2,5},{3,4},{4,8},{5,9},{6,10},{7,11},{8,15},{9,14},{1... | collective-permute-start | bytes 393224 | tf_op jit(solution)/shard_map/ppermute | solution.py:261
  82.1 0.4 collective-permute-start.39
  82.5 4.4 %collective-permute-done.42.refs_8_ = bf16[16,32,128]{2,1,0:T(8,128)(2,1)S(1)} collective-permute-done((bf16[16,32,128]{2,1,0:T(8,128)(2,1)S(1)}, bf16[16,32,128]{2,1,0:T(8,128)(2,1)S(1)}, u32[]{:S(2)}, u32[]{:S(2)}) %collective-permute-start.42) | collective-permute-done | bytes 131104 | tf_op jit(solution)/shard_map/ppermute | solution.py:261
  86.9 1.4 %collective-permute-done.41.refs_7_ = bf16[16,32,128]{2,1,0:T(8,128)(2,1)S(1)} collective-permute-done((bf16[16,32,128]{2,1,0:T(8,128)(2,1)S(1)}, bf16[16,32,128]{2,1,0:T(8,128)(2,1)S(1)}, u32[]{:S(2)}, u32[]{:S(2)}) %collective-permute-start.41) | collective-permute-done | bytes 131104 | tf_op jit(solution)/shard_map/ppermute | solution.py:261
  88.3 0.8 second.7
  (57 shorter events, 2.8 us)
Async XLA Ops:
  0.0 8.9 %collective-permute-start.1 = (bf16[1,1,80,128,128]{4,3,2,1,0:T(8,128)(2,1)}, bf16[1,1,80,128,128]{4,3,2,1,0:T(8,128)(2,1)S(1)}, u32[]{:S(2)}, u32[]{:S(2)}) collective-permute-start(bf16[1,1,80,128,128]{4,3,2,1,0:T(8,128)(2,1)} %blocks_in.1), channel_id=1, source_target_pairs={{0,4},{1,5},{2,6},{3,7},{4,0},{5,1},{6,2},{7,3},{8,12},{9,13},{10,... | collective-permute-start | bytes 7864328 | tf_op jit(solution)/shard_map/ppermute | solution.py:261
  3.6 6.7 %collective-permute-start.4 = (f32[5,32,128]{2,1,0:T(8,128)S(1)}, f32[5,32,128]{2,1,0:T(8,128)S(1)}, u32[]{:S(2)}, u32[]{:S(2)}) collective-permute-start(f32[5,32,128]{2,1,0:T(8,128)S(1)} %get-tuple-element.23._.refs_2_), channel_id=1, source_target_pairs={{0,3},{1,2},{2,1},{3,0},{4,7},{5,6},{6,5},{7,4},{8,11},{9,10},{10,... | collective-permute-start | bytes 245768 | tf_op jit(solution)/shard_map/ppermute | solution.py:261
  7.1 4.9 %collective-permute-start.3 = (f32[5,32,128]{2,1,0:T(8,128)S(1)}, f32[5,32,128]{2,1,0:T(8,128)S(1)}, u32[]{:S(2)}, u32[]{:S(2)}) collective-permute-start(f32[5,32,128]{2,1,0:T(8,128)S(1)} %get-tuple-element.23._.refs_2_), channel_id=1, source_target_pairs={{0,2},{1,3},{2,0},{3,1},{4,6},{5,7},{6,4},{7,5},{8,10},{9,11},{10,... | collective-permute-start | bytes 245768 | tf_op jit(solution)/shard_map/ppermute | solution.py:261
  7.6 4.6 %collective-permute-start.2 = (f32[5,32,128]{2,1,0:T(8,128)S(1)}, f32[5,32,128]{2,1,0:T(8,128)S(1)}, u32[]{:S(2)}, u32[]{:S(2)}) collective-permute-start(f32[5,32,128]{2,1,0:T(8,128)S(1)} %get-tuple-element.23._.refs_2_), channel_id=1, source_target_pairs={{0,1},{1,0},{2,3},{3,2},{4,5},{5,4},{6,7},{7,6},{8,9},{9,8},{10,11... | collective-permute-start | bytes 245768 | tf_op jit(solution)/shard_map/ppermute | solution.py:261
  7.8 1.1 %collective-permute-start = (s32[2,80]{1,0:T(2,128)S(1)}, s32[2,80]{1,0:T(2,128)S(1)}, u32[]{:S(2)}, u32[]{:S(2)}) collective-permute-start(s32[2,80]{1,0:T(2,128)S(1)} %get-tuple-element.20), channel_id=1, source_target_pairs={{0,4},{1,5},{2,6},{3,7},{4,0},{5,1},{6,2},{7,3},{8,12},{9,13},{10,... | collective-permute-start | bytes 1928 | tf_op jit(solution)/shard_map/ppermute | solution.py:261
  12.9 8.3 %collective-permute-start.5 = (bf16[32,32,128]{2,1,0:T(8,128)(2,1)S(1)}, bf16[32,32,128]{2,1,0:T(8,128)(2,1)S(1)}, u32[]{:S(2)}, u32[]{:S(2)}) collective-permute-start(bf16[32,32,128]{2,1,0:T(8,128)(2,1)S(1)} %get-tuple-element.25.image.refs_4_), channel_id=1, source_target_pairs={{0,4},{1,5},{2,6},{3,7},{4,0},{5,1},{6,2},{7,3},{8,12},{9,13},{10,... | collective-permute-start | bytes 786440 | tf_op jit(solution)/shard_map/ppermute | solution.py:261
  13.6 6.2 %collective-permute-start.9 = (bf16[16,32,128]{2,1,0:T(8,128)(2,1)S(1)}, bf16[16,32,128]{2,1,0:T(8,128)(2,1)S(1)}, u32[]{:S(2)}, u32[]{:S(2)}) collective-permute-start(bf16[16,32,128]{2,1,0:T(8,128)(2,1)S(1)} %project.7), channel_id=1, source_target_pairs={{0,7},{1,6},{2,5},{3,4},{4,8},{5,9},{6,10},{7,11},{8,15},{9,14},{1... | collective-permute-start | bytes 393224 | tf_op jit(solution)/shard_map/ppermute | solution.py:261
  14.7 6.5 %collective-permute-start.8 = (bf16[16,32,128]{2,1,0:T(8,128)(2,1)S(1)}, bf16[16,32,128]{2,1,0:T(8,128)(2,1)S(1)}, u32[]{:S(2)}, u32[]{:S(2)}) collective-permute-start(bf16[16,32,128]{2,1,0:T(8,128)(2,1)S(1)} %project.7), channel_id=1, source_target_pairs={{0,6},{1,7},{2,4},{3,5},{4,8},{5,9},{6,10},{7,11},{8,14},{9,15},{1... | collective-permute-start | bytes 393224 | tf_op jit(solution)/shard_map/ppermute | solution.py:261
  15.2 6.0 %collective-permute-start.7 = (bf16[16,32,128]{2,1,0:T(8,128)(2,1)S(1)}, bf16[16,32,128]{2,1,0:T(8,128)(2,1)S(1)}, u32[]{:S(2)}, u32[]{:S(2)}) collective-permute-start(bf16[16,32,128]{2,1,0:T(8,128)(2,1)S(1)} %project.7), channel_id=1, source_target_pairs={{0,5},{1,4},{2,7},{3,6},{4,0},{5,1},{6,2},{7,3},{8,13},{9,12},{10,... | collective-permute-start | bytes 393224 | tf_op jit(solution)/shard_map/ppermute | solution.py:261
  16.7 4.5 %collective-permute-start.6 = (bf16[16,32,128]{2,1,0:T(8,128)(2,1)S(1)}, bf16[16,32,128]{2,1,0:T(8,128)(2,1)S(1)}, u32[]{:S(2)}, u32[]{:S(2)}) collective-permute-start(bf16[16,32,128]{2,1,0:T(8,128)(2,1)S(1)} %project.7), channel_id=1, source_target_pairs={{0,4},{1,5},{2,6},{3,7},{4,0},{5,1},{6,2},{7,3},{8,12},{9,13},{10,... | collective-permute-start | bytes 393224 | tf_op jit(solution)/shard_map/ppermute | solution.py:261
  21.3 6.4 %collective-permute-start.10 = (bf16[32,32,128]{2,1,0:T(8,128)(2,1)S(1)}, bf16[32,32,128]{2,1,0:T(8,128)(2,1)S(1)}, u32[]{:S(2)}, u32[]{:S(2)}) collective-permute-start(bf16[32,32,128]{2,1,0:T(8,128)(2,1)S(1)} %get-tuple-element.27), channel_id=1, source_target_pairs={{0,1},{1,0},{2,3},{3,2},{4,12},{5,13},{6,14},{7,15},{8,9},{9,8},{1... | collective-permute-start | bytes 786440 | tf_op jit(solution)/shard_map/ppermute | solution.py:261
  27.7 6.8 %collective-permute-start.11 = (bf16[32,32,128]{2,1,0:T(8,128)(2,1)S(1)}, bf16[32,32,128]{2,1,0:T(8,128)(2,1)S(1)}, u32[]{:S(2)}, u32[]{:S(2)}) collective-permute-start(bf16[32,32,128]{2,1,0:T(8,128)(2,1)S(1)} %collective-permute-done.10.image), channel_id=1, source_target_pairs={{0,4},{1,5},{2,6},{3,7},{4,0},{5,1},{6,2},{7,3},{8,12},{9,13},{10,... | collective-permute-start | bytes 786440 | tf_op jit(solution)/shard_map/ppermute | solution.py:261
  27.7 5.4 %collective-permute-start.15 = (bf16[16,32,128]{2,1,0:T(8,128)(2,1)S(1)}, bf16[16,32,128]{2,1,0:T(8,128)(2,1)S(1)}, u32[]{:S(2)}, u32[]{:S(2)}) collective-permute-start(bf16[16,32,128]{2,1,0:T(8,128)(2,1)S(1)} %project.8), channel_id=1, source_target_pairs={{0,12},{1,13},{2,14},{3,15},{4,3},{5,2},{6,1},{7,0},{8,20},{9,21},... | collective-permute-start | bytes 393224 | tf_op jit(solution)/shard_map/ppermute | solution.py:261
  27.9 6.5 %collective-permute-start.14 = (bf16[16,32,128]{2,1,0:T(8,128)(2,1)S(1)}, bf16[16,32,128]{2,1,0:T(8,128)(2,1)S(1)}, u32[]{:S(2)}, u32[]{:S(2)}) collective-permute-start(bf16[16,32,128]{2,1,0:T(8,128)(2,1)S(1)} %project.8), channel_id=1, source_target_pairs={{0,12},{1,13},{2,14},{3,15},{4,2},{5,3},{6,0},{7,1},{8,20},{9,21},... | collective-permute-start | bytes 393224 | tf_op jit(solution)/shard_map/ppermute | solution.py:261
  28.4 6.0 %collective-permute-start.13 = (bf16[16,32,128]{2,1,0:T(8,128)(2,1)S(1)}, bf16[16,32,128]{2,1,0:T(8,128)(2,1)S(1)}, u32[]{:S(2)}, u32[]{:S(2)}) collective-permute-start(bf16[16,32,128]{2,1,0:T(8,128)(2,1)S(1)} %project.8), channel_id=1, source_target_pairs={{0,4},{1,5},{2,6},{3,7},{4,1},{5,0},{6,3},{7,2},{8,12},{9,13},{10,... | collective-permute-start | bytes 393224 | tf_op jit(solution)/shard_map/ppermute | solution.py:261
  29.4 5.1 %collective-permute-start.12 = (bf16[16,32,128]{2,1,0:T(8,128)(2,1)S(1)}, bf16[16,32,128]{2,1,0:T(8,128)(2,1)S(1)}, u32[]{:S(2)}, u32[]{:S(2)}) collective-permute-start(bf16[16,32,128]{2,1,0:T(8,128)(2,1)S(1)} %project.8), channel_id=1, source_target_pairs={{0,4},{1,5},{2,6},{3,7},{4,0},{5,1},{6,2},{7,3},{8,12},{9,13},{10,... | collective-permute-start | bytes 393224 | tf_op jit(solution)/shard_map/ppermute | solution.py:261
  34.5 9.1 %collective-permute-start.16 = (bf16[32,32,128]{2,1,0:T(8,128)(2,1)S(1)}, bf16[32,32,128]{2,1,0:T(8,128)(2,1)S(1)}, u32[]{:S(2)}, u32[]{:S(2)}) collective-permute-start(bf16[32,32,128]{2,1,0:T(8,128)(2,1)S(1)} %first.5.image.refs_4_), channel_id=1, source_target_pairs={{0,4},{1,5},{2,6},{3,7},{4,0},{5,1},{6,2},{7,3},{8,12},{9,13},{10,... | collective-permute-start | bytes 786440 | tf_op jit(solution)/shard_map/ppermute | solution.py:261
  35.9 6.2 %collective-permute-start.20 = (bf16[16,32,128]{2,1,0:T(8,128)(2,1)S(1)}, bf16[16,32,128]{2,1,0:T(8,128)(2,1)S(1)}, u32[]{:S(2)}, u32[]{:S(2)}) collective-permute-start(bf16[16,32,128]{2,1,0:T(8,128)(2,1)S(1)} %project.9), channel_id=1, source_target_pairs={{0,7},{1,6},{2,5},{3,4},{4,8},{5,9},{6,10},{7,11},{8,15},{9,14},{1... | collective-permute-start | bytes 393224 | tf_op jit(solution)/shard_map/ppermute | solution.py:261
  37.2 6.3 %collective-permute-start.19 = (bf16[16,32,128]{2,1,0:T(8,128)(2,1)S(1)}, bf16[16,32,128]{2,1,0:T(8,128)(2,1)S(1)}, u32[]{:S(2)}, u32[]{:S(2)}) collective-permute-start(bf16[16,32,128]{2,1,0:T(8,128)(2,1)S(1)} %project.9), channel_id=1, source_target_pairs={{0,6},{1,7},{2,4},{3,5},{4,8},{5,9},{6,10},{7,11},{8,14},{9,15},{1... | collective-permute-start | bytes 393224 | tf_op jit(solution)/shard_map/ppermute | solution.py:261
  37.2 6.3 %collective-permute-start.18 = (bf16[16,32,128]{2,1,0:T(8,128)(2,1)S(1)}, bf16[16,32,128]{2,1,0:T(8,128)(2,1)S(1)}, u32[]{:S(2)}, u32[]{:S(2)}) collective-permute-start(bf16[16,32,128]{2,1,0:T(8,128)(2,1)S(1)} %project.9), channel_id=1, source_target_pairs={{0,5},{1,4},{2,7},{3,6},{4,0},{5,1},{6,2},{7,3},{8,13},{9,12},{10,... | collective-permute-start | bytes 393224 | tf_op jit(solution)/shard_map/ppermute | solution.py:261
  37.6 6.0 %collective-permute-start.17 = (bf16[16,32,128]{2,1,0:T(8,128)(2,1)S(1)}, bf16[16,32,128]{2,1,0:T(8,128)(2,1)S(1)}, u32[]{:S(2)}, u32[]{:S(2)}) collective-permute-start(bf16[16,32,128]{2,1,0:T(8,128)(2,1)S(1)} %project.9), channel_id=1, source_target_pairs={{0,4},{1,5},{2,6},{3,7},{4,0},{5,1},{6,2},{7,3},{8,12},{9,13},{10,... | collective-permute-start | bytes 393224 | tf_op jit(solution)/shard_map/ppermute | solution.py:261
  43.6 6.4 %collective-permute-start.21 = (bf16[32,32,128]{2,1,0:T(8,128)(2,1)S(1)}, bf16[32,32,128]{2,1,0:T(8,128)(2,1)S(1)}, u32[]{:S(2)}, u32[]{:S(2)}) collective-permute-start(bf16[32,32,128]{2,1,0:T(8,128)(2,1)S(1)} %get-tuple-element.29), channel_id=1, source_target_pairs={{0,1},{1,0},{2,3},{3,2},{4,28},{5,29},{6,30},{7,31},{8,9},{9,8},{1... | collective-permute-start | bytes 786440 | tf_op jit(solution)/shard_map/ppermute | solution.py:261
  50.0 6.8 %collective-permute-start.22 = (bf16[32,32,128]{2,1,0:T(8,128)(2,1)S(1)}, bf16[32,32,128]{2,1,0:T(8,128)(2,1)S(1)}, u32[]{:S(2)}, u32[]{:S(2)}) collective-permute-start(bf16[32,32,128]{2,1,0:T(8,128)(2,1)S(1)} %collective-permute-done.21.image), channel_id=1, source_target_pairs={{0,4},{1,5},{2,6},{3,7},{4,0},{5,1},{6,2},{7,3},{8,12},{9,13},{10,... | collective-permute-start | bytes 786440 | tf_op jit(solution)/shard_map/ppermute | solution.py:261
  50.3 5.4 %collective-permute-start.26 = (bf16[16,32,128]{2,1,0:T(8,128)(2,1)S(1)}, bf16[16,32,128]{2,1,0:T(8,128)(2,1)S(1)}, u32[]{:S(2)}, u32[]{:S(2)}) collective-permute-start(bf16[16,32,128]{2,1,0:T(8,128)(2,1)S(1)} %project.10), channel_id=1, source_target_pairs={{0,12},{1,13},{2,14},{3,15},{4,3},{5,2},{6,1},{7,0},{8,20},{9,21},... | collective-permute-start | bytes 393224 | tf_op jit(solution)/shard_map/ppermute | solution.py:261
  50.5 6.3 %collective-permute-start.25 = (bf16[16,32,128]{2,1,0:T(8,128)(2,1)S(1)}, bf16[16,32,128]{2,1,0:T(8,128)(2,1)S(1)}, u32[]{:S(2)}, u32[]{:S(2)}) collective-permute-start(bf16[16,32,128]{2,1,0:T(8,128)(2,1)S(1)} %project.10), channel_id=1, source_target_pairs={{0,12},{1,13},{2,14},{3,15},{4,2},{5,3},{6,0},{7,1},{8,20},{9,21},... | collective-permute-start | bytes 393224 | tf_op jit(solution)/shard_map/ppermute | solution.py:261
  52.1 4.7 %collective-permute-start.24 = (bf16[16,32,128]{2,1,0:T(8,128)(2,1)S(1)}, bf16[16,32,128]{2,1,0:T(8,128)(2,1)S(1)}, u32[]{:S(2)}, u32[]{:S(2)}) collective-permute-start(bf16[16,32,128]{2,1,0:T(8,128)(2,1)S(1)} %project.10), channel_id=1, source_target_pairs={{0,4},{1,5},{2,6},{3,7},{4,1},{5,0},{6,3},{7,2},{8,12},{9,13},{10,... | collective-permute-start | bytes 393224 | tf_op jit(solution)/shard_map/ppermute | solution.py:261
  52.1 4.7 %collective-permute-start.23 = (bf16[16,32,128]{2,1,0:T(8,128)(2,1)S(1)}, bf16[16,32,128]{2,1,0:T(8,128)(2,1)S(1)}, u32[]{:S(2)}, u32[]{:S(2)}) collective-permute-start(bf16[16,32,128]{2,1,0:T(8,128)(2,1)S(1)} %project.10), channel_id=1, source_target_pairs={{0,4},{1,5},{2,6},{3,7},{4,0},{5,1},{6,2},{7,3},{8,12},{9,13},{10,... | collective-permute-start | bytes 393224 | tf_op jit(solution)/shard_map/ppermute | solution.py:261
  56.8 9.0 %collective-permute-start.27 = (bf16[32,32,128]{2,1,0:T(8,128)(2,1)S(1)}, bf16[32,32,128]{2,1,0:T(8,128)(2,1)S(1)}, u32[]{:S(2)}, u32[]{:S(2)}) collective-permute-start(bf16[32,32,128]{2,1,0:T(8,128)(2,1)S(1)} %first.6.image.refs_4_), channel_id=1, source_target_pairs={{0,4},{1,5},{2,6},{3,7},{4,0},{5,1},{6,2},{7,3},{8,12},{9,13},{10,... | collective-permute-start | bytes 786440 | tf_op jit(solution)/shard_map/ppermute | solution.py:261
  58.2 6.2 %collective-permute-start.31 = (bf16[16,32,128]{2,1,0:T(8,128)(2,1)S(1)}, bf16[16,32,128]{2,1,0:T(8,128)(2,1)S(1)}, u32[]{:S(2)}, u32[]{:S(2)}) collective-permute-start(bf16[16,32,128]{2,1,0:T(8,128)(2,1)S(1)} %project.11), channel_id=1, source_target_pairs={{0,7},{1,6},{2,5},{3,4},{4,8},{5,9},{6,10},{7,11},{8,15},{9,14},{1... | collective-permute-start | bytes 393224 | tf_op jit(solution)/shard_map/ppermute | solution.py:261
  59.5 6.3 %collective-permute-start.30 = (bf16[16,32,128]{2,1,0:T(8,128)(2,1)S(1)}, bf16[16,32,128]{2,1,0:T(8,128)(2,1)S(1)}, u32[]{:S(2)}, u32[]{:S(2)}) collective-permute-start(bf16[16,32,128]{2,1,0:T(8,128)(2,1)S(1)} %project.11), channel_id=1, source_target_pairs={{0,6},{1,7},{2,4},{3,5},{4,8},{5,9},{6,10},{7,11},{8,14},{9,15},{1... | collective-permute-start | bytes 393224 | tf_op jit(solution)/shard_map/ppermute | solution.py:261
  59.5 6.3 %collective-permute-start.29 = (bf16[16,32,128]{2,1,0:T(8,128)(2,1)S(1)}, bf16[16,32,128]{2,1,0:T(8,128)(2,1)S(1)}, u32[]{:S(2)}, u32[]{:S(2)}) collective-permute-start(bf16[16,32,128]{2,1,0:T(8,128)(2,1)S(1)} %project.11), channel_id=1, source_target_pairs={{0,5},{1,4},{2,7},{3,6},{4,0},{5,1},{6,2},{7,3},{8,13},{9,12},{10,... | collective-permute-start | bytes 393224 | tf_op jit(solution)/shard_map/ppermute | solution.py:261
  61.0 4.8 %collective-permute-start.28 = (bf16[16,32,128]{2,1,0:T(8,128)(2,1)S(1)}, bf16[16,32,128]{2,1,0:T(8,128)(2,1)S(1)}, u32[]{:S(2)}, u32[]{:S(2)}) collective-permute-start(bf16[16,32,128]{2,1,0:T(8,128)(2,1)S(1)} %project.11), channel_id=1, source_target_pairs={{0,4},{1,5},{2,6},{3,7},{4,0},{5,1},{6,2},{7,3},{8,12},{9,13},{10,... | collective-permute-start | bytes 393224 | tf_op jit(solution)/shard_map/ppermute | solution.py:261
  66.1 6.4 %collective-permute-start.32 = (bf16[32,32,128]{2,1,0:T(8,128)(2,1)S(1)}, bf16[32,32,128]{2,1,0:T(8,128)(2,1)S(1)}, u32[]{:S(2)}, u32[]{:S(2)}) collective-permute-start(bf16[32,32,128]{2,1,0:T(8,128)(2,1)S(1)} %get-tuple-element.31), channel_id=1, source_target_pairs={{0,1},{1,0},{2,3},{3,2},{4,12},{5,13},{6,14},{7,15},{8,9},{9,8},{1... | collective-permute-start | bytes 786440 | tf_op jit(solution)/shard_map/ppermute | solution.py:261
  72.5 6.8 %collective-permute-start.33 = (bf16[32,32,128]{2,1,0:T(8,128)(2,1)S(1)}, bf16[32,32,128]{2,1,0:T(8,128)(2,1)S(1)}, u32[]{:S(2)}, u32[]{:S(2)}) collective-permute-start(bf16[32,32,128]{2,1,0:T(8,128)(2,1)S(1)} %collective-permute-done.32.image), channel_id=1, source_target_pairs={{0,4},{1,5},{2,6},{3,7},{4,0},{5,1},{6,2},{7,3},{8,12},{9,13},{10,... | collective-permute-start | bytes 786440 | tf_op jit(solution)/shard_map/ppermute | solution.py:261
  72.5 5.4 %collective-permute-start.37 = (bf16[16,32,128]{2,1,0:T(8,128)(2,1)S(1)}, bf16[16,32,128]{2,1,0:T(8,128)(2,1)S(1)}, u32[]{:S(2)}, u32[]{:S(2)}) collective-permute-start(bf16[16,32,128]{2,1,0:T(8,128)(2,1)S(1)} %project.12), channel_id=1, source_target_pairs={{0,12},{1,13},{2,14},{3,15},{4,3},{5,2},{6,1},{7,0},{8,20},{9,21},... | collective-permute-start | bytes 393224 | tf_op jit(solution)/shard_map/ppermute | solution.py:261
  72.5 6.7 %collective-permute-start.36 = (bf16[16,32,128]{2,1,0:T(8,128)(2,1)S(1)}, bf16[16,32,128]{2,1,0:T(8,128)(2,1)S(1)}, u32[]{:S(2)}, u32[]{:S(2)}) collective-permute-start(bf16[16,32,128]{2,1,0:T(8,128)(2,1)S(1)} %project.12), channel_id=1, source_target_pairs={{0,12},{1,13},{2,14},{3,15},{4,2},{5,3},{6,0},{7,1},{8,20},{9,21},... | collective-permute-start | bytes 393224 | tf_op jit(solution)/shard_map/ppermute | solution.py:261
  73.1 6.1 %collective-permute-start.35 = (bf16[16,32,128]{2,1,0:T(8,128)(2,1)S(1)}, bf16[16,32,128]{2,1,0:T(8,128)(2,1)S(1)}, u32[]{:S(2)}, u32[]{:S(2)}) collective-permute-start(bf16[16,32,128]{2,1,0:T(8,128)(2,1)S(1)} %project.12), channel_id=1, source_target_pairs={{0,4},{1,5},{2,6},{3,7},{4,1},{5,0},{6,3},{7,2},{8,12},{9,13},{10,... | collective-permute-start | bytes 393224 | tf_op jit(solution)/shard_map/ppermute | solution.py:261
  74.2 5.1 %collective-permute-start.34 = (bf16[16,32,128]{2,1,0:T(8,128)(2,1)S(1)}, bf16[16,32,128]{2,1,0:T(8,128)(2,1)S(1)}, u32[]{:S(2)}, u32[]{:S(2)}) collective-permute-start(bf16[16,32,128]{2,1,0:T(8,128)(2,1)S(1)} %project.12), channel_id=1, source_target_pairs={{0,4},{1,5},{2,6},{3,7},{4,0},{5,1},{6,2},{7,3},{8,12},{9,13},{10,... | collective-permute-start | bytes 393224 | tf_op jit(solution)/shard_map/ppermute | solution.py:261
  79.3 9.1 %collective-permute-start.38 = (bf16[32,32,128]{2,1,0:T(8,128)(2,1)S(1)}, bf16[32,32,128]{2,1,0:T(8,128)(2,1)S(1)}, u32[]{:S(2)}, u32[]{:S(2)}) collective-permute-start(bf16[32,32,128]{2,1,0:T(8,128)(2,1)S(1)} %first.7.image.refs_4_), channel_id=1, source_target_pairs={{0,4},{1,5},{2,6},{3,7},{4,0},{5,1},{6,2},{7,3},{8,12},{9,13},{10,... | collective-permute-start | bytes 786440 | tf_op jit(solution)/shard_map/ppermute | solution.py:261
  80.7 6.2 %collective-permute-start.42 = (bf16[16,32,128]{2,1,0:T(8,128)(2,1)S(1)}, bf16[16,32,128]{2,1,0:T(8,128)(2,1)S(1)}, u32[]{:S(2)}, u32[]{:S(2)}) collective-permute-start(bf16[16,32,128]{2,1,0:T(8,128)(2,1)S(1)} %project.13), channel_id=1, source_target_pairs={{0,7},{1,6},{2,5},{3,4},{4,8},{5,9},{6,10},{7,11},{8,15},{9,14},{1... | collective-permute-start | bytes 393224 | tf_op jit(solution)/shard_map/ppermute | solution.py:261
  82.0 6.3 %collective-permute-start.41 = (bf16[16,32,128]{2,1,0:T(8,128)(2,1)S(1)}, bf16[16,32,128]{2,1,0:T(8,128)(2,1)S(1)}, u32[]{:S(2)}, u32[]{:S(2)}) collective-permute-start(bf16[16,32,128]{2,1,0:T(8,128)(2,1)S(1)} %project.13), channel_id=1, source_target_pairs={{0,6},{1,7},{2,4},{3,5},{4,8},{5,9},{6,10},{7,11},{8,14},{9,15},{1... | collective-permute-start | bytes 393224 | tf_op jit(solution)/shard_map/ppermute | solution.py:261
  82.0 6.3 %collective-permute-start.40 = (bf16[16,32,128]{2,1,0:T(8,128)(2,1)S(1)}, bf16[16,32,128]{2,1,0:T(8,128)(2,1)S(1)}, u32[]{:S(2)}, u32[]{:S(2)}) collective-permute-start(bf16[16,32,128]{2,1,0:T(8,128)(2,1)S(1)} %project.13), channel_id=1, source_target_pairs={{0,5},{1,4},{2,7},{3,6},{4,0},{5,1},{6,2},{7,3},{8,13},{9,12},{10,... | collective-permute-start | bytes 393224 | tf_op jit(solution)/shard_map/ppermute | solution.py:261
  82.1 6.2 %collective-permute-start.39 = (bf16[16,32,128]{2,1,0:T(8,128)(2,1)S(1)}, bf16[16,32,128]{2,1,0:T(8,128)(2,1)S(1)}, u32[]{:S(2)}, u32[]{:S(2)}) collective-permute-start(bf16[16,32,128]{2,1,0:T(8,128)(2,1)S(1)} %project.13), channel_id=1, source_target_pairs={{0,4},{1,5},{2,6},{3,7},{4,0},{5,1},{6,2},{7,3},{8,12},{9,13},{10,... | collective-permute-start | bytes 393224 | tf_op jit(solution)/shard_map/ppermute | solution.py:261

commit v11 on v9

--- a/solution.py
+++ b/solution.py
@@ -11,6 +11,8 @@
 PIX = 4096
 CB = PIX // BS
 relaxation = 0.5
+
+UPDATE_FLOPS = 10**10
 
 DIRECT = 4
 
@@ -168,65 +170,74 @@
         project(info, tall, image, terms)
 
 
-def first_kernel(place, n_notes, n_terms, *refs):
+def update_kernel(place, core, n_notes, n_terms, *refs):
     refs = list(refs)
-    info, wide, tall = take(refs, 3)
-    if place == 0:
+    info, wide = take(refs, 2)
+    if n_notes:
         notes, terms_in = take(refs, n_notes), []
-        shot, terms, rays, w_scr, x_scr, rays_scr = refs
+        change, rays, w_scr, rays_scr = refs
         gather_rays(info, notes, rays, rays_scr)
     else:
-        rays, image_in = take(refs, 2)
+        (rays,) = take(refs, 1)
         terms_in = take(refs, n_terms)
-        shot, terms, w_scr, x_scr = refs
+        change, w_scr = refs
+
+    @pl.when(on_core(info, place, core))
+    def _():
+        weights(rays, terms_in, w_scr)
+        change[...] = jnp.zeros_like(change)
+        back_project(info, wide, w_scr, change)
+
+
+def first_kernel(place, *refs):
+    refs = list(refs)
+    info, tall, change = take(refs, 3)
+    image_in = take(refs, 1)[0] if place > 0 else None
+    shot, terms = refs
 
     @pl.when(on_core(info, place, 0))
     def _():
-        weights(rays, terms_in, w_scr)
-        if place == 0:
-            x_scr[...] = jnp.zeros_like(x_scr)
-        else:
-            x_scr[...] = image_in[...].astype(jnp.float32)
-        back_project(info, wide, w_scr, x_scr)
-        shot[...] = x_scr[...].astype(jnp.bfloat16)
+        value = change[...]
+        if image_in is not None:
+            value = value + image_in[...].astype(jnp.float32)
+        shot[...] = value.astype(jnp.bfloat16)
         project(info, tall, shot, terms)
 
 
-def second_kernel(place, last, n_terms, *refs):
+def second_kernel(place, last, *refs):
     refs = list(refs)
-    info, rays, wide, image_in, shot = take(refs, 5)
-    terms_in = take(refs, n_terms)
+    info, change, image_in, shot = take(refs, 4)
     held = take(refs, 1) if place > 0 else []
     image = None if last else take(refs, 1)[0]
-    out, w_scr, x_scr = refs
+    (out,) = refs
     batches, per_batch, _ = out.shape
 
+    def value(c):
+        return change[c] + image_in[c].astype(jnp.float32)
+
     def write(source):
-        if not last:
-            out[...] = source[...].astype(jnp.bfloat16)
-            return
         for c in range(CB):
-            value = source[c].astype(jnp.float32).reshape(batches, per_batch, BS)
-            out[:, :, c * BS : (c + 1) * BS] = value.astype(jnp.bfloat16)
+            if last:
+                block = source(c).reshape(batches, per_batch, BS)
+                out[:, :, c * BS : (c + 1) * BS] = block.astype(jnp.bfloat16)
+            else:
+                out[c] = source(c).astype(jnp.bfloat16)
 
     @pl.when(on_core(info, place, 1))
     def _():
-        weights(rays, terms_in, w_scr)
-        x_scr[...] = image_in[...].astype(jnp.float32)
-        back_project(info, wide, w_scr, x_scr)
+        write(value)
         if not last:
-            image[...] = x_scr[...].astype(jnp.bfloat16)
-        write(x_scr)
+            image[...] = out[...]
 
     @pl.when(on_core(info, place, 0))
     def _():
-        write(shot)
+        write(lambda c: shot[c].astype(jnp.float32))
 
     if held:
 
         @pl.when(info[0, 0] != place)
         def _():
-            write(held[0])
+            write(lambda c: held[0][c].astype(jnp.float32))
 
 
 def per_device(blocks, block_rows, block_cols, sinogram):
@@ -278,7 +289,7 @@
             for d in range(tiles)
         ]
 
-    def call(kernel, smem, operands, out_shape, scratch, name):
+    def call(kernel, smem, operands, out_shape, scratch, name, flops=0):
         many = isinstance(out_shape, tuple)
         return pl.pallas_call(
             kernel,
@@ -287,6 +298,9 @@
             out_specs=(VMEM,) * len(out_shape) if many else VMEM,
             scratch_shapes=scratch,
             compiler_params=PARAMS,
+            cost_estimate=pl.CostEstimate(
+                flops=flops, bytes_accessed=0, transcendentals=0
+            ),
             name=name,
         )(*operands)
 
@@ -347,16 +361,32 @@
 
     held = []
     image, rays = None, None
+    change_out = jax.ShapeDtypeStruct(image_shape, jnp.float32)
+
+    def updated(place, core, terms):
+        return call(
+            functools.partial(update_kernel, place, core, 0, len(terms)),
+            1,
+            [info, wide, rays] + terms,
+            change_out,
+            [w_scr],
+            "update",
+            UPDATE_FLOPS,
+        )
+
     for place in range(places):
+        last = place == places - 1
         if place == 0:
-            shot, terms, rays = call(
-                functools.partial(first_kernel, place, len(notes), 0),
+            change, rays = call(
+                functools.partial(update_kernel, place, 0, len(notes), 0),
                 1,
-                [info, wide, tall] + notes,
-                (image_out, terms_out, rays_out),
-                [w_scr, x_scr, rays_scr],
-                "first",
+                [info, wide] + notes,
+                (change_out, rays_out),
+                [w_scr, rays_scr],
+                "update",
+                UPDATE_FLOPS,
             )
+            before = []
         else:
             def hop(p, c, t):
                 return ((2 * place - 1 - p) % places, c, t) if c else (p, c, t ^ 1)
@@ -370,25 +400,23 @@
                 [],
                 "project",
             )
-            image = swapped(image)
-            terms = passed(terms, 1)
-            shot, terms = call(
-                functools.partial(first_kernel, place, 0, len(terms)),
-                1,
-                [info, wide, tall, rays, image] + terms,
-                (image_out, terms_out),
-                [w_scr, x_scr],
-                "first",
-            )
-        image = swapped(shot)
-        terms = passed(terms, 0)
-        last = place == places - 1
+            change = updated(place, 0, passed(terms, 1))
+            before = [swapped(image)]
+        shot, terms = call(
+            functools.partial(first_kernel, place),
+            1,
+            [info, tall, change] + before,
+            (image_out, terms_out),
+            [],
+            "first",
+        )
+        change = updated(place, 1, passed(terms, 0))
         outs = call(
-            functools.partial(second_kernel, place, last, len(terms)),
+            functools.partial(second_kernel, place, last),
             1,
-            [info, rays, wide, image, shot] + terms + held,
+            [info, change, swapped(shot), shot] + held,
             final_out if last else (image_out, image_out),
-            [w_scr, x_scr],
+            [],
             "second",
         )
         if last:

time: 81.2 us -> 75.6 us (0.931)
  starting transfers between devices: 36.7 us -> 30.9 us
    ppermute x43, starting transfers between devices: 36.7 us -> 30.9 us  [sent(): return lax.ppermute(value, ('subset', 'tile'), pairs)]
    pallas_call x11 -> x19, Pallas kernels: 2.17 us -> 2.15 us  [call(): pl.pallas_call(kernel, out_shape=out_shape, in_specs=[SMEM] * smem + [VME...]
  transfers between devices with their start and end apart: 43 -> 43, of which waited for: 19 -> 20; matrix products, arithmetic and copies ran while one was open for 0% -> 0% of each run, Pallas kernels for 7% -> 7%
where the time goes in v11:
time: 75.6 us; the launch traced here: 75.4 us
  waiting for transfers between devices  37.2 us (49%)
  starting transfers between devices  30.9 us (41%)
  Pallas kernels  7.01 us (9%)
    ppermute x43, waiting for transfers between devices, sent(): return lax.ppermute(value, ('subset', 'tile'), pairs)  37.2 us
    ppermute x43, starting transfers between devices, sent(): return lax.ppermute(value, ('subset', 'tile'), pairs)  30.9 us
    pallas_call x1, Pallas kernels, per_device(): pl.pallas_call(functools.partial(head_kernel, row_blocks, chunks), out_sh...  3.06 us
    pallas_call x19, Pallas kernels, call(): pl.pallas_call(kernel, out_shape=out_shape, in_specs=[SMEM] * smem + [VME...  2.15 us
  transfers between devices with their start and end apart: 43, of which 20 were waited for; matrix products, arithmetic and copies ran while one was open for 0% of the time, Pallas kernels for 7%

profile of v11, /device:TPU:25, one launch (start us, length us, event | category | flops | bytes accessed | tf_op | source)
XLA Modules:
  0.0 75.4 jit_solution(7136187989323603431)
XLA Ops:
  0.0 0.7 collective-permute-start.1
  0.8 3.1 %head.1 = (f32[5,32,128]{2,1,0:T(8,128)S(1)}, s32[2,80]{1,0:T(2,128)S(1)}, s32[3,80]{1,0:T(4,128)S(4)}, bf16[1,1,80,128,128]{4,3,2,1,0:T(8,128)(2,1)S(1)}) custom-call(s32[3]{0:T(128)S(1)} %pad_add_fusion.pos, s32[1,1,80]{2,1,0:T(1,128)} %rows_in.1, s32[1,1,80]{2,1,0:T(1,128)} %cols_in.1, bf16[1,1,80,128,128]{4,3,2,1,0:T(8,128)(2,1)} %blocks_in.1, ...), custom_call_target="tpu_custom_call" | custom-call | tf_op jit(solution)/shard_map/head/pallas_call | solution.py:309
  3.8 2.2 %collective-permute-start.4 = (f32[5,32,128]{2,1,0:T(8,128)S(1)}, f32[5,32,128]{2,1,0:T(8,128)S(1)}, u32[]{:S(2)}, u32[]{:S(2)}) collective-permute-start(f32[5,32,128]{2,1,0:T(8,128)S(1)} %get-tuple-element.31._.refs_2_), channel_id=1, source_target_pairs={{0,3},{1,2},{2,1},{3,0},{4,7},{5,6},{6,5},{7,4},{8,11},{9,10},{10,... | collective-permute-start | bytes 245768 | tf_op jit(solution)/shard_map/ppermute | solution.py:273
  6.5 0.8 %collective-permute-start = (s32[2,80]{1,0:T(2,128)S(1)}, s32[2,80]{1,0:T(2,128)S(1)}, u32[]{:S(2)}, u32[]{:S(2)}) collective-permute-start(s32[2,80]{1,0:T(2,128)S(1)} %get-tuple-element.28), channel_id=1, source_target_pairs={{0,4},{1,5},{2,6},{3,7},{4,0},{5,1},{6,2},{7,3},{8,12},{9,13},{10,... | collective-permute-start | bytes 1928 | tf_op jit(solution)/shard_map/ppermute | solution.py:273
  7.4 0.5 pack_own.1.refs_1_
  7.9 0.3 collective-permute-done.table2
  8.2 1.3 %pack_other.1 = (s32[3,80]{1,0:T(4,128)S(4)}, bf16[16,640,128]{2,1,0:T(8,128)(2,1)S(1)}) custom-call(s32[3,80]{1,0:T(4,128)S(4)} %get-tuple-element.27.own, s32[2,80]{1,0:T(2,128)S(1)} %collective-permute-done.table2, bf16[1,1,80,128,128]{4,3,2,1,0:T(8,128)(2,1)S(1)} %collective-permute-done.1.blocks2), custom_call_target="tpu_custom_call" | custom-call | tf_op jit(solution)/shard_map/pack_other/pallas_call | solution.py:349
  9.6 1.2 %collective-permute-done.3.refs_4_ = f32[5,32,128]{2,1,0:T(8,128)S(1)} collective-permute-done((f32[5,32,128]{2,1,0:T(8,128)S(1)}, f32[5,32,128]{2,1,0:T(8,128)S(1)}, u32[]{:S(2)}, u32[]{:S(2)}) %collective-permute-start.3) | collective-permute-done | bytes 81952 | tf_op jit(solution)/shard_map/ppermute | solution.py:273
  10.8 0.8 %collective-permute-start.8 = (bf16[16,32,128]{2,1,0:T(8,128)(2,1)S(1)}, bf16[16,32,128]{2,1,0:T(8,128)(2,1)S(1)}, u32[]{:S(2)}, u32[]{:S(2)}) collective-permute-start(bf16[16,32,128]{2,1,0:T(8,128)(2,1)S(1)} %get-tuple-element.35), channel_id=1, source_target_pairs={{0,7},{1,6},{2,5},{3,4},{4,0},{5,1},{6,2},{7,3},{8,15},{9,14},{10,... | collective-permute-start | bytes 393224 | tf_op jit(solution)/shard_map/ppermute | solution.py:273
  11.6 0.7 collective-permute-start.7
  12.3 0.9 %collective-permute-start.6 = (bf16[16,32,128]{2,1,0:T(8,128)(2,1)S(1)}, bf16[16,32,128]{2,1,0:T(8,128)(2,1)S(1)}, u32[]{:S(2)}, u32[]{:S(2)}) collective-permute-start(bf16[16,32,128]{2,1,0:T(8,128)(2,1)S(1)} %get-tuple-element.35), channel_id=1, source_target_pairs={{0,5},{1,4},{2,7},{3,6},{4,0},{5,1},{6,2},{7,3},{8,13},{9,12},{10,... | collective-permute-start | bytes 393224 | tf_op jit(solution)/shard_map/ppermute | solution.py:273
  13.2 1.1 %collective-permute-start.5 = (bf16[16,32,128]{2,1,0:T(8,128)(2,1)S(1)}, bf16[16,32,128]{2,1,0:T(8,128)(2,1)S(1)}, u32[]{:S(2)}, u32[]{:S(2)}) collective-permute-start(bf16[16,32,128]{2,1,0:T(8,128)(2,1)S(1)} %get-tuple-element.35), channel_id=1, source_target_pairs={{0,4},{1,5},{2,6},{3,7},{4,0},{5,1},{6,2},{7,3},{8,12},{9,13},{10,... | collective-permute-start | bytes 393224 | tf_op jit(solution)/shard_map/ppermute | solution.py:273
  14.3 2.0 %collective-permute-done.8.refs_6_ = bf16[16,32,128]{2,1,0:T(8,128)(2,1)S(1)} collective-permute-done((bf16[16,32,128]{2,1,0:T(8,128)(2,1)S(1)}, bf16[16,32,128]{2,1,0:T(8,128)(2,1)S(1)}, u32[]{:S(2)}, u32[]{:S(2)}) %collective-permute-start.8) | collective-permute-done | bytes 131104 | tf_op jit(solution)/shard_map/ppermute | solution.py:273
  16.3 1.3 %collective-permute-done.7.refs_5_ = bf16[16,32,128]{2,1,0:T(8,128)(2,1)S(1)} collective-permute-done((bf16[16,32,128]{2,1,0:T(8,128)(2,1)S(1)}, bf16[16,32,128]{2,1,0:T(8,128)(2,1)S(1)}, u32[]{:S(2)}, u32[]{:S(2)}) %collective-permute-start.7) | collective-permute-done | bytes 131104 | tf_op jit(solution)/shard_map/ppermute | solution.py:273
  18.1 5.1 %collective-permute-done.10.image = bf16[32,32,128]{2,1,0:T(8,128)(2,1)S(1)} collective-permute-done((bf16[32,32,128]{2,1,0:T(8,128)(2,1)S(1)}, bf16[32,32,128]{2,1,0:T(8,128)(2,1)S(1)}, u32[]{:S(2)}, u32[]{:S(2)}) %collective-permute-start.10) | collective-permute-done | bytes 262176 | tf_op jit(solution)/shard_map/ppermute | solution.py:273
  23.2 1.5 %collective-permute-start.14 = (bf16[16,32,128]{2,1,0:T(8,128)(2,1)S(1)}, bf16[16,32,128]{2,1,0:T(8,128)(2,1)S(1)}, u32[]{:S(2)}, u32[]{:S(2)}) collective-permute-start(bf16[16,32,128]{2,1,0:T(8,128)(2,1)S(1)} %project.3), channel_id=1, source_target_pairs={{0,4},{1,5},{2,6},{3,7},{4,3},{5,2},{6,1},{7,0},{8,12},{9,13},{10,... | collective-permute-start | bytes 393224 | tf_op jit(solution)/shard_map/ppermute | solution.py:273
  24.7 1.0 %collective-permute-start.12 = (bf16[16,32,128]{2,1,0:T(8,128)(2,1)S(1)}, bf16[16,32,128]{2,1,0:T(8,128)(2,1)S(1)}, u32[]{:S(2)}, u32[]{:S(2)}) collective-permute-start(bf16[16,32,128]{2,1,0:T(8,128)(2,1)S(1)} %project.3), channel_id=1, source_target_pairs={{0,4},{1,5},{2,6},{3,7},{4,1},{5,0},{6,3},{7,2},{8,12},{9,13},{10,... | collective-permute-start | bytes 393224 | tf_op jit(solution)/shard_map/ppermute | solution.py:273
  25.7 0.5 collective-permute-start.15
  26.2 0.4 collective-permute-done.14.refs_6_
  26.6 1.4 %collective-permute-done.13.refs_5_ = bf16[16,32,128]{2,1,0:T(8,128)(2,1)S(1)} collective-permute-done((bf16[16,32,128]{2,1,0:T(8,128)(2,1)S(1)}, bf16[16,32,128]{2,1,0:T(8,128)(2,1)S(1)}, u32[]{:S(2)}, u32[]{:S(2)}) %collective-permute-start.13) | collective-permute-done | bytes 131104 | tf_op jit(solution)/shard_map/ppermute | solution.py:273
  28.0 1.8 %collective-permute-start.19 = (bf16[16,32,128]{2,1,0:T(8,128)(2,1)S(1)}, bf16[16,32,128]{2,1,0:T(8,128)(2,1)S(1)}, u32[]{:S(2)}, u32[]{:S(2)}) collective-permute-start(bf16[16,32,128]{2,1,0:T(8,128)(2,1)S(1)} %get-tuple-element.38), channel_id=1, source_target_pairs={{0,7},{1,6},{2,5},{3,4},{4,0},{5,1},{6,2},{7,3},{8,15},{9,14},{10,... | collective-permute-start | bytes 393224 | tf_op jit(solution)/shard_map/ppermute | solution.py:273
  29.9 1.1 %collective-permute-start.17 = (bf16[16,32,128]{2,1,0:T(8,128)(2,1)S(1)}, bf16[16,32,128]{2,1,0:T(8,128)(2,1)S(1)}, u32[]{:S(2)}, u32[]{:S(2)}) collective-permute-start(bf16[16,32,128]{2,1,0:T(8,128)(2,1)S(1)} %get-tuple-element.38), channel_id=1, source_target_pairs={{0,5},{1,4},{2,7},{3,6},{4,0},{5,1},{6,2},{7,3},{8,13},{9,12},{10,... | collective-permute-start | bytes 393224 | tf_op jit(solution)/shard_map/ppermute | solution.py:273
  31.2 0.4 collective-permute-start.20
  31.6 2.1 %collective-permute-done.19.refs_6_ = bf16[16,32,128]{2,1,0:T(8,128)(2,1)S(1)} collective-permute-done((bf16[16,32,128]{2,1,0:T(8,128)(2,1)S(1)}, bf16[16,32,128]{2,1,0:T(8,128)(2,1)S(1)}, u32[]{:S(2)}, u32[]{:S(2)}) %collective-permute-start.19) | collective-permute-done | bytes 131104 | tf_op jit(solution)/shard_map/ppermute | solution.py:273
  33.7 1.3 %collective-permute-done.18.refs_5_ = bf16[16,32,128]{2,1,0:T(8,128)(2,1)S(1)} collective-permute-done((bf16[16,32,128]{2,1,0:T(8,128)(2,1)S(1)}, bf16[16,32,128]{2,1,0:T(8,128)(2,1)S(1)}, u32[]{:S(2)}, u32[]{:S(2)}) %collective-permute-start.18) | collective-permute-done | bytes 131104 | tf_op jit(solution)/shard_map/ppermute | solution.py:273
  35.1 0.3 collective-permute-start.21
  35.4 6.9 %collective-permute-done.21.image = bf16[32,32,128]{2,1,0:T(8,128)(2,1)S(1)} collective-permute-done((bf16[32,32,128]{2,1,0:T(8,128)(2,1)S(1)}, bf16[32,32,128]{2,1,0:T(8,128)(2,1)S(1)}, u32[]{:S(2)}, u32[]{:S(2)}) %collective-permute-start.21) | collective-permute-done | bytes 262176 | tf_op jit(solution)/shard_map/ppermute | solution.py:273
  42.3 1.2 %collective-permute-start.24 = (bf16[16,32,128]{2,1,0:T(8,128)(2,1)S(1)}, bf16[16,32,128]{2,1,0:T(8,128)(2,1)S(1)}, u32[]{:S(2)}, u32[]{:S(2)}) collective-permute-start(bf16[16,32,128]{2,1,0:T(8,128)(2,1)S(1)} %project.4), channel_id=1, source_target_pairs={{0,4},{1,5},{2,6},{3,7},{4,2},{5,3},{6,0},{7,1},{8,12},{9,13},{10,... | collective-permute-start | bytes 393224 | tf_op jit(solution)/shard_map/ppermute | solution.py:273
  43.5 0.5 collective-permute-start.22
  44.3 1.9 %collective-permute-done.24.refs_5_ = bf16[16,32,128]{2,1,0:T(8,128)(2,1)S(1)} collective-permute-done((bf16[16,32,128]{2,1,0:T(8,128)(2,1)S(1)}, bf16[16,32,128]{2,1,0:T(8,128)(2,1)S(1)}, u32[]{:S(2)}, u32[]{:S(2)}) %collective-permute-start.24) | collective-permute-done | bytes 131104 | tf_op jit(solution)/shard_map/ppermute | solution.py:273
  46.2 1.8 %collective-permute-start.30 = (bf16[16,32,128]{2,1,0:T(8,128)(2,1)S(1)}, bf16[16,32,128]{2,1,0:T(8,128)(2,1)S(1)}, u32[]{:S(2)}, u32[]{:S(2)}) collective-permute-start(bf16[16,32,128]{2,1,0:T(8,128)(2,1)S(1)} %get-tuple-element.42), channel_id=1, source_target_pairs={{0,7},{1,6},{2,5},{3,4},{4,0},{5,1},{6,2},{7,3},{8,15},{9,14},{10,... | collective-permute-start | bytes 393224 | tf_op jit(solution)/shard_map/ppermute | solution.py:273
  48.1 1.1 %collective-permute-start.28 = (bf16[16,32,128]{2,1,0:T(8,128)(2,1)S(1)}, bf16[16,32,128]{2,1,0:T(8,128)(2,1)S(1)}, u32[]{:S(2)}, u32[]{:S(2)}) collective-permute-start(bf16[16,32,128]{2,1,0:T(8,128)(2,1)S(1)} %get-tuple-element.42), channel_id=1, source_target_pairs={{0,5},{1,4},{2,7},{3,6},{4,0},{5,1},{6,2},{7,3},{8,13},{9,12},{10,... | collective-permute-start | bytes 393224 | tf_op jit(solution)/shard_map/ppermute | solution.py:273
  49.3 0.4 collective-permute-start.31
  49.7 2.1 %collective-permute-done.30.refs_6_ = bf16[16,32,128]{2,1,0:T(8,128)(2,1)S(1)} collective-permute-done((bf16[16,32,128]{2,1,0:T(8,128)(2,1)S(1)}, bf16[16,32,128]{2,1,0:T(8,128)(2,1)S(1)}, u32[]{:S(2)}, u32[]{:S(2)}) %collective-permute-start.30) | collective-permute-done | bytes 131104 | tf_op jit(solution)/shard_map/ppermute | solution.py:273
  51.8 1.3 %collective-permute-done.29.refs_5_ = bf16[16,32,128]{2,1,0:T(8,128)(2,1)S(1)} collective-permute-done((bf16[16,32,128]{2,1,0:T(8,128)(2,1)S(1)}, bf16[16,32,128]{2,1,0:T(8,128)(2,1)S(1)}, u32[]{:S(2)}, u32[]{:S(2)}) %collective-permute-start.29) | collective-permute-done | bytes 131104 | tf_op jit(solution)/shard_map/ppermute | solution.py:273
  53.2 4.4 %collective-permute-start.32 = (bf16[32,32,128]{2,1,0:T(8,128)(2,1)S(1)}, bf16[32,32,128]{2,1,0:T(8,128)(2,1)S(1)}, u32[]{:S(2)}, u32[]{:S(2)}) collective-permute-start(bf16[32,32,128]{2,1,0:T(8,128)(2,1)S(1)} %get-tuple-element.45), channel_id=1, source_target_pairs={{0,1},{1,0},{2,3},{3,2},{4,12},{5,13},{6,14},{7,15},{8,9},{9,8},{1... | collective-permute-start | bytes 786440 | tf_op jit(solution)/shard_map/ppermute | solution.py:273
  57.6 3.8 %collective-permute-done.32.image = bf16[32,32,128]{2,1,0:T(8,128)(2,1)S(1)} collective-permute-done((bf16[32,32,128]{2,1,0:T(8,128)(2,1)S(1)}, bf16[32,32,128]{2,1,0:T(8,128)(2,1)S(1)}, u32[]{:S(2)}, u32[]{:S(2)}) %collective-permute-start.32) | collective-permute-done | bytes 262176 | tf_op jit(solution)/shard_map/ppermute | solution.py:273
  61.4 0.5 project.5
  62.0 1.1 %collective-permute-start.35 = (bf16[16,32,128]{2,1,0:T(8,128)(2,1)S(1)}, bf16[16,32,128]{2,1,0:T(8,128)(2,1)S(1)}, u32[]{:S(2)}, u32[]{:S(2)}) collective-permute-start(bf16[16,32,128]{2,1,0:T(8,128)(2,1)S(1)} %project.5), channel_id=1, source_target_pairs={{0,4},{1,5},{2,6},{3,7},{4,2},{5,3},{6,0},{7,1},{8,12},{9,13},{10,... | collective-permute-start | bytes 393224 | tf_op jit(solution)/shard_map/ppermute | solution.py:273
  63.2 0.5 collective-permute-start.33
  64.0 1.8 %collective-permute-done.35.refs_5_ = bf16[16,32,128]{2,1,0:T(8,128)(2,1)S(1)} collective-permute-done((bf16[16,32,128]{2,1,0:T(8,128)(2,1)S(1)}, bf16[16,32,128]{2,1,0:T(8,128)(2,1)S(1)}, u32[]{:S(2)}, u32[]{:S(2)}) %collective-permute-start.35) | collective-permute-done | bytes 131104 | tf_op jit(solution)/shard_map/ppermute | solution.py:273
  65.8 3.1 %collective-permute-start.41 = (bf16[16,32,128]{2,1,0:T(8,128)(2,1)S(1)}, bf16[16,32,128]{2,1,0:T(8,128)(2,1)S(1)}, u32[]{:S(2)}, u32[]{:S(2)}) collective-permute-start(bf16[16,32,128]{2,1,0:T(8,128)(2,1)S(1)} %get-tuple-element.46), channel_id=1, source_target_pairs={{0,7},{1,6},{2,5},{3,4},{4,0},{5,1},{6,2},{7,3},{8,15},{9,14},{10,... | collective-permute-start | bytes 393224 | tf_op jit(solution)/shard_map/ppermute | solution.py:273
  69.0 1.1 %collective-permute-start.39 = (bf16[16,32,128]{2,1,0:T(8,128)(2,1)S(1)}, bf16[16,32,128]{2,1,0:T(8,128)(2,1)S(1)}, u32[]{:S(2)}, u32[]{:S(2)}) collective-permute-start(bf16[16,32,128]{2,1,0:T(8,128)(2,1)S(1)} %get-tuple-element.46), channel_id=1, source_target_pairs={{0,5},{1,4},{2,7},{3,6},{4,0},{5,1},{6,2},{7,3},{8,13},{9,12},{10,... | collective-permute-start | bytes 393224 | tf_op jit(solution)/shard_map/ppermute | solution.py:273
  70.1 0.4 collective-permute-start.42
  70.5 2.2 %collective-permute-done.41.refs_6_ = bf16[16,32,128]{2,1,0:T(8,128)(2,1)S(1)} collective-permute-done((bf16[16,32,128]{2,1,0:T(8,128)(2,1)S(1)}, bf16[16,32,128]{2,1,0:T(8,128)(2,1)S(1)}, u32[]{:S(2)}, u32[]{:S(2)}) %collective-permute-start.41) | collective-permute-done | bytes 131104 | tf_op jit(solution)/shard_map/ppermute | solution.py:273
  72.7 1.3 %collective-permute-done.40.refs_5_ = bf16[16,32,128]{2,1,0:T(8,128)(2,1)S(1)} collective-permute-done((bf16[16,32,128]{2,1,0:T(8,128)(2,1)S(1)}, bf16[16,32,128]{2,1,0:T(8,128)(2,1)S(1)}, u32[]{:S(2)}, u32[]{:S(2)}) %collective-permute-start.40) | collective-permute-done | bytes 131104 | tf_op jit(solution)/shard_map/ppermute | solution.py:273
  74.1 0.6 update.15.refs_1_
  74.7 0.8 %second.7 = bf16[4,8,4096]{2,1,0:T(8,128)(2,1)} custom-call(s32[3,80]{1,0:T(4,128)S(4)} %get-tuple-element.29.refs_0_.info, f32[32,32,128]{2,1,0:T(8,128)S(1)} %update.15.refs_1_, bf16[32,32,128]{2,1,0:T(8,128)(2,1)S(1)} %collective-permute-done.42.refs_2_, bf16[32,32,128]{2,1,0:T(8,128)(2,1)S(1)} %get-tuple-element.47.refs_3_, ...), custom_call_target="tpu_custom_call" | custom-call | tf_op jit(solution)/shard_map/second/pallas_call | solution.py:294
  (61 shorter events, 2.5 us)
Async XLA Ops:
  0.0 8.2 %collective-permute-start.1 = (bf16[1,1,80,128,128]{4,3,2,1,0:T(8,128)(2,1)}, bf16[1,1,80,128,128]{4,3,2,1,0:T(8,128)(2,1)S(1)}, u32[]{:S(2)}, u32[]{:S(2)}) collective-permute-start(bf16[1,1,80,128,128]{4,3,2,1,0:T(8,128)(2,1)} %blocks_in.1), channel_id=1, source_target_pairs={{0,4},{1,5},{2,6},{3,7},{4,0},{5,1},{6,2},{7,3},{8,12},{9,13},{10,... | collective-permute-start | bytes 7864328 | tf_op jit(solution)/shard_map/ppermute | solution.py:273
  3.8 5.7 %collective-permute-start.4 = (f32[5,32,128]{2,1,0:T(8,128)S(1)}, f32[5,32,128]{2,1,0:T(8,128)S(1)}, u32[]{:S(2)}, u32[]{:S(2)}) collective-permute-start(f32[5,32,128]{2,1,0:T(8,128)S(1)} %get-tuple-element.31._.refs_2_), channel_id=1, source_target_pairs={{0,3},{1,2},{2,1},{3,0},{4,7},{5,6},{6,5},{7,4},{8,11},{9,10},{10,... | collective-permute-start | bytes 245768 | tf_op jit(solution)/shard_map/ppermute | solution.py:273
  6.1 4.7 %collective-permute-start.3 = (f32[5,32,128]{2,1,0:T(8,128)S(1)}, f32[5,32,128]{2,1,0:T(8,128)S(1)}, u32[]{:S(2)}, u32[]{:S(2)}) collective-permute-start(f32[5,32,128]{2,1,0:T(8,128)S(1)} %get-tuple-element.31._.refs_2_), channel_id=1, source_target_pairs={{0,2},{1,3},{2,0},{3,1},{4,6},{5,7},{6,4},{7,5},{8,10},{9,11},{10,... | collective-permute-start | bytes 245768 | tf_op jit(solution)/shard_map/ppermute | solution.py:273
  6.3 4.5 %collective-permute-start.2 = (f32[5,32,128]{2,1,0:T(8,128)S(1)}, f32[5,32,128]{2,1,0:T(8,128)S(1)}, u32[]{:S(2)}, u32[]{:S(2)}) collective-permute-start(f32[5,32,128]{2,1,0:T(8,128)S(1)} %get-tuple-element.31._.refs_2_), channel_id=1, source_target_pairs={{0,1},{1,0},{2,3},{3,2},{4,5},{5,4},{6,7},{7,6},{8,9},{9,8},{10,11... | collective-permute-start | bytes 245768 | tf_op jit(solution)/shard_map/ppermute | solution.py:273
  6.5 1.7 %collective-permute-start = (s32[2,80]{1,0:T(2,128)S(1)}, s32[2,80]{1,0:T(2,128)S(1)}, u32[]{:S(2)}, u32[]{:S(2)}) collective-permute-start(s32[2,80]{1,0:T(2,128)S(1)} %get-tuple-element.28), channel_id=1, source_target_pairs={{0,4},{1,5},{2,6},{3,7},{4,0},{5,1},{6,2},{7,3},{8,12},{9,13},{10,... | collective-permute-start | bytes 1928 | tf_op jit(solution)/shard_map/ppermute | solution.py:273
  10.8 5.4 %collective-permute-start.8 = (bf16[16,32,128]{2,1,0:T(8,128)(2,1)S(1)}, bf16[16,32,128]{2,1,0:T(8,128)(2,1)S(1)}, u32[]{:S(2)}, u32[]{:S(2)}) collective-permute-start(bf16[16,32,128]{2,1,0:T(8,128)(2,1)S(1)} %get-tuple-element.35), channel_id=1, source_target_pairs={{0,7},{1,6},{2,5},{3,4},{4,0},{5,1},{6,2},{7,3},{8,15},{9,14},{10,... | collective-permute-start | bytes 393224 | tf_op jit(solution)/shard_map/ppermute | solution.py:273
  11.6 6.0 %collective-permute-start.7 = (bf16[16,32,128]{2,1,0:T(8,128)(2,1)S(1)}, bf16[16,32,128]{2,1,0:T(8,128)(2,1)S(1)}, u32[]{:S(2)}, u32[]{:S(2)}) collective-permute-start(bf16[16,32,128]{2,1,0:T(8,128)(2,1)S(1)} %get-tuple-element.35), channel_id=1, source_target_pairs={{0,6},{1,7},{2,4},{3,5},{4,0},{5,1},{6,2},{7,3},{8,14},{9,15},{10,... | collective-permute-start | bytes 393224 | tf_op jit(solution)/shard_map/ppermute | solution.py:273
  12.3 5.6 %collective-permute-start.6 = (bf16[16,32,128]{2,1,0:T(8,128)(2,1)S(1)}, bf16[16,32,128]{2,1,0:T(8,128)(2,1)S(1)}, u32[]{:S(2)}, u32[]{:S(2)}) collective-permute-start(bf16[16,32,128]{2,1,0:T(8,128)(2,1)S(1)} %get-tuple-element.35), channel_id=1, source_target_pairs={{0,5},{1,4},{2,7},{3,6},{4,0},{5,1},{6,2},{7,3},{8,13},{9,12},{10,... | collective-permute-start | bytes 393224 | tf_op jit(solution)/shard_map/ppermute | solution.py:273
  13.2 4.7 %collective-permute-start.5 = (bf16[16,32,128]{2,1,0:T(8,128)(2,1)S(1)}, bf16[16,32,128]{2,1,0:T(8,128)(2,1)S(1)}, u32[]{:S(2)}, u32[]{:S(2)}) collective-permute-start(bf16[16,32,128]{2,1,0:T(8,128)(2,1)S(1)} %get-tuple-element.35), channel_id=1, source_target_pairs={{0,4},{1,5},{2,6},{3,7},{4,0},{5,1},{6,2},{7,3},{8,12},{9,13},{10,... | collective-permute-start | bytes 393224 | tf_op jit(solution)/shard_map/ppermute | solution.py:273
  14.3 3.6 %collective-permute-start.9 = (bf16[32,32,128]{2,1,0:T(8,128)(2,1)S(1)}, bf16[32,32,128]{2,1,0:T(8,128)(2,1)S(1)}, u32[]{:S(2)}, u32[]{:S(2)}) collective-permute-start(bf16[32,32,128]{2,1,0:T(8,128)(2,1)S(1)} %get-tuple-element.36.refs_3_), channel_id=1, source_target_pairs={{0,4},{1,5},{2,6},{3,7},{4,0},{5,1},{6,2},{7,3},{8,12},{9,13},{10,... | collective-permute-start | bytes 786440 | tf_op jit(solution)/shard_map/ppermute | solution.py:273
  17.9 5.3 %collective-permute-start.10 = (bf16[32,32,128]{2,1,0:T(8,128)(2,1)S(1)}, bf16[32,32,128]{2,1,0:T(8,128)(2,1)S(1)}, u32[]{:S(2)}, u32[]{:S(2)}) collective-permute-start(bf16[32,32,128]{2,1,0:T(8,128)(2,1)S(1)} %get-tuple-element.37), channel_id=1, source_target_pairs={{0,1},{1,0},{2,3},{3,2},{4,12},{5,13},{6,14},{7,15},{8,9},{9,8},{1... | collective-permute-start | bytes 786440 | tf_op jit(solution)/shard_map/ppermute | solution.py:273
  23.2 3.4 %collective-permute-start.14 = (bf16[16,32,128]{2,1,0:T(8,128)(2,1)S(1)}, bf16[16,32,128]{2,1,0:T(8,128)(2,1)S(1)}, u32[]{:S(2)}, u32[]{:S(2)}) collective-permute-start(bf16[16,32,128]{2,1,0:T(8,128)(2,1)S(1)} %project.3), channel_id=1, source_target_pairs={{0,4},{1,5},{2,6},{3,7},{4,3},{5,2},{6,1},{7,0},{8,12},{9,13},{10,... | collective-permute-start | bytes 393224 | tf_op jit(solution)/shard_map/ppermute | solution.py:273
  24.7 3.3 %collective-permute-start.13 = (bf16[16,32,128]{2,1,0:T(8,128)(2,1)S(1)}, bf16[16,32,128]{2,1,0:T(8,128)(2,1)S(1)}, u32[]{:S(2)}, u32[]{:S(2)}) collective-permute-start(bf16[16,32,128]{2,1,0:T(8,128)(2,1)S(1)} %project.3), channel_id=1, source_target_pairs={{0,4},{1,5},{2,6},{3,7},{4,2},{5,3},{6,0},{7,1},{8,12},{9,13},{10,... | collective-permute-start | bytes 393224 | tf_op jit(solution)/shard_map/ppermute | solution.py:273
  24.7 3.4 %collective-permute-start.12 = (bf16[16,32,128]{2,1,0:T(8,128)(2,1)S(1)}, bf16[16,32,128]{2,1,0:T(8,128)(2,1)S(1)}, u32[]{:S(2)}, u32[]{:S(2)}) collective-permute-start(bf16[16,32,128]{2,1,0:T(8,128)(2,1)S(1)} %project.3), channel_id=1, source_target_pairs={{0,4},{1,5},{2,6},{3,7},{4,1},{5,0},{6,3},{7,2},{8,12},{9,13},{10,... | collective-permute-start | bytes 393224 | tf_op jit(solution)/shard_map/ppermute | solution.py:273
  25.7 2.3 %collective-permute-start.11 = (bf16[16,32,128]{2,1,0:T(8,128)(2,1)S(1)}, bf16[16,32,128]{2,1,0:T(8,128)(2,1)S(1)}, u32[]{:S(2)}, u32[]{:S(2)}) collective-permute-start(bf16[16,32,128]{2,1,0:T(8,128)(2,1)S(1)} %project.3), channel_id=1, source_target_pairs={{0,4},{1,5},{2,6},{3,7},{4,0},{5,1},{6,2},{7,3},{8,12},{9,13},{10,... | collective-permute-start | bytes 393224 | tf_op jit(solution)/shard_map/ppermute | solution.py:273
  25.7 2.3 %collective-permute-start.15 = (bf16[32,32,128]{2,1,0:T(8,128)(2,1)S(1)}, bf16[32,32,128]{2,1,0:T(8,128)(2,1)S(1)}, u32[]{:S(2)}, u32[]{:S(2)}) collective-permute-start(bf16[32,32,128]{2,1,0:T(8,128)(2,1)S(1)} %collective-permute-done.10.image), channel_id=1, source_target_pairs={{0,4},{1,5},{2,6},{3,7},{4,0},{5,1},{6,2},{7,3},{8,12},{9,13},{10,... | collective-permute-start | bytes 786440 | tf_op jit(solution)/shard_map/ppermute | solution.py:273
  28.0 5.7 %collective-permute-start.19 = (bf16[16,32,128]{2,1,0:T(8,128)(2,1)S(1)}, bf16[16,32,128]{2,1,0:T(8,128)(2,1)S(1)}, u32[]{:S(2)}, u32[]{:S(2)}) collective-permute-start(bf16[16,32,128]{2,1,0:T(8,128)(2,1)S(1)} %get-tuple-element.38), channel_id=1, source_target_pairs={{0,7},{1,6},{2,5},{3,4},{4,0},{5,1},{6,2},{7,3},{8,15},{9,14},{10,... | collective-permute-start | bytes 393224 | tf_op jit(solution)/shard_map/ppermute | solution.py:273
  29.9 5.1 %collective-permute-start.18 = (bf16[16,32,128]{2,1,0:T(8,128)(2,1)S(1)}, bf16[16,32,128]{2,1,0:T(8,128)(2,1)S(1)}, u32[]{:S(2)}, u32[]{:S(2)}) collective-permute-start(bf16[16,32,128]{2,1,0:T(8,128)(2,1)S(1)} %get-tuple-element.38), channel_id=1, source_target_pairs={{0,6},{1,7},{2,4},{3,5},{4,0},{5,1},{6,2},{7,3},{8,14},{9,15},{10,... | collective-permute-start | bytes 393224 | tf_op jit(solution)/shard_map/ppermute | solution.py:273
  29.9 5.1 %collective-permute-start.17 = (bf16[16,32,128]{2,1,0:T(8,128)(2,1)S(1)}, bf16[16,32,128]{2,1,0:T(8,128)(2,1)S(1)}, u32[]{:S(2)}, u32[]{:S(2)}) collective-permute-start(bf16[16,32,128]{2,1,0:T(8,128)(2,1)S(1)} %get-tuple-element.38), channel_id=1, source_target_pairs={{0,5},{1,4},{2,7},{3,6},{4,0},{5,1},{6,2},{7,3},{8,13},{9,12},{10,... | collective-permute-start | bytes 393224 | tf_op jit(solution)/shard_map/ppermute | solution.py:273
  31.1 4.0 %collective-permute-start.16 = (bf16[16,32,128]{2,1,0:T(8,128)(2,1)S(1)}, bf16[16,32,128]{2,1,0:T(8,128)(2,1)S(1)}, u32[]{:S(2)}, u32[]{:S(2)}) collective-permute-start(bf16[16,32,128]{2,1,0:T(8,128)(2,1)S(1)} %get-tuple-element.38), channel_id=1, source_target_pairs={{0,4},{1,5},{2,6},{3,7},{4,0},{5,1},{6,2},{7,3},{8,12},{9,13},{10,... | collective-permute-start | bytes 393224 | tf_op jit(solution)/shard_map/ppermute | solution.py:273
  31.2 3.9 %collective-permute-start.20 = (bf16[32,32,128]{2,1,0:T(8,128)(2,1)S(1)}, bf16[32,32,128]{2,1,0:T(8,128)(2,1)S(1)}, u32[]{:S(2)}, u32[]{:S(2)}) collective-permute-start(bf16[32,32,128]{2,1,0:T(8,128)(2,1)S(1)} %get-tuple-element.39.refs_3_), channel_id=1, source_target_pairs={{0,4},{1,5},{2,6},{3,7},{4,0},{5,1},{6,2},{7,3},{8,12},{9,13},{10,... | collective-permute-start | bytes 786440 | tf_op jit(solution)/shard_map/ppermute | solution.py:273
  35.1 7.2 %collective-permute-start.21 = (bf16[32,32,128]{2,1,0:T(8,128)(2,1)S(1)}, bf16[32,32,128]{2,1,0:T(8,128)(2,1)S(1)}, u32[]{:S(2)}, u32[]{:S(2)}) collective-permute-start(bf16[32,32,128]{2,1,0:T(8,128)(2,1)S(1)} %get-tuple-element.41), channel_id=1, source_target_pairs={{0,1},{1,0},{2,3},{3,2},{4,28},{5,29},{6,30},{7,31},{8,9},{9,8},{1... | collective-permute-start | bytes 786440 | tf_op jit(solution)/shard_map/ppermute | solution.py:273
  42.3 2.0 %collective-permute-start.25 = (bf16[16,32,128]{2,1,0:T(8,128)(2,1)S(1)}, bf16[16,32,128]{2,1,0:T(8,128)(2,1)S(1)}, u32[]{:S(2)}, u32[]{:S(2)}) collective-permute-start(bf16[16,32,128]{2,1,0:T(8,128)(2,1)S(1)} %project.4), channel_id=1, source_target_pairs={{0,4},{1,5},{2,6},{3,7},{4,3},{5,2},{6,1},{7,0},{8,12},{9,13},{10,... | collective-permute-start | bytes 393224 | tf_op jit(solution)/shard_map/ppermute | solution.py:273
  42.3 3.8 %collective-permute-start.24 = (bf16[16,32,128]{2,1,0:T(8,128)(2,1)S(1)}, bf16[16,32,128]{2,1,0:T(8,128)(2,1)S(1)}, u32[]{:S(2)}, u32[]{:S(2)}) collective-permute-start(bf16[16,32,128]{2,1,0:T(8,128)(2,1)S(1)} %project.4), channel_id=1, source_target_pairs={{0,4},{1,5},{2,6},{3,7},{4,2},{5,3},{6,0},{7,1},{8,12},{9,13},{10,... | collective-permute-start | bytes 393224 | tf_op jit(solution)/shard_map/ppermute | solution.py:273
  43.5 2.6 %collective-permute-start.23 = (bf16[16,32,128]{2,1,0:T(8,128)(2,1)S(1)}, bf16[16,32,128]{2,1,0:T(8,128)(2,1)S(1)}, u32[]{:S(2)}, u32[]{:S(2)}) collective-permute-start(bf16[16,32,128]{2,1,0:T(8,128)(2,1)S(1)} %project.4), channel_id=1, source_target_pairs={{0,4},{1,5},{2,6},{3,7},{4,1},{5,0},{6,3},{7,2},{8,12},{9,13},{10,... | collective-permute-start | bytes 393224 | tf_op jit(solution)/shard_map/ppermute | solution.py:273
  43.5 2.6 %collective-permute-start.22 = (bf16[16,32,128]{2,1,0:T(8,128)(2,1)S(1)}, bf16[16,32,128]{2,1,0:T(8,128)(2,1)S(1)}, u32[]{:S(2)}, u32[]{:S(2)}) collective-permute-start(bf16[16,32,128]{2,1,0:T(8,128)(2,1)S(1)} %project.4), channel_id=1, source_target_pairs={{0,4},{1,5},{2,6},{3,7},{4,0},{5,1},{6,2},{7,3},{8,12},{9,13},{10,... | collective-permute-start | bytes 393224 | tf_op jit(solution)/shard_map/ppermute | solution.py:273
  44.0 2.1 %collective-permute-start.26 = (bf16[32,32,128]{2,1,0:T(8,128)(2,1)S(1)}, bf16[32,32,128]{2,1,0:T(8,128)(2,1)S(1)}, u32[]{:S(2)}, u32[]{:S(2)}) collective-permute-start(bf16[32,32,128]{2,1,0:T(8,128)(2,1)S(1)} %collective-permute-done.21.image), channel_id=1, source_target_pairs={{0,4},{1,5},{2,6},{3,7},{4,0},{5,1},{6,2},{7,3},{8,12},{9,13},{10,... | collective-permute-start | bytes 786440 | tf_op jit(solution)/shard_map/ppermute | solution.py:273
  46.2 5.7 %collective-permute-start.30 = (bf16[16,32,128]{2,1,0:T(8,128)(2,1)S(1)}, bf16[16,32,128]{2,1,0:T(8,128)(2,1)S(1)}, u32[]{:S(2)}, u32[]{:S(2)}) collective-permute-start(bf16[16,32,128]{2,1,0:T(8,128)(2,1)S(1)} %get-tuple-element.42), channel_id=1, source_target_pairs={{0,7},{1,6},{2,5},{3,4},{4,0},{5,1},{6,2},{7,3},{8,15},{9,14},{10,... | collective-permute-start | bytes 393224 | tf_op jit(solution)/shard_map/ppermute | solution.py:273
  48.0 5.1 %collective-permute-start.29 = (bf16[16,32,128]{2,1,0:T(8,128)(2,1)S(1)}, bf16[16,32,128]{2,1,0:T(8,128)(2,1)S(1)}, u32[]{:S(2)}, u32[]{:S(2)}) collective-permute-start(bf16[16,32,128]{2,1,0:T(8,128)(2,1)S(1)} %get-tuple-element.42), channel_id=1, source_target_pairs={{0,6},{1,7},{2,4},{3,5},{4,0},{5,1},{6,2},{7,3},{8,14},{9,15},{10,... | collective-permute-start | bytes 393224 | tf_op jit(solution)/shard_map/ppermute | solution.py:273
  48.1 5.1 %collective-permute-start.28 = (bf16[16,32,128]{2,1,0:T(8,128)(2,1)S(1)}, bf16[16,32,128]{2,1,0:T(8,128)(2,1)S(1)}, u32[]{:S(2)}, u32[]{:S(2)}) collective-permute-start(bf16[16,32,128]{2,1,0:T(8,128)(2,1)S(1)} %get-tuple-element.42), channel_id=1, source_target_pairs={{0,5},{1,4},{2,7},{3,6},{4,0},{5,1},{6,2},{7,3},{8,13},{9,12},{10,... | collective-permute-start | bytes 393224 | tf_op jit(solution)/shard_map/ppermute | solution.py:273
  49.2 4.0 %collective-permute-start.27 = (bf16[16,32,128]{2,1,0:T(8,128)(2,1)S(1)}, bf16[16,32,128]{2,1,0:T(8,128)(2,1)S(1)}, u32[]{:S(2)}, u32[]{:S(2)}) collective-permute-start(bf16[16,32,128]{2,1,0:T(8,128)(2,1)S(1)} %get-tuple-element.42), channel_id=1, source_target_pairs={{0,4},{1,5},{2,6},{3,7},{4,0},{5,1},{6,2},{7,3},{8,12},{9,13},{10,... | collective-permute-start | bytes 393224 | tf_op jit(solution)/shard_map/ppermute | solution.py:273
  49.3 3.9 %collective-permute-start.31 = (bf16[32,32,128]{2,1,0:T(8,128)(2,1)S(1)}, bf16[32,32,128]{2,1,0:T(8,128)(2,1)S(1)}, u32[]{:S(2)}, u32[]{:S(2)}) collective-permute-start(bf16[32,32,128]{2,1,0:T(8,128)(2,1)S(1)} %get-tuple-element.43.refs_3_), channel_id=1, source_target_pairs={{0,4},{1,5},{2,6},{3,7},{4,0},{5,1},{6,2},{7,3},{8,12},{9,13},{10,... | collective-permute-start | bytes 786440 | tf_op jit(solution)/shard_map/ppermute | solution.py:273
  53.2 8.1 %collective-permute-start.32 = (bf16[32,32,128]{2,1,0:T(8,128)(2,1)S(1)}, bf16[32,32,128]{2,1,0:T(8,128)(2,1)S(1)}, u32[]{:S(2)}, u32[]{:S(2)}) collective-permute-start(bf16[32,32,128]{2,1,0:T(8,128)(2,1)S(1)} %get-tuple-element.45), channel_id=1, source_target_pairs={{0,1},{1,0},{2,3},{3,2},{4,12},{5,13},{6,14},{7,15},{8,9},{9,8},{1... | collective-permute-start | bytes 786440 | tf_op jit(solution)/shard_map/ppermute | solution.py:273
  61.9 2.0 %collective-permute-start.36 = (bf16[16,32,128]{2,1,0:T(8,128)(2,1)S(1)}, bf16[16,32,128]{2,1,0:T(8,128)(2,1)S(1)}, u32[]{:S(2)}, u32[]{:S(2)}) collective-permute-start(bf16[16,32,128]{2,1,0:T(8,128)(2,1)S(1)} %project.5), channel_id=1, source_target_pairs={{0,4},{1,5},{2,6},{3,7},{4,3},{5,2},{6,1},{7,0},{8,12},{9,13},{10,... | collective-permute-start | bytes 393224 | tf_op jit(solution)/shard_map/ppermute | solution.py:273
  62.0 3.7 %collective-permute-start.35 = (bf16[16,32,128]{2,1,0:T(8,128)(2,1)S(1)}, bf16[16,32,128]{2,1,0:T(8,128)(2,1)S(1)}, u32[]{:S(2)}, u32[]{:S(2)}) collective-permute-start(bf16[16,32,128]{2,1,0:T(8,128)(2,1)S(1)} %project.5), channel_id=1, source_target_pairs={{0,4},{1,5},{2,6},{3,7},{4,2},{5,3},{6,0},{7,1},{8,12},{9,13},{10,... | collective-permute-start | bytes 393224 | tf_op jit(solution)/shard_map/ppermute | solution.py:273
  63.2 2.6 %collective-permute-start.34 = (bf16[16,32,128]{2,1,0:T(8,128)(2,1)S(1)}, bf16[16,32,128]{2,1,0:T(8,128)(2,1)S(1)}, u32[]{:S(2)}, u32[]{:S(2)}) collective-permute-start(bf16[16,32,128]{2,1,0:T(8,128)(2,1)S(1)} %project.5), channel_id=1, source_target_pairs={{0,4},{1,5},{2,6},{3,7},{4,1},{5,0},{6,3},{7,2},{8,12},{9,13},{10,... | collective-permute-start | bytes 393224 | tf_op jit(solution)/shard_map/ppermute | solution.py:273
  63.2 2.6 %collective-permute-start.33 = (bf16[16,32,128]{2,1,0:T(8,128)(2,1)S(1)}, bf16[16,32,128]{2,1,0:T(8,128)(2,1)S(1)}, u32[]{:S(2)}, u32[]{:S(2)}) collective-permute-start(bf16[16,32,128]{2,1,0:T(8,128)(2,1)S(1)} %project.5), channel_id=1, source_target_pairs={{0,4},{1,5},{2,6},{3,7},{4,0},{5,1},{6,2},{7,3},{8,12},{9,13},{10,... | collective-permute-start | bytes 393224 | tf_op jit(solution)/shard_map/ppermute | solution.py:273
  63.7 2.1 %collective-permute-start.37 = (bf16[32,32,128]{2,1,0:T(8,128)(2,1)S(1)}, bf16[32,32,128]{2,1,0:T(8,128)(2,1)S(1)}, u32[]{:S(2)}, u32[]{:S(2)}) collective-permute-start(bf16[32,32,128]{2,1,0:T(8,128)(2,1)S(1)} %collective-permute-done.32.image), channel_id=1, source_target_pairs={{0,4},{1,5},{2,6},{3,7},{4,0},{5,1},{6,2},{7,3},{8,12},{9,13},{10,... | collective-permute-start | bytes 786440 | tf_op jit(solution)/shard_map/ppermute | solution.py:273
  65.8 7.0 %collective-permute-start.41 = (bf16[16,32,128]{2,1,0:T(8,128)(2,1)S(1)}, bf16[16,32,128]{2,1,0:T(8,128)(2,1)S(1)}, u32[]{:S(2)}, u32[]{:S(2)}) collective-permute-start(bf16[16,32,128]{2,1,0:T(8,128)(2,1)S(1)} %get-tuple-element.46), channel_id=1, source_target_pairs={{0,7},{1,6},{2,5},{3,4},{4,0},{5,1},{6,2},{7,3},{8,15},{9,14},{10,... | collective-permute-start | bytes 393224 | tf_op jit(solution)/shard_map/ppermute | solution.py:273
  68.9 5.2 %collective-permute-start.40 = (bf16[16,32,128]{2,1,0:T(8,128)(2,1)S(1)}, bf16[16,32,128]{2,1,0:T(8,128)(2,1)S(1)}, u32[]{:S(2)}, u32[]{:S(2)}) collective-permute-start(bf16[16,32,128]{2,1,0:T(8,128)(2,1)S(1)} %get-tuple-element.46), channel_id=1, source_target_pairs={{0,6},{1,7},{2,4},{3,5},{4,0},{5,1},{6,2},{7,3},{8,14},{9,15},{10,... | collective-permute-start | bytes 393224 | tf_op jit(solution)/shard_map/ppermute | solution.py:273
  69.0 5.1 %collective-permute-start.39 = (bf16[16,32,128]{2,1,0:T(8,128)(2,1)S(1)}, bf16[16,32,128]{2,1,0:T(8,128)(2,1)S(1)}, u32[]{:S(2)}, u32[]{:S(2)}) collective-permute-start(bf16[16,32,128]{2,1,0:T(8,128)(2,1)S(1)} %get-tuple-element.46), channel_id=1, source_target_pairs={{0,5},{1,4},{2,7},{3,6},{4,0},{5,1},{6,2},{7,3},{8,13},{9,12},{10,... | collective-permute-start | bytes 393224 | tf_op jit(solution)/shard_map/ppermute | solution.py:273
  70.0 4.0 %collective-permute-start.38 = (bf16[16,32,128]{2,1,0:T(8,128)(2,1)S(1)}, bf16[16,32,128]{2,1,0:T(8,128)(2,1)S(1)}, u32[]{:S(2)}, u32[]{:S(2)}) collective-permute-start(bf16[16,32,128]{2,1,0:T(8,128)(2,1)S(1)} %get-tuple-element.46), channel_id=1, source_target_pairs={{0,4},{1,5},{2,6},{3,7},{4,0},{5,1},{6,2},{7,3},{8,12},{9,13},{10,... | collective-permute-start | bytes 393224 | tf_op jit(solution)/shard_map/ppermute | solution.py:273
  70.1 4.5 %collective-permute-start.42 = (bf16[32,32,128]{2,1,0:T(8,128)(2,1)S(1)}, bf16[32,32,128]{2,1,0:T(8,128)(2,1)S(1)}, u32[]{:S(2)}, u32[]{:S(2)}) collective-permute-start(bf16[32,32,128]{2,1,0:T(8,128)(2,1)S(1)} %get-tuple-element.47.refs_3_), channel_id=1, source_target_pairs={{0,4},{1,5},{2,6},{3,7},{4,0},{5,1},{6,2},{7,3},{8,12},{9,13},{10,... | collective-permute-start | bytes 786440 | tf_op jit(solution)/shard_map/ppermute | solution.py:273

commit v12 on v11

--- a/solution.py
+++ b/solution.py
@@ -27,23 +27,21 @@
     return lax.dot_general(lhs, rhs, dims, preferred_element_type=jnp.float32)
 
 
-def head_kernel(row_blocks, chunks, pos, rows_in, cols_in, blocks_in, rays_in, *refs):
-    note, table, own, blocks, rows, cols, rays, seen, squares, sems = refs
+def head_kernel(row_blocks, chunks, pos, rows_in, cols_in, blocks_in, *refs):
+    norms, table, own, blocks, rows, cols, seen, squares, sems = refs
     count = blocks.shape[2]
     each = count // row_blocks
     per_chunk = count // chunks
-    batches, per_batch, here = rays.shape
-    quarter = here // BS
     small = [
         pltpu.make_async_copy(src, dst, sems.at[i])
-        for i, (src, dst) in enumerate(((rows_in, rows), (cols_in, cols), (rays_in, rays)))
+        for i, (src, dst) in enumerate(((rows_in, rows), (cols_in, cols)))
     ]
     large = []
     for k in range(chunks):
         where = pl.ds(k * per_chunk, per_chunk)
         large.append(
             pltpu.make_async_copy(
-                blocks_in.at[0, 0, where], blocks.at[0, 0, where], sems.at[3 + k]
+                blocks_in.at[0, 0, where], blocks.at[0, 0, where], sems.at[2 + k]
             )
         )
     for copy in small + large:
@@ -63,9 +61,6 @@
         for out, first in ((table, 0), (own, 1)):
             out[first, at] = n
             out[first + 1, at] = col
-    for i in range(quarter):
-        parts = [rays[g, :, i * BS : (i + 1) * BS] for g in range(batches)]
-        note[i] = jnp.concatenate(parts, axis=0)
     for k in range(chunks):
         large[k].wait()
         for n in range(k * per_chunk, (k + 1) * per_chunk):
@@ -82,7 +77,7 @@
         fine = (left - coarse.astype(jnp.float32)).astype(jnp.bfloat16)
         total = dot(coarse, ones, NN) + dot(fine, ones, NN)
         total = jnp.sum(jnp.where(on_diagonal, total, 0.0), axis=0, keepdims=True)
-        note[quarter, r : r + 1] = total
+        norms[r : r + 1] = total
 
 
 def pack_own_kernel(own, blocks, _, wide):
@@ -108,20 +103,37 @@
             tall[r, j * BS : (j + 1) * BS] = block.T
 
 
-def gather_rays(info, notes, rays, rays_scr):
-    tiles, quarter, _, _ = rays_scr.shape
-    row_blocks = tiles * quarter
-    if len(notes) > 1:
-        norms = sum(ref[quarter] for ref in notes)[0:row_blocks]
-        for i, ref in enumerate(notes):
-            rays_scr[info[0, 2] ^ i] = ref[0:quarter]
+def arrange_kernel(own, norms, *refs):
+    refs = list(refs)
+    norms_out, measured = refs[-2:]
+    tiles = measured.shape[0] // (refs[0].shape[-1] // BS)
+    quarter = measured.shape[0] // tiles
+    norms_out[...] = norms[...]
+
+    def arrange(tile, ref, *where):
+        for i in range(quarter):
+            columns = slice(i * BS, (i + 1) * BS)
+            parts = [ref[where + (g, slice(None), columns)] for g in range(ref.shape[-3])]
+            measured[tile * quarter + i] = jnp.concatenate(parts, axis=0)
+
+    if len(refs) > 3:
+        for i, ref in enumerate(refs[:-2]):
+            arrange(own[0, 2] ^ i, ref)
     else:
-        norms = sum(notes[0][t, quarter] for t in range(tiles))[0:row_blocks]
-        rays_scr[...] = notes[0][:, 0:quarter]
-    scale = relaxation / norms
+        for t in range(tiles):
+            arrange(t, refs[0], t)
+
+
+def scale_rays(norms, measured, rays):
+    row_blocks = measured.shape[0]
+    if len(norms) > 1:
+        total = sum(ref[...] for ref in norms)
+    else:
+        total = sum(norms[0][t] for t in range(norms[0].shape[0]))
+    scale = relaxation / total
     for r in range(row_blocks):
         row = scale[r : r + 1]
-        rays[r] = rays_scr[r // quarter, r % quarter] * row
+        rays[r] = measured[r] * row
         rays[row_blocks, r : r + 1] = row
 
 
@@ -174,9 +186,9 @@
     refs = list(refs)
     info, wide = take(refs, 2)
     if n_notes:
-        notes, terms_in = take(refs, n_notes), []
-        change, rays, w_scr, rays_scr = refs
-        gather_rays(info, notes, rays, rays_scr)
+        norms, measured, terms_in = take(refs, n_notes), take(refs, 1)[0], []
+        change, rays, w_scr = refs
+        scale_rays(norms, measured, rays)
     else:
         (rays,) = take(refs, 1)
         terms_in = take(refs, n_terms)
@@ -261,7 +273,6 @@
     final_out = jax.ShapeDtypeStruct((batches, per_batch, PIX), jnp.bfloat16)
     w_scr = pltpu.VMEM((row_blocks, slices, BS), jnp.bfloat16)
     x_scr = pltpu.VMEM(image_shape, jnp.float32)
-    rays_scr = pltpu.VMEM((tiles, quarter, slices, BS), jnp.float32)
 
     def sent(value, target):
         pairs = []
@@ -304,25 +315,25 @@
             name=name,
         )(*operands)
 
+    measured = spread(sinogram)
     blocks2 = swapped(blocks)
     chunks = 8 if count % 8 == 0 else 1
-    note, table, own, blocks = pl.pallas_call(
+    norms, table, own, blocks = pl.pallas_call(
         functools.partial(head_kernel, row_blocks, chunks),
         out_shape=(
-            jax.ShapeDtypeStruct((quarter + 1, slices, BS), jnp.float32),
+            jax.ShapeDtypeStruct((row_blocks, BS), jnp.float32),
             jax.ShapeDtypeStruct((2, count), jnp.int32),
             pltpu.SMEM((3, count), jnp.int32),
             pltpu.VMEM(blocks.shape, blocks.dtype),
         ),
-        in_specs=[SMEM] + [pl.BlockSpec(memory_space=pltpu.HBM)] * 4,
+        in_specs=[SMEM] + [pl.BlockSpec(memory_space=pltpu.HBM)] * 3,
         out_specs=(VMEM, SMEM, SMEM, VMEM),
         scratch_shapes=[
             pltpu.SMEM(block_rows.shape, jnp.int32),
             pltpu.SMEM(block_cols.shape, jnp.int32),
-            pltpu.VMEM(sinogram.shape, jnp.float32),
             pltpu.SMEM((row_blocks,), jnp.int32),
             pltpu.VMEM((row_blocks, BS, BS), jnp.float32),
-            pltpu.SemaphoreType.DMA((3 + chunks,)),
+            pltpu.SemaphoreType.DMA((2 + chunks,)),
         ],
         compiler_params=PARAMS,
         name="head",
@@ -330,10 +341,21 @@
         pos,
         *(
             pltpu.with_memory_space_constraint(value, pltpu.HBM)
-            for value in (block_rows, block_cols, blocks, sinogram)
+            for value in (block_rows, block_cols, blocks)
         ),
     )
-    notes = spread(note)
+    norms, measured = call(
+        arrange_kernel,
+        1,
+        [pltpu.with_memory_space_constraint(own, pltpu.SMEM), norms] + measured,
+        (
+            jax.ShapeDtypeStruct(norms.shape, norms.dtype),
+            jax.ShapeDtypeStruct((row_blocks, slices, BS), jnp.float32),
+        ),
+        [],
+        "arrange",
+    )
+    every = spread(norms)
     table2 = swapped(table)
 
     own = pltpu.with_memory_space_constraint(own, pltpu.SMEM)
@@ -345,7 +367,7 @@
         out_specs=VMEM,
         compiler_params=PARAMS,
         name="pack_own",
-    )(own, blocks, note)
+    )(own, blocks, norms)
     info, tall = pl.pallas_call(
         pack_other_kernel,
         out_shape=(
@@ -378,11 +400,11 @@
         last = place == places - 1
         if place == 0:
             change, rays = call(
-                functools.partial(update_kernel, place, 0, len(notes), 0),
+                functools.partial(update_kernel, place, 0, len(every), 0),
                 1,
-                [info, wide] + notes,
+                [info, wide] + every + [measured],
                 (change_out, rays_out),
-                [w_scr, rays_scr],
+                [w_scr],
                 "update",
                 UPDATE_FLOPS,
             )

time: 75.6 us -> 79 us (1.045)
  starting transfers between devices: 30.9 us -> 34.9 us
    ppermute x43 -> x46, starting transfers between devices: 30.9 us -> 34.9 us  [sent(): return lax.ppermute(value, ('subset', 'tile'), pairs)]
    ppermute x43 -> x46, waiting for transfers between devices: 37.2 us -> 36.5 us  [sent(): return lax.ppermute(value, ('subset', 'tile'), pairs)]
    pallas_call x19 -> x20, Pallas kernels: 2.15 us -> 2.17 us  [call(): pl.pallas_call(kernel, out_shape=out_shape, in_specs=[SMEM] * smem + [VME...]
  transfers between devices with their start and end apart: 43 -> 46, of which waited for: 20 -> 19; matrix products, arithmetic and copies ran while one was open for 0% -> 0% of each run, Pallas kernels for 7% -> 7%
where the time goes in v12:
time: 79 us; the launch traced here: 78.8 us
  waiting for transfers between devices  36.5 us (46%)
  starting transfers between devices  34.9 us (44%)
  Pallas kernels  7.02 us (9%)
    ppermute x46, waiting for transfers between devices, sent(): return lax.ppermute(value, ('subset', 'tile'), pairs)  36.5 us
    ppermute x46, starting transfers between devices, sent(): return lax.ppermute(value, ('subset', 'tile'), pairs)  34.9 us
    pallas_call x1, Pallas kernels, per_device(): pl.pallas_call(functools.partial(head_kernel, row_blocks, chunks), out_sh...  3.05 us
    pallas_call x20, Pallas kernels, call(): pl.pallas_call(kernel, out_shape=out_shape, in_specs=[SMEM] * smem + [VME...  2.17 us
  transfers between devices with their start and end apart: 46, of which 19 were waited for; matrix products, arithmetic and copies ran while one was open for 0% of the time, Pallas kernels for 7%

profile of v12, /device:TPU:25, one launch (start us, length us, event | category | flops | bytes accessed | tf_op | source)
XLA Modules:
  0.0 78.8 jit_solution(360994076847824979)
XLA Ops:
  0.0 0.7 collective-permute-start.1
  0.7 1.2 %collective-permute-start.3 = (f32[4,8,512]{2,1,0:T(8,128)}, f32[4,8,512]{2,1,0:T(8,128)S(1)}, u32[]{:S(2)}, u32[]{:S(2)}) collective-permute-start(f32[4,8,512]{2,1,0:T(8,128)} %refs_0_.1), channel_id=1, source_target_pairs={{0,2},{1,3},{2,0},{3,1},{4,6},{5,7},{6,4},{7,5},{8,10},{9,11},{10,... | collective-permute-start | bytes 196616 | tf_op jit(solution)/shard_map/ppermute | solution.py:284
  1.9 1.2 %collective-permute-start.2 = (f32[4,8,512]{2,1,0:T(8,128)}, f32[4,8,512]{2,1,0:T(8,128)S(1)}, u32[]{:S(2)}, u32[]{:S(2)}) collective-permute-start(f32[4,8,512]{2,1,0:T(8,128)} %refs_0_.1), channel_id=1, source_target_pairs={{0,1},{1,0},{2,3},{3,2},{4,5},{5,4},{6,7},{7,6},{8,9},{9,8},{10,11... | collective-permute-start | bytes 196616 | tf_op jit(solution)/shard_map/ppermute | solution.py:284
  3.4 3.1 %head.1 = (f32[16,128]{1,0:T(8,128)S(1)}, s32[2,80]{1,0:T(2,128)S(1)}, s32[3,80]{1,0:T(4,128)S(4)}, bf16[1,1,80,128,128]{4,3,2,1,0:T(8,128)(2,1)S(1)}) custom-call(s32[3]{0:T(128)S(1)} %pad_add_fusion.pos, s32[1,1,80]{2,1,0:T(1,128)} %rows_in.1, s32[1,1,80]{2,1,0:T(1,128)} %cols_in.1, bf16[1,1,80,128,128]{4,3,2,1,0:T(8,128)(2,1)} %blocks_in.1), custom_call_target="tpu_custom_call" | custom-call | tf_op jit(solution)/shard_map/head/pallas_call | solution.py:321
  6.5 0.9 %collective-permute-done.4.refs_3_ = f32[4,8,512]{2,1,0:T(8,128)S(1)} collective-permute-done((f32[4,8,512]{2,1,0:T(8,128)}, f32[4,8,512]{2,1,0:T(8,128)S(1)}, u32[]{:S(2)}, u32[]{:S(2)}) %collective-permute-start.4) | collective-permute-done | bytes 65568 | tf_op jit(solution)/shard_map/ppermute | solution.py:284
  7.4 1.4 %collective-permute-start.7 = (f32[16,128]{1,0:T(8,128)S(1)}, f32[16,128]{1,0:T(8,128)S(1)}, u32[]{:S(2)}, u32[]{:S(2)}) collective-permute-start(f32[16,128]{1,0:T(8,128)S(1)} %get-tuple-element.34._.refs_2_), channel_id=1, source_target_pairs={{0,3},{1,2},{2,1},{3,0},{4,7},{5,6},{6,5},{7,4},{8,11},{9,10},{10,... | collective-permute-start | bytes 24584 | tf_op jit(solution)/shard_map/ppermute | solution.py:284
  8.8 0.4 collective-permute-start.6
  9.2 0.9 %collective-permute-start.5 = (f32[16,128]{1,0:T(8,128)S(1)}, f32[16,128]{1,0:T(8,128)S(1)}, u32[]{:S(2)}, u32[]{:S(2)}) collective-permute-start(f32[16,128]{1,0:T(8,128)S(1)} %get-tuple-element.34._.refs_2_), channel_id=1, source_target_pairs={{0,1},{1,0},{2,3},{3,2},{4,5},{5,4},{6,7},{7,6},{8,9},{9,8},{10,11... | collective-permute-start | bytes 24584 | tf_op jit(solution)/shard_map/ppermute | solution.py:284
  10.1 2.6 %collective-permute-start = (s32[2,80]{1,0:T(2,128)S(1)}, s32[2,80]{1,0:T(2,128)S(1)}, u32[]{:S(2)}, u32[]{:S(2)}) collective-permute-start(s32[2,80]{1,0:T(2,128)S(1)} %get-tuple-element.30), channel_id=1, source_target_pairs={{0,4},{1,5},{2,6},{3,7},{4,0},{5,1},{6,2},{7,3},{8,12},{9,13},{10,... | collective-permute-start | bytes 1928 | tf_op jit(solution)/shard_map/ppermute | solution.py:284
  12.7 0.5 pack_own.1.refs_1_
  13.5 1.3 %pack_other.1 = (s32[3,80]{1,0:T(4,128)S(4)}, bf16[16,640,128]{2,1,0:T(8,128)(2,1)S(1)}) custom-call(s32[3,80]{1,0:T(4,128)S(4)} %get-tuple-element.29.own, s32[2,80]{1,0:T(2,128)S(1)} %collective-permute-done.table2, bf16[1,1,80,128,128]{4,3,2,1,0:T(8,128)(2,1)S(1)} %collective-permute-done.1.blocks2), custom_call_target="tpu_custom_call" | custom-call | tf_op jit(solution)/shard_map/pack_other/pallas_call | solution.py:371
  15.3 1.1 %collective-permute-start.10 = (bf16[16,32,128]{2,1,0:T(8,128)(2,1)S(1)}, bf16[16,32,128]{2,1,0:T(8,128)(2,1)S(1)}, u32[]{:S(2)}, u32[]{:S(2)}) collective-permute-start(bf16[16,32,128]{2,1,0:T(8,128)(2,1)S(1)} %get-tuple-element.39), channel_id=1, source_target_pairs={{0,6},{1,7},{2,4},{3,5},{4,0},{5,1},{6,2},{7,3},{8,14},{9,15},{10,... | collective-permute-start | bytes 393224 | tf_op jit(solution)/shard_map/ppermute | solution.py:284
  16.4 0.8 collective-permute-start.8
  17.2 3.2 %collective-permute-done.11.refs_6_ = bf16[16,32,128]{2,1,0:T(8,128)(2,1)S(1)} collective-permute-done((bf16[16,32,128]{2,1,0:T(8,128)(2,1)S(1)}, bf16[16,32,128]{2,1,0:T(8,128)(2,1)S(1)}, u32[]{:S(2)}, u32[]{:S(2)}) %collective-permute-start.11) | collective-permute-done | bytes 131104 | tf_op jit(solution)/shard_map/ppermute | solution.py:284
  20.4 0.7 collective-permute-done.10.refs_5_
  21.4 5.1 %collective-permute-done.13.image = bf16[32,32,128]{2,1,0:T(8,128)(2,1)S(1)} collective-permute-done((bf16[32,32,128]{2,1,0:T(8,128)(2,1)S(1)}, bf16[32,32,128]{2,1,0:T(8,128)(2,1)S(1)}, u32[]{:S(2)}, u32[]{:S(2)}) %collective-permute-start.13) | collective-permute-done | bytes 262176 | tf_op jit(solution)/shard_map/ppermute | solution.py:284
  26.5 1.6 %collective-permute-start.17 = (bf16[16,32,128]{2,1,0:T(8,128)(2,1)S(1)}, bf16[16,32,128]{2,1,0:T(8,128)(2,1)S(1)}, u32[]{:S(2)}, u32[]{:S(2)}) collective-permute-start(bf16[16,32,128]{2,1,0:T(8,128)(2,1)S(1)} %project.3), channel_id=1, source_target_pairs={{0,4},{1,5},{2,6},{3,7},{4,3},{5,2},{6,1},{7,0},{8,12},{9,13},{10,... | collective-permute-start | bytes 393224 | tf_op jit(solution)/shard_map/ppermute | solution.py:284
  28.1 1.0 %collective-permute-start.15 = (bf16[16,32,128]{2,1,0:T(8,128)(2,1)S(1)}, bf16[16,32,128]{2,1,0:T(8,128)(2,1)S(1)}, u32[]{:S(2)}, u32[]{:S(2)}) collective-permute-start(bf16[16,32,128]{2,1,0:T(8,128)(2,1)S(1)} %project.3), channel_id=1, source_target_pairs={{0,4},{1,5},{2,6},{3,7},{4,1},{5,0},{6,3},{7,2},{8,12},{9,13},{10,... | collective-permute-start | bytes 393224 | tf_op jit(solution)/shard_map/ppermute | solution.py:284
  29.0 0.5 collective-permute-start.18
  29.6 0.5 collective-permute-done.17.refs_6_
  30.0 1.4 %collective-permute-done.16.refs_5_ = bf16[16,32,128]{2,1,0:T(8,128)(2,1)S(1)} collective-permute-done((bf16[16,32,128]{2,1,0:T(8,128)(2,1)S(1)}, bf16[16,32,128]{2,1,0:T(8,128)(2,1)S(1)}, u32[]{:S(2)}, u32[]{:S(2)}) %collective-permute-start.16) | collective-permute-done | bytes 131104 | tf_op jit(solution)/shard_map/ppermute | solution.py:284
  31.4 1.8 %collective-permute-start.22 = (bf16[16,32,128]{2,1,0:T(8,128)(2,1)S(1)}, bf16[16,32,128]{2,1,0:T(8,128)(2,1)S(1)}, u32[]{:S(2)}, u32[]{:S(2)}) collective-permute-start(bf16[16,32,128]{2,1,0:T(8,128)(2,1)S(1)} %get-tuple-element.42), channel_id=1, source_target_pairs={{0,7},{1,6},{2,5},{3,4},{4,0},{5,1},{6,2},{7,3},{8,15},{9,14},{10,... | collective-permute-start | bytes 393224 | tf_op jit(solution)/shard_map/ppermute | solution.py:284
  33.3 1.2 %collective-permute-start.20 = (bf16[16,32,128]{2,1,0:T(8,128)(2,1)S(1)}, bf16[16,32,128]{2,1,0:T(8,128)(2,1)S(1)}, u32[]{:S(2)}, u32[]{:S(2)}) collective-permute-start(bf16[16,32,128]{2,1,0:T(8,128)(2,1)S(1)} %get-tuple-element.42), channel_id=1, source_target_pairs={{0,5},{1,4},{2,7},{3,6},{4,0},{5,1},{6,2},{7,3},{8,13},{9,12},{10,... | collective-permute-start | bytes 393224 | tf_op jit(solution)/shard_map/ppermute | solution.py:284
  34.5 0.4 collective-permute-start.23
  35.0 2.0 %collective-permute-done.22.refs_6_ = bf16[16,32,128]{2,1,0:T(8,128)(2,1)S(1)} collective-permute-done((bf16[16,32,128]{2,1,0:T(8,128)(2,1)S(1)}, bf16[16,32,128]{2,1,0:T(8,128)(2,1)S(1)}, u32[]{:S(2)}, u32[]{:S(2)}) %collective-permute-start.22) | collective-permute-done | bytes 131104 | tf_op jit(solution)/shard_map/ppermute | solution.py:284
  37.0 1.3 %collective-permute-done.21.refs_5_ = bf16[16,32,128]{2,1,0:T(8,128)(2,1)S(1)} collective-permute-done((bf16[16,32,128]{2,1,0:T(8,128)(2,1)S(1)}, bf16[16,32,128]{2,1,0:T(8,128)(2,1)S(1)}, u32[]{:S(2)}, u32[]{:S(2)}) %collective-permute-start.21) | collective-permute-done | bytes 131104 | tf_op jit(solution)/shard_map/ppermute | solution.py:284
  38.4 0.8 %collective-permute-start.24 = (bf16[32,32,128]{2,1,0:T(8,128)(2,1)S(1)}, bf16[32,32,128]{2,1,0:T(8,128)(2,1)S(1)}, u32[]{:S(2)}, u32[]{:S(2)}) collective-permute-start(bf16[32,32,128]{2,1,0:T(8,128)(2,1)S(1)} %get-tuple-element.45), channel_id=1, source_target_pairs={{0,1},{1,0},{2,3},{3,2},{4,28},{5,29},{6,30},{7,31},{8,9},{9,8},{1... | collective-permute-start | bytes 786440 | tf_op jit(solution)/shard_map/ppermute | solution.py:284
  39.2 6.4 %collective-permute-done.24.image = bf16[32,32,128]{2,1,0:T(8,128)(2,1)S(1)} collective-permute-done((bf16[32,32,128]{2,1,0:T(8,128)(2,1)S(1)}, bf16[32,32,128]{2,1,0:T(8,128)(2,1)S(1)}, u32[]{:S(2)}, u32[]{:S(2)}) %collective-permute-start.24) | collective-permute-done | bytes 262176 | tf_op jit(solution)/shard_map/ppermute | solution.py:284
  45.6 1.3 %collective-permute-start.27 = (bf16[16,32,128]{2,1,0:T(8,128)(2,1)S(1)}, bf16[16,32,128]{2,1,0:T(8,128)(2,1)S(1)}, u32[]{:S(2)}, u32[]{:S(2)}) collective-permute-start(bf16[16,32,128]{2,1,0:T(8,128)(2,1)S(1)} %project.4), channel_id=1, source_target_pairs={{0,4},{1,5},{2,6},{3,7},{4,2},{5,3},{6,0},{7,1},{8,12},{9,13},{10,... | collective-permute-start | bytes 393224 | tf_op jit(solution)/shard_map/ppermute | solution.py:284
  46.9 0.5 collective-permute-start.25
  47.5 2.0 %collective-permute-done.27.refs_5_ = bf16[16,32,128]{2,1,0:T(8,128)(2,1)S(1)} collective-permute-done((bf16[16,32,128]{2,1,0:T(8,128)(2,1)S(1)}, bf16[16,32,128]{2,1,0:T(8,128)(2,1)S(1)}, u32[]{:S(2)}, u32[]{:S(2)}) %collective-permute-start.27) | collective-permute-done | bytes 131104 | tf_op jit(solution)/shard_map/ppermute | solution.py:284
  49.5 1.8 %collective-permute-start.33 = (bf16[16,32,128]{2,1,0:T(8,128)(2,1)S(1)}, bf16[16,32,128]{2,1,0:T(8,128)(2,1)S(1)}, u32[]{:S(2)}, u32[]{:S(2)}) collective-permute-start(bf16[16,32,128]{2,1,0:T(8,128)(2,1)S(1)} %get-tuple-element.46), channel_id=1, source_target_pairs={{0,7},{1,6},{2,5},{3,4},{4,0},{5,1},{6,2},{7,3},{8,15},{9,14},{10,... | collective-permute-start | bytes 393224 | tf_op jit(solution)/shard_map/ppermute | solution.py:284
  51.4 1.2 %collective-permute-start.31 = (bf16[16,32,128]{2,1,0:T(8,128)(2,1)S(1)}, bf16[16,32,128]{2,1,0:T(8,128)(2,1)S(1)}, u32[]{:S(2)}, u32[]{:S(2)}) collective-permute-start(bf16[16,32,128]{2,1,0:T(8,128)(2,1)S(1)} %get-tuple-element.46), channel_id=1, source_target_pairs={{0,5},{1,4},{2,7},{3,6},{4,0},{5,1},{6,2},{7,3},{8,13},{9,12},{10,... | collective-permute-start | bytes 393224 | tf_op jit(solution)/shard_map/ppermute | solution.py:284
  52.7 0.4 collective-permute-start.34
  53.1 2.0 %collective-permute-done.33.refs_6_ = bf16[16,32,128]{2,1,0:T(8,128)(2,1)S(1)} collective-permute-done((bf16[16,32,128]{2,1,0:T(8,128)(2,1)S(1)}, bf16[16,32,128]{2,1,0:T(8,128)(2,1)S(1)}, u32[]{:S(2)}, u32[]{:S(2)}) %collective-permute-start.33) | collective-permute-done | bytes 131104 | tf_op jit(solution)/shard_map/ppermute | solution.py:284
  55.1 1.3 %collective-permute-done.32.refs_5_ = bf16[16,32,128]{2,1,0:T(8,128)(2,1)S(1)} collective-permute-done((bf16[16,32,128]{2,1,0:T(8,128)(2,1)S(1)}, bf16[16,32,128]{2,1,0:T(8,128)(2,1)S(1)}, u32[]{:S(2)}, u32[]{:S(2)}) %collective-permute-start.32) | collective-permute-done | bytes 131104 | tf_op jit(solution)/shard_map/ppermute | solution.py:284
  56.5 4.5 %collective-permute-start.35 = (bf16[32,32,128]{2,1,0:T(8,128)(2,1)S(1)}, bf16[32,32,128]{2,1,0:T(8,128)(2,1)S(1)}, u32[]{:S(2)}, u32[]{:S(2)}) collective-permute-start(bf16[32,32,128]{2,1,0:T(8,128)(2,1)S(1)} %get-tuple-element.49), channel_id=1, source_target_pairs={{0,1},{1,0},{2,3},{3,2},{4,12},{5,13},{6,14},{7,15},{8,9},{9,8},{1... | collective-permute-start | bytes 786440 | tf_op jit(solution)/shard_map/ppermute | solution.py:284
  61.0 3.8 %collective-permute-done.35.image = bf16[32,32,128]{2,1,0:T(8,128)(2,1)S(1)} collective-permute-done((bf16[32,32,128]{2,1,0:T(8,128)(2,1)S(1)}, bf16[32,32,128]{2,1,0:T(8,128)(2,1)S(1)}, u32[]{:S(2)}, u32[]{:S(2)}) %collective-permute-start.35) | collective-permute-done | bytes 262176 | tf_op jit(solution)/shard_map/ppermute | solution.py:284
  64.8 0.5 project.5
  65.4 1.0 %collective-permute-start.38 = (bf16[16,32,128]{2,1,0:T(8,128)(2,1)S(1)}, bf16[16,32,128]{2,1,0:T(8,128)(2,1)S(1)}, u32[]{:S(2)}, u32[]{:S(2)}) collective-permute-start(bf16[16,32,128]{2,1,0:T(8,128)(2,1)S(1)} %project.5), channel_id=1, source_target_pairs={{0,4},{1,5},{2,6},{3,7},{4,2},{5,3},{6,0},{7,1},{8,12},{9,13},{10,... | collective-permute-start | bytes 393224 | tf_op jit(solution)/shard_map/ppermute | solution.py:284
  67.3 1.9 %collective-permute-done.38.refs_5_ = bf16[16,32,128]{2,1,0:T(8,128)(2,1)S(1)} collective-permute-done((bf16[16,32,128]{2,1,0:T(8,128)(2,1)S(1)}, bf16[16,32,128]{2,1,0:T(8,128)(2,1)S(1)}, u32[]{:S(2)}, u32[]{:S(2)}) %collective-permute-start.38) | collective-permute-done | bytes 131104 | tf_op jit(solution)/shard_map/ppermute | solution.py:284
  69.2 3.0 %collective-permute-start.44 = (bf16[16,32,128]{2,1,0:T(8,128)(2,1)S(1)}, bf16[16,32,128]{2,1,0:T(8,128)(2,1)S(1)}, u32[]{:S(2)}, u32[]{:S(2)}) collective-permute-start(bf16[16,32,128]{2,1,0:T(8,128)(2,1)S(1)} %get-tuple-element.50), channel_id=1, source_target_pairs={{0,7},{1,6},{2,5},{3,4},{4,0},{5,1},{6,2},{7,3},{8,15},{9,14},{10,... | collective-permute-start | bytes 393224 | tf_op jit(solution)/shard_map/ppermute | solution.py:284
  72.3 1.2 %collective-permute-start.42 = (bf16[16,32,128]{2,1,0:T(8,128)(2,1)S(1)}, bf16[16,32,128]{2,1,0:T(8,128)(2,1)S(1)}, u32[]{:S(2)}, u32[]{:S(2)}) collective-permute-start(bf16[16,32,128]{2,1,0:T(8,128)(2,1)S(1)} %get-tuple-element.50), channel_id=1, source_target_pairs={{0,5},{1,4},{2,7},{3,6},{4,0},{5,1},{6,2},{7,3},{8,13},{9,12},{10,... | collective-permute-start | bytes 393224 | tf_op jit(solution)/shard_map/ppermute | solution.py:284
  73.5 0.5 collective-permute-start.45
  74.0 2.1 %collective-permute-done.44.refs_6_ = bf16[16,32,128]{2,1,0:T(8,128)(2,1)S(1)} collective-permute-done((bf16[16,32,128]{2,1,0:T(8,128)(2,1)S(1)}, bf16[16,32,128]{2,1,0:T(8,128)(2,1)S(1)}, u32[]{:S(2)}, u32[]{:S(2)}) %collective-permute-start.44) | collective-permute-done | bytes 131104 | tf_op jit(solution)/shard_map/ppermute | solution.py:284
  76.1 1.3 %collective-permute-done.43.refs_5_ = bf16[16,32,128]{2,1,0:T(8,128)(2,1)S(1)} collective-permute-done((bf16[16,32,128]{2,1,0:T(8,128)(2,1)S(1)}, bf16[16,32,128]{2,1,0:T(8,128)(2,1)S(1)}, u32[]{:S(2)}, u32[]{:S(2)}) %collective-permute-start.43) | collective-permute-done | bytes 131104 | tf_op jit(solution)/shard_map/ppermute | solution.py:284
  77.4 0.6 update.15.refs_1_
  78.0 0.8 second.7
  (70 shorter events, 3.2 us)
Async XLA Ops:
  0.0 7.4 %copy-start = (f32[4,8,512]{2,1,0:T(8,128)S(1)}, f32[4,8,512]{2,1,0:T(8,128)}, u32[]{:S(2)}) copy-start(f32[4,8,512]{2,1,0:T(8,128)} %refs_0_.1) | copy-start | bytes 196612
  0.0 13.5 %collective-permute-start.1 = (bf16[1,1,80,128,128]{4,3,2,1,0:T(8,128)(2,1)}, bf16[1,1,80,128,128]{4,3,2,1,0:T(8,128)(2,1)S(1)}, u32[]{:S(2)}, u32[]{:S(2)}) collective-permute-start(bf16[1,1,80,128,128]{4,3,2,1,0:T(8,128)(2,1)} %blocks_in.1), channel_id=1, source_target_pairs={{0,4},{1,5},{2,6},{3,7},{4,0},{5,1},{6,2},{7,3},{8,12},{9,13},{10,... | collective-permute-start | bytes 7864328 | tf_op jit(solution)/shard_map/ppermute | solution.py:284
  0.7 5.8 %collective-permute-start.3 = (f32[4,8,512]{2,1,0:T(8,128)}, f32[4,8,512]{2,1,0:T(8,128)S(1)}, u32[]{:S(2)}, u32[]{:S(2)}) collective-permute-start(f32[4,8,512]{2,1,0:T(8,128)} %refs_0_.1), channel_id=1, source_target_pairs={{0,2},{1,3},{2,0},{3,1},{4,6},{5,7},{6,4},{7,5},{8,10},{9,11},{10,... | collective-permute-start | bytes 196616 | tf_op jit(solution)/shard_map/ppermute | solution.py:284
  1.9 4.6 %collective-permute-start.2 = (f32[4,8,512]{2,1,0:T(8,128)}, f32[4,8,512]{2,1,0:T(8,128)S(1)}, u32[]{:S(2)}, u32[]{:S(2)}) collective-permute-start(f32[4,8,512]{2,1,0:T(8,128)} %refs_0_.1), channel_id=1, source_target_pairs={{0,1},{1,0},{2,3},{3,2},{4,5},{5,4},{6,7},{7,6},{8,9},{9,8},{10,11... | collective-permute-start | bytes 196616 | tf_op jit(solution)/shard_map/ppermute | solution.py:284
  3.1 4.2 %collective-permute-start.4 = (f32[4,8,512]{2,1,0:T(8,128)}, f32[4,8,512]{2,1,0:T(8,128)S(1)}, u32[]{:S(2)}, u32[]{:S(2)}) collective-permute-start(f32[4,8,512]{2,1,0:T(8,128)} %refs_0_.1), channel_id=1, source_target_pairs={{0,3},{1,2},{2,1},{3,0},{4,7},{5,6},{6,5},{7,4},{8,11},{9,10},{10,... | collective-permute-start | bytes 196616 | tf_op jit(solution)/shard_map/ppermute | solution.py:284
  7.4 7.5 %collective-permute-start.7 = (f32[16,128]{1,0:T(8,128)S(1)}, f32[16,128]{1,0:T(8,128)S(1)}, u32[]{:S(2)}, u32[]{:S(2)}) collective-permute-start(f32[16,128]{1,0:T(8,128)S(1)} %get-tuple-element.34._.refs_2_), channel_id=1, source_target_pairs={{0,3},{1,2},{2,1},{3,0},{4,7},{5,6},{6,5},{7,4},{8,11},{9,10},{10,... | collective-permute-start | bytes 24584 | tf_op jit(solution)/shard_map/ppermute | solution.py:284
  8.8 6.1 %collective-permute-start.6 = (f32[16,128]{1,0:T(8,128)S(1)}, f32[16,128]{1,0:T(8,128)S(1)}, u32[]{:S(2)}, u32[]{:S(2)}) collective-permute-start(f32[16,128]{1,0:T(8,128)S(1)} %get-tuple-element.34._.refs_2_), channel_id=1, source_target_pairs={{0,2},{1,3},{2,0},{3,1},{4,6},{5,7},{6,4},{7,5},{8,10},{9,11},{10,... | collective-permute-start | bytes 24584 | tf_op jit(solution)/shard_map/ppermute | solution.py:284
  9.2 5.7 %collective-permute-start.5 = (f32[16,128]{1,0:T(8,128)S(1)}, f32[16,128]{1,0:T(8,128)S(1)}, u32[]{:S(2)}, u32[]{:S(2)}) collective-permute-start(f32[16,128]{1,0:T(8,128)S(1)} %get-tuple-element.34._.refs_2_), channel_id=1, source_target_pairs={{0,1},{1,0},{2,3},{3,2},{4,5},{5,4},{6,7},{7,6},{8,9},{9,8},{10,11... | collective-permute-start | bytes 24584 | tf_op jit(solution)/shard_map/ppermute | solution.py:284
  10.1 3.4 %collective-permute-start = (s32[2,80]{1,0:T(2,128)S(1)}, s32[2,80]{1,0:T(2,128)S(1)}, u32[]{:S(2)}, u32[]{:S(2)}) collective-permute-start(s32[2,80]{1,0:T(2,128)S(1)} %get-tuple-element.30), channel_id=1, source_target_pairs={{0,4},{1,5},{2,6},{3,7},{4,0},{5,1},{6,2},{7,3},{8,12},{9,13},{10,... | collective-permute-start | bytes 1928 | tf_op jit(solution)/shard_map/ppermute | solution.py:284
  15.0 5.5 %collective-permute-start.11 = (bf16[16,32,128]{2,1,0:T(8,128)(2,1)S(1)}, bf16[16,32,128]{2,1,0:T(8,128)(2,1)S(1)}, u32[]{:S(2)}, u32[]{:S(2)}) collective-permute-start(bf16[16,32,128]{2,1,0:T(8,128)(2,1)S(1)} %get-tuple-element.39), channel_id=1, source_target_pairs={{0,7},{1,6},{2,5},{3,4},{4,0},{5,1},{6,2},{7,3},{8,15},{9,14},{10,... | collective-permute-start | bytes 393224 | tf_op jit(solution)/shard_map/ppermute | solution.py:284
  15.3 5.8 %collective-permute-start.10 = (bf16[16,32,128]{2,1,0:T(8,128)(2,1)S(1)}, bf16[16,32,128]{2,1,0:T(8,128)(2,1)S(1)}, u32[]{:S(2)}, u32[]{:S(2)}) collective-permute-start(bf16[16,32,128]{2,1,0:T(8,128)(2,1)S(1)} %get-tuple-element.39), channel_id=1, source_target_pairs={{0,6},{1,7},{2,4},{3,5},{4,0},{5,1},{6,2},{7,3},{8,14},{9,15},{10,... | collective-permute-start | bytes 393224 | tf_op jit(solution)/shard_map/ppermute | solution.py:284
  16.4 4.7 %collective-permute-start.9 = (bf16[16,32,128]{2,1,0:T(8,128)(2,1)S(1)}, bf16[16,32,128]{2,1,0:T(8,128)(2,1)S(1)}, u32[]{:S(2)}, u32[]{:S(2)}) collective-permute-start(bf16[16,32,128]{2,1,0:T(8,128)(2,1)S(1)} %get-tuple-element.39), channel_id=1, source_target_pairs={{0,5},{1,4},{2,7},{3,6},{4,0},{5,1},{6,2},{7,3},{8,13},{9,12},{10,... | collective-permute-start | bytes 393224 | tf_op jit(solution)/shard_map/ppermute | solution.py:284
  16.4 4.7 %collective-permute-start.8 = (bf16[16,32,128]{2,1,0:T(8,128)(2,1)S(1)}, bf16[16,32,128]{2,1,0:T(8,128)(2,1)S(1)}, u32[]{:S(2)}, u32[]{:S(2)}) collective-permute-start(bf16[16,32,128]{2,1,0:T(8,128)(2,1)S(1)} %get-tuple-element.39), channel_id=1, source_target_pairs={{0,4},{1,5},{2,6},{3,7},{4,0},{5,1},{6,2},{7,3},{8,12},{9,13},{10,... | collective-permute-start | bytes 393224 | tf_op jit(solution)/shard_map/ppermute | solution.py:284
  17.2 3.9 %collective-permute-start.12 = (bf16[32,32,128]{2,1,0:T(8,128)(2,1)S(1)}, bf16[32,32,128]{2,1,0:T(8,128)(2,1)S(1)}, u32[]{:S(2)}, u32[]{:S(2)}) collective-permute-start(bf16[32,32,128]{2,1,0:T(8,128)(2,1)S(1)} %get-tuple-element.40.refs_3_), channel_id=1, source_target_pairs={{0,4},{1,5},{2,6},{3,7},{4,0},{5,1},{6,2},{7,3},{8,12},{9,13},{10,... | collective-permute-start | bytes 786440 | tf_op jit(solution)/shard_map/ppermute | solution.py:284
  21.2 5.3 %collective-permute-start.13 = (bf16[32,32,128]{2,1,0:T(8,128)(2,1)S(1)}, bf16[32,32,128]{2,1,0:T(8,128)(2,1)S(1)}, u32[]{:S(2)}, u32[]{:S(2)}) collective-permute-start(bf16[32,32,128]{2,1,0:T(8,128)(2,1)S(1)} %get-tuple-element.41), channel_id=1, source_target_pairs={{0,1},{1,0},{2,3},{3,2},{4,12},{5,13},{6,14},{7,15},{8,9},{9,8},{1... | collective-permute-start | bytes 786440 | tf_op jit(solution)/shard_map/ppermute | solution.py:284
  26.5 3.5 %collective-permute-start.17 = (bf16[16,32,128]{2,1,0:T(8,128)(2,1)S(1)}, bf16[16,32,128]{2,1,0:T(8,128)(2,1)S(1)}, u32[]{:S(2)}, u32[]{:S(2)}) collective-permute-start(bf16[16,32,128]{2,1,0:T(8,128)(2,1)S(1)} %project.3), channel_id=1, source_target_pairs={{0,4},{1,5},{2,6},{3,7},{4,3},{5,2},{6,1},{7,0},{8,12},{9,13},{10,... | collective-permute-start | bytes 393224 | tf_op jit(solution)/shard_map/ppermute | solution.py:284
  28.0 3.3 %collective-permute-start.16 = (bf16[16,32,128]{2,1,0:T(8,128)(2,1)S(1)}, bf16[16,32,128]{2,1,0:T(8,128)(2,1)S(1)}, u32[]{:S(2)}, u32[]{:S(2)}) collective-permute-start(bf16[16,32,128]{2,1,0:T(8,128)(2,1)S(1)} %project.3), channel_id=1, source_target_pairs={{0,4},{1,5},{2,6},{3,7},{4,2},{5,3},{6,0},{7,1},{8,12},{9,13},{10,... | collective-permute-start | bytes 393224 | tf_op jit(solution)/shard_map/ppermute | solution.py:284
  28.1 3.4 %collective-permute-start.15 = (bf16[16,32,128]{2,1,0:T(8,128)(2,1)S(1)}, bf16[16,32,128]{2,1,0:T(8,128)(2,1)S(1)}, u32[]{:S(2)}, u32[]{:S(2)}) collective-permute-start(bf16[16,32,128]{2,1,0:T(8,128)(2,1)S(1)} %project.3), channel_id=1, source_target_pairs={{0,4},{1,5},{2,6},{3,7},{4,1},{5,0},{6,3},{7,2},{8,12},{9,13},{10,... | collective-permute-start | bytes 393224 | tf_op jit(solution)/shard_map/ppermute | solution.py:284
  29.0 2.4 %collective-permute-start.14 = (bf16[16,32,128]{2,1,0:T(8,128)(2,1)S(1)}, bf16[16,32,128]{2,1,0:T(8,128)(2,1)S(1)}, u32[]{:S(2)}, u32[]{:S(2)}) collective-permute-start(bf16[16,32,128]{2,1,0:T(8,128)(2,1)S(1)} %project.3), channel_id=1, source_target_pairs={{0,4},{1,5},{2,6},{3,7},{4,0},{5,1},{6,2},{7,3},{8,12},{9,13},{10,... | collective-permute-start | bytes 393224 | tf_op jit(solution)/shard_map/ppermute | solution.py:284
  29.0 2.4 %collective-permute-start.18 = (bf16[32,32,128]{2,1,0:T(8,128)(2,1)S(1)}, bf16[32,32,128]{2,1,0:T(8,128)(2,1)S(1)}, u32[]{:S(2)}, u32[]{:S(2)}) collective-permute-start(bf16[32,32,128]{2,1,0:T(8,128)(2,1)S(1)} %collective-permute-done.13.image), channel_id=1, source_target_pairs={{0,4},{1,5},{2,6},{3,7},{4,0},{5,1},{6,2},{7,3},{8,12},{9,13},{10,... | collective-permute-start | bytes 786440 | tf_op jit(solution)/shard_map/ppermute | solution.py:284
  31.4 5.6 %collective-permute-start.22 = (bf16[16,32,128]{2,1,0:T(8,128)(2,1)S(1)}, bf16[16,32,128]{2,1,0:T(8,128)(2,1)S(1)}, u32[]{:S(2)}, u32[]{:S(2)}) collective-permute-start(bf16[16,32,128]{2,1,0:T(8,128)(2,1)S(1)} %get-tuple-element.42), channel_id=1, source_target_pairs={{0,7},{1,6},{2,5},{3,4},{4,0},{5,1},{6,2},{7,3},{8,15},{9,14},{10,... | collective-permute-start | bytes 393224 | tf_op jit(solution)/shard_map/ppermute | solution.py:284
  33.2 5.1 %collective-permute-start.21 = (bf16[16,32,128]{2,1,0:T(8,128)(2,1)S(1)}, bf16[16,32,128]{2,1,0:T(8,128)(2,1)S(1)}, u32[]{:S(2)}, u32[]{:S(2)}) collective-permute-start(bf16[16,32,128]{2,1,0:T(8,128)(2,1)S(1)} %get-tuple-element.42), channel_id=1, source_target_pairs={{0,6},{1,7},{2,4},{3,5},{4,0},{5,1},{6,2},{7,3},{8,14},{9,15},{10,... | collective-permute-start | bytes 393224 | tf_op jit(solution)/shard_map/ppermute | solution.py:284
  33.3 5.0 %collective-permute-start.20 = (bf16[16,32,128]{2,1,0:T(8,128)(2,1)S(1)}, bf16[16,32,128]{2,1,0:T(8,128)(2,1)S(1)}, u32[]{:S(2)}, u32[]{:S(2)}) collective-permute-start(bf16[16,32,128]{2,1,0:T(8,128)(2,1)S(1)} %get-tuple-element.42), channel_id=1, source_target_pairs={{0,5},{1,4},{2,7},{3,6},{4,0},{5,1},{6,2},{7,3},{8,13},{9,12},{10,... | collective-permute-start | bytes 393224 | tf_op jit(solution)/shard_map/ppermute | solution.py:284
  34.4 3.9 %collective-permute-start.19 = (bf16[16,32,128]{2,1,0:T(8,128)(2,1)S(1)}, bf16[16,32,128]{2,1,0:T(8,128)(2,1)S(1)}, u32[]{:S(2)}, u32[]{:S(2)}) collective-permute-start(bf16[16,32,128]{2,1,0:T(8,128)(2,1)S(1)} %get-tuple-element.42), channel_id=1, source_target_pairs={{0,4},{1,5},{2,6},{3,7},{4,0},{5,1},{6,2},{7,3},{8,12},{9,13},{10,... | collective-permute-start | bytes 393224 | tf_op jit(solution)/shard_map/ppermute | solution.py:284
  34.5 3.8 %collective-permute-start.23 = (bf16[32,32,128]{2,1,0:T(8,128)(2,1)S(1)}, bf16[32,32,128]{2,1,0:T(8,128)(2,1)S(1)}, u32[]{:S(2)}, u32[]{:S(2)}) collective-permute-start(bf16[32,32,128]{2,1,0:T(8,128)(2,1)S(1)} %get-tuple-element.43.refs_3_), channel_id=1, source_target_pairs={{0,4},{1,5},{2,6},{3,7},{4,0},{5,1},{6,2},{7,3},{8,12},{9,13},{10,... | collective-permute-start | bytes 786440 | tf_op jit(solution)/shard_map/ppermute | solution.py:284
  38.4 7.2 %collective-permute-start.24 = (bf16[32,32,128]{2,1,0:T(8,128)(2,1)S(1)}, bf16[32,32,128]{2,1,0:T(8,128)(2,1)S(1)}, u32[]{:S(2)}, u32[]{:S(2)}) collective-permute-start(bf16[32,32,128]{2,1,0:T(8,128)(2,1)S(1)} %get-tuple-element.45), channel_id=1, source_target_pairs={{0,1},{1,0},{2,3},{3,2},{4,28},{5,29},{6,30},{7,31},{8,9},{9,8},{1... | collective-permute-start | bytes 786440 | tf_op jit(solution)/shard_map/ppermute | solution.py:284
  45.6 2.0 %collective-permute-start.28 = (bf16[16,32,128]{2,1,0:T(8,128)(2,1)S(1)}, bf16[16,32,128]{2,1,0:T(8,128)(2,1)S(1)}, u32[]{:S(2)}, u32[]{:S(2)}) collective-permute-start(bf16[16,32,128]{2,1,0:T(8,128)(2,1)S(1)} %project.4), channel_id=1, source_target_pairs={{0,4},{1,5},{2,6},{3,7},{4,3},{5,2},{6,1},{7,0},{8,12},{9,13},{10,... | collective-permute-start | bytes 393224 | tf_op jit(solution)/shard_map/ppermute | solution.py:284
  45.6 3.9 %collective-permute-start.27 = (bf16[16,32,128]{2,1,0:T(8,128)(2,1)S(1)}, bf16[16,32,128]{2,1,0:T(8,128)(2,1)S(1)}, u32[]{:S(2)}, u32[]{:S(2)}) collective-permute-start(bf16[16,32,128]{2,1,0:T(8,128)(2,1)S(1)} %project.4), channel_id=1, source_target_pairs={{0,4},{1,5},{2,6},{3,7},{4,2},{5,3},{6,0},{7,1},{8,12},{9,13},{10,... | collective-permute-start | bytes 393224 | tf_op jit(solution)/shard_map/ppermute | solution.py:284
  46.9 2.6 %collective-permute-start.26 = (bf16[16,32,128]{2,1,0:T(8,128)(2,1)S(1)}, bf16[16,32,128]{2,1,0:T(8,128)(2,1)S(1)}, u32[]{:S(2)}, u32[]{:S(2)}) collective-permute-start(bf16[16,32,128]{2,1,0:T(8,128)(2,1)S(1)} %project.4), channel_id=1, source_target_pairs={{0,4},{1,5},{2,6},{3,7},{4,1},{5,0},{6,3},{7,2},{8,12},{9,13},{10,... | collective-permute-start | bytes 393224 | tf_op jit(solution)/shard_map/ppermute | solution.py:284
  46.9 2.6 %collective-permute-start.25 = (bf16[16,32,128]{2,1,0:T(8,128)(2,1)S(1)}, bf16[16,32,128]{2,1,0:T(8,128)(2,1)S(1)}, u32[]{:S(2)}, u32[]{:S(2)}) collective-permute-start(bf16[16,32,128]{2,1,0:T(8,128)(2,1)S(1)} %project.4), channel_id=1, source_target_pairs={{0,4},{1,5},{2,6},{3,7},{4,0},{5,1},{6,2},{7,3},{8,12},{9,13},{10,... | collective-permute-start | bytes 393224 | tf_op jit(solution)/shard_map/ppermute | solution.py:284
  47.4 2.1 %collective-permute-start.29 = (bf16[32,32,128]{2,1,0:T(8,128)(2,1)S(1)}, bf16[32,32,128]{2,1,0:T(8,128)(2,1)S(1)}, u32[]{:S(2)}, u32[]{:S(2)}) collective-permute-start(bf16[32,32,128]{2,1,0:T(8,128)(2,1)S(1)} %collective-permute-done.24.image), channel_id=1, source_target_pairs={{0,4},{1,5},{2,6},{3,7},{4,0},{5,1},{6,2},{7,3},{8,12},{9,13},{10,... | collective-permute-start | bytes 786440 | tf_op jit(solution)/shard_map/ppermute | solution.py:284
  49.5 5.6 %collective-permute-start.33 = (bf16[16,32,128]{2,1,0:T(8,128)(2,1)S(1)}, bf16[16,32,128]{2,1,0:T(8,128)(2,1)S(1)}, u32[]{:S(2)}, u32[]{:S(2)}) collective-permute-start(bf16[16,32,128]{2,1,0:T(8,128)(2,1)S(1)} %get-tuple-element.46), channel_id=1, source_target_pairs={{0,7},{1,6},{2,5},{3,4},{4,0},{5,1},{6,2},{7,3},{8,15},{9,14},{10,... | collective-permute-start | bytes 393224 | tf_op jit(solution)/shard_map/ppermute | solution.py:284
  51.3 5.1 %collective-permute-start.32 = (bf16[16,32,128]{2,1,0:T(8,128)(2,1)S(1)}, bf16[16,32,128]{2,1,0:T(8,128)(2,1)S(1)}, u32[]{:S(2)}, u32[]{:S(2)}) collective-permute-start(bf16[16,32,128]{2,1,0:T(8,128)(2,1)S(1)} %get-tuple-element.46), channel_id=1, source_target_pairs={{0,6},{1,7},{2,4},{3,5},{4,0},{5,1},{6,2},{7,3},{8,14},{9,15},{10,... | collective-permute-start | bytes 393224 | tf_op jit(solution)/shard_map/ppermute | solution.py:284
  51.4 5.0 %collective-permute-start.31 = (bf16[16,32,128]{2,1,0:T(8,128)(2,1)S(1)}, bf16[16,32,128]{2,1,0:T(8,128)(2,1)S(1)}, u32[]{:S(2)}, u32[]{:S(2)}) collective-permute-start(bf16[16,32,128]{2,1,0:T(8,128)(2,1)S(1)} %get-tuple-element.46), channel_id=1, source_target_pairs={{0,5},{1,4},{2,7},{3,6},{4,0},{5,1},{6,2},{7,3},{8,13},{9,12},{10,... | collective-permute-start | bytes 393224 | tf_op jit(solution)/shard_map/ppermute | solution.py:284
  52.6 3.9 %collective-permute-start.30 = (bf16[16,32,128]{2,1,0:T(8,128)(2,1)S(1)}, bf16[16,32,128]{2,1,0:T(8,128)(2,1)S(1)}, u32[]{:S(2)}, u32[]{:S(2)}) collective-permute-start(bf16[16,32,128]{2,1,0:T(8,128)(2,1)S(1)} %get-tuple-element.46), channel_id=1, source_target_pairs={{0,4},{1,5},{2,6},{3,7},{4,0},{5,1},{6,2},{7,3},{8,12},{9,13},{10,... | collective-permute-start | bytes 393224 | tf_op jit(solution)/shard_map/ppermute | solution.py:284
  52.7 3.8 %collective-permute-start.34 = (bf16[32,32,128]{2,1,0:T(8,128)(2,1)S(1)}, bf16[32,32,128]{2,1,0:T(8,128)(2,1)S(1)}, u32[]{:S(2)}, u32[]{:S(2)}) collective-permute-start(bf16[32,32,128]{2,1,0:T(8,128)(2,1)S(1)} %get-tuple-element.47.refs_3_), channel_id=1, source_target_pairs={{0,4},{1,5},{2,6},{3,7},{4,0},{5,1},{6,2},{7,3},{8,12},{9,13},{10,... | collective-permute-start | bytes 786440 | tf_op jit(solution)/shard_map/ppermute | solution.py:284
  56.5 8.2 %collective-permute-start.35 = (bf16[32,32,128]{2,1,0:T(8,128)(2,1)S(1)}, bf16[32,32,128]{2,1,0:T(8,128)(2,1)S(1)}, u32[]{:S(2)}, u32[]{:S(2)}) collective-permute-start(bf16[32,32,128]{2,1,0:T(8,128)(2,1)S(1)} %get-tuple-element.49), channel_id=1, source_target_pairs={{0,1},{1,0},{2,3},{3,2},{4,12},{5,13},{6,14},{7,15},{8,9},{9,8},{1... | collective-permute-start | bytes 786440 | tf_op jit(solution)/shard_map/ppermute | solution.py:284
  65.3 2.0 %collective-permute-start.39 = (bf16[16,32,128]{2,1,0:T(8,128)(2,1)S(1)}, bf16[16,32,128]{2,1,0:T(8,128)(2,1)S(1)}, u32[]{:S(2)}, u32[]{:S(2)}) collective-permute-start(bf16[16,32,128]{2,1,0:T(8,128)(2,1)S(1)} %project.5), channel_id=1, source_target_pairs={{0,4},{1,5},{2,6},{3,7},{4,3},{5,2},{6,1},{7,0},{8,12},{9,13},{10,... | collective-permute-start | bytes 393224 | tf_op jit(solution)/shard_map/ppermute | solution.py:284
  65.4 3.8 %collective-permute-start.38 = (bf16[16,32,128]{2,1,0:T(8,128)(2,1)S(1)}, bf16[16,32,128]{2,1,0:T(8,128)(2,1)S(1)}, u32[]{:S(2)}, u32[]{:S(2)}) collective-permute-start(bf16[16,32,128]{2,1,0:T(8,128)(2,1)S(1)} %project.5), channel_id=1, source_target_pairs={{0,4},{1,5},{2,6},{3,7},{4,2},{5,3},{6,0},{7,1},{8,12},{9,13},{10,... | collective-permute-start | bytes 393224 | tf_op jit(solution)/shard_map/ppermute | solution.py:284
  66.4 2.8 %collective-permute-start.37 = (bf16[16,32,128]{2,1,0:T(8,128)(2,1)S(1)}, bf16[16,32,128]{2,1,0:T(8,128)(2,1)S(1)}, u32[]{:S(2)}, u32[]{:S(2)}) collective-permute-start(bf16[16,32,128]{2,1,0:T(8,128)(2,1)S(1)} %project.5), channel_id=1, source_target_pairs={{0,4},{1,5},{2,6},{3,7},{4,1},{5,0},{6,3},{7,2},{8,12},{9,13},{10,... | collective-permute-start | bytes 393224 | tf_op jit(solution)/shard_map/ppermute | solution.py:284
  66.6 2.6 %collective-permute-start.36 = (bf16[16,32,128]{2,1,0:T(8,128)(2,1)S(1)}, bf16[16,32,128]{2,1,0:T(8,128)(2,1)S(1)}, u32[]{:S(2)}, u32[]{:S(2)}) collective-permute-start(bf16[16,32,128]{2,1,0:T(8,128)(2,1)S(1)} %project.5), channel_id=1, source_target_pairs={{0,4},{1,5},{2,6},{3,7},{4,0},{5,1},{6,2},{7,3},{8,12},{9,13},{10,... | collective-permute-start | bytes 393224 | tf_op jit(solution)/shard_map/ppermute | solution.py:284
  66.9 2.3 %collective-permute-start.40 = (bf16[32,32,128]{2,1,0:T(8,128)(2,1)S(1)}, bf16[32,32,128]{2,1,0:T(8,128)(2,1)S(1)}, u32[]{:S(2)}, u32[]{:S(2)}) collective-permute-start(bf16[32,32,128]{2,1,0:T(8,128)(2,1)S(1)} %collective-permute-done.35.image), channel_id=1, source_target_pairs={{0,4},{1,5},{2,6},{3,7},{4,0},{5,1},{6,2},{7,3},{8,12},{9,13},{10,... | collective-permute-start | bytes 786440 | tf_op jit(solution)/shard_map/ppermute | solution.py:284
  69.2 6.9 %collective-permute-start.44 = (bf16[16,32,128]{2,1,0:T(8,128)(2,1)S(1)}, bf16[16,32,128]{2,1,0:T(8,128)(2,1)S(1)}, u32[]{:S(2)}, u32[]{:S(2)}) collective-permute-start(bf16[16,32,128]{2,1,0:T(8,128)(2,1)S(1)} %get-tuple-element.50), channel_id=1, source_target_pairs={{0,7},{1,6},{2,5},{3,4},{4,0},{5,1},{6,2},{7,3},{8,15},{9,14},{10,... | collective-permute-start | bytes 393224 | tf_op jit(solution)/shard_map/ppermute | solution.py:284
  72.2 5.2 %collective-permute-start.43 = (bf16[16,32,128]{2,1,0:T(8,128)(2,1)S(1)}, bf16[16,32,128]{2,1,0:T(8,128)(2,1)S(1)}, u32[]{:S(2)}, u32[]{:S(2)}) collective-permute-start(bf16[16,32,128]{2,1,0:T(8,128)(2,1)S(1)} %get-tuple-element.50), channel_id=1, source_target_pairs={{0,6},{1,7},{2,4},{3,5},{4,0},{5,1},{6,2},{7,3},{8,14},{9,15},{10,... | collective-permute-start | bytes 393224 | tf_op jit(solution)/shard_map/ppermute | solution.py:284
  72.3 5.2 %collective-permute-start.42 = (bf16[16,32,128]{2,1,0:T(8,128)(2,1)S(1)}, bf16[16,32,128]{2,1,0:T(8,128)(2,1)S(1)}, u32[]{:S(2)}, u32[]{:S(2)}) collective-permute-start(bf16[16,32,128]{2,1,0:T(8,128)(2,1)S(1)} %get-tuple-element.50), channel_id=1, source_target_pairs={{0,5},{1,4},{2,7},{3,6},{4,0},{5,1},{6,2},{7,3},{8,13},{9,12},{10,... | collective-permute-start | bytes 393224 | tf_op jit(solution)/shard_map/ppermute | solution.py:284
  73.5 3.9 %collective-permute-start.41 = (bf16[16,32,128]{2,1,0:T(8,128)(2,1)S(1)}, bf16[16,32,128]{2,1,0:T(8,128)(2,1)S(1)}, u32[]{:S(2)}, u32[]{:S(2)}) collective-permute-start(bf16[16,32,128]{2,1,0:T(8,128)(2,1)S(1)} %get-tuple-element.50), channel_id=1, source_target_pairs={{0,4},{1,5},{2,6},{3,7},{4,0},{5,1},{6,2},{7,3},{8,12},{9,13},{10,... | collective-permute-start | bytes 393224 | tf_op jit(solution)/shard_map/ppermute | solution.py:284
  73.5 4.5 %collective-permute-start.45 = (bf16[32,32,128]{2,1,0:T(8,128)(2,1)S(1)}, bf16[32,32,128]{2,1,0:T(8,128)(2,1)S(1)}, u32[]{:S(2)}, u32[]{:S(2)}) collective-permute-start(bf16[32,32,128]{2,1,0:T(8,128)(2,1)S(1)} %get-tuple-element.51.refs_3_), channel_id=1, source_target_pairs={{0,4},{1,5},{2,6},{3,7},{4,0},{5,1},{6,2},{7,3},{8,12},{9,13},{10,... | collective-permute-start | bytes 786440 | tf_op jit(solution)/shard_map/ppermute | solution.py:284

commit v13 on v11

--- a/solution.py
+++ b/solution.py
@@ -28,7 +28,7 @@
 
 
 def head_kernel(row_blocks, chunks, pos, rows_in, cols_in, blocks_in, rays_in, *refs):
-    note, table, own, blocks, rows, cols, rays, seen, squares, sems = refs
+    note, table, own, blocks, rows, cols, rays, seen, squares, norms, sems = refs
     count = blocks.shape[2]
     each = count // row_blocks
     per_chunk = count // chunks
@@ -55,23 +55,21 @@
         own[0, i] = pos[i]
     for r in range(row_blocks):
         seen[r] = r * each
-    for n in range(count):
-        row = rows[0, 0, n]
-        at = seen[row]
-        seen[row] = at + 1
-        col = cols[0, 0, n]
-        for out, first in ((table, 0), (own, 1)):
-            out[first, at] = n
-            out[first + 1, at] = col
     for i in range(quarter):
         parts = [rays[g, :, i * BS : (i + 1) * BS] for g in range(batches)]
-        note[i] = jnp.concatenate(parts, axis=0)
+        note[i] = jnp.concatenate(parts, axis=0).astype(jnp.bfloat16)
     for k in range(chunks):
         large[k].wait()
         for n in range(k * per_chunk, (k + 1) * per_chunk):
             block = blocks[0, 0, n].astype(jnp.float32)
             row = rows[0, 0, n]
             squares[row] = squares[row] + block * block
+            at = seen[row]
+            seen[row] = at + 1
+            col = cols[0, 0, n]
+            for out, first in ((table, 0), (own, 1)):
+                out[first, at] = n
+                out[first + 1, at] = col
     ones = jnp.ones((BS, BS), jnp.bfloat16)
     on_diagonal = lax.broadcasted_iota(jnp.int32, (BS, BS), 0) == lax.broadcasted_iota(
         jnp.int32, (BS, BS), 1
@@ -82,7 +80,14 @@
         fine = (left - coarse.astype(jnp.float32)).astype(jnp.bfloat16)
         total = dot(coarse, ones, NN) + dot(fine, ones, NN)
         total = jnp.sum(jnp.where(on_diagonal, total, 0.0), axis=0, keepdims=True)
-        note[quarter, r : r + 1] = total
+        norms[r : r + 1] = total
+    coarse = norms[...].astype(jnp.bfloat16)
+    fine = (norms[...] - coarse.astype(jnp.float32)).astype(jnp.bfloat16)
+    parts = [coarse, fine]
+    pad = note.shape[1] - 2 * row_blocks
+    if pad:
+        parts.append(jnp.zeros((pad, BS), jnp.bfloat16))
+    note[quarter] = jnp.concatenate(parts, axis=0)
 
 
 def pack_own_kernel(own, blocks, _, wide):
@@ -112,13 +117,14 @@
     tiles, quarter, _, _ = rays_scr.shape
     row_blocks = tiles * quarter
     if len(notes) > 1:
-        norms = sum(ref[quarter] for ref in notes)[0:row_blocks]
+        parts = [ref[quarter] for ref in notes]
         for i, ref in enumerate(notes):
-            rays_scr[info[0, 2] ^ i] = ref[0:quarter]
+            rays_scr[info[0, 2] ^ i] = ref[0:quarter].astype(jnp.float32)
     else:
-        norms = sum(notes[0][t, quarter] for t in range(tiles))[0:row_blocks]
-        rays_scr[...] = notes[0][:, 0:quarter]
-    scale = relaxation / norms
+        parts = [notes[0][t, quarter] for t in range(tiles)]
+        rays_scr[...] = notes[0][:, 0:quarter].astype(jnp.float32)
+    norms = sum(part.astype(jnp.float32) for part in parts)
+    scale = relaxation / (norms[0:row_blocks] + norms[row_blocks : 2 * row_blocks])
     for r in range(row_blocks):
         row = scale[r : r + 1]
         rays[r] = rays_scr[r // quarter, r % quarter] * row
@@ -309,7 +315,7 @@
     note, table, own, blocks = pl.pallas_call(
         functools.partial(head_kernel, row_blocks, chunks),
         out_shape=(
-            jax.ShapeDtypeStruct((quarter + 1, slices, BS), jnp.float32),
+            jax.ShapeDtypeStruct((quarter + 1, slices, BS), jnp.bfloat16),
             jax.ShapeDtypeStruct((2, count), jnp.int32),
             pltpu.SMEM((3, count), jnp.int32),
             pltpu.VMEM(blocks.shape, blocks.dtype),
@@ -322,6 +328,7 @@
             pltpu.VMEM(sinogram.shape, jnp.float32),
             pltpu.SMEM((row_blocks,), jnp.int32),
             pltpu.VMEM((row_blocks, BS, BS), jnp.float32),
+            pltpu.VMEM((row_blocks, BS), jnp.float32),
             pltpu.SemaphoreType.DMA((3 + chunks,)),
         ],
         compiler_params=PARAMS,
@@ -389,7 +396,9 @@
             before = []
         else:
             def hop(p, c, t):
-                return ((2 * place - 1 - p) % places, c, t) if c else (p, c, t ^ 1)
+                if c == 1 and p in (place - 1, place):
+                    return 2 * place - 1 - p, c, t
+                return p, c, t ^ 1
 
             image = sent(image, hop)
             terms = call(

time: 75.6 us -> 77.2 us (1.021)
  waiting for transfers between devices: 37.2 us -> 40.1 us
  starting transfers between devices: 30.9 us -> 29.4 us
    ppermute x43, waiting for transfers between devices: 37.2 us -> 40.1 us  [sent(): return lax.ppermute(value, ('subset', 'tile'), pairs)]
    ppermute x43, starting transfers between devices: 30.9 us -> 29.4 us  [sent(): return lax.ppermute(value, ('subset', 'tile'), pairs)]
where the time goes in v13:
time: 77.2 us; the launch traced here: 77 us
  waiting for transfers between devices  40.1 us (52%)
  starting transfers between devices  29.4 us (38%)
  Pallas kernels  7.23 us (9%)
    ppermute x43, waiting for transfers between devices, sent(): return lax.ppermute(value, ('subset', 'tile'), pairs)  40.1 us
    ppermute x43, starting transfers between devices, sent(): return lax.ppermute(value, ('subset', 'tile'), pairs)  29.4 us
    pallas_call x1, Pallas kernels, per_device(): pl.pallas_call(functools.partial(head_kernel, row_blocks, chunks), out_sh...  3.09 us
    pallas_call x19, Pallas kernels, call(): pl.pallas_call(kernel, out_shape=out_shape, in_specs=[SMEM] * smem + [VME...  2.34 us
  transfers between devices with their start and end apart: 43, of which 20 were waited for; matrix products, arithmetic and copies ran while one was open for 0% of the time, Pallas kernels for 7%

profile of v13, /device:TPU:25, one launch (start us, length us, event | category | flops | bytes accessed | tf_op | source)
XLA Modules:
  0.0 77.0 jit_solution(16212110664618547519)
XLA Ops:
  0.0 0.7 collective-permute-start.1
  0.8 3.1 %head.1 = (bf16[5,32,128]{2,1,0:T(8,128)(2,1)S(1)}, s32[2,80]{1,0:T(2,128)S(1)}, s32[3,80]{1,0:T(4,128)S(4)}, bf16[1,1,80,128,128]{4,3,2,1,0:T(8,128)(2,1)S(1)}) custom-call(s32[3]{0:T(128)S(1)} %pad_add_fusion.pos, s32[1,1,80]{2,1,0:T(1,128)} %rows_in.1, s32[1,1,80]{2,1,0:T(1,128)} %cols_in.1, bf16[1,1,80,128,128]{4,3,2,1,0:T(8,128)(2,1)} %blocks_in.1, ...), custom_call_target="tpu_custom_call" | custom-call | tf_op jit(solution)/shard_map/head/pallas_call | solution.py:315
  3.9 2.2 %collective-permute-start.4 = (bf16[5,32,128]{2,1,0:T(8,128)(2,1)S(1)}, bf16[5,32,128]{2,1,0:T(8,128)(2,1)S(1)}, u32[]{:S(2)}, u32[]{:S(2)}) collective-permute-start(bf16[5,32,128]{2,1,0:T(8,128)(2,1)S(1)} %get-tuple-element.31._.refs_2_), channel_id=1, source_target_pairs={{0,3},{1,2},{2,1},{3,0},{4,7},{5,6},{6,5},{7,4},{8,11},{9,10},{10,... | collective-permute-start | bytes 122888 | tf_op jit(solution)/shard_map/ppermute | solution.py:279
  6.6 0.8 %collective-permute-start = (s32[2,80]{1,0:T(2,128)S(1)}, s32[2,80]{1,0:T(2,128)S(1)}, u32[]{:S(2)}, u32[]{:S(2)}) collective-permute-start(s32[2,80]{1,0:T(2,128)S(1)} %get-tuple-element.28), channel_id=1, source_target_pairs={{0,4},{1,5},{2,6},{3,7},{4,0},{5,1},{6,2},{7,3},{8,12},{9,13},{10,... | collective-permute-start | bytes 1928 | tf_op jit(solution)/shard_map/ppermute | solution.py:279
  7.4 0.5 pack_own.1.refs_1_
  8.2 1.3 %pack_other.1 = (s32[3,80]{1,0:T(4,128)S(4)}, bf16[16,640,128]{2,1,0:T(8,128)(2,1)S(1)}) custom-call(s32[3,80]{1,0:T(4,128)S(4)} %get-tuple-element.27.own, s32[2,80]{1,0:T(2,128)S(1)} %collective-permute-done.table2, bf16[1,1,80,128,128]{4,3,2,1,0:T(8,128)(2,1)S(1)} %collective-permute-done.1.blocks2), custom_call_target="tpu_custom_call" | custom-call | tf_op jit(solution)/shard_map/pack_other/pallas_call | solution.py:356
  9.7 1.3 %collective-permute-start.8 = (bf16[16,32,128]{2,1,0:T(8,128)(2,1)S(1)}, bf16[16,32,128]{2,1,0:T(8,128)(2,1)S(1)}, u32[]{:S(2)}, u32[]{:S(2)}) collective-permute-start(bf16[16,32,128]{2,1,0:T(8,128)(2,1)S(1)} %get-tuple-element.35), channel_id=1, source_target_pairs={{0,7},{1,6},{2,5},{3,4},{4,0},{5,1},{6,2},{7,3},{8,15},{9,14},{10,... | collective-permute-start | bytes 393224 | tf_op jit(solution)/shard_map/ppermute | solution.py:279
  11.0 1.3 %collective-permute-start.7 = (bf16[16,32,128]{2,1,0:T(8,128)(2,1)S(1)}, bf16[16,32,128]{2,1,0:T(8,128)(2,1)S(1)}, u32[]{:S(2)}, u32[]{:S(2)}) collective-permute-start(bf16[16,32,128]{2,1,0:T(8,128)(2,1)S(1)} %get-tuple-element.35), channel_id=1, source_target_pairs={{0,6},{1,7},{2,4},{3,5},{4,0},{5,1},{6,2},{7,3},{8,14},{9,15},{10,... | collective-permute-start | bytes 393224 | tf_op jit(solution)/shard_map/ppermute | solution.py:279
  12.3 0.3 collective-permute-start.6
  13.1 2.0 %collective-permute-done.8.refs_6_ = bf16[16,32,128]{2,1,0:T(8,128)(2,1)S(1)} collective-permute-done((bf16[16,32,128]{2,1,0:T(8,128)(2,1)S(1)}, bf16[16,32,128]{2,1,0:T(8,128)(2,1)S(1)}, u32[]{:S(2)}, u32[]{:S(2)}) %collective-permute-start.8) | collective-permute-done | bytes 131104 | tf_op jit(solution)/shard_map/ppermute | solution.py:279
  15.1 1.3 %collective-permute-done.7.refs_5_ = bf16[16,32,128]{2,1,0:T(8,128)(2,1)S(1)} collective-permute-done((bf16[16,32,128]{2,1,0:T(8,128)(2,1)S(1)}, bf16[16,32,128]{2,1,0:T(8,128)(2,1)S(1)}, u32[]{:S(2)}, u32[]{:S(2)}) %collective-permute-start.7) | collective-permute-done | bytes 131104 | tf_op jit(solution)/shard_map/ppermute | solution.py:279
  16.7 1.1 %collective-permute-start.10 = (bf16[32,32,128]{2,1,0:T(8,128)(2,1)S(1)}, bf16[32,32,128]{2,1,0:T(8,128)(2,1)S(1)}, u32[]{:S(2)}, u32[]{:S(2)}) collective-permute-start(bf16[32,32,128]{2,1,0:T(8,128)(2,1)S(1)} %get-tuple-element.37), channel_id=1, source_target_pairs={{0,1},{1,0},{2,3},{3,2},{4,12},{5,13},{6,14},{7,15},{8,9},{9,8},{1... | collective-permute-start | bytes 786440 | tf_op jit(solution)/shard_map/ppermute | solution.py:279
  17.8 7.2 %collective-permute-done.10.image = bf16[32,32,128]{2,1,0:T(8,128)(2,1)S(1)} collective-permute-done((bf16[32,32,128]{2,1,0:T(8,128)(2,1)S(1)}, bf16[32,32,128]{2,1,0:T(8,128)(2,1)S(1)}, u32[]{:S(2)}, u32[]{:S(2)}) %collective-permute-start.10) | collective-permute-done | bytes 262176 | tf_op jit(solution)/shard_map/ppermute | solution.py:279
  25.4 1.0 %collective-permute-start.12 = (bf16[16,32,128]{2,1,0:T(8,128)(2,1)S(1)}, bf16[16,32,128]{2,1,0:T(8,128)(2,1)S(1)}, u32[]{:S(2)}, u32[]{:S(2)}) collective-permute-start(bf16[16,32,128]{2,1,0:T(8,128)(2,1)S(1)} %project.3), channel_id=1, source_target_pairs={{0,4},{1,5},{2,6},{3,7},{4,1},{5,0},{6,3},{7,2},{8,12},{9,13},{10,... | collective-permute-start | bytes 393224 | tf_op jit(solution)/shard_map/ppermute | solution.py:279
  26.4 0.5 collective-permute-start.15
  27.1 1.7 %collective-permute-done.13.refs_5_ = bf16[16,32,128]{2,1,0:T(8,128)(2,1)S(1)} collective-permute-done((bf16[16,32,128]{2,1,0:T(8,128)(2,1)S(1)}, bf16[16,32,128]{2,1,0:T(8,128)(2,1)S(1)}, u32[]{:S(2)}, u32[]{:S(2)}) %collective-permute-start.13) | collective-permute-done | bytes 131104 | tf_op jit(solution)/shard_map/ppermute | solution.py:279
  28.8 2.7 %collective-permute-start.19 = (bf16[16,32,128]{2,1,0:T(8,128)(2,1)S(1)}, bf16[16,32,128]{2,1,0:T(8,128)(2,1)S(1)}, u32[]{:S(2)}, u32[]{:S(2)}) collective-permute-start(bf16[16,32,128]{2,1,0:T(8,128)(2,1)S(1)} %get-tuple-element.38), channel_id=1, source_target_pairs={{0,7},{1,6},{2,5},{3,4},{4,0},{5,1},{6,2},{7,3},{8,15},{9,14},{10,... | collective-permute-start | bytes 393224 | tf_op jit(solution)/shard_map/ppermute | solution.py:279
  31.5 1.4 %collective-permute-start.17 = (bf16[16,32,128]{2,1,0:T(8,128)(2,1)S(1)}, bf16[16,32,128]{2,1,0:T(8,128)(2,1)S(1)}, u32[]{:S(2)}, u32[]{:S(2)}) collective-permute-start(bf16[16,32,128]{2,1,0:T(8,128)(2,1)S(1)} %get-tuple-element.38), channel_id=1, source_target_pairs={{0,5},{1,4},{2,7},{3,6},{4,0},{5,1},{6,2},{7,3},{8,13},{9,12},{10,... | collective-permute-start | bytes 393224 | tf_op jit(solution)/shard_map/ppermute | solution.py:279
  33.0 0.5 collective-permute-start.20
  33.5 1.8 %collective-permute-done.19.refs_6_ = bf16[16,32,128]{2,1,0:T(8,128)(2,1)S(1)} collective-permute-done((bf16[16,32,128]{2,1,0:T(8,128)(2,1)S(1)}, bf16[16,32,128]{2,1,0:T(8,128)(2,1)S(1)}, u32[]{:S(2)}, u32[]{:S(2)}) %collective-permute-start.19) | collective-permute-done | bytes 131104 | tf_op jit(solution)/shard_map/ppermute | solution.py:279
  35.3 1.3 %collective-permute-done.18.refs_5_ = bf16[16,32,128]{2,1,0:T(8,128)(2,1)S(1)} collective-permute-done((bf16[16,32,128]{2,1,0:T(8,128)(2,1)S(1)}, bf16[16,32,128]{2,1,0:T(8,128)(2,1)S(1)}, u32[]{:S(2)}, u32[]{:S(2)}) %collective-permute-start.18) | collective-permute-done | bytes 131104 | tf_op jit(solution)/shard_map/ppermute | solution.py:279
  36.7 1.1 %collective-permute-start.21 = (bf16[32,32,128]{2,1,0:T(8,128)(2,1)S(1)}, bf16[32,32,128]{2,1,0:T(8,128)(2,1)S(1)}, u32[]{:S(2)}, u32[]{:S(2)}) collective-permute-start(bf16[32,32,128]{2,1,0:T(8,128)(2,1)S(1)} %get-tuple-element.41), channel_id=1, source_target_pairs={{0,1},{1,0},{2,3},{3,2},{4,5},{5,4},{6,7},{7,6},{8,9},{9,8},{10,11... | collective-permute-start | bytes 786440 | tf_op jit(solution)/shard_map/ppermute | solution.py:279
  37.8 7.1 %collective-permute-done.21.image = bf16[32,32,128]{2,1,0:T(8,128)(2,1)S(1)} collective-permute-done((bf16[32,32,128]{2,1,0:T(8,128)(2,1)S(1)}, bf16[32,32,128]{2,1,0:T(8,128)(2,1)S(1)}, u32[]{:S(2)}, u32[]{:S(2)}) %collective-permute-start.21) | collective-permute-done | bytes 262176 | tf_op jit(solution)/shard_map/ppermute | solution.py:279
  44.9 1.7 %collective-permute-start.25 = (bf16[16,32,128]{2,1,0:T(8,128)(2,1)S(1)}, bf16[16,32,128]{2,1,0:T(8,128)(2,1)S(1)}, u32[]{:S(2)}, u32[]{:S(2)}) collective-permute-start(bf16[16,32,128]{2,1,0:T(8,128)(2,1)S(1)} %project.4), channel_id=1, source_target_pairs={{0,4},{1,5},{2,6},{3,7},{4,3},{5,2},{6,1},{7,0},{8,12},{9,13},{10,... | collective-permute-start | bytes 393224 | tf_op jit(solution)/shard_map/ppermute | solution.py:279
  46.6 0.3 collective-permute-start.23
  47.1 0.3 collective-permute-start.26
  47.4 1.1 %collective-permute-done.25.refs_6_ = bf16[16,32,128]{2,1,0:T(8,128)(2,1)S(1)} collective-permute-done((bf16[16,32,128]{2,1,0:T(8,128)(2,1)S(1)}, bf16[16,32,128]{2,1,0:T(8,128)(2,1)S(1)}, u32[]{:S(2)}, u32[]{:S(2)}) %collective-permute-start.25) | collective-permute-done | bytes 131104 | tf_op jit(solution)/shard_map/ppermute | solution.py:279
  48.5 1.0 %collective-permute-done.24.refs_5_ = bf16[16,32,128]{2,1,0:T(8,128)(2,1)S(1)} collective-permute-done((bf16[16,32,128]{2,1,0:T(8,128)(2,1)S(1)}, bf16[16,32,128]{2,1,0:T(8,128)(2,1)S(1)}, u32[]{:S(2)}, u32[]{:S(2)}) %collective-permute-start.24) | collective-permute-done | bytes 131104 | tf_op jit(solution)/shard_map/ppermute | solution.py:279
  49.6 0.4 collective-permute-done.23.refs_4_
  49.9 1.6 %collective-permute-start.30 = (bf16[16,32,128]{2,1,0:T(8,128)(2,1)S(1)}, bf16[16,32,128]{2,1,0:T(8,128)(2,1)S(1)}, u32[]{:S(2)}, u32[]{:S(2)}) collective-permute-start(bf16[16,32,128]{2,1,0:T(8,128)(2,1)S(1)} %get-tuple-element.42), channel_id=1, source_target_pairs={{0,7},{1,6},{2,5},{3,4},{4,0},{5,1},{6,2},{7,3},{8,15},{9,14},{10,... | collective-permute-start | bytes 393224 | tf_op jit(solution)/shard_map/ppermute | solution.py:279
  51.6 1.2 %collective-permute-start.28 = (bf16[16,32,128]{2,1,0:T(8,128)(2,1)S(1)}, bf16[16,32,128]{2,1,0:T(8,128)(2,1)S(1)}, u32[]{:S(2)}, u32[]{:S(2)}) collective-permute-start(bf16[16,32,128]{2,1,0:T(8,128)(2,1)S(1)} %get-tuple-element.42), channel_id=1, source_target_pairs={{0,5},{1,4},{2,7},{3,6},{4,0},{5,1},{6,2},{7,3},{8,13},{9,12},{10,... | collective-permute-start | bytes 393224 | tf_op jit(solution)/shard_map/ppermute | solution.py:279
  53.3 2.1 %collective-permute-done.30.refs_6_ = bf16[16,32,128]{2,1,0:T(8,128)(2,1)S(1)} collective-permute-done((bf16[16,32,128]{2,1,0:T(8,128)(2,1)S(1)}, bf16[16,32,128]{2,1,0:T(8,128)(2,1)S(1)}, u32[]{:S(2)}, u32[]{:S(2)}) %collective-permute-start.30) | collective-permute-done | bytes 131104 | tf_op jit(solution)/shard_map/ppermute | solution.py:279
  55.4 1.3 %collective-permute-done.29.refs_5_ = bf16[16,32,128]{2,1,0:T(8,128)(2,1)S(1)} collective-permute-done((bf16[16,32,128]{2,1,0:T(8,128)(2,1)S(1)}, bf16[16,32,128]{2,1,0:T(8,128)(2,1)S(1)}, u32[]{:S(2)}, u32[]{:S(2)}) %collective-permute-start.29) | collective-permute-done | bytes 131104 | tf_op jit(solution)/shard_map/ppermute | solution.py:279
  57.0 5.5 %collective-permute-done.32.image = bf16[32,32,128]{2,1,0:T(8,128)(2,1)S(1)} collective-permute-done((bf16[32,32,128]{2,1,0:T(8,128)(2,1)S(1)}, bf16[32,32,128]{2,1,0:T(8,128)(2,1)S(1)}, u32[]{:S(2)}, u32[]{:S(2)}) %collective-permute-start.32) | collective-permute-done | bytes 262176 | tf_op jit(solution)/shard_map/ppermute | solution.py:279
  62.5 0.5 project.5
  63.1 0.7 collective-permute-start.36
  63.8 0.5 collective-permute-start.35
  64.3 0.5 collective-permute-start.34
  64.8 0.5 collective-permute-start.37
  65.3 0.4 collective-permute-done.36.refs_6_
  65.7 1.7 %collective-permute-done.35.refs_5_ = bf16[16,32,128]{2,1,0:T(8,128)(2,1)S(1)} collective-permute-done((bf16[16,32,128]{2,1,0:T(8,128)(2,1)S(1)}, bf16[16,32,128]{2,1,0:T(8,128)(2,1)S(1)}, u32[]{:S(2)}, u32[]{:S(2)}) %collective-permute-start.35) | collective-permute-done | bytes 131104 | tf_op jit(solution)/shard_map/ppermute | solution.py:279
  67.5 3.2 %collective-permute-start.41 = (bf16[16,32,128]{2,1,0:T(8,128)(2,1)S(1)}, bf16[16,32,128]{2,1,0:T(8,128)(2,1)S(1)}, u32[]{:S(2)}, u32[]{:S(2)}) collective-permute-start(bf16[16,32,128]{2,1,0:T(8,128)(2,1)S(1)} %get-tuple-element.46), channel_id=1, source_target_pairs={{0,7},{1,6},{2,5},{3,4},{4,0},{5,1},{6,2},{7,3},{8,15},{9,14},{10,... | collective-permute-start | bytes 393224 | tf_op jit(solution)/shard_map/ppermute | solution.py:279
  70.8 0.9 %collective-permute-start.39 = (bf16[16,32,128]{2,1,0:T(8,128)(2,1)S(1)}, bf16[16,32,128]{2,1,0:T(8,128)(2,1)S(1)}, u32[]{:S(2)}, u32[]{:S(2)}) collective-permute-start(bf16[16,32,128]{2,1,0:T(8,128)(2,1)S(1)} %get-tuple-element.46), channel_id=1, source_target_pairs={{0,5},{1,4},{2,7},{3,6},{4,0},{5,1},{6,2},{7,3},{8,13},{9,12},{10,... | collective-permute-start | bytes 393224 | tf_op jit(solution)/shard_map/ppermute | solution.py:279
  71.7 0.5 collective-permute-start.42
  72.2 2.1 %collective-permute-done.41.refs_6_ = bf16[16,32,128]{2,1,0:T(8,128)(2,1)S(1)} collective-permute-done((bf16[16,32,128]{2,1,0:T(8,128)(2,1)S(1)}, bf16[16,32,128]{2,1,0:T(8,128)(2,1)S(1)}, u32[]{:S(2)}, u32[]{:S(2)}) %collective-permute-start.41) | collective-permute-done | bytes 131104 | tf_op jit(solution)/shard_map/ppermute | solution.py:279
  74.3 1.3 %collective-permute-done.40.refs_5_ = bf16[16,32,128]{2,1,0:T(8,128)(2,1)S(1)} collective-permute-done((bf16[16,32,128]{2,1,0:T(8,128)(2,1)S(1)}, bf16[16,32,128]{2,1,0:T(8,128)(2,1)S(1)}, u32[]{:S(2)}, u32[]{:S(2)}) %collective-permute-start.40) | collective-permute-done | bytes 131104 | tf_op jit(solution)/shard_map/ppermute | solution.py:279
  75.7 0.6 update.15.refs_1_
  76.3 0.8 %second.7 = bf16[4,8,4096]{2,1,0:T(8,128)(2,1)} custom-call(s32[3,80]{1,0:T(4,128)S(4)} %get-tuple-element.29.refs_0_.info, f32[32,32,128]{2,1,0:T(8,128)S(1)} %update.15.refs_1_, bf16[32,32,128]{2,1,0:T(8,128)(2,1)S(1)} %collective-permute-done.42.refs_2_, bf16[32,32,128]{2,1,0:T(8,128)(2,1)S(1)} %get-tuple-element.47.refs_3_, ...), custom_call_target="tpu_custom_call" | custom-call | tf_op jit(solution)/shard_map/second/pallas_call | solution.py:300
  (61 shorter events, 3.6 us)
Async XLA Ops:
  0.0 8.2 %collective-permute-start.1 = (bf16[1,1,80,128,128]{4,3,2,1,0:T(8,128)(2,1)}, bf16[1,1,80,128,128]{4,3,2,1,0:T(8,128)(2,1)S(1)}, u32[]{:S(2)}, u32[]{:S(2)}) collective-permute-start(bf16[1,1,80,128,128]{4,3,2,1,0:T(8,128)(2,1)} %blocks_in.1), channel_id=1, source_target_pairs={{0,4},{1,5},{2,6},{3,7},{4,0},{5,1},{6,2},{7,3},{8,12},{9,13},{10,... | collective-permute-start | bytes 7864328 | tf_op jit(solution)/shard_map/ppermute | solution.py:279
  3.9 5.7 %collective-permute-start.4 = (bf16[5,32,128]{2,1,0:T(8,128)(2,1)S(1)}, bf16[5,32,128]{2,1,0:T(8,128)(2,1)S(1)}, u32[]{:S(2)}, u32[]{:S(2)}) collective-permute-start(bf16[5,32,128]{2,1,0:T(8,128)(2,1)S(1)} %get-tuple-element.31._.refs_2_), channel_id=1, source_target_pairs={{0,3},{1,2},{2,1},{3,0},{4,7},{5,6},{6,5},{7,4},{8,11},{9,10},{10,... | collective-permute-start | bytes 122888 | tf_op jit(solution)/shard_map/ppermute | solution.py:279
  6.1 3.5 %collective-permute-start.3 = (bf16[5,32,128]{2,1,0:T(8,128)(2,1)S(1)}, bf16[5,32,128]{2,1,0:T(8,128)(2,1)S(1)}, u32[]{:S(2)}, u32[]{:S(2)}) collective-permute-start(bf16[5,32,128]{2,1,0:T(8,128)(2,1)S(1)} %get-tuple-element.31._.refs_2_), channel_id=1, source_target_pairs={{0,2},{1,3},{2,0},{3,1},{4,6},{5,7},{6,4},{7,5},{8,10},{9,11},{10,... | collective-permute-start | bytes 122888 | tf_op jit(solution)/shard_map/ppermute | solution.py:279
  6.3 3.3 %collective-permute-start.2 = (bf16[5,32,128]{2,1,0:T(8,128)(2,1)S(1)}, bf16[5,32,128]{2,1,0:T(8,128)(2,1)S(1)}, u32[]{:S(2)}, u32[]{:S(2)}) collective-permute-start(bf16[5,32,128]{2,1,0:T(8,128)(2,1)S(1)} %get-tuple-element.31._.refs_2_), channel_id=1, source_target_pairs={{0,1},{1,0},{2,3},{3,2},{4,5},{5,4},{6,7},{7,6},{8,9},{9,8},{10,11... | collective-permute-start | bytes 122888 | tf_op jit(solution)/shard_map/ppermute | solution.py:279
  6.6 1.7 %collective-permute-start = (s32[2,80]{1,0:T(2,128)S(1)}, s32[2,80]{1,0:T(2,128)S(1)}, u32[]{:S(2)}, u32[]{:S(2)}) collective-permute-start(s32[2,80]{1,0:T(2,128)S(1)} %get-tuple-element.28), channel_id=1, source_target_pairs={{0,4},{1,5},{2,6},{3,7},{4,0},{5,1},{6,2},{7,3},{8,12},{9,13},{10,... | collective-permute-start | bytes 1928 | tf_op jit(solution)/shard_map/ppermute | solution.py:279
  9.7 5.4 %collective-permute-start.8 = (bf16[16,32,128]{2,1,0:T(8,128)(2,1)S(1)}, bf16[16,32,128]{2,1,0:T(8,128)(2,1)S(1)}, u32[]{:S(2)}, u32[]{:S(2)}) collective-permute-start(bf16[16,32,128]{2,1,0:T(8,128)(2,1)S(1)} %get-tuple-element.35), channel_id=1, source_target_pairs={{0,7},{1,6},{2,5},{3,4},{4,0},{5,1},{6,2},{7,3},{8,15},{9,14},{10,... | collective-permute-start | bytes 393224 | tf_op jit(solution)/shard_map/ppermute | solution.py:279
  11.0 5.4 %collective-permute-start.7 = (bf16[16,32,128]{2,1,0:T(8,128)(2,1)S(1)}, bf16[16,32,128]{2,1,0:T(8,128)(2,1)S(1)}, u32[]{:S(2)}, u32[]{:S(2)}) collective-permute-start(bf16[16,32,128]{2,1,0:T(8,128)(2,1)S(1)} %get-tuple-element.35), channel_id=1, source_target_pairs={{0,6},{1,7},{2,4},{3,5},{4,0},{5,1},{6,2},{7,3},{8,14},{9,15},{10,... | collective-permute-start | bytes 393224 | tf_op jit(solution)/shard_map/ppermute | solution.py:279
  12.3 4.4 %collective-permute-start.6 = (bf16[16,32,128]{2,1,0:T(8,128)(2,1)S(1)}, bf16[16,32,128]{2,1,0:T(8,128)(2,1)S(1)}, u32[]{:S(2)}, u32[]{:S(2)}) collective-permute-start(bf16[16,32,128]{2,1,0:T(8,128)(2,1)S(1)} %get-tuple-element.35), channel_id=1, source_target_pairs={{0,5},{1,4},{2,7},{3,6},{4,0},{5,1},{6,2},{7,3},{8,13},{9,12},{10,... | collective-permute-start | bytes 393224 | tf_op jit(solution)/shard_map/ppermute | solution.py:279
  12.6 4.1 %collective-permute-start.5 = (bf16[16,32,128]{2,1,0:T(8,128)(2,1)S(1)}, bf16[16,32,128]{2,1,0:T(8,128)(2,1)S(1)}, u32[]{:S(2)}, u32[]{:S(2)}) collective-permute-start(bf16[16,32,128]{2,1,0:T(8,128)(2,1)S(1)} %get-tuple-element.35), channel_id=1, source_target_pairs={{0,4},{1,5},{2,6},{3,7},{4,0},{5,1},{6,2},{7,3},{8,12},{9,13},{10,... | collective-permute-start | bytes 393224 | tf_op jit(solution)/shard_map/ppermute | solution.py:279
  12.9 3.7 %collective-permute-start.9 = (bf16[32,32,128]{2,1,0:T(8,128)(2,1)S(1)}, bf16[32,32,128]{2,1,0:T(8,128)(2,1)S(1)}, u32[]{:S(2)}, u32[]{:S(2)}) collective-permute-start(bf16[32,32,128]{2,1,0:T(8,128)(2,1)S(1)} %get-tuple-element.36.refs_3_), channel_id=1, source_target_pairs={{0,4},{1,5},{2,6},{3,7},{4,0},{5,1},{6,2},{7,3},{8,12},{9,13},{10,... | collective-permute-start | bytes 786440 | tf_op jit(solution)/shard_map/ppermute | solution.py:279
  16.7 8.3 %collective-permute-start.10 = (bf16[32,32,128]{2,1,0:T(8,128)(2,1)S(1)}, bf16[32,32,128]{2,1,0:T(8,128)(2,1)S(1)}, u32[]{:S(2)}, u32[]{:S(2)}) collective-permute-start(bf16[32,32,128]{2,1,0:T(8,128)(2,1)S(1)} %get-tuple-element.37), channel_id=1, source_target_pairs={{0,1},{1,0},{2,3},{3,2},{4,12},{5,13},{6,14},{7,15},{8,9},{9,8},{1... | collective-permute-start | bytes 786440 | tf_op jit(solution)/shard_map/ppermute | solution.py:279
  25.1 2.0 %collective-permute-start.14 = (bf16[16,32,128]{2,1,0:T(8,128)(2,1)S(1)}, bf16[16,32,128]{2,1,0:T(8,128)(2,1)S(1)}, u32[]{:S(2)}, u32[]{:S(2)}) collective-permute-start(bf16[16,32,128]{2,1,0:T(8,128)(2,1)S(1)} %project.3), channel_id=1, source_target_pairs={{0,4},{1,5},{2,6},{3,7},{4,3},{5,2},{6,1},{7,0},{8,12},{9,13},{10,... | collective-permute-start | bytes 393224 | tf_op jit(solution)/shard_map/ppermute | solution.py:279
  25.1 3.6 %collective-permute-start.13 = (bf16[16,32,128]{2,1,0:T(8,128)(2,1)S(1)}, bf16[16,32,128]{2,1,0:T(8,128)(2,1)S(1)}, u32[]{:S(2)}, u32[]{:S(2)}) collective-permute-start(bf16[16,32,128]{2,1,0:T(8,128)(2,1)S(1)} %project.3), channel_id=1, source_target_pairs={{0,4},{1,5},{2,6},{3,7},{4,2},{5,3},{6,0},{7,1},{8,12},{9,13},{10,... | collective-permute-start | bytes 393224 | tf_op jit(solution)/shard_map/ppermute | solution.py:279
  25.4 3.3 %collective-permute-start.12 = (bf16[16,32,128]{2,1,0:T(8,128)(2,1)S(1)}, bf16[16,32,128]{2,1,0:T(8,128)(2,1)S(1)}, u32[]{:S(2)}, u32[]{:S(2)}) collective-permute-start(bf16[16,32,128]{2,1,0:T(8,128)(2,1)S(1)} %project.3), channel_id=1, source_target_pairs={{0,4},{1,5},{2,6},{3,7},{4,1},{5,0},{6,3},{7,2},{8,12},{9,13},{10,... | collective-permute-start | bytes 393224 | tf_op jit(solution)/shard_map/ppermute | solution.py:279
  26.4 2.3 %collective-permute-start.11 = (bf16[16,32,128]{2,1,0:T(8,128)(2,1)S(1)}, bf16[16,32,128]{2,1,0:T(8,128)(2,1)S(1)}, u32[]{:S(2)}, u32[]{:S(2)}) collective-permute-start(bf16[16,32,128]{2,1,0:T(8,128)(2,1)S(1)} %project.3), channel_id=1, source_target_pairs={{0,4},{1,5},{2,6},{3,7},{4,0},{5,1},{6,2},{7,3},{8,12},{9,13},{10,... | collective-permute-start | bytes 393224 | tf_op jit(solution)/shard_map/ppermute | solution.py:279
  26.4 2.3 %collective-permute-start.15 = (bf16[32,32,128]{2,1,0:T(8,128)(2,1)S(1)}, bf16[32,32,128]{2,1,0:T(8,128)(2,1)S(1)}, u32[]{:S(2)}, u32[]{:S(2)}) collective-permute-start(bf16[32,32,128]{2,1,0:T(8,128)(2,1)S(1)} %collective-permute-done.10.image), channel_id=1, source_target_pairs={{0,4},{1,5},{2,6},{3,7},{4,0},{5,1},{6,2},{7,3},{8,12},{9,13},{10,... | collective-permute-start | bytes 786440 | tf_op jit(solution)/shard_map/ppermute | solution.py:279
  28.8 6.5 %collective-permute-start.19 = (bf16[16,32,128]{2,1,0:T(8,128)(2,1)S(1)}, bf16[16,32,128]{2,1,0:T(8,128)(2,1)S(1)}, u32[]{:S(2)}, u32[]{:S(2)}) collective-permute-start(bf16[16,32,128]{2,1,0:T(8,128)(2,1)S(1)} %get-tuple-element.38), channel_id=1, source_target_pairs={{0,7},{1,6},{2,5},{3,4},{4,0},{5,1},{6,2},{7,3},{8,15},{9,14},{10,... | collective-permute-start | bytes 393224 | tf_op jit(solution)/shard_map/ppermute | solution.py:279
  31.5 5.2 %collective-permute-start.18 = (bf16[16,32,128]{2,1,0:T(8,128)(2,1)S(1)}, bf16[16,32,128]{2,1,0:T(8,128)(2,1)S(1)}, u32[]{:S(2)}, u32[]{:S(2)}) collective-permute-start(bf16[16,32,128]{2,1,0:T(8,128)(2,1)S(1)} %get-tuple-element.38), channel_id=1, source_target_pairs={{0,6},{1,7},{2,4},{3,5},{4,0},{5,1},{6,2},{7,3},{8,14},{9,15},{10,... | collective-permute-start | bytes 393224 | tf_op jit(solution)/shard_map/ppermute | solution.py:279
  31.5 5.1 %collective-permute-start.17 = (bf16[16,32,128]{2,1,0:T(8,128)(2,1)S(1)}, bf16[16,32,128]{2,1,0:T(8,128)(2,1)S(1)}, u32[]{:S(2)}, u32[]{:S(2)}) collective-permute-start(bf16[16,32,128]{2,1,0:T(8,128)(2,1)S(1)} %get-tuple-element.38), channel_id=1, source_target_pairs={{0,5},{1,4},{2,7},{3,6},{4,0},{5,1},{6,2},{7,3},{8,13},{9,12},{10,... | collective-permute-start | bytes 393224 | tf_op jit(solution)/shard_map/ppermute | solution.py:279
  33.0 3.7 %collective-permute-start.16 = (bf16[16,32,128]{2,1,0:T(8,128)(2,1)S(1)}, bf16[16,32,128]{2,1,0:T(8,128)(2,1)S(1)}, u32[]{:S(2)}, u32[]{:S(2)}) collective-permute-start(bf16[16,32,128]{2,1,0:T(8,128)(2,1)S(1)} %get-tuple-element.38), channel_id=1, source_target_pairs={{0,4},{1,5},{2,6},{3,7},{4,0},{5,1},{6,2},{7,3},{8,12},{9,13},{10,... | collective-permute-start | bytes 393224 | tf_op jit(solution)/shard_map/ppermute | solution.py:279
  33.0 3.7 %collective-permute-start.20 = (bf16[32,32,128]{2,1,0:T(8,128)(2,1)S(1)}, bf16[32,32,128]{2,1,0:T(8,128)(2,1)S(1)}, u32[]{:S(2)}, u32[]{:S(2)}) collective-permute-start(bf16[32,32,128]{2,1,0:T(8,128)(2,1)S(1)} %get-tuple-element.39.refs_3_), channel_id=1, source_target_pairs={{0,4},{1,5},{2,6},{3,7},{4,0},{5,1},{6,2},{7,3},{8,12},{9,13},{10,... | collective-permute-start | bytes 786440 | tf_op jit(solution)/shard_map/ppermute | solution.py:279
  36.7 8.2 %collective-permute-start.21 = (bf16[32,32,128]{2,1,0:T(8,128)(2,1)S(1)}, bf16[32,32,128]{2,1,0:T(8,128)(2,1)S(1)}, u32[]{:S(2)}, u32[]{:S(2)}) collective-permute-start(bf16[32,32,128]{2,1,0:T(8,128)(2,1)S(1)} %get-tuple-element.41), channel_id=1, source_target_pairs={{0,1},{1,0},{2,3},{3,2},{4,5},{5,4},{6,7},{7,6},{8,9},{9,8},{10,11... | collective-permute-start | bytes 786440 | tf_op jit(solution)/shard_map/ppermute | solution.py:279
  44.9 3.6 %collective-permute-start.25 = (bf16[16,32,128]{2,1,0:T(8,128)(2,1)S(1)}, bf16[16,32,128]{2,1,0:T(8,128)(2,1)S(1)}, u32[]{:S(2)}, u32[]{:S(2)}) collective-permute-start(bf16[16,32,128]{2,1,0:T(8,128)(2,1)S(1)} %project.4), channel_id=1, source_target_pairs={{0,4},{1,5},{2,6},{3,7},{4,3},{5,2},{6,1},{7,0},{8,12},{9,13},{10,... | collective-permute-start | bytes 393224 | tf_op jit(solution)/shard_map/ppermute | solution.py:279
  46.6 3.0 %collective-permute-start.24 = (bf16[16,32,128]{2,1,0:T(8,128)(2,1)S(1)}, bf16[16,32,128]{2,1,0:T(8,128)(2,1)S(1)}, u32[]{:S(2)}, u32[]{:S(2)}) collective-permute-start(bf16[16,32,128]{2,1,0:T(8,128)(2,1)S(1)} %project.4), channel_id=1, source_target_pairs={{0,4},{1,5},{2,6},{3,7},{4,2},{5,3},{6,0},{7,1},{8,12},{9,13},{10,... | collective-permute-start | bytes 393224 | tf_op jit(solution)/shard_map/ppermute | solution.py:279
  46.6 3.4 %collective-permute-start.23 = (bf16[16,32,128]{2,1,0:T(8,128)(2,1)S(1)}, bf16[16,32,128]{2,1,0:T(8,128)(2,1)S(1)}, u32[]{:S(2)}, u32[]{:S(2)}) collective-permute-start(bf16[16,32,128]{2,1,0:T(8,128)(2,1)S(1)} %project.4), channel_id=1, source_target_pairs={{0,4},{1,5},{2,6},{3,7},{4,1},{5,0},{6,3},{7,2},{8,12},{9,13},{10,... | collective-permute-start | bytes 393224 | tf_op jit(solution)/shard_map/ppermute | solution.py:279
  46.9 3.0 %collective-permute-start.22 = (bf16[16,32,128]{2,1,0:T(8,128)(2,1)S(1)}, bf16[16,32,128]{2,1,0:T(8,128)(2,1)S(1)}, u32[]{:S(2)}, u32[]{:S(2)}) collective-permute-start(bf16[16,32,128]{2,1,0:T(8,128)(2,1)S(1)} %project.4), channel_id=1, source_target_pairs={{0,4},{1,5},{2,6},{3,7},{4,0},{5,1},{6,2},{7,3},{8,12},{9,13},{10,... | collective-permute-start | bytes 393224 | tf_op jit(solution)/shard_map/ppermute | solution.py:279
  47.1 2.9 %collective-permute-start.26 = (bf16[32,32,128]{2,1,0:T(8,128)(2,1)S(1)}, bf16[32,32,128]{2,1,0:T(8,128)(2,1)S(1)}, u32[]{:S(2)}, u32[]{:S(2)}) collective-permute-start(bf16[32,32,128]{2,1,0:T(8,128)(2,1)S(1)} %collective-permute-done.21.image), channel_id=1, source_target_pairs={{0,4},{1,5},{2,6},{3,7},{4,0},{5,1},{6,2},{7,3},{8,12},{9,13},{10,... | collective-permute-start | bytes 786440 | tf_op jit(solution)/shard_map/ppermute | solution.py:279
  49.9 5.4 %collective-permute-start.30 = (bf16[16,32,128]{2,1,0:T(8,128)(2,1)S(1)}, bf16[16,32,128]{2,1,0:T(8,128)(2,1)S(1)}, u32[]{:S(2)}, u32[]{:S(2)}) collective-permute-start(bf16[16,32,128]{2,1,0:T(8,128)(2,1)S(1)} %get-tuple-element.42), channel_id=1, source_target_pairs={{0,7},{1,6},{2,5},{3,4},{4,0},{5,1},{6,2},{7,3},{8,15},{9,14},{10,... | collective-permute-start | bytes 393224 | tf_op jit(solution)/shard_map/ppermute | solution.py:279
  51.5 5.1 %collective-permute-start.29 = (bf16[16,32,128]{2,1,0:T(8,128)(2,1)S(1)}, bf16[16,32,128]{2,1,0:T(8,128)(2,1)S(1)}, u32[]{:S(2)}, u32[]{:S(2)}) collective-permute-start(bf16[16,32,128]{2,1,0:T(8,128)(2,1)S(1)} %get-tuple-element.42), channel_id=1, source_target_pairs={{0,6},{1,7},{2,4},{3,5},{4,0},{5,1},{6,2},{7,3},{8,14},{9,15},{10,... | collective-permute-start | bytes 393224 | tf_op jit(solution)/shard_map/ppermute | solution.py:279
  51.6 5.1 %collective-permute-start.28 = (bf16[16,32,128]{2,1,0:T(8,128)(2,1)S(1)}, bf16[16,32,128]{2,1,0:T(8,128)(2,1)S(1)}, u32[]{:S(2)}, u32[]{:S(2)}) collective-permute-start(bf16[16,32,128]{2,1,0:T(8,128)(2,1)S(1)} %get-tuple-element.42), channel_id=1, source_target_pairs={{0,5},{1,4},{2,7},{3,6},{4,0},{5,1},{6,2},{7,3},{8,13},{9,12},{10,... | collective-permute-start | bytes 393224 | tf_op jit(solution)/shard_map/ppermute | solution.py:279
  52.8 3.9 %collective-permute-start.27 = (bf16[16,32,128]{2,1,0:T(8,128)(2,1)S(1)}, bf16[16,32,128]{2,1,0:T(8,128)(2,1)S(1)}, u32[]{:S(2)}, u32[]{:S(2)}) collective-permute-start(bf16[16,32,128]{2,1,0:T(8,128)(2,1)S(1)} %get-tuple-element.42), channel_id=1, source_target_pairs={{0,4},{1,5},{2,6},{3,7},{4,0},{5,1},{6,2},{7,3},{8,12},{9,13},{10,... | collective-permute-start | bytes 393224 | tf_op jit(solution)/shard_map/ppermute | solution.py:279
  53.1 3.6 %collective-permute-start.31 = (bf16[32,32,128]{2,1,0:T(8,128)(2,1)S(1)}, bf16[32,32,128]{2,1,0:T(8,128)(2,1)S(1)}, u32[]{:S(2)}, u32[]{:S(2)}) collective-permute-start(bf16[32,32,128]{2,1,0:T(8,128)(2,1)S(1)} %get-tuple-element.43.refs_3_), channel_id=1, source_target_pairs={{0,4},{1,5},{2,6},{3,7},{4,0},{5,1},{6,2},{7,3},{8,12},{9,13},{10,... | collective-permute-start | bytes 786440 | tf_op jit(solution)/shard_map/ppermute | solution.py:279
  57.0 5.6 %collective-permute-start.32 = (bf16[32,32,128]{2,1,0:T(8,128)(2,1)S(1)}, bf16[32,32,128]{2,1,0:T(8,128)(2,1)S(1)}, u32[]{:S(2)}, u32[]{:S(2)}) collective-permute-start(bf16[32,32,128]{2,1,0:T(8,128)(2,1)S(1)} %get-tuple-element.45), channel_id=1, source_target_pairs={{0,1},{1,0},{2,3},{3,2},{4,5},{5,4},{6,7},{7,6},{8,9},{9,8},{10,11... | collective-permute-start | bytes 786440 | tf_op jit(solution)/shard_map/ppermute | solution.py:279
  63.1 2.7 %collective-permute-start.36 = (bf16[16,32,128]{2,1,0:T(8,128)(2,1)S(1)}, bf16[16,32,128]{2,1,0:T(8,128)(2,1)S(1)}, u32[]{:S(2)}, u32[]{:S(2)}) collective-permute-start(bf16[16,32,128]{2,1,0:T(8,128)(2,1)S(1)} %project.5), channel_id=1, source_target_pairs={{0,4},{1,5},{2,6},{3,7},{4,3},{5,2},{6,1},{7,0},{8,12},{9,13},{10,... | collective-permute-start | bytes 393224 | tf_op jit(solution)/shard_map/ppermute | solution.py:279
  63.8 3.7 %collective-permute-start.35 = (bf16[16,32,128]{2,1,0:T(8,128)(2,1)S(1)}, bf16[16,32,128]{2,1,0:T(8,128)(2,1)S(1)}, u32[]{:S(2)}, u32[]{:S(2)}) collective-permute-start(bf16[16,32,128]{2,1,0:T(8,128)(2,1)S(1)} %project.5), channel_id=1, source_target_pairs={{0,4},{1,5},{2,6},{3,7},{4,2},{5,3},{6,0},{7,1},{8,12},{9,13},{10,... | collective-permute-start | bytes 393224 | tf_op jit(solution)/shard_map/ppermute | solution.py:279
  64.3 3.2 %collective-permute-start.34 = (bf16[16,32,128]{2,1,0:T(8,128)(2,1)S(1)}, bf16[16,32,128]{2,1,0:T(8,128)(2,1)S(1)}, u32[]{:S(2)}, u32[]{:S(2)}) collective-permute-start(bf16[16,32,128]{2,1,0:T(8,128)(2,1)S(1)} %project.5), channel_id=1, source_target_pairs={{0,4},{1,5},{2,6},{3,7},{4,1},{5,0},{6,3},{7,2},{8,12},{9,13},{10,... | collective-permute-start | bytes 393224 | tf_op jit(solution)/shard_map/ppermute | solution.py:279
  64.8 2.6 %collective-permute-start.33 = (bf16[16,32,128]{2,1,0:T(8,128)(2,1)S(1)}, bf16[16,32,128]{2,1,0:T(8,128)(2,1)S(1)}, u32[]{:S(2)}, u32[]{:S(2)}) collective-permute-start(bf16[16,32,128]{2,1,0:T(8,128)(2,1)S(1)} %project.5), channel_id=1, source_target_pairs={{0,4},{1,5},{2,6},{3,7},{4,0},{5,1},{6,2},{7,3},{8,12},{9,13},{10,... | collective-permute-start | bytes 393224 | tf_op jit(solution)/shard_map/ppermute | solution.py:279
  64.8 2.6 %collective-permute-start.37 = (bf16[32,32,128]{2,1,0:T(8,128)(2,1)S(1)}, bf16[32,32,128]{2,1,0:T(8,128)(2,1)S(1)}, u32[]{:S(2)}, u32[]{:S(2)}) collective-permute-start(bf16[32,32,128]{2,1,0:T(8,128)(2,1)S(1)} %collective-permute-done.32.image), channel_id=1, source_target_pairs={{0,4},{1,5},{2,6},{3,7},{4,0},{5,1},{6,2},{7,3},{8,12},{9,13},{10,... | collective-permute-start | bytes 786440 | tf_op jit(solution)/shard_map/ppermute | solution.py:279
  67.5 6.8 %collective-permute-start.41 = (bf16[16,32,128]{2,1,0:T(8,128)(2,1)S(1)}, bf16[16,32,128]{2,1,0:T(8,128)(2,1)S(1)}, u32[]{:S(2)}, u32[]{:S(2)}) collective-permute-start(bf16[16,32,128]{2,1,0:T(8,128)(2,1)S(1)} %get-tuple-element.46), channel_id=1, source_target_pairs={{0,7},{1,6},{2,5},{3,4},{4,0},{5,1},{6,2},{7,3},{8,15},{9,14},{10,... | collective-permute-start | bytes 393224 | tf_op jit(solution)/shard_map/ppermute | solution.py:279
  70.7 4.9 %collective-permute-start.40 = (bf16[16,32,128]{2,1,0:T(8,128)(2,1)S(1)}, bf16[16,32,128]{2,1,0:T(8,128)(2,1)S(1)}, u32[]{:S(2)}, u32[]{:S(2)}) collective-permute-start(bf16[16,32,128]{2,1,0:T(8,128)(2,1)S(1)} %get-tuple-element.46), channel_id=1, source_target_pairs={{0,6},{1,7},{2,4},{3,5},{4,0},{5,1},{6,2},{7,3},{8,14},{9,15},{10,... | collective-permute-start | bytes 393224 | tf_op jit(solution)/shard_map/ppermute | solution.py:279
  70.8 4.9 %collective-permute-start.39 = (bf16[16,32,128]{2,1,0:T(8,128)(2,1)S(1)}, bf16[16,32,128]{2,1,0:T(8,128)(2,1)S(1)}, u32[]{:S(2)}, u32[]{:S(2)}) collective-permute-start(bf16[16,32,128]{2,1,0:T(8,128)(2,1)S(1)} %get-tuple-element.46), channel_id=1, source_target_pairs={{0,5},{1,4},{2,7},{3,6},{4,0},{5,1},{6,2},{7,3},{8,13},{9,12},{10,... | collective-permute-start | bytes 393224 | tf_op jit(solution)/shard_map/ppermute | solution.py:279
  71.7 3.9 %collective-permute-start.38 = (bf16[16,32,128]{2,1,0:T(8,128)(2,1)S(1)}, bf16[16,32,128]{2,1,0:T(8,128)(2,1)S(1)}, u32[]{:S(2)}, u32[]{:S(2)}) collective-permute-start(bf16[16,32,128]{2,1,0:T(8,128)(2,1)S(1)} %get-tuple-element.46), channel_id=1, source_target_pairs={{0,4},{1,5},{2,6},{3,7},{4,0},{5,1},{6,2},{7,3},{8,12},{9,13},{10,... | collective-permute-start | bytes 393224 | tf_op jit(solution)/shard_map/ppermute | solution.py:279
  71.7 4.5 %collective-permute-start.42 = (bf16[32,32,128]{2,1,0:T(8,128)(2,1)S(1)}, bf16[32,32,128]{2,1,0:T(8,128)(2,1)S(1)}, u32[]{:S(2)}, u32[]{:S(2)}) collective-permute-start(bf16[32,32,128]{2,1,0:T(8,128)(2,1)S(1)} %get-tuple-element.47.refs_3_), channel_id=1, source_target_pairs={{0,4},{1,5},{2,6},{3,7},{4,0},{5,1},{6,2},{7,3},{8,12},{9,13},{10,... | collective-permute-start | bytes 786440 | tf_op jit(solution)/shard_map/ppermute | solution.py:279

commit v14 on v13

--- a/solution.py
+++ b/solution.py
@@ -396,9 +396,11 @@
             before = []
         else:
             def hop(p, c, t):
-                if c == 1 and p in (place - 1, place):
-                    return 2 * place - 1 - p, c, t
-                return p, c, t ^ 1
+                if p == place - 1:
+                    return (place, 1, t) if c else (p, 1, t)
+                if p == place:
+                    return (p, 0, t) if c else (place - 1, 0, t)
+                return p, 1 - c, t
 
             image = sent(image, hop)
             terms = call(

time: 77.2 us -> 71.1 us (0.921)
  waiting for transfers between devices: 40.1 us -> 35.7 us
  starting transfers between devices: 29.4 us -> 27.7 us
    ppermute x43, waiting for transfers between devices: 40.1 us -> 35.7 us  [sent(): return lax.ppermute(value, ('subset', 'tile'), pairs)]
    ppermute x43, starting transfers between devices: 29.4 us -> 27.7 us  [sent(): return lax.ppermute(value, ('subset', 'tile'), pairs)]
  transfers between devices with their start and end apart: 43 -> 43, of which waited for: 20 -> 18; matrix products, arithmetic and copies ran while one was open for 0% -> 0% of each run, Pallas kernels for 7% -> 8%
where the time goes in v14:
time: 71.1 us; the launch traced here: 71 us
  waiting for transfers between devices  35.7 us (50%)
  starting transfers between devices  27.7 us (39%)
  Pallas kernels  7.22 us (10%)
    ppermute x43, waiting for transfers between devices, sent(): return lax.ppermute(value, ('subset', 'tile'), pairs)  35.7 us
    ppermute x43, starting transfers between devices, sent(): return lax.ppermute(value, ('subset', 'tile'), pairs)  27.7 us
    pallas_call x1, Pallas kernels, per_device(): pl.pallas_call(functools.partial(head_kernel, row_blocks, chunks), out_sh...  3.09 us
    pallas_call x19, Pallas kernels, call(): pl.pallas_call(kernel, out_shape=out_shape, in_specs=[SMEM] * smem + [VME...  2.33 us
  transfers between devices with their start and end apart: 43, of which 18 were waited for; matrix products, arithmetic and copies ran while one was open for 0% of the time, Pallas kernels for 8%

profile of v14, /device:TPU:25, one launch (start us, length us, event | category | flops | bytes accessed | tf_op | source)
XLA Modules:
  0.0 71.0 jit_solution(3089390621258760485)
XLA Ops:
  0.0 0.7 collective-permute-start.1
  0.8 3.1 %head.1 = (bf16[5,32,128]{2,1,0:T(8,128)(2,1)S(1)}, s32[2,80]{1,0:T(2,128)S(1)}, s32[3,80]{1,0:T(4,128)S(4)}, bf16[1,1,80,128,128]{4,3,2,1,0:T(8,128)(2,1)S(1)}) custom-call(s32[3]{0:T(128)S(1)} %pad_add_fusion.pos, s32[1,1,80]{2,1,0:T(1,128)} %rows_in.1, s32[1,1,80]{2,1,0:T(1,128)} %cols_in.1, bf16[1,1,80,128,128]{4,3,2,1,0:T(8,128)(2,1)} %blocks_in.1, ...), custom_call_target="tpu_custom_call" | custom-call | tf_op jit(solution)/shard_map/head/pallas_call | solution.py:315
  3.9 2.2 %collective-permute-start.4 = (bf16[5,32,128]{2,1,0:T(8,128)(2,1)S(1)}, bf16[5,32,128]{2,1,0:T(8,128)(2,1)S(1)}, u32[]{:S(2)}, u32[]{:S(2)}) collective-permute-start(bf16[5,32,128]{2,1,0:T(8,128)(2,1)S(1)} %get-tuple-element.31._.refs_2_), channel_id=1, source_target_pairs={{0,3},{1,2},{2,1},{3,0},{4,7},{5,6},{6,5},{7,4},{8,11},{9,10},{10,... | collective-permute-start | bytes 122888 | tf_op jit(solution)/shard_map/ppermute | solution.py:279
  6.3 0.3 collective-permute-start.2
  6.6 0.8 %collective-permute-start = (s32[2,80]{1,0:T(2,128)S(1)}, s32[2,80]{1,0:T(2,128)S(1)}, u32[]{:S(2)}, u32[]{:S(2)}) collective-permute-start(s32[2,80]{1,0:T(2,128)S(1)} %get-tuple-element.28), channel_id=1, source_target_pairs={{0,4},{1,5},{2,6},{3,7},{4,0},{5,1},{6,2},{7,3},{8,12},{9,13},{10,... | collective-permute-start | bytes 1928 | tf_op jit(solution)/shard_map/ppermute | solution.py:279
  7.4 0.5 pack_own.1.refs_1_
  7.9 0.3 collective-permute-done.table2
  8.2 1.3 %pack_other.1 = (s32[3,80]{1,0:T(4,128)S(4)}, bf16[16,640,128]{2,1,0:T(8,128)(2,1)S(1)}) custom-call(s32[3,80]{1,0:T(4,128)S(4)} %get-tuple-element.27.own, s32[2,80]{1,0:T(2,128)S(1)} %collective-permute-done.table2, bf16[1,1,80,128,128]{4,3,2,1,0:T(8,128)(2,1)S(1)} %collective-permute-done.1.blocks2), custom_call_target="tpu_custom_call" | custom-call | tf_op jit(solution)/shard_map/pack_other/pallas_call | solution.py:356
  9.7 1.3 %collective-permute-start.8 = (bf16[16,32,128]{2,1,0:T(8,128)(2,1)S(1)}, bf16[16,32,128]{2,1,0:T(8,128)(2,1)S(1)}, u32[]{:S(2)}, u32[]{:S(2)}) collective-permute-start(bf16[16,32,128]{2,1,0:T(8,128)(2,1)S(1)} %get-tuple-element.35), channel_id=1, source_target_pairs={{0,7},{1,6},{2,5},{3,4},{4,0},{5,1},{6,2},{7,3},{8,15},{9,14},{10,... | collective-permute-start | bytes 393224 | tf_op jit(solution)/shard_map/ppermute | solution.py:279
  11.0 1.3 %collective-permute-start.7 = (bf16[16,32,128]{2,1,0:T(8,128)(2,1)S(1)}, bf16[16,32,128]{2,1,0:T(8,128)(2,1)S(1)}, u32[]{:S(2)}, u32[]{:S(2)}) collective-permute-start(bf16[16,32,128]{2,1,0:T(8,128)(2,1)S(1)} %get-tuple-element.35), channel_id=1, source_target_pairs={{0,6},{1,7},{2,4},{3,5},{4,0},{5,1},{6,2},{7,3},{8,14},{9,15},{10,... | collective-permute-start | bytes 393224 | tf_op jit(solution)/shard_map/ppermute | solution.py:279
  12.3 0.3 collective-permute-start.6
  12.6 0.3 collective-permute-start.5
  13.1 2.0 %collective-permute-done.8.refs_6_ = bf16[16,32,128]{2,1,0:T(8,128)(2,1)S(1)} collective-permute-done((bf16[16,32,128]{2,1,0:T(8,128)(2,1)S(1)}, bf16[16,32,128]{2,1,0:T(8,128)(2,1)S(1)}, u32[]{:S(2)}, u32[]{:S(2)}) %collective-permute-start.8) | collective-permute-done | bytes 131104 | tf_op jit(solution)/shard_map/ppermute | solution.py:279
  15.1 1.3 %collective-permute-done.7.refs_5_ = bf16[16,32,128]{2,1,0:T(8,128)(2,1)S(1)} collective-permute-done((bf16[16,32,128]{2,1,0:T(8,128)(2,1)S(1)}, bf16[16,32,128]{2,1,0:T(8,128)(2,1)S(1)}, u32[]{:S(2)}, u32[]{:S(2)}) %collective-permute-start.7) | collective-permute-done | bytes 131104 | tf_op jit(solution)/shard_map/ppermute | solution.py:279
  16.4 0.3 collective-permute-done.6.refs_4_
  16.8 1.5 %collective-permute-done.10.image = bf16[32,32,128]{2,1,0:T(8,128)(2,1)S(1)} collective-permute-done((bf16[32,32,128]{2,1,0:T(8,128)(2,1)S(1)}, bf16[32,32,128]{2,1,0:T(8,128)(2,1)S(1)}, u32[]{:S(2)}, u32[]{:S(2)}) %collective-permute-start.10) | collective-permute-done | bytes 262176 | tf_op jit(solution)/shard_map/ppermute | solution.py:279
  18.3 1.4 %collective-permute-start.14 = (bf16[16,32,128]{2,1,0:T(8,128)(2,1)S(1)}, bf16[16,32,128]{2,1,0:T(8,128)(2,1)S(1)}, u32[]{:S(2)}, u32[]{:S(2)}) collective-permute-start(bf16[16,32,128]{2,1,0:T(8,128)(2,1)S(1)} %project.3), channel_id=1, source_target_pairs={{0,4},{1,5},{2,6},{3,7},{4,3},{5,2},{6,1},{7,0},{8,12},{9,13},{10,... | collective-permute-start | bytes 393224 | tf_op jit(solution)/shard_map/ppermute | solution.py:279
  19.7 1.2 %collective-permute-start.12 = (bf16[16,32,128]{2,1,0:T(8,128)(2,1)S(1)}, bf16[16,32,128]{2,1,0:T(8,128)(2,1)S(1)}, u32[]{:S(2)}, u32[]{:S(2)}) collective-permute-start(bf16[16,32,128]{2,1,0:T(8,128)(2,1)S(1)} %project.3), channel_id=1, source_target_pairs={{0,4},{1,5},{2,6},{3,7},{4,1},{5,0},{6,3},{7,2},{8,12},{9,13},{10,... | collective-permute-start | bytes 393224 | tf_op jit(solution)/shard_map/ppermute | solution.py:279
  20.9 0.5 collective-permute-start.15
  21.6 1.4 %collective-permute-done.13.refs_5_ = bf16[16,32,128]{2,1,0:T(8,128)(2,1)S(1)} collective-permute-done((bf16[16,32,128]{2,1,0:T(8,128)(2,1)S(1)}, bf16[16,32,128]{2,1,0:T(8,128)(2,1)S(1)}, u32[]{:S(2)}, u32[]{:S(2)}) %collective-permute-start.13) | collective-permute-done | bytes 131104 | tf_op jit(solution)/shard_map/ppermute | solution.py:279
  23.0 2.1 %collective-permute-start.19 = (bf16[16,32,128]{2,1,0:T(8,128)(2,1)S(1)}, bf16[16,32,128]{2,1,0:T(8,128)(2,1)S(1)}, u32[]{:S(2)}, u32[]{:S(2)}) collective-permute-start(bf16[16,32,128]{2,1,0:T(8,128)(2,1)S(1)} %get-tuple-element.38), channel_id=1, source_target_pairs={{0,7},{1,6},{2,5},{3,4},{4,0},{5,1},{6,2},{7,3},{8,15},{9,14},{10,... | collective-permute-start | bytes 393224 | tf_op jit(solution)/shard_map/ppermute | solution.py:279
  25.2 0.9 %collective-permute-start.17 = (bf16[16,32,128]{2,1,0:T(8,128)(2,1)S(1)}, bf16[16,32,128]{2,1,0:T(8,128)(2,1)S(1)}, u32[]{:S(2)}, u32[]{:S(2)}) collective-permute-start(bf16[16,32,128]{2,1,0:T(8,128)(2,1)S(1)} %get-tuple-element.38), channel_id=1, source_target_pairs={{0,5},{1,4},{2,7},{3,6},{4,0},{5,1},{6,2},{7,3},{8,13},{9,12},{10,... | collective-permute-start | bytes 393224 | tf_op jit(solution)/shard_map/ppermute | solution.py:279
  26.2 0.4 collective-permute-start.20
  26.6 2.3 %collective-permute-done.19.refs_6_ = bf16[16,32,128]{2,1,0:T(8,128)(2,1)S(1)} collective-permute-done((bf16[16,32,128]{2,1,0:T(8,128)(2,1)S(1)}, bf16[16,32,128]{2,1,0:T(8,128)(2,1)S(1)}, u32[]{:S(2)}, u32[]{:S(2)}) %collective-permute-start.19) | collective-permute-done | bytes 131104 | tf_op jit(solution)/shard_map/ppermute | solution.py:279
  28.9 1.3 %collective-permute-done.18.refs_5_ = bf16[16,32,128]{2,1,0:T(8,128)(2,1)S(1)} collective-permute-done((bf16[16,32,128]{2,1,0:T(8,128)(2,1)S(1)}, bf16[16,32,128]{2,1,0:T(8,128)(2,1)S(1)}, u32[]{:S(2)}, u32[]{:S(2)}) %collective-permute-start.18) | collective-permute-done | bytes 131104 | tf_op jit(solution)/shard_map/ppermute | solution.py:279
  30.4 1.5 %collective-permute-done.21.image = bf16[32,32,128]{2,1,0:T(8,128)(2,1)S(1)} collective-permute-done((bf16[32,32,128]{2,1,0:T(8,128)(2,1)S(1)}, bf16[32,32,128]{2,1,0:T(8,128)(2,1)S(1)}, u32[]{:S(2)}, u32[]{:S(2)}) %collective-permute-start.21) | collective-permute-done | bytes 262176 | tf_op jit(solution)/shard_map/ppermute | solution.py:279
  31.9 1.2 %collective-permute-start.25 = (bf16[16,32,128]{2,1,0:T(8,128)(2,1)S(1)}, bf16[16,32,128]{2,1,0:T(8,128)(2,1)S(1)}, u32[]{:S(2)}, u32[]{:S(2)}) collective-permute-start(bf16[16,32,128]{2,1,0:T(8,128)(2,1)S(1)} %project.4), channel_id=1, source_target_pairs={{0,4},{1,5},{2,6},{3,7},{4,3},{5,2},{6,1},{7,0},{8,12},{9,13},{10,... | collective-permute-start | bytes 393224 | tf_op jit(solution)/shard_map/ppermute | solution.py:279
  33.1 1.0 %collective-permute-start.23 = (bf16[16,32,128]{2,1,0:T(8,128)(2,1)S(1)}, bf16[16,32,128]{2,1,0:T(8,128)(2,1)S(1)}, u32[]{:S(2)}, u32[]{:S(2)}) collective-permute-start(bf16[16,32,128]{2,1,0:T(8,128)(2,1)S(1)} %project.4), channel_id=1, source_target_pairs={{0,4},{1,5},{2,6},{3,7},{4,1},{5,0},{6,3},{7,2},{8,12},{9,13},{10,... | collective-permute-start | bytes 393224 | tf_op jit(solution)/shard_map/ppermute | solution.py:279
  34.2 0.5 collective-permute-start.26
  34.7 0.4 collective-permute-done.25.refs_6_
  35.1 1.4 %collective-permute-done.24.refs_5_ = bf16[16,32,128]{2,1,0:T(8,128)(2,1)S(1)} collective-permute-done((bf16[16,32,128]{2,1,0:T(8,128)(2,1)S(1)}, bf16[16,32,128]{2,1,0:T(8,128)(2,1)S(1)}, u32[]{:S(2)}, u32[]{:S(2)}) %collective-permute-start.24) | collective-permute-done | bytes 131104 | tf_op jit(solution)/shard_map/ppermute | solution.py:279
  36.5 1.9 %collective-permute-start.30 = (bf16[16,32,128]{2,1,0:T(8,128)(2,1)S(1)}, bf16[16,32,128]{2,1,0:T(8,128)(2,1)S(1)}, u32[]{:S(2)}, u32[]{:S(2)}) collective-permute-start(bf16[16,32,128]{2,1,0:T(8,128)(2,1)S(1)} %get-tuple-element.42), channel_id=1, source_target_pairs={{0,7},{1,6},{2,5},{3,4},{4,0},{5,1},{6,2},{7,3},{8,15},{9,14},{10,... | collective-permute-start | bytes 393224 | tf_op jit(solution)/shard_map/ppermute | solution.py:279
  38.4 1.2 %collective-permute-start.28 = (bf16[16,32,128]{2,1,0:T(8,128)(2,1)S(1)}, bf16[16,32,128]{2,1,0:T(8,128)(2,1)S(1)}, u32[]{:S(2)}, u32[]{:S(2)}) collective-permute-start(bf16[16,32,128]{2,1,0:T(8,128)(2,1)S(1)} %get-tuple-element.42), channel_id=1, source_target_pairs={{0,5},{1,4},{2,7},{3,6},{4,0},{5,1},{6,2},{7,3},{8,13},{9,12},{10,... | collective-permute-start | bytes 393224 | tf_op jit(solution)/shard_map/ppermute | solution.py:279
  39.6 0.5 collective-permute-start.31
  40.1 2.0 %collective-permute-done.30.refs_6_ = bf16[16,32,128]{2,1,0:T(8,128)(2,1)S(1)} collective-permute-done((bf16[16,32,128]{2,1,0:T(8,128)(2,1)S(1)}, bf16[16,32,128]{2,1,0:T(8,128)(2,1)S(1)}, u32[]{:S(2)}, u32[]{:S(2)}) %collective-permute-start.30) | collective-permute-done | bytes 131104 | tf_op jit(solution)/shard_map/ppermute | solution.py:279
  42.1 1.3 %collective-permute-done.29.refs_5_ = bf16[16,32,128]{2,1,0:T(8,128)(2,1)S(1)} collective-permute-done((bf16[16,32,128]{2,1,0:T(8,128)(2,1)S(1)}, bf16[16,32,128]{2,1,0:T(8,128)(2,1)S(1)}, u32[]{:S(2)}, u32[]{:S(2)}) %collective-permute-start.29) | collective-permute-done | bytes 131104 | tf_op jit(solution)/shard_map/ppermute | solution.py:279
  43.8 13.1 %collective-permute-done.32.image = bf16[32,32,128]{2,1,0:T(8,128)(2,1)S(1)} collective-permute-done((bf16[32,32,128]{2,1,0:T(8,128)(2,1)S(1)}, bf16[32,32,128]{2,1,0:T(8,128)(2,1)S(1)}, u32[]{:S(2)}, u32[]{:S(2)}) %collective-permute-start.32) | collective-permute-done | bytes 262176 | tf_op jit(solution)/shard_map/ppermute | solution.py:279
  56.9 0.5 project.5
  57.5 1.4 %collective-permute-start.35 = (bf16[16,32,128]{2,1,0:T(8,128)(2,1)S(1)}, bf16[16,32,128]{2,1,0:T(8,128)(2,1)S(1)}, u32[]{:S(2)}, u32[]{:S(2)}) collective-permute-start(bf16[16,32,128]{2,1,0:T(8,128)(2,1)S(1)} %project.5), channel_id=1, source_target_pairs={{0,4},{1,5},{2,6},{3,7},{4,2},{5,3},{6,0},{7,1},{8,12},{9,13},{10,... | collective-permute-start | bytes 393224 | tf_op jit(solution)/shard_map/ppermute | solution.py:279
  59.0 0.4 collective-permute-start.33
  59.6 2.1 %collective-permute-done.35.refs_5_ = bf16[16,32,128]{2,1,0:T(8,128)(2,1)S(1)} collective-permute-done((bf16[16,32,128]{2,1,0:T(8,128)(2,1)S(1)}, bf16[16,32,128]{2,1,0:T(8,128)(2,1)S(1)}, u32[]{:S(2)}, u32[]{:S(2)}) %collective-permute-start.35) | collective-permute-done | bytes 131104 | tf_op jit(solution)/shard_map/ppermute | solution.py:279
  61.7 3.0 %collective-permute-start.41 = (bf16[16,32,128]{2,1,0:T(8,128)(2,1)S(1)}, bf16[16,32,128]{2,1,0:T(8,128)(2,1)S(1)}, u32[]{:S(2)}, u32[]{:S(2)}) collective-permute-start(bf16[16,32,128]{2,1,0:T(8,128)(2,1)S(1)} %get-tuple-element.46), channel_id=1, source_target_pairs={{0,7},{1,6},{2,5},{3,4},{4,0},{5,1},{6,2},{7,3},{8,15},{9,14},{10,... | collective-permute-start | bytes 393224 | tf_op jit(solution)/shard_map/ppermute | solution.py:279
  64.7 1.2 %collective-permute-start.39 = (bf16[16,32,128]{2,1,0:T(8,128)(2,1)S(1)}, bf16[16,32,128]{2,1,0:T(8,128)(2,1)S(1)}, u32[]{:S(2)}, u32[]{:S(2)}) collective-permute-start(bf16[16,32,128]{2,1,0:T(8,128)(2,1)S(1)} %get-tuple-element.46), channel_id=1, source_target_pairs={{0,5},{1,4},{2,7},{3,6},{4,0},{5,1},{6,2},{7,3},{8,13},{9,12},{10,... | collective-permute-start | bytes 393224 | tf_op jit(solution)/shard_map/ppermute | solution.py:279
  65.9 0.5 collective-permute-start.42
  66.4 1.8 %collective-permute-done.41.refs_6_ = bf16[16,32,128]{2,1,0:T(8,128)(2,1)S(1)} collective-permute-done((bf16[16,32,128]{2,1,0:T(8,128)(2,1)S(1)}, bf16[16,32,128]{2,1,0:T(8,128)(2,1)S(1)}, u32[]{:S(2)}, u32[]{:S(2)}) %collective-permute-start.41) | collective-permute-done | bytes 131104 | tf_op jit(solution)/shard_map/ppermute | solution.py:279
  68.2 1.3 %collective-permute-done.40.refs_5_ = bf16[16,32,128]{2,1,0:T(8,128)(2,1)S(1)} collective-permute-done((bf16[16,32,128]{2,1,0:T(8,128)(2,1)S(1)}, bf16[16,32,128]{2,1,0:T(8,128)(2,1)S(1)}, u32[]{:S(2)}, u32[]{:S(2)}) %collective-permute-start.40) | collective-permute-done | bytes 131104 | tf_op jit(solution)/shard_map/ppermute | solution.py:279
  69.6 0.6 update.15.refs_1_
  70.2 0.8 %second.7 = bf16[4,8,4096]{2,1,0:T(8,128)(2,1)} custom-call(s32[3,80]{1,0:T(4,128)S(4)} %get-tuple-element.29.refs_0_.info, f32[32,32,128]{2,1,0:T(8,128)S(1)} %update.15.refs_1_, bf16[32,32,128]{2,1,0:T(8,128)(2,1)S(1)} %collective-permute-done.42.refs_2_, bf16[32,32,128]{2,1,0:T(8,128)(2,1)S(1)} %get-tuple-element.47.refs_3_, ...), custom_call_target="tpu_custom_call" | custom-call | tf_op jit(solution)/shard_map/second/pallas_call | solution.py:300
  (61 shorter events, 2.2 us)
Async XLA Ops:
  0.0 8.2 %collective-permute-start.1 = (bf16[1,1,80,128,128]{4,3,2,1,0:T(8,128)(2,1)}, bf16[1,1,80,128,128]{4,3,2,1,0:T(8,128)(2,1)S(1)}, u32[]{:S(2)}, u32[]{:S(2)}) collective-permute-start(bf16[1,1,80,128,128]{4,3,2,1,0:T(8,128)(2,1)} %blocks_in.1), channel_id=1, source_target_pairs={{0,4},{1,5},{2,6},{3,7},{4,0},{5,1},{6,2},{7,3},{8,12},{9,13},{10,... | collective-permute-start | bytes 7864328 | tf_op jit(solution)/shard_map/ppermute | solution.py:279
  3.9 5.7 %collective-permute-start.4 = (bf16[5,32,128]{2,1,0:T(8,128)(2,1)S(1)}, bf16[5,32,128]{2,1,0:T(8,128)(2,1)S(1)}, u32[]{:S(2)}, u32[]{:S(2)}) collective-permute-start(bf16[5,32,128]{2,1,0:T(8,128)(2,1)S(1)} %get-tuple-element.31._.refs_2_), channel_id=1, source_target_pairs={{0,3},{1,2},{2,1},{3,0},{4,7},{5,6},{6,5},{7,4},{8,11},{9,10},{10,... | collective-permute-start | bytes 122888 | tf_op jit(solution)/shard_map/ppermute | solution.py:279
  6.1 3.5 %collective-permute-start.3 = (bf16[5,32,128]{2,1,0:T(8,128)(2,1)S(1)}, bf16[5,32,128]{2,1,0:T(8,128)(2,1)S(1)}, u32[]{:S(2)}, u32[]{:S(2)}) collective-permute-start(bf16[5,32,128]{2,1,0:T(8,128)(2,1)S(1)} %get-tuple-element.31._.refs_2_), channel_id=1, source_target_pairs={{0,2},{1,3},{2,0},{3,1},{4,6},{5,7},{6,4},{7,5},{8,10},{9,11},{10,... | collective-permute-start | bytes 122888 | tf_op jit(solution)/shard_map/ppermute | solution.py:279
  6.3 3.3 %collective-permute-start.2 = (bf16[5,32,128]{2,1,0:T(8,128)(2,1)S(1)}, bf16[5,32,128]{2,1,0:T(8,128)(2,1)S(1)}, u32[]{:S(2)}, u32[]{:S(2)}) collective-permute-start(bf16[5,32,128]{2,1,0:T(8,128)(2,1)S(1)} %get-tuple-element.31._.refs_2_), channel_id=1, source_target_pairs={{0,1},{1,0},{2,3},{3,2},{4,5},{5,4},{6,7},{7,6},{8,9},{9,8},{10,11... | collective-permute-start | bytes 122888 | tf_op jit(solution)/shard_map/ppermute | solution.py:279
  6.6 1.7 %collective-permute-start = (s32[2,80]{1,0:T(2,128)S(1)}, s32[2,80]{1,0:T(2,128)S(1)}, u32[]{:S(2)}, u32[]{:S(2)}) collective-permute-start(s32[2,80]{1,0:T(2,128)S(1)} %get-tuple-element.28), channel_id=1, source_target_pairs={{0,4},{1,5},{2,6},{3,7},{4,0},{5,1},{6,2},{7,3},{8,12},{9,13},{10,... | collective-permute-start | bytes 1928 | tf_op jit(solution)/shard_map/ppermute | solution.py:279
  9.7 5.4 %collective-permute-start.8 = (bf16[16,32,128]{2,1,0:T(8,128)(2,1)S(1)}, bf16[16,32,128]{2,1,0:T(8,128)(2,1)S(1)}, u32[]{:S(2)}, u32[]{:S(2)}) collective-permute-start(bf16[16,32,128]{2,1,0:T(8,128)(2,1)S(1)} %get-tuple-element.35), channel_id=1, source_target_pairs={{0,7},{1,6},{2,5},{3,4},{4,0},{5,1},{6,2},{7,3},{8,15},{9,14},{10,... | collective-permute-start | bytes 393224 | tf_op jit(solution)/shard_map/ppermute | solution.py:279
  11.0 5.4 %collective-permute-start.7 = (bf16[16,32,128]{2,1,0:T(8,128)(2,1)S(1)}, bf16[16,32,128]{2,1,0:T(8,128)(2,1)S(1)}, u32[]{:S(2)}, u32[]{:S(2)}) collective-permute-start(bf16[16,32,128]{2,1,0:T(8,128)(2,1)S(1)} %get-tuple-element.35), channel_id=1, source_target_pairs={{0,6},{1,7},{2,4},{3,5},{4,0},{5,1},{6,2},{7,3},{8,14},{9,15},{10,... | collective-permute-start | bytes 393224 | tf_op jit(solution)/shard_map/ppermute | solution.py:279
  12.3 4.4 %collective-permute-start.6 = (bf16[16,32,128]{2,1,0:T(8,128)(2,1)S(1)}, bf16[16,32,128]{2,1,0:T(8,128)(2,1)S(1)}, u32[]{:S(2)}, u32[]{:S(2)}) collective-permute-start(bf16[16,32,128]{2,1,0:T(8,128)(2,1)S(1)} %get-tuple-element.35), channel_id=1, source_target_pairs={{0,5},{1,4},{2,7},{3,6},{4,0},{5,1},{6,2},{7,3},{8,13},{9,12},{10,... | collective-permute-start | bytes 393224 | tf_op jit(solution)/shard_map/ppermute | solution.py:279
  12.6 4.1 %collective-permute-start.5 = (bf16[16,32,128]{2,1,0:T(8,128)(2,1)S(1)}, bf16[16,32,128]{2,1,0:T(8,128)(2,1)S(1)}, u32[]{:S(2)}, u32[]{:S(2)}) collective-permute-start(bf16[16,32,128]{2,1,0:T(8,128)(2,1)S(1)} %get-tuple-element.35), channel_id=1, source_target_pairs={{0,4},{1,5},{2,6},{3,7},{4,0},{5,1},{6,2},{7,3},{8,12},{9,13},{10,... | collective-permute-start | bytes 393224 | tf_op jit(solution)/shard_map/ppermute | solution.py:279
  12.9 3.7 %collective-permute-start.9 = (bf16[32,32,128]{2,1,0:T(8,128)(2,1)S(1)}, bf16[32,32,128]{2,1,0:T(8,128)(2,1)S(1)}, u32[]{:S(2)}, u32[]{:S(2)}) collective-permute-start(bf16[32,32,128]{2,1,0:T(8,128)(2,1)S(1)} %get-tuple-element.36.refs_3_), channel_id=1, source_target_pairs={{0,4},{1,5},{2,6},{3,7},{4,0},{5,1},{6,2},{7,3},{8,12},{9,13},{10,... | collective-permute-start | bytes 786440 | tf_op jit(solution)/shard_map/ppermute | solution.py:279
  16.7 1.6 %collective-permute-start.10 = (bf16[32,32,128]{2,1,0:T(8,128)(2,1)S(1)}, bf16[32,32,128]{2,1,0:T(8,128)(2,1)S(1)}, u32[]{:S(2)}, u32[]{:S(2)}) collective-permute-start(bf16[32,32,128]{2,1,0:T(8,128)(2,1)S(1)} %get-tuple-element.37), channel_id=1, source_target_pairs={{0,4},{1,5},{2,6},{3,7},{4,12},{5,13},{6,14},{7,15},{8,0},{9,1},{1... | collective-permute-start | bytes 786440 | tf_op jit(solution)/shard_map/ppermute | solution.py:279
  18.3 3.3 %collective-permute-start.14 = (bf16[16,32,128]{2,1,0:T(8,128)(2,1)S(1)}, bf16[16,32,128]{2,1,0:T(8,128)(2,1)S(1)}, u32[]{:S(2)}, u32[]{:S(2)}) collective-permute-start(bf16[16,32,128]{2,1,0:T(8,128)(2,1)S(1)} %project.3), channel_id=1, source_target_pairs={{0,4},{1,5},{2,6},{3,7},{4,3},{5,2},{6,1},{7,0},{8,12},{9,13},{10,... | collective-permute-start | bytes 393224 | tf_op jit(solution)/shard_map/ppermute | solution.py:279
  19.7 3.3 %collective-permute-start.13 = (bf16[16,32,128]{2,1,0:T(8,128)(2,1)S(1)}, bf16[16,32,128]{2,1,0:T(8,128)(2,1)S(1)}, u32[]{:S(2)}, u32[]{:S(2)}) collective-permute-start(bf16[16,32,128]{2,1,0:T(8,128)(2,1)S(1)} %project.3), channel_id=1, source_target_pairs={{0,4},{1,5},{2,6},{3,7},{4,2},{5,3},{6,0},{7,1},{8,12},{9,13},{10,... | collective-permute-start | bytes 393224 | tf_op jit(solution)/shard_map/ppermute | solution.py:279
  19.7 3.3 %collective-permute-start.12 = (bf16[16,32,128]{2,1,0:T(8,128)(2,1)S(1)}, bf16[16,32,128]{2,1,0:T(8,128)(2,1)S(1)}, u32[]{:S(2)}, u32[]{:S(2)}) collective-permute-start(bf16[16,32,128]{2,1,0:T(8,128)(2,1)S(1)} %project.3), channel_id=1, source_target_pairs={{0,4},{1,5},{2,6},{3,7},{4,1},{5,0},{6,3},{7,2},{8,12},{9,13},{10,... | collective-permute-start | bytes 393224 | tf_op jit(solution)/shard_map/ppermute | solution.py:279
  20.9 2.1 %collective-permute-start.11 = (bf16[16,32,128]{2,1,0:T(8,128)(2,1)S(1)}, bf16[16,32,128]{2,1,0:T(8,128)(2,1)S(1)}, u32[]{:S(2)}, u32[]{:S(2)}) collective-permute-start(bf16[16,32,128]{2,1,0:T(8,128)(2,1)S(1)} %project.3), channel_id=1, source_target_pairs={{0,4},{1,5},{2,6},{3,7},{4,0},{5,1},{6,2},{7,3},{8,12},{9,13},{10,... | collective-permute-start | bytes 393224 | tf_op jit(solution)/shard_map/ppermute | solution.py:279
  20.9 2.1 %collective-permute-start.15 = (bf16[32,32,128]{2,1,0:T(8,128)(2,1)S(1)}, bf16[32,32,128]{2,1,0:T(8,128)(2,1)S(1)}, u32[]{:S(2)}, u32[]{:S(2)}) collective-permute-start(bf16[32,32,128]{2,1,0:T(8,128)(2,1)S(1)} %collective-permute-done.10.image), channel_id=1, source_target_pairs={{0,4},{1,5},{2,6},{3,7},{4,0},{5,1},{6,2},{7,3},{8,12},{9,13},{10,... | collective-permute-start | bytes 786440 | tf_op jit(solution)/shard_map/ppermute | solution.py:279
  23.0 5.9 %collective-permute-start.19 = (bf16[16,32,128]{2,1,0:T(8,128)(2,1)S(1)}, bf16[16,32,128]{2,1,0:T(8,128)(2,1)S(1)}, u32[]{:S(2)}, u32[]{:S(2)}) collective-permute-start(bf16[16,32,128]{2,1,0:T(8,128)(2,1)S(1)} %get-tuple-element.38), channel_id=1, source_target_pairs={{0,7},{1,6},{2,5},{3,4},{4,0},{5,1},{6,2},{7,3},{8,15},{9,14},{10,... | collective-permute-start | bytes 393224 | tf_op jit(solution)/shard_map/ppermute | solution.py:279
  25.1 5.2 %collective-permute-start.18 = (bf16[16,32,128]{2,1,0:T(8,128)(2,1)S(1)}, bf16[16,32,128]{2,1,0:T(8,128)(2,1)S(1)}, u32[]{:S(2)}, u32[]{:S(2)}) collective-permute-start(bf16[16,32,128]{2,1,0:T(8,128)(2,1)S(1)} %get-tuple-element.38), channel_id=1, source_target_pairs={{0,6},{1,7},{2,4},{3,5},{4,0},{5,1},{6,2},{7,3},{8,14},{9,15},{10,... | collective-permute-start | bytes 393224 | tf_op jit(solution)/shard_map/ppermute | solution.py:279
  25.2 5.1 %collective-permute-start.17 = (bf16[16,32,128]{2,1,0:T(8,128)(2,1)S(1)}, bf16[16,32,128]{2,1,0:T(8,128)(2,1)S(1)}, u32[]{:S(2)}, u32[]{:S(2)}) collective-permute-start(bf16[16,32,128]{2,1,0:T(8,128)(2,1)S(1)} %get-tuple-element.38), channel_id=1, source_target_pairs={{0,5},{1,4},{2,7},{3,6},{4,0},{5,1},{6,2},{7,3},{8,13},{9,12},{10,... | collective-permute-start | bytes 393224 | tf_op jit(solution)/shard_map/ppermute | solution.py:279
  26.1 4.2 %collective-permute-start.16 = (bf16[16,32,128]{2,1,0:T(8,128)(2,1)S(1)}, bf16[16,32,128]{2,1,0:T(8,128)(2,1)S(1)}, u32[]{:S(2)}, u32[]{:S(2)}) collective-permute-start(bf16[16,32,128]{2,1,0:T(8,128)(2,1)S(1)} %get-tuple-element.38), channel_id=1, source_target_pairs={{0,4},{1,5},{2,6},{3,7},{4,0},{5,1},{6,2},{7,3},{8,12},{9,13},{10,... | collective-permute-start | bytes 393224 | tf_op jit(solution)/shard_map/ppermute | solution.py:279
  26.2 4.0 %collective-permute-start.20 = (bf16[32,32,128]{2,1,0:T(8,128)(2,1)S(1)}, bf16[32,32,128]{2,1,0:T(8,128)(2,1)S(1)}, u32[]{:S(2)}, u32[]{:S(2)}) collective-permute-start(bf16[32,32,128]{2,1,0:T(8,128)(2,1)S(1)} %get-tuple-element.39.refs_3_), channel_id=1, source_target_pairs={{0,4},{1,5},{2,6},{3,7},{4,0},{5,1},{6,2},{7,3},{8,12},{9,13},{10,... | collective-permute-start | bytes 786440 | tf_op jit(solution)/shard_map/ppermute | solution.py:279
  30.3 1.6 %collective-permute-start.21 = (bf16[32,32,128]{2,1,0:T(8,128)(2,1)S(1)}, bf16[32,32,128]{2,1,0:T(8,128)(2,1)S(1)}, u32[]{:S(2)}, u32[]{:S(2)}) collective-permute-start(bf16[32,32,128]{2,1,0:T(8,128)(2,1)S(1)} %get-tuple-element.41), channel_id=1, source_target_pairs={{0,4},{1,5},{2,6},{3,7},{4,0},{5,1},{6,2},{7,3},{8,12},{9,13},{10,... | collective-permute-start | bytes 786440 | tf_op jit(solution)/shard_map/ppermute | solution.py:279
  31.9 3.1 %collective-permute-start.25 = (bf16[16,32,128]{2,1,0:T(8,128)(2,1)S(1)}, bf16[16,32,128]{2,1,0:T(8,128)(2,1)S(1)}, u32[]{:S(2)}, u32[]{:S(2)}) collective-permute-start(bf16[16,32,128]{2,1,0:T(8,128)(2,1)S(1)} %project.4), channel_id=1, source_target_pairs={{0,4},{1,5},{2,6},{3,7},{4,3},{5,2},{6,1},{7,0},{8,12},{9,13},{10,... | collective-permute-start | bytes 393224 | tf_op jit(solution)/shard_map/ppermute | solution.py:279
  33.1 3.3 %collective-permute-start.24 = (bf16[16,32,128]{2,1,0:T(8,128)(2,1)S(1)}, bf16[16,32,128]{2,1,0:T(8,128)(2,1)S(1)}, u32[]{:S(2)}, u32[]{:S(2)}) collective-permute-start(bf16[16,32,128]{2,1,0:T(8,128)(2,1)S(1)} %project.4), channel_id=1, source_target_pairs={{0,4},{1,5},{2,6},{3,7},{4,2},{5,3},{6,0},{7,1},{8,12},{9,13},{10,... | collective-permute-start | bytes 393224 | tf_op jit(solution)/shard_map/ppermute | solution.py:279
  33.1 3.4 %collective-permute-start.23 = (bf16[16,32,128]{2,1,0:T(8,128)(2,1)S(1)}, bf16[16,32,128]{2,1,0:T(8,128)(2,1)S(1)}, u32[]{:S(2)}, u32[]{:S(2)}) collective-permute-start(bf16[16,32,128]{2,1,0:T(8,128)(2,1)S(1)} %project.4), channel_id=1, source_target_pairs={{0,4},{1,5},{2,6},{3,7},{4,1},{5,0},{6,3},{7,2},{8,12},{9,13},{10,... | collective-permute-start | bytes 393224 | tf_op jit(solution)/shard_map/ppermute | solution.py:279
  34.2 2.3 %collective-permute-start.22 = (bf16[16,32,128]{2,1,0:T(8,128)(2,1)S(1)}, bf16[16,32,128]{2,1,0:T(8,128)(2,1)S(1)}, u32[]{:S(2)}, u32[]{:S(2)}) collective-permute-start(bf16[16,32,128]{2,1,0:T(8,128)(2,1)S(1)} %project.4), channel_id=1, source_target_pairs={{0,4},{1,5},{2,6},{3,7},{4,0},{5,1},{6,2},{7,3},{8,12},{9,13},{10,... | collective-permute-start | bytes 393224 | tf_op jit(solution)/shard_map/ppermute | solution.py:279
  34.2 2.3 %collective-permute-start.26 = (bf16[32,32,128]{2,1,0:T(8,128)(2,1)S(1)}, bf16[32,32,128]{2,1,0:T(8,128)(2,1)S(1)}, u32[]{:S(2)}, u32[]{:S(2)}) collective-permute-start(bf16[32,32,128]{2,1,0:T(8,128)(2,1)S(1)} %collective-permute-done.21.image), channel_id=1, source_target_pairs={{0,4},{1,5},{2,6},{3,7},{4,0},{5,1},{6,2},{7,3},{8,12},{9,13},{10,... | collective-permute-start | bytes 786440 | tf_op jit(solution)/shard_map/ppermute | solution.py:279
  36.5 5.6 %collective-permute-start.30 = (bf16[16,32,128]{2,1,0:T(8,128)(2,1)S(1)}, bf16[16,32,128]{2,1,0:T(8,128)(2,1)S(1)}, u32[]{:S(2)}, u32[]{:S(2)}) collective-permute-start(bf16[16,32,128]{2,1,0:T(8,128)(2,1)S(1)} %get-tuple-element.42), channel_id=1, source_target_pairs={{0,7},{1,6},{2,5},{3,4},{4,0},{5,1},{6,2},{7,3},{8,15},{9,14},{10,... | collective-permute-start | bytes 393224 | tf_op jit(solution)/shard_map/ppermute | solution.py:279
  38.3 5.1 %collective-permute-start.29 = (bf16[16,32,128]{2,1,0:T(8,128)(2,1)S(1)}, bf16[16,32,128]{2,1,0:T(8,128)(2,1)S(1)}, u32[]{:S(2)}, u32[]{:S(2)}) collective-permute-start(bf16[16,32,128]{2,1,0:T(8,128)(2,1)S(1)} %get-tuple-element.42), channel_id=1, source_target_pairs={{0,6},{1,7},{2,4},{3,5},{4,0},{5,1},{6,2},{7,3},{8,14},{9,15},{10,... | collective-permute-start | bytes 393224 | tf_op jit(solution)/shard_map/ppermute | solution.py:279
  38.4 5.0 %collective-permute-start.28 = (bf16[16,32,128]{2,1,0:T(8,128)(2,1)S(1)}, bf16[16,32,128]{2,1,0:T(8,128)(2,1)S(1)}, u32[]{:S(2)}, u32[]{:S(2)}) collective-permute-start(bf16[16,32,128]{2,1,0:T(8,128)(2,1)S(1)} %get-tuple-element.42), channel_id=1, source_target_pairs={{0,5},{1,4},{2,7},{3,6},{4,0},{5,1},{6,2},{7,3},{8,13},{9,12},{10,... | collective-permute-start | bytes 393224 | tf_op jit(solution)/shard_map/ppermute | solution.py:279
  39.6 3.9 %collective-permute-start.27 = (bf16[16,32,128]{2,1,0:T(8,128)(2,1)S(1)}, bf16[16,32,128]{2,1,0:T(8,128)(2,1)S(1)}, u32[]{:S(2)}, u32[]{:S(2)}) collective-permute-start(bf16[16,32,128]{2,1,0:T(8,128)(2,1)S(1)} %get-tuple-element.42), channel_id=1, source_target_pairs={{0,4},{1,5},{2,6},{3,7},{4,0},{5,1},{6,2},{7,3},{8,12},{9,13},{10,... | collective-permute-start | bytes 393224 | tf_op jit(solution)/shard_map/ppermute | solution.py:279
  39.6 3.8 %collective-permute-start.31 = (bf16[32,32,128]{2,1,0:T(8,128)(2,1)S(1)}, bf16[32,32,128]{2,1,0:T(8,128)(2,1)S(1)}, u32[]{:S(2)}, u32[]{:S(2)}) collective-permute-start(bf16[32,32,128]{2,1,0:T(8,128)(2,1)S(1)} %get-tuple-element.43.refs_3_), channel_id=1, source_target_pairs={{0,4},{1,5},{2,6},{3,7},{4,0},{5,1},{6,2},{7,3},{8,12},{9,13},{10,... | collective-permute-start | bytes 786440 | tf_op jit(solution)/shard_map/ppermute | solution.py:279
  43.7 13.2 %collective-permute-start.32 = (bf16[32,32,128]{2,1,0:T(8,128)(2,1)S(1)}, bf16[32,32,128]{2,1,0:T(8,128)(2,1)S(1)}, u32[]{:S(2)}, u32[]{:S(2)}) collective-permute-start(bf16[32,32,128]{2,1,0:T(8,128)(2,1)S(1)} %get-tuple-element.45), channel_id=1, source_target_pairs={{0,4},{1,5},{2,6},{3,7},{4,0},{5,1},{6,2},{7,3},{8,12},{9,13},{10,... | collective-permute-start | bytes 786440 | tf_op jit(solution)/shard_map/ppermute | solution.py:279
  57.5 2.1 %collective-permute-start.36 = (bf16[16,32,128]{2,1,0:T(8,128)(2,1)S(1)}, bf16[16,32,128]{2,1,0:T(8,128)(2,1)S(1)}, u32[]{:S(2)}, u32[]{:S(2)}) collective-permute-start(bf16[16,32,128]{2,1,0:T(8,128)(2,1)S(1)} %project.5), channel_id=1, source_target_pairs={{0,4},{1,5},{2,6},{3,7},{4,3},{5,2},{6,1},{7,0},{8,12},{9,13},{10,... | collective-permute-start | bytes 393224 | tf_op jit(solution)/shard_map/ppermute | solution.py:279
  57.5 4.1 %collective-permute-start.35 = (bf16[16,32,128]{2,1,0:T(8,128)(2,1)S(1)}, bf16[16,32,128]{2,1,0:T(8,128)(2,1)S(1)}, u32[]{:S(2)}, u32[]{:S(2)}) collective-permute-start(bf16[16,32,128]{2,1,0:T(8,128)(2,1)S(1)} %project.5), channel_id=1, source_target_pairs={{0,4},{1,5},{2,6},{3,7},{4,2},{5,3},{6,0},{7,1},{8,12},{9,13},{10,... | collective-permute-start | bytes 393224 | tf_op jit(solution)/shard_map/ppermute | solution.py:279
  58.9 2.7 %collective-permute-start.34 = (bf16[16,32,128]{2,1,0:T(8,128)(2,1)S(1)}, bf16[16,32,128]{2,1,0:T(8,128)(2,1)S(1)}, u32[]{:S(2)}, u32[]{:S(2)}) collective-permute-start(bf16[16,32,128]{2,1,0:T(8,128)(2,1)S(1)} %project.5), channel_id=1, source_target_pairs={{0,4},{1,5},{2,6},{3,7},{4,1},{5,0},{6,3},{7,2},{8,12},{9,13},{10,... | collective-permute-start | bytes 393224 | tf_op jit(solution)/shard_map/ppermute | solution.py:279
  59.0 2.6 %collective-permute-start.33 = (bf16[16,32,128]{2,1,0:T(8,128)(2,1)S(1)}, bf16[16,32,128]{2,1,0:T(8,128)(2,1)S(1)}, u32[]{:S(2)}, u32[]{:S(2)}) collective-permute-start(bf16[16,32,128]{2,1,0:T(8,128)(2,1)S(1)} %project.5), channel_id=1, source_target_pairs={{0,4},{1,5},{2,6},{3,7},{4,0},{5,1},{6,2},{7,3},{8,12},{9,13},{10,... | collective-permute-start | bytes 393224 | tf_op jit(solution)/shard_map/ppermute | solution.py:279
  59.4 2.2 %collective-permute-start.37 = (bf16[32,32,128]{2,1,0:T(8,128)(2,1)S(1)}, bf16[32,32,128]{2,1,0:T(8,128)(2,1)S(1)}, u32[]{:S(2)}, u32[]{:S(2)}) collective-permute-start(bf16[32,32,128]{2,1,0:T(8,128)(2,1)S(1)} %collective-permute-done.32.image), channel_id=1, source_target_pairs={{0,4},{1,5},{2,6},{3,7},{4,0},{5,1},{6,2},{7,3},{8,12},{9,13},{10,... | collective-permute-start | bytes 786440 | tf_op jit(solution)/shard_map/ppermute | solution.py:279
  61.7 6.6 %collective-permute-start.41 = (bf16[16,32,128]{2,1,0:T(8,128)(2,1)S(1)}, bf16[16,32,128]{2,1,0:T(8,128)(2,1)S(1)}, u32[]{:S(2)}, u32[]{:S(2)}) collective-permute-start(bf16[16,32,128]{2,1,0:T(8,128)(2,1)S(1)} %get-tuple-element.46), channel_id=1, source_target_pairs={{0,7},{1,6},{2,5},{3,4},{4,0},{5,1},{6,2},{7,3},{8,15},{9,14},{10,... | collective-permute-start | bytes 393224 | tf_op jit(solution)/shard_map/ppermute | solution.py:279
  64.6 5.0 %collective-permute-start.40 = (bf16[16,32,128]{2,1,0:T(8,128)(2,1)S(1)}, bf16[16,32,128]{2,1,0:T(8,128)(2,1)S(1)}, u32[]{:S(2)}, u32[]{:S(2)}) collective-permute-start(bf16[16,32,128]{2,1,0:T(8,128)(2,1)S(1)} %get-tuple-element.46), channel_id=1, source_target_pairs={{0,6},{1,7},{2,4},{3,5},{4,0},{5,1},{6,2},{7,3},{8,14},{9,15},{10,... | collective-permute-start | bytes 393224 | tf_op jit(solution)/shard_map/ppermute | solution.py:279
  64.7 4.9 %collective-permute-start.39 = (bf16[16,32,128]{2,1,0:T(8,128)(2,1)S(1)}, bf16[16,32,128]{2,1,0:T(8,128)(2,1)S(1)}, u32[]{:S(2)}, u32[]{:S(2)}) collective-permute-start(bf16[16,32,128]{2,1,0:T(8,128)(2,1)S(1)} %get-tuple-element.46), channel_id=1, source_target_pairs={{0,5},{1,4},{2,7},{3,6},{4,0},{5,1},{6,2},{7,3},{8,13},{9,12},{10,... | collective-permute-start | bytes 393224 | tf_op jit(solution)/shard_map/ppermute | solution.py:279
  65.9 3.7 %collective-permute-start.38 = (bf16[16,32,128]{2,1,0:T(8,128)(2,1)S(1)}, bf16[16,32,128]{2,1,0:T(8,128)(2,1)S(1)}, u32[]{:S(2)}, u32[]{:S(2)}) collective-permute-start(bf16[16,32,128]{2,1,0:T(8,128)(2,1)S(1)} %get-tuple-element.46), channel_id=1, source_target_pairs={{0,4},{1,5},{2,6},{3,7},{4,0},{5,1},{6,2},{7,3},{8,12},{9,13},{10,... | collective-permute-start | bytes 393224 | tf_op jit(solution)/shard_map/ppermute | solution.py:279
  65.9 4.3 %collective-permute-start.42 = (bf16[32,32,128]{2,1,0:T(8,128)(2,1)S(1)}, bf16[32,32,128]{2,1,0:T(8,128)(2,1)S(1)}, u32[]{:S(2)}, u32[]{:S(2)}) collective-permute-start(bf16[32,32,128]{2,1,0:T(8,128)(2,1)S(1)} %get-tuple-element.47.refs_3_), channel_id=1, source_target_pairs={{0,4},{1,5},{2,6},{3,7},{4,0},{5,1},{6,2},{7,3},{8,12},{9,13},{10,... | collective-permute-start | bytes 786440 | tf_op jit(solution)/shard_map/ppermute | solution.py:279

commit v15 on v14

--- a/solution.py
+++ b/solution.py
@@ -287,13 +287,26 @@
             return [value] + [sent(value, lambda p, c, t: (p, c, t ^ d)) for d in far]
         return [lax.all_gather(value, "tile")]
 
-    def passed(terms, core):
+    def passed(terms, core, place):
         if not direct:
             return [swapped(lax.psum(terms, "tile"))]
-        return [
-            sent(terms, lambda p, c, t: (p, 1 - c, t ^ d if c == core else t))
-            for d in range(tiles)
-        ]
+        if core == 1:
+            ahead = place + 1 if place + 1 < places else place - 2
+        else:
+            ahead = place + 2 if place + 2 < places else 0
+        helped = place > 0 and ahead >= 0 and ahead != place
+
+        def way(d):
+            def target(p, c, t):
+                if helped and d == tiles - 1 and p in (place, ahead):
+                    if c != core:
+                        return (ahead, c, t) if p == place else (place, core, t)
+                    return (p, 1 - c, t ^ d) if p == place else (p, c, t ^ 1)
+                return p, 1 - c, t ^ d if c == core else t
+
+            return target
+
+        return [sent(terms, way(d)) for d in range(tiles)]
 
     def call(kernel, smem, operands, out_shape, scratch, name, flops=0):
         many = isinstance(out_shape, tuple)
@@ -411,7 +424,7 @@
                 [],
                 "project",
             )
-            change = updated(place, 0, passed(terms, 1))
+            change = updated(place, 0, passed(terms, 1, place))
             before = [swapped(image)]
         shot, terms = call(
             functools.partial(first_kernel, place),
@@ -421,7 +434,7 @@
             [],
             "first",
         )
-        change = updated(place, 1, passed(terms, 0))
+        change = updated(place, 1, passed(terms, 0, place))
         outs = call(
             functools.partial(second_kernel, place, last),
             1,

time: 71.1 us -> 73.9 us (1.039)
  the two profiles are of different devices: /device:TPU:25 before, /device:TPU:1 now
where the time goes in v15:
time: 73.9 us; the launch traced here: 73.7 us
  starting transfers between devices  42.9 us (58%)
  waiting for transfers between devices  23.9 us (32%)
  Pallas kernels  6.72 us (9%)
    ppermute x43, starting transfers between devices, sent(): return lax.ppermute(value, ('subset', 'tile'), pairs)  42.9 us
    ppermute x43, waiting for transfers between devices, sent(): return lax.ppermute(value, ('subset', 'tile'), pairs)  23.9 us
    pallas_call x1, Pallas kernels, per_device(): pl.pallas_call(functools.partial(head_kernel, row_blocks, chunks), out_sh...  3.09 us
    pallas_call x19, Pallas kernels, call(): pl.pallas_call(kernel, out_shape=out_shape, in_specs=[SMEM] * smem + [VME...  1.83 us
  transfers between devices with their start and end apart: 43, of which 18 were waited for; matrix products, arithmetic and copies ran while one was open for 0% of the time, Pallas kernels for 7%

profile of v15, /device:TPU:1, one launch (start us, length us, event | category | flops | bytes accessed | tf_op | source)
XLA Modules:
  0.0 73.7 jit_solution(5405135672694620073)
XLA Ops:
  0.1 3.1 %head.1 = (bf16[5,32,128]{2,1,0:T(8,128)(2,1)S(1)}, s32[2,80]{1,0:T(2,128)S(1)}, s32[3,80]{1,0:T(4,128)S(4)}, bf16[1,1,80,128,128]{4,3,2,1,0:T(8,128)(2,1)S(1)}) custom-call(s32[3]{0:T(128)S(1)} %pad_add_fusion.pos, s32[1,1,80]{2,1,0:T(1,128)} %rows_in.1, s32[1,1,80]{2,1,0:T(1,128)} %cols_in.1, bf16[1,1,80,128,128]{4,3,2,1,0:T(8,128)(2,1)} %blocks_in.1, ...), custom_call_target="tpu_custom_call" | custom-call | tf_op jit(solution)/shard_map/head/pallas_call | solution.py:328
  3.2 3.7 %collective-permute-start.4 = (bf16[5,32,128]{2,1,0:T(8,128)(2,1)S(1)}, bf16[5,32,128]{2,1,0:T(8,128)(2,1)S(1)}, u32[]{:S(2)}, u32[]{:S(2)}) collective-permute-start(bf16[5,32,128]{2,1,0:T(8,128)(2,1)S(1)} %get-tuple-element.31._.refs_2_), channel_id=1, source_target_pairs={{0,3},{1,2},{2,1},{3,0},{4,7},{5,6},{6,5},{7,4},{8,11},{9,10},{10,... | collective-permute-start | bytes 122888 | tf_op jit(solution)/shard_map/ppermute | solution.py:279
  6.9 0.2 collective-permute-start.3
  7.3 0.6 collective-permute-start
  7.8 0.5 pack_own.1.refs_1_
  8.3 0.3 collective-permute-done.table2
  8.7 1.3 %pack_other.1 = (s32[3,80]{1,0:T(4,128)S(4)}, bf16[16,640,128]{2,1,0:T(8,128)(2,1)S(1)}) custom-call(s32[3,80]{1,0:T(4,128)S(4)} %get-tuple-element.27.own, s32[2,80]{1,0:T(2,128)S(1)} %collective-permute-done.table2, bf16[1,1,80,128,128]{4,3,2,1,0:T(8,128)(2,1)S(1)} %collective-permute-done.1.blocks2), custom_call_target="tpu_custom_call" | custom-call | tf_op jit(solution)/shard_map/pack_other/pallas_call | solution.py:369
  10.1 2.9 %collective-permute-start.8 = (bf16[16,32,128]{2,1,0:T(8,128)(2,1)S(1)}, bf16[16,32,128]{2,1,0:T(8,128)(2,1)S(1)}, u32[]{:S(2)}, u32[]{:S(2)}) collective-permute-start(bf16[16,32,128]{2,1,0:T(8,128)(2,1)S(1)} %get-tuple-element.35), channel_id=1, source_target_pairs={{0,7},{1,6},{2,5},{3,4},{4,0},{5,1},{6,2},{7,3},{8,15},{9,14},{10,... | collective-permute-start | bytes 393224 | tf_op jit(solution)/shard_map/ppermute | solution.py:279
  13.0 0.2 collective-permute-start.7
  13.1 1.5 %collective-permute-start.6 = (bf16[16,32,128]{2,1,0:T(8,128)(2,1)S(1)}, bf16[16,32,128]{2,1,0:T(8,128)(2,1)S(1)}, u32[]{:S(2)}, u32[]{:S(2)}) collective-permute-start(bf16[16,32,128]{2,1,0:T(8,128)(2,1)S(1)} %get-tuple-element.35), channel_id=1, source_target_pairs={{0,5},{1,4},{2,7},{3,6},{4,0},{5,1},{6,2},{7,3},{8,13},{9,12},{10,... | collective-permute-start | bytes 393224 | tf_op jit(solution)/shard_map/ppermute | solution.py:279
  14.6 0.5 collective-permute-start.9
  15.1 1.7 %collective-permute-done.8.refs_6_ = bf16[16,32,128]{2,1,0:T(8,128)(2,1)S(1)} collective-permute-done((bf16[16,32,128]{2,1,0:T(8,128)(2,1)S(1)}, bf16[16,32,128]{2,1,0:T(8,128)(2,1)S(1)}, u32[]{:S(2)}, u32[]{:S(2)}) %collective-permute-start.8) | collective-permute-done | bytes 131104 | tf_op jit(solution)/shard_map/ppermute | solution.py:279
  16.8 1.3 %collective-permute-done.7.refs_5_ = bf16[16,32,128]{2,1,0:T(8,128)(2,1)S(1)} collective-permute-done((bf16[16,32,128]{2,1,0:T(8,128)(2,1)S(1)}, bf16[16,32,128]{2,1,0:T(8,128)(2,1)S(1)}, u32[]{:S(2)}, u32[]{:S(2)}) %collective-permute-start.7) | collective-permute-done | bytes 131104 | tf_op jit(solution)/shard_map/ppermute | solution.py:279
  18.1 0.6 update.9.refs_1_
  18.9 3.3 %collective-permute-done.10.image = bf16[32,32,128]{2,1,0:T(8,128)(2,1)S(1)} collective-permute-done((bf16[32,32,128]{2,1,0:T(8,128)(2,1)S(1)}, bf16[32,32,128]{2,1,0:T(8,128)(2,1)S(1)}, u32[]{:S(2)}, u32[]{:S(2)}) %collective-permute-start.10) | collective-permute-done | bytes 262176 | tf_op jit(solution)/shard_map/ppermute | solution.py:279
  22.3 2.9 %collective-permute-start.14 = (bf16[16,32,128]{2,1,0:T(8,128)(2,1)S(1)}, bf16[16,32,128]{2,1,0:T(8,128)(2,1)S(1)}, u32[]{:S(2)}, u32[]{:S(2)}) collective-permute-start(bf16[16,32,128]{2,1,0:T(8,128)(2,1)S(1)} %project.3), channel_id=1, source_target_pairs={{0,4},{1,5},{2,6},{3,7},{4,3},{5,2},{6,1},{7,0},{8,16},{9,17},{10,... | collective-permute-start | bytes 393224 | tf_op jit(solution)/shard_map/ppermute | solution.py:279
  25.1 1.0 %collective-permute-start.12 = (bf16[16,32,128]{2,1,0:T(8,128)(2,1)S(1)}, bf16[16,32,128]{2,1,0:T(8,128)(2,1)S(1)}, u32[]{:S(2)}, u32[]{:S(2)}) collective-permute-start(bf16[16,32,128]{2,1,0:T(8,128)(2,1)S(1)} %project.3), channel_id=1, source_target_pairs={{0,4},{1,5},{2,6},{3,7},{4,1},{5,0},{6,3},{7,2},{8,12},{9,13},{10,... | collective-permute-start | bytes 393224 | tf_op jit(solution)/shard_map/ppermute | solution.py:279
  26.1 0.5 collective-permute-start.15
  26.7 0.4 collective-permute-done.14.refs_6_
  27.1 1.4 %collective-permute-done.13.refs_5_ = bf16[16,32,128]{2,1,0:T(8,128)(2,1)S(1)} collective-permute-done((bf16[16,32,128]{2,1,0:T(8,128)(2,1)S(1)}, bf16[16,32,128]{2,1,0:T(8,128)(2,1)S(1)}, u32[]{:S(2)}, u32[]{:S(2)}) %collective-permute-start.13) | collective-permute-done | bytes 131104 | tf_op jit(solution)/shard_map/ppermute | solution.py:279
  28.5 1.8 %collective-permute-start.19 = (bf16[16,32,128]{2,1,0:T(8,128)(2,1)S(1)}, bf16[16,32,128]{2,1,0:T(8,128)(2,1)S(1)}, u32[]{:S(2)}, u32[]{:S(2)}) collective-permute-start(bf16[16,32,128]{2,1,0:T(8,128)(2,1)S(1)} %get-tuple-element.38), channel_id=1, source_target_pairs={{0,7},{1,6},{2,5},{3,4},{4,0},{5,1},{6,2},{7,3},{8,15},{9,14},{10,... | collective-permute-start | bytes 393224 | tf_op jit(solution)/shard_map/ppermute | solution.py:279
  30.4 1.1 %collective-permute-start.17 = (bf16[16,32,128]{2,1,0:T(8,128)(2,1)S(1)}, bf16[16,32,128]{2,1,0:T(8,128)(2,1)S(1)}, u32[]{:S(2)}, u32[]{:S(2)}) collective-permute-start(bf16[16,32,128]{2,1,0:T(8,128)(2,1)S(1)} %get-tuple-element.38), channel_id=1, source_target_pairs={{0,5},{1,4},{2,7},{3,6},{4,0},{5,1},{6,2},{7,3},{8,13},{9,12},{10,... | collective-permute-start | bytes 393224 | tf_op jit(solution)/shard_map/ppermute | solution.py:279
  31.6 0.4 collective-permute-start.20
  32.0 2.1 %collective-permute-done.19.refs_6_ = bf16[16,32,128]{2,1,0:T(8,128)(2,1)S(1)} collective-permute-done((bf16[16,32,128]{2,1,0:T(8,128)(2,1)S(1)}, bf16[16,32,128]{2,1,0:T(8,128)(2,1)S(1)}, u32[]{:S(2)}, u32[]{:S(2)}) %collective-permute-start.19) | collective-permute-done | bytes 131104 | tf_op jit(solution)/shard_map/ppermute | solution.py:279
  34.2 1.3 %collective-permute-done.18.refs_5_ = bf16[16,32,128]{2,1,0:T(8,128)(2,1)S(1)} collective-permute-done((bf16[16,32,128]{2,1,0:T(8,128)(2,1)S(1)}, bf16[16,32,128]{2,1,0:T(8,128)(2,1)S(1)}, u32[]{:S(2)}, u32[]{:S(2)}) %collective-permute-start.18) | collective-permute-done | bytes 131104 | tf_op jit(solution)/shard_map/ppermute | solution.py:279
  35.7 1.5 %collective-permute-done.21.image = bf16[32,32,128]{2,1,0:T(8,128)(2,1)S(1)} collective-permute-done((bf16[32,32,128]{2,1,0:T(8,128)(2,1)S(1)}, bf16[32,32,128]{2,1,0:T(8,128)(2,1)S(1)}, u32[]{:S(2)}, u32[]{:S(2)}) %collective-permute-start.21) | collective-permute-done | bytes 262176 | tf_op jit(solution)/shard_map/ppermute | solution.py:279
  37.2 1.2 %collective-permute-start.25 = (bf16[16,32,128]{2,1,0:T(8,128)(2,1)S(1)}, bf16[16,32,128]{2,1,0:T(8,128)(2,1)S(1)}, u32[]{:S(2)}, u32[]{:S(2)}) collective-permute-start(bf16[16,32,128]{2,1,0:T(8,128)(2,1)S(1)} %project.4), channel_id=1, source_target_pairs={{0,4},{1,5},{2,6},{3,7},{4,3},{5,2},{6,1},{7,0},{8,12},{9,13},{10,... | collective-permute-start | bytes 393224 | tf_op jit(solution)/shard_map/ppermute | solution.py:279
  38.4 1.2 %collective-permute-start.23 = (bf16[16,32,128]{2,1,0:T(8,128)(2,1)S(1)}, bf16[16,32,128]{2,1,0:T(8,128)(2,1)S(1)}, u32[]{:S(2)}, u32[]{:S(2)}) collective-permute-start(bf16[16,32,128]{2,1,0:T(8,128)(2,1)S(1)} %project.4), channel_id=1, source_target_pairs={{0,4},{1,5},{2,6},{3,7},{4,1},{5,0},{6,3},{7,2},{8,12},{9,13},{10,... | collective-permute-start | bytes 393224 | tf_op jit(solution)/shard_map/ppermute | solution.py:279
  39.6 0.5 collective-permute-start.26
  40.1 0.2 collective-permute-done.25.refs_6_
  40.3 1.4 %collective-permute-done.24.refs_5_ = bf16[16,32,128]{2,1,0:T(8,128)(2,1)S(1)} collective-permute-done((bf16[16,32,128]{2,1,0:T(8,128)(2,1)S(1)}, bf16[16,32,128]{2,1,0:T(8,128)(2,1)S(1)}, u32[]{:S(2)}, u32[]{:S(2)}) %collective-permute-start.24) | collective-permute-done | bytes 131104 | tf_op jit(solution)/shard_map/ppermute | solution.py:279
  41.7 8.0 %collective-permute-start.30 = (bf16[16,32,128]{2,1,0:T(8,128)(2,1)S(1)}, bf16[16,32,128]{2,1,0:T(8,128)(2,1)S(1)}, u32[]{:S(2)}, u32[]{:S(2)}) collective-permute-start(bf16[16,32,128]{2,1,0:T(8,128)(2,1)S(1)} %get-tuple-element.42), channel_id=1, source_target_pairs={{0,1},{1,0},{2,3},{3,2},{4,16},{5,17},{6,18},{7,19},{8,15},{9,14},... | collective-permute-start | bytes 393224 | tf_op jit(solution)/shard_map/ppermute | solution.py:279
  49.7 1.3 %collective-permute-start.28 = (bf16[16,32,128]{2,1,0:T(8,128)(2,1)S(1)}, bf16[16,32,128]{2,1,0:T(8,128)(2,1)S(1)}, u32[]{:S(2)}, u32[]{:S(2)}) collective-permute-start(bf16[16,32,128]{2,1,0:T(8,128)(2,1)S(1)} %get-tuple-element.42), channel_id=1, source_target_pairs={{0,5},{1,4},{2,7},{3,6},{4,0},{5,1},{6,2},{7,3},{8,13},{9,12},{10,... | collective-permute-start | bytes 393224 | tf_op jit(solution)/shard_map/ppermute | solution.py:279
  51.0 0.5 collective-permute-start.31
  51.7 2.4 %collective-permute-done.29.refs_5_ = bf16[16,32,128]{2,1,0:T(8,128)(2,1)S(1)} collective-permute-done((bf16[16,32,128]{2,1,0:T(8,128)(2,1)S(1)}, bf16[16,32,128]{2,1,0:T(8,128)(2,1)S(1)}, u32[]{:S(2)}, u32[]{:S(2)}) %collective-permute-start.29) | collective-permute-done | bytes 131104 | tf_op jit(solution)/shard_map/ppermute | solution.py:279
  54.2 0.2 second.6
  54.5 1.5 %collective-permute-done.32.image = bf16[32,32,128]{2,1,0:T(8,128)(2,1)S(1)} collective-permute-done((bf16[32,32,128]{2,1,0:T(8,128)(2,1)S(1)}, bf16[32,32,128]{2,1,0:T(8,128)(2,1)S(1)}, u32[]{:S(2)}, u32[]{:S(2)}) %collective-permute-start.32) | collective-permute-done | bytes 262176 | tf_op jit(solution)/shard_map/ppermute | solution.py:279
  56.0 1.2 %collective-permute-start.36 = (bf16[16,32,128]{2,1,0:T(8,128)(2,1)S(1)}, bf16[16,32,128]{2,1,0:T(8,128)(2,1)S(1)}, u32[]{:S(2)}, u32[]{:S(2)}) collective-permute-start(bf16[16,32,128]{2,1,0:T(8,128)(2,1)S(1)} %project.5), channel_id=1, source_target_pairs={{0,4},{1,5},{2,6},{3,7},{4,3},{5,2},{6,1},{7,0},{8,28},{9,29},{10,... | collective-permute-start | bytes 393224 | tf_op jit(solution)/shard_map/ppermute | solution.py:279
  57.3 1.2 %collective-permute-start.34 = (bf16[16,32,128]{2,1,0:T(8,128)(2,1)S(1)}, bf16[16,32,128]{2,1,0:T(8,128)(2,1)S(1)}, u32[]{:S(2)}, u32[]{:S(2)}) collective-permute-start(bf16[16,32,128]{2,1,0:T(8,128)(2,1)S(1)} %project.5), channel_id=1, source_target_pairs={{0,4},{1,5},{2,6},{3,7},{4,1},{5,0},{6,3},{7,2},{8,12},{9,13},{10,... | collective-permute-start | bytes 393224 | tf_op jit(solution)/shard_map/ppermute | solution.py:279
  58.5 0.5 collective-permute-start.37
  59.0 0.2 collective-permute-done.36.refs_6_
  59.2 1.4 %collective-permute-done.35.refs_5_ = bf16[16,32,128]{2,1,0:T(8,128)(2,1)S(1)} collective-permute-done((bf16[16,32,128]{2,1,0:T(8,128)(2,1)S(1)}, bf16[16,32,128]{2,1,0:T(8,128)(2,1)S(1)}, u32[]{:S(2)}, u32[]{:S(2)}) %collective-permute-start.35) | collective-permute-done | bytes 131104 | tf_op jit(solution)/shard_map/ppermute | solution.py:279
  60.6 7.9 %collective-permute-start.41 = (bf16[16,32,128]{2,1,0:T(8,128)(2,1)S(1)}, bf16[16,32,128]{2,1,0:T(8,128)(2,1)S(1)}, u32[]{:S(2)}, u32[]{:S(2)}) collective-permute-start(bf16[16,32,128]{2,1,0:T(8,128)(2,1)S(1)} %get-tuple-element.46), channel_id=1, source_target_pairs={{0,1},{1,0},{2,3},{3,2},{4,24},{5,25},{6,26},{7,27},{8,15},{9,14},... | collective-permute-start | bytes 393224 | tf_op jit(solution)/shard_map/ppermute | solution.py:279
  68.5 1.0 %collective-permute-start.39 = (bf16[16,32,128]{2,1,0:T(8,128)(2,1)S(1)}, bf16[16,32,128]{2,1,0:T(8,128)(2,1)S(1)}, u32[]{:S(2)}, u32[]{:S(2)}) collective-permute-start(bf16[16,32,128]{2,1,0:T(8,128)(2,1)S(1)} %get-tuple-element.46), channel_id=1, source_target_pairs={{0,5},{1,4},{2,7},{3,6},{4,0},{5,1},{6,2},{7,3},{8,13},{9,12},{10,... | collective-permute-start | bytes 393224 | tf_op jit(solution)/shard_map/ppermute | solution.py:279
  69.5 0.5 collective-permute-start.42
  70.0 0.5 collective-permute-done.41.refs_6_
  70.5 2.4 %collective-permute-done.40.refs_5_ = bf16[16,32,128]{2,1,0:T(8,128)(2,1)S(1)} collective-permute-done((bf16[16,32,128]{2,1,0:T(8,128)(2,1)S(1)}, bf16[16,32,128]{2,1,0:T(8,128)(2,1)S(1)}, u32[]{:S(2)}, u32[]{:S(2)}) %collective-permute-start.40) | collective-permute-done | bytes 131104 | tf_op jit(solution)/shard_map/ppermute | solution.py:279
  72.9 0.8 %second.7 = bf16[4,8,4096]{2,1,0:T(8,128)(2,1)} custom-call(s32[3,80]{1,0:T(4,128)S(4)} %get-tuple-element.29.refs_0_.info, f32[32,32,128]{2,1,0:T(8,128)S(1)} %update.15.refs_1_, bf16[32,32,128]{2,1,0:T(8,128)(2,1)S(1)} %collective-permute-done.42.refs_2_, bf16[32,32,128]{2,1,0:T(8,128)(2,1)S(1)} %get-tuple-element.47.refs_3_, ...), custom_call_target="tpu_custom_call" | custom-call | tf_op jit(solution)/shard_map/second/pallas_call | solution.py:313
  (61 shorter events, 1.4 us)
Async XLA Ops:
  0.0 8.7 %collective-permute-start.1 = (bf16[1,1,80,128,128]{4,3,2,1,0:T(8,128)(2,1)}, bf16[1,1,80,128,128]{4,3,2,1,0:T(8,128)(2,1)S(1)}, u32[]{:S(2)}, u32[]{:S(2)}) collective-permute-start(bf16[1,1,80,128,128]{4,3,2,1,0:T(8,128)(2,1)} %blocks_in.1), channel_id=1, source_target_pairs={{0,4},{1,5},{2,6},{3,7},{4,0},{5,1},{6,2},{7,3},{8,12},{9,13},{10,... | collective-permute-start | bytes 7864328 | tf_op jit(solution)/shard_map/ppermute | solution.py:279
  3.2 6.8 %collective-permute-start.4 = (bf16[5,32,128]{2,1,0:T(8,128)(2,1)S(1)}, bf16[5,32,128]{2,1,0:T(8,128)(2,1)S(1)}, u32[]{:S(2)}, u32[]{:S(2)}) collective-permute-start(bf16[5,32,128]{2,1,0:T(8,128)(2,1)S(1)} %get-tuple-element.31._.refs_2_), channel_id=1, source_target_pairs={{0,3},{1,2},{2,1},{3,0},{4,7},{5,6},{6,5},{7,4},{8,11},{9,10},{10,... | collective-permute-start | bytes 122888 | tf_op jit(solution)/shard_map/ppermute | solution.py:279
  6.9 3.1 %collective-permute-start.3 = (bf16[5,32,128]{2,1,0:T(8,128)(2,1)S(1)}, bf16[5,32,128]{2,1,0:T(8,128)(2,1)S(1)}, u32[]{:S(2)}, u32[]{:S(2)}) collective-permute-start(bf16[5,32,128]{2,1,0:T(8,128)(2,1)S(1)} %get-tuple-element.31._.refs_2_), channel_id=1, source_target_pairs={{0,2},{1,3},{2,0},{3,1},{4,6},{5,7},{6,4},{7,5},{8,10},{9,11},{10,... | collective-permute-start | bytes 122888 | tf_op jit(solution)/shard_map/ppermute | solution.py:279
  7.1 2.9 %collective-permute-start.2 = (bf16[5,32,128]{2,1,0:T(8,128)(2,1)S(1)}, bf16[5,32,128]{2,1,0:T(8,128)(2,1)S(1)}, u32[]{:S(2)}, u32[]{:S(2)}) collective-permute-start(bf16[5,32,128]{2,1,0:T(8,128)(2,1)S(1)} %get-tuple-element.31._.refs_2_), channel_id=1, source_target_pairs={{0,1},{1,0},{2,3},{3,2},{4,5},{5,4},{6,7},{7,6},{8,9},{9,8},{10,11... | collective-permute-start | bytes 122888 | tf_op jit(solution)/shard_map/ppermute | solution.py:279
  7.3 1.4 %collective-permute-start = (s32[2,80]{1,0:T(2,128)S(1)}, s32[2,80]{1,0:T(2,128)S(1)}, u32[]{:S(2)}, u32[]{:S(2)}) collective-permute-start(s32[2,80]{1,0:T(2,128)S(1)} %get-tuple-element.28), channel_id=1, source_target_pairs={{0,4},{1,5},{2,6},{3,7},{4,0},{5,1},{6,2},{7,3},{8,12},{9,13},{10,... | collective-permute-start | bytes 1928 | tf_op jit(solution)/shard_map/ppermute | solution.py:279
  10.1 6.7 %collective-permute-start.8 = (bf16[16,32,128]{2,1,0:T(8,128)(2,1)S(1)}, bf16[16,32,128]{2,1,0:T(8,128)(2,1)S(1)}, u32[]{:S(2)}, u32[]{:S(2)}) collective-permute-start(bf16[16,32,128]{2,1,0:T(8,128)(2,1)S(1)} %get-tuple-element.35), channel_id=1, source_target_pairs={{0,7},{1,6},{2,5},{3,4},{4,0},{5,1},{6,2},{7,3},{8,15},{9,14},{10,... | collective-permute-start | bytes 393224 | tf_op jit(solution)/shard_map/ppermute | solution.py:279
  13.0 5.2 %collective-permute-start.7 = (bf16[16,32,128]{2,1,0:T(8,128)(2,1)S(1)}, bf16[16,32,128]{2,1,0:T(8,128)(2,1)S(1)}, u32[]{:S(2)}, u32[]{:S(2)}) collective-permute-start(bf16[16,32,128]{2,1,0:T(8,128)(2,1)S(1)} %get-tuple-element.35), channel_id=1, source_target_pairs={{0,6},{1,7},{2,4},{3,5},{4,0},{5,1},{6,2},{7,3},{8,14},{9,15},{10,... | collective-permute-start | bytes 393224 | tf_op jit(solution)/shard_map/ppermute | solution.py:279
  13.1 5.0 %collective-permute-start.6 = (bf16[16,32,128]{2,1,0:T(8,128)(2,1)S(1)}, bf16[16,32,128]{2,1,0:T(8,128)(2,1)S(1)}, u32[]{:S(2)}, u32[]{:S(2)}) collective-permute-start(bf16[16,32,128]{2,1,0:T(8,128)(2,1)S(1)} %get-tuple-element.35), channel_id=1, source_target_pairs={{0,5},{1,4},{2,7},{3,6},{4,0},{5,1},{6,2},{7,3},{8,13},{9,12},{10,... | collective-permute-start | bytes 393224 | tf_op jit(solution)/shard_map/ppermute | solution.py:279
  14.6 3.5 %collective-permute-start.5 = (bf16[16,32,128]{2,1,0:T(8,128)(2,1)S(1)}, bf16[16,32,128]{2,1,0:T(8,128)(2,1)S(1)}, u32[]{:S(2)}, u32[]{:S(2)}) collective-permute-start(bf16[16,32,128]{2,1,0:T(8,128)(2,1)S(1)} %get-tuple-element.35), channel_id=1, source_target_pairs={{0,4},{1,5},{2,6},{3,7},{4,0},{5,1},{6,2},{7,3},{8,12},{9,13},{10,... | collective-permute-start | bytes 393224 | tf_op jit(solution)/shard_map/ppermute | solution.py:279
  14.6 4.1 %collective-permute-start.9 = (bf16[32,32,128]{2,1,0:T(8,128)(2,1)S(1)}, bf16[32,32,128]{2,1,0:T(8,128)(2,1)S(1)}, u32[]{:S(2)}, u32[]{:S(2)}) collective-permute-start(bf16[32,32,128]{2,1,0:T(8,128)(2,1)S(1)} %get-tuple-element.36.refs_3_), channel_id=1, source_target_pairs={{0,4},{1,5},{2,6},{3,7},{4,0},{5,1},{6,2},{7,3},{8,12},{9,13},{10,... | collective-permute-start | bytes 786440 | tf_op jit(solution)/shard_map/ppermute | solution.py:279
  18.8 3.4 %collective-permute-start.10 = (bf16[32,32,128]{2,1,0:T(8,128)(2,1)S(1)}, bf16[32,32,128]{2,1,0:T(8,128)(2,1)S(1)}, u32[]{:S(2)}, u32[]{:S(2)}) collective-permute-start(bf16[32,32,128]{2,1,0:T(8,128)(2,1)S(1)} %get-tuple-element.37), channel_id=1, source_target_pairs={{0,4},{1,5},{2,6},{3,7},{4,12},{5,13},{6,14},{7,15},{8,0},{9,1},{1... | collective-permute-start | bytes 786440 | tf_op jit(solution)/shard_map/ppermute | solution.py:279
  22.3 4.8 %collective-permute-start.14 = (bf16[16,32,128]{2,1,0:T(8,128)(2,1)S(1)}, bf16[16,32,128]{2,1,0:T(8,128)(2,1)S(1)}, u32[]{:S(2)}, u32[]{:S(2)}) collective-permute-start(bf16[16,32,128]{2,1,0:T(8,128)(2,1)S(1)} %project.3), channel_id=1, source_target_pairs={{0,4},{1,5},{2,6},{3,7},{4,3},{5,2},{6,1},{7,0},{8,16},{9,17},{10,... | collective-permute-start | bytes 393224 | tf_op jit(solution)/shard_map/ppermute | solution.py:279
  25.1 3.3 %collective-permute-start.13 = (bf16[16,32,128]{2,1,0:T(8,128)(2,1)S(1)}, bf16[16,32,128]{2,1,0:T(8,128)(2,1)S(1)}, u32[]{:S(2)}, u32[]{:S(2)}) collective-permute-start(bf16[16,32,128]{2,1,0:T(8,128)(2,1)S(1)} %project.3), channel_id=1, source_target_pairs={{0,4},{1,5},{2,6},{3,7},{4,2},{5,3},{6,0},{7,1},{8,12},{9,13},{10,... | collective-permute-start | bytes 393224 | tf_op jit(solution)/shard_map/ppermute | solution.py:279
  25.1 3.4 %collective-permute-start.12 = (bf16[16,32,128]{2,1,0:T(8,128)(2,1)S(1)}, bf16[16,32,128]{2,1,0:T(8,128)(2,1)S(1)}, u32[]{:S(2)}, u32[]{:S(2)}) collective-permute-start(bf16[16,32,128]{2,1,0:T(8,128)(2,1)S(1)} %project.3), channel_id=1, source_target_pairs={{0,4},{1,5},{2,6},{3,7},{4,1},{5,0},{6,3},{7,2},{8,12},{9,13},{10,... | collective-permute-start | bytes 393224 | tf_op jit(solution)/shard_map/ppermute | solution.py:279
  26.1 2.4 %collective-permute-start.11 = (bf16[16,32,128]{2,1,0:T(8,128)(2,1)S(1)}, bf16[16,32,128]{2,1,0:T(8,128)(2,1)S(1)}, u32[]{:S(2)}, u32[]{:S(2)}) collective-permute-start(bf16[16,32,128]{2,1,0:T(8,128)(2,1)S(1)} %project.3), channel_id=1, source_target_pairs={{0,4},{1,5},{2,6},{3,7},{4,0},{5,1},{6,2},{7,3},{8,12},{9,13},{10,... | collective-permute-start | bytes 393224 | tf_op jit(solution)/shard_map/ppermute | solution.py:279
  26.1 2.4 %collective-permute-start.15 = (bf16[32,32,128]{2,1,0:T(8,128)(2,1)S(1)}, bf16[32,32,128]{2,1,0:T(8,128)(2,1)S(1)}, u32[]{:S(2)}, u32[]{:S(2)}) collective-permute-start(bf16[32,32,128]{2,1,0:T(8,128)(2,1)S(1)} %collective-permute-done.10.image), channel_id=1, source_target_pairs={{0,4},{1,5},{2,6},{3,7},{4,0},{5,1},{6,2},{7,3},{8,12},{9,13},{10,... | collective-permute-start | bytes 786440 | tf_op jit(solution)/shard_map/ppermute | solution.py:279
  28.5 5.7 %collective-permute-start.19 = (bf16[16,32,128]{2,1,0:T(8,128)(2,1)S(1)}, bf16[16,32,128]{2,1,0:T(8,128)(2,1)S(1)}, u32[]{:S(2)}, u32[]{:S(2)}) collective-permute-start(bf16[16,32,128]{2,1,0:T(8,128)(2,1)S(1)} %get-tuple-element.38), channel_id=1, source_target_pairs={{0,7},{1,6},{2,5},{3,4},{4,0},{5,1},{6,2},{7,3},{8,15},{9,14},{10,... | collective-permute-start | bytes 393224 | tf_op jit(solution)/shard_map/ppermute | solution.py:279
  30.4 5.2 %collective-permute-start.18 = (bf16[16,32,128]{2,1,0:T(8,128)(2,1)S(1)}, bf16[16,32,128]{2,1,0:T(8,128)(2,1)S(1)}, u32[]{:S(2)}, u32[]{:S(2)}) collective-permute-start(bf16[16,32,128]{2,1,0:T(8,128)(2,1)S(1)} %get-tuple-element.38), channel_id=1, source_target_pairs={{0,6},{1,7},{2,4},{3,5},{4,0},{5,1},{6,2},{7,3},{8,14},{9,15},{10,... | collective-permute-start | bytes 393224 | tf_op jit(solution)/shard_map/ppermute | solution.py:279
  30.4 5.1 %collective-permute-start.17 = (bf16[16,32,128]{2,1,0:T(8,128)(2,1)S(1)}, bf16[16,32,128]{2,1,0:T(8,128)(2,1)S(1)}, u32[]{:S(2)}, u32[]{:S(2)}) collective-permute-start(bf16[16,32,128]{2,1,0:T(8,128)(2,1)S(1)} %get-tuple-element.38), channel_id=1, source_target_pairs={{0,5},{1,4},{2,7},{3,6},{4,0},{5,1},{6,2},{7,3},{8,13},{9,12},{10,... | collective-permute-start | bytes 393224 | tf_op jit(solution)/shard_map/ppermute | solution.py:279
  31.5 4.0 %collective-permute-start.16 = (bf16[16,32,128]{2,1,0:T(8,128)(2,1)S(1)}, bf16[16,32,128]{2,1,0:T(8,128)(2,1)S(1)}, u32[]{:S(2)}, u32[]{:S(2)}) collective-permute-start(bf16[16,32,128]{2,1,0:T(8,128)(2,1)S(1)} %get-tuple-element.38), channel_id=1, source_target_pairs={{0,4},{1,5},{2,6},{3,7},{4,0},{5,1},{6,2},{7,3},{8,12},{9,13},{10,... | collective-permute-start | bytes 393224 | tf_op jit(solution)/shard_map/ppermute | solution.py:279
  31.6 3.9 %collective-permute-start.20 = (bf16[32,32,128]{2,1,0:T(8,128)(2,1)S(1)}, bf16[32,32,128]{2,1,0:T(8,128)(2,1)S(1)}, u32[]{:S(2)}, u32[]{:S(2)}) collective-permute-start(bf16[32,32,128]{2,1,0:T(8,128)(2,1)S(1)} %get-tuple-element.39.refs_3_), channel_id=1, source_target_pairs={{0,4},{1,5},{2,6},{3,7},{4,0},{5,1},{6,2},{7,3},{8,12},{9,13},{10,... | collective-permute-start | bytes 786440 | tf_op jit(solution)/shard_map/ppermute | solution.py:279
  35.6 1.6 %collective-permute-start.21 = (bf16[32,32,128]{2,1,0:T(8,128)(2,1)S(1)}, bf16[32,32,128]{2,1,0:T(8,128)(2,1)S(1)}, u32[]{:S(2)}, u32[]{:S(2)}) collective-permute-start(bf16[32,32,128]{2,1,0:T(8,128)(2,1)S(1)} %get-tuple-element.41), channel_id=1, source_target_pairs={{0,4},{1,5},{2,6},{3,7},{4,0},{5,1},{6,2},{7,3},{8,12},{9,13},{10,... | collective-permute-start | bytes 786440 | tf_op jit(solution)/shard_map/ppermute | solution.py:279
  37.2 3.1 %collective-permute-start.25 = (bf16[16,32,128]{2,1,0:T(8,128)(2,1)S(1)}, bf16[16,32,128]{2,1,0:T(8,128)(2,1)S(1)}, u32[]{:S(2)}, u32[]{:S(2)}) collective-permute-start(bf16[16,32,128]{2,1,0:T(8,128)(2,1)S(1)} %project.4), channel_id=1, source_target_pairs={{0,4},{1,5},{2,6},{3,7},{4,3},{5,2},{6,1},{7,0},{8,12},{9,13},{10,... | collective-permute-start | bytes 393224 | tf_op jit(solution)/shard_map/ppermute | solution.py:279
  38.4 3.3 %collective-permute-start.24 = (bf16[16,32,128]{2,1,0:T(8,128)(2,1)S(1)}, bf16[16,32,128]{2,1,0:T(8,128)(2,1)S(1)}, u32[]{:S(2)}, u32[]{:S(2)}) collective-permute-start(bf16[16,32,128]{2,1,0:T(8,128)(2,1)S(1)} %project.4), channel_id=1, source_target_pairs={{0,4},{1,5},{2,6},{3,7},{4,2},{5,3},{6,0},{7,1},{8,12},{9,13},{10,... | collective-permute-start | bytes 393224 | tf_op jit(solution)/shard_map/ppermute | solution.py:279
  38.4 3.4 %collective-permute-start.23 = (bf16[16,32,128]{2,1,0:T(8,128)(2,1)S(1)}, bf16[16,32,128]{2,1,0:T(8,128)(2,1)S(1)}, u32[]{:S(2)}, u32[]{:S(2)}) collective-permute-start(bf16[16,32,128]{2,1,0:T(8,128)(2,1)S(1)} %project.4), channel_id=1, source_target_pairs={{0,4},{1,5},{2,6},{3,7},{4,1},{5,0},{6,3},{7,2},{8,12},{9,13},{10,... | collective-permute-start | bytes 393224 | tf_op jit(solution)/shard_map/ppermute | solution.py:279
  39.6 2.1 %collective-permute-start.22 = (bf16[16,32,128]{2,1,0:T(8,128)(2,1)S(1)}, bf16[16,32,128]{2,1,0:T(8,128)(2,1)S(1)}, u32[]{:S(2)}, u32[]{:S(2)}) collective-permute-start(bf16[16,32,128]{2,1,0:T(8,128)(2,1)S(1)} %project.4), channel_id=1, source_target_pairs={{0,4},{1,5},{2,6},{3,7},{4,0},{5,1},{6,2},{7,3},{8,12},{9,13},{10,... | collective-permute-start | bytes 393224 | tf_op jit(solution)/shard_map/ppermute | solution.py:279
  39.6 2.2 %collective-permute-start.26 = (bf16[32,32,128]{2,1,0:T(8,128)(2,1)S(1)}, bf16[32,32,128]{2,1,0:T(8,128)(2,1)S(1)}, u32[]{:S(2)}, u32[]{:S(2)}) collective-permute-start(bf16[32,32,128]{2,1,0:T(8,128)(2,1)S(1)} %collective-permute-done.21.image), channel_id=1, source_target_pairs={{0,4},{1,5},{2,6},{3,7},{4,0},{5,1},{6,2},{7,3},{8,12},{9,13},{10,... | collective-permute-start | bytes 786440 | tf_op jit(solution)/shard_map/ppermute | solution.py:279
  41.7 9.9 %collective-permute-start.30 = (bf16[16,32,128]{2,1,0:T(8,128)(2,1)S(1)}, bf16[16,32,128]{2,1,0:T(8,128)(2,1)S(1)}, u32[]{:S(2)}, u32[]{:S(2)}) collective-permute-start(bf16[16,32,128]{2,1,0:T(8,128)(2,1)S(1)} %get-tuple-element.42), channel_id=1, source_target_pairs={{0,1},{1,0},{2,3},{3,2},{4,16},{5,17},{6,18},{7,19},{8,15},{9,14},... | collective-permute-start | bytes 393224 | tf_op jit(solution)/shard_map/ppermute | solution.py:279
  49.7 4.4 %collective-permute-start.29 = (bf16[16,32,128]{2,1,0:T(8,128)(2,1)S(1)}, bf16[16,32,128]{2,1,0:T(8,128)(2,1)S(1)}, u32[]{:S(2)}, u32[]{:S(2)}) collective-permute-start(bf16[16,32,128]{2,1,0:T(8,128)(2,1)S(1)} %get-tuple-element.42), channel_id=1, source_target_pairs={{0,6},{1,7},{2,4},{3,5},{4,0},{5,1},{6,2},{7,3},{8,14},{9,15},{10,... | collective-permute-start | bytes 393224 | tf_op jit(solution)/shard_map/ppermute | solution.py:279
  49.7 4.4 %collective-permute-start.28 = (bf16[16,32,128]{2,1,0:T(8,128)(2,1)S(1)}, bf16[16,32,128]{2,1,0:T(8,128)(2,1)S(1)}, u32[]{:S(2)}, u32[]{:S(2)}) collective-permute-start(bf16[16,32,128]{2,1,0:T(8,128)(2,1)S(1)} %get-tuple-element.42), channel_id=1, source_target_pairs={{0,5},{1,4},{2,7},{3,6},{4,0},{5,1},{6,2},{7,3},{8,13},{9,12},{10,... | collective-permute-start | bytes 393224 | tf_op jit(solution)/shard_map/ppermute | solution.py:279
  51.0 3.1 %collective-permute-start.27 = (bf16[16,32,128]{2,1,0:T(8,128)(2,1)S(1)}, bf16[16,32,128]{2,1,0:T(8,128)(2,1)S(1)}, u32[]{:S(2)}, u32[]{:S(2)}) collective-permute-start(bf16[16,32,128]{2,1,0:T(8,128)(2,1)S(1)} %get-tuple-element.42), channel_id=1, source_target_pairs={{0,4},{1,5},{2,6},{3,7},{4,0},{5,1},{6,2},{7,3},{8,12},{9,13},{10,... | collective-permute-start | bytes 393224 | tf_op jit(solution)/shard_map/ppermute | solution.py:279
  51.0 3.1 %collective-permute-start.31 = (bf16[32,32,128]{2,1,0:T(8,128)(2,1)S(1)}, bf16[32,32,128]{2,1,0:T(8,128)(2,1)S(1)}, u32[]{:S(2)}, u32[]{:S(2)}) collective-permute-start(bf16[32,32,128]{2,1,0:T(8,128)(2,1)S(1)} %get-tuple-element.43.refs_3_), channel_id=1, source_target_pairs={{0,4},{1,5},{2,6},{3,7},{4,0},{5,1},{6,2},{7,3},{8,12},{9,13},{10,... | collective-permute-start | bytes 786440 | tf_op jit(solution)/shard_map/ppermute | solution.py:279
  54.4 1.6 %collective-permute-start.32 = (bf16[32,32,128]{2,1,0:T(8,128)(2,1)S(1)}, bf16[32,32,128]{2,1,0:T(8,128)(2,1)S(1)}, u32[]{:S(2)}, u32[]{:S(2)}) collective-permute-start(bf16[32,32,128]{2,1,0:T(8,128)(2,1)S(1)} %get-tuple-element.45), channel_id=1, source_target_pairs={{0,4},{1,5},{2,6},{3,7},{4,0},{5,1},{6,2},{7,3},{8,12},{9,13},{10,... | collective-permute-start | bytes 786440 | tf_op jit(solution)/shard_map/ppermute | solution.py:279
  56.0 3.2 %collective-permute-start.36 = (bf16[16,32,128]{2,1,0:T(8,128)(2,1)S(1)}, bf16[16,32,128]{2,1,0:T(8,128)(2,1)S(1)}, u32[]{:S(2)}, u32[]{:S(2)}) collective-permute-start(bf16[16,32,128]{2,1,0:T(8,128)(2,1)S(1)} %project.5), channel_id=1, source_target_pairs={{0,4},{1,5},{2,6},{3,7},{4,3},{5,2},{6,1},{7,0},{8,28},{9,29},{10,... | collective-permute-start | bytes 393224 | tf_op jit(solution)/shard_map/ppermute | solution.py:279
  57.2 3.4 %collective-permute-start.35 = (bf16[16,32,128]{2,1,0:T(8,128)(2,1)S(1)}, bf16[16,32,128]{2,1,0:T(8,128)(2,1)S(1)}, u32[]{:S(2)}, u32[]{:S(2)}) collective-permute-start(bf16[16,32,128]{2,1,0:T(8,128)(2,1)S(1)} %project.5), channel_id=1, source_target_pairs={{0,4},{1,5},{2,6},{3,7},{4,2},{5,3},{6,0},{7,1},{8,12},{9,13},{10,... | collective-permute-start | bytes 393224 | tf_op jit(solution)/shard_map/ppermute | solution.py:279
  57.3 3.3 %collective-permute-start.34 = (bf16[16,32,128]{2,1,0:T(8,128)(2,1)S(1)}, bf16[16,32,128]{2,1,0:T(8,128)(2,1)S(1)}, u32[]{:S(2)}, u32[]{:S(2)}) collective-permute-start(bf16[16,32,128]{2,1,0:T(8,128)(2,1)S(1)} %project.5), channel_id=1, source_target_pairs={{0,4},{1,5},{2,6},{3,7},{4,1},{5,0},{6,3},{7,2},{8,12},{9,13},{10,... | collective-permute-start | bytes 393224 | tf_op jit(solution)/shard_map/ppermute | solution.py:279
  58.5 2.1 %collective-permute-start.33 = (bf16[16,32,128]{2,1,0:T(8,128)(2,1)S(1)}, bf16[16,32,128]{2,1,0:T(8,128)(2,1)S(1)}, u32[]{:S(2)}, u32[]{:S(2)}) collective-permute-start(bf16[16,32,128]{2,1,0:T(8,128)(2,1)S(1)} %project.5), channel_id=1, source_target_pairs={{0,4},{1,5},{2,6},{3,7},{4,0},{5,1},{6,2},{7,3},{8,12},{9,13},{10,... | collective-permute-start | bytes 393224 | tf_op jit(solution)/shard_map/ppermute | solution.py:279
  58.5 2.1 %collective-permute-start.37 = (bf16[32,32,128]{2,1,0:T(8,128)(2,1)S(1)}, bf16[32,32,128]{2,1,0:T(8,128)(2,1)S(1)}, u32[]{:S(2)}, u32[]{:S(2)}) collective-permute-start(bf16[32,32,128]{2,1,0:T(8,128)(2,1)S(1)} %collective-permute-done.32.image), channel_id=1, source_target_pairs={{0,4},{1,5},{2,6},{3,7},{4,0},{5,1},{6,2},{7,3},{8,12},{9,13},{10,... | collective-permute-start | bytes 786440 | tf_op jit(solution)/shard_map/ppermute | solution.py:279
  60.6 9.8 %collective-permute-start.41 = (bf16[16,32,128]{2,1,0:T(8,128)(2,1)S(1)}, bf16[16,32,128]{2,1,0:T(8,128)(2,1)S(1)}, u32[]{:S(2)}, u32[]{:S(2)}) collective-permute-start(bf16[16,32,128]{2,1,0:T(8,128)(2,1)S(1)} %get-tuple-element.46), channel_id=1, source_target_pairs={{0,1},{1,0},{2,3},{3,2},{4,24},{5,25},{6,26},{7,27},{8,15},{9,14},... | collective-permute-start | bytes 393224 | tf_op jit(solution)/shard_map/ppermute | solution.py:279
  68.5 4.4 %collective-permute-start.40 = (bf16[16,32,128]{2,1,0:T(8,128)(2,1)S(1)}, bf16[16,32,128]{2,1,0:T(8,128)(2,1)S(1)}, u32[]{:S(2)}, u32[]{:S(2)}) collective-permute-start(bf16[16,32,128]{2,1,0:T(8,128)(2,1)S(1)} %get-tuple-element.46), channel_id=1, source_target_pairs={{0,6},{1,7},{2,4},{3,5},{4,0},{5,1},{6,2},{7,3},{8,14},{9,15},{10,... | collective-permute-start | bytes 393224 | tf_op jit(solution)/shard_map/ppermute | solution.py:279
  68.5 4.4 %collective-permute-start.39 = (bf16[16,32,128]{2,1,0:T(8,128)(2,1)S(1)}, bf16[16,32,128]{2,1,0:T(8,128)(2,1)S(1)}, u32[]{:S(2)}, u32[]{:S(2)}) collective-permute-start(bf16[16,32,128]{2,1,0:T(8,128)(2,1)S(1)} %get-tuple-element.46), channel_id=1, source_target_pairs={{0,5},{1,4},{2,7},{3,6},{4,0},{5,1},{6,2},{7,3},{8,13},{9,12},{10,... | collective-permute-start | bytes 393224 | tf_op jit(solution)/shard_map/ppermute | solution.py:279
  69.5 3.5 %collective-permute-start.38 = (bf16[16,32,128]{2,1,0:T(8,128)(2,1)S(1)}, bf16[16,32,128]{2,1,0:T(8,128)(2,1)S(1)}, u32[]{:S(2)}, u32[]{:S(2)}) collective-permute-start(bf16[16,32,128]{2,1,0:T(8,128)(2,1)S(1)} %get-tuple-element.46), channel_id=1, source_target_pairs={{0,4},{1,5},{2,6},{3,7},{4,0},{5,1},{6,2},{7,3},{8,12},{9,13},{10,... | collective-permute-start | bytes 393224 | tf_op jit(solution)/shard_map/ppermute | solution.py:279
  69.5 3.4 %collective-permute-start.42 = (bf16[32,32,128]{2,1,0:T(8,128)(2,1)S(1)}, bf16[32,32,128]{2,1,0:T(8,128)(2,1)S(1)}, u32[]{:S(2)}, u32[]{:S(2)}) collective-permute-start(bf16[32,32,128]{2,1,0:T(8,128)(2,1)S(1)} %get-tuple-element.47.refs_3_), channel_id=1, source_target_pairs={{0,4},{1,5},{2,6},{3,7},{4,0},{5,1},{6,2},{7,3},{8,12},{9,13},{10,... | collective-permute-start | bytes 786440 | tf_op jit(solution)/shard_map/ppermute | solution.py:279

commit v16 on v15

--- a/solution.py
+++ b/solution.py
@@ -290,11 +290,8 @@
     def passed(terms, core, place):
         if not direct:
             return [swapped(lax.psum(terms, "tile"))]
-        if core == 1:
-            ahead = place + 1 if place + 1 < places else place - 2
-        else:
-            ahead = place + 2 if place + 2 < places else 0
-        helped = place > 0 and ahead >= 0 and ahead != place
+        ahead = place + 2 if place + 2 < places else 0
+        helped = core == 0 and place > 0
 
         def way(d):
             def target(p, c, t):

time: 73.9 us -> 74.9 us (1.014)
  starting transfers between devices: 42.9 us -> 44.2 us
    ppermute x43, starting transfers between devices: 42.9 us -> 44.2 us  [sent(): return lax.ppermute(value, ('subset', 'tile'), pairs)]
where the time goes in v16:
time: 74.9 us; the launch traced here: 74.7 us
  starting transfers between devices  44.2 us (59%)
  waiting for transfers between devices  23.6 us (32%)
  Pallas kernels  6.73 us (9%)
    ppermute x43, starting transfers between devices, sent(): return lax.ppermute(value, ('subset', 'tile'), pairs)  44.2 us
    ppermute x43, waiting for transfers between devices, sent(): return lax.ppermute(value, ('subset', 'tile'), pairs)  23.6 us
    pallas_call x1, Pallas kernels, per_device(): pl.pallas_call(functools.partial(head_kernel, row_blocks, chunks), out_sh...  3.09 us
    pallas_call x19, Pallas kernels, call(): pl.pallas_call(kernel, out_shape=out_shape, in_specs=[SMEM] * smem + [VME...  1.84 us
  transfers between devices with their start and end apart: 43, of which 18 were waited for; matrix products, arithmetic and copies ran while one was open for 0% of the time, Pallas kernels for 7%

profile of v16, /device:TPU:1, one launch (start us, length us, event | category | flops | bytes accessed | tf_op | source)
XLA Modules:
  0.0 74.7 jit_solution(9483641417512103900)
XLA Ops:
  0.1 3.1 %head.1 = (bf16[5,32,128]{2,1,0:T(8,128)(2,1)S(1)}, s32[2,80]{1,0:T(2,128)S(1)}, s32[3,80]{1,0:T(4,128)S(4)}, bf16[1,1,80,128,128]{4,3,2,1,0:T(8,128)(2,1)S(1)}) custom-call(s32[3]{0:T(128)S(1)} %pad_add_fusion.pos, s32[1,1,80]{2,1,0:T(1,128)} %rows_in.1, s32[1,1,80]{2,1,0:T(1,128)} %cols_in.1, bf16[1,1,80,128,128]{4,3,2,1,0:T(8,128)(2,1)} %blocks_in.1, ...), custom_call_target="tpu_custom_call" | custom-call | tf_op jit(solution)/shard_map/head/pallas_call | solution.py:325
  3.2 3.7 %collective-permute-start.4 = (bf16[5,32,128]{2,1,0:T(8,128)(2,1)S(1)}, bf16[5,32,128]{2,1,0:T(8,128)(2,1)S(1)}, u32[]{:S(2)}, u32[]{:S(2)}) collective-permute-start(bf16[5,32,128]{2,1,0:T(8,128)(2,1)S(1)} %get-tuple-element.31._.refs_2_), channel_id=1, source_target_pairs={{0,3},{1,2},{2,1},{3,0},{4,7},{5,6},{6,5},{7,4},{8,11},{9,10},{10,... | collective-permute-start | bytes 122888 | tf_op jit(solution)/shard_map/ppermute | solution.py:279
  6.9 0.2 collective-permute-start.3
  7.3 0.6 collective-permute-start
  7.8 0.5 pack_own.1.refs_1_
  8.3 0.3 collective-permute-done.table2
  8.7 1.3 %pack_other.1 = (s32[3,80]{1,0:T(4,128)S(4)}, bf16[16,640,128]{2,1,0:T(8,128)(2,1)S(1)}) custom-call(s32[3,80]{1,0:T(4,128)S(4)} %get-tuple-element.27.own, s32[2,80]{1,0:T(2,128)S(1)} %collective-permute-done.table2, bf16[1,1,80,128,128]{4,3,2,1,0:T(8,128)(2,1)S(1)} %collective-permute-done.1.blocks2), custom_call_target="tpu_custom_call" | custom-call | tf_op jit(solution)/shard_map/pack_other/pallas_call | solution.py:366
  10.1 2.9 %collective-permute-start.8 = (bf16[16,32,128]{2,1,0:T(8,128)(2,1)S(1)}, bf16[16,32,128]{2,1,0:T(8,128)(2,1)S(1)}, u32[]{:S(2)}, u32[]{:S(2)}) collective-permute-start(bf16[16,32,128]{2,1,0:T(8,128)(2,1)S(1)} %get-tuple-element.35), channel_id=1, source_target_pairs={{0,7},{1,6},{2,5},{3,4},{4,0},{5,1},{6,2},{7,3},{8,15},{9,14},{10,... | collective-permute-start | bytes 393224 | tf_op jit(solution)/shard_map/ppermute | solution.py:279
  13.1 1.5 %collective-permute-start.6 = (bf16[16,32,128]{2,1,0:T(8,128)(2,1)S(1)}, bf16[16,32,128]{2,1,0:T(8,128)(2,1)S(1)}, u32[]{:S(2)}, u32[]{:S(2)}) collective-permute-start(bf16[16,32,128]{2,1,0:T(8,128)(2,1)S(1)} %get-tuple-element.35), channel_id=1, source_target_pairs={{0,5},{1,4},{2,7},{3,6},{4,0},{5,1},{6,2},{7,3},{8,13},{9,12},{10,... | collective-permute-start | bytes 393224 | tf_op jit(solution)/shard_map/ppermute | solution.py:279
  14.6 0.5 collective-permute-start.9
  15.1 1.7 %collective-permute-done.8.refs_6_ = bf16[16,32,128]{2,1,0:T(8,128)(2,1)S(1)} collective-permute-done((bf16[16,32,128]{2,1,0:T(8,128)(2,1)S(1)}, bf16[16,32,128]{2,1,0:T(8,128)(2,1)S(1)}, u32[]{:S(2)}, u32[]{:S(2)}) %collective-permute-start.8) | collective-permute-done | bytes 131104 | tf_op jit(solution)/shard_map/ppermute | solution.py:279
  16.8 1.3 %collective-permute-done.7.refs_5_ = bf16[16,32,128]{2,1,0:T(8,128)(2,1)S(1)} collective-permute-done((bf16[16,32,128]{2,1,0:T(8,128)(2,1)S(1)}, bf16[16,32,128]{2,1,0:T(8,128)(2,1)S(1)}, u32[]{:S(2)}, u32[]{:S(2)}) %collective-permute-start.7) | collective-permute-done | bytes 131104 | tf_op jit(solution)/shard_map/ppermute | solution.py:279
  18.1 0.6 update.9.refs_1_
  18.9 3.3 %collective-permute-done.10.image = bf16[32,32,128]{2,1,0:T(8,128)(2,1)S(1)} collective-permute-done((bf16[32,32,128]{2,1,0:T(8,128)(2,1)S(1)}, bf16[32,32,128]{2,1,0:T(8,128)(2,1)S(1)}, u32[]{:S(2)}, u32[]{:S(2)}) %collective-permute-start.10) | collective-permute-done | bytes 262176 | tf_op jit(solution)/shard_map/ppermute | solution.py:279
  22.3 2.9 %collective-permute-start.14 = (bf16[16,32,128]{2,1,0:T(8,128)(2,1)S(1)}, bf16[16,32,128]{2,1,0:T(8,128)(2,1)S(1)}, u32[]{:S(2)}, u32[]{:S(2)}) collective-permute-start(bf16[16,32,128]{2,1,0:T(8,128)(2,1)S(1)} %project.3), channel_id=1, source_target_pairs={{0,4},{1,5},{2,6},{3,7},{4,3},{5,2},{6,1},{7,0},{8,12},{9,13},{10,... | collective-permute-start | bytes 393224 | tf_op jit(solution)/shard_map/ppermute | solution.py:279
  25.1 1.0 %collective-permute-start.12 = (bf16[16,32,128]{2,1,0:T(8,128)(2,1)S(1)}, bf16[16,32,128]{2,1,0:T(8,128)(2,1)S(1)}, u32[]{:S(2)}, u32[]{:S(2)}) collective-permute-start(bf16[16,32,128]{2,1,0:T(8,128)(2,1)S(1)} %project.3), channel_id=1, source_target_pairs={{0,4},{1,5},{2,6},{3,7},{4,1},{5,0},{6,3},{7,2},{8,12},{9,13},{10,... | collective-permute-start | bytes 393224 | tf_op jit(solution)/shard_map/ppermute | solution.py:279
  26.1 0.5 collective-permute-start.15
  26.7 0.4 collective-permute-done.14.refs_6_
  27.1 1.4 %collective-permute-done.13.refs_5_ = bf16[16,32,128]{2,1,0:T(8,128)(2,1)S(1)} collective-permute-done((bf16[16,32,128]{2,1,0:T(8,128)(2,1)S(1)}, bf16[16,32,128]{2,1,0:T(8,128)(2,1)S(1)}, u32[]{:S(2)}, u32[]{:S(2)}) %collective-permute-start.13) | collective-permute-done | bytes 131104 | tf_op jit(solution)/shard_map/ppermute | solution.py:279
  28.5 1.8 %collective-permute-start.19 = (bf16[16,32,128]{2,1,0:T(8,128)(2,1)S(1)}, bf16[16,32,128]{2,1,0:T(8,128)(2,1)S(1)}, u32[]{:S(2)}, u32[]{:S(2)}) collective-permute-start(bf16[16,32,128]{2,1,0:T(8,128)(2,1)S(1)} %get-tuple-element.38), channel_id=1, source_target_pairs={{0,7},{1,6},{2,5},{3,4},{4,0},{5,1},{6,2},{7,3},{8,15},{9,14},{10,... | collective-permute-start | bytes 393224 | tf_op jit(solution)/shard_map/ppermute | solution.py:279
  30.4 1.1 %collective-permute-start.17 = (bf16[16,32,128]{2,1,0:T(8,128)(2,1)S(1)}, bf16[16,32,128]{2,1,0:T(8,128)(2,1)S(1)}, u32[]{:S(2)}, u32[]{:S(2)}) collective-permute-start(bf16[16,32,128]{2,1,0:T(8,128)(2,1)S(1)} %get-tuple-element.38), channel_id=1, source_target_pairs={{0,5},{1,4},{2,7},{3,6},{4,0},{5,1},{6,2},{7,3},{8,13},{9,12},{10,... | collective-permute-start | bytes 393224 | tf_op jit(solution)/shard_map/ppermute | solution.py:279
  31.6 0.4 collective-permute-start.20
  32.0 2.1 %collective-permute-done.19.refs_6_ = bf16[16,32,128]{2,1,0:T(8,128)(2,1)S(1)} collective-permute-done((bf16[16,32,128]{2,1,0:T(8,128)(2,1)S(1)}, bf16[16,32,128]{2,1,0:T(8,128)(2,1)S(1)}, u32[]{:S(2)}, u32[]{:S(2)}) %collective-permute-start.19) | collective-permute-done | bytes 131104 | tf_op jit(solution)/shard_map/ppermute | solution.py:279
  34.2 1.3 %collective-permute-done.18.refs_5_ = bf16[16,32,128]{2,1,0:T(8,128)(2,1)S(1)} collective-permute-done((bf16[16,32,128]{2,1,0:T(8,128)(2,1)S(1)}, bf16[16,32,128]{2,1,0:T(8,128)(2,1)S(1)}, u32[]{:S(2)}, u32[]{:S(2)}) %collective-permute-start.18) | collective-permute-done | bytes 131104 | tf_op jit(solution)/shard_map/ppermute | solution.py:279
  35.7 1.5 %collective-permute-done.21.image = bf16[32,32,128]{2,1,0:T(8,128)(2,1)S(1)} collective-permute-done((bf16[32,32,128]{2,1,0:T(8,128)(2,1)S(1)}, bf16[32,32,128]{2,1,0:T(8,128)(2,1)S(1)}, u32[]{:S(2)}, u32[]{:S(2)}) %collective-permute-start.21) | collective-permute-done | bytes 262176 | tf_op jit(solution)/shard_map/ppermute | solution.py:279
  37.2 1.2 %collective-permute-start.25 = (bf16[16,32,128]{2,1,0:T(8,128)(2,1)S(1)}, bf16[16,32,128]{2,1,0:T(8,128)(2,1)S(1)}, u32[]{:S(2)}, u32[]{:S(2)}) collective-permute-start(bf16[16,32,128]{2,1,0:T(8,128)(2,1)S(1)} %project.4), channel_id=1, source_target_pairs={{0,4},{1,5},{2,6},{3,7},{4,3},{5,2},{6,1},{7,0},{8,12},{9,13},{10,... | collective-permute-start | bytes 393224 | tf_op jit(solution)/shard_map/ppermute | solution.py:279
  38.4 1.2 %collective-permute-start.23 = (bf16[16,32,128]{2,1,0:T(8,128)(2,1)S(1)}, bf16[16,32,128]{2,1,0:T(8,128)(2,1)S(1)}, u32[]{:S(2)}, u32[]{:S(2)}) collective-permute-start(bf16[16,32,128]{2,1,0:T(8,128)(2,1)S(1)} %project.4), channel_id=1, source_target_pairs={{0,4},{1,5},{2,6},{3,7},{4,1},{5,0},{6,3},{7,2},{8,12},{9,13},{10,... | collective-permute-start | bytes 393224 | tf_op jit(solution)/shard_map/ppermute | solution.py:279
  39.6 0.5 collective-permute-start.26
  40.1 0.2 collective-permute-done.25.refs_6_
  40.3 1.4 %collective-permute-done.24.refs_5_ = bf16[16,32,128]{2,1,0:T(8,128)(2,1)S(1)} collective-permute-done((bf16[16,32,128]{2,1,0:T(8,128)(2,1)S(1)}, bf16[16,32,128]{2,1,0:T(8,128)(2,1)S(1)}, u32[]{:S(2)}, u32[]{:S(2)}) %collective-permute-start.24) | collective-permute-done | bytes 131104 | tf_op jit(solution)/shard_map/ppermute | solution.py:279
  41.7 8.8 %collective-permute-start.30 = (bf16[16,32,128]{2,1,0:T(8,128)(2,1)S(1)}, bf16[16,32,128]{2,1,0:T(8,128)(2,1)S(1)}, u32[]{:S(2)}, u32[]{:S(2)}) collective-permute-start(bf16[16,32,128]{2,1,0:T(8,128)(2,1)S(1)} %get-tuple-element.42), channel_id=1, source_target_pairs={{0,1},{1,0},{2,3},{3,2},{4,16},{5,17},{6,18},{7,19},{8,15},{9,14},... | collective-permute-start | bytes 393224 | tf_op jit(solution)/shard_map/ppermute | solution.py:279
  50.5 1.3 %collective-permute-start.28 = (bf16[16,32,128]{2,1,0:T(8,128)(2,1)S(1)}, bf16[16,32,128]{2,1,0:T(8,128)(2,1)S(1)}, u32[]{:S(2)}, u32[]{:S(2)}) collective-permute-start(bf16[16,32,128]{2,1,0:T(8,128)(2,1)S(1)} %get-tuple-element.42), channel_id=1, source_target_pairs={{0,5},{1,4},{2,7},{3,6},{4,0},{5,1},{6,2},{7,3},{8,13},{9,12},{10,... | collective-permute-start | bytes 393224 | tf_op jit(solution)/shard_map/ppermute | solution.py:279
  51.8 0.5 collective-permute-start.31
  52.3 0.2 collective-permute-done.30.refs_6_
  52.5 2.4 %collective-permute-done.29.refs_5_ = bf16[16,32,128]{2,1,0:T(8,128)(2,1)S(1)} collective-permute-done((bf16[16,32,128]{2,1,0:T(8,128)(2,1)S(1)}, bf16[16,32,128]{2,1,0:T(8,128)(2,1)S(1)}, u32[]{:S(2)}, u32[]{:S(2)}) %collective-permute-start.29) | collective-permute-done | bytes 131104 | tf_op jit(solution)/shard_map/ppermute | solution.py:279
  55.0 0.3 second.6
  55.3 1.5 %collective-permute-done.32.image = bf16[32,32,128]{2,1,0:T(8,128)(2,1)S(1)} collective-permute-done((bf16[32,32,128]{2,1,0:T(8,128)(2,1)S(1)}, bf16[32,32,128]{2,1,0:T(8,128)(2,1)S(1)}, u32[]{:S(2)}, u32[]{:S(2)}) %collective-permute-start.32) | collective-permute-done | bytes 262176 | tf_op jit(solution)/shard_map/ppermute | solution.py:279
  56.8 1.2 %collective-permute-start.36 = (bf16[16,32,128]{2,1,0:T(8,128)(2,1)S(1)}, bf16[16,32,128]{2,1,0:T(8,128)(2,1)S(1)}, u32[]{:S(2)}, u32[]{:S(2)}) collective-permute-start(bf16[16,32,128]{2,1,0:T(8,128)(2,1)S(1)} %project.5), channel_id=1, source_target_pairs={{0,4},{1,5},{2,6},{3,7},{4,3},{5,2},{6,1},{7,0},{8,12},{9,13},{10,... | collective-permute-start | bytes 393224 | tf_op jit(solution)/shard_map/ppermute | solution.py:279
  58.0 1.2 %collective-permute-start.34 = (bf16[16,32,128]{2,1,0:T(8,128)(2,1)S(1)}, bf16[16,32,128]{2,1,0:T(8,128)(2,1)S(1)}, u32[]{:S(2)}, u32[]{:S(2)}) collective-permute-start(bf16[16,32,128]{2,1,0:T(8,128)(2,1)S(1)} %project.5), channel_id=1, source_target_pairs={{0,4},{1,5},{2,6},{3,7},{4,1},{5,0},{6,3},{7,2},{8,12},{9,13},{10,... | collective-permute-start | bytes 393224 | tf_op jit(solution)/shard_map/ppermute | solution.py:279
  59.2 0.5 collective-permute-start.37
  59.8 0.2 collective-permute-done.36.refs_6_
  59.9 1.4 %collective-permute-done.35.refs_5_ = bf16[16,32,128]{2,1,0:T(8,128)(2,1)S(1)} collective-permute-done((bf16[16,32,128]{2,1,0:T(8,128)(2,1)S(1)}, bf16[16,32,128]{2,1,0:T(8,128)(2,1)S(1)}, u32[]{:S(2)}, u32[]{:S(2)}) %collective-permute-start.35) | collective-permute-done | bytes 131104 | tf_op jit(solution)/shard_map/ppermute | solution.py:279
  61.4 8.2 %collective-permute-start.41 = (bf16[16,32,128]{2,1,0:T(8,128)(2,1)S(1)}, bf16[16,32,128]{2,1,0:T(8,128)(2,1)S(1)}, u32[]{:S(2)}, u32[]{:S(2)}) collective-permute-start(bf16[16,32,128]{2,1,0:T(8,128)(2,1)S(1)} %get-tuple-element.46), channel_id=1, source_target_pairs={{0,1},{1,0},{2,3},{3,2},{4,24},{5,25},{6,26},{7,27},{8,15},{9,14},... | collective-permute-start | bytes 393224 | tf_op jit(solution)/shard_map/ppermute | solution.py:279
  69.6 1.3 %collective-permute-start.39 = (bf16[16,32,128]{2,1,0:T(8,128)(2,1)S(1)}, bf16[16,32,128]{2,1,0:T(8,128)(2,1)S(1)}, u32[]{:S(2)}, u32[]{:S(2)}) collective-permute-start(bf16[16,32,128]{2,1,0:T(8,128)(2,1)S(1)} %get-tuple-element.46), channel_id=1, source_target_pairs={{0,5},{1,4},{2,7},{3,6},{4,0},{5,1},{6,2},{7,3},{8,13},{9,12},{10,... | collective-permute-start | bytes 393224 | tf_op jit(solution)/shard_map/ppermute | solution.py:279
  70.8 0.5 collective-permute-start.42
  71.3 0.2 collective-permute-done.41.refs_6_
  71.5 2.4 %collective-permute-done.40.refs_5_ = bf16[16,32,128]{2,1,0:T(8,128)(2,1)S(1)} collective-permute-done((bf16[16,32,128]{2,1,0:T(8,128)(2,1)S(1)}, bf16[16,32,128]{2,1,0:T(8,128)(2,1)S(1)}, u32[]{:S(2)}, u32[]{:S(2)}) %collective-permute-start.40) | collective-permute-done | bytes 131104 | tf_op jit(solution)/shard_map/ppermute | solution.py:279
  74.0 0.8 %second.7 = bf16[4,8,4096]{2,1,0:T(8,128)(2,1)} custom-call(s32[3,80]{1,0:T(4,128)S(4)} %get-tuple-element.29.refs_0_.info, f32[32,32,128]{2,1,0:T(8,128)S(1)} %update.15.refs_1_, bf16[32,32,128]{2,1,0:T(8,128)(2,1)S(1)} %collective-permute-done.42.refs_2_, bf16[32,32,128]{2,1,0:T(8,128)(2,1)S(1)} %get-tuple-element.47.refs_3_, ...), custom_call_target="tpu_custom_call" | custom-call | tf_op jit(solution)/shard_map/second/pallas_call | solution.py:310
  (61 shorter events, 1.2 us)
Async XLA Ops:
  0.0 8.7 %collective-permute-start.1 = (bf16[1,1,80,128,128]{4,3,2,1,0:T(8,128)(2,1)}, bf16[1,1,80,128,128]{4,3,2,1,0:T(8,128)(2,1)S(1)}, u32[]{:S(2)}, u32[]{:S(2)}) collective-permute-start(bf16[1,1,80,128,128]{4,3,2,1,0:T(8,128)(2,1)} %blocks_in.1), channel_id=1, source_target_pairs={{0,4},{1,5},{2,6},{3,7},{4,0},{5,1},{6,2},{7,3},{8,12},{9,13},{10,... | collective-permute-start | bytes 7864328 | tf_op jit(solution)/shard_map/ppermute | solution.py:279
  3.2 6.8 %collective-permute-start.4 = (bf16[5,32,128]{2,1,0:T(8,128)(2,1)S(1)}, bf16[5,32,128]{2,1,0:T(8,128)(2,1)S(1)}, u32[]{:S(2)}, u32[]{:S(2)}) collective-permute-start(bf16[5,32,128]{2,1,0:T(8,128)(2,1)S(1)} %get-tuple-element.31._.refs_2_), channel_id=1, source_target_pairs={{0,3},{1,2},{2,1},{3,0},{4,7},{5,6},{6,5},{7,4},{8,11},{9,10},{10,... | collective-permute-start | bytes 122888 | tf_op jit(solution)/shard_map/ppermute | solution.py:279
  6.9 3.1 %collective-permute-start.3 = (bf16[5,32,128]{2,1,0:T(8,128)(2,1)S(1)}, bf16[5,32,128]{2,1,0:T(8,128)(2,1)S(1)}, u32[]{:S(2)}, u32[]{:S(2)}) collective-permute-start(bf16[5,32,128]{2,1,0:T(8,128)(2,1)S(1)} %get-tuple-element.31._.refs_2_), channel_id=1, source_target_pairs={{0,2},{1,3},{2,0},{3,1},{4,6},{5,7},{6,4},{7,5},{8,10},{9,11},{10,... | collective-permute-start | bytes 122888 | tf_op jit(solution)/shard_map/ppermute | solution.py:279
  7.1 2.9 %collective-permute-start.2 = (bf16[5,32,128]{2,1,0:T(8,128)(2,1)S(1)}, bf16[5,32,128]{2,1,0:T(8,128)(2,1)S(1)}, u32[]{:S(2)}, u32[]{:S(2)}) collective-permute-start(bf16[5,32,128]{2,1,0:T(8,128)(2,1)S(1)} %get-tuple-element.31._.refs_2_), channel_id=1, source_target_pairs={{0,1},{1,0},{2,3},{3,2},{4,5},{5,4},{6,7},{7,6},{8,9},{9,8},{10,11... | collective-permute-start | bytes 122888 | tf_op jit(solution)/shard_map/ppermute | solution.py:279
  7.3 1.4 %collective-permute-start = (s32[2,80]{1,0:T(2,128)S(1)}, s32[2,80]{1,0:T(2,128)S(1)}, u32[]{:S(2)}, u32[]{:S(2)}) collective-permute-start(s32[2,80]{1,0:T(2,128)S(1)} %get-tuple-element.28), channel_id=1, source_target_pairs={{0,4},{1,5},{2,6},{3,7},{4,0},{5,1},{6,2},{7,3},{8,12},{9,13},{10,... | collective-permute-start | bytes 1928 | tf_op jit(solution)/shard_map/ppermute | solution.py:279
  10.1 6.7 %collective-permute-start.8 = (bf16[16,32,128]{2,1,0:T(8,128)(2,1)S(1)}, bf16[16,32,128]{2,1,0:T(8,128)(2,1)S(1)}, u32[]{:S(2)}, u32[]{:S(2)}) collective-permute-start(bf16[16,32,128]{2,1,0:T(8,128)(2,1)S(1)} %get-tuple-element.35), channel_id=1, source_target_pairs={{0,7},{1,6},{2,5},{3,4},{4,0},{5,1},{6,2},{7,3},{8,15},{9,14},{10,... | collective-permute-start | bytes 393224 | tf_op jit(solution)/shard_map/ppermute | solution.py:279
  13.0 5.2 %collective-permute-start.7 = (bf16[16,32,128]{2,1,0:T(8,128)(2,1)S(1)}, bf16[16,32,128]{2,1,0:T(8,128)(2,1)S(1)}, u32[]{:S(2)}, u32[]{:S(2)}) collective-permute-start(bf16[16,32,128]{2,1,0:T(8,128)(2,1)S(1)} %get-tuple-element.35), channel_id=1, source_target_pairs={{0,6},{1,7},{2,4},{3,5},{4,0},{5,1},{6,2},{7,3},{8,14},{9,15},{10,... | collective-permute-start | bytes 393224 | tf_op jit(solution)/shard_map/ppermute | solution.py:279
  13.1 5.0 %collective-permute-start.6 = (bf16[16,32,128]{2,1,0:T(8,128)(2,1)S(1)}, bf16[16,32,128]{2,1,0:T(8,128)(2,1)S(1)}, u32[]{:S(2)}, u32[]{:S(2)}) collective-permute-start(bf16[16,32,128]{2,1,0:T(8,128)(2,1)S(1)} %get-tuple-element.35), channel_id=1, source_target_pairs={{0,5},{1,4},{2,7},{3,6},{4,0},{5,1},{6,2},{7,3},{8,13},{9,12},{10,... | collective-permute-start | bytes 393224 | tf_op jit(solution)/shard_map/ppermute | solution.py:279
  14.6 3.5 %collective-permute-start.5 = (bf16[16,32,128]{2,1,0:T(8,128)(2,1)S(1)}, bf16[16,32,128]{2,1,0:T(8,128)(2,1)S(1)}, u32[]{:S(2)}, u32[]{:S(2)}) collective-permute-start(bf16[16,32,128]{2,1,0:T(8,128)(2,1)S(1)} %get-tuple-element.35), channel_id=1, source_target_pairs={{0,4},{1,5},{2,6},{3,7},{4,0},{5,1},{6,2},{7,3},{8,12},{9,13},{10,... | collective-permute-start | bytes 393224 | tf_op jit(solution)/shard_map/ppermute | solution.py:279
  14.6 4.1 %collective-permute-start.9 = (bf16[32,32,128]{2,1,0:T(8,128)(2,1)S(1)}, bf16[32,32,128]{2,1,0:T(8,128)(2,1)S(1)}, u32[]{:S(2)}, u32[]{:S(2)}) collective-permute-start(bf16[32,32,128]{2,1,0:T(8,128)(2,1)S(1)} %get-tuple-element.36.refs_3_), channel_id=1, source_target_pairs={{0,4},{1,5},{2,6},{3,7},{4,0},{5,1},{6,2},{7,3},{8,12},{9,13},{10,... | collective-permute-start | bytes 786440 | tf_op jit(solution)/shard_map/ppermute | solution.py:279
  18.8 3.4 %collective-permute-start.10 = (bf16[32,32,128]{2,1,0:T(8,128)(2,1)S(1)}, bf16[32,32,128]{2,1,0:T(8,128)(2,1)S(1)}, u32[]{:S(2)}, u32[]{:S(2)}) collective-permute-start(bf16[32,32,128]{2,1,0:T(8,128)(2,1)S(1)} %get-tuple-element.37), channel_id=1, source_target_pairs={{0,4},{1,5},{2,6},{3,7},{4,12},{5,13},{6,14},{7,15},{8,0},{9,1},{1... | collective-permute-start | bytes 786440 | tf_op jit(solution)/shard_map/ppermute | solution.py:279
  22.3 4.8 %collective-permute-start.14 = (bf16[16,32,128]{2,1,0:T(8,128)(2,1)S(1)}, bf16[16,32,128]{2,1,0:T(8,128)(2,1)S(1)}, u32[]{:S(2)}, u32[]{:S(2)}) collective-permute-start(bf16[16,32,128]{2,1,0:T(8,128)(2,1)S(1)} %project.3), channel_id=1, source_target_pairs={{0,4},{1,5},{2,6},{3,7},{4,3},{5,2},{6,1},{7,0},{8,12},{9,13},{10,... | collective-permute-start | bytes 393224 | tf_op jit(solution)/shard_map/ppermute | solution.py:279
  25.1 3.3 %collective-permute-start.13 = (bf16[16,32,128]{2,1,0:T(8,128)(2,1)S(1)}, bf16[16,32,128]{2,1,0:T(8,128)(2,1)S(1)}, u32[]{:S(2)}, u32[]{:S(2)}) collective-permute-start(bf16[16,32,128]{2,1,0:T(8,128)(2,1)S(1)} %project.3), channel_id=1, source_target_pairs={{0,4},{1,5},{2,6},{3,7},{4,2},{5,3},{6,0},{7,1},{8,12},{9,13},{10,... | collective-permute-start | bytes 393224 | tf_op jit(solution)/shard_map/ppermute | solution.py:279
  25.1 3.4 %collective-permute-start.12 = (bf16[16,32,128]{2,1,0:T(8,128)(2,1)S(1)}, bf16[16,32,128]{2,1,0:T(8,128)(2,1)S(1)}, u32[]{:S(2)}, u32[]{:S(2)}) collective-permute-start(bf16[16,32,128]{2,1,0:T(8,128)(2,1)S(1)} %project.3), channel_id=1, source_target_pairs={{0,4},{1,5},{2,6},{3,7},{4,1},{5,0},{6,3},{7,2},{8,12},{9,13},{10,... | collective-permute-start | bytes 393224 | tf_op jit(solution)/shard_map/ppermute | solution.py:279
  26.1 2.4 %collective-permute-start.11 = (bf16[16,32,128]{2,1,0:T(8,128)(2,1)S(1)}, bf16[16,32,128]{2,1,0:T(8,128)(2,1)S(1)}, u32[]{:S(2)}, u32[]{:S(2)}) collective-permute-start(bf16[16,32,128]{2,1,0:T(8,128)(2,1)S(1)} %project.3), channel_id=1, source_target_pairs={{0,4},{1,5},{2,6},{3,7},{4,0},{5,1},{6,2},{7,3},{8,12},{9,13},{10,... | collective-permute-start | bytes 393224 | tf_op jit(solution)/shard_map/ppermute | solution.py:279
  26.1 2.4 %collective-permute-start.15 = (bf16[32,32,128]{2,1,0:T(8,128)(2,1)S(1)}, bf16[32,32,128]{2,1,0:T(8,128)(2,1)S(1)}, u32[]{:S(2)}, u32[]{:S(2)}) collective-permute-start(bf16[32,32,128]{2,1,0:T(8,128)(2,1)S(1)} %collective-permute-done.10.image), channel_id=1, source_target_pairs={{0,4},{1,5},{2,6},{3,7},{4,0},{5,1},{6,2},{7,3},{8,12},{9,13},{10,... | collective-permute-start | bytes 786440 | tf_op jit(solution)/shard_map/ppermute | solution.py:279
  28.5 5.7 %collective-permute-start.19 = (bf16[16,32,128]{2,1,0:T(8,128)(2,1)S(1)}, bf16[16,32,128]{2,1,0:T(8,128)(2,1)S(1)}, u32[]{:S(2)}, u32[]{:S(2)}) collective-permute-start(bf16[16,32,128]{2,1,0:T(8,128)(2,1)S(1)} %get-tuple-element.38), channel_id=1, source_target_pairs={{0,7},{1,6},{2,5},{3,4},{4,0},{5,1},{6,2},{7,3},{8,15},{9,14},{10,... | collective-permute-start | bytes 393224 | tf_op jit(solution)/shard_map/ppermute | solution.py:279
  30.3 5.2 %collective-permute-start.18 = (bf16[16,32,128]{2,1,0:T(8,128)(2,1)S(1)}, bf16[16,32,128]{2,1,0:T(8,128)(2,1)S(1)}, u32[]{:S(2)}, u32[]{:S(2)}) collective-permute-start(bf16[16,32,128]{2,1,0:T(8,128)(2,1)S(1)} %get-tuple-element.38), channel_id=1, source_target_pairs={{0,6},{1,7},{2,4},{3,5},{4,0},{5,1},{6,2},{7,3},{8,14},{9,15},{10,... | collective-permute-start | bytes 393224 | tf_op jit(solution)/shard_map/ppermute | solution.py:279
  30.4 5.1 %collective-permute-start.17 = (bf16[16,32,128]{2,1,0:T(8,128)(2,1)S(1)}, bf16[16,32,128]{2,1,0:T(8,128)(2,1)S(1)}, u32[]{:S(2)}, u32[]{:S(2)}) collective-permute-start(bf16[16,32,128]{2,1,0:T(8,128)(2,1)S(1)} %get-tuple-element.38), channel_id=1, source_target_pairs={{0,5},{1,4},{2,7},{3,6},{4,0},{5,1},{6,2},{7,3},{8,13},{9,12},{10,... | collective-permute-start | bytes 393224 | tf_op jit(solution)/shard_map/ppermute | solution.py:279
  31.5 4.0 %collective-permute-start.16 = (bf16[16,32,128]{2,1,0:T(8,128)(2,1)S(1)}, bf16[16,32,128]{2,1,0:T(8,128)(2,1)S(1)}, u32[]{:S(2)}, u32[]{:S(2)}) collective-permute-start(bf16[16,32,128]{2,1,0:T(8,128)(2,1)S(1)} %get-tuple-element.38), channel_id=1, source_target_pairs={{0,4},{1,5},{2,6},{3,7},{4,0},{5,1},{6,2},{7,3},{8,12},{9,13},{10,... | collective-permute-start | bytes 393224 | tf_op jit(solution)/shard_map/ppermute | solution.py:279
  31.6 3.9 %collective-permute-start.20 = (bf16[32,32,128]{2,1,0:T(8,128)(2,1)S(1)}, bf16[32,32,128]{2,1,0:T(8,128)(2,1)S(1)}, u32[]{:S(2)}, u32[]{:S(2)}) collective-permute-start(bf16[32,32,128]{2,1,0:T(8,128)(2,1)S(1)} %get-tuple-element.39.refs_3_), channel_id=1, source_target_pairs={{0,4},{1,5},{2,6},{3,7},{4,0},{5,1},{6,2},{7,3},{8,12},{9,13},{10,... | collective-permute-start | bytes 786440 | tf_op jit(solution)/shard_map/ppermute | solution.py:279
  35.6 1.6 %collective-permute-start.21 = (bf16[32,32,128]{2,1,0:T(8,128)(2,1)S(1)}, bf16[32,32,128]{2,1,0:T(8,128)(2,1)S(1)}, u32[]{:S(2)}, u32[]{:S(2)}) collective-permute-start(bf16[32,32,128]{2,1,0:T(8,128)(2,1)S(1)} %get-tuple-element.41), channel_id=1, source_target_pairs={{0,4},{1,5},{2,6},{3,7},{4,0},{5,1},{6,2},{7,3},{8,12},{9,13},{10,... | collective-permute-start | bytes 786440 | tf_op jit(solution)/shard_map/ppermute | solution.py:279
  37.2 3.1 %collective-permute-start.25 = (bf16[16,32,128]{2,1,0:T(8,128)(2,1)S(1)}, bf16[16,32,128]{2,1,0:T(8,128)(2,1)S(1)}, u32[]{:S(2)}, u32[]{:S(2)}) collective-permute-start(bf16[16,32,128]{2,1,0:T(8,128)(2,1)S(1)} %project.4), channel_id=1, source_target_pairs={{0,4},{1,5},{2,6},{3,7},{4,3},{5,2},{6,1},{7,0},{8,12},{9,13},{10,... | collective-permute-start | bytes 393224 | tf_op jit(solution)/shard_map/ppermute | solution.py:279
  38.4 3.3 %collective-permute-start.24 = (bf16[16,32,128]{2,1,0:T(8,128)(2,1)S(1)}, bf16[16,32,128]{2,1,0:T(8,128)(2,1)S(1)}, u32[]{:S(2)}, u32[]{:S(2)}) collective-permute-start(bf16[16,32,128]{2,1,0:T(8,128)(2,1)S(1)} %project.4), channel_id=1, source_target_pairs={{0,4},{1,5},{2,6},{3,7},{4,2},{5,3},{6,0},{7,1},{8,12},{9,13},{10,... | collective-permute-start | bytes 393224 | tf_op jit(solution)/shard_map/ppermute | solution.py:279
  38.4 3.4 %collective-permute-start.23 = (bf16[16,32,128]{2,1,0:T(8,128)(2,1)S(1)}, bf16[16,32,128]{2,1,0:T(8,128)(2,1)S(1)}, u32[]{:S(2)}, u32[]{:S(2)}) collective-permute-start(bf16[16,32,128]{2,1,0:T(8,128)(2,1)S(1)} %project.4), channel_id=1, source_target_pairs={{0,4},{1,5},{2,6},{3,7},{4,1},{5,0},{6,3},{7,2},{8,12},{9,13},{10,... | collective-permute-start | bytes 393224 | tf_op jit(solution)/shard_map/ppermute | solution.py:279
  39.6 2.2 %collective-permute-start.22 = (bf16[16,32,128]{2,1,0:T(8,128)(2,1)S(1)}, bf16[16,32,128]{2,1,0:T(8,128)(2,1)S(1)}, u32[]{:S(2)}, u32[]{:S(2)}) collective-permute-start(bf16[16,32,128]{2,1,0:T(8,128)(2,1)S(1)} %project.4), channel_id=1, source_target_pairs={{0,4},{1,5},{2,6},{3,7},{4,0},{5,1},{6,2},{7,3},{8,12},{9,13},{10,... | collective-permute-start | bytes 393224 | tf_op jit(solution)/shard_map/ppermute | solution.py:279
  39.6 2.2 %collective-permute-start.26 = (bf16[32,32,128]{2,1,0:T(8,128)(2,1)S(1)}, bf16[32,32,128]{2,1,0:T(8,128)(2,1)S(1)}, u32[]{:S(2)}, u32[]{:S(2)}) collective-permute-start(bf16[32,32,128]{2,1,0:T(8,128)(2,1)S(1)} %collective-permute-done.21.image), channel_id=1, source_target_pairs={{0,4},{1,5},{2,6},{3,7},{4,0},{5,1},{6,2},{7,3},{8,12},{9,13},{10,... | collective-permute-start | bytes 786440 | tf_op jit(solution)/shard_map/ppermute | solution.py:279
  41.7 10.8 %collective-permute-start.30 = (bf16[16,32,128]{2,1,0:T(8,128)(2,1)S(1)}, bf16[16,32,128]{2,1,0:T(8,128)(2,1)S(1)}, u32[]{:S(2)}, u32[]{:S(2)}) collective-permute-start(bf16[16,32,128]{2,1,0:T(8,128)(2,1)S(1)} %get-tuple-element.42), channel_id=1, source_target_pairs={{0,1},{1,0},{2,3},{3,2},{4,16},{5,17},{6,18},{7,19},{8,15},{9,14},... | collective-permute-start | bytes 393224 | tf_op jit(solution)/shard_map/ppermute | solution.py:279
  50.5 4.4 %collective-permute-start.29 = (bf16[16,32,128]{2,1,0:T(8,128)(2,1)S(1)}, bf16[16,32,128]{2,1,0:T(8,128)(2,1)S(1)}, u32[]{:S(2)}, u32[]{:S(2)}) collective-permute-start(bf16[16,32,128]{2,1,0:T(8,128)(2,1)S(1)} %get-tuple-element.42), channel_id=1, source_target_pairs={{0,6},{1,7},{2,4},{3,5},{4,0},{5,1},{6,2},{7,3},{8,14},{9,15},{10,... | collective-permute-start | bytes 393224 | tf_op jit(solution)/shard_map/ppermute | solution.py:279
  50.5 4.4 %collective-permute-start.28 = (bf16[16,32,128]{2,1,0:T(8,128)(2,1)S(1)}, bf16[16,32,128]{2,1,0:T(8,128)(2,1)S(1)}, u32[]{:S(2)}, u32[]{:S(2)}) collective-permute-start(bf16[16,32,128]{2,1,0:T(8,128)(2,1)S(1)} %get-tuple-element.42), channel_id=1, source_target_pairs={{0,5},{1,4},{2,7},{3,6},{4,0},{5,1},{6,2},{7,3},{8,13},{9,12},{10,... | collective-permute-start | bytes 393224 | tf_op jit(solution)/shard_map/ppermute | solution.py:279
  51.8 3.1 %collective-permute-start.27 = (bf16[16,32,128]{2,1,0:T(8,128)(2,1)S(1)}, bf16[16,32,128]{2,1,0:T(8,128)(2,1)S(1)}, u32[]{:S(2)}, u32[]{:S(2)}) collective-permute-start(bf16[16,32,128]{2,1,0:T(8,128)(2,1)S(1)} %get-tuple-element.42), channel_id=1, source_target_pairs={{0,4},{1,5},{2,6},{3,7},{4,0},{5,1},{6,2},{7,3},{8,12},{9,13},{10,... | collective-permute-start | bytes 393224 | tf_op jit(solution)/shard_map/ppermute | solution.py:279
  51.8 3.1 %collective-permute-start.31 = (bf16[32,32,128]{2,1,0:T(8,128)(2,1)S(1)}, bf16[32,32,128]{2,1,0:T(8,128)(2,1)S(1)}, u32[]{:S(2)}, u32[]{:S(2)}) collective-permute-start(bf16[32,32,128]{2,1,0:T(8,128)(2,1)S(1)} %get-tuple-element.43.refs_3_), channel_id=1, source_target_pairs={{0,4},{1,5},{2,6},{3,7},{4,0},{5,1},{6,2},{7,3},{8,12},{9,13},{10,... | collective-permute-start | bytes 786440 | tf_op jit(solution)/shard_map/ppermute | solution.py:279
  55.2 1.6 %collective-permute-start.32 = (bf16[32,32,128]{2,1,0:T(8,128)(2,1)S(1)}, bf16[32,32,128]{2,1,0:T(8,128)(2,1)S(1)}, u32[]{:S(2)}, u32[]{:S(2)}) collective-permute-start(bf16[32,32,128]{2,1,0:T(8,128)(2,1)S(1)} %get-tuple-element.45), channel_id=1, source_target_pairs={{0,4},{1,5},{2,6},{3,7},{4,0},{5,1},{6,2},{7,3},{8,12},{9,13},{10,... | collective-permute-start | bytes 786440 | tf_op jit(solution)/shard_map/ppermute | solution.py:279
  56.8 3.2 %collective-permute-start.36 = (bf16[16,32,128]{2,1,0:T(8,128)(2,1)S(1)}, bf16[16,32,128]{2,1,0:T(8,128)(2,1)S(1)}, u32[]{:S(2)}, u32[]{:S(2)}) collective-permute-start(bf16[16,32,128]{2,1,0:T(8,128)(2,1)S(1)} %project.5), channel_id=1, source_target_pairs={{0,4},{1,5},{2,6},{3,7},{4,3},{5,2},{6,1},{7,0},{8,12},{9,13},{10,... | collective-permute-start | bytes 393224 | tf_op jit(solution)/shard_map/ppermute | solution.py:279
  58.0 3.4 %collective-permute-start.35 = (bf16[16,32,128]{2,1,0:T(8,128)(2,1)S(1)}, bf16[16,32,128]{2,1,0:T(8,128)(2,1)S(1)}, u32[]{:S(2)}, u32[]{:S(2)}) collective-permute-start(bf16[16,32,128]{2,1,0:T(8,128)(2,1)S(1)} %project.5), channel_id=1, source_target_pairs={{0,4},{1,5},{2,6},{3,7},{4,2},{5,3},{6,0},{7,1},{8,12},{9,13},{10,... | collective-permute-start | bytes 393224 | tf_op jit(solution)/shard_map/ppermute | solution.py:279
  58.0 3.3 %collective-permute-start.34 = (bf16[16,32,128]{2,1,0:T(8,128)(2,1)S(1)}, bf16[16,32,128]{2,1,0:T(8,128)(2,1)S(1)}, u32[]{:S(2)}, u32[]{:S(2)}) collective-permute-start(bf16[16,32,128]{2,1,0:T(8,128)(2,1)S(1)} %project.5), channel_id=1, source_target_pairs={{0,4},{1,5},{2,6},{3,7},{4,1},{5,0},{6,3},{7,2},{8,12},{9,13},{10,... | collective-permute-start | bytes 393224 | tf_op jit(solution)/shard_map/ppermute | solution.py:279
  59.2 2.1 %collective-permute-start.33 = (bf16[16,32,128]{2,1,0:T(8,128)(2,1)S(1)}, bf16[16,32,128]{2,1,0:T(8,128)(2,1)S(1)}, u32[]{:S(2)}, u32[]{:S(2)}) collective-permute-start(bf16[16,32,128]{2,1,0:T(8,128)(2,1)S(1)} %project.5), channel_id=1, source_target_pairs={{0,4},{1,5},{2,6},{3,7},{4,0},{5,1},{6,2},{7,3},{8,12},{9,13},{10,... | collective-permute-start | bytes 393224 | tf_op jit(solution)/shard_map/ppermute | solution.py:279
  59.2 2.1 %collective-permute-start.37 = (bf16[32,32,128]{2,1,0:T(8,128)(2,1)S(1)}, bf16[32,32,128]{2,1,0:T(8,128)(2,1)S(1)}, u32[]{:S(2)}, u32[]{:S(2)}) collective-permute-start(bf16[32,32,128]{2,1,0:T(8,128)(2,1)S(1)} %collective-permute-done.32.image), channel_id=1, source_target_pairs={{0,4},{1,5},{2,6},{3,7},{4,0},{5,1},{6,2},{7,3},{8,12},{9,13},{10,... | collective-permute-start | bytes 786440 | tf_op jit(solution)/shard_map/ppermute | solution.py:279
  61.4 10.1 %collective-permute-start.41 = (bf16[16,32,128]{2,1,0:T(8,128)(2,1)S(1)}, bf16[16,32,128]{2,1,0:T(8,128)(2,1)S(1)}, u32[]{:S(2)}, u32[]{:S(2)}) collective-permute-start(bf16[16,32,128]{2,1,0:T(8,128)(2,1)S(1)} %get-tuple-element.46), channel_id=1, source_target_pairs={{0,1},{1,0},{2,3},{3,2},{4,24},{5,25},{6,26},{7,27},{8,15},{9,14},... | collective-permute-start | bytes 393224 | tf_op jit(solution)/shard_map/ppermute | solution.py:279
  69.6 4.4 %collective-permute-start.40 = (bf16[16,32,128]{2,1,0:T(8,128)(2,1)S(1)}, bf16[16,32,128]{2,1,0:T(8,128)(2,1)S(1)}, u32[]{:S(2)}, u32[]{:S(2)}) collective-permute-start(bf16[16,32,128]{2,1,0:T(8,128)(2,1)S(1)} %get-tuple-element.46), channel_id=1, source_target_pairs={{0,6},{1,7},{2,4},{3,5},{4,0},{5,1},{6,2},{7,3},{8,14},{9,15},{10,... | collective-permute-start | bytes 393224 | tf_op jit(solution)/shard_map/ppermute | solution.py:279
  69.6 4.4 %collective-permute-start.39 = (bf16[16,32,128]{2,1,0:T(8,128)(2,1)S(1)}, bf16[16,32,128]{2,1,0:T(8,128)(2,1)S(1)}, u32[]{:S(2)}, u32[]{:S(2)}) collective-permute-start(bf16[16,32,128]{2,1,0:T(8,128)(2,1)S(1)} %get-tuple-element.46), channel_id=1, source_target_pairs={{0,5},{1,4},{2,7},{3,6},{4,0},{5,1},{6,2},{7,3},{8,13},{9,12},{10,... | collective-permute-start | bytes 393224 | tf_op jit(solution)/shard_map/ppermute | solution.py:279
  70.8 3.1 %collective-permute-start.38 = (bf16[16,32,128]{2,1,0:T(8,128)(2,1)S(1)}, bf16[16,32,128]{2,1,0:T(8,128)(2,1)S(1)}, u32[]{:S(2)}, u32[]{:S(2)}) collective-permute-start(bf16[16,32,128]{2,1,0:T(8,128)(2,1)S(1)} %get-tuple-element.46), channel_id=1, source_target_pairs={{0,4},{1,5},{2,6},{3,7},{4,0},{5,1},{6,2},{7,3},{8,12},{9,13},{10,... | collective-permute-start | bytes 393224 | tf_op jit(solution)/shard_map/ppermute | solution.py:279
  70.8 3.1 %collective-permute-start.42 = (bf16[32,32,128]{2,1,0:T(8,128)(2,1)S(1)}, bf16[32,32,128]{2,1,0:T(8,128)(2,1)S(1)}, u32[]{:S(2)}, u32[]{:S(2)}) collective-permute-start(bf16[32,32,128]{2,1,0:T(8,128)(2,1)S(1)} %get-tuple-element.47.refs_3_), channel_id=1, source_target_pairs={{0,4},{1,5},{2,6},{3,7},{4,0},{5,1},{6,2},{7,3},{8,12},{9,13},{10,... | collective-permute-start | bytes 786440 | tf_op jit(solution)/shard_map/ppermute | solution.py:279

commit v17 on v16

--- a/solution.py
+++ b/solution.py
@@ -290,8 +290,8 @@
     def passed(terms, core, place):
         if not direct:
             return [swapped(lax.psum(terms, "tile"))]
-        ahead = place + 2 if place + 2 < places else 0
-        helped = core == 0 and place > 0
+        ahead = 0
+        helped = core == 0 and 0 < place == places - 1
 
         def way(d):
             def target(p, c, t):

time: 74.9 us -> 74 us (0.988)
  starting transfers between devices: 44.2 us -> 42.3 us
  waiting for transfers between devices: 23.6 us -> 24.6 us
    ppermute x43, starting transfers between devices: 44.2 us -> 42.3 us  [sent(): return lax.ppermute(value, ('subset', 'tile'), pairs)]
    ppermute x43, waiting for transfers between devices: 23.6 us -> 24.6 us  [sent(): return lax.ppermute(value, ('subset', 'tile'), pairs)]
where the time goes in v17:
time: 74 us; the launch traced here: 73.8 us
  starting transfers between devices  42.3 us (57%)
  waiting for transfers between devices  24.6 us (33%)
  Pallas kernels  6.72 us (9%)
    ppermute x43, starting transfers between devices, sent(): return lax.ppermute(value, ('subset', 'tile'), pairs)  42.3 us
    ppermute x43, waiting for transfers between devices, sent(): return lax.ppermute(value, ('subset', 'tile'), pairs)  24.6 us
    pallas_call x1, Pallas kernels, per_device(): pl.pallas_call(functools.partial(head_kernel, row_blocks, chunks), out_sh...  3.09 us
    pallas_call x19, Pallas kernels, call(): pl.pallas_call(kernel, out_shape=out_shape, in_specs=[SMEM] * smem + [VME...  1.83 us
  transfers between devices with their start and end apart: 43, of which 18 were waited for; matrix products, arithmetic and copies ran while one was open for 0% of the time, Pallas kernels for 7%

profile of v17, /device:TPU:1, one launch (start us, length us, event | category | flops | bytes accessed | tf_op | source)
XLA Modules:
  0.0 73.8 jit_solution(325653426280264557)
XLA Ops:
  0.1 3.1 %head.1 = (bf16[5,32,128]{2,1,0:T(8,128)(2,1)S(1)}, s32[2,80]{1,0:T(2,128)S(1)}, s32[3,80]{1,0:T(4,128)S(4)}, bf16[1,1,80,128,128]{4,3,2,1,0:T(8,128)(2,1)S(1)}) custom-call(s32[3]{0:T(128)S(1)} %pad_add_fusion.pos, s32[1,1,80]{2,1,0:T(1,128)} %rows_in.1, s32[1,1,80]{2,1,0:T(1,128)} %cols_in.1, bf16[1,1,80,128,128]{4,3,2,1,0:T(8,128)(2,1)} %blocks_in.1, ...), custom_call_target="tpu_custom_call" | custom-call | tf_op jit(solution)/shard_map/head/pallas_call | solution.py:325
  3.2 3.7 %collective-permute-start.4 = (bf16[5,32,128]{2,1,0:T(8,128)(2,1)S(1)}, bf16[5,32,128]{2,1,0:T(8,128)(2,1)S(1)}, u32[]{:S(2)}, u32[]{:S(2)}) collective-permute-start(bf16[5,32,128]{2,1,0:T(8,128)(2,1)S(1)} %get-tuple-element.31._.refs_2_), channel_id=1, source_target_pairs={{0,3},{1,2},{2,1},{3,0},{4,7},{5,6},{6,5},{7,4},{8,11},{9,10},{10,... | collective-permute-start | bytes 122888 | tf_op jit(solution)/shard_map/ppermute | solution.py:279
  6.9 0.2 collective-permute-start.3
  7.3 0.6 collective-permute-start
  7.8 0.5 pack_own.1.refs_1_
  8.3 0.3 collective-permute-done.table2
  8.7 1.3 %pack_other.1 = (s32[3,80]{1,0:T(4,128)S(4)}, bf16[16,640,128]{2,1,0:T(8,128)(2,1)S(1)}) custom-call(s32[3,80]{1,0:T(4,128)S(4)} %get-tuple-element.27.own, s32[2,80]{1,0:T(2,128)S(1)} %collective-permute-done.table2, bf16[1,1,80,128,128]{4,3,2,1,0:T(8,128)(2,1)S(1)} %collective-permute-done.1.blocks2), custom_call_target="tpu_custom_call" | custom-call | tf_op jit(solution)/shard_map/pack_other/pallas_call | solution.py:366
  10.1 2.9 %collective-permute-start.8 = (bf16[16,32,128]{2,1,0:T(8,128)(2,1)S(1)}, bf16[16,32,128]{2,1,0:T(8,128)(2,1)S(1)}, u32[]{:S(2)}, u32[]{:S(2)}) collective-permute-start(bf16[16,32,128]{2,1,0:T(8,128)(2,1)S(1)} %get-tuple-element.35), channel_id=1, source_target_pairs={{0,7},{1,6},{2,5},{3,4},{4,0},{5,1},{6,2},{7,3},{8,15},{9,14},{10,... | collective-permute-start | bytes 393224 | tf_op jit(solution)/shard_map/ppermute | solution.py:279
  13.0 0.1 collective-permute-start.7
  13.1 1.5 %collective-permute-start.6 = (bf16[16,32,128]{2,1,0:T(8,128)(2,1)S(1)}, bf16[16,32,128]{2,1,0:T(8,128)(2,1)S(1)}, u32[]{:S(2)}, u32[]{:S(2)}) collective-permute-start(bf16[16,32,128]{2,1,0:T(8,128)(2,1)S(1)} %get-tuple-element.35), channel_id=1, source_target_pairs={{0,5},{1,4},{2,7},{3,6},{4,0},{5,1},{6,2},{7,3},{8,13},{9,12},{10,... | collective-permute-start | bytes 393224 | tf_op jit(solution)/shard_map/ppermute | solution.py:279
  14.6 0.5 collective-permute-start.9
  15.1 1.7 %collective-permute-done.8.refs_6_ = bf16[16,32,128]{2,1,0:T(8,128)(2,1)S(1)} collective-permute-done((bf16[16,32,128]{2,1,0:T(8,128)(2,1)S(1)}, bf16[16,32,128]{2,1,0:T(8,128)(2,1)S(1)}, u32[]{:S(2)}, u32[]{:S(2)}) %collective-permute-start.8) | collective-permute-done | bytes 131104 | tf_op jit(solution)/shard_map/ppermute | solution.py:279
  16.8 1.3 %collective-permute-done.7.refs_5_ = bf16[16,32,128]{2,1,0:T(8,128)(2,1)S(1)} collective-permute-done((bf16[16,32,128]{2,1,0:T(8,128)(2,1)S(1)}, bf16[16,32,128]{2,1,0:T(8,128)(2,1)S(1)}, u32[]{:S(2)}, u32[]{:S(2)}) %collective-permute-start.7) | collective-permute-done | bytes 131104 | tf_op jit(solution)/shard_map/ppermute | solution.py:279
  18.1 0.6 update.9.refs_1_
  18.9 3.3 %collective-permute-done.10.image = bf16[32,32,128]{2,1,0:T(8,128)(2,1)S(1)} collective-permute-done((bf16[32,32,128]{2,1,0:T(8,128)(2,1)S(1)}, bf16[32,32,128]{2,1,0:T(8,128)(2,1)S(1)}, u32[]{:S(2)}, u32[]{:S(2)}) %collective-permute-start.10) | collective-permute-done | bytes 262176 | tf_op jit(solution)/shard_map/ppermute | solution.py:279
  22.3 2.9 %collective-permute-start.14 = (bf16[16,32,128]{2,1,0:T(8,128)(2,1)S(1)}, bf16[16,32,128]{2,1,0:T(8,128)(2,1)S(1)}, u32[]{:S(2)}, u32[]{:S(2)}) collective-permute-start(bf16[16,32,128]{2,1,0:T(8,128)(2,1)S(1)} %project.3), channel_id=1, source_target_pairs={{0,4},{1,5},{2,6},{3,7},{4,3},{5,2},{6,1},{7,0},{8,12},{9,13},{10,... | collective-permute-start | bytes 393224 | tf_op jit(solution)/shard_map/ppermute | solution.py:279
  25.1 1.0 %collective-permute-start.12 = (bf16[16,32,128]{2,1,0:T(8,128)(2,1)S(1)}, bf16[16,32,128]{2,1,0:T(8,128)(2,1)S(1)}, u32[]{:S(2)}, u32[]{:S(2)}) collective-permute-start(bf16[16,32,128]{2,1,0:T(8,128)(2,1)S(1)} %project.3), channel_id=1, source_target_pairs={{0,4},{1,5},{2,6},{3,7},{4,1},{5,0},{6,3},{7,2},{8,12},{9,13},{10,... | collective-permute-start | bytes 393224 | tf_op jit(solution)/shard_map/ppermute | solution.py:279
  26.1 0.5 collective-permute-start.15
  26.7 0.4 collective-permute-done.14.refs_6_
  27.1 1.4 %collective-permute-done.13.refs_5_ = bf16[16,32,128]{2,1,0:T(8,128)(2,1)S(1)} collective-permute-done((bf16[16,32,128]{2,1,0:T(8,128)(2,1)S(1)}, bf16[16,32,128]{2,1,0:T(8,128)(2,1)S(1)}, u32[]{:S(2)}, u32[]{:S(2)}) %collective-permute-start.13) | collective-permute-done | bytes 131104 | tf_op jit(solution)/shard_map/ppermute | solution.py:279
  28.5 1.8 %collective-permute-start.19 = (bf16[16,32,128]{2,1,0:T(8,128)(2,1)S(1)}, bf16[16,32,128]{2,1,0:T(8,128)(2,1)S(1)}, u32[]{:S(2)}, u32[]{:S(2)}) collective-permute-start(bf16[16,32,128]{2,1,0:T(8,128)(2,1)S(1)} %get-tuple-element.38), channel_id=1, source_target_pairs={{0,7},{1,6},{2,5},{3,4},{4,0},{5,1},{6,2},{7,3},{8,15},{9,14},{10,... | collective-permute-start | bytes 393224 | tf_op jit(solution)/shard_map/ppermute | solution.py:279
  30.4 1.1 %collective-permute-start.17 = (bf16[16,32,128]{2,1,0:T(8,128)(2,1)S(1)}, bf16[16,32,128]{2,1,0:T(8,128)(2,1)S(1)}, u32[]{:S(2)}, u32[]{:S(2)}) collective-permute-start(bf16[16,32,128]{2,1,0:T(8,128)(2,1)S(1)} %get-tuple-element.38), channel_id=1, source_target_pairs={{0,5},{1,4},{2,7},{3,6},{4,0},{5,1},{6,2},{7,3},{8,13},{9,12},{10,... | collective-permute-start | bytes 393224 | tf_op jit(solution)/shard_map/ppermute | solution.py:279
  31.6 0.4 collective-permute-start.20
  32.0 2.1 %collective-permute-done.19.refs_6_ = bf16[16,32,128]{2,1,0:T(8,128)(2,1)S(1)} collective-permute-done((bf16[16,32,128]{2,1,0:T(8,128)(2,1)S(1)}, bf16[16,32,128]{2,1,0:T(8,128)(2,1)S(1)}, u32[]{:S(2)}, u32[]{:S(2)}) %collective-permute-start.19) | collective-permute-done | bytes 131104 | tf_op jit(solution)/shard_map/ppermute | solution.py:279
  34.2 1.3 %collective-permute-done.18.refs_5_ = bf16[16,32,128]{2,1,0:T(8,128)(2,1)S(1)} collective-permute-done((bf16[16,32,128]{2,1,0:T(8,128)(2,1)S(1)}, bf16[16,32,128]{2,1,0:T(8,128)(2,1)S(1)}, u32[]{:S(2)}, u32[]{:S(2)}) %collective-permute-start.18) | collective-permute-done | bytes 131104 | tf_op jit(solution)/shard_map/ppermute | solution.py:279
  35.7 1.5 %collective-permute-done.21.image = bf16[32,32,128]{2,1,0:T(8,128)(2,1)S(1)} collective-permute-done((bf16[32,32,128]{2,1,0:T(8,128)(2,1)S(1)}, bf16[32,32,128]{2,1,0:T(8,128)(2,1)S(1)}, u32[]{:S(2)}, u32[]{:S(2)}) %collective-permute-start.21) | collective-permute-done | bytes 262176 | tf_op jit(solution)/shard_map/ppermute | solution.py:279
  37.2 1.2 %collective-permute-start.25 = (bf16[16,32,128]{2,1,0:T(8,128)(2,1)S(1)}, bf16[16,32,128]{2,1,0:T(8,128)(2,1)S(1)}, u32[]{:S(2)}, u32[]{:S(2)}) collective-permute-start(bf16[16,32,128]{2,1,0:T(8,128)(2,1)S(1)} %project.4), channel_id=1, source_target_pairs={{0,4},{1,5},{2,6},{3,7},{4,3},{5,2},{6,1},{7,0},{8,12},{9,13},{10,... | collective-permute-start | bytes 393224 | tf_op jit(solution)/shard_map/ppermute | solution.py:279
  38.4 1.2 %collective-permute-start.23 = (bf16[16,32,128]{2,1,0:T(8,128)(2,1)S(1)}, bf16[16,32,128]{2,1,0:T(8,128)(2,1)S(1)}, u32[]{:S(2)}, u32[]{:S(2)}) collective-permute-start(bf16[16,32,128]{2,1,0:T(8,128)(2,1)S(1)} %project.4), channel_id=1, source_target_pairs={{0,4},{1,5},{2,6},{3,7},{4,1},{5,0},{6,3},{7,2},{8,12},{9,13},{10,... | collective-permute-start | bytes 393224 | tf_op jit(solution)/shard_map/ppermute | solution.py:279
  39.6 0.5 collective-permute-start.26
  40.1 0.2 collective-permute-done.25.refs_6_
  40.3 1.4 %collective-permute-done.24.refs_5_ = bf16[16,32,128]{2,1,0:T(8,128)(2,1)S(1)} collective-permute-done((bf16[16,32,128]{2,1,0:T(8,128)(2,1)S(1)}, bf16[16,32,128]{2,1,0:T(8,128)(2,1)S(1)}, u32[]{:S(2)}, u32[]{:S(2)}) %collective-permute-start.24) | collective-permute-done | bytes 131104 | tf_op jit(solution)/shard_map/ppermute | solution.py:279
  41.7 2.0 %collective-permute-start.30 = (bf16[16,32,128]{2,1,0:T(8,128)(2,1)S(1)}, bf16[16,32,128]{2,1,0:T(8,128)(2,1)S(1)}, u32[]{:S(2)}, u32[]{:S(2)}) collective-permute-start(bf16[16,32,128]{2,1,0:T(8,128)(2,1)S(1)} %get-tuple-element.42), channel_id=1, source_target_pairs={{0,7},{1,6},{2,5},{3,4},{4,0},{5,1},{6,2},{7,3},{8,15},{9,14},{10,... | collective-permute-start | bytes 393224 | tf_op jit(solution)/shard_map/ppermute | solution.py:279
  43.8 1.0 %collective-permute-start.28 = (bf16[16,32,128]{2,1,0:T(8,128)(2,1)S(1)}, bf16[16,32,128]{2,1,0:T(8,128)(2,1)S(1)}, u32[]{:S(2)}, u32[]{:S(2)}) collective-permute-start(bf16[16,32,128]{2,1,0:T(8,128)(2,1)S(1)} %get-tuple-element.42), channel_id=1, source_target_pairs={{0,5},{1,4},{2,7},{3,6},{4,0},{5,1},{6,2},{7,3},{8,13},{9,12},{10,... | collective-permute-start | bytes 393224 | tf_op jit(solution)/shard_map/ppermute | solution.py:279
  44.9 0.5 collective-permute-start.31
  45.3 2.2 %collective-permute-done.30.refs_6_ = bf16[16,32,128]{2,1,0:T(8,128)(2,1)S(1)} collective-permute-done((bf16[16,32,128]{2,1,0:T(8,128)(2,1)S(1)}, bf16[16,32,128]{2,1,0:T(8,128)(2,1)S(1)}, u32[]{:S(2)}, u32[]{:S(2)}) %collective-permute-start.30) | collective-permute-done | bytes 131104 | tf_op jit(solution)/shard_map/ppermute | solution.py:279
  47.5 1.3 %collective-permute-done.29.refs_5_ = bf16[16,32,128]{2,1,0:T(8,128)(2,1)S(1)} collective-permute-done((bf16[16,32,128]{2,1,0:T(8,128)(2,1)S(1)}, bf16[16,32,128]{2,1,0:T(8,128)(2,1)S(1)}, u32[]{:S(2)}, u32[]{:S(2)}) %collective-permute-start.29) | collective-permute-done | bytes 131104 | tf_op jit(solution)/shard_map/ppermute | solution.py:279
  48.9 0.3 second.6
  49.2 1.5 %collective-permute-done.32.image = bf16[32,32,128]{2,1,0:T(8,128)(2,1)S(1)} collective-permute-done((bf16[32,32,128]{2,1,0:T(8,128)(2,1)S(1)}, bf16[32,32,128]{2,1,0:T(8,128)(2,1)S(1)}, u32[]{:S(2)}, u32[]{:S(2)}) %collective-permute-start.32) | collective-permute-done | bytes 262176 | tf_op jit(solution)/shard_map/ppermute | solution.py:279
  50.7 1.2 %collective-permute-start.36 = (bf16[16,32,128]{2,1,0:T(8,128)(2,1)S(1)}, bf16[16,32,128]{2,1,0:T(8,128)(2,1)S(1)}, u32[]{:S(2)}, u32[]{:S(2)}) collective-permute-start(bf16[16,32,128]{2,1,0:T(8,128)(2,1)S(1)} %project.5), channel_id=1, source_target_pairs={{0,4},{1,5},{2,6},{3,7},{4,3},{5,2},{6,1},{7,0},{8,12},{9,13},{10,... | collective-permute-start | bytes 393224 | tf_op jit(solution)/shard_map/ppermute | solution.py:279
  51.9 1.0 %collective-permute-start.34 = (bf16[16,32,128]{2,1,0:T(8,128)(2,1)S(1)}, bf16[16,32,128]{2,1,0:T(8,128)(2,1)S(1)}, u32[]{:S(2)}, u32[]{:S(2)}) collective-permute-start(bf16[16,32,128]{2,1,0:T(8,128)(2,1)S(1)} %project.5), channel_id=1, source_target_pairs={{0,4},{1,5},{2,6},{3,7},{4,1},{5,0},{6,3},{7,2},{8,12},{9,13},{10,... | collective-permute-start | bytes 393224 | tf_op jit(solution)/shard_map/ppermute | solution.py:279
  53.0 0.5 collective-permute-start.37
  53.5 0.4 collective-permute-done.36.refs_6_
  53.9 1.4 %collective-permute-done.35.refs_5_ = bf16[16,32,128]{2,1,0:T(8,128)(2,1)S(1)} collective-permute-done((bf16[16,32,128]{2,1,0:T(8,128)(2,1)S(1)}, bf16[16,32,128]{2,1,0:T(8,128)(2,1)S(1)}, u32[]{:S(2)}, u32[]{:S(2)}) %collective-permute-start.35) | collective-permute-done | bytes 131104 | tf_op jit(solution)/shard_map/ppermute | solution.py:279
  55.3 13.4 %collective-permute-start.41 = (bf16[16,32,128]{2,1,0:T(8,128)(2,1)S(1)}, bf16[16,32,128]{2,1,0:T(8,128)(2,1)S(1)}, u32[]{:S(2)}, u32[]{:S(2)}) collective-permute-start(bf16[16,32,128]{2,1,0:T(8,128)(2,1)S(1)} %get-tuple-element.46), channel_id=1, source_target_pairs={{0,1},{1,0},{2,3},{3,2},{4,24},{5,25},{6,26},{7,27},{8,15},{9,14},... | collective-permute-start | bytes 393224 | tf_op jit(solution)/shard_map/ppermute | solution.py:279
  68.7 1.3 %collective-permute-start.39 = (bf16[16,32,128]{2,1,0:T(8,128)(2,1)S(1)}, bf16[16,32,128]{2,1,0:T(8,128)(2,1)S(1)}, u32[]{:S(2)}, u32[]{:S(2)}) collective-permute-start(bf16[16,32,128]{2,1,0:T(8,128)(2,1)S(1)} %get-tuple-element.46), channel_id=1, source_target_pairs={{0,5},{1,4},{2,7},{3,6},{4,0},{5,1},{6,2},{7,3},{8,13},{9,12},{10,... | collective-permute-start | bytes 393224 | tf_op jit(solution)/shard_map/ppermute | solution.py:279
  69.9 0.5 collective-permute-start.42
  70.6 2.4 %collective-permute-done.40.refs_5_ = bf16[16,32,128]{2,1,0:T(8,128)(2,1)S(1)} collective-permute-done((bf16[16,32,128]{2,1,0:T(8,128)(2,1)S(1)}, bf16[16,32,128]{2,1,0:T(8,128)(2,1)S(1)}, u32[]{:S(2)}, u32[]{:S(2)}) %collective-permute-start.40) | collective-permute-done | bytes 131104 | tf_op jit(solution)/shard_map/ppermute | solution.py:279
  73.1 0.8 %second.7 = bf16[4,8,4096]{2,1,0:T(8,128)(2,1)} custom-call(s32[3,80]{1,0:T(4,128)S(4)} %get-tuple-element.29.refs_0_.info, f32[32,32,128]{2,1,0:T(8,128)S(1)} %update.15.refs_1_, bf16[32,32,128]{2,1,0:T(8,128)(2,1)S(1)} %collective-permute-done.42.refs_2_, bf16[32,32,128]{2,1,0:T(8,128)(2,1)S(1)} %get-tuple-element.47.refs_3_, ...), custom_call_target="tpu_custom_call" | custom-call | tf_op jit(solution)/shard_map/second/pallas_call | solution.py:310
  (61 shorter events, 1.3 us)
Async XLA Ops:
  0.0 8.7 %collective-permute-start.1 = (bf16[1,1,80,128,128]{4,3,2,1,0:T(8,128)(2,1)}, bf16[1,1,80,128,128]{4,3,2,1,0:T(8,128)(2,1)S(1)}, u32[]{:S(2)}, u32[]{:S(2)}) collective-permute-start(bf16[1,1,80,128,128]{4,3,2,1,0:T(8,128)(2,1)} %blocks_in.1), channel_id=1, source_target_pairs={{0,4},{1,5},{2,6},{3,7},{4,0},{5,1},{6,2},{7,3},{8,12},{9,13},{10,... | collective-permute-start | bytes 7864328 | tf_op jit(solution)/shard_map/ppermute | solution.py:279
  3.2 6.8 %collective-permute-start.4 = (bf16[5,32,128]{2,1,0:T(8,128)(2,1)S(1)}, bf16[5,32,128]{2,1,0:T(8,128)(2,1)S(1)}, u32[]{:S(2)}, u32[]{:S(2)}) collective-permute-start(bf16[5,32,128]{2,1,0:T(8,128)(2,1)S(1)} %get-tuple-element.31._.refs_2_), channel_id=1, source_target_pairs={{0,3},{1,2},{2,1},{3,0},{4,7},{5,6},{6,5},{7,4},{8,11},{9,10},{10,... | collective-permute-start | bytes 122888 | tf_op jit(solution)/shard_map/ppermute | solution.py:279
  6.9 3.1 %collective-permute-start.3 = (bf16[5,32,128]{2,1,0:T(8,128)(2,1)S(1)}, bf16[5,32,128]{2,1,0:T(8,128)(2,1)S(1)}, u32[]{:S(2)}, u32[]{:S(2)}) collective-permute-start(bf16[5,32,128]{2,1,0:T(8,128)(2,1)S(1)} %get-tuple-element.31._.refs_2_), channel_id=1, source_target_pairs={{0,2},{1,3},{2,0},{3,1},{4,6},{5,7},{6,4},{7,5},{8,10},{9,11},{10,... | collective-permute-start | bytes 122888 | tf_op jit(solution)/shard_map/ppermute | solution.py:279
  7.1 2.9 %collective-permute-start.2 = (bf16[5,32,128]{2,1,0:T(8,128)(2,1)S(1)}, bf16[5,32,128]{2,1,0:T(8,128)(2,1)S(1)}, u32[]{:S(2)}, u32[]{:S(2)}) collective-permute-start(bf16[5,32,128]{2,1,0:T(8,128)(2,1)S(1)} %get-tuple-element.31._.refs_2_), channel_id=1, source_target_pairs={{0,1},{1,0},{2,3},{3,2},{4,5},{5,4},{6,7},{7,6},{8,9},{9,8},{10,11... | collective-permute-start | bytes 122888 | tf_op jit(solution)/shard_map/ppermute | solution.py:279
  7.3 1.4 %collective-permute-start = (s32[2,80]{1,0:T(2,128)S(1)}, s32[2,80]{1,0:T(2,128)S(1)}, u32[]{:S(2)}, u32[]{:S(2)}) collective-permute-start(s32[2,80]{1,0:T(2,128)S(1)} %get-tuple-element.28), channel_id=1, source_target_pairs={{0,4},{1,5},{2,6},{3,7},{4,0},{5,1},{6,2},{7,3},{8,12},{9,13},{10,... | collective-permute-start | bytes 1928 | tf_op jit(solution)/shard_map/ppermute | solution.py:279
  10.1 6.7 %collective-permute-start.8 = (bf16[16,32,128]{2,1,0:T(8,128)(2,1)S(1)}, bf16[16,32,128]{2,1,0:T(8,128)(2,1)S(1)}, u32[]{:S(2)}, u32[]{:S(2)}) collective-permute-start(bf16[16,32,128]{2,1,0:T(8,128)(2,1)S(1)} %get-tuple-element.35), channel_id=1, source_target_pairs={{0,7},{1,6},{2,5},{3,4},{4,0},{5,1},{6,2},{7,3},{8,15},{9,14},{10,... | collective-permute-start | bytes 393224 | tf_op jit(solution)/shard_map/ppermute | solution.py:279
  13.0 5.2 %collective-permute-start.7 = (bf16[16,32,128]{2,1,0:T(8,128)(2,1)S(1)}, bf16[16,32,128]{2,1,0:T(8,128)(2,1)S(1)}, u32[]{:S(2)}, u32[]{:S(2)}) collective-permute-start(bf16[16,32,128]{2,1,0:T(8,128)(2,1)S(1)} %get-tuple-element.35), channel_id=1, source_target_pairs={{0,6},{1,7},{2,4},{3,5},{4,0},{5,1},{6,2},{7,3},{8,14},{9,15},{10,... | collective-permute-start | bytes 393224 | tf_op jit(solution)/shard_map/ppermute | solution.py:279
  13.1 5.0 %collective-permute-start.6 = (bf16[16,32,128]{2,1,0:T(8,128)(2,1)S(1)}, bf16[16,32,128]{2,1,0:T(8,128)(2,1)S(1)}, u32[]{:S(2)}, u32[]{:S(2)}) collective-permute-start(bf16[16,32,128]{2,1,0:T(8,128)(2,1)S(1)} %get-tuple-element.35), channel_id=1, source_target_pairs={{0,5},{1,4},{2,7},{3,6},{4,0},{5,1},{6,2},{7,3},{8,13},{9,12},{10,... | collective-permute-start | bytes 393224 | tf_op jit(solution)/shard_map/ppermute | solution.py:279
  14.6 3.5 %collective-permute-start.5 = (bf16[16,32,128]{2,1,0:T(8,128)(2,1)S(1)}, bf16[16,32,128]{2,1,0:T(8,128)(2,1)S(1)}, u32[]{:S(2)}, u32[]{:S(2)}) collective-permute-start(bf16[16,32,128]{2,1,0:T(8,128)(2,1)S(1)} %get-tuple-element.35), channel_id=1, source_target_pairs={{0,4},{1,5},{2,6},{3,7},{4,0},{5,1},{6,2},{7,3},{8,12},{9,13},{10,... | collective-permute-start | bytes 393224 | tf_op jit(solution)/shard_map/ppermute | solution.py:279
  14.6 4.1 %collective-permute-start.9 = (bf16[32,32,128]{2,1,0:T(8,128)(2,1)S(1)}, bf16[32,32,128]{2,1,0:T(8,128)(2,1)S(1)}, u32[]{:S(2)}, u32[]{:S(2)}) collective-permute-start(bf16[32,32,128]{2,1,0:T(8,128)(2,1)S(1)} %get-tuple-element.36.refs_3_), channel_id=1, source_target_pairs={{0,4},{1,5},{2,6},{3,7},{4,0},{5,1},{6,2},{7,3},{8,12},{9,13},{10,... | collective-permute-start | bytes 786440 | tf_op jit(solution)/shard_map/ppermute | solution.py:279
  18.8 3.4 %collective-permute-start.10 = (bf16[32,32,128]{2,1,0:T(8,128)(2,1)S(1)}, bf16[32,32,128]{2,1,0:T(8,128)(2,1)S(1)}, u32[]{:S(2)}, u32[]{:S(2)}) collective-permute-start(bf16[32,32,128]{2,1,0:T(8,128)(2,1)S(1)} %get-tuple-element.37), channel_id=1, source_target_pairs={{0,4},{1,5},{2,6},{3,7},{4,12},{5,13},{6,14},{7,15},{8,0},{9,1},{1... | collective-permute-start | bytes 786440 | tf_op jit(solution)/shard_map/ppermute | solution.py:279
  22.3 4.8 %collective-permute-start.14 = (bf16[16,32,128]{2,1,0:T(8,128)(2,1)S(1)}, bf16[16,32,128]{2,1,0:T(8,128)(2,1)S(1)}, u32[]{:S(2)}, u32[]{:S(2)}) collective-permute-start(bf16[16,32,128]{2,1,0:T(8,128)(2,1)S(1)} %project.3), channel_id=1, source_target_pairs={{0,4},{1,5},{2,6},{3,7},{4,3},{5,2},{6,1},{7,0},{8,12},{9,13},{10,... | collective-permute-start | bytes 393224 | tf_op jit(solution)/shard_map/ppermute | solution.py:279
  25.1 3.3 %collective-permute-start.13 = (bf16[16,32,128]{2,1,0:T(8,128)(2,1)S(1)}, bf16[16,32,128]{2,1,0:T(8,128)(2,1)S(1)}, u32[]{:S(2)}, u32[]{:S(2)}) collective-permute-start(bf16[16,32,128]{2,1,0:T(8,128)(2,1)S(1)} %project.3), channel_id=1, source_target_pairs={{0,4},{1,5},{2,6},{3,7},{4,2},{5,3},{6,0},{7,1},{8,12},{9,13},{10,... | collective-permute-start | bytes 393224 | tf_op jit(solution)/shard_map/ppermute | solution.py:279
  25.1 3.4 %collective-permute-start.12 = (bf16[16,32,128]{2,1,0:T(8,128)(2,1)S(1)}, bf16[16,32,128]{2,1,0:T(8,128)(2,1)S(1)}, u32[]{:S(2)}, u32[]{:S(2)}) collective-permute-start(bf16[16,32,128]{2,1,0:T(8,128)(2,1)S(1)} %project.3), channel_id=1, source_target_pairs={{0,4},{1,5},{2,6},{3,7},{4,1},{5,0},{6,3},{7,2},{8,12},{9,13},{10,... | collective-permute-start | bytes 393224 | tf_op jit(solution)/shard_map/ppermute | solution.py:279
  26.1 2.4 %collective-permute-start.11 = (bf16[16,32,128]{2,1,0:T(8,128)(2,1)S(1)}, bf16[16,32,128]{2,1,0:T(8,128)(2,1)S(1)}, u32[]{:S(2)}, u32[]{:S(2)}) collective-permute-start(bf16[16,32,128]{2,1,0:T(8,128)(2,1)S(1)} %project.3), channel_id=1, source_target_pairs={{0,4},{1,5},{2,6},{3,7},{4,0},{5,1},{6,2},{7,3},{8,12},{9,13},{10,... | collective-permute-start | bytes 393224 | tf_op jit(solution)/shard_map/ppermute | solution.py:279
  26.1 2.4 %collective-permute-start.15 = (bf16[32,32,128]{2,1,0:T(8,128)(2,1)S(1)}, bf16[32,32,128]{2,1,0:T(8,128)(2,1)S(1)}, u32[]{:S(2)}, u32[]{:S(2)}) collective-permute-start(bf16[32,32,128]{2,1,0:T(8,128)(2,1)S(1)} %collective-permute-done.10.image), channel_id=1, source_target_pairs={{0,4},{1,5},{2,6},{3,7},{4,0},{5,1},{6,2},{7,3},{8,12},{9,13},{10,... | collective-permute-start | bytes 786440 | tf_op jit(solution)/shard_map/ppermute | solution.py:279
  28.5 5.7 %collective-permute-start.19 = (bf16[16,32,128]{2,1,0:T(8,128)(2,1)S(1)}, bf16[16,32,128]{2,1,0:T(8,128)(2,1)S(1)}, u32[]{:S(2)}, u32[]{:S(2)}) collective-permute-start(bf16[16,32,128]{2,1,0:T(8,128)(2,1)S(1)} %get-tuple-element.38), channel_id=1, source_target_pairs={{0,7},{1,6},{2,5},{3,4},{4,0},{5,1},{6,2},{7,3},{8,15},{9,14},{10,... | collective-permute-start | bytes 393224 | tf_op jit(solution)/shard_map/ppermute | solution.py:279
  30.3 5.2 %collective-permute-start.18 = (bf16[16,32,128]{2,1,0:T(8,128)(2,1)S(1)}, bf16[16,32,128]{2,1,0:T(8,128)(2,1)S(1)}, u32[]{:S(2)}, u32[]{:S(2)}) collective-permute-start(bf16[16,32,128]{2,1,0:T(8,128)(2,1)S(1)} %get-tuple-element.38), channel_id=1, source_target_pairs={{0,6},{1,7},{2,4},{3,5},{4,0},{5,1},{6,2},{7,3},{8,14},{9,15},{10,... | collective-permute-start | bytes 393224 | tf_op jit(solution)/shard_map/ppermute | solution.py:279
  30.4 5.1 %collective-permute-start.17 = (bf16[16,32,128]{2,1,0:T(8,128)(2,1)S(1)}, bf16[16,32,128]{2,1,0:T(8,128)(2,1)S(1)}, u32[]{:S(2)}, u32[]{:S(2)}) collective-permute-start(bf16[16,32,128]{2,1,0:T(8,128)(2,1)S(1)} %get-tuple-element.38), channel_id=1, source_target_pairs={{0,5},{1,4},{2,7},{3,6},{4,0},{5,1},{6,2},{7,3},{8,13},{9,12},{10,... | collective-permute-start | bytes 393224 | tf_op jit(solution)/shard_map/ppermute | solution.py:279
  31.5 4.0 %collective-permute-start.16 = (bf16[16,32,128]{2,1,0:T(8,128)(2,1)S(1)}, bf16[16,32,128]{2,1,0:T(8,128)(2,1)S(1)}, u32[]{:S(2)}, u32[]{:S(2)}) collective-permute-start(bf16[16,32,128]{2,1,0:T(8,128)(2,1)S(1)} %get-tuple-element.38), channel_id=1, source_target_pairs={{0,4},{1,5},{2,6},{3,7},{4,0},{5,1},{6,2},{7,3},{8,12},{9,13},{10,... | collective-permute-start | bytes 393224 | tf_op jit(solution)/shard_map/ppermute | solution.py:279
  31.6 3.9 %collective-permute-start.20 = (bf16[32,32,128]{2,1,0:T(8,128)(2,1)S(1)}, bf16[32,32,128]{2,1,0:T(8,128)(2,1)S(1)}, u32[]{:S(2)}, u32[]{:S(2)}) collective-permute-start(bf16[32,32,128]{2,1,0:T(8,128)(2,1)S(1)} %get-tuple-element.39.refs_3_), channel_id=1, source_target_pairs={{0,4},{1,5},{2,6},{3,7},{4,0},{5,1},{6,2},{7,3},{8,12},{9,13},{10,... | collective-permute-start | bytes 786440 | tf_op jit(solution)/shard_map/ppermute | solution.py:279
  35.6 1.6 %collective-permute-start.21 = (bf16[32,32,128]{2,1,0:T(8,128)(2,1)S(1)}, bf16[32,32,128]{2,1,0:T(8,128)(2,1)S(1)}, u32[]{:S(2)}, u32[]{:S(2)}) collective-permute-start(bf16[32,32,128]{2,1,0:T(8,128)(2,1)S(1)} %get-tuple-element.41), channel_id=1, source_target_pairs={{0,4},{1,5},{2,6},{3,7},{4,0},{5,1},{6,2},{7,3},{8,12},{9,13},{10,... | collective-permute-start | bytes 786440 | tf_op jit(solution)/shard_map/ppermute | solution.py:279
  37.2 3.1 %collective-permute-start.25 = (bf16[16,32,128]{2,1,0:T(8,128)(2,1)S(1)}, bf16[16,32,128]{2,1,0:T(8,128)(2,1)S(1)}, u32[]{:S(2)}, u32[]{:S(2)}) collective-permute-start(bf16[16,32,128]{2,1,0:T(8,128)(2,1)S(1)} %project.4), channel_id=1, source_target_pairs={{0,4},{1,5},{2,6},{3,7},{4,3},{5,2},{6,1},{7,0},{8,12},{9,13},{10,... | collective-permute-start | bytes 393224 | tf_op jit(solution)/shard_map/ppermute | solution.py:279
  38.4 3.3 %collective-permute-start.24 = (bf16[16,32,128]{2,1,0:T(8,128)(2,1)S(1)}, bf16[16,32,128]{2,1,0:T(8,128)(2,1)S(1)}, u32[]{:S(2)}, u32[]{:S(2)}) collective-permute-start(bf16[16,32,128]{2,1,0:T(8,128)(2,1)S(1)} %project.4), channel_id=1, source_target_pairs={{0,4},{1,5},{2,6},{3,7},{4,2},{5,3},{6,0},{7,1},{8,12},{9,13},{10,... | collective-permute-start | bytes 393224 | tf_op jit(solution)/shard_map/ppermute | solution.py:279
  38.4 3.4 %collective-permute-start.23 = (bf16[16,32,128]{2,1,0:T(8,128)(2,1)S(1)}, bf16[16,32,128]{2,1,0:T(8,128)(2,1)S(1)}, u32[]{:S(2)}, u32[]{:S(2)}) collective-permute-start(bf16[16,32,128]{2,1,0:T(8,128)(2,1)S(1)} %project.4), channel_id=1, source_target_pairs={{0,4},{1,5},{2,6},{3,7},{4,1},{5,0},{6,3},{7,2},{8,12},{9,13},{10,... | collective-permute-start | bytes 393224 | tf_op jit(solution)/shard_map/ppermute | solution.py:279
  39.6 2.1 %collective-permute-start.22 = (bf16[16,32,128]{2,1,0:T(8,128)(2,1)S(1)}, bf16[16,32,128]{2,1,0:T(8,128)(2,1)S(1)}, u32[]{:S(2)}, u32[]{:S(2)}) collective-permute-start(bf16[16,32,128]{2,1,0:T(8,128)(2,1)S(1)} %project.4), channel_id=1, source_target_pairs={{0,4},{1,5},{2,6},{3,7},{4,0},{5,1},{6,2},{7,3},{8,12},{9,13},{10,... | collective-permute-start | bytes 393224 | tf_op jit(solution)/shard_map/ppermute | solution.py:279
  39.6 2.2 %collective-permute-start.26 = (bf16[32,32,128]{2,1,0:T(8,128)(2,1)S(1)}, bf16[32,32,128]{2,1,0:T(8,128)(2,1)S(1)}, u32[]{:S(2)}, u32[]{:S(2)}) collective-permute-start(bf16[32,32,128]{2,1,0:T(8,128)(2,1)S(1)} %collective-permute-done.21.image), channel_id=1, source_target_pairs={{0,4},{1,5},{2,6},{3,7},{4,0},{5,1},{6,2},{7,3},{8,12},{9,13},{10,... | collective-permute-start | bytes 786440 | tf_op jit(solution)/shard_map/ppermute | solution.py:279
  41.7 5.8 %collective-permute-start.30 = (bf16[16,32,128]{2,1,0:T(8,128)(2,1)S(1)}, bf16[16,32,128]{2,1,0:T(8,128)(2,1)S(1)}, u32[]{:S(2)}, u32[]{:S(2)}) collective-permute-start(bf16[16,32,128]{2,1,0:T(8,128)(2,1)S(1)} %get-tuple-element.42), channel_id=1, source_target_pairs={{0,7},{1,6},{2,5},{3,4},{4,0},{5,1},{6,2},{7,3},{8,15},{9,14},{10,... | collective-permute-start | bytes 393224 | tf_op jit(solution)/shard_map/ppermute | solution.py:279
  43.7 5.1 %collective-permute-start.29 = (bf16[16,32,128]{2,1,0:T(8,128)(2,1)S(1)}, bf16[16,32,128]{2,1,0:T(8,128)(2,1)S(1)}, u32[]{:S(2)}, u32[]{:S(2)}) collective-permute-start(bf16[16,32,128]{2,1,0:T(8,128)(2,1)S(1)} %get-tuple-element.42), channel_id=1, source_target_pairs={{0,6},{1,7},{2,4},{3,5},{4,0},{5,1},{6,2},{7,3},{8,14},{9,15},{10,... | collective-permute-start | bytes 393224 | tf_op jit(solution)/shard_map/ppermute | solution.py:279
  43.8 5.0 %collective-permute-start.28 = (bf16[16,32,128]{2,1,0:T(8,128)(2,1)S(1)}, bf16[16,32,128]{2,1,0:T(8,128)(2,1)S(1)}, u32[]{:S(2)}, u32[]{:S(2)}) collective-permute-start(bf16[16,32,128]{2,1,0:T(8,128)(2,1)S(1)} %get-tuple-element.42), channel_id=1, source_target_pairs={{0,5},{1,4},{2,7},{3,6},{4,0},{5,1},{6,2},{7,3},{8,13},{9,12},{10,... | collective-permute-start | bytes 393224 | tf_op jit(solution)/shard_map/ppermute | solution.py:279
  44.8 4.0 %collective-permute-start.27 = (bf16[16,32,128]{2,1,0:T(8,128)(2,1)S(1)}, bf16[16,32,128]{2,1,0:T(8,128)(2,1)S(1)}, u32[]{:S(2)}, u32[]{:S(2)}) collective-permute-start(bf16[16,32,128]{2,1,0:T(8,128)(2,1)S(1)} %get-tuple-element.42), channel_id=1, source_target_pairs={{0,4},{1,5},{2,6},{3,7},{4,0},{5,1},{6,2},{7,3},{8,12},{9,13},{10,... | collective-permute-start | bytes 393224 | tf_op jit(solution)/shard_map/ppermute | solution.py:279
  44.9 4.0 %collective-permute-start.31 = (bf16[32,32,128]{2,1,0:T(8,128)(2,1)S(1)}, bf16[32,32,128]{2,1,0:T(8,128)(2,1)S(1)}, u32[]{:S(2)}, u32[]{:S(2)}) collective-permute-start(bf16[32,32,128]{2,1,0:T(8,128)(2,1)S(1)} %get-tuple-element.43.refs_3_), channel_id=1, source_target_pairs={{0,4},{1,5},{2,6},{3,7},{4,0},{5,1},{6,2},{7,3},{8,12},{9,13},{10,... | collective-permute-start | bytes 786440 | tf_op jit(solution)/shard_map/ppermute | solution.py:279
  49.1 1.6 %collective-permute-start.32 = (bf16[32,32,128]{2,1,0:T(8,128)(2,1)S(1)}, bf16[32,32,128]{2,1,0:T(8,128)(2,1)S(1)}, u32[]{:S(2)}, u32[]{:S(2)}) collective-permute-start(bf16[32,32,128]{2,1,0:T(8,128)(2,1)S(1)} %get-tuple-element.45), channel_id=1, source_target_pairs={{0,4},{1,5},{2,6},{3,7},{4,0},{5,1},{6,2},{7,3},{8,12},{9,13},{10,... | collective-permute-start | bytes 786440 | tf_op jit(solution)/shard_map/ppermute | solution.py:279
  50.7 3.2 %collective-permute-start.36 = (bf16[16,32,128]{2,1,0:T(8,128)(2,1)S(1)}, bf16[16,32,128]{2,1,0:T(8,128)(2,1)S(1)}, u32[]{:S(2)}, u32[]{:S(2)}) collective-permute-start(bf16[16,32,128]{2,1,0:T(8,128)(2,1)S(1)} %project.5), channel_id=1, source_target_pairs={{0,4},{1,5},{2,6},{3,7},{4,3},{5,2},{6,1},{7,0},{8,12},{9,13},{10,... | collective-permute-start | bytes 393224 | tf_op jit(solution)/shard_map/ppermute | solution.py:279
  51.9 3.3 %collective-permute-start.35 = (bf16[16,32,128]{2,1,0:T(8,128)(2,1)S(1)}, bf16[16,32,128]{2,1,0:T(8,128)(2,1)S(1)}, u32[]{:S(2)}, u32[]{:S(2)}) collective-permute-start(bf16[16,32,128]{2,1,0:T(8,128)(2,1)S(1)} %project.5), channel_id=1, source_target_pairs={{0,4},{1,5},{2,6},{3,7},{4,2},{5,3},{6,0},{7,1},{8,12},{9,13},{10,... | collective-permute-start | bytes 393224 | tf_op jit(solution)/shard_map/ppermute | solution.py:279
  51.9 3.4 %collective-permute-start.34 = (bf16[16,32,128]{2,1,0:T(8,128)(2,1)S(1)}, bf16[16,32,128]{2,1,0:T(8,128)(2,1)S(1)}, u32[]{:S(2)}, u32[]{:S(2)}) collective-permute-start(bf16[16,32,128]{2,1,0:T(8,128)(2,1)S(1)} %project.5), channel_id=1, source_target_pairs={{0,4},{1,5},{2,6},{3,7},{4,1},{5,0},{6,3},{7,2},{8,12},{9,13},{10,... | collective-permute-start | bytes 393224 | tf_op jit(solution)/shard_map/ppermute | solution.py:279
  53.0 2.3 %collective-permute-start.33 = (bf16[16,32,128]{2,1,0:T(8,128)(2,1)S(1)}, bf16[16,32,128]{2,1,0:T(8,128)(2,1)S(1)}, u32[]{:S(2)}, u32[]{:S(2)}) collective-permute-start(bf16[16,32,128]{2,1,0:T(8,128)(2,1)S(1)} %project.5), channel_id=1, source_target_pairs={{0,4},{1,5},{2,6},{3,7},{4,0},{5,1},{6,2},{7,3},{8,12},{9,13},{10,... | collective-permute-start | bytes 393224 | tf_op jit(solution)/shard_map/ppermute | solution.py:279
  53.0 2.3 %collective-permute-start.37 = (bf16[32,32,128]{2,1,0:T(8,128)(2,1)S(1)}, bf16[32,32,128]{2,1,0:T(8,128)(2,1)S(1)}, u32[]{:S(2)}, u32[]{:S(2)}) collective-permute-start(bf16[32,32,128]{2,1,0:T(8,128)(2,1)S(1)} %collective-permute-done.32.image), channel_id=1, source_target_pairs={{0,4},{1,5},{2,6},{3,7},{4,0},{5,1},{6,2},{7,3},{8,12},{9,13},{10,... | collective-permute-start | bytes 786440 | tf_op jit(solution)/shard_map/ppermute | solution.py:279
  55.3 15.3 %collective-permute-start.41 = (bf16[16,32,128]{2,1,0:T(8,128)(2,1)S(1)}, bf16[16,32,128]{2,1,0:T(8,128)(2,1)S(1)}, u32[]{:S(2)}, u32[]{:S(2)}) collective-permute-start(bf16[16,32,128]{2,1,0:T(8,128)(2,1)S(1)} %get-tuple-element.46), channel_id=1, source_target_pairs={{0,1},{1,0},{2,3},{3,2},{4,24},{5,25},{6,26},{7,27},{8,15},{9,14},... | collective-permute-start | bytes 393224 | tf_op jit(solution)/shard_map/ppermute | solution.py:279
  68.6 4.4 %collective-permute-start.40 = (bf16[16,32,128]{2,1,0:T(8,128)(2,1)S(1)}, bf16[16,32,128]{2,1,0:T(8,128)(2,1)S(1)}, u32[]{:S(2)}, u32[]{:S(2)}) collective-permute-start(bf16[16,32,128]{2,1,0:T(8,128)(2,1)S(1)} %get-tuple-element.46), channel_id=1, source_target_pairs={{0,6},{1,7},{2,4},{3,5},{4,0},{5,1},{6,2},{7,3},{8,14},{9,15},{10,... | collective-permute-start | bytes 393224 | tf_op jit(solution)/shard_map/ppermute | solution.py:279
  68.7 4.4 %collective-permute-start.39 = (bf16[16,32,128]{2,1,0:T(8,128)(2,1)S(1)}, bf16[16,32,128]{2,1,0:T(8,128)(2,1)S(1)}, u32[]{:S(2)}, u32[]{:S(2)}) collective-permute-start(bf16[16,32,128]{2,1,0:T(8,128)(2,1)S(1)} %get-tuple-element.46), channel_id=1, source_target_pairs={{0,5},{1,4},{2,7},{3,6},{4,0},{5,1},{6,2},{7,3},{8,13},{9,12},{10,... | collective-permute-start | bytes 393224 | tf_op jit(solution)/shard_map/ppermute | solution.py:279
  69.9 3.1 %collective-permute-start.38 = (bf16[16,32,128]{2,1,0:T(8,128)(2,1)S(1)}, bf16[16,32,128]{2,1,0:T(8,128)(2,1)S(1)}, u32[]{:S(2)}, u32[]{:S(2)}) collective-permute-start(bf16[16,32,128]{2,1,0:T(8,128)(2,1)S(1)} %get-tuple-element.46), channel_id=1, source_target_pairs={{0,4},{1,5},{2,6},{3,7},{4,0},{5,1},{6,2},{7,3},{8,12},{9,13},{10,... | collective-permute-start | bytes 393224 | tf_op jit(solution)/shard_map/ppermute | solution.py:279
  69.9 3.1 %collective-permute-start.42 = (bf16[32,32,128]{2,1,0:T(8,128)(2,1)S(1)}, bf16[32,32,128]{2,1,0:T(8,128)(2,1)S(1)}, u32[]{:S(2)}, u32[]{:S(2)}) collective-permute-start(bf16[32,32,128]{2,1,0:T(8,128)(2,1)S(1)} %get-tuple-element.47.refs_3_), channel_id=1, source_target_pairs={{0,4},{1,5},{2,6},{3,7},{4,0},{5,1},{6,2},{7,3},{8,12},{9,13},{10,... | collective-permute-start | bytes 786440 | tf_op jit(solution)/shard_map/ppermute | solution.py:279

commit v18 on v14

--- a/solution.py
+++ b/solution.py
@@ -28,7 +28,7 @@
 
 
 def head_kernel(row_blocks, chunks, pos, rows_in, cols_in, blocks_in, rays_in, *refs):
-    note, table, own, blocks, rows, cols, rays, seen, squares, norms, sems = refs
+    note, table, own, blocks, rows, cols, rays, seen, squares, squares2, norms, sems = refs
     count = blocks.shape[2]
     each = count // row_blocks
     per_chunk = count // chunks
@@ -49,6 +49,7 @@
     for copy in small + large:
         copy.start()
     squares[...] = jnp.zeros_like(squares)
+    squares2[...] = jnp.zeros_like(squares2)
     for copy in small:
         copy.wait()
     for i in range(3):
@@ -63,7 +64,8 @@
         for n in range(k * per_chunk, (k + 1) * per_chunk):
             block = blocks[0, 0, n].astype(jnp.float32)
             row = rows[0, 0, n]
-            squares[row] = squares[row] + block * block
+            into = squares2 if n % 2 else squares
+            into[row] = into[row] + block * block
             at = seen[row]
             seen[row] = at + 1
             col = cols[0, 0, n]
@@ -75,7 +77,7 @@
         jnp.int32, (BS, BS), 1
     )
     for r in range(row_blocks):
-        left = squares[r]
+        left = squares[r] + squares2[r]
         coarse = left.astype(jnp.bfloat16)
         fine = (left - coarse.astype(jnp.float32)).astype(jnp.bfloat16)
         total = dot(coarse, ones, NN) + dot(fine, ones, NN)
@@ -141,14 +143,15 @@
         w_scr[r] = left.astype(jnp.bfloat16)
 
 
-def back_project(info, wide, w_scr, image):
+def back_project(info, wide, w_scr, changes):
     row_blocks = wide.shape[0]
     each = wide.shape[2] // BS
     for r in range(row_blocks):
         back = dot(w_scr[r], wide[r], NN)
         for j in range(each):
             col = info[1, r * each + j]
-            image[col] = image[col] + back[:, j * BS : (j + 1) * BS]
+            into = changes[(r * each + j) % 2]
+            into[col] = into[col] + back[:, j * BS : (j + 1) * BS]
 
 
 def project(info, tall, image, terms):
@@ -181,29 +184,30 @@
     info, wide = take(refs, 2)
     if n_notes:
         notes, terms_in = take(refs, n_notes), []
-        change, rays, w_scr, rays_scr = refs
+        change, change2, rays, w_scr, rays_scr = refs
         gather_rays(info, notes, rays, rays_scr)
     else:
         (rays,) = take(refs, 1)
         terms_in = take(refs, n_terms)
-        change, w_scr = refs
+        change, change2, w_scr = refs
 
     @pl.when(on_core(info, place, core))
     def _():
         weights(rays, terms_in, w_scr)
         change[...] = jnp.zeros_like(change)
-        back_project(info, wide, w_scr, change)
+        change2[...] = jnp.zeros_like(change2)
+        back_project(info, wide, w_scr, (change, change2))
 
 
 def first_kernel(place, *refs):
     refs = list(refs)
-    info, tall, change = take(refs, 3)
+    info, tall, change, change2 = take(refs, 4)
     image_in = take(refs, 1)[0] if place > 0 else None
     shot, terms = refs
 
     @pl.when(on_core(info, place, 0))
     def _():
-        value = change[...]
+        value = change[...] + change2[...]
         if image_in is not None:
             value = value + image_in[...].astype(jnp.float32)
         shot[...] = value.astype(jnp.bfloat16)
@@ -212,14 +216,14 @@
 
 def second_kernel(place, last, *refs):
     refs = list(refs)
-    info, change, image_in, shot = take(refs, 4)
+    info, change, change2, image_in, shot = take(refs, 5)
     held = take(refs, 1) if place > 0 else []
     image = None if last else take(refs, 1)[0]
     (out,) = refs
     batches, per_batch, _ = out.shape
 
     def value(c):
-        return change[c] + image_in[c].astype(jnp.float32)
+        return change[c] + change2[c] + image_in[c].astype(jnp.float32)
 
     def write(source):
         for c in range(CB):
@@ -327,6 +331,7 @@
             pltpu.SMEM(block_cols.shape, jnp.int32),
             pltpu.VMEM(sinogram.shape, jnp.float32),
             pltpu.SMEM((row_blocks,), jnp.int32),
+            pltpu.VMEM((row_blocks, BS, BS), jnp.float32),
             pltpu.VMEM((row_blocks, BS, BS), jnp.float32),
             pltpu.VMEM((row_blocks, BS), jnp.float32),
             pltpu.SemaphoreType.DMA((3 + chunks,)),
@@ -375,7 +380,7 @@
             functools.partial(update_kernel, place, core, 0, len(terms)),
             1,
             [info, wide, rays] + terms,
-            change_out,
+            (change_out, change_out),
             [w_scr],
             "update",
             UPDATE_FLOPS,
@@ -384,11 +389,11 @@
     for place in range(places):
         last = place == places - 1
         if place == 0:
-            change, rays = call(
+            *changes, rays = call(
                 functools.partial(update_kernel, place, 0, len(notes), 0),
                 1,
                 [info, wide] + notes,
-                (change_out, rays_out),
+                (change_out, change_out, rays_out),
                 [w_scr, rays_scr],
                 "update",
                 UPDATE_FLOPS,
@@ -411,21 +416,21 @@
                 [],
                 "project",
             )
-            change = updated(place, 0, passed(terms, 1))
+            changes = updated(place, 0, passed(terms, 1))
             before = [swapped(image)]
         shot, terms = call(
             functools.partial(first_kernel, place),
             1,
-            [info, tall, change] + before,
+            [info, tall, *changes] + before,
             (image_out, terms_out),
             [],
             "first",
         )
-        change = updated(place, 1, passed(terms, 0))
+        changes = updated(place, 1, passed(terms, 0))
         outs = call(
             functools.partial(second_kernel, place, last),
             1,
-            [info, change, swapped(shot), shot] + held,
+            [info, *changes, swapped(shot), shot] + held,
             final_out if last else (image_out, image_out),
             [],
             "second",

time: 71.1 us -> 71.2 us (level)
  no operation moved by 1% of the time
where the time goes in v18:
time: 71.2 us; the launch traced here: 71.1 us
  waiting for transfers between devices  35.9 us (50%)
  starting transfers between devices  27.7 us (39%)
  Pallas kernels  7.21 us (10%)
    ppermute x43, waiting for transfers between devices, sent(): return lax.ppermute(value, ('subset', 'tile'), pairs)  35.9 us
    ppermute x43, starting transfers between devices, sent(): return lax.ppermute(value, ('subset', 'tile'), pairs)  27.7 us
    pallas_call x1, Pallas kernels, per_device(): pl.pallas_call(functools.partial(head_kernel, row_blocks, chunks), out_sh...  3.08 us
    pallas_call x19, Pallas kernels, call(): pl.pallas_call(kernel, out_shape=out_shape, in_specs=[SMEM] * smem + [VME...  2.33 us
  transfers between devices with their start and end apart: 43, of which 18 were waited for; matrix products, arithmetic and copies ran while one was open for 0% of the time, Pallas kernels for 8%

profile of v18, /device:TPU:25, one launch (start us, length us, event | category | flops | bytes accessed | tf_op | source)
XLA Modules:
  0.0 71.1 jit_solution(1766894030157950578)
XLA Ops:
  0.0 0.7 collective-permute-start.1
  0.8 3.1 %head.1 = (bf16[5,32,128]{2,1,0:T(8,128)(2,1)S(1)}, s32[2,80]{1,0:T(2,128)S(1)}, s32[3,80]{1,0:T(4,128)S(4)}, bf16[1,1,80,128,128]{4,3,2,1,0:T(8,128)(2,1)S(1)}) custom-call(s32[3]{0:T(128)S(1)} %pad_add_fusion.pos, s32[1,1,80]{2,1,0:T(1,128)} %rows_in.1, s32[1,1,80]{2,1,0:T(1,128)} %cols_in.1, bf16[1,1,80,128,128]{4,3,2,1,0:T(8,128)(2,1)} %blocks_in.1, ...), custom_call_target="tpu_custom_call" | custom-call | tf_op jit(solution)/shard_map/head/pallas_call | solution.py:319
  3.8 2.2 %collective-permute-start.4 = (bf16[5,32,128]{2,1,0:T(8,128)(2,1)S(1)}, bf16[5,32,128]{2,1,0:T(8,128)(2,1)S(1)}, u32[]{:S(2)}, u32[]{:S(2)}) collective-permute-start(bf16[5,32,128]{2,1,0:T(8,128)(2,1)S(1)} %get-tuple-element.46._.refs_2_), channel_id=1, source_target_pairs={{0,3},{1,2},{2,1},{3,0},{4,7},{5,6},{6,5},{7,4},{8,11},{9,10},{10,... | collective-permute-start | bytes 122888 | tf_op jit(solution)/shard_map/ppermute | solution.py:283
  6.3 0.3 collective-permute-start.2
  6.6 0.8 %collective-permute-start = (s32[2,80]{1,0:T(2,128)S(1)}, s32[2,80]{1,0:T(2,128)S(1)}, u32[]{:S(2)}, u32[]{:S(2)}) collective-permute-start(s32[2,80]{1,0:T(2,128)S(1)} %get-tuple-element.43), channel_id=1, source_target_pairs={{0,4},{1,5},{2,6},{3,7},{4,0},{5,1},{6,2},{7,3},{8,12},{9,13},{10,... | collective-permute-start | bytes 1928 | tf_op jit(solution)/shard_map/ppermute | solution.py:283
  7.4 0.5 pack_own.1.refs_1_
  7.9 0.3 collective-permute-done.table2
  8.2 1.3 %pack_other.1 = (s32[3,80]{1,0:T(4,128)S(4)}, bf16[16,640,128]{2,1,0:T(8,128)(2,1)S(1)}) custom-call(s32[3,80]{1,0:T(4,128)S(4)} %get-tuple-element.42.own, s32[2,80]{1,0:T(2,128)S(1)} %collective-permute-done.table2, bf16[1,1,80,128,128]{4,3,2,1,0:T(8,128)(2,1)S(1)} %collective-permute-done.1.blocks2), custom_call_target="tpu_custom_call" | custom-call | tf_op jit(solution)/shard_map/pack_other/pallas_call | solution.py:361
  9.7 1.3 %collective-permute-start.8 = (bf16[16,32,128]{2,1,0:T(8,128)(2,1)S(1)}, bf16[16,32,128]{2,1,0:T(8,128)(2,1)S(1)}, u32[]{:S(2)}, u32[]{:S(2)}) collective-permute-start(bf16[16,32,128]{2,1,0:T(8,128)(2,1)S(1)} %get-tuple-element.51), channel_id=1, source_target_pairs={{0,7},{1,6},{2,5},{3,4},{4,0},{5,1},{6,2},{7,3},{8,15},{9,14},{10,... | collective-permute-start | bytes 393224 | tf_op jit(solution)/shard_map/ppermute | solution.py:283
  11.0 1.3 %collective-permute-start.7 = (bf16[16,32,128]{2,1,0:T(8,128)(2,1)S(1)}, bf16[16,32,128]{2,1,0:T(8,128)(2,1)S(1)}, u32[]{:S(2)}, u32[]{:S(2)}) collective-permute-start(bf16[16,32,128]{2,1,0:T(8,128)(2,1)S(1)} %get-tuple-element.51), channel_id=1, source_target_pairs={{0,6},{1,7},{2,4},{3,5},{4,0},{5,1},{6,2},{7,3},{8,14},{9,15},{10,... | collective-permute-start | bytes 393224 | tf_op jit(solution)/shard_map/ppermute | solution.py:283
  12.3 0.3 collective-permute-start.6
  12.6 0.3 collective-permute-start.5
  13.1 2.0 %collective-permute-done.8.refs_6_ = bf16[16,32,128]{2,1,0:T(8,128)(2,1)S(1)} collective-permute-done((bf16[16,32,128]{2,1,0:T(8,128)(2,1)S(1)}, bf16[16,32,128]{2,1,0:T(8,128)(2,1)S(1)}, u32[]{:S(2)}, u32[]{:S(2)}) %collective-permute-start.8) | collective-permute-done | bytes 131104 | tf_op jit(solution)/shard_map/ppermute | solution.py:283
  15.1 1.3 %collective-permute-done.7.refs_5_ = bf16[16,32,128]{2,1,0:T(8,128)(2,1)S(1)} collective-permute-done((bf16[16,32,128]{2,1,0:T(8,128)(2,1)S(1)}, bf16[16,32,128]{2,1,0:T(8,128)(2,1)S(1)}, u32[]{:S(2)}, u32[]{:S(2)}) %collective-permute-start.7) | collective-permute-done | bytes 131104 | tf_op jit(solution)/shard_map/ppermute | solution.py:283
  16.4 0.3 collective-permute-done.6.refs_4_
  16.8 1.5 %collective-permute-done.10.image = bf16[32,32,128]{2,1,0:T(8,128)(2,1)S(1)} collective-permute-done((bf16[32,32,128]{2,1,0:T(8,128)(2,1)S(1)}, bf16[32,32,128]{2,1,0:T(8,128)(2,1)S(1)}, u32[]{:S(2)}, u32[]{:S(2)}) %collective-permute-start.10) | collective-permute-done | bytes 262176 | tf_op jit(solution)/shard_map/ppermute | solution.py:283
  18.3 1.4 %collective-permute-start.14 = (bf16[16,32,128]{2,1,0:T(8,128)(2,1)S(1)}, bf16[16,32,128]{2,1,0:T(8,128)(2,1)S(1)}, u32[]{:S(2)}, u32[]{:S(2)}) collective-permute-start(bf16[16,32,128]{2,1,0:T(8,128)(2,1)S(1)} %project.3), channel_id=1, source_target_pairs={{0,4},{1,5},{2,6},{3,7},{4,3},{5,2},{6,1},{7,0},{8,12},{9,13},{10,... | collective-permute-start | bytes 393224 | tf_op jit(solution)/shard_map/ppermute | solution.py:283
  19.7 1.2 %collective-permute-start.12 = (bf16[16,32,128]{2,1,0:T(8,128)(2,1)S(1)}, bf16[16,32,128]{2,1,0:T(8,128)(2,1)S(1)}, u32[]{:S(2)}, u32[]{:S(2)}) collective-permute-start(bf16[16,32,128]{2,1,0:T(8,128)(2,1)S(1)} %project.3), channel_id=1, source_target_pairs={{0,4},{1,5},{2,6},{3,7},{4,1},{5,0},{6,3},{7,2},{8,12},{9,13},{10,... | collective-permute-start | bytes 393224 | tf_op jit(solution)/shard_map/ppermute | solution.py:283
  20.9 0.5 collective-permute-start.15
  21.6 1.4 %collective-permute-done.13.refs_5_ = bf16[16,32,128]{2,1,0:T(8,128)(2,1)S(1)} collective-permute-done((bf16[16,32,128]{2,1,0:T(8,128)(2,1)S(1)}, bf16[16,32,128]{2,1,0:T(8,128)(2,1)S(1)}, u32[]{:S(2)}, u32[]{:S(2)}) %collective-permute-start.13) | collective-permute-done | bytes 131104 | tf_op jit(solution)/shard_map/ppermute | solution.py:283
  23.0 2.1 %collective-permute-start.19 = (bf16[16,32,128]{2,1,0:T(8,128)(2,1)S(1)}, bf16[16,32,128]{2,1,0:T(8,128)(2,1)S(1)}, u32[]{:S(2)}, u32[]{:S(2)}) collective-permute-start(bf16[16,32,128]{2,1,0:T(8,128)(2,1)S(1)} %get-tuple-element.58), channel_id=1, source_target_pairs={{0,7},{1,6},{2,5},{3,4},{4,0},{5,1},{6,2},{7,3},{8,15},{9,14},{10,... | collective-permute-start | bytes 393224 | tf_op jit(solution)/shard_map/ppermute | solution.py:283
  25.2 0.9 %collective-permute-start.17 = (bf16[16,32,128]{2,1,0:T(8,128)(2,1)S(1)}, bf16[16,32,128]{2,1,0:T(8,128)(2,1)S(1)}, u32[]{:S(2)}, u32[]{:S(2)}) collective-permute-start(bf16[16,32,128]{2,1,0:T(8,128)(2,1)S(1)} %get-tuple-element.58), channel_id=1, source_target_pairs={{0,5},{1,4},{2,7},{3,6},{4,0},{5,1},{6,2},{7,3},{8,13},{9,12},{10,... | collective-permute-start | bytes 393224 | tf_op jit(solution)/shard_map/ppermute | solution.py:283
  26.2 0.4 collective-permute-start.20
  26.6 2.3 %collective-permute-done.19.refs_6_ = bf16[16,32,128]{2,1,0:T(8,128)(2,1)S(1)} collective-permute-done((bf16[16,32,128]{2,1,0:T(8,128)(2,1)S(1)}, bf16[16,32,128]{2,1,0:T(8,128)(2,1)S(1)}, u32[]{:S(2)}, u32[]{:S(2)}) %collective-permute-start.19) | collective-permute-done | bytes 131104 | tf_op jit(solution)/shard_map/ppermute | solution.py:283
  28.9 1.3 %collective-permute-done.18.refs_5_ = bf16[16,32,128]{2,1,0:T(8,128)(2,1)S(1)} collective-permute-done((bf16[16,32,128]{2,1,0:T(8,128)(2,1)S(1)}, bf16[16,32,128]{2,1,0:T(8,128)(2,1)S(1)}, u32[]{:S(2)}, u32[]{:S(2)}) %collective-permute-start.18) | collective-permute-done | bytes 131104 | tf_op jit(solution)/shard_map/ppermute | solution.py:283
  30.4 1.5 %collective-permute-done.21.image = bf16[32,32,128]{2,1,0:T(8,128)(2,1)S(1)} collective-permute-done((bf16[32,32,128]{2,1,0:T(8,128)(2,1)S(1)}, bf16[32,32,128]{2,1,0:T(8,128)(2,1)S(1)}, u32[]{:S(2)}, u32[]{:S(2)}) %collective-permute-start.21) | collective-permute-done | bytes 262176 | tf_op jit(solution)/shard_map/ppermute | solution.py:283
  31.9 1.2 %collective-permute-start.25 = (bf16[16,32,128]{2,1,0:T(8,128)(2,1)S(1)}, bf16[16,32,128]{2,1,0:T(8,128)(2,1)S(1)}, u32[]{:S(2)}, u32[]{:S(2)}) collective-permute-start(bf16[16,32,128]{2,1,0:T(8,128)(2,1)S(1)} %project.4), channel_id=1, source_target_pairs={{0,4},{1,5},{2,6},{3,7},{4,3},{5,2},{6,1},{7,0},{8,12},{9,13},{10,... | collective-permute-start | bytes 393224 | tf_op jit(solution)/shard_map/ppermute | solution.py:283
  33.1 1.0 %collective-permute-start.23 = (bf16[16,32,128]{2,1,0:T(8,128)(2,1)S(1)}, bf16[16,32,128]{2,1,0:T(8,128)(2,1)S(1)}, u32[]{:S(2)}, u32[]{:S(2)}) collective-permute-start(bf16[16,32,128]{2,1,0:T(8,128)(2,1)S(1)} %project.4), channel_id=1, source_target_pairs={{0,4},{1,5},{2,6},{3,7},{4,1},{5,0},{6,3},{7,2},{8,12},{9,13},{10,... | collective-permute-start | bytes 393224 | tf_op jit(solution)/shard_map/ppermute | solution.py:283
  34.2 0.5 collective-permute-start.26
  34.7 0.4 collective-permute-done.25.refs_6_
  35.1 1.4 %collective-permute-done.24.refs_5_ = bf16[16,32,128]{2,1,0:T(8,128)(2,1)S(1)} collective-permute-done((bf16[16,32,128]{2,1,0:T(8,128)(2,1)S(1)}, bf16[16,32,128]{2,1,0:T(8,128)(2,1)S(1)}, u32[]{:S(2)}, u32[]{:S(2)}) %collective-permute-start.24) | collective-permute-done | bytes 131104 | tf_op jit(solution)/shard_map/ppermute | solution.py:283
  36.5 1.9 %collective-permute-start.30 = (bf16[16,32,128]{2,1,0:T(8,128)(2,1)S(1)}, bf16[16,32,128]{2,1,0:T(8,128)(2,1)S(1)}, u32[]{:S(2)}, u32[]{:S(2)}) collective-permute-start(bf16[16,32,128]{2,1,0:T(8,128)(2,1)S(1)} %get-tuple-element.66), channel_id=1, source_target_pairs={{0,7},{1,6},{2,5},{3,4},{4,0},{5,1},{6,2},{7,3},{8,15},{9,14},{10,... | collective-permute-start | bytes 393224 | tf_op jit(solution)/shard_map/ppermute | solution.py:283
  38.4 1.2 %collective-permute-start.28 = (bf16[16,32,128]{2,1,0:T(8,128)(2,1)S(1)}, bf16[16,32,128]{2,1,0:T(8,128)(2,1)S(1)}, u32[]{:S(2)}, u32[]{:S(2)}) collective-permute-start(bf16[16,32,128]{2,1,0:T(8,128)(2,1)S(1)} %get-tuple-element.66), channel_id=1, source_target_pairs={{0,5},{1,4},{2,7},{3,6},{4,0},{5,1},{6,2},{7,3},{8,13},{9,12},{10,... | collective-permute-start | bytes 393224 | tf_op jit(solution)/shard_map/ppermute | solution.py:283
  39.6 0.5 collective-permute-start.31
  40.1 2.0 %collective-permute-done.30.refs_6_ = bf16[16,32,128]{2,1,0:T(8,128)(2,1)S(1)} collective-permute-done((bf16[16,32,128]{2,1,0:T(8,128)(2,1)S(1)}, bf16[16,32,128]{2,1,0:T(8,128)(2,1)S(1)}, u32[]{:S(2)}, u32[]{:S(2)}) %collective-permute-start.30) | collective-permute-done | bytes 131104 | tf_op jit(solution)/shard_map/ppermute | solution.py:283
  42.1 1.3 %collective-permute-done.29.refs_5_ = bf16[16,32,128]{2,1,0:T(8,128)(2,1)S(1)} collective-permute-done((bf16[16,32,128]{2,1,0:T(8,128)(2,1)S(1)}, bf16[16,32,128]{2,1,0:T(8,128)(2,1)S(1)}, u32[]{:S(2)}, u32[]{:S(2)}) %collective-permute-start.29) | collective-permute-done | bytes 131104 | tf_op jit(solution)/shard_map/ppermute | solution.py:283
  43.8 13.2 %collective-permute-done.32.image = bf16[32,32,128]{2,1,0:T(8,128)(2,1)S(1)} collective-permute-done((bf16[32,32,128]{2,1,0:T(8,128)(2,1)S(1)}, bf16[32,32,128]{2,1,0:T(8,128)(2,1)S(1)}, u32[]{:S(2)}, u32[]{:S(2)}) %collective-permute-start.32) | collective-permute-done | bytes 262176 | tf_op jit(solution)/shard_map/ppermute | solution.py:283
  57.0 0.5 project.5
  57.6 1.4 %collective-permute-start.35 = (bf16[16,32,128]{2,1,0:T(8,128)(2,1)S(1)}, bf16[16,32,128]{2,1,0:T(8,128)(2,1)S(1)}, u32[]{:S(2)}, u32[]{:S(2)}) collective-permute-start(bf16[16,32,128]{2,1,0:T(8,128)(2,1)S(1)} %project.5), channel_id=1, source_target_pairs={{0,4},{1,5},{2,6},{3,7},{4,2},{5,3},{6,0},{7,1},{8,12},{9,13},{10,... | collective-permute-start | bytes 393224 | tf_op jit(solution)/shard_map/ppermute | solution.py:283
  59.1 0.4 collective-permute-start.33
  59.6 2.1 %collective-permute-done.35.refs_5_ = bf16[16,32,128]{2,1,0:T(8,128)(2,1)S(1)} collective-permute-done((bf16[16,32,128]{2,1,0:T(8,128)(2,1)S(1)}, bf16[16,32,128]{2,1,0:T(8,128)(2,1)S(1)}, u32[]{:S(2)}, u32[]{:S(2)}) %collective-permute-start.35) | collective-permute-done | bytes 131104 | tf_op jit(solution)/shard_map/ppermute | solution.py:283
  61.7 3.0 %collective-permute-start.41 = (bf16[16,32,128]{2,1,0:T(8,128)(2,1)S(1)}, bf16[16,32,128]{2,1,0:T(8,128)(2,1)S(1)}, u32[]{:S(2)}, u32[]{:S(2)}) collective-permute-start(bf16[16,32,128]{2,1,0:T(8,128)(2,1)S(1)} %get-tuple-element.74), channel_id=1, source_target_pairs={{0,7},{1,6},{2,5},{3,4},{4,0},{5,1},{6,2},{7,3},{8,15},{9,14},{10,... | collective-permute-start | bytes 393224 | tf_op jit(solution)/shard_map/ppermute | solution.py:283
  64.7 1.2 %collective-permute-start.39 = (bf16[16,32,128]{2,1,0:T(8,128)(2,1)S(1)}, bf16[16,32,128]{2,1,0:T(8,128)(2,1)S(1)}, u32[]{:S(2)}, u32[]{:S(2)}) collective-permute-start(bf16[16,32,128]{2,1,0:T(8,128)(2,1)S(1)} %get-tuple-element.74), channel_id=1, source_target_pairs={{0,5},{1,4},{2,7},{3,6},{4,0},{5,1},{6,2},{7,3},{8,13},{9,12},{10,... | collective-permute-start | bytes 393224 | tf_op jit(solution)/shard_map/ppermute | solution.py:283
  66.0 0.5 collective-permute-start.42
  66.5 1.8 %collective-permute-done.41.refs_6_ = bf16[16,32,128]{2,1,0:T(8,128)(2,1)S(1)} collective-permute-done((bf16[16,32,128]{2,1,0:T(8,128)(2,1)S(1)}, bf16[16,32,128]{2,1,0:T(8,128)(2,1)S(1)}, u32[]{:S(2)}, u32[]{:S(2)}) %collective-permute-start.41) | collective-permute-done | bytes 131104 | tf_op jit(solution)/shard_map/ppermute | solution.py:283
  68.3 1.3 %collective-permute-done.40.refs_5_ = bf16[16,32,128]{2,1,0:T(8,128)(2,1)S(1)} collective-permute-done((bf16[16,32,128]{2,1,0:T(8,128)(2,1)S(1)}, bf16[16,32,128]{2,1,0:T(8,128)(2,1)S(1)}, u32[]{:S(2)}, u32[]{:S(2)}) %collective-permute-start.40) | collective-permute-done | bytes 131104 | tf_op jit(solution)/shard_map/ppermute | solution.py:283
  69.7 0.6 update.15
  70.3 0.8 %second.7 = bf16[4,8,4096]{2,1,0:T(8,128)(2,1)} custom-call(s32[3,80]{1,0:T(4,128)S(4)} %get-tuple-element.44.refs_0_.info, f32[32,32,128]{2,1,0:T(8,128)S(1)} %get-tuple-element.75.refs_1_, f32[32,32,128]{2,1,0:T(8,128)S(1)} %get-tuple-element.76.refs_2_, bf16[32,32,128]{2,1,0:T(8,128)(2,1)S(1)} %collective-permute-done.42.refs_3_, ...), custom_call_target="tpu_custom_call" | custom-call | tf_op jit(solution)/shard_map/second/pallas_call | solution.py:304
  (61 shorter events, 2.2 us)
Async XLA Ops:
  0.0 8.2 %collective-permute-start.1 = (bf16[1,1,80,128,128]{4,3,2,1,0:T(8,128)(2,1)}, bf16[1,1,80,128,128]{4,3,2,1,0:T(8,128)(2,1)S(1)}, u32[]{:S(2)}, u32[]{:S(2)}) collective-permute-start(bf16[1,1,80,128,128]{4,3,2,1,0:T(8,128)(2,1)} %blocks_in.1), channel_id=1, source_target_pairs={{0,4},{1,5},{2,6},{3,7},{4,0},{5,1},{6,2},{7,3},{8,12},{9,13},{10,... | collective-permute-start | bytes 7864328 | tf_op jit(solution)/shard_map/ppermute | solution.py:283
  3.8 5.7 %collective-permute-start.4 = (bf16[5,32,128]{2,1,0:T(8,128)(2,1)S(1)}, bf16[5,32,128]{2,1,0:T(8,128)(2,1)S(1)}, u32[]{:S(2)}, u32[]{:S(2)}) collective-permute-start(bf16[5,32,128]{2,1,0:T(8,128)(2,1)S(1)} %get-tuple-element.46._.refs_2_), channel_id=1, source_target_pairs={{0,3},{1,2},{2,1},{3,0},{4,7},{5,6},{6,5},{7,4},{8,11},{9,10},{10,... | collective-permute-start | bytes 122888 | tf_op jit(solution)/shard_map/ppermute | solution.py:283
  6.1 3.5 %collective-permute-start.3 = (bf16[5,32,128]{2,1,0:T(8,128)(2,1)S(1)}, bf16[5,32,128]{2,1,0:T(8,128)(2,1)S(1)}, u32[]{:S(2)}, u32[]{:S(2)}) collective-permute-start(bf16[5,32,128]{2,1,0:T(8,128)(2,1)S(1)} %get-tuple-element.46._.refs_2_), channel_id=1, source_target_pairs={{0,2},{1,3},{2,0},{3,1},{4,6},{5,7},{6,4},{7,5},{8,10},{9,11},{10,... | collective-permute-start | bytes 122888 | tf_op jit(solution)/shard_map/ppermute | solution.py:283
  6.3 3.3 %collective-permute-start.2 = (bf16[5,32,128]{2,1,0:T(8,128)(2,1)S(1)}, bf16[5,32,128]{2,1,0:T(8,128)(2,1)S(1)}, u32[]{:S(2)}, u32[]{:S(2)}) collective-permute-start(bf16[5,32,128]{2,1,0:T(8,128)(2,1)S(1)} %get-tuple-element.46._.refs_2_), channel_id=1, source_target_pairs={{0,1},{1,0},{2,3},{3,2},{4,5},{5,4},{6,7},{7,6},{8,9},{9,8},{10,11... | collective-permute-start | bytes 122888 | tf_op jit(solution)/shard_map/ppermute | solution.py:283
  6.6 1.7 %collective-permute-start = (s32[2,80]{1,0:T(2,128)S(1)}, s32[2,80]{1,0:T(2,128)S(1)}, u32[]{:S(2)}, u32[]{:S(2)}) collective-permute-start(s32[2,80]{1,0:T(2,128)S(1)} %get-tuple-element.43), channel_id=1, source_target_pairs={{0,4},{1,5},{2,6},{3,7},{4,0},{5,1},{6,2},{7,3},{8,12},{9,13},{10,... | collective-permute-start | bytes 1928 | tf_op jit(solution)/shard_map/ppermute | solution.py:283
  9.7 5.4 %collective-permute-start.8 = (bf16[16,32,128]{2,1,0:T(8,128)(2,1)S(1)}, bf16[16,32,128]{2,1,0:T(8,128)(2,1)S(1)}, u32[]{:S(2)}, u32[]{:S(2)}) collective-permute-start(bf16[16,32,128]{2,1,0:T(8,128)(2,1)S(1)} %get-tuple-element.51), channel_id=1, source_target_pairs={{0,7},{1,6},{2,5},{3,4},{4,0},{5,1},{6,2},{7,3},{8,15},{9,14},{10,... | collective-permute-start | bytes 393224 | tf_op jit(solution)/shard_map/ppermute | solution.py:283
  11.0 5.4 %collective-permute-start.7 = (bf16[16,32,128]{2,1,0:T(8,128)(2,1)S(1)}, bf16[16,32,128]{2,1,0:T(8,128)(2,1)S(1)}, u32[]{:S(2)}, u32[]{:S(2)}) collective-permute-start(bf16[16,32,128]{2,1,0:T(8,128)(2,1)S(1)} %get-tuple-element.51), channel_id=1, source_target_pairs={{0,6},{1,7},{2,4},{3,5},{4,0},{5,1},{6,2},{7,3},{8,14},{9,15},{10,... | collective-permute-start | bytes 393224 | tf_op jit(solution)/shard_map/ppermute | solution.py:283
  12.3 4.4 %collective-permute-start.6 = (bf16[16,32,128]{2,1,0:T(8,128)(2,1)S(1)}, bf16[16,32,128]{2,1,0:T(8,128)(2,1)S(1)}, u32[]{:S(2)}, u32[]{:S(2)}) collective-permute-start(bf16[16,32,128]{2,1,0:T(8,128)(2,1)S(1)} %get-tuple-element.51), channel_id=1, source_target_pairs={{0,5},{1,4},{2,7},{3,6},{4,0},{5,1},{6,2},{7,3},{8,13},{9,12},{10,... | collective-permute-start | bytes 393224 | tf_op jit(solution)/shard_map/ppermute | solution.py:283
  12.6 4.1 %collective-permute-start.5 = (bf16[16,32,128]{2,1,0:T(8,128)(2,1)S(1)}, bf16[16,32,128]{2,1,0:T(8,128)(2,1)S(1)}, u32[]{:S(2)}, u32[]{:S(2)}) collective-permute-start(bf16[16,32,128]{2,1,0:T(8,128)(2,1)S(1)} %get-tuple-element.51), channel_id=1, source_target_pairs={{0,4},{1,5},{2,6},{3,7},{4,0},{5,1},{6,2},{7,3},{8,12},{9,13},{10,... | collective-permute-start | bytes 393224 | tf_op jit(solution)/shard_map/ppermute | solution.py:283
  12.9 3.8 %collective-permute-start.9 = (bf16[32,32,128]{2,1,0:T(8,128)(2,1)S(1)}, bf16[32,32,128]{2,1,0:T(8,128)(2,1)S(1)}, u32[]{:S(2)}, u32[]{:S(2)}) collective-permute-start(bf16[32,32,128]{2,1,0:T(8,128)(2,1)S(1)} %get-tuple-element.54.refs_4_), channel_id=1, source_target_pairs={{0,4},{1,5},{2,6},{3,7},{4,0},{5,1},{6,2},{7,3},{8,12},{9,13},{10,... | collective-permute-start | bytes 786440 | tf_op jit(solution)/shard_map/ppermute | solution.py:283
  16.7 1.6 %collective-permute-start.10 = (bf16[32,32,128]{2,1,0:T(8,128)(2,1)S(1)}, bf16[32,32,128]{2,1,0:T(8,128)(2,1)S(1)}, u32[]{:S(2)}, u32[]{:S(2)}) collective-permute-start(bf16[32,32,128]{2,1,0:T(8,128)(2,1)S(1)} %get-tuple-element.55), channel_id=1, source_target_pairs={{0,4},{1,5},{2,6},{3,7},{4,12},{5,13},{6,14},{7,15},{8,0},{9,1},{1... | collective-permute-start | bytes 786440 | tf_op jit(solution)/shard_map/ppermute | solution.py:283
  18.3 3.3 %collective-permute-start.14 = (bf16[16,32,128]{2,1,0:T(8,128)(2,1)S(1)}, bf16[16,32,128]{2,1,0:T(8,128)(2,1)S(1)}, u32[]{:S(2)}, u32[]{:S(2)}) collective-permute-start(bf16[16,32,128]{2,1,0:T(8,128)(2,1)S(1)} %project.3), channel_id=1, source_target_pairs={{0,4},{1,5},{2,6},{3,7},{4,3},{5,2},{6,1},{7,0},{8,12},{9,13},{10,... | collective-permute-start | bytes 393224 | tf_op jit(solution)/shard_map/ppermute | solution.py:283
  19.7 3.3 %collective-permute-start.13 = (bf16[16,32,128]{2,1,0:T(8,128)(2,1)S(1)}, bf16[16,32,128]{2,1,0:T(8,128)(2,1)S(1)}, u32[]{:S(2)}, u32[]{:S(2)}) collective-permute-start(bf16[16,32,128]{2,1,0:T(8,128)(2,1)S(1)} %project.3), channel_id=1, source_target_pairs={{0,4},{1,5},{2,6},{3,7},{4,2},{5,3},{6,0},{7,1},{8,12},{9,13},{10,... | collective-permute-start | bytes 393224 | tf_op jit(solution)/shard_map/ppermute | solution.py:283
  19.7 3.3 %collective-permute-start.12 = (bf16[16,32,128]{2,1,0:T(8,128)(2,1)S(1)}, bf16[16,32,128]{2,1,0:T(8,128)(2,1)S(1)}, u32[]{:S(2)}, u32[]{:S(2)}) collective-permute-start(bf16[16,32,128]{2,1,0:T(8,128)(2,1)S(1)} %project.3), channel_id=1, source_target_pairs={{0,4},{1,5},{2,6},{3,7},{4,1},{5,0},{6,3},{7,2},{8,12},{9,13},{10,... | collective-permute-start | bytes 393224 | tf_op jit(solution)/shard_map/ppermute | solution.py:283
  20.9 2.1 %collective-permute-start.11 = (bf16[16,32,128]{2,1,0:T(8,128)(2,1)S(1)}, bf16[16,32,128]{2,1,0:T(8,128)(2,1)S(1)}, u32[]{:S(2)}, u32[]{:S(2)}) collective-permute-start(bf16[16,32,128]{2,1,0:T(8,128)(2,1)S(1)} %project.3), channel_id=1, source_target_pairs={{0,4},{1,5},{2,6},{3,7},{4,0},{5,1},{6,2},{7,3},{8,12},{9,13},{10,... | collective-permute-start | bytes 393224 | tf_op jit(solution)/shard_map/ppermute | solution.py:283
  20.9 2.1 %collective-permute-start.15 = (bf16[32,32,128]{2,1,0:T(8,128)(2,1)S(1)}, bf16[32,32,128]{2,1,0:T(8,128)(2,1)S(1)}, u32[]{:S(2)}, u32[]{:S(2)}) collective-permute-start(bf16[32,32,128]{2,1,0:T(8,128)(2,1)S(1)} %collective-permute-done.10.image), channel_id=1, source_target_pairs={{0,4},{1,5},{2,6},{3,7},{4,0},{5,1},{6,2},{7,3},{8,12},{9,13},{10,... | collective-permute-start | bytes 786440 | tf_op jit(solution)/shard_map/ppermute | solution.py:283
  23.0 5.9 %collective-permute-start.19 = (bf16[16,32,128]{2,1,0:T(8,128)(2,1)S(1)}, bf16[16,32,128]{2,1,0:T(8,128)(2,1)S(1)}, u32[]{:S(2)}, u32[]{:S(2)}) collective-permute-start(bf16[16,32,128]{2,1,0:T(8,128)(2,1)S(1)} %get-tuple-element.58), channel_id=1, source_target_pairs={{0,7},{1,6},{2,5},{3,4},{4,0},{5,1},{6,2},{7,3},{8,15},{9,14},{10,... | collective-permute-start | bytes 393224 | tf_op jit(solution)/shard_map/ppermute | solution.py:283
  25.1 5.2 %collective-permute-start.18 = (bf16[16,32,128]{2,1,0:T(8,128)(2,1)S(1)}, bf16[16,32,128]{2,1,0:T(8,128)(2,1)S(1)}, u32[]{:S(2)}, u32[]{:S(2)}) collective-permute-start(bf16[16,32,128]{2,1,0:T(8,128)(2,1)S(1)} %get-tuple-element.58), channel_id=1, source_target_pairs={{0,6},{1,7},{2,4},{3,5},{4,0},{5,1},{6,2},{7,3},{8,14},{9,15},{10,... | collective-permute-start | bytes 393224 | tf_op jit(solution)/shard_map/ppermute | solution.py:283
  25.2 5.1 %collective-permute-start.17 = (bf16[16,32,128]{2,1,0:T(8,128)(2,1)S(1)}, bf16[16,32,128]{2,1,0:T(8,128)(2,1)S(1)}, u32[]{:S(2)}, u32[]{:S(2)}) collective-permute-start(bf16[16,32,128]{2,1,0:T(8,128)(2,1)S(1)} %get-tuple-element.58), channel_id=1, source_target_pairs={{0,5},{1,4},{2,7},{3,6},{4,0},{5,1},{6,2},{7,3},{8,13},{9,12},{10,... | collective-permute-start | bytes 393224 | tf_op jit(solution)/shard_map/ppermute | solution.py:283
  26.1 4.2 %collective-permute-start.16 = (bf16[16,32,128]{2,1,0:T(8,128)(2,1)S(1)}, bf16[16,32,128]{2,1,0:T(8,128)(2,1)S(1)}, u32[]{:S(2)}, u32[]{:S(2)}) collective-permute-start(bf16[16,32,128]{2,1,0:T(8,128)(2,1)S(1)} %get-tuple-element.58), channel_id=1, source_target_pairs={{0,4},{1,5},{2,6},{3,7},{4,0},{5,1},{6,2},{7,3},{8,12},{9,13},{10,... | collective-permute-start | bytes 393224 | tf_op jit(solution)/shard_map/ppermute | solution.py:283
  26.2 4.0 %collective-permute-start.20 = (bf16[32,32,128]{2,1,0:T(8,128)(2,1)S(1)}, bf16[32,32,128]{2,1,0:T(8,128)(2,1)S(1)}, u32[]{:S(2)}, u32[]{:S(2)}) collective-permute-start(bf16[32,32,128]{2,1,0:T(8,128)(2,1)S(1)} %get-tuple-element.61.refs_4_), channel_id=1, source_target_pairs={{0,4},{1,5},{2,6},{3,7},{4,0},{5,1},{6,2},{7,3},{8,12},{9,13},{10,... | collective-permute-start | bytes 786440 | tf_op jit(solution)/shard_map/ppermute | solution.py:283
  30.3 1.6 %collective-permute-start.21 = (bf16[32,32,128]{2,1,0:T(8,128)(2,1)S(1)}, bf16[32,32,128]{2,1,0:T(8,128)(2,1)S(1)}, u32[]{:S(2)}, u32[]{:S(2)}) collective-permute-start(bf16[32,32,128]{2,1,0:T(8,128)(2,1)S(1)} %get-tuple-element.63), channel_id=1, source_target_pairs={{0,4},{1,5},{2,6},{3,7},{4,0},{5,1},{6,2},{7,3},{8,12},{9,13},{10,... | collective-permute-start | bytes 786440 | tf_op jit(solution)/shard_map/ppermute | solution.py:283
  31.9 3.1 %collective-permute-start.25 = (bf16[16,32,128]{2,1,0:T(8,128)(2,1)S(1)}, bf16[16,32,128]{2,1,0:T(8,128)(2,1)S(1)}, u32[]{:S(2)}, u32[]{:S(2)}) collective-permute-start(bf16[16,32,128]{2,1,0:T(8,128)(2,1)S(1)} %project.4), channel_id=1, source_target_pairs={{0,4},{1,5},{2,6},{3,7},{4,3},{5,2},{6,1},{7,0},{8,12},{9,13},{10,... | collective-permute-start | bytes 393224 | tf_op jit(solution)/shard_map/ppermute | solution.py:283
  33.1 3.3 %collective-permute-start.24 = (bf16[16,32,128]{2,1,0:T(8,128)(2,1)S(1)}, bf16[16,32,128]{2,1,0:T(8,128)(2,1)S(1)}, u32[]{:S(2)}, u32[]{:S(2)}) collective-permute-start(bf16[16,32,128]{2,1,0:T(8,128)(2,1)S(1)} %project.4), channel_id=1, source_target_pairs={{0,4},{1,5},{2,6},{3,7},{4,2},{5,3},{6,0},{7,1},{8,12},{9,13},{10,... | collective-permute-start | bytes 393224 | tf_op jit(solution)/shard_map/ppermute | solution.py:283
  33.1 3.4 %collective-permute-start.23 = (bf16[16,32,128]{2,1,0:T(8,128)(2,1)S(1)}, bf16[16,32,128]{2,1,0:T(8,128)(2,1)S(1)}, u32[]{:S(2)}, u32[]{:S(2)}) collective-permute-start(bf16[16,32,128]{2,1,0:T(8,128)(2,1)S(1)} %project.4), channel_id=1, source_target_pairs={{0,4},{1,5},{2,6},{3,7},{4,1},{5,0},{6,3},{7,2},{8,12},{9,13},{10,... | collective-permute-start | bytes 393224 | tf_op jit(solution)/shard_map/ppermute | solution.py:283
  34.1 2.3 %collective-permute-start.22 = (bf16[16,32,128]{2,1,0:T(8,128)(2,1)S(1)}, bf16[16,32,128]{2,1,0:T(8,128)(2,1)S(1)}, u32[]{:S(2)}, u32[]{:S(2)}) collective-permute-start(bf16[16,32,128]{2,1,0:T(8,128)(2,1)S(1)} %project.4), channel_id=1, source_target_pairs={{0,4},{1,5},{2,6},{3,7},{4,0},{5,1},{6,2},{7,3},{8,12},{9,13},{10,... | collective-permute-start | bytes 393224 | tf_op jit(solution)/shard_map/ppermute | solution.py:283
  34.2 2.3 %collective-permute-start.26 = (bf16[32,32,128]{2,1,0:T(8,128)(2,1)S(1)}, bf16[32,32,128]{2,1,0:T(8,128)(2,1)S(1)}, u32[]{:S(2)}, u32[]{:S(2)}) collective-permute-start(bf16[32,32,128]{2,1,0:T(8,128)(2,1)S(1)} %collective-permute-done.21.image), channel_id=1, source_target_pairs={{0,4},{1,5},{2,6},{3,7},{4,0},{5,1},{6,2},{7,3},{8,12},{9,13},{10,... | collective-permute-start | bytes 786440 | tf_op jit(solution)/shard_map/ppermute | solution.py:283
  36.5 5.6 %collective-permute-start.30 = (bf16[16,32,128]{2,1,0:T(8,128)(2,1)S(1)}, bf16[16,32,128]{2,1,0:T(8,128)(2,1)S(1)}, u32[]{:S(2)}, u32[]{:S(2)}) collective-permute-start(bf16[16,32,128]{2,1,0:T(8,128)(2,1)S(1)} %get-tuple-element.66), channel_id=1, source_target_pairs={{0,7},{1,6},{2,5},{3,4},{4,0},{5,1},{6,2},{7,3},{8,15},{9,14},{10,... | collective-permute-start | bytes 393224 | tf_op jit(solution)/shard_map/ppermute | solution.py:283
  38.3 5.1 %collective-permute-start.29 = (bf16[16,32,128]{2,1,0:T(8,128)(2,1)S(1)}, bf16[16,32,128]{2,1,0:T(8,128)(2,1)S(1)}, u32[]{:S(2)}, u32[]{:S(2)}) collective-permute-start(bf16[16,32,128]{2,1,0:T(8,128)(2,1)S(1)} %get-tuple-element.66), channel_id=1, source_target_pairs={{0,6},{1,7},{2,4},{3,5},{4,0},{5,1},{6,2},{7,3},{8,14},{9,15},{10,... | collective-permute-start | bytes 393224 | tf_op jit(solution)/shard_map/ppermute | solution.py:283
  38.4 5.0 %collective-permute-start.28 = (bf16[16,32,128]{2,1,0:T(8,128)(2,1)S(1)}, bf16[16,32,128]{2,1,0:T(8,128)(2,1)S(1)}, u32[]{:S(2)}, u32[]{:S(2)}) collective-permute-start(bf16[16,32,128]{2,1,0:T(8,128)(2,1)S(1)} %get-tuple-element.66), channel_id=1, source_target_pairs={{0,5},{1,4},{2,7},{3,6},{4,0},{5,1},{6,2},{7,3},{8,13},{9,12},{10,... | collective-permute-start | bytes 393224 | tf_op jit(solution)/shard_map/ppermute | solution.py:283
  39.6 3.9 %collective-permute-start.27 = (bf16[16,32,128]{2,1,0:T(8,128)(2,1)S(1)}, bf16[16,32,128]{2,1,0:T(8,128)(2,1)S(1)}, u32[]{:S(2)}, u32[]{:S(2)}) collective-permute-start(bf16[16,32,128]{2,1,0:T(8,128)(2,1)S(1)} %get-tuple-element.66), channel_id=1, source_target_pairs={{0,4},{1,5},{2,6},{3,7},{4,0},{5,1},{6,2},{7,3},{8,12},{9,13},{10,... | collective-permute-start | bytes 393224 | tf_op jit(solution)/shard_map/ppermute | solution.py:283
  39.6 3.8 %collective-permute-start.31 = (bf16[32,32,128]{2,1,0:T(8,128)(2,1)S(1)}, bf16[32,32,128]{2,1,0:T(8,128)(2,1)S(1)}, u32[]{:S(2)}, u32[]{:S(2)}) collective-permute-start(bf16[32,32,128]{2,1,0:T(8,128)(2,1)S(1)} %get-tuple-element.69.refs_4_), channel_id=1, source_target_pairs={{0,4},{1,5},{2,6},{3,7},{4,0},{5,1},{6,2},{7,3},{8,12},{9,13},{10,... | collective-permute-start | bytes 786440 | tf_op jit(solution)/shard_map/ppermute | solution.py:283
  43.7 13.3 %collective-permute-start.32 = (bf16[32,32,128]{2,1,0:T(8,128)(2,1)S(1)}, bf16[32,32,128]{2,1,0:T(8,128)(2,1)S(1)}, u32[]{:S(2)}, u32[]{:S(2)}) collective-permute-start(bf16[32,32,128]{2,1,0:T(8,128)(2,1)S(1)} %get-tuple-element.71), channel_id=1, source_target_pairs={{0,4},{1,5},{2,6},{3,7},{4,0},{5,1},{6,2},{7,3},{8,12},{9,13},{10,... | collective-permute-start | bytes 786440 | tf_op jit(solution)/shard_map/ppermute | solution.py:283
  57.5 2.1 %collective-permute-start.36 = (bf16[16,32,128]{2,1,0:T(8,128)(2,1)S(1)}, bf16[16,32,128]{2,1,0:T(8,128)(2,1)S(1)}, u32[]{:S(2)}, u32[]{:S(2)}) collective-permute-start(bf16[16,32,128]{2,1,0:T(8,128)(2,1)S(1)} %project.5), channel_id=1, source_target_pairs={{0,4},{1,5},{2,6},{3,7},{4,3},{5,2},{6,1},{7,0},{8,12},{9,13},{10,... | collective-permute-start | bytes 393224 | tf_op jit(solution)/shard_map/ppermute | solution.py:283
  57.6 4.1 %collective-permute-start.35 = (bf16[16,32,128]{2,1,0:T(8,128)(2,1)S(1)}, bf16[16,32,128]{2,1,0:T(8,128)(2,1)S(1)}, u32[]{:S(2)}, u32[]{:S(2)}) collective-permute-start(bf16[16,32,128]{2,1,0:T(8,128)(2,1)S(1)} %project.5), channel_id=1, source_target_pairs={{0,4},{1,5},{2,6},{3,7},{4,2},{5,3},{6,0},{7,1},{8,12},{9,13},{10,... | collective-permute-start | bytes 393224 | tf_op jit(solution)/shard_map/ppermute | solution.py:283
  59.0 2.7 %collective-permute-start.34 = (bf16[16,32,128]{2,1,0:T(8,128)(2,1)S(1)}, bf16[16,32,128]{2,1,0:T(8,128)(2,1)S(1)}, u32[]{:S(2)}, u32[]{:S(2)}) collective-permute-start(bf16[16,32,128]{2,1,0:T(8,128)(2,1)S(1)} %project.5), channel_id=1, source_target_pairs={{0,4},{1,5},{2,6},{3,7},{4,1},{5,0},{6,3},{7,2},{8,12},{9,13},{10,... | collective-permute-start | bytes 393224 | tf_op jit(solution)/shard_map/ppermute | solution.py:283
  59.1 2.6 %collective-permute-start.33 = (bf16[16,32,128]{2,1,0:T(8,128)(2,1)S(1)}, bf16[16,32,128]{2,1,0:T(8,128)(2,1)S(1)}, u32[]{:S(2)}, u32[]{:S(2)}) collective-permute-start(bf16[16,32,128]{2,1,0:T(8,128)(2,1)S(1)} %project.5), channel_id=1, source_target_pairs={{0,4},{1,5},{2,6},{3,7},{4,0},{5,1},{6,2},{7,3},{8,12},{9,13},{10,... | collective-permute-start | bytes 393224 | tf_op jit(solution)/shard_map/ppermute | solution.py:283
  59.5 2.2 %collective-permute-start.37 = (bf16[32,32,128]{2,1,0:T(8,128)(2,1)S(1)}, bf16[32,32,128]{2,1,0:T(8,128)(2,1)S(1)}, u32[]{:S(2)}, u32[]{:S(2)}) collective-permute-start(bf16[32,32,128]{2,1,0:T(8,128)(2,1)S(1)} %collective-permute-done.32.image), channel_id=1, source_target_pairs={{0,4},{1,5},{2,6},{3,7},{4,0},{5,1},{6,2},{7,3},{8,12},{9,13},{10,... | collective-permute-start | bytes 786440 | tf_op jit(solution)/shard_map/ppermute | solution.py:283
  61.7 6.6 %collective-permute-start.41 = (bf16[16,32,128]{2,1,0:T(8,128)(2,1)S(1)}, bf16[16,32,128]{2,1,0:T(8,128)(2,1)S(1)}, u32[]{:S(2)}, u32[]{:S(2)}) collective-permute-start(bf16[16,32,128]{2,1,0:T(8,128)(2,1)S(1)} %get-tuple-element.74), channel_id=1, source_target_pairs={{0,7},{1,6},{2,5},{3,4},{4,0},{5,1},{6,2},{7,3},{8,15},{9,14},{10,... | collective-permute-start | bytes 393224 | tf_op jit(solution)/shard_map/ppermute | solution.py:283
  64.7 5.0 %collective-permute-start.40 = (bf16[16,32,128]{2,1,0:T(8,128)(2,1)S(1)}, bf16[16,32,128]{2,1,0:T(8,128)(2,1)S(1)}, u32[]{:S(2)}, u32[]{:S(2)}) collective-permute-start(bf16[16,32,128]{2,1,0:T(8,128)(2,1)S(1)} %get-tuple-element.74), channel_id=1, source_target_pairs={{0,6},{1,7},{2,4},{3,5},{4,0},{5,1},{6,2},{7,3},{8,14},{9,15},{10,... | collective-permute-start | bytes 393224 | tf_op jit(solution)/shard_map/ppermute | solution.py:283
  64.7 4.9 %collective-permute-start.39 = (bf16[16,32,128]{2,1,0:T(8,128)(2,1)S(1)}, bf16[16,32,128]{2,1,0:T(8,128)(2,1)S(1)}, u32[]{:S(2)}, u32[]{:S(2)}) collective-permute-start(bf16[16,32,128]{2,1,0:T(8,128)(2,1)S(1)} %get-tuple-element.74), channel_id=1, source_target_pairs={{0,5},{1,4},{2,7},{3,6},{4,0},{5,1},{6,2},{7,3},{8,13},{9,12},{10,... | collective-permute-start | bytes 393224 | tf_op jit(solution)/shard_map/ppermute | solution.py:283
  66.0 3.7 %collective-permute-start.38 = (bf16[16,32,128]{2,1,0:T(8,128)(2,1)S(1)}, bf16[16,32,128]{2,1,0:T(8,128)(2,1)S(1)}, u32[]{:S(2)}, u32[]{:S(2)}) collective-permute-start(bf16[16,32,128]{2,1,0:T(8,128)(2,1)S(1)} %get-tuple-element.74), channel_id=1, source_target_pairs={{0,4},{1,5},{2,6},{3,7},{4,0},{5,1},{6,2},{7,3},{8,12},{9,13},{10,... | collective-permute-start | bytes 393224 | tf_op jit(solution)/shard_map/ppermute | solution.py:283
  66.0 4.3 %collective-permute-start.42 = (bf16[32,32,128]{2,1,0:T(8,128)(2,1)S(1)}, bf16[32,32,128]{2,1,0:T(8,128)(2,1)S(1)}, u32[]{:S(2)}, u32[]{:S(2)}) collective-permute-start(bf16[32,32,128]{2,1,0:T(8,128)(2,1)S(1)} %get-tuple-element.77.refs_4_), channel_id=1, source_target_pairs={{0,4},{1,5},{2,6},{3,7},{4,0},{5,1},{6,2},{7,3},{8,12},{9,13},{10,... | collective-permute-start | bytes 786440 | tf_op jit(solution)/shard_map/ppermute | solution.py:283

commit v19 on v14

--- a/solution.py
+++ b/solution.py
@@ -170,9 +170,11 @@
     return jnp.logical_and(info[0, 0] == place, info[0, 1] == core)
 
 
-def project_kernel(place, info, image, tall, terms):
+def project_kernel(place, info, lower, upper, tall, terms, image):
     @pl.when(on_core(info, place, 1))
     def _():
+        image[: CB // 2] = lower[...]
+        image[CB // 2 :] = upper[...]
         project(info, tall, image, terms)
 
 
@@ -214,7 +216,7 @@
     refs = list(refs)
     info, change, image_in, shot = take(refs, 4)
     held = take(refs, 1) if place > 0 else []
-    image = None if last else take(refs, 1)[0]
+    parts = [] if last else take(refs, 2)
     (out,) = refs
     batches, per_batch, _ = out.shape
 
@@ -232,8 +234,8 @@
     @pl.when(on_core(info, place, 1))
     def _():
         write(value)
-        if not last:
-            image[...] = out[...]
+        for i, part in enumerate(parts):
+            part[...] = out[i * (CB // 2) : (i + 1) * (CB // 2)]
 
     @pl.when(on_core(info, place, 0))
     def _():
@@ -262,6 +264,7 @@
 
     image_shape = (CB, slices, BS)
     image_out = jax.ShapeDtypeStruct(image_shape, jnp.bfloat16)
+    part_out = jax.ShapeDtypeStruct((CB // 2, slices, BS), jnp.bfloat16)
     terms_out = jax.ShapeDtypeStruct((row_blocks, slices, BS), jnp.bfloat16)
     rays_out = jax.ShapeDtypeStruct((row_blocks + 1, slices, BS), jnp.float32)
     final_out = jax.ShapeDtypeStruct((batches, per_batch, PIX), jnp.bfloat16)
@@ -367,7 +370,7 @@
     info = pltpu.with_memory_space_constraint(info, pltpu.SMEM)
 
     held = []
-    image, rays = None, None
+    parts, rays = None, None
     change_out = jax.ShapeDtypeStruct(image_shape, jnp.float32)
 
     def updated(place, core, terms):
@@ -402,12 +405,11 @@
                     return (p, 0, t) if c else (place - 1, 0, t)
                 return p, 1 - c, t
 
-            image = sent(image, hop)
-            terms = call(
+            terms, image = call(
                 functools.partial(project_kernel, place),
                 1,
-                [info, image, tall],
-                terms_out,
+                [info] + [sent(part, hop) for part in parts] + [tall],
+                (terms_out, image_out),
                 [],
                 "project",
             )
@@ -426,14 +428,14 @@
             functools.partial(second_kernel, place, last),
             1,
             [info, change, swapped(shot), shot] + held,
-            final_out if last else (image_out, image_out),
+            final_out if last else (part_out, part_out, image_out),
             [],
             "second",
         )
         if last:
             return outs[None]
-        image = outs[0]
-        held = [outs[1]]
+        parts = outs[:2]
+        held = [outs[2]]
 
 
 def solution(mesh):

time: 71.1 us -> 71.1 us (level)
  starting transfers between devices: 27.7 us -> 37.1 us
  waiting for transfers between devices: 35.7 us -> 26.5 us
    ppermute x43 -> x46, starting transfers between devices: 27.7 us -> 37.1 us  [sent(): return lax.ppermute(value, ('subset', 'tile'), pairs)]
    ppermute x43 -> x46, waiting for transfers between devices: 35.7 us -> 26.5 us  [sent(): return lax.ppermute(value, ('subset', 'tile'), pairs)]
  transfers between devices with their start and end apart: 43 -> 46, of which waited for: 18 -> 22; matrix products, arithmetic and copies ran while one was open for 0% -> 0% of each run, Pallas kernels for 8% -> 8%
where the time goes in v19:
time: 71.1 us; the launch traced here: 71 us
  starting transfers between devices  37.1 us (52%)
  waiting for transfers between devices  26.5 us (37%)
  Pallas kernels  7.05 us (10%)
    ppermute x46, starting transfers between devices, sent(): return lax.ppermute(value, ('subset', 'tile'), pairs)  37.1 us
    ppermute x46, waiting for transfers between devices, sent(): return lax.ppermute(value, ('subset', 'tile'), pairs)  26.5 us
    pallas_call x1, Pallas kernels, per_device(): pl.pallas_call(functools.partial(head_kernel, row_blocks, chunks), out_sh...  3.09 us
    pallas_call x19, Pallas kernels, call(): pl.pallas_call(kernel, out_shape=out_shape, in_specs=[SMEM] * smem + [VME...  2.16 us
  transfers between devices with their start and end apart: 46, of which 22 were waited for; matrix products, arithmetic and copies ran while one was open for 0% of the time, Pallas kernels for 8%

profile of v19, /device:TPU:25, one launch (start us, length us, event | category | flops | bytes accessed | tf_op | source)
XLA Modules:
  0.0 71.0 jit_solution(10692856815205021669)
XLA Ops:
  0.0 0.7 collective-permute-start.1
  0.8 3.1 %head.1 = (bf16[5,32,128]{2,1,0:T(8,128)(2,1)S(1)}, s32[2,80]{1,0:T(2,128)S(1)}, s32[3,80]{1,0:T(4,128)S(4)}, bf16[1,1,80,128,128]{4,3,2,1,0:T(8,128)(2,1)S(1)}) custom-call(s32[3]{0:T(128)S(1)} %pad_add_fusion.pos, s32[1,1,80]{2,1,0:T(1,128)} %rows_in.1, s32[1,1,80]{2,1,0:T(1,128)} %cols_in.1, bf16[1,1,80,128,128]{4,3,2,1,0:T(8,128)(2,1)} %blocks_in.1, ...), custom_call_target="tpu_custom_call" | custom-call | tf_op jit(solution)/shard_map/head/pallas_call | solution.py:318
  3.9 2.2 %collective-permute-start.4 = (bf16[5,32,128]{2,1,0:T(8,128)(2,1)S(1)}, bf16[5,32,128]{2,1,0:T(8,128)(2,1)S(1)}, u32[]{:S(2)}, u32[]{:S(2)}) collective-permute-start(bf16[5,32,128]{2,1,0:T(8,128)(2,1)S(1)} %get-tuple-element.40._.refs_2_), channel_id=1, source_target_pairs={{0,3},{1,2},{2,1},{3,0},{4,7},{5,6},{6,5},{7,4},{8,11},{9,10},{10,... | collective-permute-start | bytes 122888 | tf_op jit(solution)/shard_map/ppermute | solution.py:282
  6.6 0.8 %collective-permute-start = (s32[2,80]{1,0:T(2,128)S(1)}, s32[2,80]{1,0:T(2,128)S(1)}, u32[]{:S(2)}, u32[]{:S(2)}) collective-permute-start(s32[2,80]{1,0:T(2,128)S(1)} %get-tuple-element.37), channel_id=1, source_target_pairs={{0,4},{1,5},{2,6},{3,7},{4,0},{5,1},{6,2},{7,3},{8,12},{9,13},{10,... | collective-permute-start | bytes 1928 | tf_op jit(solution)/shard_map/ppermute | solution.py:282
  7.4 0.5 pack_own.1.refs_1_
  8.2 1.3 %pack_other.1 = (s32[3,80]{1,0:T(4,128)S(4)}, bf16[16,640,128]{2,1,0:T(8,128)(2,1)S(1)}) custom-call(s32[3,80]{1,0:T(4,128)S(4)} %get-tuple-element.36.own, s32[2,80]{1,0:T(2,128)S(1)} %collective-permute-done.table2, bf16[1,1,80,128,128]{4,3,2,1,0:T(8,128)(2,1)S(1)} %collective-permute-done.1.blocks2), custom_call_target="tpu_custom_call" | custom-call | tf_op jit(solution)/shard_map/pack_other/pallas_call | solution.py:359
  9.7 1.3 %collective-permute-start.8 = (bf16[16,32,128]{2,1,0:T(8,128)(2,1)S(1)}, bf16[16,32,128]{2,1,0:T(8,128)(2,1)S(1)}, u32[]{:S(2)}, u32[]{:S(2)}) collective-permute-start(bf16[16,32,128]{2,1,0:T(8,128)(2,1)S(1)} %get-tuple-element.44), channel_id=1, source_target_pairs={{0,7},{1,6},{2,5},{3,4},{4,0},{5,1},{6,2},{7,3},{8,15},{9,14},{10,... | collective-permute-start | bytes 393224 | tf_op jit(solution)/shard_map/ppermute | solution.py:282
  11.0 1.3 %collective-permute-start.7 = (bf16[16,32,128]{2,1,0:T(8,128)(2,1)S(1)}, bf16[16,32,128]{2,1,0:T(8,128)(2,1)S(1)}, u32[]{:S(2)}, u32[]{:S(2)}) collective-permute-start(bf16[16,32,128]{2,1,0:T(8,128)(2,1)S(1)} %get-tuple-element.44), channel_id=1, source_target_pairs={{0,6},{1,7},{2,4},{3,5},{4,0},{5,1},{6,2},{7,3},{8,14},{9,15},{10,... | collective-permute-start | bytes 393224 | tf_op jit(solution)/shard_map/ppermute | solution.py:282
  12.3 0.3 collective-permute-start.6
  13.1 2.0 %collective-permute-done.8.refs_6_ = bf16[16,32,128]{2,1,0:T(8,128)(2,1)S(1)} collective-permute-done((bf16[16,32,128]{2,1,0:T(8,128)(2,1)S(1)}, bf16[16,32,128]{2,1,0:T(8,128)(2,1)S(1)}, u32[]{:S(2)}, u32[]{:S(2)}) %collective-permute-start.8) | collective-permute-done | bytes 131104 | tf_op jit(solution)/shard_map/ppermute | solution.py:282
  15.1 1.3 %collective-permute-done.7.refs_5_ = bf16[16,32,128]{2,1,0:T(8,128)(2,1)S(1)} collective-permute-done((bf16[16,32,128]{2,1,0:T(8,128)(2,1)S(1)}, bf16[16,32,128]{2,1,0:T(8,128)(2,1)S(1)}, u32[]{:S(2)}, u32[]{:S(2)}) %collective-permute-start.7) | collective-permute-done | bytes 131104 | tf_op jit(solution)/shard_map/ppermute | solution.py:282
  16.8 0.5 collective-permute-start.11
  17.3 0.8 %collective-permute-done.10.lower = bf16[16,32,128]{2,1,0:T(8,128)(2,1)S(1)} collective-permute-done((bf16[16,32,128]{2,1,0:T(8,128)(2,1)S(1)}, bf16[16,32,128]{2,1,0:T(8,128)(2,1)S(1)}, u32[]{:S(2)}, u32[]{:S(2)}) %collective-permute-start.10) | collective-permute-done | bytes 131104 | tf_op jit(solution)/shard_map/ppermute | solution.py:282
  18.3 1.5 %collective-permute-start.15 = (bf16[16,32,128]{2,1,0:T(8,128)(2,1)S(1)}, bf16[16,32,128]{2,1,0:T(8,128)(2,1)S(1)}, u32[]{:S(2)}, u32[]{:S(2)}) collective-permute-start(bf16[16,32,128]{2,1,0:T(8,128)(2,1)S(1)} %get-tuple-element.48), channel_id=1, source_target_pairs={{0,4},{1,5},{2,6},{3,7},{4,3},{5,2},{6,1},{7,0},{8,12},{9,13},{10,... | collective-permute-start | bytes 393224 | tf_op jit(solution)/shard_map/ppermute | solution.py:282
  19.9 1.2 %collective-permute-start.13 = (bf16[16,32,128]{2,1,0:T(8,128)(2,1)S(1)}, bf16[16,32,128]{2,1,0:T(8,128)(2,1)S(1)}, u32[]{:S(2)}, u32[]{:S(2)}) collective-permute-start(bf16[16,32,128]{2,1,0:T(8,128)(2,1)S(1)} %get-tuple-element.48), channel_id=1, source_target_pairs={{0,4},{1,5},{2,6},{3,7},{4,1},{5,0},{6,3},{7,2},{8,12},{9,13},{10,... | collective-permute-start | bytes 393224 | tf_op jit(solution)/shard_map/ppermute | solution.py:282
  21.1 0.5 collective-permute-start.16
  21.8 1.4 %collective-permute-done.14.refs_5_ = bf16[16,32,128]{2,1,0:T(8,128)(2,1)S(1)} collective-permute-done((bf16[16,32,128]{2,1,0:T(8,128)(2,1)S(1)}, bf16[16,32,128]{2,1,0:T(8,128)(2,1)S(1)}, u32[]{:S(2)}, u32[]{:S(2)}) %collective-permute-start.14) | collective-permute-done | bytes 131104 | tf_op jit(solution)/shard_map/ppermute | solution.py:282
  23.2 2.1 %collective-permute-start.20 = (bf16[16,32,128]{2,1,0:T(8,128)(2,1)S(1)}, bf16[16,32,128]{2,1,0:T(8,128)(2,1)S(1)}, u32[]{:S(2)}, u32[]{:S(2)}) collective-permute-start(bf16[16,32,128]{2,1,0:T(8,128)(2,1)S(1)} %get-tuple-element.50), channel_id=1, source_target_pairs={{0,7},{1,6},{2,5},{3,4},{4,0},{5,1},{6,2},{7,3},{8,15},{9,14},{10,... | collective-permute-start | bytes 393224 | tf_op jit(solution)/shard_map/ppermute | solution.py:282
  25.3 0.9 %collective-permute-start.18 = (bf16[16,32,128]{2,1,0:T(8,128)(2,1)S(1)}, bf16[16,32,128]{2,1,0:T(8,128)(2,1)S(1)}, u32[]{:S(2)}, u32[]{:S(2)}) collective-permute-start(bf16[16,32,128]{2,1,0:T(8,128)(2,1)S(1)} %get-tuple-element.50), channel_id=1, source_target_pairs={{0,5},{1,4},{2,7},{3,6},{4,0},{5,1},{6,2},{7,3},{8,13},{9,12},{10,... | collective-permute-start | bytes 393224 | tf_op jit(solution)/shard_map/ppermute | solution.py:282
  26.3 0.4 collective-permute-start.21
  26.8 2.4 %collective-permute-done.20.refs_6_ = bf16[16,32,128]{2,1,0:T(8,128)(2,1)S(1)} collective-permute-done((bf16[16,32,128]{2,1,0:T(8,128)(2,1)S(1)}, bf16[16,32,128]{2,1,0:T(8,128)(2,1)S(1)}, u32[]{:S(2)}, u32[]{:S(2)}) %collective-permute-start.20) | collective-permute-done | bytes 131104 | tf_op jit(solution)/shard_map/ppermute | solution.py:282
  29.1 1.3 %collective-permute-done.19.refs_5_ = bf16[16,32,128]{2,1,0:T(8,128)(2,1)S(1)} collective-permute-done((bf16[16,32,128]{2,1,0:T(8,128)(2,1)S(1)}, bf16[16,32,128]{2,1,0:T(8,128)(2,1)S(1)}, u32[]{:S(2)}, u32[]{:S(2)}) %collective-permute-start.19) | collective-permute-done | bytes 131104 | tf_op jit(solution)/shard_map/ppermute | solution.py:282
  30.6 0.5 collective-permute-start.23
  31.1 0.8 %collective-permute-done.22.lower = bf16[16,32,128]{2,1,0:T(8,128)(2,1)S(1)} collective-permute-done((bf16[16,32,128]{2,1,0:T(8,128)(2,1)S(1)}, bf16[16,32,128]{2,1,0:T(8,128)(2,1)S(1)}, u32[]{:S(2)}, u32[]{:S(2)}) %collective-permute-start.22) | collective-permute-done | bytes 131104 | tf_op jit(solution)/shard_map/ppermute | solution.py:282
  32.1 1.4 %collective-permute-start.27 = (bf16[16,32,128]{2,1,0:T(8,128)(2,1)S(1)}, bf16[16,32,128]{2,1,0:T(8,128)(2,1)S(1)}, u32[]{:S(2)}, u32[]{:S(2)}) collective-permute-start(bf16[16,32,128]{2,1,0:T(8,128)(2,1)S(1)} %get-tuple-element.55), channel_id=1, source_target_pairs={{0,4},{1,5},{2,6},{3,7},{4,3},{5,2},{6,1},{7,0},{8,12},{9,13},{10,... | collective-permute-start | bytes 393224 | tf_op jit(solution)/shard_map/ppermute | solution.py:282
  33.5 1.0 %collective-permute-start.25 = (bf16[16,32,128]{2,1,0:T(8,128)(2,1)S(1)}, bf16[16,32,128]{2,1,0:T(8,128)(2,1)S(1)}, u32[]{:S(2)}, u32[]{:S(2)}) collective-permute-start(bf16[16,32,128]{2,1,0:T(8,128)(2,1)S(1)} %get-tuple-element.55), channel_id=1, source_target_pairs={{0,4},{1,5},{2,6},{3,7},{4,1},{5,0},{6,3},{7,2},{8,12},{9,13},{10,... | collective-permute-start | bytes 393224 | tf_op jit(solution)/shard_map/ppermute | solution.py:282
  34.5 0.5 collective-permute-start.28
  35.0 0.5 collective-permute-done.27.refs_6_
  35.4 1.4 %collective-permute-done.26.refs_5_ = bf16[16,32,128]{2,1,0:T(8,128)(2,1)S(1)} collective-permute-done((bf16[16,32,128]{2,1,0:T(8,128)(2,1)S(1)}, bf16[16,32,128]{2,1,0:T(8,128)(2,1)S(1)}, u32[]{:S(2)}, u32[]{:S(2)}) %collective-permute-start.26) | collective-permute-done | bytes 131104 | tf_op jit(solution)/shard_map/ppermute | solution.py:282
  36.9 1.8 %collective-permute-start.32 = (bf16[16,32,128]{2,1,0:T(8,128)(2,1)S(1)}, bf16[16,32,128]{2,1,0:T(8,128)(2,1)S(1)}, u32[]{:S(2)}, u32[]{:S(2)}) collective-permute-start(bf16[16,32,128]{2,1,0:T(8,128)(2,1)S(1)} %get-tuple-element.57), channel_id=1, source_target_pairs={{0,7},{1,6},{2,5},{3,4},{4,0},{5,1},{6,2},{7,3},{8,15},{9,14},{10,... | collective-permute-start | bytes 393224 | tf_op jit(solution)/shard_map/ppermute | solution.py:282
  38.7 1.2 %collective-permute-start.30 = (bf16[16,32,128]{2,1,0:T(8,128)(2,1)S(1)}, bf16[16,32,128]{2,1,0:T(8,128)(2,1)S(1)}, u32[]{:S(2)}, u32[]{:S(2)}) collective-permute-start(bf16[16,32,128]{2,1,0:T(8,128)(2,1)S(1)} %get-tuple-element.57), channel_id=1, source_target_pairs={{0,5},{1,4},{2,7},{3,6},{4,0},{5,1},{6,2},{7,3},{8,13},{9,12},{10,... | collective-permute-start | bytes 393224 | tf_op jit(solution)/shard_map/ppermute | solution.py:282
  40.0 0.5 collective-permute-start.33
  40.5 2.0 %collective-permute-done.32.refs_6_ = bf16[16,32,128]{2,1,0:T(8,128)(2,1)S(1)} collective-permute-done((bf16[16,32,128]{2,1,0:T(8,128)(2,1)S(1)}, bf16[16,32,128]{2,1,0:T(8,128)(2,1)S(1)}, u32[]{:S(2)}, u32[]{:S(2)}) %collective-permute-start.32) | collective-permute-done | bytes 131104 | tf_op jit(solution)/shard_map/ppermute | solution.py:282
  42.4 1.3 %collective-permute-done.31.refs_5_ = bf16[16,32,128]{2,1,0:T(8,128)(2,1)S(1)} collective-permute-done((bf16[16,32,128]{2,1,0:T(8,128)(2,1)S(1)}, bf16[16,32,128]{2,1,0:T(8,128)(2,1)S(1)}, u32[]{:S(2)}, u32[]{:S(2)}) %collective-permute-start.31) | collective-permute-done | bytes 131104 | tf_op jit(solution)/shard_map/ppermute | solution.py:282
  43.9 8.3 %collective-permute-start.35 = (bf16[16,32,128]{2,1,0:T(8,128)(2,1)S(1)}, bf16[16,32,128]{2,1,0:T(8,128)(2,1)S(1)}, u32[]{:S(2)}, u32[]{:S(2)}) collective-permute-start(bf16[16,32,128]{2,1,0:T(8,128)(2,1)S(1)} %get-tuple-element.61), channel_id=1, source_target_pairs={{0,4},{1,5},{2,6},{3,7},{4,0},{5,1},{6,2},{7,3},{8,12},{9,13},{10,... | collective-permute-start | bytes 393224 | tf_op jit(solution)/shard_map/ppermute | solution.py:282
  52.2 3.3 %collective-permute-done.34.lower = bf16[16,32,128]{2,1,0:T(8,128)(2,1)S(1)} collective-permute-done((bf16[16,32,128]{2,1,0:T(8,128)(2,1)S(1)}, bf16[16,32,128]{2,1,0:T(8,128)(2,1)S(1)}, u32[]{:S(2)}, u32[]{:S(2)}) %collective-permute-start.34) | collective-permute-done | bytes 131104 | tf_op jit(solution)/shard_map/ppermute | solution.py:282
  55.5 1.4 %collective-permute-done.35.upper = bf16[16,32,128]{2,1,0:T(8,128)(2,1)S(1)} collective-permute-done((bf16[16,32,128]{2,1,0:T(8,128)(2,1)S(1)}, bf16[16,32,128]{2,1,0:T(8,128)(2,1)S(1)}, u32[]{:S(2)}, u32[]{:S(2)}) %collective-permute-start.35) | collective-permute-done | bytes 131104 | tf_op jit(solution)/shard_map/ppermute | solution.py:282
  56.9 0.6 project.5
  57.5 1.3 %collective-permute-start.38 = (bf16[16,32,128]{2,1,0:T(8,128)(2,1)S(1)}, bf16[16,32,128]{2,1,0:T(8,128)(2,1)S(1)}, u32[]{:S(2)}, u32[]{:S(2)}) collective-permute-start(bf16[16,32,128]{2,1,0:T(8,128)(2,1)S(1)} %get-tuple-element.62), channel_id=1, source_target_pairs={{0,4},{1,5},{2,6},{3,7},{4,2},{5,3},{6,0},{7,1},{8,12},{9,13},{10,... | collective-permute-start | bytes 393224 | tf_op jit(solution)/shard_map/ppermute | solution.py:282
  58.9 0.4 collective-permute-start.36
  59.5 2.0 %collective-permute-done.38.refs_5_ = bf16[16,32,128]{2,1,0:T(8,128)(2,1)S(1)} collective-permute-done((bf16[16,32,128]{2,1,0:T(8,128)(2,1)S(1)}, bf16[16,32,128]{2,1,0:T(8,128)(2,1)S(1)}, u32[]{:S(2)}, u32[]{:S(2)}) %collective-permute-start.38) | collective-permute-done | bytes 131104 | tf_op jit(solution)/shard_map/ppermute | solution.py:282
  61.5 3.0 %collective-permute-start.44 = (bf16[16,32,128]{2,1,0:T(8,128)(2,1)S(1)}, bf16[16,32,128]{2,1,0:T(8,128)(2,1)S(1)}, u32[]{:S(2)}, u32[]{:S(2)}) collective-permute-start(bf16[16,32,128]{2,1,0:T(8,128)(2,1)S(1)} %get-tuple-element.64), channel_id=1, source_target_pairs={{0,7},{1,6},{2,5},{3,4},{4,0},{5,1},{6,2},{7,3},{8,15},{9,14},{10,... | collective-permute-start | bytes 393224 | tf_op jit(solution)/shard_map/ppermute | solution.py:282
  64.5 1.2 %collective-permute-start.42 = (bf16[16,32,128]{2,1,0:T(8,128)(2,1)S(1)}, bf16[16,32,128]{2,1,0:T(8,128)(2,1)S(1)}, u32[]{:S(2)}, u32[]{:S(2)}) collective-permute-start(bf16[16,32,128]{2,1,0:T(8,128)(2,1)S(1)} %get-tuple-element.64), channel_id=1, source_target_pairs={{0,5},{1,4},{2,7},{3,6},{4,0},{5,1},{6,2},{7,3},{8,13},{9,12},{10,... | collective-permute-start | bytes 393224 | tf_op jit(solution)/shard_map/ppermute | solution.py:282
  65.8 0.5 collective-permute-start.45
  66.3 2.0 %collective-permute-done.44.refs_6_ = bf16[16,32,128]{2,1,0:T(8,128)(2,1)S(1)} collective-permute-done((bf16[16,32,128]{2,1,0:T(8,128)(2,1)S(1)}, bf16[16,32,128]{2,1,0:T(8,128)(2,1)S(1)}, u32[]{:S(2)}, u32[]{:S(2)}) %collective-permute-start.44) | collective-permute-done | bytes 131104 | tf_op jit(solution)/shard_map/ppermute | solution.py:282
  68.3 1.3 %collective-permute-done.43.refs_5_ = bf16[16,32,128]{2,1,0:T(8,128)(2,1)S(1)} collective-permute-done((bf16[16,32,128]{2,1,0:T(8,128)(2,1)S(1)}, bf16[16,32,128]{2,1,0:T(8,128)(2,1)S(1)}, u32[]{:S(2)}, u32[]{:S(2)}) %collective-permute-start.43) | collective-permute-done | bytes 131104 | tf_op jit(solution)/shard_map/ppermute | solution.py:282
  69.6 0.6 update.15.refs_1_
  70.2 0.8 %second.7 = bf16[4,8,4096]{2,1,0:T(8,128)(2,1)} custom-call(s32[3,80]{1,0:T(4,128)S(4)} %get-tuple-element.38.refs_0_.info, f32[32,32,128]{2,1,0:T(8,128)S(1)} %update.15.refs_1_, bf16[32,32,128]{2,1,0:T(8,128)(2,1)S(1)} %collective-permute-done.45.refs_2_, bf16[32,32,128]{2,1,0:T(8,128)(2,1)S(1)} %get-tuple-element.65.refs_3_, ...), custom_call_target="tpu_custom_call" | custom-call | tf_op jit(solution)/shard_map/second/pallas_call | solution.py:303
  (67 shorter events, 3.5 us)
Async XLA Ops:
  0.0 8.2 %collective-permute-start.1 = (bf16[1,1,80,128,128]{4,3,2,1,0:T(8,128)(2,1)}, bf16[1,1,80,128,128]{4,3,2,1,0:T(8,128)(2,1)S(1)}, u32[]{:S(2)}, u32[]{:S(2)}) collective-permute-start(bf16[1,1,80,128,128]{4,3,2,1,0:T(8,128)(2,1)} %blocks_in.1), channel_id=1, source_target_pairs={{0,4},{1,5},{2,6},{3,7},{4,0},{5,1},{6,2},{7,3},{8,12},{9,13},{10,... | collective-permute-start | bytes 7864328 | tf_op jit(solution)/shard_map/ppermute | solution.py:282
  3.9 5.7 %collective-permute-start.4 = (bf16[5,32,128]{2,1,0:T(8,128)(2,1)S(1)}, bf16[5,32,128]{2,1,0:T(8,128)(2,1)S(1)}, u32[]{:S(2)}, u32[]{:S(2)}) collective-permute-start(bf16[5,32,128]{2,1,0:T(8,128)(2,1)S(1)} %get-tuple-element.40._.refs_2_), channel_id=1, source_target_pairs={{0,3},{1,2},{2,1},{3,0},{4,7},{5,6},{6,5},{7,4},{8,11},{9,10},{10,... | collective-permute-start | bytes 122888 | tf_op jit(solution)/shard_map/ppermute | solution.py:282
  6.1 3.5 %collective-permute-start.3 = (bf16[5,32,128]{2,1,0:T(8,128)(2,1)S(1)}, bf16[5,32,128]{2,1,0:T(8,128)(2,1)S(1)}, u32[]{:S(2)}, u32[]{:S(2)}) collective-permute-start(bf16[5,32,128]{2,1,0:T(8,128)(2,1)S(1)} %get-tuple-element.40._.refs_2_), channel_id=1, source_target_pairs={{0,2},{1,3},{2,0},{3,1},{4,6},{5,7},{6,4},{7,5},{8,10},{9,11},{10,... | collective-permute-start | bytes 122888 | tf_op jit(solution)/shard_map/ppermute | solution.py:282
  6.3 3.3 %collective-permute-start.2 = (bf16[5,32,128]{2,1,0:T(8,128)(2,1)S(1)}, bf16[5,32,128]{2,1,0:T(8,128)(2,1)S(1)}, u32[]{:S(2)}, u32[]{:S(2)}) collective-permute-start(bf16[5,32,128]{2,1,0:T(8,128)(2,1)S(1)} %get-tuple-element.40._.refs_2_), channel_id=1, source_target_pairs={{0,1},{1,0},{2,3},{3,2},{4,5},{5,4},{6,7},{7,6},{8,9},{9,8},{10,11... | collective-permute-start | bytes 122888 | tf_op jit(solution)/shard_map/ppermute | solution.py:282
  6.6 1.7 %collective-permute-start = (s32[2,80]{1,0:T(2,128)S(1)}, s32[2,80]{1,0:T(2,128)S(1)}, u32[]{:S(2)}, u32[]{:S(2)}) collective-permute-start(s32[2,80]{1,0:T(2,128)S(1)} %get-tuple-element.37), channel_id=1, source_target_pairs={{0,4},{1,5},{2,6},{3,7},{4,0},{5,1},{6,2},{7,3},{8,12},{9,13},{10,... | collective-permute-start | bytes 1928 | tf_op jit(solution)/shard_map/ppermute | solution.py:282
  9.7 5.4 %collective-permute-start.8 = (bf16[16,32,128]{2,1,0:T(8,128)(2,1)S(1)}, bf16[16,32,128]{2,1,0:T(8,128)(2,1)S(1)}, u32[]{:S(2)}, u32[]{:S(2)}) collective-permute-start(bf16[16,32,128]{2,1,0:T(8,128)(2,1)S(1)} %get-tuple-element.44), channel_id=1, source_target_pairs={{0,7},{1,6},{2,5},{3,4},{4,0},{5,1},{6,2},{7,3},{8,15},{9,14},{10,... | collective-permute-start | bytes 393224 | tf_op jit(solution)/shard_map/ppermute | solution.py:282
  11.0 5.4 %collective-permute-start.7 = (bf16[16,32,128]{2,1,0:T(8,128)(2,1)S(1)}, bf16[16,32,128]{2,1,0:T(8,128)(2,1)S(1)}, u32[]{:S(2)}, u32[]{:S(2)}) collective-permute-start(bf16[16,32,128]{2,1,0:T(8,128)(2,1)S(1)} %get-tuple-element.44), channel_id=1, source_target_pairs={{0,6},{1,7},{2,4},{3,5},{4,0},{5,1},{6,2},{7,3},{8,14},{9,15},{10,... | collective-permute-start | bytes 393224 | tf_op jit(solution)/shard_map/ppermute | solution.py:282
  12.3 4.4 %collective-permute-start.6 = (bf16[16,32,128]{2,1,0:T(8,128)(2,1)S(1)}, bf16[16,32,128]{2,1,0:T(8,128)(2,1)S(1)}, u32[]{:S(2)}, u32[]{:S(2)}) collective-permute-start(bf16[16,32,128]{2,1,0:T(8,128)(2,1)S(1)} %get-tuple-element.44), channel_id=1, source_target_pairs={{0,5},{1,4},{2,7},{3,6},{4,0},{5,1},{6,2},{7,3},{8,13},{9,12},{10,... | collective-permute-start | bytes 393224 | tf_op jit(solution)/shard_map/ppermute | solution.py:282
  12.6 4.1 %collective-permute-start.5 = (bf16[16,32,128]{2,1,0:T(8,128)(2,1)S(1)}, bf16[16,32,128]{2,1,0:T(8,128)(2,1)S(1)}, u32[]{:S(2)}, u32[]{:S(2)}) collective-permute-start(bf16[16,32,128]{2,1,0:T(8,128)(2,1)S(1)} %get-tuple-element.44), channel_id=1, source_target_pairs={{0,4},{1,5},{2,6},{3,7},{4,0},{5,1},{6,2},{7,3},{8,12},{9,13},{10,... | collective-permute-start | bytes 393224 | tf_op jit(solution)/shard_map/ppermute | solution.py:282
  12.9 3.7 %collective-permute-start.9 = (bf16[32,32,128]{2,1,0:T(8,128)(2,1)S(1)}, bf16[32,32,128]{2,1,0:T(8,128)(2,1)S(1)}, u32[]{:S(2)}, u32[]{:S(2)}) collective-permute-start(bf16[32,32,128]{2,1,0:T(8,128)(2,1)S(1)} %get-tuple-element.45.refs_3_), channel_id=1, source_target_pairs={{0,4},{1,5},{2,6},{3,7},{4,0},{5,1},{6,2},{7,3},{8,12},{9,13},{10,... | collective-permute-start | bytes 786440 | tf_op jit(solution)/shard_map/ppermute | solution.py:282
  16.7 1.4 %collective-permute-start.10 = (bf16[16,32,128]{2,1,0:T(8,128)(2,1)S(1)}, bf16[16,32,128]{2,1,0:T(8,128)(2,1)S(1)}, u32[]{:S(2)}, u32[]{:S(2)}) collective-permute-start(bf16[16,32,128]{2,1,0:T(8,128)(2,1)S(1)} %get-tuple-element.46), channel_id=1, source_target_pairs={{0,4},{1,5},{2,6},{3,7},{4,12},{5,13},{6,14},{7,15},{8,0},{9,1},{1... | collective-permute-start | bytes 393224 | tf_op jit(solution)/shard_map/ppermute | solution.py:282
  16.8 1.5 %collective-permute-start.11 = (bf16[16,32,128]{2,1,0:T(8,128)(2,1)S(1)}, bf16[16,32,128]{2,1,0:T(8,128)(2,1)S(1)}, u32[]{:S(2)}, u32[]{:S(2)}) collective-permute-start(bf16[16,32,128]{2,1,0:T(8,128)(2,1)S(1)} %get-tuple-element.47), channel_id=1, source_target_pairs={{0,4},{1,5},{2,6},{3,7},{4,12},{5,13},{6,14},{7,15},{8,0},{9,1},{1... | collective-permute-start | bytes 393224 | tf_op jit(solution)/shard_map/ppermute | solution.py:282
  18.3 3.5 %collective-permute-start.15 = (bf16[16,32,128]{2,1,0:T(8,128)(2,1)S(1)}, bf16[16,32,128]{2,1,0:T(8,128)(2,1)S(1)}, u32[]{:S(2)}, u32[]{:S(2)}) collective-permute-start(bf16[16,32,128]{2,1,0:T(8,128)(2,1)S(1)} %get-tuple-element.48), channel_id=1, source_target_pairs={{0,4},{1,5},{2,6},{3,7},{4,3},{5,2},{6,1},{7,0},{8,12},{9,13},{10,... | collective-permute-start | bytes 393224 | tf_op jit(solution)/shard_map/ppermute | solution.py:282
  19.8 3.3 %collective-permute-start.14 = (bf16[16,32,128]{2,1,0:T(8,128)(2,1)S(1)}, bf16[16,32,128]{2,1,0:T(8,128)(2,1)S(1)}, u32[]{:S(2)}, u32[]{:S(2)}) collective-permute-start(bf16[16,32,128]{2,1,0:T(8,128)(2,1)S(1)} %get-tuple-element.48), channel_id=1, source_target_pairs={{0,4},{1,5},{2,6},{3,7},{4,2},{5,3},{6,0},{7,1},{8,12},{9,13},{10,... | collective-permute-start | bytes 393224 | tf_op jit(solution)/shard_map/ppermute | solution.py:282
  19.9 3.4 %collective-permute-start.13 = (bf16[16,32,128]{2,1,0:T(8,128)(2,1)S(1)}, bf16[16,32,128]{2,1,0:T(8,128)(2,1)S(1)}, u32[]{:S(2)}, u32[]{:S(2)}) collective-permute-start(bf16[16,32,128]{2,1,0:T(8,128)(2,1)S(1)} %get-tuple-element.48), channel_id=1, source_target_pairs={{0,4},{1,5},{2,6},{3,7},{4,1},{5,0},{6,3},{7,2},{8,12},{9,13},{10,... | collective-permute-start | bytes 393224 | tf_op jit(solution)/shard_map/ppermute | solution.py:282
  21.1 2.1 %collective-permute-start.12 = (bf16[16,32,128]{2,1,0:T(8,128)(2,1)S(1)}, bf16[16,32,128]{2,1,0:T(8,128)(2,1)S(1)}, u32[]{:S(2)}, u32[]{:S(2)}) collective-permute-start(bf16[16,32,128]{2,1,0:T(8,128)(2,1)S(1)} %get-tuple-element.48), channel_id=1, source_target_pairs={{0,4},{1,5},{2,6},{3,7},{4,0},{5,1},{6,2},{7,3},{8,12},{9,13},{10,... | collective-permute-start | bytes 393224 | tf_op jit(solution)/shard_map/ppermute | solution.py:282
  21.1 2.1 %collective-permute-start.16 = (bf16[32,32,128]{2,1,0:T(8,128)(2,1)S(1)}, bf16[32,32,128]{2,1,0:T(8,128)(2,1)S(1)}, u32[]{:S(2)}, u32[]{:S(2)}) collective-permute-start(bf16[32,32,128]{2,1,0:T(8,128)(2,1)S(1)} %get-tuple-element.49), channel_id=1, source_target_pairs={{0,4},{1,5},{2,6},{3,7},{4,0},{5,1},{6,2},{7,3},{8,12},{9,13},{10,... | collective-permute-start | bytes 786440 | tf_op jit(solution)/shard_map/ppermute | solution.py:282
  23.2 5.9 %collective-permute-start.20 = (bf16[16,32,128]{2,1,0:T(8,128)(2,1)S(1)}, bf16[16,32,128]{2,1,0:T(8,128)(2,1)S(1)}, u32[]{:S(2)}, u32[]{:S(2)}) collective-permute-start(bf16[16,32,128]{2,1,0:T(8,128)(2,1)S(1)} %get-tuple-element.50), channel_id=1, source_target_pairs={{0,7},{1,6},{2,5},{3,4},{4,0},{5,1},{6,2},{7,3},{8,15},{9,14},{10,... | collective-permute-start | bytes 393224 | tf_op jit(solution)/shard_map/ppermute | solution.py:282
  25.3 5.2 %collective-permute-start.19 = (bf16[16,32,128]{2,1,0:T(8,128)(2,1)S(1)}, bf16[16,32,128]{2,1,0:T(8,128)(2,1)S(1)}, u32[]{:S(2)}, u32[]{:S(2)}) collective-permute-start(bf16[16,32,128]{2,1,0:T(8,128)(2,1)S(1)} %get-tuple-element.50), channel_id=1, source_target_pairs={{0,6},{1,7},{2,4},{3,5},{4,0},{5,1},{6,2},{7,3},{8,14},{9,15},{10,... | collective-permute-start | bytes 393224 | tf_op jit(solution)/shard_map/ppermute | solution.py:282
  25.3 5.1 %collective-permute-start.18 = (bf16[16,32,128]{2,1,0:T(8,128)(2,1)S(1)}, bf16[16,32,128]{2,1,0:T(8,128)(2,1)S(1)}, u32[]{:S(2)}, u32[]{:S(2)}) collective-permute-start(bf16[16,32,128]{2,1,0:T(8,128)(2,1)S(1)} %get-tuple-element.50), channel_id=1, source_target_pairs={{0,5},{1,4},{2,7},{3,6},{4,0},{5,1},{6,2},{7,3},{8,13},{9,12},{10,... | collective-permute-start | bytes 393224 | tf_op jit(solution)/shard_map/ppermute | solution.py:282
  26.2 4.2 %collective-permute-start.17 = (bf16[16,32,128]{2,1,0:T(8,128)(2,1)S(1)}, bf16[16,32,128]{2,1,0:T(8,128)(2,1)S(1)}, u32[]{:S(2)}, u32[]{:S(2)}) collective-permute-start(bf16[16,32,128]{2,1,0:T(8,128)(2,1)S(1)} %get-tuple-element.50), channel_id=1, source_target_pairs={{0,4},{1,5},{2,6},{3,7},{4,0},{5,1},{6,2},{7,3},{8,12},{9,13},{10,... | collective-permute-start | bytes 393224 | tf_op jit(solution)/shard_map/ppermute | solution.py:282
  26.3 4.1 %collective-permute-start.21 = (bf16[32,32,128]{2,1,0:T(8,128)(2,1)S(1)}, bf16[32,32,128]{2,1,0:T(8,128)(2,1)S(1)}, u32[]{:S(2)}, u32[]{:S(2)}) collective-permute-start(bf16[32,32,128]{2,1,0:T(8,128)(2,1)S(1)} %get-tuple-element.51.refs_3_), channel_id=1, source_target_pairs={{0,4},{1,5},{2,6},{3,7},{4,0},{5,1},{6,2},{7,3},{8,12},{9,13},{10,... | collective-permute-start | bytes 786440 | tf_op jit(solution)/shard_map/ppermute | solution.py:282
  30.5 1.4 %collective-permute-start.22 = (bf16[16,32,128]{2,1,0:T(8,128)(2,1)S(1)}, bf16[16,32,128]{2,1,0:T(8,128)(2,1)S(1)}, u32[]{:S(2)}, u32[]{:S(2)}) collective-permute-start(bf16[16,32,128]{2,1,0:T(8,128)(2,1)S(1)} %get-tuple-element.53), channel_id=1, source_target_pairs={{0,4},{1,5},{2,6},{3,7},{4,0},{5,1},{6,2},{7,3},{8,12},{9,13},{10,... | collective-permute-start | bytes 393224 | tf_op jit(solution)/shard_map/ppermute | solution.py:282
  30.6 1.5 %collective-permute-start.23 = (bf16[16,32,128]{2,1,0:T(8,128)(2,1)S(1)}, bf16[16,32,128]{2,1,0:T(8,128)(2,1)S(1)}, u32[]{:S(2)}, u32[]{:S(2)}) collective-permute-start(bf16[16,32,128]{2,1,0:T(8,128)(2,1)S(1)} %get-tuple-element.54), channel_id=1, source_target_pairs={{0,4},{1,5},{2,6},{3,7},{4,0},{5,1},{6,2},{7,3},{8,12},{9,13},{10,... | collective-permute-start | bytes 393224 | tf_op jit(solution)/shard_map/ppermute | solution.py:282
  32.1 3.3 %collective-permute-start.27 = (bf16[16,32,128]{2,1,0:T(8,128)(2,1)S(1)}, bf16[16,32,128]{2,1,0:T(8,128)(2,1)S(1)}, u32[]{:S(2)}, u32[]{:S(2)}) collective-permute-start(bf16[16,32,128]{2,1,0:T(8,128)(2,1)S(1)} %get-tuple-element.55), channel_id=1, source_target_pairs={{0,4},{1,5},{2,6},{3,7},{4,3},{5,2},{6,1},{7,0},{8,12},{9,13},{10,... | collective-permute-start | bytes 393224 | tf_op jit(solution)/shard_map/ppermute | solution.py:282
  33.5 3.3 %collective-permute-start.26 = (bf16[16,32,128]{2,1,0:T(8,128)(2,1)S(1)}, bf16[16,32,128]{2,1,0:T(8,128)(2,1)S(1)}, u32[]{:S(2)}, u32[]{:S(2)}) collective-permute-start(bf16[16,32,128]{2,1,0:T(8,128)(2,1)S(1)} %get-tuple-element.55), channel_id=1, source_target_pairs={{0,4},{1,5},{2,6},{3,7},{4,2},{5,3},{6,0},{7,1},{8,12},{9,13},{10,... | collective-permute-start | bytes 393224 | tf_op jit(solution)/shard_map/ppermute | solution.py:282
  33.5 3.4 %collective-permute-start.25 = (bf16[16,32,128]{2,1,0:T(8,128)(2,1)S(1)}, bf16[16,32,128]{2,1,0:T(8,128)(2,1)S(1)}, u32[]{:S(2)}, u32[]{:S(2)}) collective-permute-start(bf16[16,32,128]{2,1,0:T(8,128)(2,1)S(1)} %get-tuple-element.55), channel_id=1, source_target_pairs={{0,4},{1,5},{2,6},{3,7},{4,1},{5,0},{6,3},{7,2},{8,12},{9,13},{10,... | collective-permute-start | bytes 393224 | tf_op jit(solution)/shard_map/ppermute | solution.py:282
  34.5 2.4 %collective-permute-start.24 = (bf16[16,32,128]{2,1,0:T(8,128)(2,1)S(1)}, bf16[16,32,128]{2,1,0:T(8,128)(2,1)S(1)}, u32[]{:S(2)}, u32[]{:S(2)}) collective-permute-start(bf16[16,32,128]{2,1,0:T(8,128)(2,1)S(1)} %get-tuple-element.55), channel_id=1, source_target_pairs={{0,4},{1,5},{2,6},{3,7},{4,0},{5,1},{6,2},{7,3},{8,12},{9,13},{10,... | collective-permute-start | bytes 393224 | tf_op jit(solution)/shard_map/ppermute | solution.py:282
  34.5 2.4 %collective-permute-start.28 = (bf16[32,32,128]{2,1,0:T(8,128)(2,1)S(1)}, bf16[32,32,128]{2,1,0:T(8,128)(2,1)S(1)}, u32[]{:S(2)}, u32[]{:S(2)}) collective-permute-start(bf16[32,32,128]{2,1,0:T(8,128)(2,1)S(1)} %get-tuple-element.56), channel_id=1, source_target_pairs={{0,4},{1,5},{2,6},{3,7},{4,0},{5,1},{6,2},{7,3},{8,12},{9,13},{10,... | collective-permute-start | bytes 786440 | tf_op jit(solution)/shard_map/ppermute | solution.py:282
  36.9 5.6 %collective-permute-start.32 = (bf16[16,32,128]{2,1,0:T(8,128)(2,1)S(1)}, bf16[16,32,128]{2,1,0:T(8,128)(2,1)S(1)}, u32[]{:S(2)}, u32[]{:S(2)}) collective-permute-start(bf16[16,32,128]{2,1,0:T(8,128)(2,1)S(1)} %get-tuple-element.57), channel_id=1, source_target_pairs={{0,7},{1,6},{2,5},{3,4},{4,0},{5,1},{6,2},{7,3},{8,15},{9,14},{10,... | collective-permute-start | bytes 393224 | tf_op jit(solution)/shard_map/ppermute | solution.py:282
  38.7 5.1 %collective-permute-start.31 = (bf16[16,32,128]{2,1,0:T(8,128)(2,1)S(1)}, bf16[16,32,128]{2,1,0:T(8,128)(2,1)S(1)}, u32[]{:S(2)}, u32[]{:S(2)}) collective-permute-start(bf16[16,32,128]{2,1,0:T(8,128)(2,1)S(1)} %get-tuple-element.57), channel_id=1, source_target_pairs={{0,6},{1,7},{2,4},{3,5},{4,0},{5,1},{6,2},{7,3},{8,14},{9,15},{10,... | collective-permute-start | bytes 393224 | tf_op jit(solution)/shard_map/ppermute | solution.py:282
  38.7 5.0 %collective-permute-start.30 = (bf16[16,32,128]{2,1,0:T(8,128)(2,1)S(1)}, bf16[16,32,128]{2,1,0:T(8,128)(2,1)S(1)}, u32[]{:S(2)}, u32[]{:S(2)}) collective-permute-start(bf16[16,32,128]{2,1,0:T(8,128)(2,1)S(1)} %get-tuple-element.57), channel_id=1, source_target_pairs={{0,5},{1,4},{2,7},{3,6},{4,0},{5,1},{6,2},{7,3},{8,13},{9,12},{10,... | collective-permute-start | bytes 393224 | tf_op jit(solution)/shard_map/ppermute | solution.py:282
  39.9 3.8 %collective-permute-start.29 = (bf16[16,32,128]{2,1,0:T(8,128)(2,1)S(1)}, bf16[16,32,128]{2,1,0:T(8,128)(2,1)S(1)}, u32[]{:S(2)}, u32[]{:S(2)}) collective-permute-start(bf16[16,32,128]{2,1,0:T(8,128)(2,1)S(1)} %get-tuple-element.57), channel_id=1, source_target_pairs={{0,4},{1,5},{2,6},{3,7},{4,0},{5,1},{6,2},{7,3},{8,12},{9,13},{10,... | collective-permute-start | bytes 393224 | tf_op jit(solution)/shard_map/ppermute | solution.py:282
  40.0 3.8 %collective-permute-start.33 = (bf16[32,32,128]{2,1,0:T(8,128)(2,1)S(1)}, bf16[32,32,128]{2,1,0:T(8,128)(2,1)S(1)}, u32[]{:S(2)}, u32[]{:S(2)}) collective-permute-start(bf16[32,32,128]{2,1,0:T(8,128)(2,1)S(1)} %get-tuple-element.58.refs_3_), channel_id=1, source_target_pairs={{0,4},{1,5},{2,6},{3,7},{4,0},{5,1},{6,2},{7,3},{8,12},{9,13},{10,... | collective-permute-start | bytes 786440 | tf_op jit(solution)/shard_map/ppermute | solution.py:282
  43.8 11.7 %collective-permute-start.34 = (bf16[16,32,128]{2,1,0:T(8,128)(2,1)S(1)}, bf16[16,32,128]{2,1,0:T(8,128)(2,1)S(1)}, u32[]{:S(2)}, u32[]{:S(2)}) collective-permute-start(bf16[16,32,128]{2,1,0:T(8,128)(2,1)S(1)} %get-tuple-element.60), channel_id=1, source_target_pairs={{0,4},{1,5},{2,6},{3,7},{4,0},{5,1},{6,2},{7,3},{8,12},{9,13},{10,... | collective-permute-start | bytes 393224 | tf_op jit(solution)/shard_map/ppermute | solution.py:282
  43.9 13.0 %collective-permute-start.35 = (bf16[16,32,128]{2,1,0:T(8,128)(2,1)S(1)}, bf16[16,32,128]{2,1,0:T(8,128)(2,1)S(1)}, u32[]{:S(2)}, u32[]{:S(2)}) collective-permute-start(bf16[16,32,128]{2,1,0:T(8,128)(2,1)S(1)} %get-tuple-element.61), channel_id=1, source_target_pairs={{0,4},{1,5},{2,6},{3,7},{4,0},{5,1},{6,2},{7,3},{8,12},{9,13},{10,... | collective-permute-start | bytes 393224 | tf_op jit(solution)/shard_map/ppermute | solution.py:282
  57.5 2.0 %collective-permute-start.39 = (bf16[16,32,128]{2,1,0:T(8,128)(2,1)S(1)}, bf16[16,32,128]{2,1,0:T(8,128)(2,1)S(1)}, u32[]{:S(2)}, u32[]{:S(2)}) collective-permute-start(bf16[16,32,128]{2,1,0:T(8,128)(2,1)S(1)} %get-tuple-element.62), channel_id=1, source_target_pairs={{0,4},{1,5},{2,6},{3,7},{4,3},{5,2},{6,1},{7,0},{8,12},{9,13},{10,... | collective-permute-start | bytes 393224 | tf_op jit(solution)/shard_map/ppermute | solution.py:282
  57.5 3.9 %collective-permute-start.38 = (bf16[16,32,128]{2,1,0:T(8,128)(2,1)S(1)}, bf16[16,32,128]{2,1,0:T(8,128)(2,1)S(1)}, u32[]{:S(2)}, u32[]{:S(2)}) collective-permute-start(bf16[16,32,128]{2,1,0:T(8,128)(2,1)S(1)} %get-tuple-element.62), channel_id=1, source_target_pairs={{0,4},{1,5},{2,6},{3,7},{4,2},{5,3},{6,0},{7,1},{8,12},{9,13},{10,... | collective-permute-start | bytes 393224 | tf_op jit(solution)/shard_map/ppermute | solution.py:282
  58.8 2.7 %collective-permute-start.37 = (bf16[16,32,128]{2,1,0:T(8,128)(2,1)S(1)}, bf16[16,32,128]{2,1,0:T(8,128)(2,1)S(1)}, u32[]{:S(2)}, u32[]{:S(2)}) collective-permute-start(bf16[16,32,128]{2,1,0:T(8,128)(2,1)S(1)} %get-tuple-element.62), channel_id=1, source_target_pairs={{0,4},{1,5},{2,6},{3,7},{4,1},{5,0},{6,3},{7,2},{8,12},{9,13},{10,... | collective-permute-start | bytes 393224 | tf_op jit(solution)/shard_map/ppermute | solution.py:282
  58.9 2.6 %collective-permute-start.36 = (bf16[16,32,128]{2,1,0:T(8,128)(2,1)S(1)}, bf16[16,32,128]{2,1,0:T(8,128)(2,1)S(1)}, u32[]{:S(2)}, u32[]{:S(2)}) collective-permute-start(bf16[16,32,128]{2,1,0:T(8,128)(2,1)S(1)} %get-tuple-element.62), channel_id=1, source_target_pairs={{0,4},{1,5},{2,6},{3,7},{4,0},{5,1},{6,2},{7,3},{8,12},{9,13},{10,... | collective-permute-start | bytes 393224 | tf_op jit(solution)/shard_map/ppermute | solution.py:282
  59.3 2.1 %collective-permute-start.40 = (bf16[32,32,128]{2,1,0:T(8,128)(2,1)S(1)}, bf16[32,32,128]{2,1,0:T(8,128)(2,1)S(1)}, u32[]{:S(2)}, u32[]{:S(2)}) collective-permute-start(bf16[32,32,128]{2,1,0:T(8,128)(2,1)S(1)} %get-tuple-element.63), channel_id=1, source_target_pairs={{0,4},{1,5},{2,6},{3,7},{4,0},{5,1},{6,2},{7,3},{8,12},{9,13},{10,... | collective-permute-start | bytes 786440 | tf_op jit(solution)/shard_map/ppermute | solution.py:282
  61.5 6.8 %collective-permute-start.44 = (bf16[16,32,128]{2,1,0:T(8,128)(2,1)S(1)}, bf16[16,32,128]{2,1,0:T(8,128)(2,1)S(1)}, u32[]{:S(2)}, u32[]{:S(2)}) collective-permute-start(bf16[16,32,128]{2,1,0:T(8,128)(2,1)S(1)} %get-tuple-element.64), channel_id=1, source_target_pairs={{0,7},{1,6},{2,5},{3,4},{4,0},{5,1},{6,2},{7,3},{8,15},{9,14},{10,... | collective-permute-start | bytes 393224 | tf_op jit(solution)/shard_map/ppermute | solution.py:282
  64.5 5.1 %collective-permute-start.43 = (bf16[16,32,128]{2,1,0:T(8,128)(2,1)S(1)}, bf16[16,32,128]{2,1,0:T(8,128)(2,1)S(1)}, u32[]{:S(2)}, u32[]{:S(2)}) collective-permute-start(bf16[16,32,128]{2,1,0:T(8,128)(2,1)S(1)} %get-tuple-element.64), channel_id=1, source_target_pairs={{0,6},{1,7},{2,4},{3,5},{4,0},{5,1},{6,2},{7,3},{8,14},{9,15},{10,... | collective-permute-start | bytes 393224 | tf_op jit(solution)/shard_map/ppermute | solution.py:282
  64.5 5.1 %collective-permute-start.42 = (bf16[16,32,128]{2,1,0:T(8,128)(2,1)S(1)}, bf16[16,32,128]{2,1,0:T(8,128)(2,1)S(1)}, u32[]{:S(2)}, u32[]{:S(2)}) collective-permute-start(bf16[16,32,128]{2,1,0:T(8,128)(2,1)S(1)} %get-tuple-element.64), channel_id=1, source_target_pairs={{0,5},{1,4},{2,7},{3,6},{4,0},{5,1},{6,2},{7,3},{8,13},{9,12},{10,... | collective-permute-start | bytes 393224 | tf_op jit(solution)/shard_map/ppermute | solution.py:282
  65.8 3.8 %collective-permute-start.41 = (bf16[16,32,128]{2,1,0:T(8,128)(2,1)S(1)}, bf16[16,32,128]{2,1,0:T(8,128)(2,1)S(1)}, u32[]{:S(2)}, u32[]{:S(2)}) collective-permute-start(bf16[16,32,128]{2,1,0:T(8,128)(2,1)S(1)} %get-tuple-element.64), channel_id=1, source_target_pairs={{0,4},{1,5},{2,6},{3,7},{4,0},{5,1},{6,2},{7,3},{8,12},{9,13},{10,... | collective-permute-start | bytes 393224 | tf_op jit(solution)/shard_map/ppermute | solution.py:282
  65.8 4.4 %collective-permute-start.45 = (bf16[32,32,128]{2,1,0:T(8,128)(2,1)S(1)}, bf16[32,32,128]{2,1,0:T(8,128)(2,1)S(1)}, u32[]{:S(2)}, u32[]{:S(2)}) collective-permute-start(bf16[32,32,128]{2,1,0:T(8,128)(2,1)S(1)} %get-tuple-element.65.refs_3_), channel_id=1, source_target_pairs={{0,4},{1,5},{2,6},{3,7},{4,0},{5,1},{6,2},{7,3},{8,12},{9,13},{10,... | collective-permute-start | bytes 786440 | tf_op jit(solution)/shard_map/ppermute | solution.py:282

commit v20 on v14

--- a/solution.py
+++ b/solution.py
@@ -131,14 +131,22 @@
         rays[row_blocks, r : r + 1] = row
 
 
-def weights(rays, terms, w_scr):
-    row_blocks = w_scr.shape[0]
-    for r in range(row_blocks):
-        left = rays[r]
+def rest_of(rays, left, terms, out):
+    row_blocks = out.shape[0]
+    for r in range(row_blocks):
+        rest = left[r]
         if terms:
             total = sum(ref[r].astype(jnp.float32) for ref in terms)
-            left = left - total * rays[row_blocks, r : r + 1]
-        w_scr[r] = left.astype(jnp.bfloat16)
+            rest = rest - total * rays[row_blocks, r : r + 1]
+        out[r] = rest.astype(out.dtype)
+
+
+def early_kernel(place, core, info, rays, *refs):
+    terms, left = refs[:-1], refs[-1]
+
+    @pl.when(on_core(info, place, core))
+    def _():
+        rest_of(rays, rays, terms, left)
 
 
 def back_project(info, wide, w_scr, image):
@@ -183,14 +191,15 @@
         notes, terms_in = take(refs, n_notes), []
         change, rays, w_scr, rays_scr = refs
         gather_rays(info, notes, rays, rays_scr)
+        left = rays
     else:
-        (rays,) = take(refs, 1)
+        rays, left = take(refs, 2)
         terms_in = take(refs, n_terms)
         change, w_scr = refs
 
     @pl.when(on_core(info, place, core))
     def _():
-        weights(rays, terms_in, w_scr)
+        rest_of(rays, left, terms_in, w_scr)
         change[...] = jnp.zeros_like(change)
         back_project(info, wide, w_scr, change)
 
@@ -368,13 +377,25 @@
 
     held = []
     image, rays = None, None
+    left_out = jax.ShapeDtypeStruct((row_blocks, slices, BS), jnp.float32)
     change_out = jax.ShapeDtypeStruct(image_shape, jnp.float32)
 
     def updated(place, core, terms):
+        left = rays
+        if len(terms) > 2:
+            left = call(
+                functools.partial(early_kernel, place, core),
+                1,
+                [info, rays] + terms[1::2],
+                left_out,
+                [],
+                "early",
+            )
+            terms = terms[0::2]
         return call(
             functools.partial(update_kernel, place, core, 0, len(terms)),
             1,
-            [info, wide, rays] + terms,
+            [info, wide, rays, left] + terms,
             change_out,
             [w_scr],
             "update",

time: 71.1 us -> 71 us (level)
    pallas_call x19 -> x26, Pallas kernels: 2.33 us -> 2.18 us  [call(): pl.pallas_call(kernel, out_shape=out_shape, in_specs=[SMEM] * smem + [VME...]
  transfers between devices with their start and end apart: 43 -> 43, of which waited for: 18 -> 24; matrix products, arithmetic and copies ran while one was open for 0% -> 0% of each run, Pallas kernels for 8% -> 8%
where the time goes in v20:
time: 71 us; the launch traced here: 70.8 us
  waiting for transfers between devices  36.1 us (51%)
  starting transfers between devices  27.3 us (38%)
  Pallas kernels  7.06 us (10%)
    ppermute x43, waiting for transfers between devices, sent(): return lax.ppermute(value, ('subset', 'tile'), pairs)  36.1 us
    ppermute x43, starting transfers between devices, sent(): return lax.ppermute(value, ('subset', 'tile'), pairs)  27.3 us
    pallas_call x1, Pallas kernels, per_device(): pl.pallas_call(functools.partial(head_kernel, row_blocks, chunks), out_sh...  3.09 us
    pallas_call x26, Pallas kernels, call(): pl.pallas_call(kernel, out_shape=out_shape, in_specs=[SMEM] * smem + [VME...  2.18 us
  transfers between devices with their start and end apart: 43, of which 24 were waited for; matrix products, arithmetic and copies ran while one was open for 0% of the time, Pallas kernels for 8%

profile of v20, /device:TPU:25, one launch (start us, length us, event | category | flops | bytes accessed | tf_op | source)
XLA Modules:
  0.0 70.8 jit_solution(17957845573570924140)
XLA Ops:
  0.0 0.7 collective-permute-start.1
  0.8 3.1 %head.1 = (bf16[5,32,128]{2,1,0:T(8,128)(2,1)S(1)}, s32[2,80]{1,0:T(2,128)S(1)}, s32[3,80]{1,0:T(4,128)S(4)}, bf16[1,1,80,128,128]{4,3,2,1,0:T(8,128)(2,1)S(1)}) custom-call(s32[3]{0:T(128)S(1)} %pad_add_fusion.pos, s32[1,1,80]{2,1,0:T(1,128)} %rows_in.1, s32[1,1,80]{2,1,0:T(1,128)} %cols_in.1, bf16[1,1,80,128,128]{4,3,2,1,0:T(8,128)(2,1)} %blocks_in.1, ...), custom_call_target="tpu_custom_call" | custom-call | tf_op jit(solution)/shard_map/head/pallas_call | solution.py:324
  3.9 2.2 %collective-permute-start.4 = (bf16[5,32,128]{2,1,0:T(8,128)(2,1)S(1)}, bf16[5,32,128]{2,1,0:T(8,128)(2,1)S(1)}, u32[]{:S(2)}, u32[]{:S(2)}) collective-permute-start(bf16[5,32,128]{2,1,0:T(8,128)(2,1)S(1)} %get-tuple-element.31._.refs_2_), channel_id=1, source_target_pairs={{0,3},{1,2},{2,1},{3,0},{4,7},{5,6},{6,5},{7,4},{8,11},{9,10},{10,... | collective-permute-start | bytes 122888 | tf_op jit(solution)/shard_map/ppermute | solution.py:288
  6.6 0.8 %collective-permute-start = (s32[2,80]{1,0:T(2,128)S(1)}, s32[2,80]{1,0:T(2,128)S(1)}, u32[]{:S(2)}, u32[]{:S(2)}) collective-permute-start(s32[2,80]{1,0:T(2,128)S(1)} %get-tuple-element.28), channel_id=1, source_target_pairs={{0,4},{1,5},{2,6},{3,7},{4,0},{5,1},{6,2},{7,3},{8,12},{9,13},{10,... | collective-permute-start | bytes 1928 | tf_op jit(solution)/shard_map/ppermute | solution.py:288
  7.4 0.5 pack_own.1.refs_1_
  7.9 0.3 collective-permute-done.table2
  8.2 1.3 %pack_other.1 = (s32[3,80]{1,0:T(4,128)S(4)}, bf16[16,640,128]{2,1,0:T(8,128)(2,1)S(1)}) custom-call(s32[3,80]{1,0:T(4,128)S(4)} %get-tuple-element.27.own, s32[2,80]{1,0:T(2,128)S(1)} %collective-permute-done.table2, bf16[1,1,80,128,128]{4,3,2,1,0:T(8,128)(2,1)S(1)} %collective-permute-done.1.blocks2), custom_call_target="tpu_custom_call" | custom-call | tf_op jit(solution)/shard_map/pack_other/pallas_call | solution.py:365
  9.7 1.3 %collective-permute-start.6 = (bf16[16,32,128]{2,1,0:T(8,128)(2,1)S(1)}, bf16[16,32,128]{2,1,0:T(8,128)(2,1)S(1)}, u32[]{:S(2)}, u32[]{:S(2)}) collective-permute-start(bf16[16,32,128]{2,1,0:T(8,128)(2,1)S(1)} %get-tuple-element.35), channel_id=1, source_target_pairs={{0,7},{1,6},{2,5},{3,4},{4,0},{5,1},{6,2},{7,3},{8,15},{9,14},{10,... | collective-permute-start | bytes 393224 | tf_op jit(solution)/shard_map/ppermute | solution.py:288
  11.0 1.3 %collective-permute-start.5 = (bf16[16,32,128]{2,1,0:T(8,128)(2,1)S(1)}, bf16[16,32,128]{2,1,0:T(8,128)(2,1)S(1)}, u32[]{:S(2)}, u32[]{:S(2)}) collective-permute-start(bf16[16,32,128]{2,1,0:T(8,128)(2,1)S(1)} %get-tuple-element.35), channel_id=1, source_target_pairs={{0,5},{1,4},{2,7},{3,6},{4,0},{5,1},{6,2},{7,3},{8,13},{9,12},{10,... | collective-permute-start | bytes 393224 | tf_op jit(solution)/shard_map/ppermute | solution.py:288
  12.3 0.6 collective-permute-start.7
  12.9 2.1 %collective-permute-done.6.refs_1_ = bf16[16,32,128]{2,1,0:T(8,128)(2,1)S(1)} collective-permute-done((bf16[16,32,128]{2,1,0:T(8,128)(2,1)S(1)}, bf16[16,32,128]{2,1,0:T(8,128)(2,1)S(1)}, u32[]{:S(2)}, u32[]{:S(2)}) %collective-permute-start.6) | collective-permute-done | bytes 131104 | tf_op jit(solution)/shard_map/ppermute | solution.py:288
  15.0 1.5 %collective-permute-done.5.refs_0_ = bf16[16,32,128]{2,1,0:T(8,128)(2,1)S(1)} collective-permute-done((bf16[16,32,128]{2,1,0:T(8,128)(2,1)S(1)}, bf16[16,32,128]{2,1,0:T(8,128)(2,1)S(1)}, u32[]{:S(2)}, u32[]{:S(2)}) %collective-permute-start.5) | collective-permute-done | bytes 131104 | tf_op jit(solution)/shard_map/ppermute | solution.py:288
  16.8 1.5 %collective-permute-done.10.image = bf16[32,32,128]{2,1,0:T(8,128)(2,1)S(1)} collective-permute-done((bf16[32,32,128]{2,1,0:T(8,128)(2,1)S(1)}, bf16[32,32,128]{2,1,0:T(8,128)(2,1)S(1)}, u32[]{:S(2)}, u32[]{:S(2)}) %collective-permute-start.10) | collective-permute-done | bytes 262176 | tf_op jit(solution)/shard_map/ppermute | solution.py:288
  18.3 1.6 %collective-permute-start.12 = (bf16[16,32,128]{2,1,0:T(8,128)(2,1)S(1)}, bf16[16,32,128]{2,1,0:T(8,128)(2,1)S(1)}, u32[]{:S(2)}, u32[]{:S(2)}) collective-permute-start(bf16[16,32,128]{2,1,0:T(8,128)(2,1)S(1)} %project.3), channel_id=1, source_target_pairs={{0,4},{1,5},{2,6},{3,7},{4,3},{5,2},{6,1},{7,0},{8,12},{9,13},{10,... | collective-permute-start | bytes 393224 | tf_op jit(solution)/shard_map/ppermute | solution.py:288
  19.9 1.1 %collective-permute-start.14 = (bf16[16,32,128]{2,1,0:T(8,128)(2,1)S(1)}, bf16[16,32,128]{2,1,0:T(8,128)(2,1)S(1)}, u32[]{:S(2)}, u32[]{:S(2)}) collective-permute-start(bf16[16,32,128]{2,1,0:T(8,128)(2,1)S(1)} %project.3), channel_id=1, source_target_pairs={{0,4},{1,5},{2,6},{3,7},{4,2},{5,3},{6,0},{7,1},{8,12},{9,13},{10,... | collective-permute-start | bytes 393224 | tf_op jit(solution)/shard_map/ppermute | solution.py:288
  21.0 0.5 collective-permute-start.15
  21.5 0.4 collective-permute-done.12.refs_1_
  21.9 1.4 %collective-permute-done.11.refs_0_ = bf16[16,32,128]{2,1,0:T(8,128)(2,1)S(1)} collective-permute-done((bf16[16,32,128]{2,1,0:T(8,128)(2,1)S(1)}, bf16[16,32,128]{2,1,0:T(8,128)(2,1)S(1)}, u32[]{:S(2)}, u32[]{:S(2)}) %collective-permute-start.11) | collective-permute-done | bytes 131104 | tf_op jit(solution)/shard_map/ppermute | solution.py:288
  23.2 0.3 collective-permute-done.14.refs_5_
  23.5 1.7 %collective-permute-start.17 = (bf16[16,32,128]{2,1,0:T(8,128)(2,1)S(1)}, bf16[16,32,128]{2,1,0:T(8,128)(2,1)S(1)}, u32[]{:S(2)}, u32[]{:S(2)}) collective-permute-start(bf16[16,32,128]{2,1,0:T(8,128)(2,1)S(1)} %get-tuple-element.38), channel_id=1, source_target_pairs={{0,7},{1,6},{2,5},{3,4},{4,0},{5,1},{6,2},{7,3},{8,15},{9,14},{10,... | collective-permute-start | bytes 393224 | tf_op jit(solution)/shard_map/ppermute | solution.py:288
  25.3 1.4 %collective-permute-start.19 = (bf16[16,32,128]{2,1,0:T(8,128)(2,1)S(1)}, bf16[16,32,128]{2,1,0:T(8,128)(2,1)S(1)}, u32[]{:S(2)}, u32[]{:S(2)}) collective-permute-start(bf16[16,32,128]{2,1,0:T(8,128)(2,1)S(1)} %get-tuple-element.38), channel_id=1, source_target_pairs={{0,6},{1,7},{2,4},{3,5},{4,0},{5,1},{6,2},{7,3},{8,14},{9,15},{10,... | collective-permute-start | bytes 393224 | tf_op jit(solution)/shard_map/ppermute | solution.py:288
  26.7 0.5 collective-permute-start.20
  27.2 2.2 %collective-permute-done.17.refs_1_ = bf16[16,32,128]{2,1,0:T(8,128)(2,1)S(1)} collective-permute-done((bf16[16,32,128]{2,1,0:T(8,128)(2,1)S(1)}, bf16[16,32,128]{2,1,0:T(8,128)(2,1)S(1)}, u32[]{:S(2)}, u32[]{:S(2)}) %collective-permute-start.17) | collective-permute-done | bytes 131104 | tf_op jit(solution)/shard_map/ppermute | solution.py:288
  29.4 0.8 %collective-permute-done.16.refs_0_ = bf16[16,32,128]{2,1,0:T(8,128)(2,1)S(1)} collective-permute-done((bf16[16,32,128]{2,1,0:T(8,128)(2,1)S(1)}, bf16[16,32,128]{2,1,0:T(8,128)(2,1)S(1)}, u32[]{:S(2)}, u32[]{:S(2)}) %collective-permute-start.16) | collective-permute-done | bytes 131104 | tf_op jit(solution)/shard_map/ppermute | solution.py:288
  30.2 0.5 collective-permute-done.19.refs_5_
  30.9 1.5 %collective-permute-done.21.image = bf16[32,32,128]{2,1,0:T(8,128)(2,1)S(1)} collective-permute-done((bf16[32,32,128]{2,1,0:T(8,128)(2,1)S(1)}, bf16[32,32,128]{2,1,0:T(8,128)(2,1)S(1)}, u32[]{:S(2)}, u32[]{:S(2)}) %collective-permute-start.21) | collective-permute-done | bytes 262176 | tf_op jit(solution)/shard_map/ppermute | solution.py:288
  32.4 0.8 %collective-permute-start.23 = (bf16[16,32,128]{2,1,0:T(8,128)(2,1)S(1)}, bf16[16,32,128]{2,1,0:T(8,128)(2,1)S(1)}, u32[]{:S(2)}, u32[]{:S(2)}) collective-permute-start(bf16[16,32,128]{2,1,0:T(8,128)(2,1)S(1)} %project.4), channel_id=1, source_target_pairs={{0,4},{1,5},{2,6},{3,7},{4,3},{5,2},{6,1},{7,0},{8,12},{9,13},{10,... | collective-permute-start | bytes 393224 | tf_op jit(solution)/shard_map/ppermute | solution.py:288
  33.4 1.2 %collective-permute-start.25 = (bf16[16,32,128]{2,1,0:T(8,128)(2,1)S(1)}, bf16[16,32,128]{2,1,0:T(8,128)(2,1)S(1)}, u32[]{:S(2)}, u32[]{:S(2)}) collective-permute-start(bf16[16,32,128]{2,1,0:T(8,128)(2,1)S(1)} %project.4), channel_id=1, source_target_pairs={{0,4},{1,5},{2,6},{3,7},{4,2},{5,3},{6,0},{7,1},{8,12},{9,13},{10,... | collective-permute-start | bytes 393224 | tf_op jit(solution)/shard_map/ppermute | solution.py:288
  34.6 0.5 collective-permute-start.26
  35.2 1.4 %collective-permute-done.22.refs_0_ = bf16[16,32,128]{2,1,0:T(8,128)(2,1)S(1)} collective-permute-done((bf16[16,32,128]{2,1,0:T(8,128)(2,1)S(1)}, bf16[16,32,128]{2,1,0:T(8,128)(2,1)S(1)}, u32[]{:S(2)}, u32[]{:S(2)}) %collective-permute-start.22) | collective-permute-done | bytes 131104 | tf_op jit(solution)/shard_map/ppermute | solution.py:288
  36.6 0.8 %collective-permute-done.25.refs_5_ = bf16[16,32,128]{2,1,0:T(8,128)(2,1)S(1)} collective-permute-done((bf16[16,32,128]{2,1,0:T(8,128)(2,1)S(1)}, bf16[16,32,128]{2,1,0:T(8,128)(2,1)S(1)}, u32[]{:S(2)}, u32[]{:S(2)}) %collective-permute-start.25) | collective-permute-done | bytes 131104 | tf_op jit(solution)/shard_map/ppermute | solution.py:288
  37.3 2.0 %collective-permute-start.28 = (bf16[16,32,128]{2,1,0:T(8,128)(2,1)S(1)}, bf16[16,32,128]{2,1,0:T(8,128)(2,1)S(1)}, u32[]{:S(2)}, u32[]{:S(2)}) collective-permute-start(bf16[16,32,128]{2,1,0:T(8,128)(2,1)S(1)} %get-tuple-element.42), channel_id=1, source_target_pairs={{0,7},{1,6},{2,5},{3,4},{4,0},{5,1},{6,2},{7,3},{8,15},{9,14},{10,... | collective-permute-start | bytes 393224 | tf_op jit(solution)/shard_map/ppermute | solution.py:288
  39.4 0.9 %collective-permute-start.30 = (bf16[16,32,128]{2,1,0:T(8,128)(2,1)S(1)}, bf16[16,32,128]{2,1,0:T(8,128)(2,1)S(1)}, u32[]{:S(2)}, u32[]{:S(2)}) collective-permute-start(bf16[16,32,128]{2,1,0:T(8,128)(2,1)S(1)} %get-tuple-element.42), channel_id=1, source_target_pairs={{0,6},{1,7},{2,4},{3,5},{4,0},{5,1},{6,2},{7,3},{8,14},{9,15},{10,... | collective-permute-start | bytes 393224 | tf_op jit(solution)/shard_map/ppermute | solution.py:288
  40.5 0.3 collective-permute-start.31
  40.8 1.9 %collective-permute-done.28.refs_1_ = bf16[16,32,128]{2,1,0:T(8,128)(2,1)S(1)} collective-permute-done((bf16[16,32,128]{2,1,0:T(8,128)(2,1)S(1)}, bf16[16,32,128]{2,1,0:T(8,128)(2,1)S(1)}, u32[]{:S(2)}, u32[]{:S(2)}) %collective-permute-start.28) | collective-permute-done | bytes 131104 | tf_op jit(solution)/shard_map/ppermute | solution.py:288
  42.7 1.1 %collective-permute-done.27.refs_0_ = bf16[16,32,128]{2,1,0:T(8,128)(2,1)S(1)} collective-permute-done((bf16[16,32,128]{2,1,0:T(8,128)(2,1)S(1)}, bf16[16,32,128]{2,1,0:T(8,128)(2,1)S(1)}, u32[]{:S(2)}, u32[]{:S(2)}) %collective-permute-start.27) | collective-permute-done | bytes 131104 | tf_op jit(solution)/shard_map/ppermute | solution.py:288
  44.3 12.5 %collective-permute-done.32.image = bf16[32,32,128]{2,1,0:T(8,128)(2,1)S(1)} collective-permute-done((bf16[32,32,128]{2,1,0:T(8,128)(2,1)S(1)}, bf16[32,32,128]{2,1,0:T(8,128)(2,1)S(1)}, u32[]{:S(2)}, u32[]{:S(2)}) %collective-permute-start.32) | collective-permute-done | bytes 262176 | tf_op jit(solution)/shard_map/ppermute | solution.py:288
  56.8 0.5 project.5
  57.4 1.5 %collective-permute-start.33 = (bf16[16,32,128]{2,1,0:T(8,128)(2,1)S(1)}, bf16[16,32,128]{2,1,0:T(8,128)(2,1)S(1)}, u32[]{:S(2)}, u32[]{:S(2)}) collective-permute-start(bf16[16,32,128]{2,1,0:T(8,128)(2,1)S(1)} %project.5), channel_id=1, source_target_pairs={{0,4},{1,5},{2,6},{3,7},{4,1},{5,0},{6,3},{7,2},{8,12},{9,13},{10,... | collective-permute-start | bytes 393224 | tf_op jit(solution)/shard_map/ppermute | solution.py:288
  58.9 0.5 collective-permute-start.35
  59.4 1.4 %collective-permute-done.33.refs_0_ = bf16[16,32,128]{2,1,0:T(8,128)(2,1)S(1)} collective-permute-done((bf16[16,32,128]{2,1,0:T(8,128)(2,1)S(1)}, bf16[16,32,128]{2,1,0:T(8,128)(2,1)S(1)}, u32[]{:S(2)}, u32[]{:S(2)}) %collective-permute-start.33) | collective-permute-done | bytes 131104 | tf_op jit(solution)/shard_map/ppermute | solution.py:288
  60.8 0.7 collective-permute-done.36.refs_5_
  61.5 3.1 %collective-permute-start.39 = (bf16[16,32,128]{2,1,0:T(8,128)(2,1)S(1)}, bf16[16,32,128]{2,1,0:T(8,128)(2,1)S(1)}, u32[]{:S(2)}, u32[]{:S(2)}) collective-permute-start(bf16[16,32,128]{2,1,0:T(8,128)(2,1)S(1)} %get-tuple-element.46), channel_id=1, source_target_pairs={{0,7},{1,6},{2,5},{3,4},{4,0},{5,1},{6,2},{7,3},{8,15},{9,14},{10,... | collective-permute-start | bytes 393224 | tf_op jit(solution)/shard_map/ppermute | solution.py:288
  64.7 0.9 %collective-permute-start.41 = (bf16[16,32,128]{2,1,0:T(8,128)(2,1)S(1)}, bf16[16,32,128]{2,1,0:T(8,128)(2,1)S(1)}, u32[]{:S(2)}, u32[]{:S(2)}) collective-permute-start(bf16[16,32,128]{2,1,0:T(8,128)(2,1)S(1)} %get-tuple-element.46), channel_id=1, source_target_pairs={{0,6},{1,7},{2,4},{3,5},{4,0},{5,1},{6,2},{7,3},{8,14},{9,15},{10,... | collective-permute-start | bytes 393224 | tf_op jit(solution)/shard_map/ppermute | solution.py:288
  66.1 1.9 %collective-permute-done.39.refs_1_ = bf16[16,32,128]{2,1,0:T(8,128)(2,1)S(1)} collective-permute-done((bf16[16,32,128]{2,1,0:T(8,128)(2,1)S(1)}, bf16[16,32,128]{2,1,0:T(8,128)(2,1)S(1)}, u32[]{:S(2)}, u32[]{:S(2)}) %collective-permute-start.39) | collective-permute-done | bytes 131104 | tf_op jit(solution)/shard_map/ppermute | solution.py:288
  68.0 1.1 %collective-permute-done.38.refs_0_ = bf16[16,32,128]{2,1,0:T(8,128)(2,1)S(1)} collective-permute-done((bf16[16,32,128]{2,1,0:T(8,128)(2,1)S(1)}, bf16[16,32,128]{2,1,0:T(8,128)(2,1)S(1)}, u32[]{:S(2)}, u32[]{:S(2)}) %collective-permute-start.38) | collective-permute-done | bytes 131104 | tf_op jit(solution)/shard_map/ppermute | solution.py:288
  69.4 0.6 update.15.refs_1_
  70.0 0.8 %second.7 = bf16[4,8,4096]{2,1,0:T(8,128)(2,1)} custom-call(s32[3,80]{1,0:T(4,128)S(4)} %get-tuple-element.29.refs_0_.info, f32[32,32,128]{2,1,0:T(8,128)S(1)} %update.15.refs_1_, bf16[32,32,128]{2,1,0:T(8,128)(2,1)S(1)} %collective-permute-done.42.refs_2_, bf16[32,32,128]{2,1,0:T(8,128)(2,1)S(1)} %get-tuple-element.47.refs_3_, ...), custom_call_target="tpu_custom_call" | custom-call | tf_op jit(solution)/shard_map/second/pallas_call | solution.py:309
  (68 shorter events, 2.9 us)
Async XLA Ops:
  0.0 8.2 %collective-permute-start.1 = (bf16[1,1,80,128,128]{4,3,2,1,0:T(8,128)(2,1)}, bf16[1,1,80,128,128]{4,3,2,1,0:T(8,128)(2,1)S(1)}, u32[]{:S(2)}, u32[]{:S(2)}) collective-permute-start(bf16[1,1,80,128,128]{4,3,2,1,0:T(8,128)(2,1)} %blocks_in.1), channel_id=1, source_target_pairs={{0,4},{1,5},{2,6},{3,7},{4,0},{5,1},{6,2},{7,3},{8,12},{9,13},{10,... | collective-permute-start | bytes 7864328 | tf_op jit(solution)/shard_map/ppermute | solution.py:288
  3.9 5.7 %collective-permute-start.4 = (bf16[5,32,128]{2,1,0:T(8,128)(2,1)S(1)}, bf16[5,32,128]{2,1,0:T(8,128)(2,1)S(1)}, u32[]{:S(2)}, u32[]{:S(2)}) collective-permute-start(bf16[5,32,128]{2,1,0:T(8,128)(2,1)S(1)} %get-tuple-element.31._.refs_2_), channel_id=1, source_target_pairs={{0,3},{1,2},{2,1},{3,0},{4,7},{5,6},{6,5},{7,4},{8,11},{9,10},{10,... | collective-permute-start | bytes 122888 | tf_op jit(solution)/shard_map/ppermute | solution.py:288
  6.1 3.5 %collective-permute-start.3 = (bf16[5,32,128]{2,1,0:T(8,128)(2,1)S(1)}, bf16[5,32,128]{2,1,0:T(8,128)(2,1)S(1)}, u32[]{:S(2)}, u32[]{:S(2)}) collective-permute-start(bf16[5,32,128]{2,1,0:T(8,128)(2,1)S(1)} %get-tuple-element.31._.refs_2_), channel_id=1, source_target_pairs={{0,2},{1,3},{2,0},{3,1},{4,6},{5,7},{6,4},{7,5},{8,10},{9,11},{10,... | collective-permute-start | bytes 122888 | tf_op jit(solution)/shard_map/ppermute | solution.py:288
  6.3 3.3 %collective-permute-start.2 = (bf16[5,32,128]{2,1,0:T(8,128)(2,1)S(1)}, bf16[5,32,128]{2,1,0:T(8,128)(2,1)S(1)}, u32[]{:S(2)}, u32[]{:S(2)}) collective-permute-start(bf16[5,32,128]{2,1,0:T(8,128)(2,1)S(1)} %get-tuple-element.31._.refs_2_), channel_id=1, source_target_pairs={{0,1},{1,0},{2,3},{3,2},{4,5},{5,4},{6,7},{7,6},{8,9},{9,8},{10,11... | collective-permute-start | bytes 122888 | tf_op jit(solution)/shard_map/ppermute | solution.py:288
  6.6 1.7 %collective-permute-start = (s32[2,80]{1,0:T(2,128)S(1)}, s32[2,80]{1,0:T(2,128)S(1)}, u32[]{:S(2)}, u32[]{:S(2)}) collective-permute-start(s32[2,80]{1,0:T(2,128)S(1)} %get-tuple-element.28), channel_id=1, source_target_pairs={{0,4},{1,5},{2,6},{3,7},{4,0},{5,1},{6,2},{7,3},{8,12},{9,13},{10,... | collective-permute-start | bytes 1928 | tf_op jit(solution)/shard_map/ppermute | solution.py:288
  9.7 5.3 %collective-permute-start.6 = (bf16[16,32,128]{2,1,0:T(8,128)(2,1)S(1)}, bf16[16,32,128]{2,1,0:T(8,128)(2,1)S(1)}, u32[]{:S(2)}, u32[]{:S(2)}) collective-permute-start(bf16[16,32,128]{2,1,0:T(8,128)(2,1)S(1)} %get-tuple-element.35), channel_id=1, source_target_pairs={{0,7},{1,6},{2,5},{3,4},{4,0},{5,1},{6,2},{7,3},{8,15},{9,14},{10,... | collective-permute-start | bytes 393224 | tf_op jit(solution)/shard_map/ppermute | solution.py:288
  11.0 5.5 %collective-permute-start.5 = (bf16[16,32,128]{2,1,0:T(8,128)(2,1)S(1)}, bf16[16,32,128]{2,1,0:T(8,128)(2,1)S(1)}, u32[]{:S(2)}, u32[]{:S(2)}) collective-permute-start(bf16[16,32,128]{2,1,0:T(8,128)(2,1)S(1)} %get-tuple-element.35), channel_id=1, source_target_pairs={{0,5},{1,4},{2,7},{3,6},{4,0},{5,1},{6,2},{7,3},{8,13},{9,12},{10,... | collective-permute-start | bytes 393224 | tf_op jit(solution)/shard_map/ppermute | solution.py:288
  12.3 4.4 %collective-permute-start.8 = (bf16[16,32,128]{2,1,0:T(8,128)(2,1)S(1)}, bf16[16,32,128]{2,1,0:T(8,128)(2,1)S(1)}, u32[]{:S(2)}, u32[]{:S(2)}) collective-permute-start(bf16[16,32,128]{2,1,0:T(8,128)(2,1)S(1)} %get-tuple-element.35), channel_id=1, source_target_pairs={{0,6},{1,7},{2,4},{3,5},{4,0},{5,1},{6,2},{7,3},{8,14},{9,15},{10,... | collective-permute-start | bytes 393224 | tf_op jit(solution)/shard_map/ppermute | solution.py:288
  12.3 4.4 %collective-permute-start.7 = (bf16[16,32,128]{2,1,0:T(8,128)(2,1)S(1)}, bf16[16,32,128]{2,1,0:T(8,128)(2,1)S(1)}, u32[]{:S(2)}, u32[]{:S(2)}) collective-permute-start(bf16[16,32,128]{2,1,0:T(8,128)(2,1)S(1)} %get-tuple-element.35), channel_id=1, source_target_pairs={{0,4},{1,5},{2,6},{3,7},{4,0},{5,1},{6,2},{7,3},{8,12},{9,13},{10,... | collective-permute-start | bytes 393224 | tf_op jit(solution)/shard_map/ppermute | solution.py:288
  12.9 3.8 %collective-permute-start.9 = (bf16[32,32,128]{2,1,0:T(8,128)(2,1)S(1)}, bf16[32,32,128]{2,1,0:T(8,128)(2,1)S(1)}, u32[]{:S(2)}, u32[]{:S(2)}) collective-permute-start(bf16[32,32,128]{2,1,0:T(8,128)(2,1)S(1)} %get-tuple-element.36.refs_3_), channel_id=1, source_target_pairs={{0,4},{1,5},{2,6},{3,7},{4,0},{5,1},{6,2},{7,3},{8,12},{9,13},{10,... | collective-permute-start | bytes 786440 | tf_op jit(solution)/shard_map/ppermute | solution.py:288
  16.7 1.6 %collective-permute-start.10 = (bf16[32,32,128]{2,1,0:T(8,128)(2,1)S(1)}, bf16[32,32,128]{2,1,0:T(8,128)(2,1)S(1)}, u32[]{:S(2)}, u32[]{:S(2)}) collective-permute-start(bf16[32,32,128]{2,1,0:T(8,128)(2,1)S(1)} %get-tuple-element.37), channel_id=1, source_target_pairs={{0,4},{1,5},{2,6},{3,7},{4,12},{5,13},{6,14},{7,15},{8,0},{9,1},{1... | collective-permute-start | bytes 786440 | tf_op jit(solution)/shard_map/ppermute | solution.py:288
  18.3 3.6 %collective-permute-start.12 = (bf16[16,32,128]{2,1,0:T(8,128)(2,1)S(1)}, bf16[16,32,128]{2,1,0:T(8,128)(2,1)S(1)}, u32[]{:S(2)}, u32[]{:S(2)}) collective-permute-start(bf16[16,32,128]{2,1,0:T(8,128)(2,1)S(1)} %project.3), channel_id=1, source_target_pairs={{0,4},{1,5},{2,6},{3,7},{4,3},{5,2},{6,1},{7,0},{8,12},{9,13},{10,... | collective-permute-start | bytes 393224 | tf_op jit(solution)/shard_map/ppermute | solution.py:288
  19.9 3.3 %collective-permute-start.11 = (bf16[16,32,128]{2,1,0:T(8,128)(2,1)S(1)}, bf16[16,32,128]{2,1,0:T(8,128)(2,1)S(1)}, u32[]{:S(2)}, u32[]{:S(2)}) collective-permute-start(bf16[16,32,128]{2,1,0:T(8,128)(2,1)S(1)} %project.3), channel_id=1, source_target_pairs={{0,4},{1,5},{2,6},{3,7},{4,1},{5,0},{6,3},{7,2},{8,12},{9,13},{10,... | collective-permute-start | bytes 393224 | tf_op jit(solution)/shard_map/ppermute | solution.py:288
  19.9 3.6 %collective-permute-start.14 = (bf16[16,32,128]{2,1,0:T(8,128)(2,1)S(1)}, bf16[16,32,128]{2,1,0:T(8,128)(2,1)S(1)}, u32[]{:S(2)}, u32[]{:S(2)}) collective-permute-start(bf16[16,32,128]{2,1,0:T(8,128)(2,1)S(1)} %project.3), channel_id=1, source_target_pairs={{0,4},{1,5},{2,6},{3,7},{4,2},{5,3},{6,0},{7,1},{8,12},{9,13},{10,... | collective-permute-start | bytes 393224 | tf_op jit(solution)/shard_map/ppermute | solution.py:288
  21.0 2.5 %collective-permute-start.13 = (bf16[16,32,128]{2,1,0:T(8,128)(2,1)S(1)}, bf16[16,32,128]{2,1,0:T(8,128)(2,1)S(1)}, u32[]{:S(2)}, u32[]{:S(2)}) collective-permute-start(bf16[16,32,128]{2,1,0:T(8,128)(2,1)S(1)} %project.3), channel_id=1, source_target_pairs={{0,4},{1,5},{2,6},{3,7},{4,0},{5,1},{6,2},{7,3},{8,12},{9,13},{10,... | collective-permute-start | bytes 393224 | tf_op jit(solution)/shard_map/ppermute | solution.py:288
  21.0 2.5 %collective-permute-start.15 = (bf16[32,32,128]{2,1,0:T(8,128)(2,1)S(1)}, bf16[32,32,128]{2,1,0:T(8,128)(2,1)S(1)}, u32[]{:S(2)}, u32[]{:S(2)}) collective-permute-start(bf16[32,32,128]{2,1,0:T(8,128)(2,1)S(1)} %collective-permute-done.10.image), channel_id=1, source_target_pairs={{0,4},{1,5},{2,6},{3,7},{4,0},{5,1},{6,2},{7,3},{8,12},{9,13},{10,... | collective-permute-start | bytes 786440 | tf_op jit(solution)/shard_map/ppermute | solution.py:288
  23.5 5.9 %collective-permute-start.17 = (bf16[16,32,128]{2,1,0:T(8,128)(2,1)S(1)}, bf16[16,32,128]{2,1,0:T(8,128)(2,1)S(1)}, u32[]{:S(2)}, u32[]{:S(2)}) collective-permute-start(bf16[16,32,128]{2,1,0:T(8,128)(2,1)S(1)} %get-tuple-element.38), channel_id=1, source_target_pairs={{0,7},{1,6},{2,5},{3,4},{4,0},{5,1},{6,2},{7,3},{8,15},{9,14},{10,... | collective-permute-start | bytes 393224 | tf_op jit(solution)/shard_map/ppermute | solution.py:288
  25.2 5.0 %collective-permute-start.16 = (bf16[16,32,128]{2,1,0:T(8,128)(2,1)S(1)}, bf16[16,32,128]{2,1,0:T(8,128)(2,1)S(1)}, u32[]{:S(2)}, u32[]{:S(2)}) collective-permute-start(bf16[16,32,128]{2,1,0:T(8,128)(2,1)S(1)} %get-tuple-element.38), channel_id=1, source_target_pairs={{0,5},{1,4},{2,7},{3,6},{4,0},{5,1},{6,2},{7,3},{8,13},{9,12},{10,... | collective-permute-start | bytes 393224 | tf_op jit(solution)/shard_map/ppermute | solution.py:288
  25.3 5.5 %collective-permute-start.19 = (bf16[16,32,128]{2,1,0:T(8,128)(2,1)S(1)}, bf16[16,32,128]{2,1,0:T(8,128)(2,1)S(1)}, u32[]{:S(2)}, u32[]{:S(2)}) collective-permute-start(bf16[16,32,128]{2,1,0:T(8,128)(2,1)S(1)} %get-tuple-element.38), channel_id=1, source_target_pairs={{0,6},{1,7},{2,4},{3,5},{4,0},{5,1},{6,2},{7,3},{8,14},{9,15},{10,... | collective-permute-start | bytes 393224 | tf_op jit(solution)/shard_map/ppermute | solution.py:288
  26.7 4.1 %collective-permute-start.18 = (bf16[16,32,128]{2,1,0:T(8,128)(2,1)S(1)}, bf16[16,32,128]{2,1,0:T(8,128)(2,1)S(1)}, u32[]{:S(2)}, u32[]{:S(2)}) collective-permute-start(bf16[16,32,128]{2,1,0:T(8,128)(2,1)S(1)} %get-tuple-element.38), channel_id=1, source_target_pairs={{0,4},{1,5},{2,6},{3,7},{4,0},{5,1},{6,2},{7,3},{8,12},{9,13},{10,... | collective-permute-start | bytes 393224 | tf_op jit(solution)/shard_map/ppermute | solution.py:288
  26.7 4.1 %collective-permute-start.20 = (bf16[32,32,128]{2,1,0:T(8,128)(2,1)S(1)}, bf16[32,32,128]{2,1,0:T(8,128)(2,1)S(1)}, u32[]{:S(2)}, u32[]{:S(2)}) collective-permute-start(bf16[32,32,128]{2,1,0:T(8,128)(2,1)S(1)} %get-tuple-element.39.refs_3_), channel_id=1, source_target_pairs={{0,4},{1,5},{2,6},{3,7},{4,0},{5,1},{6,2},{7,3},{8,12},{9,13},{10,... | collective-permute-start | bytes 786440 | tf_op jit(solution)/shard_map/ppermute | solution.py:288
  30.8 1.6 %collective-permute-start.21 = (bf16[32,32,128]{2,1,0:T(8,128)(2,1)S(1)}, bf16[32,32,128]{2,1,0:T(8,128)(2,1)S(1)}, u32[]{:S(2)}, u32[]{:S(2)}) collective-permute-start(bf16[32,32,128]{2,1,0:T(8,128)(2,1)S(1)} %get-tuple-element.41), channel_id=1, source_target_pairs={{0,4},{1,5},{2,6},{3,7},{4,0},{5,1},{6,2},{7,3},{8,12},{9,13},{10,... | collective-permute-start | bytes 786440 | tf_op jit(solution)/shard_map/ppermute | solution.py:288
  32.4 2.8 %collective-permute-start.23 = (bf16[16,32,128]{2,1,0:T(8,128)(2,1)S(1)}, bf16[16,32,128]{2,1,0:T(8,128)(2,1)S(1)}, u32[]{:S(2)}, u32[]{:S(2)}) collective-permute-start(bf16[16,32,128]{2,1,0:T(8,128)(2,1)S(1)} %project.4), channel_id=1, source_target_pairs={{0,4},{1,5},{2,6},{3,7},{4,3},{5,2},{6,1},{7,0},{8,12},{9,13},{10,... | collective-permute-start | bytes 393224 | tf_op jit(solution)/shard_map/ppermute | solution.py:288
  33.3 3.3 %collective-permute-start.22 = (bf16[16,32,128]{2,1,0:T(8,128)(2,1)S(1)}, bf16[16,32,128]{2,1,0:T(8,128)(2,1)S(1)}, u32[]{:S(2)}, u32[]{:S(2)}) collective-permute-start(bf16[16,32,128]{2,1,0:T(8,128)(2,1)S(1)} %project.4), channel_id=1, source_target_pairs={{0,4},{1,5},{2,6},{3,7},{4,1},{5,0},{6,3},{7,2},{8,12},{9,13},{10,... | collective-permute-start | bytes 393224 | tf_op jit(solution)/shard_map/ppermute | solution.py:288
  33.4 3.9 %collective-permute-start.25 = (bf16[16,32,128]{2,1,0:T(8,128)(2,1)S(1)}, bf16[16,32,128]{2,1,0:T(8,128)(2,1)S(1)}, u32[]{:S(2)}, u32[]{:S(2)}) collective-permute-start(bf16[16,32,128]{2,1,0:T(8,128)(2,1)S(1)} %project.4), channel_id=1, source_target_pairs={{0,4},{1,5},{2,6},{3,7},{4,2},{5,3},{6,0},{7,1},{8,12},{9,13},{10,... | collective-permute-start | bytes 393224 | tf_op jit(solution)/shard_map/ppermute | solution.py:288
  34.6 2.7 %collective-permute-start.24 = (bf16[16,32,128]{2,1,0:T(8,128)(2,1)S(1)}, bf16[16,32,128]{2,1,0:T(8,128)(2,1)S(1)}, u32[]{:S(2)}, u32[]{:S(2)}) collective-permute-start(bf16[16,32,128]{2,1,0:T(8,128)(2,1)S(1)} %project.4), channel_id=1, source_target_pairs={{0,4},{1,5},{2,6},{3,7},{4,0},{5,1},{6,2},{7,3},{8,12},{9,13},{10,... | collective-permute-start | bytes 393224 | tf_op jit(solution)/shard_map/ppermute | solution.py:288
  34.6 2.7 %collective-permute-start.26 = (bf16[32,32,128]{2,1,0:T(8,128)(2,1)S(1)}, bf16[32,32,128]{2,1,0:T(8,128)(2,1)S(1)}, u32[]{:S(2)}, u32[]{:S(2)}) collective-permute-start(bf16[32,32,128]{2,1,0:T(8,128)(2,1)S(1)} %collective-permute-done.21.image), channel_id=1, source_target_pairs={{0,4},{1,5},{2,6},{3,7},{4,0},{5,1},{6,2},{7,3},{8,12},{9,13},{10,... | collective-permute-start | bytes 786440 | tf_op jit(solution)/shard_map/ppermute | solution.py:288
  37.3 5.4 %collective-permute-start.28 = (bf16[16,32,128]{2,1,0:T(8,128)(2,1)S(1)}, bf16[16,32,128]{2,1,0:T(8,128)(2,1)S(1)}, u32[]{:S(2)}, u32[]{:S(2)}) collective-permute-start(bf16[16,32,128]{2,1,0:T(8,128)(2,1)S(1)} %get-tuple-element.42), channel_id=1, source_target_pairs={{0,7},{1,6},{2,5},{3,4},{4,0},{5,1},{6,2},{7,3},{8,15},{9,14},{10,... | collective-permute-start | bytes 393224 | tf_op jit(solution)/shard_map/ppermute | solution.py:288
  39.3 4.5 %collective-permute-start.27 = (bf16[16,32,128]{2,1,0:T(8,128)(2,1)S(1)}, bf16[16,32,128]{2,1,0:T(8,128)(2,1)S(1)}, u32[]{:S(2)}, u32[]{:S(2)}) collective-permute-start(bf16[16,32,128]{2,1,0:T(8,128)(2,1)S(1)} %get-tuple-element.42), channel_id=1, source_target_pairs={{0,5},{1,4},{2,7},{3,6},{4,0},{5,1},{6,2},{7,3},{8,13},{9,12},{10,... | collective-permute-start | bytes 393224 | tf_op jit(solution)/shard_map/ppermute | solution.py:288
  39.4 4.7 %collective-permute-start.30 = (bf16[16,32,128]{2,1,0:T(8,128)(2,1)S(1)}, bf16[16,32,128]{2,1,0:T(8,128)(2,1)S(1)}, u32[]{:S(2)}, u32[]{:S(2)}) collective-permute-start(bf16[16,32,128]{2,1,0:T(8,128)(2,1)S(1)} %get-tuple-element.42), channel_id=1, source_target_pairs={{0,6},{1,7},{2,4},{3,5},{4,0},{5,1},{6,2},{7,3},{8,14},{9,15},{10,... | collective-permute-start | bytes 393224 | tf_op jit(solution)/shard_map/ppermute | solution.py:288
  40.3 3.8 %collective-permute-start.29 = (bf16[16,32,128]{2,1,0:T(8,128)(2,1)S(1)}, bf16[16,32,128]{2,1,0:T(8,128)(2,1)S(1)}, u32[]{:S(2)}, u32[]{:S(2)}) collective-permute-start(bf16[16,32,128]{2,1,0:T(8,128)(2,1)S(1)} %get-tuple-element.42), channel_id=1, source_target_pairs={{0,4},{1,5},{2,6},{3,7},{4,0},{5,1},{6,2},{7,3},{8,12},{9,13},{10,... | collective-permute-start | bytes 393224 | tf_op jit(solution)/shard_map/ppermute | solution.py:288
  40.5 3.6 %collective-permute-start.31 = (bf16[32,32,128]{2,1,0:T(8,128)(2,1)S(1)}, bf16[32,32,128]{2,1,0:T(8,128)(2,1)S(1)}, u32[]{:S(2)}, u32[]{:S(2)}) collective-permute-start(bf16[32,32,128]{2,1,0:T(8,128)(2,1)S(1)} %get-tuple-element.43.refs_3_), channel_id=1, source_target_pairs={{0,4},{1,5},{2,6},{3,7},{4,0},{5,1},{6,2},{7,3},{8,12},{9,13},{10,... | collective-permute-start | bytes 786440 | tf_op jit(solution)/shard_map/ppermute | solution.py:288
  44.2 12.6 %collective-permute-start.32 = (bf16[32,32,128]{2,1,0:T(8,128)(2,1)S(1)}, bf16[32,32,128]{2,1,0:T(8,128)(2,1)S(1)}, u32[]{:S(2)}, u32[]{:S(2)}) collective-permute-start(bf16[32,32,128]{2,1,0:T(8,128)(2,1)S(1)} %get-tuple-element.45), channel_id=1, source_target_pairs={{0,4},{1,5},{2,6},{3,7},{4,0},{5,1},{6,2},{7,3},{8,12},{9,13},{10,... | collective-permute-start | bytes 786440 | tf_op jit(solution)/shard_map/ppermute | solution.py:288
  57.3 2.1 %collective-permute-start.34 = (bf16[16,32,128]{2,1,0:T(8,128)(2,1)S(1)}, bf16[16,32,128]{2,1,0:T(8,128)(2,1)S(1)}, u32[]{:S(2)}, u32[]{:S(2)}) collective-permute-start(bf16[16,32,128]{2,1,0:T(8,128)(2,1)S(1)} %project.5), channel_id=1, source_target_pairs={{0,4},{1,5},{2,6},{3,7},{4,3},{5,2},{6,1},{7,0},{8,12},{9,13},{10,... | collective-permute-start | bytes 393224 | tf_op jit(solution)/shard_map/ppermute | solution.py:288
  57.4 3.5 %collective-permute-start.33 = (bf16[16,32,128]{2,1,0:T(8,128)(2,1)S(1)}, bf16[16,32,128]{2,1,0:T(8,128)(2,1)S(1)}, u32[]{:S(2)}, u32[]{:S(2)}) collective-permute-start(bf16[16,32,128]{2,1,0:T(8,128)(2,1)S(1)} %project.5), channel_id=1, source_target_pairs={{0,4},{1,5},{2,6},{3,7},{4,1},{5,0},{6,3},{7,2},{8,12},{9,13},{10,... | collective-permute-start | bytes 393224 | tf_op jit(solution)/shard_map/ppermute | solution.py:288
  58.9 2.6 %collective-permute-start.36 = (bf16[16,32,128]{2,1,0:T(8,128)(2,1)S(1)}, bf16[16,32,128]{2,1,0:T(8,128)(2,1)S(1)}, u32[]{:S(2)}, u32[]{:S(2)}) collective-permute-start(bf16[16,32,128]{2,1,0:T(8,128)(2,1)S(1)} %project.5), channel_id=1, source_target_pairs={{0,4},{1,5},{2,6},{3,7},{4,2},{5,3},{6,0},{7,1},{8,12},{9,13},{10,... | collective-permute-start | bytes 393224 | tf_op jit(solution)/shard_map/ppermute | solution.py:288
  58.9 2.6 %collective-permute-start.35 = (bf16[16,32,128]{2,1,0:T(8,128)(2,1)S(1)}, bf16[16,32,128]{2,1,0:T(8,128)(2,1)S(1)}, u32[]{:S(2)}, u32[]{:S(2)}) collective-permute-start(bf16[16,32,128]{2,1,0:T(8,128)(2,1)S(1)} %project.5), channel_id=1, source_target_pairs={{0,4},{1,5},{2,6},{3,7},{4,0},{5,1},{6,2},{7,3},{8,12},{9,13},{10,... | collective-permute-start | bytes 393224 | tf_op jit(solution)/shard_map/ppermute | solution.py:288
  59.4 2.1 %collective-permute-start.37 = (bf16[32,32,128]{2,1,0:T(8,128)(2,1)S(1)}, bf16[32,32,128]{2,1,0:T(8,128)(2,1)S(1)}, u32[]{:S(2)}, u32[]{:S(2)}) collective-permute-start(bf16[32,32,128]{2,1,0:T(8,128)(2,1)S(1)} %collective-permute-done.32.image), channel_id=1, source_target_pairs={{0,4},{1,5},{2,6},{3,7},{4,0},{5,1},{6,2},{7,3},{8,12},{9,13},{10,... | collective-permute-start | bytes 786440 | tf_op jit(solution)/shard_map/ppermute | solution.py:288
  61.5 6.5 %collective-permute-start.39 = (bf16[16,32,128]{2,1,0:T(8,128)(2,1)S(1)}, bf16[16,32,128]{2,1,0:T(8,128)(2,1)S(1)}, u32[]{:S(2)}, u32[]{:S(2)}) collective-permute-start(bf16[16,32,128]{2,1,0:T(8,128)(2,1)S(1)} %get-tuple-element.46), channel_id=1, source_target_pairs={{0,7},{1,6},{2,5},{3,4},{4,0},{5,1},{6,2},{7,3},{8,15},{9,14},{10,... | collective-permute-start | bytes 393224 | tf_op jit(solution)/shard_map/ppermute | solution.py:288
  64.6 4.5 %collective-permute-start.38 = (bf16[16,32,128]{2,1,0:T(8,128)(2,1)S(1)}, bf16[16,32,128]{2,1,0:T(8,128)(2,1)S(1)}, u32[]{:S(2)}, u32[]{:S(2)}) collective-permute-start(bf16[16,32,128]{2,1,0:T(8,128)(2,1)S(1)} %get-tuple-element.46), channel_id=1, source_target_pairs={{0,5},{1,4},{2,7},{3,6},{4,0},{5,1},{6,2},{7,3},{8,13},{9,12},{10,... | collective-permute-start | bytes 393224 | tf_op jit(solution)/shard_map/ppermute | solution.py:288
  64.7 4.7 %collective-permute-start.41 = (bf16[16,32,128]{2,1,0:T(8,128)(2,1)S(1)}, bf16[16,32,128]{2,1,0:T(8,128)(2,1)S(1)}, u32[]{:S(2)}, u32[]{:S(2)}) collective-permute-start(bf16[16,32,128]{2,1,0:T(8,128)(2,1)S(1)} %get-tuple-element.46), channel_id=1, source_target_pairs={{0,6},{1,7},{2,4},{3,5},{4,0},{5,1},{6,2},{7,3},{8,14},{9,15},{10,... | collective-permute-start | bytes 393224 | tf_op jit(solution)/shard_map/ppermute | solution.py:288
  65.6 3.8 %collective-permute-start.40 = (bf16[16,32,128]{2,1,0:T(8,128)(2,1)S(1)}, bf16[16,32,128]{2,1,0:T(8,128)(2,1)S(1)}, u32[]{:S(2)}, u32[]{:S(2)}) collective-permute-start(bf16[16,32,128]{2,1,0:T(8,128)(2,1)S(1)} %get-tuple-element.46), channel_id=1, source_target_pairs={{0,4},{1,5},{2,6},{3,7},{4,0},{5,1},{6,2},{7,3},{8,12},{9,13},{10,... | collective-permute-start | bytes 393224 | tf_op jit(solution)/shard_map/ppermute | solution.py:288
  65.9 4.1 %collective-permute-start.42 = (bf16[32,32,128]{2,1,0:T(8,128)(2,1)S(1)}, bf16[32,32,128]{2,1,0:T(8,128)(2,1)S(1)}, u32[]{:S(2)}, u32[]{:S(2)}) collective-permute-start(bf16[32,32,128]{2,1,0:T(8,128)(2,1)S(1)} %get-tuple-element.47.refs_3_), channel_id=1, source_target_pairs={{0,4},{1,5},{2,6},{3,7},{4,0},{5,1},{6,2},{7,3},{8,12},{9,13},{10,... | collective-permute-start | bytes 786440 | tf_op jit(solution)/shard_map/ppermute | solution.py:288

commit v21 on v14

--- a/solution.py
+++ b/solution.py
@@ -214,20 +214,35 @@
     refs = list(refs)
     info, change, image_in, shot = take(refs, 4)
     held = take(refs, 1) if place > 0 else []
-    image = None if last else take(refs, 1)[0]
-    (out,) = refs
+    sink, sems, image = None, None, None
+    if last:
+        sink, out, sems = refs
+    else:
+        image, out = refs
     batches, per_batch, _ = out.shape
 
-    def value(c):
-        return change[c] + image_in[c].astype(jnp.float32)
+    def value(where):
+        return change[where] + image_in[where].astype(jnp.float32)
 
     def write(source):
-        for c in range(CB):
-            if last:
-                block = source(c).reshape(batches, per_batch, BS)
-                out[:, :, c * BS : (c + 1) * BS] = block.astype(jnp.bfloat16)
-            else:
+        if not last:
+            for c in range(CB):
                 out[c] = source(c).astype(jnp.bfloat16)
+            return
+        parts = 2 if batches % 2 == 0 and batches * per_batch % 32 == 0 else 1
+        group = batches // parts
+        copies = []
+        for g in range(parts):
+            rows = slice(g * group * per_batch, (g + 1) * group * per_batch)
+            mine = slice(g * group, (g + 1) * group)
+            for c in range(CB):
+                block = source((c, rows)).reshape(group, per_batch, BS)
+                out[mine, :, c * BS : (c + 1) * BS] = block.astype(jnp.bfloat16)
+            where = pl.ds(g * group, group)
+            copies.append(pltpu.make_async_copy(out.at[where], sink.at[where], sems.at[g]))
+            copies[-1].start()
+        for copy in copies:
+            copy.wait()
 
     @pl.when(on_core(info, place, 1))
     def _():
@@ -237,13 +252,13 @@
 
     @pl.when(on_core(info, place, 0))
     def _():
-        write(lambda c: shot[c].astype(jnp.float32))
+        write(lambda where: shot[where].astype(jnp.float32))
 
     if held:
 
         @pl.when(info[0, 0] != place)
         def _():
-            write(lambda c: held[0][c].astype(jnp.float32))
+            write(lambda where: held[0][where].astype(jnp.float32))
 
 
 def per_device(blocks, block_rows, block_cols, sinogram):
@@ -422,16 +437,29 @@
             "first",
         )
         change = updated(place, 1, passed(terms, 0))
+        operands = [info, change, swapped(shot), shot] + held
+        if last:
+            images = pl.pallas_call(
+                functools.partial(second_kernel, place, last),
+                out_shape=final_out,
+                in_specs=[SMEM] + [VMEM] * (len(operands) - 1),
+                out_specs=pl.BlockSpec(memory_space=pl.ANY),
+                scratch_shapes=[
+                    pltpu.VMEM(final_out.shape, jnp.bfloat16),
+                    pltpu.SemaphoreType.DMA((2,)),
+                ],
+                compiler_params=PARAMS,
+                name="second",
+            )(*operands)
+            return images[None]
         outs = call(
             functools.partial(second_kernel, place, last),
             1,
-            [info, change, swapped(shot), shot] + held,
-            final_out if last else (image_out, image_out),
+            operands,
+            (image_out, image_out),
             [],
             "second",
         )
-        if last:
-            return outs[None]
         image = outs[0]
         held = [outs[1]]
 

time: 71.1 us -> 71.3 us (level)
    pallas_call x19 -> x18, Pallas kernels: 2.33 us -> 1.55 us  [call(): pl.pallas_call(kernel, out_shape=out_shape, in_specs=[SMEM] * smem + [VME...]
    pallas_call x0 -> x1, Pallas kernels: none -> 0.75 us  [per_device(): pl.pallas_call(functools.partial(second_kernel, place, last), out_shape=f...]
where the time goes in v21:
time: 71.3 us; the launch traced here: 71.1 us
  waiting for transfers between devices  35.8 us (50%)
  starting transfers between devices  27.7 us (39%)
  Pallas kernels  7.19 us (10%)
    ppermute x43, waiting for transfers between devices, sent(): return lax.ppermute(value, ('subset', 'tile'), pairs)  35.8 us
    ppermute x43, starting transfers between devices, sent(): return lax.ppermute(value, ('subset', 'tile'), pairs)  27.7 us
    pallas_call x1, Pallas kernels, per_device(): pl.pallas_call(functools.partial(head_kernel, row_blocks, chunks), out_sh...  3.09 us
    pallas_call x18, Pallas kernels, call(): pl.pallas_call(kernel, out_shape=out_shape, in_specs=[SMEM] * smem + [VME...  1.55 us
  transfers between devices with their start and end apart: 43, of which 18 were waited for; matrix products, arithmetic and copies ran while one was open for 0% of the time, Pallas kernels for 8%

profile of v21, /device:TPU:25, one launch (start us, length us, event | category | flops | bytes accessed | tf_op | source)
XLA Modules:
  0.0 71.1 jit_solution(2473854269951638189)
XLA Ops:
  0.0 0.7 collective-permute-start.1
  0.8 3.1 %head.1 = (bf16[5,32,128]{2,1,0:T(8,128)(2,1)S(1)}, s32[2,80]{1,0:T(2,128)S(1)}, s32[3,80]{1,0:T(4,128)S(4)}, bf16[1,1,80,128,128]{4,3,2,1,0:T(8,128)(2,1)S(1)}) custom-call(s32[3]{0:T(128)S(1)} %pad_add_fusion.pos, s32[1,1,80]{2,1,0:T(1,128)} %rows_in.1, s32[1,1,80]{2,1,0:T(1,128)} %cols_in.1, bf16[1,1,80,128,128]{4,3,2,1,0:T(8,128)(2,1)} %blocks_in.1, ...), custom_call_target="tpu_custom_call" | custom-call | tf_op jit(solution)/shard_map/head/pallas_call | solution.py:330
  3.9 2.2 %collective-permute-start.4 = (bf16[5,32,128]{2,1,0:T(8,128)(2,1)S(1)}, bf16[5,32,128]{2,1,0:T(8,128)(2,1)S(1)}, u32[]{:S(2)}, u32[]{:S(2)}) collective-permute-start(bf16[5,32,128]{2,1,0:T(8,128)(2,1)S(1)} %get-tuple-element.31._.refs_2_), channel_id=1, source_target_pairs={{0,3},{1,2},{2,1},{3,0},{4,7},{5,6},{6,5},{7,4},{8,11},{9,10},{10,... | collective-permute-start | bytes 122888 | tf_op jit(solution)/shard_map/ppermute | solution.py:294
  6.3 0.3 collective-permute-start.2
  6.6 0.8 %collective-permute-start = (s32[2,80]{1,0:T(2,128)S(1)}, s32[2,80]{1,0:T(2,128)S(1)}, u32[]{:S(2)}, u32[]{:S(2)}) collective-permute-start(s32[2,80]{1,0:T(2,128)S(1)} %get-tuple-element.28), channel_id=1, source_target_pairs={{0,4},{1,5},{2,6},{3,7},{4,0},{5,1},{6,2},{7,3},{8,12},{9,13},{10,... | collective-permute-start | bytes 1928 | tf_op jit(solution)/shard_map/ppermute | solution.py:294
  7.4 0.5 pack_own.1.refs_1_
  7.9 0.3 collective-permute-done.table2
  8.2 1.3 %pack_other.1 = (s32[3,80]{1,0:T(4,128)S(4)}, bf16[16,640,128]{2,1,0:T(8,128)(2,1)S(1)}) custom-call(s32[3,80]{1,0:T(4,128)S(4)} %get-tuple-element.27.own, s32[2,80]{1,0:T(2,128)S(1)} %collective-permute-done.table2, bf16[1,1,80,128,128]{4,3,2,1,0:T(8,128)(2,1)S(1)} %collective-permute-done.1.blocks2), custom_call_target="tpu_custom_call" | custom-call | tf_op jit(solution)/shard_map/pack_other/pallas_call | solution.py:371
  9.7 1.3 %collective-permute-start.8 = (bf16[16,32,128]{2,1,0:T(8,128)(2,1)S(1)}, bf16[16,32,128]{2,1,0:T(8,128)(2,1)S(1)}, u32[]{:S(2)}, u32[]{:S(2)}) collective-permute-start(bf16[16,32,128]{2,1,0:T(8,128)(2,1)S(1)} %get-tuple-element.35), channel_id=1, source_target_pairs={{0,7},{1,6},{2,5},{3,4},{4,0},{5,1},{6,2},{7,3},{8,15},{9,14},{10,... | collective-permute-start | bytes 393224 | tf_op jit(solution)/shard_map/ppermute | solution.py:294
  11.0 1.3 %collective-permute-start.7 = (bf16[16,32,128]{2,1,0:T(8,128)(2,1)S(1)}, bf16[16,32,128]{2,1,0:T(8,128)(2,1)S(1)}, u32[]{:S(2)}, u32[]{:S(2)}) collective-permute-start(bf16[16,32,128]{2,1,0:T(8,128)(2,1)S(1)} %get-tuple-element.35), channel_id=1, source_target_pairs={{0,6},{1,7},{2,4},{3,5},{4,0},{5,1},{6,2},{7,3},{8,14},{9,15},{10,... | collective-permute-start | bytes 393224 | tf_op jit(solution)/shard_map/ppermute | solution.py:294
  12.3 0.3 collective-permute-start.6
  12.6 0.3 collective-permute-start.5
  13.1 2.0 %collective-permute-done.8.refs_6_ = bf16[16,32,128]{2,1,0:T(8,128)(2,1)S(1)} collective-permute-done((bf16[16,32,128]{2,1,0:T(8,128)(2,1)S(1)}, bf16[16,32,128]{2,1,0:T(8,128)(2,1)S(1)}, u32[]{:S(2)}, u32[]{:S(2)}) %collective-permute-start.8) | collective-permute-done | bytes 131104 | tf_op jit(solution)/shard_map/ppermute | solution.py:294
  15.1 1.3 %collective-permute-done.7.refs_5_ = bf16[16,32,128]{2,1,0:T(8,128)(2,1)S(1)} collective-permute-done((bf16[16,32,128]{2,1,0:T(8,128)(2,1)S(1)}, bf16[16,32,128]{2,1,0:T(8,128)(2,1)S(1)}, u32[]{:S(2)}, u32[]{:S(2)}) %collective-permute-start.7) | collective-permute-done | bytes 131104 | tf_op jit(solution)/shard_map/ppermute | solution.py:294
  16.4 0.3 collective-permute-done.6.refs_4_
  16.8 1.5 %collective-permute-done.10.image = bf16[32,32,128]{2,1,0:T(8,128)(2,1)S(1)} collective-permute-done((bf16[32,32,128]{2,1,0:T(8,128)(2,1)S(1)}, bf16[32,32,128]{2,1,0:T(8,128)(2,1)S(1)}, u32[]{:S(2)}, u32[]{:S(2)}) %collective-permute-start.10) | collective-permute-done | bytes 262176 | tf_op jit(solution)/shard_map/ppermute | solution.py:294
  18.3 1.4 %collective-permute-start.14 = (bf16[16,32,128]{2,1,0:T(8,128)(2,1)S(1)}, bf16[16,32,128]{2,1,0:T(8,128)(2,1)S(1)}, u32[]{:S(2)}, u32[]{:S(2)}) collective-permute-start(bf16[16,32,128]{2,1,0:T(8,128)(2,1)S(1)} %project.3), channel_id=1, source_target_pairs={{0,4},{1,5},{2,6},{3,7},{4,3},{5,2},{6,1},{7,0},{8,12},{9,13},{10,... | collective-permute-start | bytes 393224 | tf_op jit(solution)/shard_map/ppermute | solution.py:294
  19.7 1.2 %collective-permute-start.12 = (bf16[16,32,128]{2,1,0:T(8,128)(2,1)S(1)}, bf16[16,32,128]{2,1,0:T(8,128)(2,1)S(1)}, u32[]{:S(2)}, u32[]{:S(2)}) collective-permute-start(bf16[16,32,128]{2,1,0:T(8,128)(2,1)S(1)} %project.3), channel_id=1, source_target_pairs={{0,4},{1,5},{2,6},{3,7},{4,1},{5,0},{6,3},{7,2},{8,12},{9,13},{10,... | collective-permute-start | bytes 393224 | tf_op jit(solution)/shard_map/ppermute | solution.py:294
  20.9 0.5 collective-permute-start.15
  21.6 1.4 %collective-permute-done.13.refs_5_ = bf16[16,32,128]{2,1,0:T(8,128)(2,1)S(1)} collective-permute-done((bf16[16,32,128]{2,1,0:T(8,128)(2,1)S(1)}, bf16[16,32,128]{2,1,0:T(8,128)(2,1)S(1)}, u32[]{:S(2)}, u32[]{:S(2)}) %collective-permute-start.13) | collective-permute-done | bytes 131104 | tf_op jit(solution)/shard_map/ppermute | solution.py:294
  23.0 2.1 %collective-permute-start.19 = (bf16[16,32,128]{2,1,0:T(8,128)(2,1)S(1)}, bf16[16,32,128]{2,1,0:T(8,128)(2,1)S(1)}, u32[]{:S(2)}, u32[]{:S(2)}) collective-permute-start(bf16[16,32,128]{2,1,0:T(8,128)(2,1)S(1)} %get-tuple-element.38), channel_id=1, source_target_pairs={{0,7},{1,6},{2,5},{3,4},{4,0},{5,1},{6,2},{7,3},{8,15},{9,14},{10,... | collective-permute-start | bytes 393224 | tf_op jit(solution)/shard_map/ppermute | solution.py:294
  25.2 0.9 %collective-permute-start.17 = (bf16[16,32,128]{2,1,0:T(8,128)(2,1)S(1)}, bf16[16,32,128]{2,1,0:T(8,128)(2,1)S(1)}, u32[]{:S(2)}, u32[]{:S(2)}) collective-permute-start(bf16[16,32,128]{2,1,0:T(8,128)(2,1)S(1)} %get-tuple-element.38), channel_id=1, source_target_pairs={{0,5},{1,4},{2,7},{3,6},{4,0},{5,1},{6,2},{7,3},{8,13},{9,12},{10,... | collective-permute-start | bytes 393224 | tf_op jit(solution)/shard_map/ppermute | solution.py:294
  26.2 0.4 collective-permute-start.20
  26.6 2.3 %collective-permute-done.19.refs_6_ = bf16[16,32,128]{2,1,0:T(8,128)(2,1)S(1)} collective-permute-done((bf16[16,32,128]{2,1,0:T(8,128)(2,1)S(1)}, bf16[16,32,128]{2,1,0:T(8,128)(2,1)S(1)}, u32[]{:S(2)}, u32[]{:S(2)}) %collective-permute-start.19) | collective-permute-done | bytes 131104 | tf_op jit(solution)/shard_map/ppermute | solution.py:294
  28.9 1.3 %collective-permute-done.18.refs_5_ = bf16[16,32,128]{2,1,0:T(8,128)(2,1)S(1)} collective-permute-done((bf16[16,32,128]{2,1,0:T(8,128)(2,1)S(1)}, bf16[16,32,128]{2,1,0:T(8,128)(2,1)S(1)}, u32[]{:S(2)}, u32[]{:S(2)}) %collective-permute-start.18) | collective-permute-done | bytes 131104 | tf_op jit(solution)/shard_map/ppermute | solution.py:294
  30.4 1.5 %collective-permute-done.21.image = bf16[32,32,128]{2,1,0:T(8,128)(2,1)S(1)} collective-permute-done((bf16[32,32,128]{2,1,0:T(8,128)(2,1)S(1)}, bf16[32,32,128]{2,1,0:T(8,128)(2,1)S(1)}, u32[]{:S(2)}, u32[]{:S(2)}) %collective-permute-start.21) | collective-permute-done | bytes 262176 | tf_op jit(solution)/shard_map/ppermute | solution.py:294
  31.9 1.2 %collective-permute-start.25 = (bf16[16,32,128]{2,1,0:T(8,128)(2,1)S(1)}, bf16[16,32,128]{2,1,0:T(8,128)(2,1)S(1)}, u32[]{:S(2)}, u32[]{:S(2)}) collective-permute-start(bf16[16,32,128]{2,1,0:T(8,128)(2,1)S(1)} %project.4), channel_id=1, source_target_pairs={{0,4},{1,5},{2,6},{3,7},{4,3},{5,2},{6,1},{7,0},{8,12},{9,13},{10,... | collective-permute-start | bytes 393224 | tf_op jit(solution)/shard_map/ppermute | solution.py:294
  33.1 1.0 %collective-permute-start.23 = (bf16[16,32,128]{2,1,0:T(8,128)(2,1)S(1)}, bf16[16,32,128]{2,1,0:T(8,128)(2,1)S(1)}, u32[]{:S(2)}, u32[]{:S(2)}) collective-permute-start(bf16[16,32,128]{2,1,0:T(8,128)(2,1)S(1)} %project.4), channel_id=1, source_target_pairs={{0,4},{1,5},{2,6},{3,7},{4,1},{5,0},{6,3},{7,2},{8,12},{9,13},{10,... | collective-permute-start | bytes 393224 | tf_op jit(solution)/shard_map/ppermute | solution.py:294
  34.2 0.5 collective-permute-start.26
  34.7 0.4 collective-permute-done.25.refs_6_
  35.1 1.4 %collective-permute-done.24.refs_5_ = bf16[16,32,128]{2,1,0:T(8,128)(2,1)S(1)} collective-permute-done((bf16[16,32,128]{2,1,0:T(8,128)(2,1)S(1)}, bf16[16,32,128]{2,1,0:T(8,128)(2,1)S(1)}, u32[]{:S(2)}, u32[]{:S(2)}) %collective-permute-start.24) | collective-permute-done | bytes 131104 | tf_op jit(solution)/shard_map/ppermute | solution.py:294
  36.5 1.9 %collective-permute-start.30 = (bf16[16,32,128]{2,1,0:T(8,128)(2,1)S(1)}, bf16[16,32,128]{2,1,0:T(8,128)(2,1)S(1)}, u32[]{:S(2)}, u32[]{:S(2)}) collective-permute-start(bf16[16,32,128]{2,1,0:T(8,128)(2,1)S(1)} %get-tuple-element.42), channel_id=1, source_target_pairs={{0,7},{1,6},{2,5},{3,4},{4,0},{5,1},{6,2},{7,3},{8,15},{9,14},{10,... | collective-permute-start | bytes 393224 | tf_op jit(solution)/shard_map/ppermute | solution.py:294
  38.4 1.2 %collective-permute-start.28 = (bf16[16,32,128]{2,1,0:T(8,128)(2,1)S(1)}, bf16[16,32,128]{2,1,0:T(8,128)(2,1)S(1)}, u32[]{:S(2)}, u32[]{:S(2)}) collective-permute-start(bf16[16,32,128]{2,1,0:T(8,128)(2,1)S(1)} %get-tuple-element.42), channel_id=1, source_target_pairs={{0,5},{1,4},{2,7},{3,6},{4,0},{5,1},{6,2},{7,3},{8,13},{9,12},{10,... | collective-permute-start | bytes 393224 | tf_op jit(solution)/shard_map/ppermute | solution.py:294
  39.6 0.5 collective-permute-start.31
  40.1 2.0 %collective-permute-done.30.refs_6_ = bf16[16,32,128]{2,1,0:T(8,128)(2,1)S(1)} collective-permute-done((bf16[16,32,128]{2,1,0:T(8,128)(2,1)S(1)}, bf16[16,32,128]{2,1,0:T(8,128)(2,1)S(1)}, u32[]{:S(2)}, u32[]{:S(2)}) %collective-permute-start.30) | collective-permute-done | bytes 131104 | tf_op jit(solution)/shard_map/ppermute | solution.py:294
  42.1 1.3 %collective-permute-done.29.refs_5_ = bf16[16,32,128]{2,1,0:T(8,128)(2,1)S(1)} collective-permute-done((bf16[16,32,128]{2,1,0:T(8,128)(2,1)S(1)}, bf16[16,32,128]{2,1,0:T(8,128)(2,1)S(1)}, u32[]{:S(2)}, u32[]{:S(2)}) %collective-permute-start.29) | collective-permute-done | bytes 131104 | tf_op jit(solution)/shard_map/ppermute | solution.py:294
  43.8 13.1 %collective-permute-done.32.image = bf16[32,32,128]{2,1,0:T(8,128)(2,1)S(1)} collective-permute-done((bf16[32,32,128]{2,1,0:T(8,128)(2,1)S(1)}, bf16[32,32,128]{2,1,0:T(8,128)(2,1)S(1)}, u32[]{:S(2)}, u32[]{:S(2)}) %collective-permute-start.32) | collective-permute-done | bytes 262176 | tf_op jit(solution)/shard_map/ppermute | solution.py:294
  56.9 0.5 project.5
  57.5 1.4 %collective-permute-start.35 = (bf16[16,32,128]{2,1,0:T(8,128)(2,1)S(1)}, bf16[16,32,128]{2,1,0:T(8,128)(2,1)S(1)}, u32[]{:S(2)}, u32[]{:S(2)}) collective-permute-start(bf16[16,32,128]{2,1,0:T(8,128)(2,1)S(1)} %project.5), channel_id=1, source_target_pairs={{0,4},{1,5},{2,6},{3,7},{4,2},{5,3},{6,0},{7,1},{8,12},{9,13},{10,... | collective-permute-start | bytes 393224 | tf_op jit(solution)/shard_map/ppermute | solution.py:294
  59.0 0.4 collective-permute-start.33
  59.6 2.1 %collective-permute-done.35.refs_5_ = bf16[16,32,128]{2,1,0:T(8,128)(2,1)S(1)} collective-permute-done((bf16[16,32,128]{2,1,0:T(8,128)(2,1)S(1)}, bf16[16,32,128]{2,1,0:T(8,128)(2,1)S(1)}, u32[]{:S(2)}, u32[]{:S(2)}) %collective-permute-start.35) | collective-permute-done | bytes 131104 | tf_op jit(solution)/shard_map/ppermute | solution.py:294
  61.7 3.0 %collective-permute-start.41 = (bf16[16,32,128]{2,1,0:T(8,128)(2,1)S(1)}, bf16[16,32,128]{2,1,0:T(8,128)(2,1)S(1)}, u32[]{:S(2)}, u32[]{:S(2)}) collective-permute-start(bf16[16,32,128]{2,1,0:T(8,128)(2,1)S(1)} %get-tuple-element.46), channel_id=1, source_target_pairs={{0,7},{1,6},{2,5},{3,4},{4,0},{5,1},{6,2},{7,3},{8,15},{9,14},{10,... | collective-permute-start | bytes 393224 | tf_op jit(solution)/shard_map/ppermute | solution.py:294
  64.7 1.2 %collective-permute-start.39 = (bf16[16,32,128]{2,1,0:T(8,128)(2,1)S(1)}, bf16[16,32,128]{2,1,0:T(8,128)(2,1)S(1)}, u32[]{:S(2)}, u32[]{:S(2)}) collective-permute-start(bf16[16,32,128]{2,1,0:T(8,128)(2,1)S(1)} %get-tuple-element.46), channel_id=1, source_target_pairs={{0,5},{1,4},{2,7},{3,6},{4,0},{5,1},{6,2},{7,3},{8,13},{9,12},{10,... | collective-permute-start | bytes 393224 | tf_op jit(solution)/shard_map/ppermute | solution.py:294
  65.9 0.5 collective-permute-start.42
  66.4 1.8 %collective-permute-done.41.refs_6_ = bf16[16,32,128]{2,1,0:T(8,128)(2,1)S(1)} collective-permute-done((bf16[16,32,128]{2,1,0:T(8,128)(2,1)S(1)}, bf16[16,32,128]{2,1,0:T(8,128)(2,1)S(1)}, u32[]{:S(2)}, u32[]{:S(2)}) %collective-permute-start.41) | collective-permute-done | bytes 131104 | tf_op jit(solution)/shard_map/ppermute | solution.py:294
  68.2 1.3 %collective-permute-done.40.refs_5_ = bf16[16,32,128]{2,1,0:T(8,128)(2,1)S(1)} collective-permute-done((bf16[16,32,128]{2,1,0:T(8,128)(2,1)S(1)}, bf16[16,32,128]{2,1,0:T(8,128)(2,1)S(1)}, u32[]{:S(2)}, u32[]{:S(2)}) %collective-permute-start.40) | collective-permute-done | bytes 131104 | tf_op jit(solution)/shard_map/ppermute | solution.py:294
  69.6 0.6 update.15.refs_1_
  70.2 0.7 %second.7 = bf16[4,8,4096]{2,1,0:T(8,128)(2,1)} custom-call(s32[3,80]{1,0:T(4,128)S(4)} %get-tuple-element.29.refs_0_.info, f32[32,32,128]{2,1,0:T(8,128)S(1)} %update.15.refs_1_, bf16[32,32,128]{2,1,0:T(8,128)(2,1)S(1)} %collective-permute-done.42.refs_2_, bf16[32,32,128]{2,1,0:T(8,128)(2,1)S(1)} %get-tuple-element.47.refs_3_, ...), custom_call_target="tpu_custom_call" | custom-call | tf_op jit(solution)/shard_map/second/pallas_call | solution.py:442
  (61 shorter events, 2.2 us)
Async XLA Ops:
  0.0 8.2 %collective-permute-start.1 = (bf16[1,1,80,128,128]{4,3,2,1,0:T(8,128)(2,1)}, bf16[1,1,80,128,128]{4,3,2,1,0:T(8,128)(2,1)S(1)}, u32[]{:S(2)}, u32[]{:S(2)}) collective-permute-start(bf16[1,1,80,128,128]{4,3,2,1,0:T(8,128)(2,1)} %blocks_in.1), channel_id=1, source_target_pairs={{0,4},{1,5},{2,6},{3,7},{4,0},{5,1},{6,2},{7,3},{8,12},{9,13},{10,... | collective-permute-start | bytes 7864328 | tf_op jit(solution)/shard_map/ppermute | solution.py:294
  3.9 5.7 %collective-permute-start.4 = (bf16[5,32,128]{2,1,0:T(8,128)(2,1)S(1)}, bf16[5,32,128]{2,1,0:T(8,128)(2,1)S(1)}, u32[]{:S(2)}, u32[]{:S(2)}) collective-permute-start(bf16[5,32,128]{2,1,0:T(8,128)(2,1)S(1)} %get-tuple-element.31._.refs_2_), channel_id=1, source_target_pairs={{0,3},{1,2},{2,1},{3,0},{4,7},{5,6},{6,5},{7,4},{8,11},{9,10},{10,... | collective-permute-start | bytes 122888 | tf_op jit(solution)/shard_map/ppermute | solution.py:294
  6.1 3.5 %collective-permute-start.3 = (bf16[5,32,128]{2,1,0:T(8,128)(2,1)S(1)}, bf16[5,32,128]{2,1,0:T(8,128)(2,1)S(1)}, u32[]{:S(2)}, u32[]{:S(2)}) collective-permute-start(bf16[5,32,128]{2,1,0:T(8,128)(2,1)S(1)} %get-tuple-element.31._.refs_2_), channel_id=1, source_target_pairs={{0,2},{1,3},{2,0},{3,1},{4,6},{5,7},{6,4},{7,5},{8,10},{9,11},{10,... | collective-permute-start | bytes 122888 | tf_op jit(solution)/shard_map/ppermute | solution.py:294
  6.3 3.3 %collective-permute-start.2 = (bf16[5,32,128]{2,1,0:T(8,128)(2,1)S(1)}, bf16[5,32,128]{2,1,0:T(8,128)(2,1)S(1)}, u32[]{:S(2)}, u32[]{:S(2)}) collective-permute-start(bf16[5,32,128]{2,1,0:T(8,128)(2,1)S(1)} %get-tuple-element.31._.refs_2_), channel_id=1, source_target_pairs={{0,1},{1,0},{2,3},{3,2},{4,5},{5,4},{6,7},{7,6},{8,9},{9,8},{10,11... | collective-permute-start | bytes 122888 | tf_op jit(solution)/shard_map/ppermute | solution.py:294
  6.6 1.7 %collective-permute-start = (s32[2,80]{1,0:T(2,128)S(1)}, s32[2,80]{1,0:T(2,128)S(1)}, u32[]{:S(2)}, u32[]{:S(2)}) collective-permute-start(s32[2,80]{1,0:T(2,128)S(1)} %get-tuple-element.28), channel_id=1, source_target_pairs={{0,4},{1,5},{2,6},{3,7},{4,0},{5,1},{6,2},{7,3},{8,12},{9,13},{10,... | collective-permute-start | bytes 1928 | tf_op jit(solution)/shard_map/ppermute | solution.py:294
  9.7 5.4 %collective-permute-start.8 = (bf16[16,32,128]{2,1,0:T(8,128)(2,1)S(1)}, bf16[16,32,128]{2,1,0:T(8,128)(2,1)S(1)}, u32[]{:S(2)}, u32[]{:S(2)}) collective-permute-start(bf16[16,32,128]{2,1,0:T(8,128)(2,1)S(1)} %get-tuple-element.35), channel_id=1, source_target_pairs={{0,7},{1,6},{2,5},{3,4},{4,0},{5,1},{6,2},{7,3},{8,15},{9,14},{10,... | collective-permute-start | bytes 393224 | tf_op jit(solution)/shard_map/ppermute | solution.py:294
  11.0 5.4 %collective-permute-start.7 = (bf16[16,32,128]{2,1,0:T(8,128)(2,1)S(1)}, bf16[16,32,128]{2,1,0:T(8,128)(2,1)S(1)}, u32[]{:S(2)}, u32[]{:S(2)}) collective-permute-start(bf16[16,32,128]{2,1,0:T(8,128)(2,1)S(1)} %get-tuple-element.35), channel_id=1, source_target_pairs={{0,6},{1,7},{2,4},{3,5},{4,0},{5,1},{6,2},{7,3},{8,14},{9,15},{10,... | collective-permute-start | bytes 393224 | tf_op jit(solution)/shard_map/ppermute | solution.py:294
  12.3 4.4 %collective-permute-start.6 = (bf16[16,32,128]{2,1,0:T(8,128)(2,1)S(1)}, bf16[16,32,128]{2,1,0:T(8,128)(2,1)S(1)}, u32[]{:S(2)}, u32[]{:S(2)}) collective-permute-start(bf16[16,32,128]{2,1,0:T(8,128)(2,1)S(1)} %get-tuple-element.35), channel_id=1, source_target_pairs={{0,5},{1,4},{2,7},{3,6},{4,0},{5,1},{6,2},{7,3},{8,13},{9,12},{10,... | collective-permute-start | bytes 393224 | tf_op jit(solution)/shard_map/ppermute | solution.py:294
  12.6 4.1 %collective-permute-start.5 = (bf16[16,32,128]{2,1,0:T(8,128)(2,1)S(1)}, bf16[16,32,128]{2,1,0:T(8,128)(2,1)S(1)}, u32[]{:S(2)}, u32[]{:S(2)}) collective-permute-start(bf16[16,32,128]{2,1,0:T(8,128)(2,1)S(1)} %get-tuple-element.35), channel_id=1, source_target_pairs={{0,4},{1,5},{2,6},{3,7},{4,0},{5,1},{6,2},{7,3},{8,12},{9,13},{10,... | collective-permute-start | bytes 393224 | tf_op jit(solution)/shard_map/ppermute | solution.py:294
  12.9 3.7 %collective-permute-start.9 = (bf16[32,32,128]{2,1,0:T(8,128)(2,1)S(1)}, bf16[32,32,128]{2,1,0:T(8,128)(2,1)S(1)}, u32[]{:S(2)}, u32[]{:S(2)}) collective-permute-start(bf16[32,32,128]{2,1,0:T(8,128)(2,1)S(1)} %get-tuple-element.36.refs_3_), channel_id=1, source_target_pairs={{0,4},{1,5},{2,6},{3,7},{4,0},{5,1},{6,2},{7,3},{8,12},{9,13},{10,... | collective-permute-start | bytes 786440 | tf_op jit(solution)/shard_map/ppermute | solution.py:294
  16.7 1.6 %collective-permute-start.10 = (bf16[32,32,128]{2,1,0:T(8,128)(2,1)S(1)}, bf16[32,32,128]{2,1,0:T(8,128)(2,1)S(1)}, u32[]{:S(2)}, u32[]{:S(2)}) collective-permute-start(bf16[32,32,128]{2,1,0:T(8,128)(2,1)S(1)} %get-tuple-element.37), channel_id=1, source_target_pairs={{0,4},{1,5},{2,6},{3,7},{4,12},{5,13},{6,14},{7,15},{8,0},{9,1},{1... | collective-permute-start | bytes 786440 | tf_op jit(solution)/shard_map/ppermute | solution.py:294
  18.3 3.3 %collective-permute-start.14 = (bf16[16,32,128]{2,1,0:T(8,128)(2,1)S(1)}, bf16[16,32,128]{2,1,0:T(8,128)(2,1)S(1)}, u32[]{:S(2)}, u32[]{:S(2)}) collective-permute-start(bf16[16,32,128]{2,1,0:T(8,128)(2,1)S(1)} %project.3), channel_id=1, source_target_pairs={{0,4},{1,5},{2,6},{3,7},{4,3},{5,2},{6,1},{7,0},{8,12},{9,13},{10,... | collective-permute-start | bytes 393224 | tf_op jit(solution)/shard_map/ppermute | solution.py:294
  19.7 3.3 %collective-permute-start.13 = (bf16[16,32,128]{2,1,0:T(8,128)(2,1)S(1)}, bf16[16,32,128]{2,1,0:T(8,128)(2,1)S(1)}, u32[]{:S(2)}, u32[]{:S(2)}) collective-permute-start(bf16[16,32,128]{2,1,0:T(8,128)(2,1)S(1)} %project.3), channel_id=1, source_target_pairs={{0,4},{1,5},{2,6},{3,7},{4,2},{5,3},{6,0},{7,1},{8,12},{9,13},{10,... | collective-permute-start | bytes 393224 | tf_op jit(solution)/shard_map/ppermute | solution.py:294
  19.7 3.3 %collective-permute-start.12 = (bf16[16,32,128]{2,1,0:T(8,128)(2,1)S(1)}, bf16[16,32,128]{2,1,0:T(8,128)(2,1)S(1)}, u32[]{:S(2)}, u32[]{:S(2)}) collective-permute-start(bf16[16,32,128]{2,1,0:T(8,128)(2,1)S(1)} %project.3), channel_id=1, source_target_pairs={{0,4},{1,5},{2,6},{3,7},{4,1},{5,0},{6,3},{7,2},{8,12},{9,13},{10,... | collective-permute-start | bytes 393224 | tf_op jit(solution)/shard_map/ppermute | solution.py:294
  20.9 2.1 %collective-permute-start.11 = (bf16[16,32,128]{2,1,0:T(8,128)(2,1)S(1)}, bf16[16,32,128]{2,1,0:T(8,128)(2,1)S(1)}, u32[]{:S(2)}, u32[]{:S(2)}) collective-permute-start(bf16[16,32,128]{2,1,0:T(8,128)(2,1)S(1)} %project.3), channel_id=1, source_target_pairs={{0,4},{1,5},{2,6},{3,7},{4,0},{5,1},{6,2},{7,3},{8,12},{9,13},{10,... | collective-permute-start | bytes 393224 | tf_op jit(solution)/shard_map/ppermute | solution.py:294
  20.9 2.1 %collective-permute-start.15 = (bf16[32,32,128]{2,1,0:T(8,128)(2,1)S(1)}, bf16[32,32,128]{2,1,0:T(8,128)(2,1)S(1)}, u32[]{:S(2)}, u32[]{:S(2)}) collective-permute-start(bf16[32,32,128]{2,1,0:T(8,128)(2,1)S(1)} %collective-permute-done.10.image), channel_id=1, source_target_pairs={{0,4},{1,5},{2,6},{3,7},{4,0},{5,1},{6,2},{7,3},{8,12},{9,13},{10,... | collective-permute-start | bytes 786440 | tf_op jit(solution)/shard_map/ppermute | solution.py:294
  23.0 5.9 %collective-permute-start.19 = (bf16[16,32,128]{2,1,0:T(8,128)(2,1)S(1)}, bf16[16,32,128]{2,1,0:T(8,128)(2,1)S(1)}, u32[]{:S(2)}, u32[]{:S(2)}) collective-permute-start(bf16[16,32,128]{2,1,0:T(8,128)(2,1)S(1)} %get-tuple-element.38), channel_id=1, source_target_pairs={{0,7},{1,6},{2,5},{3,4},{4,0},{5,1},{6,2},{7,3},{8,15},{9,14},{10,... | collective-permute-start | bytes 393224 | tf_op jit(solution)/shard_map/ppermute | solution.py:294
  25.1 5.2 %collective-permute-start.18 = (bf16[16,32,128]{2,1,0:T(8,128)(2,1)S(1)}, bf16[16,32,128]{2,1,0:T(8,128)(2,1)S(1)}, u32[]{:S(2)}, u32[]{:S(2)}) collective-permute-start(bf16[16,32,128]{2,1,0:T(8,128)(2,1)S(1)} %get-tuple-element.38), channel_id=1, source_target_pairs={{0,6},{1,7},{2,4},{3,5},{4,0},{5,1},{6,2},{7,3},{8,14},{9,15},{10,... | collective-permute-start | bytes 393224 | tf_op jit(solution)/shard_map/ppermute | solution.py:294
  25.2 5.1 %collective-permute-start.17 = (bf16[16,32,128]{2,1,0:T(8,128)(2,1)S(1)}, bf16[16,32,128]{2,1,0:T(8,128)(2,1)S(1)}, u32[]{:S(2)}, u32[]{:S(2)}) collective-permute-start(bf16[16,32,128]{2,1,0:T(8,128)(2,1)S(1)} %get-tuple-element.38), channel_id=1, source_target_pairs={{0,5},{1,4},{2,7},{3,6},{4,0},{5,1},{6,2},{7,3},{8,13},{9,12},{10,... | collective-permute-start | bytes 393224 | tf_op jit(solution)/shard_map/ppermute | solution.py:294
  26.1 4.2 %collective-permute-start.16 = (bf16[16,32,128]{2,1,0:T(8,128)(2,1)S(1)}, bf16[16,32,128]{2,1,0:T(8,128)(2,1)S(1)}, u32[]{:S(2)}, u32[]{:S(2)}) collective-permute-start(bf16[16,32,128]{2,1,0:T(8,128)(2,1)S(1)} %get-tuple-element.38), channel_id=1, source_target_pairs={{0,4},{1,5},{2,6},{3,7},{4,0},{5,1},{6,2},{7,3},{8,12},{9,13},{10,... | collective-permute-start | bytes 393224 | tf_op jit(solution)/shard_map/ppermute | solution.py:294
  26.2 4.0 %collective-permute-start.20 = (bf16[32,32,128]{2,1,0:T(8,128)(2,1)S(1)}, bf16[32,32,128]{2,1,0:T(8,128)(2,1)S(1)}, u32[]{:S(2)}, u32[]{:S(2)}) collective-permute-start(bf16[32,32,128]{2,1,0:T(8,128)(2,1)S(1)} %get-tuple-element.39.refs_3_), channel_id=1, source_target_pairs={{0,4},{1,5},{2,6},{3,7},{4,0},{5,1},{6,2},{7,3},{8,12},{9,13},{10,... | collective-permute-start | bytes 786440 | tf_op jit(solution)/shard_map/ppermute | solution.py:294
  30.3 1.6 %collective-permute-start.21 = (bf16[32,32,128]{2,1,0:T(8,128)(2,1)S(1)}, bf16[32,32,128]{2,1,0:T(8,128)(2,1)S(1)}, u32[]{:S(2)}, u32[]{:S(2)}) collective-permute-start(bf16[32,32,128]{2,1,0:T(8,128)(2,1)S(1)} %get-tuple-element.41), channel_id=1, source_target_pairs={{0,4},{1,5},{2,6},{3,7},{4,0},{5,1},{6,2},{7,3},{8,12},{9,13},{10,... | collective-permute-start | bytes 786440 | tf_op jit(solution)/shard_map/ppermute | solution.py:294
  31.9 3.1 %collective-permute-start.25 = (bf16[16,32,128]{2,1,0:T(8,128)(2,1)S(1)}, bf16[16,32,128]{2,1,0:T(8,128)(2,1)S(1)}, u32[]{:S(2)}, u32[]{:S(2)}) collective-permute-start(bf16[16,32,128]{2,1,0:T(8,128)(2,1)S(1)} %project.4), channel_id=1, source_target_pairs={{0,4},{1,5},{2,6},{3,7},{4,3},{5,2},{6,1},{7,0},{8,12},{9,13},{10,... | collective-permute-start | bytes 393224 | tf_op jit(solution)/shard_map/ppermute | solution.py:294
  33.1 3.3 %collective-permute-start.24 = (bf16[16,32,128]{2,1,0:T(8,128)(2,1)S(1)}, bf16[16,32,128]{2,1,0:T(8,128)(2,1)S(1)}, u32[]{:S(2)}, u32[]{:S(2)}) collective-permute-start(bf16[16,32,128]{2,1,0:T(8,128)(2,1)S(1)} %project.4), channel_id=1, source_target_pairs={{0,4},{1,5},{2,6},{3,7},{4,2},{5,3},{6,0},{7,1},{8,12},{9,13},{10,... | collective-permute-start | bytes 393224 | tf_op jit(solution)/shard_map/ppermute | solution.py:294
  33.1 3.4 %collective-permute-start.23 = (bf16[16,32,128]{2,1,0:T(8,128)(2,1)S(1)}, bf16[16,32,128]{2,1,0:T(8,128)(2,1)S(1)}, u32[]{:S(2)}, u32[]{:S(2)}) collective-permute-start(bf16[16,32,128]{2,1,0:T(8,128)(2,1)S(1)} %project.4), channel_id=1, source_target_pairs={{0,4},{1,5},{2,6},{3,7},{4,1},{5,0},{6,3},{7,2},{8,12},{9,13},{10,... | collective-permute-start | bytes 393224 | tf_op jit(solution)/shard_map/ppermute | solution.py:294
  34.2 2.3 %collective-permute-start.22 = (bf16[16,32,128]{2,1,0:T(8,128)(2,1)S(1)}, bf16[16,32,128]{2,1,0:T(8,128)(2,1)S(1)}, u32[]{:S(2)}, u32[]{:S(2)}) collective-permute-start(bf16[16,32,128]{2,1,0:T(8,128)(2,1)S(1)} %project.4), channel_id=1, source_target_pairs={{0,4},{1,5},{2,6},{3,7},{4,0},{5,1},{6,2},{7,3},{8,12},{9,13},{10,... | collective-permute-start | bytes 393224 | tf_op jit(solution)/shard_map/ppermute | solution.py:294
  34.2 2.3 %collective-permute-start.26 = (bf16[32,32,128]{2,1,0:T(8,128)(2,1)S(1)}, bf16[32,32,128]{2,1,0:T(8,128)(2,1)S(1)}, u32[]{:S(2)}, u32[]{:S(2)}) collective-permute-start(bf16[32,32,128]{2,1,0:T(8,128)(2,1)S(1)} %collective-permute-done.21.image), channel_id=1, source_target_pairs={{0,4},{1,5},{2,6},{3,7},{4,0},{5,1},{6,2},{7,3},{8,12},{9,13},{10,... | collective-permute-start | bytes 786440 | tf_op jit(solution)/shard_map/ppermute | solution.py:294
  36.5 5.6 %collective-permute-start.30 = (bf16[16,32,128]{2,1,0:T(8,128)(2,1)S(1)}, bf16[16,32,128]{2,1,0:T(8,128)(2,1)S(1)}, u32[]{:S(2)}, u32[]{:S(2)}) collective-permute-start(bf16[16,32,128]{2,1,0:T(8,128)(2,1)S(1)} %get-tuple-element.42), channel_id=1, source_target_pairs={{0,7},{1,6},{2,5},{3,4},{4,0},{5,1},{6,2},{7,3},{8,15},{9,14},{10,... | collective-permute-start | bytes 393224 | tf_op jit(solution)/shard_map/ppermute | solution.py:294
  38.3 5.1 %collective-permute-start.29 = (bf16[16,32,128]{2,1,0:T(8,128)(2,1)S(1)}, bf16[16,32,128]{2,1,0:T(8,128)(2,1)S(1)}, u32[]{:S(2)}, u32[]{:S(2)}) collective-permute-start(bf16[16,32,128]{2,1,0:T(8,128)(2,1)S(1)} %get-tuple-element.42), channel_id=1, source_target_pairs={{0,6},{1,7},{2,4},{3,5},{4,0},{5,1},{6,2},{7,3},{8,14},{9,15},{10,... | collective-permute-start | bytes 393224 | tf_op jit(solution)/shard_map/ppermute | solution.py:294
  38.4 5.0 %collective-permute-start.28 = (bf16[16,32,128]{2,1,0:T(8,128)(2,1)S(1)}, bf16[16,32,128]{2,1,0:T(8,128)(2,1)S(1)}, u32[]{:S(2)}, u32[]{:S(2)}) collective-permute-start(bf16[16,32,128]{2,1,0:T(8,128)(2,1)S(1)} %get-tuple-element.42), channel_id=1, source_target_pairs={{0,5},{1,4},{2,7},{3,6},{4,0},{5,1},{6,2},{7,3},{8,13},{9,12},{10,... | collective-permute-start | bytes 393224 | tf_op jit(solution)/shard_map/ppermute | solution.py:294
  39.6 3.9 %collective-permute-start.27 = (bf16[16,32,128]{2,1,0:T(8,128)(2,1)S(1)}, bf16[16,32,128]{2,1,0:T(8,128)(2,1)S(1)}, u32[]{:S(2)}, u32[]{:S(2)}) collective-permute-start(bf16[16,32,128]{2,1,0:T(8,128)(2,1)S(1)} %get-tuple-element.42), channel_id=1, source_target_pairs={{0,4},{1,5},{2,6},{3,7},{4,0},{5,1},{6,2},{7,3},{8,12},{9,13},{10,... | collective-permute-start | bytes 393224 | tf_op jit(solution)/shard_map/ppermute | solution.py:294
  39.6 3.8 %collective-permute-start.31 = (bf16[32,32,128]{2,1,0:T(8,128)(2,1)S(1)}, bf16[32,32,128]{2,1,0:T(8,128)(2,1)S(1)}, u32[]{:S(2)}, u32[]{:S(2)}) collective-permute-start(bf16[32,32,128]{2,1,0:T(8,128)(2,1)S(1)} %get-tuple-element.43.refs_3_), channel_id=1, source_target_pairs={{0,4},{1,5},{2,6},{3,7},{4,0},{5,1},{6,2},{7,3},{8,12},{9,13},{10,... | collective-permute-start | bytes 786440 | tf_op jit(solution)/shard_map/ppermute | solution.py:294
  43.7 13.2 %collective-permute-start.32 = (bf16[32,32,128]{2,1,0:T(8,128)(2,1)S(1)}, bf16[32,32,128]{2,1,0:T(8,128)(2,1)S(1)}, u32[]{:S(2)}, u32[]{:S(2)}) collective-permute-start(bf16[32,32,128]{2,1,0:T(8,128)(2,1)S(1)} %get-tuple-element.45), channel_id=1, source_target_pairs={{0,4},{1,5},{2,6},{3,7},{4,0},{5,1},{6,2},{7,3},{8,12},{9,13},{10,... | collective-permute-start | bytes 786440 | tf_op jit(solution)/shard_map/ppermute | solution.py:294
  57.5 2.1 %collective-permute-start.36 = (bf16[16,32,128]{2,1,0:T(8,128)(2,1)S(1)}, bf16[16,32,128]{2,1,0:T(8,128)(2,1)S(1)}, u32[]{:S(2)}, u32[]{:S(2)}) collective-permute-start(bf16[16,32,128]{2,1,0:T(8,128)(2,1)S(1)} %project.5), channel_id=1, source_target_pairs={{0,4},{1,5},{2,6},{3,7},{4,3},{5,2},{6,1},{7,0},{8,12},{9,13},{10,... | collective-permute-start | bytes 393224 | tf_op jit(solution)/shard_map/ppermute | solution.py:294
  57.5 4.1 %collective-permute-start.35 = (bf16[16,32,128]{2,1,0:T(8,128)(2,1)S(1)}, bf16[16,32,128]{2,1,0:T(8,128)(2,1)S(1)}, u32[]{:S(2)}, u32[]{:S(2)}) collective-permute-start(bf16[16,32,128]{2,1,0:T(8,128)(2,1)S(1)} %project.5), channel_id=1, source_target_pairs={{0,4},{1,5},{2,6},{3,7},{4,2},{5,3},{6,0},{7,1},{8,12},{9,13},{10,... | collective-permute-start | bytes 393224 | tf_op jit(solution)/shard_map/ppermute | solution.py:294
  58.9 2.7 %collective-permute-start.34 = (bf16[16,32,128]{2,1,0:T(8,128)(2,1)S(1)}, bf16[16,32,128]{2,1,0:T(8,128)(2,1)S(1)}, u32[]{:S(2)}, u32[]{:S(2)}) collective-permute-start(bf16[16,32,128]{2,1,0:T(8,128)(2,1)S(1)} %project.5), channel_id=1, source_target_pairs={{0,4},{1,5},{2,6},{3,7},{4,1},{5,0},{6,3},{7,2},{8,12},{9,13},{10,... | collective-permute-start | bytes 393224 | tf_op jit(solution)/shard_map/ppermute | solution.py:294
  59.0 2.6 %collective-permute-start.33 = (bf16[16,32,128]{2,1,0:T(8,128)(2,1)S(1)}, bf16[16,32,128]{2,1,0:T(8,128)(2,1)S(1)}, u32[]{:S(2)}, u32[]{:S(2)}) collective-permute-start(bf16[16,32,128]{2,1,0:T(8,128)(2,1)S(1)} %project.5), channel_id=1, source_target_pairs={{0,4},{1,5},{2,6},{3,7},{4,0},{5,1},{6,2},{7,3},{8,12},{9,13},{10,... | collective-permute-start | bytes 393224 | tf_op jit(solution)/shard_map/ppermute | solution.py:294
  59.4 2.2 %collective-permute-start.37 = (bf16[32,32,128]{2,1,0:T(8,128)(2,1)S(1)}, bf16[32,32,128]{2,1,0:T(8,128)(2,1)S(1)}, u32[]{:S(2)}, u32[]{:S(2)}) collective-permute-start(bf16[32,32,128]{2,1,0:T(8,128)(2,1)S(1)} %collective-permute-done.32.image), channel_id=1, source_target_pairs={{0,4},{1,5},{2,6},{3,7},{4,0},{5,1},{6,2},{7,3},{8,12},{9,13},{10,... | collective-permute-start | bytes 786440 | tf_op jit(solution)/shard_map/ppermute | solution.py:294
  61.7 6.6 %collective-permute-start.41 = (bf16[16,32,128]{2,1,0:T(8,128)(2,1)S(1)}, bf16[16,32,128]{2,1,0:T(8,128)(2,1)S(1)}, u32[]{:S(2)}, u32[]{:S(2)}) collective-permute-start(bf16[16,32,128]{2,1,0:T(8,128)(2,1)S(1)} %get-tuple-element.46), channel_id=1, source_target_pairs={{0,7},{1,6},{2,5},{3,4},{4,0},{5,1},{6,2},{7,3},{8,15},{9,14},{10,... | collective-permute-start | bytes 393224 | tf_op jit(solution)/shard_map/ppermute | solution.py:294
  64.6 5.0 %collective-permute-start.40 = (bf16[16,32,128]{2,1,0:T(8,128)(2,1)S(1)}, bf16[16,32,128]{2,1,0:T(8,128)(2,1)S(1)}, u32[]{:S(2)}, u32[]{:S(2)}) collective-permute-start(bf16[16,32,128]{2,1,0:T(8,128)(2,1)S(1)} %get-tuple-element.46), channel_id=1, source_target_pairs={{0,6},{1,7},{2,4},{3,5},{4,0},{5,1},{6,2},{7,3},{8,14},{9,15},{10,... | collective-permute-start | bytes 393224 | tf_op jit(solution)/shard_map/ppermute | solution.py:294
  64.7 4.9 %collective-permute-start.39 = (bf16[16,32,128]{2,1,0:T(8,128)(2,1)S(1)}, bf16[16,32,128]{2,1,0:T(8,128)(2,1)S(1)}, u32[]{:S(2)}, u32[]{:S(2)}) collective-permute-start(bf16[16,32,128]{2,1,0:T(8,128)(2,1)S(1)} %get-tuple-element.46), channel_id=1, source_target_pairs={{0,5},{1,4},{2,7},{3,6},{4,0},{5,1},{6,2},{7,3},{8,13},{9,12},{10,... | collective-permute-start | bytes 393224 | tf_op jit(solution)/shard_map/ppermute | solution.py:294
  65.9 3.7 %collective-permute-start.38 = (bf16[16,32,128]{2,1,0:T(8,128)(2,1)S(1)}, bf16[16,32,128]{2,1,0:T(8,128)(2,1)S(1)}, u32[]{:S(2)}, u32[]{:S(2)}) collective-permute-start(bf16[16,32,128]{2,1,0:T(8,128)(2,1)S(1)} %get-tuple-element.46), channel_id=1, source_target_pairs={{0,4},{1,5},{2,6},{3,7},{4,0},{5,1},{6,2},{7,3},{8,12},{9,13},{10,... | collective-permute-start | bytes 393224 | tf_op jit(solution)/shard_map/ppermute | solution.py:294
  65.9 4.3 %collective-permute-start.42 = (bf16[32,32,128]{2,1,0:T(8,128)(2,1)S(1)}, bf16[32,32,128]{2,1,0:T(8,128)(2,1)S(1)}, u32[]{:S(2)}, u32[]{:S(2)}) collective-permute-start(bf16[32,32,128]{2,1,0:T(8,128)(2,1)S(1)} %get-tuple-element.47.refs_3_), channel_id=1, source_target_pairs={{0,4},{1,5},{2,6},{3,7},{4,0},{5,1},{6,2},{7,3},{8,12},{9,13},{10,... | collective-permute-start | bytes 786440 | tf_op jit(solution)/shard_map/ppermute | solution.py:294

commit v22 on v14

--- a/solution.py
+++ b/solution.py
@@ -28,7 +28,7 @@
 
 
 def head_kernel(row_blocks, chunks, pos, rows_in, cols_in, blocks_in, rays_in, *refs):
-    note, table, own, blocks, rows, cols, rays, seen, squares, norms, sems = refs
+    note, table, own, blocks, rows, cols, rays, seen, norms, sems = refs
     count = blocks.shape[2]
     each = count // row_blocks
     per_chunk = count // chunks
@@ -48,7 +48,6 @@
         )
     for copy in small + large:
         copy.start()
-    squares[...] = jnp.zeros_like(squares)
     for copy in small:
         copy.wait()
     for i in range(3):
@@ -58,24 +57,25 @@
     for i in range(quarter):
         parts = [rays[g, :, i * BS : (i + 1) * BS] for g in range(batches)]
         note[i] = jnp.concatenate(parts, axis=0).astype(jnp.bfloat16)
-    for k in range(chunks):
-        large[k].wait()
-        for n in range(k * per_chunk, (k + 1) * per_chunk):
-            block = blocks[0, 0, n].astype(jnp.float32)
-            row = rows[0, 0, n]
-            squares[row] = squares[row] + block * block
-            at = seen[row]
-            seen[row] = at + 1
-            col = cols[0, 0, n]
-            for out, first in ((table, 0), (own, 1)):
-                out[first, at] = n
-                out[first + 1, at] = col
+    for n in range(count):
+        row = rows[0, 0, n]
+        at = seen[row]
+        seen[row] = at + 1
+        col = cols[0, 0, n]
+        for out, first in ((table, 0), (own, 1)):
+            out[first, at] = n
+            out[first + 1, at] = col
+    for copy in large:
+        copy.wait()
     ones = jnp.ones((BS, BS), jnp.bfloat16)
     on_diagonal = lax.broadcasted_iota(jnp.int32, (BS, BS), 0) == lax.broadcasted_iota(
         jnp.int32, (BS, BS), 1
     )
     for r in range(row_blocks):
-        left = squares[r]
+        left = 0.0
+        for k in range(r * each, (r + 1) * each):
+            block = blocks[0, 0, own[1, k]].astype(jnp.float32)
+            left = left + block * block
         coarse = left.astype(jnp.bfloat16)
         fine = (left - coarse.astype(jnp.float32)).astype(jnp.bfloat16)
         total = dot(coarse, ones, NN) + dot(fine, ones, NN)
@@ -327,7 +327,6 @@
             pltpu.SMEM(block_cols.shape, jnp.int32),
             pltpu.VMEM(sinogram.shape, jnp.float32),
             pltpu.SMEM((row_blocks,), jnp.int32),
-            pltpu.VMEM((row_blocks, BS, BS), jnp.float32),
             pltpu.VMEM((row_blocks, BS), jnp.float32),
             pltpu.SemaphoreType.DMA((3 + chunks,)),
         ],

time: 71.1 us -> 71.5 us (level)
  no operation moved by 1% of the time
where the time goes in v22:
time: 71.5 us; the launch traced here: 71.3 us
  waiting for transfers between devices  35.8 us (50%)
  starting transfers between devices  27.7 us (39%)
  Pallas kernels  7.59 us (11%)
    ppermute x43, waiting for transfers between devices, sent(): return lax.ppermute(value, ('subset', 'tile'), pairs)  35.8 us
    ppermute x43, starting transfers between devices, sent(): return lax.ppermute(value, ('subset', 'tile'), pairs)  27.7 us
    pallas_call x1, Pallas kernels, per_device(): pl.pallas_call(functools.partial(head_kernel, row_blocks, chunks), out_sh...  3.46 us
    pallas_call x19, Pallas kernels, call(): pl.pallas_call(kernel, out_shape=out_shape, in_specs=[SMEM] * smem + [VME...  2.33 us
  transfers between devices with their start and end apart: 43, of which 18 were waited for; matrix products, arithmetic and copies ran while one was open for 0% of the time, Pallas kernels for 8%

profile of v22, /device:TPU:25, one launch (start us, length us, event | category | flops | bytes accessed | tf_op | source)
XLA Modules:
  0.0 71.3 jit_solution(2334240567775935489)
XLA Ops:
  0.0 0.7 collective-permute-start.1
  0.8 3.5 %head.1 = (bf16[5,32,128]{2,1,0:T(8,128)(2,1)S(1)}, s32[2,80]{1,0:T(2,128)S(1)}, s32[3,80]{1,0:T(4,128)S(4)}, bf16[1,1,80,128,128]{4,3,2,1,0:T(8,128)(2,1)S(1)}) custom-call(s32[3]{0:T(128)S(1)} %pad_add_fusion.pos, s32[1,1,80]{2,1,0:T(1,128)} %rows_in.1, s32[1,1,80]{2,1,0:T(1,128)} %cols_in.1, bf16[1,1,80,128,128]{4,3,2,1,0:T(8,128)(2,1)} %blocks_in.1, ...), custom_call_target="tpu_custom_call" | custom-call | tf_op jit(solution)/shard_map/head/pallas_call | solution.py:315
  4.2 2.2 %collective-permute-start.4 = (bf16[5,32,128]{2,1,0:T(8,128)(2,1)S(1)}, bf16[5,32,128]{2,1,0:T(8,128)(2,1)S(1)}, u32[]{:S(2)}, u32[]{:S(2)}) collective-permute-start(bf16[5,32,128]{2,1,0:T(8,128)(2,1)S(1)} %get-tuple-element.31._.refs_2_), channel_id=1, source_target_pairs={{0,3},{1,2},{2,1},{3,0},{4,7},{5,6},{6,5},{7,4},{8,11},{9,10},{10,... | collective-permute-start | bytes 122888 | tf_op jit(solution)/shard_map/ppermute | solution.py:279
  6.7 0.3 collective-permute-start.2
  6.9 0.8 %collective-permute-start = (s32[2,80]{1,0:T(2,128)S(1)}, s32[2,80]{1,0:T(2,128)S(1)}, u32[]{:S(2)}, u32[]{:S(2)}) collective-permute-start(s32[2,80]{1,0:T(2,128)S(1)} %get-tuple-element.28), channel_id=1, source_target_pairs={{0,4},{1,5},{2,6},{3,7},{4,0},{5,1},{6,2},{7,3},{8,12},{9,13},{10,... | collective-permute-start | bytes 1928 | tf_op jit(solution)/shard_map/ppermute | solution.py:279
  7.8 0.5 pack_own.1.refs_1_
  8.3 0.3 collective-permute-done.table2
  8.6 1.3 %pack_other.1 = (s32[3,80]{1,0:T(4,128)S(4)}, bf16[16,640,128]{2,1,0:T(8,128)(2,1)S(1)}) custom-call(s32[3,80]{1,0:T(4,128)S(4)} %get-tuple-element.27.own, s32[2,80]{1,0:T(2,128)S(1)} %collective-permute-done.table2, bf16[1,1,80,128,128]{4,3,2,1,0:T(8,128)(2,1)S(1)} %collective-permute-done.1.blocks2), custom_call_target="tpu_custom_call" | custom-call | tf_op jit(solution)/shard_map/pack_other/pallas_call | solution.py:355
  10.0 1.3 %collective-permute-start.8 = (bf16[16,32,128]{2,1,0:T(8,128)(2,1)S(1)}, bf16[16,32,128]{2,1,0:T(8,128)(2,1)S(1)}, u32[]{:S(2)}, u32[]{:S(2)}) collective-permute-start(bf16[16,32,128]{2,1,0:T(8,128)(2,1)S(1)} %get-tuple-element.35), channel_id=1, source_target_pairs={{0,7},{1,6},{2,5},{3,4},{4,0},{5,1},{6,2},{7,3},{8,15},{9,14},{10,... | collective-permute-start | bytes 393224 | tf_op jit(solution)/shard_map/ppermute | solution.py:279
  11.4 1.3 %collective-permute-start.7 = (bf16[16,32,128]{2,1,0:T(8,128)(2,1)S(1)}, bf16[16,32,128]{2,1,0:T(8,128)(2,1)S(1)}, u32[]{:S(2)}, u32[]{:S(2)}) collective-permute-start(bf16[16,32,128]{2,1,0:T(8,128)(2,1)S(1)} %get-tuple-element.35), channel_id=1, source_target_pairs={{0,6},{1,7},{2,4},{3,5},{4,0},{5,1},{6,2},{7,3},{8,14},{9,15},{10,... | collective-permute-start | bytes 393224 | tf_op jit(solution)/shard_map/ppermute | solution.py:279
  12.7 0.3 collective-permute-start.6
  13.0 0.3 collective-permute-start.5
  13.5 2.0 %collective-permute-done.8.refs_6_ = bf16[16,32,128]{2,1,0:T(8,128)(2,1)S(1)} collective-permute-done((bf16[16,32,128]{2,1,0:T(8,128)(2,1)S(1)}, bf16[16,32,128]{2,1,0:T(8,128)(2,1)S(1)}, u32[]{:S(2)}, u32[]{:S(2)}) %collective-permute-start.8) | collective-permute-done | bytes 131104 | tf_op jit(solution)/shard_map/ppermute | solution.py:279
  15.5 1.3 %collective-permute-done.7.refs_5_ = bf16[16,32,128]{2,1,0:T(8,128)(2,1)S(1)} collective-permute-done((bf16[16,32,128]{2,1,0:T(8,128)(2,1)S(1)}, bf16[16,32,128]{2,1,0:T(8,128)(2,1)S(1)}, u32[]{:S(2)}, u32[]{:S(2)}) %collective-permute-start.7) | collective-permute-done | bytes 131104 | tf_op jit(solution)/shard_map/ppermute | solution.py:279
  16.8 0.3 collective-permute-done.6.refs_4_
  17.1 1.5 %collective-permute-done.10.image = bf16[32,32,128]{2,1,0:T(8,128)(2,1)S(1)} collective-permute-done((bf16[32,32,128]{2,1,0:T(8,128)(2,1)S(1)}, bf16[32,32,128]{2,1,0:T(8,128)(2,1)S(1)}, u32[]{:S(2)}, u32[]{:S(2)}) %collective-permute-start.10) | collective-permute-done | bytes 262176 | tf_op jit(solution)/shard_map/ppermute | solution.py:279
  18.7 1.4 %collective-permute-start.14 = (bf16[16,32,128]{2,1,0:T(8,128)(2,1)S(1)}, bf16[16,32,128]{2,1,0:T(8,128)(2,1)S(1)}, u32[]{:S(2)}, u32[]{:S(2)}) collective-permute-start(bf16[16,32,128]{2,1,0:T(8,128)(2,1)S(1)} %project.3), channel_id=1, source_target_pairs={{0,4},{1,5},{2,6},{3,7},{4,3},{5,2},{6,1},{7,0},{8,12},{9,13},{10,... | collective-permute-start | bytes 393224 | tf_op jit(solution)/shard_map/ppermute | solution.py:279
  20.1 1.2 %collective-permute-start.12 = (bf16[16,32,128]{2,1,0:T(8,128)(2,1)S(1)}, bf16[16,32,128]{2,1,0:T(8,128)(2,1)S(1)}, u32[]{:S(2)}, u32[]{:S(2)}) collective-permute-start(bf16[16,32,128]{2,1,0:T(8,128)(2,1)S(1)} %project.3), channel_id=1, source_target_pairs={{0,4},{1,5},{2,6},{3,7},{4,1},{5,0},{6,3},{7,2},{8,12},{9,13},{10,... | collective-permute-start | bytes 393224 | tf_op jit(solution)/shard_map/ppermute | solution.py:279
  21.3 0.5 collective-permute-start.15
  22.0 1.4 %collective-permute-done.13.refs_5_ = bf16[16,32,128]{2,1,0:T(8,128)(2,1)S(1)} collective-permute-done((bf16[16,32,128]{2,1,0:T(8,128)(2,1)S(1)}, bf16[16,32,128]{2,1,0:T(8,128)(2,1)S(1)}, u32[]{:S(2)}, u32[]{:S(2)}) %collective-permute-start.13) | collective-permute-done | bytes 131104 | tf_op jit(solution)/shard_map/ppermute | solution.py:279
  23.4 2.1 %collective-permute-start.19 = (bf16[16,32,128]{2,1,0:T(8,128)(2,1)S(1)}, bf16[16,32,128]{2,1,0:T(8,128)(2,1)S(1)}, u32[]{:S(2)}, u32[]{:S(2)}) collective-permute-start(bf16[16,32,128]{2,1,0:T(8,128)(2,1)S(1)} %get-tuple-element.38), channel_id=1, source_target_pairs={{0,7},{1,6},{2,5},{3,4},{4,0},{5,1},{6,2},{7,3},{8,15},{9,14},{10,... | collective-permute-start | bytes 393224 | tf_op jit(solution)/shard_map/ppermute | solution.py:279
  25.5 0.9 %collective-permute-start.17 = (bf16[16,32,128]{2,1,0:T(8,128)(2,1)S(1)}, bf16[16,32,128]{2,1,0:T(8,128)(2,1)S(1)}, u32[]{:S(2)}, u32[]{:S(2)}) collective-permute-start(bf16[16,32,128]{2,1,0:T(8,128)(2,1)S(1)} %get-tuple-element.38), channel_id=1, source_target_pairs={{0,5},{1,4},{2,7},{3,6},{4,0},{5,1},{6,2},{7,3},{8,13},{9,12},{10,... | collective-permute-start | bytes 393224 | tf_op jit(solution)/shard_map/ppermute | solution.py:279
  26.6 0.4 collective-permute-start.20
  27.0 2.3 %collective-permute-done.19.refs_6_ = bf16[16,32,128]{2,1,0:T(8,128)(2,1)S(1)} collective-permute-done((bf16[16,32,128]{2,1,0:T(8,128)(2,1)S(1)}, bf16[16,32,128]{2,1,0:T(8,128)(2,1)S(1)}, u32[]{:S(2)}, u32[]{:S(2)}) %collective-permute-start.19) | collective-permute-done | bytes 131104 | tf_op jit(solution)/shard_map/ppermute | solution.py:279
  29.3 1.3 %collective-permute-done.18.refs_5_ = bf16[16,32,128]{2,1,0:T(8,128)(2,1)S(1)} collective-permute-done((bf16[16,32,128]{2,1,0:T(8,128)(2,1)S(1)}, bf16[16,32,128]{2,1,0:T(8,128)(2,1)S(1)}, u32[]{:S(2)}, u32[]{:S(2)}) %collective-permute-start.18) | collective-permute-done | bytes 131104 | tf_op jit(solution)/shard_map/ppermute | solution.py:279
  30.8 1.5 %collective-permute-done.21.image = bf16[32,32,128]{2,1,0:T(8,128)(2,1)S(1)} collective-permute-done((bf16[32,32,128]{2,1,0:T(8,128)(2,1)S(1)}, bf16[32,32,128]{2,1,0:T(8,128)(2,1)S(1)}, u32[]{:S(2)}, u32[]{:S(2)}) %collective-permute-start.21) | collective-permute-done | bytes 262176 | tf_op jit(solution)/shard_map/ppermute | solution.py:279
  32.3 1.2 %collective-permute-start.25 = (bf16[16,32,128]{2,1,0:T(8,128)(2,1)S(1)}, bf16[16,32,128]{2,1,0:T(8,128)(2,1)S(1)}, u32[]{:S(2)}, u32[]{:S(2)}) collective-permute-start(bf16[16,32,128]{2,1,0:T(8,128)(2,1)S(1)} %project.4), channel_id=1, source_target_pairs={{0,4},{1,5},{2,6},{3,7},{4,3},{5,2},{6,1},{7,0},{8,12},{9,13},{10,... | collective-permute-start | bytes 393224 | tf_op jit(solution)/shard_map/ppermute | solution.py:279
  33.5 1.0 %collective-permute-start.23 = (bf16[16,32,128]{2,1,0:T(8,128)(2,1)S(1)}, bf16[16,32,128]{2,1,0:T(8,128)(2,1)S(1)}, u32[]{:S(2)}, u32[]{:S(2)}) collective-permute-start(bf16[16,32,128]{2,1,0:T(8,128)(2,1)S(1)} %project.4), channel_id=1, source_target_pairs={{0,4},{1,5},{2,6},{3,7},{4,1},{5,0},{6,3},{7,2},{8,12},{9,13},{10,... | collective-permute-start | bytes 393224 | tf_op jit(solution)/shard_map/ppermute | solution.py:279
  34.5 0.5 collective-permute-start.26
  35.0 0.4 collective-permute-done.25.refs_6_
  35.4 1.4 %collective-permute-done.24.refs_5_ = bf16[16,32,128]{2,1,0:T(8,128)(2,1)S(1)} collective-permute-done((bf16[16,32,128]{2,1,0:T(8,128)(2,1)S(1)}, bf16[16,32,128]{2,1,0:T(8,128)(2,1)S(1)}, u32[]{:S(2)}, u32[]{:S(2)}) %collective-permute-start.24) | collective-permute-done | bytes 131104 | tf_op jit(solution)/shard_map/ppermute | solution.py:279
  36.9 1.9 %collective-permute-start.30 = (bf16[16,32,128]{2,1,0:T(8,128)(2,1)S(1)}, bf16[16,32,128]{2,1,0:T(8,128)(2,1)S(1)}, u32[]{:S(2)}, u32[]{:S(2)}) collective-permute-start(bf16[16,32,128]{2,1,0:T(8,128)(2,1)S(1)} %get-tuple-element.42), channel_id=1, source_target_pairs={{0,7},{1,6},{2,5},{3,4},{4,0},{5,1},{6,2},{7,3},{8,15},{9,14},{10,... | collective-permute-start | bytes 393224 | tf_op jit(solution)/shard_map/ppermute | solution.py:279
  38.8 1.2 %collective-permute-start.28 = (bf16[16,32,128]{2,1,0:T(8,128)(2,1)S(1)}, bf16[16,32,128]{2,1,0:T(8,128)(2,1)S(1)}, u32[]{:S(2)}, u32[]{:S(2)}) collective-permute-start(bf16[16,32,128]{2,1,0:T(8,128)(2,1)S(1)} %get-tuple-element.42), channel_id=1, source_target_pairs={{0,5},{1,4},{2,7},{3,6},{4,0},{5,1},{6,2},{7,3},{8,13},{9,12},{10,... | collective-permute-start | bytes 393224 | tf_op jit(solution)/shard_map/ppermute | solution.py:279
  40.0 0.5 collective-permute-start.31
  40.5 2.0 %collective-permute-done.30.refs_6_ = bf16[16,32,128]{2,1,0:T(8,128)(2,1)S(1)} collective-permute-done((bf16[16,32,128]{2,1,0:T(8,128)(2,1)S(1)}, bf16[16,32,128]{2,1,0:T(8,128)(2,1)S(1)}, u32[]{:S(2)}, u32[]{:S(2)}) %collective-permute-start.30) | collective-permute-done | bytes 131104 | tf_op jit(solution)/shard_map/ppermute | solution.py:279
  42.5 1.3 %collective-permute-done.29.refs_5_ = bf16[16,32,128]{2,1,0:T(8,128)(2,1)S(1)} collective-permute-done((bf16[16,32,128]{2,1,0:T(8,128)(2,1)S(1)}, bf16[16,32,128]{2,1,0:T(8,128)(2,1)S(1)}, u32[]{:S(2)}, u32[]{:S(2)}) %collective-permute-start.29) | collective-permute-done | bytes 131104 | tf_op jit(solution)/shard_map/ppermute | solution.py:279
  44.2 13.1 %collective-permute-done.32.image = bf16[32,32,128]{2,1,0:T(8,128)(2,1)S(1)} collective-permute-done((bf16[32,32,128]{2,1,0:T(8,128)(2,1)S(1)}, bf16[32,32,128]{2,1,0:T(8,128)(2,1)S(1)}, u32[]{:S(2)}, u32[]{:S(2)}) %collective-permute-start.32) | collective-permute-done | bytes 262176 | tf_op jit(solution)/shard_map/ppermute | solution.py:279
  57.3 0.5 project.5
  57.9 1.4 %collective-permute-start.35 = (bf16[16,32,128]{2,1,0:T(8,128)(2,1)S(1)}, bf16[16,32,128]{2,1,0:T(8,128)(2,1)S(1)}, u32[]{:S(2)}, u32[]{:S(2)}) collective-permute-start(bf16[16,32,128]{2,1,0:T(8,128)(2,1)S(1)} %project.5), channel_id=1, source_target_pairs={{0,4},{1,5},{2,6},{3,7},{4,2},{5,3},{6,0},{7,1},{8,12},{9,13},{10,... | collective-permute-start | bytes 393224 | tf_op jit(solution)/shard_map/ppermute | solution.py:279
  59.4 0.4 collective-permute-start.33
  59.9 2.1 %collective-permute-done.35.refs_5_ = bf16[16,32,128]{2,1,0:T(8,128)(2,1)S(1)} collective-permute-done((bf16[16,32,128]{2,1,0:T(8,128)(2,1)S(1)}, bf16[16,32,128]{2,1,0:T(8,128)(2,1)S(1)}, u32[]{:S(2)}, u32[]{:S(2)}) %collective-permute-start.35) | collective-permute-done | bytes 131104 | tf_op jit(solution)/shard_map/ppermute | solution.py:279
  62.0 3.0 %collective-permute-start.41 = (bf16[16,32,128]{2,1,0:T(8,128)(2,1)S(1)}, bf16[16,32,128]{2,1,0:T(8,128)(2,1)S(1)}, u32[]{:S(2)}, u32[]{:S(2)}) collective-permute-start(bf16[16,32,128]{2,1,0:T(8,128)(2,1)S(1)} %get-tuple-element.46), channel_id=1, source_target_pairs={{0,7},{1,6},{2,5},{3,4},{4,0},{5,1},{6,2},{7,3},{8,15},{9,14},{10,... | collective-permute-start | bytes 393224 | tf_op jit(solution)/shard_map/ppermute | solution.py:279
  65.0 1.2 %collective-permute-start.39 = (bf16[16,32,128]{2,1,0:T(8,128)(2,1)S(1)}, bf16[16,32,128]{2,1,0:T(8,128)(2,1)S(1)}, u32[]{:S(2)}, u32[]{:S(2)}) collective-permute-start(bf16[16,32,128]{2,1,0:T(8,128)(2,1)S(1)} %get-tuple-element.46), channel_id=1, source_target_pairs={{0,5},{1,4},{2,7},{3,6},{4,0},{5,1},{6,2},{7,3},{8,13},{9,12},{10,... | collective-permute-start | bytes 393224 | tf_op jit(solution)/shard_map/ppermute | solution.py:279
  66.3 0.5 collective-permute-start.42
  66.8 1.8 %collective-permute-done.41.refs_6_ = bf16[16,32,128]{2,1,0:T(8,128)(2,1)S(1)} collective-permute-done((bf16[16,32,128]{2,1,0:T(8,128)(2,1)S(1)}, bf16[16,32,128]{2,1,0:T(8,128)(2,1)S(1)}, u32[]{:S(2)}, u32[]{:S(2)}) %collective-permute-start.41) | collective-permute-done | bytes 131104 | tf_op jit(solution)/shard_map/ppermute | solution.py:279
  68.6 1.3 %collective-permute-done.40.refs_5_ = bf16[16,32,128]{2,1,0:T(8,128)(2,1)S(1)} collective-permute-done((bf16[16,32,128]{2,1,0:T(8,128)(2,1)S(1)}, bf16[16,32,128]{2,1,0:T(8,128)(2,1)S(1)}, u32[]{:S(2)}, u32[]{:S(2)}) %collective-permute-start.40) | collective-permute-done | bytes 131104 | tf_op jit(solution)/shard_map/ppermute | solution.py:279
  70.0 0.6 update.15.refs_1_
  70.6 0.8 %second.7 = bf16[4,8,4096]{2,1,0:T(8,128)(2,1)} custom-call(s32[3,80]{1,0:T(4,128)S(4)} %get-tuple-element.29.refs_0_.info, f32[32,32,128]{2,1,0:T(8,128)S(1)} %update.15.refs_1_, bf16[32,32,128]{2,1,0:T(8,128)(2,1)S(1)} %collective-permute-done.42.refs_2_, bf16[32,32,128]{2,1,0:T(8,128)(2,1)S(1)} %get-tuple-element.47.refs_3_, ...), custom_call_target="tpu_custom_call" | custom-call | tf_op jit(solution)/shard_map/second/pallas_call | solution.py:300
  (61 shorter events, 2.2 us)
Async XLA Ops:
  0.0 8.6 %collective-permute-start.1 = (bf16[1,1,80,128,128]{4,3,2,1,0:T(8,128)(2,1)}, bf16[1,1,80,128,128]{4,3,2,1,0:T(8,128)(2,1)S(1)}, u32[]{:S(2)}, u32[]{:S(2)}) collective-permute-start(bf16[1,1,80,128,128]{4,3,2,1,0:T(8,128)(2,1)} %blocks_in.1), channel_id=1, source_target_pairs={{0,4},{1,5},{2,6},{3,7},{4,0},{5,1},{6,2},{7,3},{8,12},{9,13},{10,... | collective-permute-start | bytes 7864328 | tf_op jit(solution)/shard_map/ppermute | solution.py:279
  4.2 5.7 %collective-permute-start.4 = (bf16[5,32,128]{2,1,0:T(8,128)(2,1)S(1)}, bf16[5,32,128]{2,1,0:T(8,128)(2,1)S(1)}, u32[]{:S(2)}, u32[]{:S(2)}) collective-permute-start(bf16[5,32,128]{2,1,0:T(8,128)(2,1)S(1)} %get-tuple-element.31._.refs_2_), channel_id=1, source_target_pairs={{0,3},{1,2},{2,1},{3,0},{4,7},{5,6},{6,5},{7,4},{8,11},{9,10},{10,... | collective-permute-start | bytes 122888 | tf_op jit(solution)/shard_map/ppermute | solution.py:279
  6.5 3.5 %collective-permute-start.3 = (bf16[5,32,128]{2,1,0:T(8,128)(2,1)S(1)}, bf16[5,32,128]{2,1,0:T(8,128)(2,1)S(1)}, u32[]{:S(2)}, u32[]{:S(2)}) collective-permute-start(bf16[5,32,128]{2,1,0:T(8,128)(2,1)S(1)} %get-tuple-element.31._.refs_2_), channel_id=1, source_target_pairs={{0,2},{1,3},{2,0},{3,1},{4,6},{5,7},{6,4},{7,5},{8,10},{9,11},{10,... | collective-permute-start | bytes 122888 | tf_op jit(solution)/shard_map/ppermute | solution.py:279
  6.7 3.3 %collective-permute-start.2 = (bf16[5,32,128]{2,1,0:T(8,128)(2,1)S(1)}, bf16[5,32,128]{2,1,0:T(8,128)(2,1)S(1)}, u32[]{:S(2)}, u32[]{:S(2)}) collective-permute-start(bf16[5,32,128]{2,1,0:T(8,128)(2,1)S(1)} %get-tuple-element.31._.refs_2_), channel_id=1, source_target_pairs={{0,1},{1,0},{2,3},{3,2},{4,5},{5,4},{6,7},{7,6},{8,9},{9,8},{10,11... | collective-permute-start | bytes 122888 | tf_op jit(solution)/shard_map/ppermute | solution.py:279
  6.9 1.7 %collective-permute-start = (s32[2,80]{1,0:T(2,128)S(1)}, s32[2,80]{1,0:T(2,128)S(1)}, u32[]{:S(2)}, u32[]{:S(2)}) collective-permute-start(s32[2,80]{1,0:T(2,128)S(1)} %get-tuple-element.28), channel_id=1, source_target_pairs={{0,4},{1,5},{2,6},{3,7},{4,0},{5,1},{6,2},{7,3},{8,12},{9,13},{10,... | collective-permute-start | bytes 1928 | tf_op jit(solution)/shard_map/ppermute | solution.py:279
  10.0 5.4 %collective-permute-start.8 = (bf16[16,32,128]{2,1,0:T(8,128)(2,1)S(1)}, bf16[16,32,128]{2,1,0:T(8,128)(2,1)S(1)}, u32[]{:S(2)}, u32[]{:S(2)}) collective-permute-start(bf16[16,32,128]{2,1,0:T(8,128)(2,1)S(1)} %get-tuple-element.35), channel_id=1, source_target_pairs={{0,7},{1,6},{2,5},{3,4},{4,0},{5,1},{6,2},{7,3},{8,15},{9,14},{10,... | collective-permute-start | bytes 393224 | tf_op jit(solution)/shard_map/ppermute | solution.py:279
  11.4 5.4 %collective-permute-start.7 = (bf16[16,32,128]{2,1,0:T(8,128)(2,1)S(1)}, bf16[16,32,128]{2,1,0:T(8,128)(2,1)S(1)}, u32[]{:S(2)}, u32[]{:S(2)}) collective-permute-start(bf16[16,32,128]{2,1,0:T(8,128)(2,1)S(1)} %get-tuple-element.35), channel_id=1, source_target_pairs={{0,6},{1,7},{2,4},{3,5},{4,0},{5,1},{6,2},{7,3},{8,14},{9,15},{10,... | collective-permute-start | bytes 393224 | tf_op jit(solution)/shard_map/ppermute | solution.py:279
  12.7 4.4 %collective-permute-start.6 = (bf16[16,32,128]{2,1,0:T(8,128)(2,1)S(1)}, bf16[16,32,128]{2,1,0:T(8,128)(2,1)S(1)}, u32[]{:S(2)}, u32[]{:S(2)}) collective-permute-start(bf16[16,32,128]{2,1,0:T(8,128)(2,1)S(1)} %get-tuple-element.35), channel_id=1, source_target_pairs={{0,5},{1,4},{2,7},{3,6},{4,0},{5,1},{6,2},{7,3},{8,13},{9,12},{10,... | collective-permute-start | bytes 393224 | tf_op jit(solution)/shard_map/ppermute | solution.py:279
  13.0 4.1 %collective-permute-start.5 = (bf16[16,32,128]{2,1,0:T(8,128)(2,1)S(1)}, bf16[16,32,128]{2,1,0:T(8,128)(2,1)S(1)}, u32[]{:S(2)}, u32[]{:S(2)}) collective-permute-start(bf16[16,32,128]{2,1,0:T(8,128)(2,1)S(1)} %get-tuple-element.35), channel_id=1, source_target_pairs={{0,4},{1,5},{2,6},{3,7},{4,0},{5,1},{6,2},{7,3},{8,12},{9,13},{10,... | collective-permute-start | bytes 393224 | tf_op jit(solution)/shard_map/ppermute | solution.py:279
  13.3 3.8 %collective-permute-start.9 = (bf16[32,32,128]{2,1,0:T(8,128)(2,1)S(1)}, bf16[32,32,128]{2,1,0:T(8,128)(2,1)S(1)}, u32[]{:S(2)}, u32[]{:S(2)}) collective-permute-start(bf16[32,32,128]{2,1,0:T(8,128)(2,1)S(1)} %get-tuple-element.36.refs_3_), channel_id=1, source_target_pairs={{0,4},{1,5},{2,6},{3,7},{4,0},{5,1},{6,2},{7,3},{8,12},{9,13},{10,... | collective-permute-start | bytes 786440 | tf_op jit(solution)/shard_map/ppermute | solution.py:279
  17.1 1.6 %collective-permute-start.10 = (bf16[32,32,128]{2,1,0:T(8,128)(2,1)S(1)}, bf16[32,32,128]{2,1,0:T(8,128)(2,1)S(1)}, u32[]{:S(2)}, u32[]{:S(2)}) collective-permute-start(bf16[32,32,128]{2,1,0:T(8,128)(2,1)S(1)} %get-tuple-element.37), channel_id=1, source_target_pairs={{0,4},{1,5},{2,6},{3,7},{4,12},{5,13},{6,14},{7,15},{8,0},{9,1},{1... | collective-permute-start | bytes 786440 | tf_op jit(solution)/shard_map/ppermute | solution.py:279
  18.7 3.3 %collective-permute-start.14 = (bf16[16,32,128]{2,1,0:T(8,128)(2,1)S(1)}, bf16[16,32,128]{2,1,0:T(8,128)(2,1)S(1)}, u32[]{:S(2)}, u32[]{:S(2)}) collective-permute-start(bf16[16,32,128]{2,1,0:T(8,128)(2,1)S(1)} %project.3), channel_id=1, source_target_pairs={{0,4},{1,5},{2,6},{3,7},{4,3},{5,2},{6,1},{7,0},{8,12},{9,13},{10,... | collective-permute-start | bytes 393224 | tf_op jit(solution)/shard_map/ppermute | solution.py:279
  20.0 3.3 %collective-permute-start.13 = (bf16[16,32,128]{2,1,0:T(8,128)(2,1)S(1)}, bf16[16,32,128]{2,1,0:T(8,128)(2,1)S(1)}, u32[]{:S(2)}, u32[]{:S(2)}) collective-permute-start(bf16[16,32,128]{2,1,0:T(8,128)(2,1)S(1)} %project.3), channel_id=1, source_target_pairs={{0,4},{1,5},{2,6},{3,7},{4,2},{5,3},{6,0},{7,1},{8,12},{9,13},{10,... | collective-permute-start | bytes 393224 | tf_op jit(solution)/shard_map/ppermute | solution.py:279
  20.1 3.3 %collective-permute-start.12 = (bf16[16,32,128]{2,1,0:T(8,128)(2,1)S(1)}, bf16[16,32,128]{2,1,0:T(8,128)(2,1)S(1)}, u32[]{:S(2)}, u32[]{:S(2)}) collective-permute-start(bf16[16,32,128]{2,1,0:T(8,128)(2,1)S(1)} %project.3), channel_id=1, source_target_pairs={{0,4},{1,5},{2,6},{3,7},{4,1},{5,0},{6,3},{7,2},{8,12},{9,13},{10,... | collective-permute-start | bytes 393224 | tf_op jit(solution)/shard_map/ppermute | solution.py:279
  21.3 2.1 %collective-permute-start.11 = (bf16[16,32,128]{2,1,0:T(8,128)(2,1)S(1)}, bf16[16,32,128]{2,1,0:T(8,128)(2,1)S(1)}, u32[]{:S(2)}, u32[]{:S(2)}) collective-permute-start(bf16[16,32,128]{2,1,0:T(8,128)(2,1)S(1)} %project.3), channel_id=1, source_target_pairs={{0,4},{1,5},{2,6},{3,7},{4,0},{5,1},{6,2},{7,3},{8,12},{9,13},{10,... | collective-permute-start | bytes 393224 | tf_op jit(solution)/shard_map/ppermute | solution.py:279
  21.3 2.1 %collective-permute-start.15 = (bf16[32,32,128]{2,1,0:T(8,128)(2,1)S(1)}, bf16[32,32,128]{2,1,0:T(8,128)(2,1)S(1)}, u32[]{:S(2)}, u32[]{:S(2)}) collective-permute-start(bf16[32,32,128]{2,1,0:T(8,128)(2,1)S(1)} %collective-permute-done.10.image), channel_id=1, source_target_pairs={{0,4},{1,5},{2,6},{3,7},{4,0},{5,1},{6,2},{7,3},{8,12},{9,13},{10,... | collective-permute-start | bytes 786440 | tf_op jit(solution)/shard_map/ppermute | solution.py:279
  23.4 5.9 %collective-permute-start.19 = (bf16[16,32,128]{2,1,0:T(8,128)(2,1)S(1)}, bf16[16,32,128]{2,1,0:T(8,128)(2,1)S(1)}, u32[]{:S(2)}, u32[]{:S(2)}) collective-permute-start(bf16[16,32,128]{2,1,0:T(8,128)(2,1)S(1)} %get-tuple-element.38), channel_id=1, source_target_pairs={{0,7},{1,6},{2,5},{3,4},{4,0},{5,1},{6,2},{7,3},{8,15},{9,14},{10,... | collective-permute-start | bytes 393224 | tf_op jit(solution)/shard_map/ppermute | solution.py:279
  25.5 5.2 %collective-permute-start.18 = (bf16[16,32,128]{2,1,0:T(8,128)(2,1)S(1)}, bf16[16,32,128]{2,1,0:T(8,128)(2,1)S(1)}, u32[]{:S(2)}, u32[]{:S(2)}) collective-permute-start(bf16[16,32,128]{2,1,0:T(8,128)(2,1)S(1)} %get-tuple-element.38), channel_id=1, source_target_pairs={{0,6},{1,7},{2,4},{3,5},{4,0},{5,1},{6,2},{7,3},{8,14},{9,15},{10,... | collective-permute-start | bytes 393224 | tf_op jit(solution)/shard_map/ppermute | solution.py:279
  25.5 5.1 %collective-permute-start.17 = (bf16[16,32,128]{2,1,0:T(8,128)(2,1)S(1)}, bf16[16,32,128]{2,1,0:T(8,128)(2,1)S(1)}, u32[]{:S(2)}, u32[]{:S(2)}) collective-permute-start(bf16[16,32,128]{2,1,0:T(8,128)(2,1)S(1)} %get-tuple-element.38), channel_id=1, source_target_pairs={{0,5},{1,4},{2,7},{3,6},{4,0},{5,1},{6,2},{7,3},{8,13},{9,12},{10,... | collective-permute-start | bytes 393224 | tf_op jit(solution)/shard_map/ppermute | solution.py:279
  26.5 4.2 %collective-permute-start.16 = (bf16[16,32,128]{2,1,0:T(8,128)(2,1)S(1)}, bf16[16,32,128]{2,1,0:T(8,128)(2,1)S(1)}, u32[]{:S(2)}, u32[]{:S(2)}) collective-permute-start(bf16[16,32,128]{2,1,0:T(8,128)(2,1)S(1)} %get-tuple-element.38), channel_id=1, source_target_pairs={{0,4},{1,5},{2,6},{3,7},{4,0},{5,1},{6,2},{7,3},{8,12},{9,13},{10,... | collective-permute-start | bytes 393224 | tf_op jit(solution)/shard_map/ppermute | solution.py:279
  26.6 4.0 %collective-permute-start.20 = (bf16[32,32,128]{2,1,0:T(8,128)(2,1)S(1)}, bf16[32,32,128]{2,1,0:T(8,128)(2,1)S(1)}, u32[]{:S(2)}, u32[]{:S(2)}) collective-permute-start(bf16[32,32,128]{2,1,0:T(8,128)(2,1)S(1)} %get-tuple-element.39.refs_3_), channel_id=1, source_target_pairs={{0,4},{1,5},{2,6},{3,7},{4,0},{5,1},{6,2},{7,3},{8,12},{9,13},{10,... | collective-permute-start | bytes 786440 | tf_op jit(solution)/shard_map/ppermute | solution.py:279
  30.7 1.6 %collective-permute-start.21 = (bf16[32,32,128]{2,1,0:T(8,128)(2,1)S(1)}, bf16[32,32,128]{2,1,0:T(8,128)(2,1)S(1)}, u32[]{:S(2)}, u32[]{:S(2)}) collective-permute-start(bf16[32,32,128]{2,1,0:T(8,128)(2,1)S(1)} %get-tuple-element.41), channel_id=1, source_target_pairs={{0,4},{1,5},{2,6},{3,7},{4,0},{5,1},{6,2},{7,3},{8,12},{9,13},{10,... | collective-permute-start | bytes 786440 | tf_op jit(solution)/shard_map/ppermute | solution.py:279
  32.3 3.1 %collective-permute-start.25 = (bf16[16,32,128]{2,1,0:T(8,128)(2,1)S(1)}, bf16[16,32,128]{2,1,0:T(8,128)(2,1)S(1)}, u32[]{:S(2)}, u32[]{:S(2)}) collective-permute-start(bf16[16,32,128]{2,1,0:T(8,128)(2,1)S(1)} %project.4), channel_id=1, source_target_pairs={{0,4},{1,5},{2,6},{3,7},{4,3},{5,2},{6,1},{7,0},{8,12},{9,13},{10,... | collective-permute-start | bytes 393224 | tf_op jit(solution)/shard_map/ppermute | solution.py:279
  33.5 3.3 %collective-permute-start.24 = (bf16[16,32,128]{2,1,0:T(8,128)(2,1)S(1)}, bf16[16,32,128]{2,1,0:T(8,128)(2,1)S(1)}, u32[]{:S(2)}, u32[]{:S(2)}) collective-permute-start(bf16[16,32,128]{2,1,0:T(8,128)(2,1)S(1)} %project.4), channel_id=1, source_target_pairs={{0,4},{1,5},{2,6},{3,7},{4,2},{5,3},{6,0},{7,1},{8,12},{9,13},{10,... | collective-permute-start | bytes 393224 | tf_op jit(solution)/shard_map/ppermute | solution.py:279
  33.5 3.4 %collective-permute-start.23 = (bf16[16,32,128]{2,1,0:T(8,128)(2,1)S(1)}, bf16[16,32,128]{2,1,0:T(8,128)(2,1)S(1)}, u32[]{:S(2)}, u32[]{:S(2)}) collective-permute-start(bf16[16,32,128]{2,1,0:T(8,128)(2,1)S(1)} %project.4), channel_id=1, source_target_pairs={{0,4},{1,5},{2,6},{3,7},{4,1},{5,0},{6,3},{7,2},{8,12},{9,13},{10,... | collective-permute-start | bytes 393224 | tf_op jit(solution)/shard_map/ppermute | solution.py:279
  34.5 2.3 %collective-permute-start.22 = (bf16[16,32,128]{2,1,0:T(8,128)(2,1)S(1)}, bf16[16,32,128]{2,1,0:T(8,128)(2,1)S(1)}, u32[]{:S(2)}, u32[]{:S(2)}) collective-permute-start(bf16[16,32,128]{2,1,0:T(8,128)(2,1)S(1)} %project.4), channel_id=1, source_target_pairs={{0,4},{1,5},{2,6},{3,7},{4,0},{5,1},{6,2},{7,3},{8,12},{9,13},{10,... | collective-permute-start | bytes 393224 | tf_op jit(solution)/shard_map/ppermute | solution.py:279
  34.5 2.3 %collective-permute-start.26 = (bf16[32,32,128]{2,1,0:T(8,128)(2,1)S(1)}, bf16[32,32,128]{2,1,0:T(8,128)(2,1)S(1)}, u32[]{:S(2)}, u32[]{:S(2)}) collective-permute-start(bf16[32,32,128]{2,1,0:T(8,128)(2,1)S(1)} %collective-permute-done.21.image), channel_id=1, source_target_pairs={{0,4},{1,5},{2,6},{3,7},{4,0},{5,1},{6,2},{7,3},{8,12},{9,13},{10,... | collective-permute-start | bytes 786440 | tf_op jit(solution)/shard_map/ppermute | solution.py:279
  36.9 5.6 %collective-permute-start.30 = (bf16[16,32,128]{2,1,0:T(8,128)(2,1)S(1)}, bf16[16,32,128]{2,1,0:T(8,128)(2,1)S(1)}, u32[]{:S(2)}, u32[]{:S(2)}) collective-permute-start(bf16[16,32,128]{2,1,0:T(8,128)(2,1)S(1)} %get-tuple-element.42), channel_id=1, source_target_pairs={{0,7},{1,6},{2,5},{3,4},{4,0},{5,1},{6,2},{7,3},{8,15},{9,14},{10,... | collective-permute-start | bytes 393224 | tf_op jit(solution)/shard_map/ppermute | solution.py:279
  38.7 5.1 %collective-permute-start.29 = (bf16[16,32,128]{2,1,0:T(8,128)(2,1)S(1)}, bf16[16,32,128]{2,1,0:T(8,128)(2,1)S(1)}, u32[]{:S(2)}, u32[]{:S(2)}) collective-permute-start(bf16[16,32,128]{2,1,0:T(8,128)(2,1)S(1)} %get-tuple-element.42), channel_id=1, source_target_pairs={{0,6},{1,7},{2,4},{3,5},{4,0},{5,1},{6,2},{7,3},{8,14},{9,15},{10,... | collective-permute-start | bytes 393224 | tf_op jit(solution)/shard_map/ppermute | solution.py:279
  38.8 5.0 %collective-permute-start.28 = (bf16[16,32,128]{2,1,0:T(8,128)(2,1)S(1)}, bf16[16,32,128]{2,1,0:T(8,128)(2,1)S(1)}, u32[]{:S(2)}, u32[]{:S(2)}) collective-permute-start(bf16[16,32,128]{2,1,0:T(8,128)(2,1)S(1)} %get-tuple-element.42), channel_id=1, source_target_pairs={{0,5},{1,4},{2,7},{3,6},{4,0},{5,1},{6,2},{7,3},{8,13},{9,12},{10,... | collective-permute-start | bytes 393224 | tf_op jit(solution)/shard_map/ppermute | solution.py:279
  39.9 3.9 %collective-permute-start.27 = (bf16[16,32,128]{2,1,0:T(8,128)(2,1)S(1)}, bf16[16,32,128]{2,1,0:T(8,128)(2,1)S(1)}, u32[]{:S(2)}, u32[]{:S(2)}) collective-permute-start(bf16[16,32,128]{2,1,0:T(8,128)(2,1)S(1)} %get-tuple-element.42), channel_id=1, source_target_pairs={{0,4},{1,5},{2,6},{3,7},{4,0},{5,1},{6,2},{7,3},{8,12},{9,13},{10,... | collective-permute-start | bytes 393224 | tf_op jit(solution)/shard_map/ppermute | solution.py:279
  40.0 3.8 %collective-permute-start.31 = (bf16[32,32,128]{2,1,0:T(8,128)(2,1)S(1)}, bf16[32,32,128]{2,1,0:T(8,128)(2,1)S(1)}, u32[]{:S(2)}, u32[]{:S(2)}) collective-permute-start(bf16[32,32,128]{2,1,0:T(8,128)(2,1)S(1)} %get-tuple-element.43.refs_3_), channel_id=1, source_target_pairs={{0,4},{1,5},{2,6},{3,7},{4,0},{5,1},{6,2},{7,3},{8,12},{9,13},{10,... | collective-permute-start | bytes 786440 | tf_op jit(solution)/shard_map/ppermute | solution.py:279
  44.1 13.2 %collective-permute-start.32 = (bf16[32,32,128]{2,1,0:T(8,128)(2,1)S(1)}, bf16[32,32,128]{2,1,0:T(8,128)(2,1)S(1)}, u32[]{:S(2)}, u32[]{:S(2)}) collective-permute-start(bf16[32,32,128]{2,1,0:T(8,128)(2,1)S(1)} %get-tuple-element.45), channel_id=1, source_target_pairs={{0,4},{1,5},{2,6},{3,7},{4,0},{5,1},{6,2},{7,3},{8,12},{9,13},{10,... | collective-permute-start | bytes 786440 | tf_op jit(solution)/shard_map/ppermute | solution.py:279
  57.8 2.1 %collective-permute-start.36 = (bf16[16,32,128]{2,1,0:T(8,128)(2,1)S(1)}, bf16[16,32,128]{2,1,0:T(8,128)(2,1)S(1)}, u32[]{:S(2)}, u32[]{:S(2)}) collective-permute-start(bf16[16,32,128]{2,1,0:T(8,128)(2,1)S(1)} %project.5), channel_id=1, source_target_pairs={{0,4},{1,5},{2,6},{3,7},{4,3},{5,2},{6,1},{7,0},{8,12},{9,13},{10,... | collective-permute-start | bytes 393224 | tf_op jit(solution)/shard_map/ppermute | solution.py:279
  57.9 4.1 %collective-permute-start.35 = (bf16[16,32,128]{2,1,0:T(8,128)(2,1)S(1)}, bf16[16,32,128]{2,1,0:T(8,128)(2,1)S(1)}, u32[]{:S(2)}, u32[]{:S(2)}) collective-permute-start(bf16[16,32,128]{2,1,0:T(8,128)(2,1)S(1)} %project.5), channel_id=1, source_target_pairs={{0,4},{1,5},{2,6},{3,7},{4,2},{5,3},{6,0},{7,1},{8,12},{9,13},{10,... | collective-permute-start | bytes 393224 | tf_op jit(solution)/shard_map/ppermute | solution.py:279
  59.3 2.7 %collective-permute-start.34 = (bf16[16,32,128]{2,1,0:T(8,128)(2,1)S(1)}, bf16[16,32,128]{2,1,0:T(8,128)(2,1)S(1)}, u32[]{:S(2)}, u32[]{:S(2)}) collective-permute-start(bf16[16,32,128]{2,1,0:T(8,128)(2,1)S(1)} %project.5), channel_id=1, source_target_pairs={{0,4},{1,5},{2,6},{3,7},{4,1},{5,0},{6,3},{7,2},{8,12},{9,13},{10,... | collective-permute-start | bytes 393224 | tf_op jit(solution)/shard_map/ppermute | solution.py:279
  59.4 2.6 %collective-permute-start.33 = (bf16[16,32,128]{2,1,0:T(8,128)(2,1)S(1)}, bf16[16,32,128]{2,1,0:T(8,128)(2,1)S(1)}, u32[]{:S(2)}, u32[]{:S(2)}) collective-permute-start(bf16[16,32,128]{2,1,0:T(8,128)(2,1)S(1)} %project.5), channel_id=1, source_target_pairs={{0,4},{1,5},{2,6},{3,7},{4,0},{5,1},{6,2},{7,3},{8,12},{9,13},{10,... | collective-permute-start | bytes 393224 | tf_op jit(solution)/shard_map/ppermute | solution.py:279
  59.8 2.2 %collective-permute-start.37 = (bf16[32,32,128]{2,1,0:T(8,128)(2,1)S(1)}, bf16[32,32,128]{2,1,0:T(8,128)(2,1)S(1)}, u32[]{:S(2)}, u32[]{:S(2)}) collective-permute-start(bf16[32,32,128]{2,1,0:T(8,128)(2,1)S(1)} %collective-permute-done.32.image), channel_id=1, source_target_pairs={{0,4},{1,5},{2,6},{3,7},{4,0},{5,1},{6,2},{7,3},{8,12},{9,13},{10,... | collective-permute-start | bytes 786440 | tf_op jit(solution)/shard_map/ppermute | solution.py:279
  62.0 6.6 %collective-permute-start.41 = (bf16[16,32,128]{2,1,0:T(8,128)(2,1)S(1)}, bf16[16,32,128]{2,1,0:T(8,128)(2,1)S(1)}, u32[]{:S(2)}, u32[]{:S(2)}) collective-permute-start(bf16[16,32,128]{2,1,0:T(8,128)(2,1)S(1)} %get-tuple-element.46), channel_id=1, source_target_pairs={{0,7},{1,6},{2,5},{3,4},{4,0},{5,1},{6,2},{7,3},{8,15},{9,14},{10,... | collective-permute-start | bytes 393224 | tf_op jit(solution)/shard_map/ppermute | solution.py:279
  65.0 5.0 %collective-permute-start.40 = (bf16[16,32,128]{2,1,0:T(8,128)(2,1)S(1)}, bf16[16,32,128]{2,1,0:T(8,128)(2,1)S(1)}, u32[]{:S(2)}, u32[]{:S(2)}) collective-permute-start(bf16[16,32,128]{2,1,0:T(8,128)(2,1)S(1)} %get-tuple-element.46), channel_id=1, source_target_pairs={{0,6},{1,7},{2,4},{3,5},{4,0},{5,1},{6,2},{7,3},{8,14},{9,15},{10,... | collective-permute-start | bytes 393224 | tf_op jit(solution)/shard_map/ppermute | solution.py:279
  65.0 4.9 %collective-permute-start.39 = (bf16[16,32,128]{2,1,0:T(8,128)(2,1)S(1)}, bf16[16,32,128]{2,1,0:T(8,128)(2,1)S(1)}, u32[]{:S(2)}, u32[]{:S(2)}) collective-permute-start(bf16[16,32,128]{2,1,0:T(8,128)(2,1)S(1)} %get-tuple-element.46), channel_id=1, source_target_pairs={{0,5},{1,4},{2,7},{3,6},{4,0},{5,1},{6,2},{7,3},{8,13},{9,12},{10,... | collective-permute-start | bytes 393224 | tf_op jit(solution)/shard_map/ppermute | solution.py:279
  66.3 3.7 %collective-permute-start.38 = (bf16[16,32,128]{2,1,0:T(8,128)(2,1)S(1)}, bf16[16,32,128]{2,1,0:T(8,128)(2,1)S(1)}, u32[]{:S(2)}, u32[]{:S(2)}) collective-permute-start(bf16[16,32,128]{2,1,0:T(8,128)(2,1)S(1)} %get-tuple-element.46), channel_id=1, source_target_pairs={{0,4},{1,5},{2,6},{3,7},{4,0},{5,1},{6,2},{7,3},{8,12},{9,13},{10,... | collective-permute-start | bytes 393224 | tf_op jit(solution)/shard_map/ppermute | solution.py:279
  66.3 4.3 %collective-permute-start.42 = (bf16[32,32,128]{2,1,0:T(8,128)(2,1)S(1)}, bf16[32,32,128]{2,1,0:T(8,128)(2,1)S(1)}, u32[]{:S(2)}, u32[]{:S(2)}) collective-permute-start(bf16[32,32,128]{2,1,0:T(8,128)(2,1)S(1)} %get-tuple-element.47.refs_3_), channel_id=1, source_target_pairs={{0,4},{1,5},{2,6},{3,7},{4,0},{5,1},{6,2},{7,3},{8,12},{9,13},{10,... | collective-permute-start | bytes 786440 | tf_op jit(solution)/shard_map/ppermute | solution.py:279

commit v23 on v14

--- a/solution.py
+++ b/solution.py
@@ -311,7 +311,7 @@
         )(*operands)
 
     blocks2 = swapped(blocks)
-    chunks = 8 if count % 8 == 0 else 1
+    chunks = 16 if count % 16 == 0 else 1
     note, table, own, blocks = pl.pallas_call(
         functools.partial(head_kernel, row_blocks, chunks),
         out_shape=(

time: 71.1 us -> 71.2 us (level)
  no operation moved by 1% of the time
where the time goes in v23:
time: 71.2 us; the launch traced here: 71 us
  waiting for transfers between devices  35.9 us (50%)
  starting transfers between devices  27.7 us (39%)
  Pallas kernels  7.1 us (10%)
    ppermute x43, waiting for transfers between devices, sent(): return lax.ppermute(value, ('subset', 'tile'), pairs)  35.9 us
    ppermute x43, starting transfers between devices, sent(): return lax.ppermute(value, ('subset', 'tile'), pairs)  27.7 us
    pallas_call x1, Pallas kernels, per_device(): pl.pallas_call(functools.partial(head_kernel, row_blocks, chunks), out_sh...  3.14 us
    pallas_call x19, Pallas kernels, call(): pl.pallas_call(kernel, out_shape=out_shape, in_specs=[SMEM] * smem + [VME...  2.16 us
  transfers between devices with their start and end apart: 43, of which 18 were waited for; matrix products, arithmetic and copies ran while one was open for 0% of the time, Pallas kernels for 8%

profile of v23, /device:TPU:25, one launch (start us, length us, event | category | flops | bytes accessed | tf_op | source)
XLA Modules:
  0.0 71.0 jit_solution(10989388054560868374)
XLA Ops:
  0.0 0.7 collective-permute-start.1
  0.8 3.1 %head.1 = (bf16[5,32,128]{2,1,0:T(8,128)(2,1)S(1)}, s32[2,80]{1,0:T(2,128)S(1)}, s32[3,80]{1,0:T(4,128)S(4)}, bf16[1,1,80,128,128]{4,3,2,1,0:T(8,128)(2,1)S(1)}) custom-call(s32[3]{0:T(128)S(1)} %pad_add_fusion.pos, s32[1,1,80]{2,1,0:T(1,128)} %rows_in.1, s32[1,1,80]{2,1,0:T(1,128)} %cols_in.1, bf16[1,1,80,128,128]{4,3,2,1,0:T(8,128)(2,1)} %blocks_in.1, ...), custom_call_target="tpu_custom_call" | custom-call | tf_op jit(solution)/shard_map/head/pallas_call | solution.py:315
  3.9 2.2 %collective-permute-start.4 = (bf16[5,32,128]{2,1,0:T(8,128)(2,1)S(1)}, bf16[5,32,128]{2,1,0:T(8,128)(2,1)S(1)}, u32[]{:S(2)}, u32[]{:S(2)}) collective-permute-start(bf16[5,32,128]{2,1,0:T(8,128)(2,1)S(1)} %get-tuple-element.31._.refs_2_), channel_id=1, source_target_pairs={{0,3},{1,2},{2,1},{3,0},{4,7},{5,6},{6,5},{7,4},{8,11},{9,10},{10,... | collective-permute-start | bytes 122888 | tf_op jit(solution)/shard_map/ppermute | solution.py:279
  6.4 0.3 collective-permute-start.2
  6.6 0.8 %collective-permute-start = (s32[2,80]{1,0:T(2,128)S(1)}, s32[2,80]{1,0:T(2,128)S(1)}, u32[]{:S(2)}, u32[]{:S(2)}) collective-permute-start(s32[2,80]{1,0:T(2,128)S(1)} %get-tuple-element.28), channel_id=1, source_target_pairs={{0,4},{1,5},{2,6},{3,7},{4,0},{5,1},{6,2},{7,3},{8,12},{9,13},{10,... | collective-permute-start | bytes 1928 | tf_op jit(solution)/shard_map/ppermute | solution.py:279
  7.5 0.5 pack_own.1.refs_1_
  7.9 0.3 collective-permute-done.table2
  8.3 1.3 %pack_other.1 = (s32[3,80]{1,0:T(4,128)S(4)}, bf16[16,640,128]{2,1,0:T(8,128)(2,1)S(1)}) custom-call(s32[3,80]{1,0:T(4,128)S(4)} %get-tuple-element.27.own, s32[2,80]{1,0:T(2,128)S(1)} %collective-permute-done.table2, bf16[1,1,80,128,128]{4,3,2,1,0:T(8,128)(2,1)S(1)} %collective-permute-done.1.blocks2), custom_call_target="tpu_custom_call" | custom-call | tf_op jit(solution)/shard_map/pack_other/pallas_call | solution.py:356
  9.7 1.3 %collective-permute-start.8 = (bf16[16,32,128]{2,1,0:T(8,128)(2,1)S(1)}, bf16[16,32,128]{2,1,0:T(8,128)(2,1)S(1)}, u32[]{:S(2)}, u32[]{:S(2)}) collective-permute-start(bf16[16,32,128]{2,1,0:T(8,128)(2,1)S(1)} %get-tuple-element.35), channel_id=1, source_target_pairs={{0,7},{1,6},{2,5},{3,4},{4,0},{5,1},{6,2},{7,3},{8,15},{9,14},{10,... | collective-permute-start | bytes 393224 | tf_op jit(solution)/shard_map/ppermute | solution.py:279
  11.1 1.3 %collective-permute-start.7 = (bf16[16,32,128]{2,1,0:T(8,128)(2,1)S(1)}, bf16[16,32,128]{2,1,0:T(8,128)(2,1)S(1)}, u32[]{:S(2)}, u32[]{:S(2)}) collective-permute-start(bf16[16,32,128]{2,1,0:T(8,128)(2,1)S(1)} %get-tuple-element.35), channel_id=1, source_target_pairs={{0,6},{1,7},{2,4},{3,5},{4,0},{5,1},{6,2},{7,3},{8,14},{9,15},{10,... | collective-permute-start | bytes 393224 | tf_op jit(solution)/shard_map/ppermute | solution.py:279
  12.3 0.3 collective-permute-start.6
  12.7 0.3 collective-permute-start.5
  13.2 2.0 %collective-permute-done.8.refs_6_ = bf16[16,32,128]{2,1,0:T(8,128)(2,1)S(1)} collective-permute-done((bf16[16,32,128]{2,1,0:T(8,128)(2,1)S(1)}, bf16[16,32,128]{2,1,0:T(8,128)(2,1)S(1)}, u32[]{:S(2)}, u32[]{:S(2)}) %collective-permute-start.8) | collective-permute-done | bytes 131104 | tf_op jit(solution)/shard_map/ppermute | solution.py:279
  15.2 1.3 %collective-permute-done.7.refs_5_ = bf16[16,32,128]{2,1,0:T(8,128)(2,1)S(1)} collective-permute-done((bf16[16,32,128]{2,1,0:T(8,128)(2,1)S(1)}, bf16[16,32,128]{2,1,0:T(8,128)(2,1)S(1)}, u32[]{:S(2)}, u32[]{:S(2)}) %collective-permute-start.7) | collective-permute-done | bytes 131104 | tf_op jit(solution)/shard_map/ppermute | solution.py:279
  16.5 0.3 collective-permute-done.6.refs_4_
  16.8 1.5 %collective-permute-done.10.image = bf16[32,32,128]{2,1,0:T(8,128)(2,1)S(1)} collective-permute-done((bf16[32,32,128]{2,1,0:T(8,128)(2,1)S(1)}, bf16[32,32,128]{2,1,0:T(8,128)(2,1)S(1)}, u32[]{:S(2)}, u32[]{:S(2)}) %collective-permute-start.10) | collective-permute-done | bytes 262176 | tf_op jit(solution)/shard_map/ppermute | solution.py:279
  18.4 1.4 %collective-permute-start.14 = (bf16[16,32,128]{2,1,0:T(8,128)(2,1)S(1)}, bf16[16,32,128]{2,1,0:T(8,128)(2,1)S(1)}, u32[]{:S(2)}, u32[]{:S(2)}) collective-permute-start(bf16[16,32,128]{2,1,0:T(8,128)(2,1)S(1)} %project.3), channel_id=1, source_target_pairs={{0,4},{1,5},{2,6},{3,7},{4,3},{5,2},{6,1},{7,0},{8,12},{9,13},{10,... | collective-permute-start | bytes 393224 | tf_op jit(solution)/shard_map/ppermute | solution.py:279
  19.7 1.2 %collective-permute-start.12 = (bf16[16,32,128]{2,1,0:T(8,128)(2,1)S(1)}, bf16[16,32,128]{2,1,0:T(8,128)(2,1)S(1)}, u32[]{:S(2)}, u32[]{:S(2)}) collective-permute-start(bf16[16,32,128]{2,1,0:T(8,128)(2,1)S(1)} %project.3), channel_id=1, source_target_pairs={{0,4},{1,5},{2,6},{3,7},{4,1},{5,0},{6,3},{7,2},{8,12},{9,13},{10,... | collective-permute-start | bytes 393224 | tf_op jit(solution)/shard_map/ppermute | solution.py:279
  20.9 0.5 collective-permute-start.15
  21.7 1.4 %collective-permute-done.13.refs_5_ = bf16[16,32,128]{2,1,0:T(8,128)(2,1)S(1)} collective-permute-done((bf16[16,32,128]{2,1,0:T(8,128)(2,1)S(1)}, bf16[16,32,128]{2,1,0:T(8,128)(2,1)S(1)}, u32[]{:S(2)}, u32[]{:S(2)}) %collective-permute-start.13) | collective-permute-done | bytes 131104 | tf_op jit(solution)/shard_map/ppermute | solution.py:279
  23.1 2.1 %collective-permute-start.19 = (bf16[16,32,128]{2,1,0:T(8,128)(2,1)S(1)}, bf16[16,32,128]{2,1,0:T(8,128)(2,1)S(1)}, u32[]{:S(2)}, u32[]{:S(2)}) collective-permute-start(bf16[16,32,128]{2,1,0:T(8,128)(2,1)S(1)} %get-tuple-element.38), channel_id=1, source_target_pairs={{0,7},{1,6},{2,5},{3,4},{4,0},{5,1},{6,2},{7,3},{8,15},{9,14},{10,... | collective-permute-start | bytes 393224 | tf_op jit(solution)/shard_map/ppermute | solution.py:279
  25.2 0.9 %collective-permute-start.17 = (bf16[16,32,128]{2,1,0:T(8,128)(2,1)S(1)}, bf16[16,32,128]{2,1,0:T(8,128)(2,1)S(1)}, u32[]{:S(2)}, u32[]{:S(2)}) collective-permute-start(bf16[16,32,128]{2,1,0:T(8,128)(2,1)S(1)} %get-tuple-element.38), channel_id=1, source_target_pairs={{0,5},{1,4},{2,7},{3,6},{4,0},{5,1},{6,2},{7,3},{8,13},{9,12},{10,... | collective-permute-start | bytes 393224 | tf_op jit(solution)/shard_map/ppermute | solution.py:279
  26.3 0.4 collective-permute-start.20
  26.6 2.3 %collective-permute-done.19.refs_6_ = bf16[16,32,128]{2,1,0:T(8,128)(2,1)S(1)} collective-permute-done((bf16[16,32,128]{2,1,0:T(8,128)(2,1)S(1)}, bf16[16,32,128]{2,1,0:T(8,128)(2,1)S(1)}, u32[]{:S(2)}, u32[]{:S(2)}) %collective-permute-start.19) | collective-permute-done | bytes 131104 | tf_op jit(solution)/shard_map/ppermute | solution.py:279
  29.0 1.3 %collective-permute-done.18.refs_5_ = bf16[16,32,128]{2,1,0:T(8,128)(2,1)S(1)} collective-permute-done((bf16[16,32,128]{2,1,0:T(8,128)(2,1)S(1)}, bf16[16,32,128]{2,1,0:T(8,128)(2,1)S(1)}, u32[]{:S(2)}, u32[]{:S(2)}) %collective-permute-start.18) | collective-permute-done | bytes 131104 | tf_op jit(solution)/shard_map/ppermute | solution.py:279
  30.5 1.5 %collective-permute-done.21.image = bf16[32,32,128]{2,1,0:T(8,128)(2,1)S(1)} collective-permute-done((bf16[32,32,128]{2,1,0:T(8,128)(2,1)S(1)}, bf16[32,32,128]{2,1,0:T(8,128)(2,1)S(1)}, u32[]{:S(2)}, u32[]{:S(2)}) %collective-permute-start.21) | collective-permute-done | bytes 262176 | tf_op jit(solution)/shard_map/ppermute | solution.py:279
  32.0 1.2 %collective-permute-start.25 = (bf16[16,32,128]{2,1,0:T(8,128)(2,1)S(1)}, bf16[16,32,128]{2,1,0:T(8,128)(2,1)S(1)}, u32[]{:S(2)}, u32[]{:S(2)}) collective-permute-start(bf16[16,32,128]{2,1,0:T(8,128)(2,1)S(1)} %project.4), channel_id=1, source_target_pairs={{0,4},{1,5},{2,6},{3,7},{4,3},{5,2},{6,1},{7,0},{8,12},{9,13},{10,... | collective-permute-start | bytes 393224 | tf_op jit(solution)/shard_map/ppermute | solution.py:279
  33.2 1.0 %collective-permute-start.23 = (bf16[16,32,128]{2,1,0:T(8,128)(2,1)S(1)}, bf16[16,32,128]{2,1,0:T(8,128)(2,1)S(1)}, u32[]{:S(2)}, u32[]{:S(2)}) collective-permute-start(bf16[16,32,128]{2,1,0:T(8,128)(2,1)S(1)} %project.4), channel_id=1, source_target_pairs={{0,4},{1,5},{2,6},{3,7},{4,1},{5,0},{6,3},{7,2},{8,12},{9,13},{10,... | collective-permute-start | bytes 393224 | tf_op jit(solution)/shard_map/ppermute | solution.py:279
  34.2 0.5 collective-permute-start.26
  34.7 0.4 collective-permute-done.25.refs_6_
  35.1 1.4 %collective-permute-done.24.refs_5_ = bf16[16,32,128]{2,1,0:T(8,128)(2,1)S(1)} collective-permute-done((bf16[16,32,128]{2,1,0:T(8,128)(2,1)S(1)}, bf16[16,32,128]{2,1,0:T(8,128)(2,1)S(1)}, u32[]{:S(2)}, u32[]{:S(2)}) %collective-permute-start.24) | collective-permute-done | bytes 131104 | tf_op jit(solution)/shard_map/ppermute | solution.py:279
  36.5 1.9 %collective-permute-start.30 = (bf16[16,32,128]{2,1,0:T(8,128)(2,1)S(1)}, bf16[16,32,128]{2,1,0:T(8,128)(2,1)S(1)}, u32[]{:S(2)}, u32[]{:S(2)}) collective-permute-start(bf16[16,32,128]{2,1,0:T(8,128)(2,1)S(1)} %get-tuple-element.42), channel_id=1, source_target_pairs={{0,7},{1,6},{2,5},{3,4},{4,0},{5,1},{6,2},{7,3},{8,15},{9,14},{10,... | collective-permute-start | bytes 393224 | tf_op jit(solution)/shard_map/ppermute | solution.py:279
  38.4 1.2 %collective-permute-start.28 = (bf16[16,32,128]{2,1,0:T(8,128)(2,1)S(1)}, bf16[16,32,128]{2,1,0:T(8,128)(2,1)S(1)}, u32[]{:S(2)}, u32[]{:S(2)}) collective-permute-start(bf16[16,32,128]{2,1,0:T(8,128)(2,1)S(1)} %get-tuple-element.42), channel_id=1, source_target_pairs={{0,5},{1,4},{2,7},{3,6},{4,0},{5,1},{6,2},{7,3},{8,13},{9,12},{10,... | collective-permute-start | bytes 393224 | tf_op jit(solution)/shard_map/ppermute | solution.py:279
  39.7 0.5 collective-permute-start.31
  40.1 2.0 %collective-permute-done.30.refs_6_ = bf16[16,32,128]{2,1,0:T(8,128)(2,1)S(1)} collective-permute-done((bf16[16,32,128]{2,1,0:T(8,128)(2,1)S(1)}, bf16[16,32,128]{2,1,0:T(8,128)(2,1)S(1)}, u32[]{:S(2)}, u32[]{:S(2)}) %collective-permute-start.30) | collective-permute-done | bytes 131104 | tf_op jit(solution)/shard_map/ppermute | solution.py:279
  42.1 1.3 %collective-permute-done.29.refs_5_ = bf16[16,32,128]{2,1,0:T(8,128)(2,1)S(1)} collective-permute-done((bf16[16,32,128]{2,1,0:T(8,128)(2,1)S(1)}, bf16[16,32,128]{2,1,0:T(8,128)(2,1)S(1)}, u32[]{:S(2)}, u32[]{:S(2)}) %collective-permute-start.29) | collective-permute-done | bytes 131104 | tf_op jit(solution)/shard_map/ppermute | solution.py:279
  43.7 13.3 %collective-permute-done.32.image = bf16[32,32,128]{2,1,0:T(8,128)(2,1)S(1)} collective-permute-done((bf16[32,32,128]{2,1,0:T(8,128)(2,1)S(1)}, bf16[32,32,128]{2,1,0:T(8,128)(2,1)S(1)}, u32[]{:S(2)}, u32[]{:S(2)}) %collective-permute-start.32) | collective-permute-done | bytes 262176 | tf_op jit(solution)/shard_map/ppermute | solution.py:279
  57.0 0.5 project.5
  57.6 1.4 %collective-permute-start.35 = (bf16[16,32,128]{2,1,0:T(8,128)(2,1)S(1)}, bf16[16,32,128]{2,1,0:T(8,128)(2,1)S(1)}, u32[]{:S(2)}, u32[]{:S(2)}) collective-permute-start(bf16[16,32,128]{2,1,0:T(8,128)(2,1)S(1)} %project.5), channel_id=1, source_target_pairs={{0,4},{1,5},{2,6},{3,7},{4,2},{5,3},{6,0},{7,1},{8,12},{9,13},{10,... | collective-permute-start | bytes 393224 | tf_op jit(solution)/shard_map/ppermute | solution.py:279
  59.1 0.4 collective-permute-start.33
  59.6 2.1 %collective-permute-done.35.refs_5_ = bf16[16,32,128]{2,1,0:T(8,128)(2,1)S(1)} collective-permute-done((bf16[16,32,128]{2,1,0:T(8,128)(2,1)S(1)}, bf16[16,32,128]{2,1,0:T(8,128)(2,1)S(1)}, u32[]{:S(2)}, u32[]{:S(2)}) %collective-permute-start.35) | collective-permute-done | bytes 131104 | tf_op jit(solution)/shard_map/ppermute | solution.py:279
  61.7 2.9 %collective-permute-start.41 = (bf16[16,32,128]{2,1,0:T(8,128)(2,1)S(1)}, bf16[16,32,128]{2,1,0:T(8,128)(2,1)S(1)}, u32[]{:S(2)}, u32[]{:S(2)}) collective-permute-start(bf16[16,32,128]{2,1,0:T(8,128)(2,1)S(1)} %get-tuple-element.46), channel_id=1, source_target_pairs={{0,7},{1,6},{2,5},{3,4},{4,0},{5,1},{6,2},{7,3},{8,15},{9,14},{10,... | collective-permute-start | bytes 393224 | tf_op jit(solution)/shard_map/ppermute | solution.py:279
  64.7 1.2 %collective-permute-start.39 = (bf16[16,32,128]{2,1,0:T(8,128)(2,1)S(1)}, bf16[16,32,128]{2,1,0:T(8,128)(2,1)S(1)}, u32[]{:S(2)}, u32[]{:S(2)}) collective-permute-start(bf16[16,32,128]{2,1,0:T(8,128)(2,1)S(1)} %get-tuple-element.46), channel_id=1, source_target_pairs={{0,5},{1,4},{2,7},{3,6},{4,0},{5,1},{6,2},{7,3},{8,13},{9,12},{10,... | collective-permute-start | bytes 393224 | tf_op jit(solution)/shard_map/ppermute | solution.py:279
  66.0 0.5 collective-permute-start.42
  66.5 1.8 %collective-permute-done.41.refs_6_ = bf16[16,32,128]{2,1,0:T(8,128)(2,1)S(1)} collective-permute-done((bf16[16,32,128]{2,1,0:T(8,128)(2,1)S(1)}, bf16[16,32,128]{2,1,0:T(8,128)(2,1)S(1)}, u32[]{:S(2)}, u32[]{:S(2)}) %collective-permute-start.41) | collective-permute-done | bytes 131104 | tf_op jit(solution)/shard_map/ppermute | solution.py:279
  68.3 1.3 %collective-permute-done.40.refs_5_ = bf16[16,32,128]{2,1,0:T(8,128)(2,1)S(1)} collective-permute-done((bf16[16,32,128]{2,1,0:T(8,128)(2,1)S(1)}, bf16[16,32,128]{2,1,0:T(8,128)(2,1)S(1)}, u32[]{:S(2)}, u32[]{:S(2)}) %collective-permute-start.40) | collective-permute-done | bytes 131104 | tf_op jit(solution)/shard_map/ppermute | solution.py:279
  69.6 0.6 update.15.refs_1_
  70.2 0.8 %second.7 = bf16[4,8,4096]{2,1,0:T(8,128)(2,1)} custom-call(s32[3,80]{1,0:T(4,128)S(4)} %get-tuple-element.29.refs_0_.info, f32[32,32,128]{2,1,0:T(8,128)S(1)} %update.15.refs_1_, bf16[32,32,128]{2,1,0:T(8,128)(2,1)S(1)} %collective-permute-done.42.refs_2_, bf16[32,32,128]{2,1,0:T(8,128)(2,1)S(1)} %get-tuple-element.47.refs_3_, ...), custom_call_target="tpu_custom_call" | custom-call | tf_op jit(solution)/shard_map/second/pallas_call | solution.py:300
  (61 shorter events, 2.0 us)
Async XLA Ops:
  0.0 8.3 %collective-permute-start.1 = (bf16[1,1,80,128,128]{4,3,2,1,0:T(8,128)(2,1)}, bf16[1,1,80,128,128]{4,3,2,1,0:T(8,128)(2,1)S(1)}, u32[]{:S(2)}, u32[]{:S(2)}) collective-permute-start(bf16[1,1,80,128,128]{4,3,2,1,0:T(8,128)(2,1)} %blocks_in.1), channel_id=1, source_target_pairs={{0,4},{1,5},{2,6},{3,7},{4,0},{5,1},{6,2},{7,3},{8,12},{9,13},{10,... | collective-permute-start | bytes 7864328 | tf_op jit(solution)/shard_map/ppermute | solution.py:279
  3.9 5.7 %collective-permute-start.4 = (bf16[5,32,128]{2,1,0:T(8,128)(2,1)S(1)}, bf16[5,32,128]{2,1,0:T(8,128)(2,1)S(1)}, u32[]{:S(2)}, u32[]{:S(2)}) collective-permute-start(bf16[5,32,128]{2,1,0:T(8,128)(2,1)S(1)} %get-tuple-element.31._.refs_2_), channel_id=1, source_target_pairs={{0,3},{1,2},{2,1},{3,0},{4,7},{5,6},{6,5},{7,4},{8,11},{9,10},{10,... | collective-permute-start | bytes 122888 | tf_op jit(solution)/shard_map/ppermute | solution.py:279
  6.1 3.5 %collective-permute-start.3 = (bf16[5,32,128]{2,1,0:T(8,128)(2,1)S(1)}, bf16[5,32,128]{2,1,0:T(8,128)(2,1)S(1)}, u32[]{:S(2)}, u32[]{:S(2)}) collective-permute-start(bf16[5,32,128]{2,1,0:T(8,128)(2,1)S(1)} %get-tuple-element.31._.refs_2_), channel_id=1, source_target_pairs={{0,2},{1,3},{2,0},{3,1},{4,6},{5,7},{6,4},{7,5},{8,10},{9,11},{10,... | collective-permute-start | bytes 122888 | tf_op jit(solution)/shard_map/ppermute | solution.py:279
  6.4 3.3 %collective-permute-start.2 = (bf16[5,32,128]{2,1,0:T(8,128)(2,1)S(1)}, bf16[5,32,128]{2,1,0:T(8,128)(2,1)S(1)}, u32[]{:S(2)}, u32[]{:S(2)}) collective-permute-start(bf16[5,32,128]{2,1,0:T(8,128)(2,1)S(1)} %get-tuple-element.31._.refs_2_), channel_id=1, source_target_pairs={{0,1},{1,0},{2,3},{3,2},{4,5},{5,4},{6,7},{7,6},{8,9},{9,8},{10,11... | collective-permute-start | bytes 122888 | tf_op jit(solution)/shard_map/ppermute | solution.py:279
  6.6 1.7 %collective-permute-start = (s32[2,80]{1,0:T(2,128)S(1)}, s32[2,80]{1,0:T(2,128)S(1)}, u32[]{:S(2)}, u32[]{:S(2)}) collective-permute-start(s32[2,80]{1,0:T(2,128)S(1)} %get-tuple-element.28), channel_id=1, source_target_pairs={{0,4},{1,5},{2,6},{3,7},{4,0},{5,1},{6,2},{7,3},{8,12},{9,13},{10,... | collective-permute-start | bytes 1928 | tf_op jit(solution)/shard_map/ppermute | solution.py:279
  9.7 5.4 %collective-permute-start.8 = (bf16[16,32,128]{2,1,0:T(8,128)(2,1)S(1)}, bf16[16,32,128]{2,1,0:T(8,128)(2,1)S(1)}, u32[]{:S(2)}, u32[]{:S(2)}) collective-permute-start(bf16[16,32,128]{2,1,0:T(8,128)(2,1)S(1)} %get-tuple-element.35), channel_id=1, source_target_pairs={{0,7},{1,6},{2,5},{3,4},{4,0},{5,1},{6,2},{7,3},{8,15},{9,14},{10,... | collective-permute-start | bytes 393224 | tf_op jit(solution)/shard_map/ppermute | solution.py:279
  11.1 5.4 %collective-permute-start.7 = (bf16[16,32,128]{2,1,0:T(8,128)(2,1)S(1)}, bf16[16,32,128]{2,1,0:T(8,128)(2,1)S(1)}, u32[]{:S(2)}, u32[]{:S(2)}) collective-permute-start(bf16[16,32,128]{2,1,0:T(8,128)(2,1)S(1)} %get-tuple-element.35), channel_id=1, source_target_pairs={{0,6},{1,7},{2,4},{3,5},{4,0},{5,1},{6,2},{7,3},{8,14},{9,15},{10,... | collective-permute-start | bytes 393224 | tf_op jit(solution)/shard_map/ppermute | solution.py:279
  12.3 4.4 %collective-permute-start.6 = (bf16[16,32,128]{2,1,0:T(8,128)(2,1)S(1)}, bf16[16,32,128]{2,1,0:T(8,128)(2,1)S(1)}, u32[]{:S(2)}, u32[]{:S(2)}) collective-permute-start(bf16[16,32,128]{2,1,0:T(8,128)(2,1)S(1)} %get-tuple-element.35), channel_id=1, source_target_pairs={{0,5},{1,4},{2,7},{3,6},{4,0},{5,1},{6,2},{7,3},{8,13},{9,12},{10,... | collective-permute-start | bytes 393224 | tf_op jit(solution)/shard_map/ppermute | solution.py:279
  12.7 4.1 %collective-permute-start.5 = (bf16[16,32,128]{2,1,0:T(8,128)(2,1)S(1)}, bf16[16,32,128]{2,1,0:T(8,128)(2,1)S(1)}, u32[]{:S(2)}, u32[]{:S(2)}) collective-permute-start(bf16[16,32,128]{2,1,0:T(8,128)(2,1)S(1)} %get-tuple-element.35), channel_id=1, source_target_pairs={{0,4},{1,5},{2,6},{3,7},{4,0},{5,1},{6,2},{7,3},{8,12},{9,13},{10,... | collective-permute-start | bytes 393224 | tf_op jit(solution)/shard_map/ppermute | solution.py:279
  13.0 3.7 %collective-permute-start.9 = (bf16[32,32,128]{2,1,0:T(8,128)(2,1)S(1)}, bf16[32,32,128]{2,1,0:T(8,128)(2,1)S(1)}, u32[]{:S(2)}, u32[]{:S(2)}) collective-permute-start(bf16[32,32,128]{2,1,0:T(8,128)(2,1)S(1)} %get-tuple-element.36.refs_3_), channel_id=1, source_target_pairs={{0,4},{1,5},{2,6},{3,7},{4,0},{5,1},{6,2},{7,3},{8,12},{9,13},{10,... | collective-permute-start | bytes 786440 | tf_op jit(solution)/shard_map/ppermute | solution.py:279
  16.8 1.6 %collective-permute-start.10 = (bf16[32,32,128]{2,1,0:T(8,128)(2,1)S(1)}, bf16[32,32,128]{2,1,0:T(8,128)(2,1)S(1)}, u32[]{:S(2)}, u32[]{:S(2)}) collective-permute-start(bf16[32,32,128]{2,1,0:T(8,128)(2,1)S(1)} %get-tuple-element.37), channel_id=1, source_target_pairs={{0,4},{1,5},{2,6},{3,7},{4,12},{5,13},{6,14},{7,15},{8,0},{9,1},{1... | collective-permute-start | bytes 786440 | tf_op jit(solution)/shard_map/ppermute | solution.py:279
  18.4 3.3 %collective-permute-start.14 = (bf16[16,32,128]{2,1,0:T(8,128)(2,1)S(1)}, bf16[16,32,128]{2,1,0:T(8,128)(2,1)S(1)}, u32[]{:S(2)}, u32[]{:S(2)}) collective-permute-start(bf16[16,32,128]{2,1,0:T(8,128)(2,1)S(1)} %project.3), channel_id=1, source_target_pairs={{0,4},{1,5},{2,6},{3,7},{4,3},{5,2},{6,1},{7,0},{8,12},{9,13},{10,... | collective-permute-start | bytes 393224 | tf_op jit(solution)/shard_map/ppermute | solution.py:279
  19.7 3.3 %collective-permute-start.13 = (bf16[16,32,128]{2,1,0:T(8,128)(2,1)S(1)}, bf16[16,32,128]{2,1,0:T(8,128)(2,1)S(1)}, u32[]{:S(2)}, u32[]{:S(2)}) collective-permute-start(bf16[16,32,128]{2,1,0:T(8,128)(2,1)S(1)} %project.3), channel_id=1, source_target_pairs={{0,4},{1,5},{2,6},{3,7},{4,2},{5,3},{6,0},{7,1},{8,12},{9,13},{10,... | collective-permute-start | bytes 393224 | tf_op jit(solution)/shard_map/ppermute | solution.py:279
  19.7 3.3 %collective-permute-start.12 = (bf16[16,32,128]{2,1,0:T(8,128)(2,1)S(1)}, bf16[16,32,128]{2,1,0:T(8,128)(2,1)S(1)}, u32[]{:S(2)}, u32[]{:S(2)}) collective-permute-start(bf16[16,32,128]{2,1,0:T(8,128)(2,1)S(1)} %project.3), channel_id=1, source_target_pairs={{0,4},{1,5},{2,6},{3,7},{4,1},{5,0},{6,3},{7,2},{8,12},{9,13},{10,... | collective-permute-start | bytes 393224 | tf_op jit(solution)/shard_map/ppermute | solution.py:279
  20.9 2.1 %collective-permute-start.11 = (bf16[16,32,128]{2,1,0:T(8,128)(2,1)S(1)}, bf16[16,32,128]{2,1,0:T(8,128)(2,1)S(1)}, u32[]{:S(2)}, u32[]{:S(2)}) collective-permute-start(bf16[16,32,128]{2,1,0:T(8,128)(2,1)S(1)} %project.3), channel_id=1, source_target_pairs={{0,4},{1,5},{2,6},{3,7},{4,0},{5,1},{6,2},{7,3},{8,12},{9,13},{10,... | collective-permute-start | bytes 393224 | tf_op jit(solution)/shard_map/ppermute | solution.py:279
  20.9 2.1 %collective-permute-start.15 = (bf16[32,32,128]{2,1,0:T(8,128)(2,1)S(1)}, bf16[32,32,128]{2,1,0:T(8,128)(2,1)S(1)}, u32[]{:S(2)}, u32[]{:S(2)}) collective-permute-start(bf16[32,32,128]{2,1,0:T(8,128)(2,1)S(1)} %collective-permute-done.10.image), channel_id=1, source_target_pairs={{0,4},{1,5},{2,6},{3,7},{4,0},{5,1},{6,2},{7,3},{8,12},{9,13},{10,... | collective-permute-start | bytes 786440 | tf_op jit(solution)/shard_map/ppermute | solution.py:279
  23.1 5.9 %collective-permute-start.19 = (bf16[16,32,128]{2,1,0:T(8,128)(2,1)S(1)}, bf16[16,32,128]{2,1,0:T(8,128)(2,1)S(1)}, u32[]{:S(2)}, u32[]{:S(2)}) collective-permute-start(bf16[16,32,128]{2,1,0:T(8,128)(2,1)S(1)} %get-tuple-element.38), channel_id=1, source_target_pairs={{0,7},{1,6},{2,5},{3,4},{4,0},{5,1},{6,2},{7,3},{8,15},{9,14},{10,... | collective-permute-start | bytes 393224 | tf_op jit(solution)/shard_map/ppermute | solution.py:279
  25.1 5.2 %collective-permute-start.18 = (bf16[16,32,128]{2,1,0:T(8,128)(2,1)S(1)}, bf16[16,32,128]{2,1,0:T(8,128)(2,1)S(1)}, u32[]{:S(2)}, u32[]{:S(2)}) collective-permute-start(bf16[16,32,128]{2,1,0:T(8,128)(2,1)S(1)} %get-tuple-element.38), channel_id=1, source_target_pairs={{0,6},{1,7},{2,4},{3,5},{4,0},{5,1},{6,2},{7,3},{8,14},{9,15},{10,... | collective-permute-start | bytes 393224 | tf_op jit(solution)/shard_map/ppermute | solution.py:279
  25.2 5.1 %collective-permute-start.17 = (bf16[16,32,128]{2,1,0:T(8,128)(2,1)S(1)}, bf16[16,32,128]{2,1,0:T(8,128)(2,1)S(1)}, u32[]{:S(2)}, u32[]{:S(2)}) collective-permute-start(bf16[16,32,128]{2,1,0:T(8,128)(2,1)S(1)} %get-tuple-element.38), channel_id=1, source_target_pairs={{0,5},{1,4},{2,7},{3,6},{4,0},{5,1},{6,2},{7,3},{8,13},{9,12},{10,... | collective-permute-start | bytes 393224 | tf_op jit(solution)/shard_map/ppermute | solution.py:279
  26.1 4.2 %collective-permute-start.16 = (bf16[16,32,128]{2,1,0:T(8,128)(2,1)S(1)}, bf16[16,32,128]{2,1,0:T(8,128)(2,1)S(1)}, u32[]{:S(2)}, u32[]{:S(2)}) collective-permute-start(bf16[16,32,128]{2,1,0:T(8,128)(2,1)S(1)} %get-tuple-element.38), channel_id=1, source_target_pairs={{0,4},{1,5},{2,6},{3,7},{4,0},{5,1},{6,2},{7,3},{8,12},{9,13},{10,... | collective-permute-start | bytes 393224 | tf_op jit(solution)/shard_map/ppermute | solution.py:279
  26.3 4.0 %collective-permute-start.20 = (bf16[32,32,128]{2,1,0:T(8,128)(2,1)S(1)}, bf16[32,32,128]{2,1,0:T(8,128)(2,1)S(1)}, u32[]{:S(2)}, u32[]{:S(2)}) collective-permute-start(bf16[32,32,128]{2,1,0:T(8,128)(2,1)S(1)} %get-tuple-element.39.refs_3_), channel_id=1, source_target_pairs={{0,4},{1,5},{2,6},{3,7},{4,0},{5,1},{6,2},{7,3},{8,12},{9,13},{10,... | collective-permute-start | bytes 786440 | tf_op jit(solution)/shard_map/ppermute | solution.py:279
  30.4 1.6 %collective-permute-start.21 = (bf16[32,32,128]{2,1,0:T(8,128)(2,1)S(1)}, bf16[32,32,128]{2,1,0:T(8,128)(2,1)S(1)}, u32[]{:S(2)}, u32[]{:S(2)}) collective-permute-start(bf16[32,32,128]{2,1,0:T(8,128)(2,1)S(1)} %get-tuple-element.41), channel_id=1, source_target_pairs={{0,4},{1,5},{2,6},{3,7},{4,0},{5,1},{6,2},{7,3},{8,12},{9,13},{10,... | collective-permute-start | bytes 786440 | tf_op jit(solution)/shard_map/ppermute | solution.py:279
  32.0 3.1 %collective-permute-start.25 = (bf16[16,32,128]{2,1,0:T(8,128)(2,1)S(1)}, bf16[16,32,128]{2,1,0:T(8,128)(2,1)S(1)}, u32[]{:S(2)}, u32[]{:S(2)}) collective-permute-start(bf16[16,32,128]{2,1,0:T(8,128)(2,1)S(1)} %project.4), channel_id=1, source_target_pairs={{0,4},{1,5},{2,6},{3,7},{4,3},{5,2},{6,1},{7,0},{8,12},{9,13},{10,... | collective-permute-start | bytes 393224 | tf_op jit(solution)/shard_map/ppermute | solution.py:279
  33.2 3.3 %collective-permute-start.24 = (bf16[16,32,128]{2,1,0:T(8,128)(2,1)S(1)}, bf16[16,32,128]{2,1,0:T(8,128)(2,1)S(1)}, u32[]{:S(2)}, u32[]{:S(2)}) collective-permute-start(bf16[16,32,128]{2,1,0:T(8,128)(2,1)S(1)} %project.4), channel_id=1, source_target_pairs={{0,4},{1,5},{2,6},{3,7},{4,2},{5,3},{6,0},{7,1},{8,12},{9,13},{10,... | collective-permute-start | bytes 393224 | tf_op jit(solution)/shard_map/ppermute | solution.py:279
  33.2 3.4 %collective-permute-start.23 = (bf16[16,32,128]{2,1,0:T(8,128)(2,1)S(1)}, bf16[16,32,128]{2,1,0:T(8,128)(2,1)S(1)}, u32[]{:S(2)}, u32[]{:S(2)}) collective-permute-start(bf16[16,32,128]{2,1,0:T(8,128)(2,1)S(1)} %project.4), channel_id=1, source_target_pairs={{0,4},{1,5},{2,6},{3,7},{4,1},{5,0},{6,3},{7,2},{8,12},{9,13},{10,... | collective-permute-start | bytes 393224 | tf_op jit(solution)/shard_map/ppermute | solution.py:279
  34.2 2.3 %collective-permute-start.22 = (bf16[16,32,128]{2,1,0:T(8,128)(2,1)S(1)}, bf16[16,32,128]{2,1,0:T(8,128)(2,1)S(1)}, u32[]{:S(2)}, u32[]{:S(2)}) collective-permute-start(bf16[16,32,128]{2,1,0:T(8,128)(2,1)S(1)} %project.4), channel_id=1, source_target_pairs={{0,4},{1,5},{2,6},{3,7},{4,0},{5,1},{6,2},{7,3},{8,12},{9,13},{10,... | collective-permute-start | bytes 393224 | tf_op jit(solution)/shard_map/ppermute | solution.py:279
  34.2 2.3 %collective-permute-start.26 = (bf16[32,32,128]{2,1,0:T(8,128)(2,1)S(1)}, bf16[32,32,128]{2,1,0:T(8,128)(2,1)S(1)}, u32[]{:S(2)}, u32[]{:S(2)}) collective-permute-start(bf16[32,32,128]{2,1,0:T(8,128)(2,1)S(1)} %collective-permute-done.21.image), channel_id=1, source_target_pairs={{0,4},{1,5},{2,6},{3,7},{4,0},{5,1},{6,2},{7,3},{8,12},{9,13},{10,... | collective-permute-start | bytes 786440 | tf_op jit(solution)/shard_map/ppermute | solution.py:279
  36.5 5.6 %collective-permute-start.30 = (bf16[16,32,128]{2,1,0:T(8,128)(2,1)S(1)}, bf16[16,32,128]{2,1,0:T(8,128)(2,1)S(1)}, u32[]{:S(2)}, u32[]{:S(2)}) collective-permute-start(bf16[16,32,128]{2,1,0:T(8,128)(2,1)S(1)} %get-tuple-element.42), channel_id=1, source_target_pairs={{0,7},{1,6},{2,5},{3,4},{4,0},{5,1},{6,2},{7,3},{8,15},{9,14},{10,... | collective-permute-start | bytes 393224 | tf_op jit(solution)/shard_map/ppermute | solution.py:279
  38.4 5.1 %collective-permute-start.29 = (bf16[16,32,128]{2,1,0:T(8,128)(2,1)S(1)}, bf16[16,32,128]{2,1,0:T(8,128)(2,1)S(1)}, u32[]{:S(2)}, u32[]{:S(2)}) collective-permute-start(bf16[16,32,128]{2,1,0:T(8,128)(2,1)S(1)} %get-tuple-element.42), channel_id=1, source_target_pairs={{0,6},{1,7},{2,4},{3,5},{4,0},{5,1},{6,2},{7,3},{8,14},{9,15},{10,... | collective-permute-start | bytes 393224 | tf_op jit(solution)/shard_map/ppermute | solution.py:279
  38.4 5.0 %collective-permute-start.28 = (bf16[16,32,128]{2,1,0:T(8,128)(2,1)S(1)}, bf16[16,32,128]{2,1,0:T(8,128)(2,1)S(1)}, u32[]{:S(2)}, u32[]{:S(2)}) collective-permute-start(bf16[16,32,128]{2,1,0:T(8,128)(2,1)S(1)} %get-tuple-element.42), channel_id=1, source_target_pairs={{0,5},{1,4},{2,7},{3,6},{4,0},{5,1},{6,2},{7,3},{8,13},{9,12},{10,... | collective-permute-start | bytes 393224 | tf_op jit(solution)/shard_map/ppermute | solution.py:279
  39.6 3.9 %collective-permute-start.27 = (bf16[16,32,128]{2,1,0:T(8,128)(2,1)S(1)}, bf16[16,32,128]{2,1,0:T(8,128)(2,1)S(1)}, u32[]{:S(2)}, u32[]{:S(2)}) collective-permute-start(bf16[16,32,128]{2,1,0:T(8,128)(2,1)S(1)} %get-tuple-element.42), channel_id=1, source_target_pairs={{0,4},{1,5},{2,6},{3,7},{4,0},{5,1},{6,2},{7,3},{8,12},{9,13},{10,... | collective-permute-start | bytes 393224 | tf_op jit(solution)/shard_map/ppermute | solution.py:279
  39.7 3.8 %collective-permute-start.31 = (bf16[32,32,128]{2,1,0:T(8,128)(2,1)S(1)}, bf16[32,32,128]{2,1,0:T(8,128)(2,1)S(1)}, u32[]{:S(2)}, u32[]{:S(2)}) collective-permute-start(bf16[32,32,128]{2,1,0:T(8,128)(2,1)S(1)} %get-tuple-element.43.refs_3_), channel_id=1, source_target_pairs={{0,4},{1,5},{2,6},{3,7},{4,0},{5,1},{6,2},{7,3},{8,12},{9,13},{10,... | collective-permute-start | bytes 786440 | tf_op jit(solution)/shard_map/ppermute | solution.py:279
  43.6 13.4 %collective-permute-start.32 = (bf16[32,32,128]{2,1,0:T(8,128)(2,1)S(1)}, bf16[32,32,128]{2,1,0:T(8,128)(2,1)S(1)}, u32[]{:S(2)}, u32[]{:S(2)}) collective-permute-start(bf16[32,32,128]{2,1,0:T(8,128)(2,1)S(1)} %get-tuple-element.45), channel_id=1, source_target_pairs={{0,4},{1,5},{2,6},{3,7},{4,0},{5,1},{6,2},{7,3},{8,12},{9,13},{10,... | collective-permute-start | bytes 786440 | tf_op jit(solution)/shard_map/ppermute | solution.py:279
  57.5 2.1 %collective-permute-start.36 = (bf16[16,32,128]{2,1,0:T(8,128)(2,1)S(1)}, bf16[16,32,128]{2,1,0:T(8,128)(2,1)S(1)}, u32[]{:S(2)}, u32[]{:S(2)}) collective-permute-start(bf16[16,32,128]{2,1,0:T(8,128)(2,1)S(1)} %project.5), channel_id=1, source_target_pairs={{0,4},{1,5},{2,6},{3,7},{4,3},{5,2},{6,1},{7,0},{8,12},{9,13},{10,... | collective-permute-start | bytes 393224 | tf_op jit(solution)/shard_map/ppermute | solution.py:279
  57.6 4.1 %collective-permute-start.35 = (bf16[16,32,128]{2,1,0:T(8,128)(2,1)S(1)}, bf16[16,32,128]{2,1,0:T(8,128)(2,1)S(1)}, u32[]{:S(2)}, u32[]{:S(2)}) collective-permute-start(bf16[16,32,128]{2,1,0:T(8,128)(2,1)S(1)} %project.5), channel_id=1, source_target_pairs={{0,4},{1,5},{2,6},{3,7},{4,2},{5,3},{6,0},{7,1},{8,12},{9,13},{10,... | collective-permute-start | bytes 393224 | tf_op jit(solution)/shard_map/ppermute | solution.py:279
  59.0 2.7 %collective-permute-start.34 = (bf16[16,32,128]{2,1,0:T(8,128)(2,1)S(1)}, bf16[16,32,128]{2,1,0:T(8,128)(2,1)S(1)}, u32[]{:S(2)}, u32[]{:S(2)}) collective-permute-start(bf16[16,32,128]{2,1,0:T(8,128)(2,1)S(1)} %project.5), channel_id=1, source_target_pairs={{0,4},{1,5},{2,6},{3,7},{4,1},{5,0},{6,3},{7,2},{8,12},{9,13},{10,... | collective-permute-start | bytes 393224 | tf_op jit(solution)/shard_map/ppermute | solution.py:279
  59.1 2.6 %collective-permute-start.33 = (bf16[16,32,128]{2,1,0:T(8,128)(2,1)S(1)}, bf16[16,32,128]{2,1,0:T(8,128)(2,1)S(1)}, u32[]{:S(2)}, u32[]{:S(2)}) collective-permute-start(bf16[16,32,128]{2,1,0:T(8,128)(2,1)S(1)} %project.5), channel_id=1, source_target_pairs={{0,4},{1,5},{2,6},{3,7},{4,0},{5,1},{6,2},{7,3},{8,12},{9,13},{10,... | collective-permute-start | bytes 393224 | tf_op jit(solution)/shard_map/ppermute | solution.py:279
  59.5 2.2 %collective-permute-start.37 = (bf16[32,32,128]{2,1,0:T(8,128)(2,1)S(1)}, bf16[32,32,128]{2,1,0:T(8,128)(2,1)S(1)}, u32[]{:S(2)}, u32[]{:S(2)}) collective-permute-start(bf16[32,32,128]{2,1,0:T(8,128)(2,1)S(1)} %collective-permute-done.32.image), channel_id=1, source_target_pairs={{0,4},{1,5},{2,6},{3,7},{4,0},{5,1},{6,2},{7,3},{8,12},{9,13},{10,... | collective-permute-start | bytes 786440 | tf_op jit(solution)/shard_map/ppermute | solution.py:279
  61.7 6.6 %collective-permute-start.41 = (bf16[16,32,128]{2,1,0:T(8,128)(2,1)S(1)}, bf16[16,32,128]{2,1,0:T(8,128)(2,1)S(1)}, u32[]{:S(2)}, u32[]{:S(2)}) collective-permute-start(bf16[16,32,128]{2,1,0:T(8,128)(2,1)S(1)} %get-tuple-element.46), channel_id=1, source_target_pairs={{0,7},{1,6},{2,5},{3,4},{4,0},{5,1},{6,2},{7,3},{8,15},{9,14},{10,... | collective-permute-start | bytes 393224 | tf_op jit(solution)/shard_map/ppermute | solution.py:279
  64.7 5.0 %collective-permute-start.40 = (bf16[16,32,128]{2,1,0:T(8,128)(2,1)S(1)}, bf16[16,32,128]{2,1,0:T(8,128)(2,1)S(1)}, u32[]{:S(2)}, u32[]{:S(2)}) collective-permute-start(bf16[16,32,128]{2,1,0:T(8,128)(2,1)S(1)} %get-tuple-element.46), channel_id=1, source_target_pairs={{0,6},{1,7},{2,4},{3,5},{4,0},{5,1},{6,2},{7,3},{8,14},{9,15},{10,... | collective-permute-start | bytes 393224 | tf_op jit(solution)/shard_map/ppermute | solution.py:279
  64.7 4.9 %collective-permute-start.39 = (bf16[16,32,128]{2,1,0:T(8,128)(2,1)S(1)}, bf16[16,32,128]{2,1,0:T(8,128)(2,1)S(1)}, u32[]{:S(2)}, u32[]{:S(2)}) collective-permute-start(bf16[16,32,128]{2,1,0:T(8,128)(2,1)S(1)} %get-tuple-element.46), channel_id=1, source_target_pairs={{0,5},{1,4},{2,7},{3,6},{4,0},{5,1},{6,2},{7,3},{8,13},{9,12},{10,... | collective-permute-start | bytes 393224 | tf_op jit(solution)/shard_map/ppermute | solution.py:279
  66.0 3.7 %collective-permute-start.38 = (bf16[16,32,128]{2,1,0:T(8,128)(2,1)S(1)}, bf16[16,32,128]{2,1,0:T(8,128)(2,1)S(1)}, u32[]{:S(2)}, u32[]{:S(2)}) collective-permute-start(bf16[16,32,128]{2,1,0:T(8,128)(2,1)S(1)} %get-tuple-element.46), channel_id=1, source_target_pairs={{0,4},{1,5},{2,6},{3,7},{4,0},{5,1},{6,2},{7,3},{8,12},{9,13},{10,... | collective-permute-start | bytes 393224 | tf_op jit(solution)/shard_map/ppermute | solution.py:279
  66.0 4.3 %collective-permute-start.42 = (bf16[32,32,128]{2,1,0:T(8,128)(2,1)S(1)}, bf16[32,32,128]{2,1,0:T(8,128)(2,1)S(1)}, u32[]{:S(2)}, u32[]{:S(2)}) collective-permute-start(bf16[32,32,128]{2,1,0:T(8,128)(2,1)S(1)} %get-tuple-element.47.refs_3_), channel_id=1, source_target_pairs={{0,4},{1,5},{2,6},{3,7},{4,0},{5,1},{6,2},{7,3},{8,12},{9,13},{10,... | collective-permute-start | bytes 786440 | tf_op jit(solution)/shard_map/ppermute | solution.py:279
